TPU v7x, 32 devices: a whole 2x2x4 slice. The times are simulated.
32 devices in a mesh: wide: 8 (over z, y), narrow: 4 (over x, core).
Axes of the slice: x: 2, y: 2, z: 4, core: 2. Of those that a mesh axis runs over, the one named last changes fastest.
Arguments:
- hidden: bfloat16 [40, 4096], P('wide', 'narrow'), may hold values from -18 to 18
- w_query: bfloat16 [4096, 4096], P('narrow', 'wide'), may hold values from -0.09375 to 0.09375
- w_keyval: bfloat16 [4096, 1024], P('narrow', 'wide'), may hold values from -0.09375 to 0.09375
- w_out: bfloat16 [4096, 4096], P('narrow', 'wide'), may hold values from -0.09375 to 0.09375
- pool: bfloat16 [4096, 16, 1024], P(('wide', 'narrow')), may hold values from -144 to 144
- page_req: int32 [4096], P(('wide', 'narrow')), may hold values from -1 to 7, as said below
- page_idx: int32 [4096], P(('wide', 'narrow')), may hold values from -1 to 511, as said below
- lengths: int32 [8], replicated, may hold values from 128 to 8192, as said below
- moves: int32 [4096, 1], P(('wide', 'narrow')), may hold values from 0 to 7; in each aligned block of 128 rows (0 to 127, 128 to 255, ...) at most 16 rows name the same one
- accepted: int32 [8], replicated, may hold values from 1 to 5
Outputs:
- attended: bfloat16 [40, 4096], P('narrow', 'wide')
- new_entries: bfloat16 [8, 5, 1024], P('wide')
- moved_pool: bfloat16 [4096, 16, 1024], P(('wide', 'narrow'))
- moved_req: int32 [4096], P(('wide', 'narrow'))
- moved_idx: int32 [4096], P(('wide', 'narrow'))
Inputs may be any that keep to these rules, and one draw needn't show every extreme that they name: Request r holds exactly ceil(lengths[r] / 16) slots, whose page numbers are 0 up to that count minus 1, each once; every other slot is free, with page_req and page_idx -1. `page_idx`: see page_req. `lengths`: each length lies either in 128 to 256 or in 6144 to 8192; exactly 4 lie in the second range. `moves`: each device sends exactly 16 of its slots to each index of wide.
All inputs are finite; a program needn't handle non-finite values.
Results may differ from a plain program's by a relative error of at most 0.03.
Values may be sent and summed in bfloat16 or wider, within the bound.
No kernel may reach another device: no remote copies, remote signals or barrier semaphores. Data moves between devices by JAX's collectives and lax.ppermute only.
A program may use at most 128 MiB of HBM per device.

v0:
```python
import math

import jax
import jax.numpy as jnp
from jax import lax
from jax.sharding import PartitionSpec as P

HEADS = 32
KVH = 4
HD = 128
STEPS = 5
PAGE = 16


NEG_FILL = -1e30


def combine(first, second):
    peak = jnp.maximum(first[0], second[0])
    lead = jnp.exp(first[0] - peak)
    trail = jnp.exp(second[0] - peak)
    return (
        peak,
        first[1] * lead + second[1] * trail,
        first[2] * lead[..., None] + second[2] * trail[..., None],
    )


def on_device(hidden, w_query, w_keyval, w_out, pool, page_req, page_idx, lengths, moves, accepted):
    wide_count = lax.axis_size("wide")
    narrow_count = lax.axis_size("narrow")
    groups = HEADS // KVH
    scale = 1.0 / math.sqrt(HD)
    rows_all = lax.all_gather(hidden, "wide", axis=0, tiled=True)
    total_rows = rows_all.shape[0]
    req_total = total_rows // STEPS
    joined = jnp.concatenate([w_query, w_keyval], axis=1)
    query_cols = w_query.shape[1]
    picked = rows_all
    projected = lax.psum_scatter(
        jnp.dot(picked, joined, preferred_element_type=jnp.float32),
        "narrow",
        scatter_dimension=0,
        tiled=True,
    ).astype(jnp.bfloat16)
    query_rows, keyval_rows = (
        lax.all_gather(projected[:, :query_cols], "narrow", axis=0, tiled=True),
        lax.all_gather(projected[:, query_cols:], "narrow", axis=0, tiled=True),
    )
    query_full, keyval_full = (
        lax.all_gather(query_rows, "wide", axis=1, tiled=True),
        lax.all_gather(keyval_rows, "wide", axis=1, tiled=True),
    )
    query = query_full.reshape(req_total, STEPS, KVH, groups, HD)
    keyval = keyval_full.reshape(req_total, STEPS, 2, KVH, HD)
    pool_size = pool.shape[0]
    capacity = pool_size // wide_count
    dest = moves[:, 0]
    order = jnp.arange(pool_size, dtype=jnp.int32)
    rank = jnp.sum((dest[:, None] == dest[None, :]) & (order[None, :] < order[:, None]), axis=1)
    target = dest * capacity + rank
    source_of = jnp.sum(jnp.where(target[None, :] == order[:, None], order[None, :], 0), axis=1)
    moved = (
        lax.all_to_all(
            jnp.take(pool, source_of, axis=0), "wide", split_axis=0, concat_axis=0, tiled=True
        ),
        lax.all_to_all(
            jnp.take(page_req, source_of), "wide", split_axis=0, concat_axis=0, tiled=True
        ),
        lax.all_to_all(
            jnp.take(page_idx, source_of), "wide", split_axis=0, concat_axis=0, tiled=True
        ),
    )
    pages = moved[0]
    requests = moved[1]
    count = pages.shape[0]
    owners = jnp.maximum(requests, 0)
    cache = pages.reshape(count, PAGE, 2, KVH, HD)
    page_query = jnp.take(query, owners, axis=0)
    scores = (
        jnp.einsum(
            "pskgd,ptkd->pkgst", page_query, cache[:, :, 0], preferred_element_type=jnp.float32
        )
        * scale
    )
    positions = moved[2][:, None] * PAGE + jnp.arange(PAGE, dtype=jnp.int32)[None, :]
    visible = (positions < jnp.take(lengths, owners)[:, None]) & (requests >= 0)[:, None]
    visible = visible[:, None, None, None, :]
    scores = jnp.where(visible, scores, NEG_FILL)
    peaks = jnp.max(scores, axis=-1)
    weights = jnp.where(visible, jnp.exp(scores - peaks[..., None]), 0.0)
    totals = jnp.sum(weights, axis=-1)
    sums = jnp.einsum(
        "pkgst,ptkd->pkgsd",
        weights.astype(jnp.bfloat16),
        cache[:, :, 1],
        preferred_element_type=jnp.float32,
    )
    member = requests[None, :] == jnp.arange(req_total, dtype=jnp.int32)[:, None]
    req_peaks = jnp.max(jnp.where(member[:, :, None, None, None], peaks[None], NEG_FILL), axis=1)
    factor = jnp.exp(peaks - jnp.take(req_peaks, owners, axis=0))
    selector = member.astype(jnp.float32)
    req_totals = jnp.dot(
        selector, (totals * factor).reshape(count, -1), precision=lax.Precision.HIGHEST
    )
    req_sums = jnp.dot(
        selector, (sums * factor[..., None]).reshape(count, -1), precision=lax.Precision.HIGHEST
    )
    req_totals = req_totals.reshape(req_total, KVH, groups, STEPS)
    req_sums = req_sums.reshape(req_total, KVH, groups, STEPS, HD)
    row_peaks = jnp.transpose(req_peaks, (0, 3, 1, 2)).reshape(total_rows, HEADS)
    row_totals = jnp.transpose(req_totals, (0, 3, 1, 2)).reshape(total_rows, HEADS)
    row_sums = jnp.transpose(req_sums, (0, 3, 1, 2, 4)).reshape(total_rows, HEADS, HD)
    state = (row_peaks, row_totals, row_sums)
    fresh_scores = (
        jnp.einsum("rskgd,rtkd->rkgst", query, keyval[:, :, 0], preferred_element_type=jnp.float32)
        * scale
    )
    causal = jnp.arange(STEPS)[None, :] <= jnp.arange(STEPS)[:, None]
    fresh_scores = jnp.where(causal, fresh_scores, NEG_FILL)
    fresh_peaks = jnp.max(fresh_scores, axis=-1)
    fresh_weights = jnp.where(causal, jnp.exp(fresh_scores - fresh_peaks[..., None]), 0.0)
    fresh_totals = jnp.sum(fresh_weights, axis=-1)
    fresh_sums = jnp.einsum(
        "rkgst,rtkd->rskgd",
        fresh_weights.astype(jnp.bfloat16),
        keyval[:, :, 1],
        preferred_element_type=jnp.float32,
    )
    self_peaks = jnp.transpose(fresh_peaks, (0, 3, 1, 2)).reshape(total_rows, HEADS)
    self_totals = jnp.transpose(fresh_totals, (0, 3, 1, 2)).reshape(total_rows, HEADS)
    self_sums = fresh_sums.reshape(total_rows, HEADS, HD)
    head_count = HEADS // narrow_count
    first_head = lax.axis_index("narrow") * head_count
    mine_peaks = lax.dynamic_slice_in_dim(self_peaks, first_head, head_count, 1)
    mine_totals = lax.dynamic_slice_in_dim(self_totals, first_head, head_count, 1)
    mine_sums = lax.dynamic_slice_in_dim(self_sums, first_head, head_count, 1)
    peak_all = lax.pmax(state[0], ("wide", "narrow"))
    lead = jnp.exp(state[0] - peak_all)
    scaled_sums = (state[2] * lead[..., None]).reshape(total_rows, HEADS * HD)
    part_sums, part_totals = (
        lax.psum_scatter(
            scaled_sums.astype(jnp.bfloat16), "narrow", scatter_dimension=1, tiled=True
        ).astype(jnp.float32),
        lax.psum_scatter(
            (state[1] * lead).astype(jnp.bfloat16), "narrow", scatter_dimension=1, tiled=True
        ).astype(jnp.float32),
    )
    full_sums, full_totals = (
        lax.psum(part_sums.astype(jnp.bfloat16), "wide").astype(jnp.float32),
        lax.psum(part_totals.astype(jnp.bfloat16), "wide").astype(jnp.float32),
    )
    block_peaks = lax.dynamic_slice_in_dim(peak_all, first_head, head_count, 1)
    final = combine(
        (block_peaks, full_totals, full_sums.reshape(total_rows, head_count, HD)),
        (mine_peaks, mine_totals, mine_sums),
    )
    attn_block = (
        (final[2] / final[1][..., None]).reshape(total_rows, head_count * HD).astype(jnp.bfloat16)
    )
    picked = attn_block
    attended = lax.psum_scatter(
        jnp.dot(picked, w_out, preferred_element_type=jnp.float32).astype(jnp.bfloat16),
        "narrow",
        scatter_dimension=0,
        tiled=True,
    )
    local_req = hidden.shape[0] // STEPS
    first_req = lax.axis_index("wide") * local_req
    fresh_rows = lax.dynamic_slice_in_dim(
        keyval_full.reshape(req_total, STEPS, -1), first_req, local_req, 0
    )
    kept = lax.dynamic_slice_in_dim(accepted, first_req, local_req, 0)
    step_ids = jnp.arange(STEPS, dtype=jnp.int32)
    new_entries = jnp.where(
        step_ids[None, :, None] < kept[:, None, None], fresh_rows, jnp.zeros((), jnp.bfloat16)
    )
    return (attended, new_entries, moved[0], moved[1], moved[2])


def solution(mesh):
    in_specs = (
        P("wide", "narrow"),
        P("narrow", "wide"),
        P("narrow", "wide"),
        P("narrow", "wide"),
        P(("wide", "narrow"), None, None),
        P(("wide", "narrow")),
        P(("wide", "narrow")),
        P(),
        P(("wide", "narrow"), None),
        P(),
    )
    out_specs = (
        P("narrow", "wide"),
        P("wide", None, None),
        P(("wide", "narrow"), None, None),
        P(("wide", "narrow")),
        P(("wide", "narrow")),
    )
    return jax.shard_map(
        on_device, mesh=mesh, in_specs=in_specs, out_specs=out_specs, check_vma=False
    )
```

profile of v0, /device:TPU:0, one launch (start us, length us, event | category | flops | bytes accessed | tf_op | source)
XLA Modules:
  0.0 537.0 jit_solution(14484445190104418206)
XLA Ops:
  8.9 1.6 gather_fusion.4
  10.5 1.6 gather_fusion.3
  12.8 7.3 %all-to-all-start = ((s32[8,16,1]{1,2,0:T(1,128)}), s32[8,16,1]{1,2,0:T(1,128)S(1)}, u32[]{:S(2)}, u32[]{:S(2)}) async-start(s32[8,16,1]{1,2,0:T(1,128)} %bitcast.1), calls=%async_computation | async-start | bytes 8192 | tf_op jit(solution)/shard_map/all_to_all | solution.py:67
  20.8 5.0 gather_fusion
  26.5 5.3 all-to-all-start.1
  31.8 4.6 broadcast_select_fusion.1
  36.4 1.7 all-to-all-done.1
  38.2 4.6 all-to-all-start.2
  42.8 112.1 %all-gather = bf16[8,5,1024]{2,1,0:T(8,128)(2,1)S(1)} all-gather(bf16[1,5,1024]{2,1,0:T(8,128)(2,1)S(1)} %bitcast.149), channel_id=1, replica_groups=mesh['wide'=8,'narrow'=4] {'wide'}, dimensions={0}, use_global_device_ids=true | all-gather | bytes 92160 | tf_op jit(solution)/shard_map/all_gather | solution.py:34
  156.5 11.3 %all-reduce = bf16[40,640]{1,0:T(8,128)(2,1)S(1)} all-reduce(f32[40,640]{1,0:T(8,128)S(1)} %fusion.29), channel_id=2, replica_groups=mesh['wide'=8,'narrow'=4] {'narrow'}, use_global_device_ids=true, to_apply=%region_2.0.clone | all-reduce | flops 25600 | bytes 153600
  167.8 5.2 all-gather.2
  173.1 26.0 %all_gather.19 = bf16[40,1024]{1,0:T(8,128)(2,1)S(1)} all-gather(bf16[40,128]{1,0:T(8,128)(2,1)S(1)} %reshape.299), channel_id=1, replica_groups=mesh['wide'=8,'narrow'=4] {'wide'}, dimensions={1}, use_global_device_ids=true | all-gather | bytes 92160 | tf_op jit(solution)/shard_map/all_gather | solution.py:52
  199.8 5.2 all-gather.1
  205.1 31.1 %all_gather.17 = bf16[40,4096]{1,0:T(8,128)(2,1)S(1)} all-gather(bf16[40,512]{1,0:T(8,128)(2,1)S(1)} %reshape.297), channel_id=1, replica_groups=mesh['wide'=8,'narrow'=4] {'wide'}, dimensions={1}, use_global_device_ids=true | all-gather | bytes 368640 | tf_op jit(solution)/shard_map/all_gather | solution.py:51
  236.9 1.3 fusion.36
  243.1 3.6 gather_fusion.1
  246.7 4.9 fusion.50
  251.8 6.8 %copy.86 = bf16[128,16,1024]{0,2,1:T(8,128)(2,1)} copy(bf16[128,16,1024]{2,1,0:T(8,128)(2,1)} %all-to-all-done.2) | data formatting | bytes 8388608 | tf_op jit(solution)/shard_map/all_to_all | solution.py:64
  258.5 4.0 fusion.59
  262.5 2.9 copy.124
  265.4 10.2 %bitcast_reduce_fusion = (f32[128,4,8,5]{2,3,1,0:T(8,128)S(1)}, f32[128,4,16,5,8]{2,4,3,1,0:T(8,128)}) fusion(pred[128,16]{1,0:T(8,128)(4,1)S(1)} %fusion.42, bf16[128,16,1,4,128]{4,1,3,0,2:T(8,128)(2,1)} %copy.124, bf16[128,5,4,8,128]{4,3,2,1,0:T(8,128)(2,1)} %gather_fusion.1, pred[128]{0:T(512)(128)(4,1)S(1)} %get-tuple-element.22), kind=kOutput, calls=%fused_computation.8 | convolution fusion | flops 87470080 | bytes 8734848 | tf_op jit(solution)/shard_map/pskgd,ptkd->pkgst/dot_general | solution.py:81
  276.4 1.9 copy.108
  279.3 2.5 gather_fusion.2
  281.7 2.5 copy.109
  284.3 2.3 copy.92
  286.6 12.2 %fusion.4 = f32[128,4,8,5]{2,3,1,0:T(8,128)} fusion(f32[128,4,16,5,8]{2,4,3,1,0:T(8,128)} %get-tuple-element.32, f32[128,4,8,5]{2,3,1,0:T(8,128)S(1)} %get-tuple-element.31, pred[128,16]{1,0:T(8,128)(4,1)} %copy-done.4), kind=kLoop, calls=%fused_computation.12 | loop fusion | flops 1617920 | bytes 1476608 | tf_op jit(solution)/shard_map/reduce_sum | solution.py:92
  298.8 3.3 copy.107
  303.0 1.5 gather.25
  304.6 1.6 reduce_max.32
  306.1 1.6 multiply_bitcast_fusion
  307.7 1.6 dot_general.44
  309.2 1.6 convolution_bitcast_fusion.1
  311.5 1.6 reshape.231
  314.7 37.7 %pmax.7 = f32[40,32]{1,0:T(8,128)} all-reduce(f32[40,32]{1,0:T(8,128)} %reshape.225), channel_id=1, replica_groups=mesh['wide'=8,'narrow'=4] {'wide','narrow'}, use_global_device_ids=true, to_apply=%region_5.7 | all-reduce | flops 1280 | bytes 10240 | tf_op jit(solution)/shard_map/pmax | solution.py:138
  353.3 2.8 copy.94
  356.1 4.6 copy.125
  360.7 11.9 %broadcast_multiply_fusion = f32[128,4,8,5,128]{4,2,3,1,0:T(8,128)} fusion(f32[128,4,8,5]{2,3,1,0:T(8,128)} %copy.94, bf16[128,16,1,4,128]{4,1,3,0,2:T(8,128)(2,1)} %copy.125, f32[128,4,16,5,8]{2,4,3,1,0:T(8,128)} %get-tuple-element.32, f32[128,4,8,5]{2,3,1,0:T(8,128)S(1)} %get-tuple-element.31, pred[128,16]{1,0:T(8,128)(4,1)S(1)} %copy-done.5), kind=kOutput, calls=%fused_computation.17 | convolution fusion | flops 88145920 | bytes 14059520 | tf_op jit(solution)/shard_map/pkgst,ptkd->pkgsd/dot_general | solution.py:93
  372.6 12.1 %copy.95 = f32[128,4,8,5,128]{0,4,3,2,1:T(8,128)} copy(f32[128,4,8,5,128]{4,2,3,1,0:T(8,128)} %broadcast_multiply_fusion) | data formatting | bytes 20971520 | tf_op jit(solution)/shard_map/mul | solution.py:107
  384.7 7.4 %fusion.26 = f32[8,5,4,8,128]{4,0,1,3,2:T(8,128)S(1)} fusion(f32[128,4,8,5,128]{0,4,3,2,1:T(8,128)} %copy.95, s32[128]{0:T(128)S(1)} %copy-done.12), kind=kOutput, calls=%fused_computation.32 | convolution fusion | flops 251659264 | bytes 11141632 | tf_op jit(solution)/shard_map/dot_general | solution.py:106
  392.7 1.1 fusion.32
  395.6 1.4 dynamic-slice_select_fusion
  397.0 12.0 %all-reduce.1 = bf16[40,32]{1,0:T(8,128)(2,1)S(1)} all-reduce(bf16[40,32]{1,0:T(8,128)(2,1)S(1)} %get-tuple-element.11), channel_id=4, replica_groups=mesh['wide'=8,'narrow'=4] {'narrow'}, use_global_device_ids=true, to_apply=%region_10.12.clone | all-reduce | flops 1280 | bytes 5120
  409.1 35.4 %psum.15 = bf16[40,8]{1,0:T(8,128)(2,1)S(1)} all-reduce(bf16[40,8]{1,0:T(8,128)(2,1)S(1)} %constant_dynamic-slice_fusion.1), channel_id=1, replica_groups=mesh['wide'=8,'narrow'=4] {'wide'}, use_global_device_ids=true, to_apply=%region_11.13 | all-reduce | flops 320 | bytes 1280 | tf_op jit(solution)/shard_map/psum | solution.py:151
  444.4 1.5 copy.132
  446.1 66.5 %all-reduce.5.cloned.1.call-done = bf16[40,8,128]{2,1,0:T(8,128)(2,1)} async-done(((bf16[40,8,128]{2,1,0:T(8,128)(2,1)}), bf16[40,8,128]{2,1,0:T(8,128)(2,1)}) %all-reduce.5.cloned.1.call-update) | async-done | bytes 81936 | tf_op jit(solution)/shard_map/psum | solution.py:150
  512.6 1.1 divide_convert_fusion
  514.0 10.5 %all-reduce.2 = bf16[40,512]{1,0:T(8,128)(2,1)S(1)} all-reduce(bf16[40,512]{1,0:T(8,128)(2,1)S(1)} %convolution_convert_fusion), channel_id=5, replica_groups=mesh['wide'=8,'narrow'=4] {'narrow'}, use_global_device_ids=true, to_apply=%region_13.15.clone | all-reduce | flops 20480 | bytes 81920
  525.1 5.0 copy.164
  (108 shorter events, 19.9 us)
Async XLA Ops:
  7.2 506.5 %copy-start = (bf16[1024,512]{1,0:T(8,128)(2,1)S(1)}, bf16[1024,512]{1,0:T(8,128)(2,1)}, u32[]{:S(2)}) copy-start(bf16[1024,512]{1,0:T(8,128)(2,1)} %param.15) | copy-start | bytes 3145732
  12.8 13.7 %all-to-all-start = ((s32[8,16,1]{1,2,0:T(1,128)}), s32[8,16,1]{1,2,0:T(1,128)S(1)}, u32[]{:S(2)}, u32[]{:S(2)}) async-start(s32[8,16,1]{1,2,0:T(1,128)} %bitcast.1), calls=%async_computation | async-start | bytes 8192 | tf_op jit(solution)/shard_map/all_to_all | solution.py:67
  26.5 11.7 %all-to-all-start.1 = ((s32[8,16,1]{1,2,0:T(1,128)}), s32[8,16,1]{1,2,0:T(1,128)S(1)}, u32[]{:S(2)}, u32[]{:S(2)}) async-start(s32[8,16,1]{1,2,0:T(1,128)} %bitcast.4), calls=%async_computation.1 | async-start | bytes 8192 | tf_op jit(solution)/shard_map/all_to_all | solution.py:70
  36.4 6.4 %copy-start.10 = (bf16[5,1024]{1,0:T(8,128)(2,1)S(1)}, bf16[5,1024]{1,0:T(8,128)(2,1)}, u32[]{:S(2)}) copy-start(bf16[5,1024]{1,0:T(8,128)(2,1)} %param.12) | copy-start | bytes 30724
  36.4 118.5 %copy-start.19 = (u32[32]{0:T(128)S(1)}, u32[32]{0:T(128)}, u32[]{:S(2)}) copy-start(u32[32]{0:T(128)} %constant.108) | copy-start | bytes 388
  36.4 119.7 %copy-start.16 = (bf16[1024,512]{1,0:T(8,128)(2,1)S(1)}, bf16[1024,512]{1,0:T(8,128)(2,1)}, u32[]{:S(2)}) copy-start(bf16[1024,512]{1,0:T(8,128)(2,1)} %param.13) | copy-start | bytes 3145732
  36.4 119.8 %copy-start.17 = (bf16[1024,128]{1,0:T(8,128)(2,1)S(1)}, bf16[1024,128]{1,0:T(8,128)(2,1)}, u32[]{:S(2)}) copy-start(bf16[1024,128]{1,0:T(8,128)(2,1)} %param.14) | copy-start | bytes 786436
  38.2 213.6 %all-to-all-start.2 = ((bf16[128,16,1024]{2,1,0:T(8,128)(2,1)}), bf16[128,16,1024]{2,1,0:T(8,128)(2,1)}, u32[]{:S(2)}, u32[]{:S(2)}) async-start(bf16[128,16,1024]{2,1,0:T(8,128)(2,1)} %broadcast_select_fusion.1), calls=%async_computation.2 | async-start | bytes 8388608 | tf_op jit(solution)/shard_map/all_to_all | solution.py:64
  42.7 197.6 %copy-start.9 = (s32[8]{0:T(128)S(1)}, s32[8]{0:T(128)}, u32[]{:S(2)}) copy-start(s32[8]{0:T(128)} %param.19) | copy-start | bytes 100
  42.7 401.7 %reduce-scatter.3.cloned.1.call-start = ((), (), s32[]{:S(2)}) async-start(), calls=%async_computation.4 | async-start | bytes 409600 | tf_op jit(solution)/shard_map/reduce_scatter | solution.py:142
  242.2 4.5 copy-start.11
  243.1 3.7 copy-start.15
  243.1 3.6 copy-start.13
  246.7 18.7 %copy-start.14 = (pred[128]{0:T(512)(128)(4,1)}, pred[128]{0:T(512)(128)(4,1)S(1)}, u32[]{:S(2)}) copy-start(pred[128]{0:T(512)(128)(4,1)S(1)} %get-tuple-element.22) | copy-start | bytes 388
  251.7 13.7 %copy-start.4 = (pred[128,16]{1,0:T(8,128)(4,1)}, pred[128,16]{1,0:T(8,128)(4,1)S(1)}, u32[]{:S(2)}) copy-start(pred[128,16]{1,0:T(8,128)(4,1)S(1)} %fusion.42) | copy-start | bytes 6148
  278.6 0.7 copy-start.1
  353.3 7.4 %copy-start.5 = (pred[128,16]{1,0:T(8,128)(4,1)S(1)}, pred[128,16]{1,0:T(8,128)(4,1)}, u32[]{:S(2)}) copy-start(pred[128,16]{1,0:T(8,128)(4,1)} %copy-done.4) | copy-start | bytes 6148
  372.6 12.1 %copy-start.12 = (s32[128]{0:T(128)S(1)}, s32[128]{0:T(128)}, u32[]{:S(2)}) copy-start(s32[128]{0:T(128)} %copy-done.11) | copy-start | bytes 1540
  384.7 7.7 %copy-start.2 = (f32[40,32]{1,0:T(8,128)S(1)}, f32[40,32]{1,0:T(8,128)}, u32[]{:S(2)}) copy-start(f32[40,32]{1,0:T(8,128)} %reshape.225) | copy-start | bytes 15364
  384.7 7.7 %copy-start.3 = (f32[40,32]{1,0:T(8,128)S(1)}, f32[40,32]{1,0:T(8,128)}, u32[]{:S(2)}) copy-start(f32[40,32]{1,0:T(8,128)} %pmax.7) | copy-start | bytes 15364
  384.7 7.8 %copy-start.6 = (f32[40,32]{1,0:T(8,128)S(1)}, f32[40,32]{1,0:T(8,128)}, u32[]{:S(2)}) copy-start(f32[40,32]{1,0:T(8,128)} %reshape.231) | copy-start | bytes 15364
  392.1 2.2 copy-start.18
  392.2 53.8 %copy-start.7 = (f32[40,32]{1,0:T(8,128)S(1)}, f32[40,32]{1,0:T(8,128)}, u32[]{:S(2)}) copy-start(f32[40,32]{1,0:T(8,128)} %reshape.232) | copy-start | bytes 15364
  392.2 53.8 %copy-start.8 = (f32[40,32]{1,0:T(8,128)S(1)}, f32[40,32]{1,0:T(8,128)}, u32[]{:S(2)}) copy-start(f32[40,32]{1,0:T(8,128)} %reshape.229) | copy-start | bytes 15364
  393.9 118.8 %all-reduce.5.cloned.1.call-start = ((), (), s32[]{:S(2)}) async-start(), calls=%async_computation.5 | async-start | bytes 163840 | tf_op jit(solution)/shard_map/psum | solution.py:150
Sparse Core Ops, SparseCore 0:
  394.0 22.6 reduce-scatter.2
  446.1 66.4 all-reduce.4
where the time goes:
time: 539 us; the launch traced here: 537 us
  blocking collectives  286 us (53%)
  local copies, waits for them, and re-layouts  82.7 us (15%)
  waiting for transfers between devices  69 us (13%)
  matrix products  33.3 us (6%)
  other arithmetic  32.7 us (6%)
  starting transfers between devices  17.2 us (3%)
  between operations  15.9 us (3%)
    all_gather x1, blocking collectives, on_device(): rows_all = lax.all_gather(hidden, 'wide', axis=0, tiled=True)  112 us
    psum x1, waiting for transfers between devices, on_device(): lax.psum(part_sums.astype(jnp.bfloat16), 'wide').astype(jnp.float32)  66.5 us
    pmax x1, blocking collectives, on_device(): peak_all = lax.pmax(state[0], ('wide', 'narrow'))  37.7 us
    psum x1, blocking collectives, on_device(): lax.psum(part_totals.astype(jnp.bfloat16), 'wide').astype(jnp.float32)  35.4 us
    unnamed x3, blocking collectives  33.8 us
    all_gather x1, blocking collectives, on_device(): lax.all_gather(query_rows, 'wide', axis=1, tiled=True)  31.1 us
    all_gather x1, blocking collectives, on_device(): lax.all_gather(keyval_rows, 'wide', axis=1, tiled=True)  26 us
    unnamed x53, local copies, waits for them, and re-layouts  16.2 us
  transfers between devices with their start and end apart: 5, of which 3 were waited for; matrix products, arithmetic and copies ran while one was open for 5% of the time, Pallas kernels for 0%

commit v1 on v0

v1 whole, which is shorter than its diff:
```python
import functools
import math

import jax
import jax.numpy as jnp
import numpy as np
from jax import lax
from jax.experimental import pallas as pl
from jax.experimental.pallas import tpu as pltpu
from jax.sharding import PartitionSpec as P

HEADS = 32
KVH = 4
HD = 128
STEPS = 5
PAGE = 16
GROUPS = HEADS // KVH
NEG_FILL = -1e30
SCALE2 = math.log2(math.e) / math.sqrt(HD)
STAT = 16
VMEM = 56 * 1024 * 1024
NT = (((1,), (1,)), ((), ()))


def up(value, unit):
    return -(-value // unit) * unit


def permute_kernel(source_ref, pool_ref, out_ref, sem):
    def start(j, carry):
        pltpu.make_async_copy(pool_ref.at[source_ref[j]], out_ref.at[j], sem).start()
        return carry

    lax.fori_loop(0, pool_ref.shape[0], start, 0)
    pltpu.make_async_copy(pool_ref, out_ref, sem).wait()


def permute_pages(source_of, pool):
    return pl.pallas_call(
        permute_kernel,
        out_shape=jax.ShapeDtypeStruct(pool.shape, pool.dtype),
        in_specs=[
            pl.BlockSpec(memory_space=pltpu.SMEM),
            pl.BlockSpec(memory_space=pl.ANY),
        ],
        out_specs=pl.BlockSpec(memory_space=pl.ANY),
        scratch_shapes=[pltpu.SemaphoreType.DMA],
        cost_estimate=pl.CostEstimate(
            flops=0, bytes_accessed=2 * pool.size * 2, transcendentals=0
        ),
    )(source_of, pool)


def attend_kernel(
    rows,
    piece,
    query_ref,
    key_ref,
    value_ref,
    new_key_ref,
    new_value_ref,
    req_ref,
    pos_ref,
    row_ref,
    new_bias_ref,
    out_ref,
    bias_ref,
    score_ref,
    weight_ref,
):
    tokens = key_ref.shape[0]
    per_block = GROUPS // query_ref.shape[0]

    @pl.when(pl.program_id(0) == 0)
    def _():
        seen = (req_ref[...] == row_ref[:, 0:1]) & (pos_ref[...] < row_ref[:, 1:2])
        bias_ref[...] = jnp.where(seen, 0.0, NEG_FILL)

    query = jnp.concatenate(
        [
            query_ref[g // per_block, :rows, pl.ds((g % per_block) * HD, HD)].astype(jnp.float32)
            for g in range(GROUPS)
        ],
        axis=0,
    ).astype(jnp.bfloat16)
    score_ref[:, :tokens] = lax.dot_general(
        query, key_ref[...], NT, preferred_element_type=jnp.float32
    )
    score_ref[:, tokens:] = lax.dot_general(
        query, new_key_ref[...], NT, preferred_element_type=jnp.float32
    )
    together = 1 if rows % 16 == 0 else 2
    span = together * rows
    peaks, totals = [], []
    for c in range(GROUPS // together):
        block = pl.ds(c * span, span)
        old = score_ref[block, :tokens].reshape(together, rows, tokens) * SCALE2 + bias_ref[...]
        new = score_ref[block, tokens:].reshape(together, rows, -1) * SCALE2 + new_bias_ref[...]
        peak = jnp.maximum(
            jnp.max(old, axis=-1, keepdims=True), jnp.max(new, axis=-1, keepdims=True)
        )
        old = jnp.exp2(old - peak)
        new = jnp.exp2(new - peak)
        totals.append(
            (jnp.sum(old, axis=-1, keepdims=True) + jnp.sum(new, axis=-1, keepdims=True)).reshape(
                span, 1
            )
        )
        peaks.append(peak.reshape(span, 1))
        weight_ref[block, :tokens] = old.reshape(span, tokens).astype(jnp.bfloat16)
        weight_ref[block, tokens:] = new.reshape(span, -1).astype(jnp.bfloat16)
    mixed = jnp.dot(
        weight_ref[:, :tokens], value_ref[...], preferred_element_type=jnp.float32
    ) + jnp.dot(weight_ref[:, tokens:], new_value_ref[...], preferred_element_type=jnp.float32)
    peak = jnp.concatenate(peaks, axis=0)
    total = jnp.concatenate(totals, axis=0)

    def cut(value):
        return value.astype(jnp.bfloat16).astype(jnp.float32)

    peak_high = cut(peak)
    peak_mid = cut(peak - peak_high)
    peak_low = peak - peak_high - peak_mid
    total_high = cut(total)
    total_low = total - total_high
    lane = lax.broadcasted_iota(jnp.int32, (GROUPS * rows, HD), 1)
    stats = jnp.zeros((GROUPS * rows, HD), jnp.float32)
    for i, part in enumerate((peak_high, peak_mid, peak_low, total_high, total_low)):
        stats = jnp.where(lane == i, part, stats)
    pick = (
        lax.broadcasted_iota(jnp.int32, (STAT, HD), 0)
        == lax.broadcasted_iota(jnp.int32, (STAT, HD), 1)
    ).astype(jnp.bfloat16)
    fill = out_ref.shape[1] - STAT - piece
    for c in range(GROUPS * rows // piece):
        part = slice(c * piece, (c + 1) * piece)
        turned = lax.dot_general(
            pick,
            jnp.concatenate(
                [stats[part], jnp.zeros((HD - piece, HD), jnp.float32)], axis=0
            ).astype(jnp.bfloat16),
            NT,
            preferred_element_type=jnp.float32,
        )
        out_ref[c] = jnp.concatenate(
            [turned, mixed[part], jnp.zeros((fill, HD), jnp.float32)], axis=0
        ).astype(jnp.bfloat16)


def attend(queries, keyval, pool, req_tok, pos_tok, row_info, new_bias, rows, piece):
    tokens = pool.shape[0]
    extra = keyval.shape[0]
    blocks = queries.shape[0] // KVH
    pieces = GROUPS * rows // piece
    height = STAT + up(piece, 16)
    whole = lambda shape: pl.BlockSpec(shape, lambda k: (0,) * len(shape))
    return pl.pallas_call(
        functools.partial(attend_kernel, rows, piece),
        grid=(KVH,),
        out_shape=jax.ShapeDtypeStruct((KVH * pieces, height, HD), jnp.bfloat16),
        in_specs=[
            pl.BlockSpec((blocks,) + queries.shape[1:], lambda k: (k, 0, 0)),
            pl.BlockSpec((tokens, HD), lambda k: (0, k)),
            pl.BlockSpec((tokens, HD), lambda k: (0, KVH + k)),
            pl.BlockSpec((extra, HD), lambda k: (0, k)),
            pl.BlockSpec((extra, HD), lambda k: (0, KVH + k)),
            whole(req_tok.shape),
            whole(pos_tok.shape),
            whole(row_info.shape),
            whole(new_bias.shape),
        ],
        out_specs=pl.BlockSpec((pieces, height, HD), lambda k: (k, 0, 0)),
        scratch_shapes=[
            pltpu.VMEM((rows, tokens), jnp.float32),
            pltpu.VMEM((GROUPS * rows, tokens + extra), jnp.float32),
            pltpu.VMEM((GROUPS * rows, tokens + extra), jnp.bfloat16),
        ],
        compiler_params=pltpu.CompilerParams(vmem_limit_bytes=VMEM),
        cost_estimate=pl.CostEstimate(
            flops=4 * HEADS * rows * (tokens + extra) * HD,
            bytes_accessed=pool.size * 2,
            transcendentals=HEADS * rows * (tokens + extra),
        ),
    )(queries, pool, pool, keyval, keyval, req_tok, pos_tok, row_info, new_bias)


def combine_kernel(piece, parts_ref, out_ref):
    count = parts_ref.shape[0]
    peaks, totals = [], []
    for i in range(count):
        stat = parts_ref[i, :STAT, :].astype(jnp.float32)
        peaks.append(stat[0:1] + stat[1:2] + stat[2:3])
        totals.append(stat[3:4] + stat[4:5])
    peak = jnp.concatenate(peaks, axis=0)
    total = jnp.concatenate(totals, axis=0)
    lead = jnp.exp2(peak - jnp.max(peak, axis=0, keepdims=True))
    whole = jnp.sum(lead * total, axis=0, keepdims=True)
    lane = lax.broadcasted_iota(jnp.int32, whole.shape, 1)
    share = lead / jnp.where(lane < piece, whole, 1.0)
    if count % HD:
        share = jnp.concatenate(
            [share, jnp.zeros((up(count, HD) - count, HD), jnp.float32)], axis=0
        )
    share = jnp.transpose(share)
    height = parts_ref.shape[1] - STAT
    result = jnp.zeros((height, HD), jnp.float32)
    for i in range(count):
        result = result + share[:height, i : i + 1] * parts_ref[i, STAT:, :].astype(jnp.float32)
    out_ref[...] = result[:piece].astype(jnp.bfloat16)


def combine(parts, piece):
    return pl.pallas_call(
        functools.partial(combine_kernel, piece),
        out_shape=jax.ShapeDtypeStruct((piece, HD), jnp.bfloat16),
        in_specs=[pl.BlockSpec(memory_space=pltpu.VMEM)],
        out_specs=pl.BlockSpec(memory_space=pltpu.VMEM),
        compiler_params=pltpu.CompilerParams(vmem_limit_bytes=VMEM),
        cost_estimate=pl.CostEstimate(
            flops=2 * parts.size, bytes_accessed=parts.size * 2, transcendentals=0
        ),
    )(parts)


def spread(block, axis):
    count = lax.axis_size(axis)
    return lax.all_to_all(
        jnp.broadcast_to(block[None], (count,) + block.shape),
        axis,
        split_axis=0,
        concat_axis=0,
        tiled=True,
    )


def on_device(hidden, w_query, w_keyval, w_out, pool, page_req, page_idx, lengths, moves, accepted):
    wide = lax.axis_size("wide")
    narrow = lax.axis_size("narrow")
    local_rows = hidden.shape[0]
    rows = local_rows * wide
    requests = rows // STEPS
    slots = pool.shape[0]
    capacity = slots // wide
    query_cols = w_query.shape[1]

    gathered = spread(hidden, "wide").reshape(rows, -1)

    dest = moves[:, 0]
    order = jnp.arange(slots, dtype=jnp.int32)
    rank = jnp.sum((dest[:, None] == dest[None, :]) & (order[None, :] < order[:, None]), axis=1)
    target = dest * capacity + rank
    chosen = target[None, :] == order[:, None]
    source_of = jnp.sum(jnp.where(chosen, order[None, :], 0), axis=1)
    sent_req = jnp.sum(jnp.where(chosen, page_req[None, :], 0), axis=1)
    sent_idx = jnp.sum(jnp.where(chosen, page_idx[None, :], 0), axis=1)
    ordered = permute_pages(source_of, pool)

    partial = jnp.concatenate(
        [
            jnp.dot(gathered, w_query, preferred_element_type=jnp.float32),
            jnp.dot(gathered, w_keyval, preferred_element_type=jnp.float32),
        ],
        axis=1,
    )
    projected = jnp.sum(spread(partial, "narrow"), axis=0).astype(jnp.bfloat16)
    shifted = sent_idx + 1
    tags = jnp.concatenate(
        [
            sent_req.reshape(wide, 1, capacity),
            (shifted // 32).reshape(wide, 1, capacity),
            (shifted % 32).reshape(wide, 1, capacity),
        ],
        axis=2,
    ).astype(jnp.bfloat16)
    height = up(rows + 1, 16)
    packed = jnp.concatenate(
        [
            jnp.broadcast_to(projected[None], (wide,) + projected.shape),
            jnp.pad(
                tags, ((0, 0), (0, height - rows - 1), (0, projected.shape[1] - 3 * capacity))
            ),
        ],
        axis=1,
    )
    received = lax.all_to_all(packed, "wide", split_axis=0, concat_axis=0, tiled=True)

    ordered, received = lax.optimization_barrier((ordered, received))
    moved_pool = lax.all_to_all(ordered, "wide", split_axis=0, concat_axis=0, tiled=True)
    tags_in = received[:, rows, : 3 * capacity].astype(jnp.int32)
    moved_req = tags_in[:, :capacity].reshape(slots)
    moved_idx = (
        tags_in[:, capacity : 2 * capacity] * 32 + tags_in[:, 2 * capacity :] - 1
    ).reshape(slots)

    keyval = jnp.transpose(received[:, :rows, query_cols:], (1, 0, 2)).reshape(rows, -1)
    extra = up(rows, HD)
    here = (lax.axis_index("wide") == 0) & (lax.axis_index("narrow") == 0)
    row_ids = np.arange(rows)[:, None]
    col_ids = np.arange(extra)[None, :]
    causal = (row_ids // STEPS == col_ids // STEPS) & (col_ids <= row_ids) & (col_ids < rows)
    new_bias = jnp.where(jnp.asarray(causal) & here, 0.0, NEG_FILL).astype(jnp.float32)
    req_tok = jnp.broadcast_to(page_req[:, None], (slots, PAGE)).reshape(1, -1)
    pos_tok = (page_idx[:, None] * PAGE + jnp.arange(PAGE, dtype=jnp.int32)[None, :]).reshape(1, -1)
    row_info = jnp.stack(
        [
            jnp.asarray(np.arange(rows) // STEPS, jnp.int32),
            jnp.broadcast_to(lengths[:, None], (requests, STEPS)).reshape(rows),
        ],
        axis=1,
    )
    piece = HEADS * rows // (wide * narrow)
    parts = attend(
        received,
        jnp.pad(keyval, ((0, extra - rows), (0, 0))),
        pool.reshape(slots * PAGE, -1),
        req_tok,
        pos_tok,
        row_info,
        new_bias,
        rows,
        piece,
    )
    parts = lax.all_to_all(parts, ("narrow", "wide"), split_axis=0, concat_axis=0, tiled=True)
    attn = spread(combine(parts, piece), "wide").reshape(-1, rows, HD)
    attn = jnp.transpose(attn, (1, 0, 2)).reshape(rows, -1)
    sums = jnp.dot(attn, w_out, preferred_element_type=jnp.float32)
    sums = sums.reshape(narrow, rows // narrow, -1)
    attended = jnp.sum(
        lax.all_to_all(sums, "narrow", split_axis=0, concat_axis=0, tiled=True), axis=0
    ).astype(jnp.bfloat16)

    local_req = local_rows // STEPS
    first_req = lax.axis_index("wide") * local_req
    fresh = lax.dynamic_slice_in_dim(keyval.reshape(requests, STEPS, -1), first_req, local_req, 0)
    kept = lax.dynamic_slice_in_dim(accepted, first_req, local_req, 0)
    new_entries = jnp.where(
        jnp.arange(STEPS)[None, :, None] < kept[:, None, None], fresh, jnp.zeros((), jnp.bfloat16)
    )
    return (attended, new_entries, moved_pool, moved_req, moved_idx)


def solution(mesh):
    in_specs = (
        P("wide", "narrow"),
        P("narrow", "wide"),
        P("narrow", "wide"),
        P("narrow", "wide"),
        P(("wide", "narrow"), None, None),
        P(("wide", "narrow")),
        P(("wide", "narrow")),
        P(),
        P(("wide", "narrow"), None),
        P(),
    )
    out_specs = (
        P("narrow", "wide"),
        P("wide", None, None),
        P(("wide", "narrow"), None, None),
        P(("wide", "narrow")),
        P(("wide", "narrow")),
    )
    return jax.shard_map(
        on_device, mesh=mesh, in_specs=in_specs, out_specs=out_specs, check_vma=False
    )
```

time: 539 us -> 322 us (0.60)
  blocking collectives: 286 us -> 38.3 us
  Pallas kernels: 0 us -> 141 us
  local copies, waits for them, and re-layouts: 82.7 us -> 13.4 us
  matrix products: 33.3 us -> 1.7 us
  waiting for transfers between devices: 69 us -> 100 us
  other arithmetic: 32.7 us -> 7.29 us
  between operations: 15.9 us -> 0.93 us
    all_gather x5 -> x0, blocking collectives: 180 us -> none  [the longest x1 112 us: on_device(): rows_all = lax.all_gather(hidden, 'wide', axis=0, tiled=True)]
    pallas_call x0 -> x3, Pallas kernels: none -> 141 us  [the longest x1 129 us: permute_pages(): pl.pallas_call(permute_kernel, out_shape=jax.ShapeDtypeStruct(pool.shape,...]
    all_to_all x3 -> x4, waiting for transfers between devices: 2.42 us -> 100 us  [the longest x1 88.4 us: on_device(): lax.all_to_all(ordered, 'wide', split_axis=0, concat_axis=0, tiled=True)]
    psum x1 -> x0, waiting for transfers between devices: 66.5 us -> none  [on_device(): lax.psum(part_sums.astype(jnp.bfloat16), 'wide').astype(jnp.float32)]
    all_to_all x0 -> x3, blocking collectives: none -> 38.3 us  [the longest x1 21.5 us: on_device(): lax.all_to_all(parts, ('narrow', 'wide'), split_axis=0, concat_axis=0, ti...]
    pmax x1 -> x0, blocking collectives: 37.7 us -> none  [on_device(): peak_all = lax.pmax(state[0], ('wide', 'narrow'))]
    psum x1 -> x0, blocking collectives: 35.4 us -> none  [on_device(): lax.psum(part_totals.astype(jnp.bfloat16), 'wide').astype(jnp.float32)]
    unnamed x3 -> x0, blocking collectives: 33.8 us -> none
  transfers between devices with their start and end apart: 5 -> 4, of which waited for: 3 -> 3; matrix products, arithmetic and copies ran while one was open for 5% -> 3% of each run, Pallas kernels for 0% -> 40%
where the time goes in v1:
time: 322 us
  Pallas kernels  141 us (44%)
  waiting for transfers between devices  100 us (31%)
  blocking collectives  38.3 us (12%)
  starting transfers between devices  18.9 us (6%)
  local copies, waits for them, and re-layouts  13.4 us (4%)
  other arithmetic  7.29 us (2%)
    pallas_call x1, Pallas kernels, permute_pages(): pl.pallas_call(permute_kernel, out_shape=jax.ShapeDtypeStruct(pool.shape,...  129 us
    all_to_all x1, waiting for transfers between devices, on_device(): lax.all_to_all(ordered, 'wide', split_axis=0, concat_axis=0, tiled=True)  88.4 us
    all_to_all x1, blocking collectives, on_device(): lax.all_to_all(parts, ('narrow', 'wide'), split_axis=0, concat_axis=0, ti...  21.5 us
    all_to_all x2, waiting for transfers between devices, spread(): lax.all_to_all(jnp.broadcast_to(block[None], (count,) + block.shape), axi...  11.7 us
    all_to_all x2, starting transfers between devices, spread(): lax.all_to_all(jnp.broadcast_to(block[None], (count,) + block.shape), axi...  10.7 us
    pallas_call x1, Pallas kernels, attend(): pl.pallas_call(functools.partial(attend_kernel, rows, piece), grid=(KVH,)...  9.84 us
    all_to_all x1, blocking collectives, spread(): lax.all_to_all(jnp.broadcast_to(block[None], (count,) + block.shape), axi...  9.81 us
    all_to_all x1, blocking collectives, on_device(): lax.all_to_all(sums, 'narrow', split_axis=0, concat_axis=0, tiled=True)  7.02 us
  transfers between devices with their start and end apart: 4, of which 3 were waited for; matrix products, arithmetic and copies ran while one was open for 3% of the time, Pallas kernels for 40%

profile of v1, /device:TPU:0, one launch (start us, length us, event | category | flops | bytes accessed | tf_op | source)
XLA Modules:
  0.0 321.6 jit_solution(5101073690565982423)
XLA Ops:
  0.6 0.0 copy-start
  0.7 1.5 broadcast_in_dim.90
  2.2 7.3 %all-to-all-start = ((bf16[8,5,1024]{2,1,0:T(8,128)(2,1)}), bf16[8,5,1024]{2,1,0:T(8,128)(2,1)S(1)}, u32[]{:S(2)}, u32[]{:S(2)}) async-start(bf16[8,5,1024]{2,1,0:T(8,128)(2,1)} %broadcast_in_dim.90), calls=%async_computation | async-start | bytes 262144 | tf_op jit(solution)/shard_map/all_to_all | solution.py:227
  9.4 0.9 convert_reduce_fusion
  10.3 0.7 multiply_add_fusion
  11.0 1.3 select_reduce_fusion.1
  12.3 0.1 add.95
  12.4 4.4 %all-to-all-done = bf16[8,5,1024]{2,1,0:T(8,128)(2,1)S(1)} async-done(((bf16[8,5,1024]{2,1,0:T(8,128)(2,1)}), bf16[8,5,1024]{2,1,0:T(8,128)(2,1)S(1)}, u32[]{:S(2)}, u32[]{:S(2)}) %all-to-all-start) | async-done | bytes 81952 | tf_op jit(solution)/shard_map/all_to_all | solution.py:227
  16.8 0.3 fusion.18
  17.1 1.1 fusion.19
  18.3 0.8 broadcast_in_dim.91
  19.1 3.5 %all-to-all-start.1 = ((f32[4,40,640]{2,1,0:T(8,128)}), f32[4,40,640]{2,1,0:T(8,128)S(1)}, u32[]{:S(2)}, u32[]{:S(2)}) async-start(f32[4,40,640]{2,1,0:T(8,128)} %broadcast_in_dim.91), calls=%async_computation.1 | async-start | bytes 819200 | tf_op jit(solution)/shard_map/all_to_all | solution.py:227
  22.6 0.1 concatenate.30
  22.7 0.1 fusion.10
  22.8 7.3 %all-to-all-done.1 = f32[4,40,640]{2,1,0:T(8,128)S(1)} async-done(((f32[4,40,640]{2,1,0:T(8,128)}), f32[4,40,640]{2,1,0:T(8,128)S(1)}, u32[]{:S(2)}, u32[]{:S(2)}) %all-to-all-start.1) | async-done | bytes 409632 | tf_op jit(solution)/shard_map/all_to_all | solution.py:227
  30.2 0.8 pad_maximum_fusion
  31.0 3.5 %all-to-all-start.2 = ((bf16[8,48,640]{2,1,0:T(8,128)(2,1)}), bf16[8,48,640]{2,1,0:T(8,128)(2,1)S(1)}, u32[]{:S(2)}, u32[]{:S(2)}) async-start(bf16[8,48,640]{2,1,0:T(8,128)(2,1)} %pad_maximum_fusion), calls=%async_computation.2 | async-start | bytes 983040 | tf_op jit(solution)/shard_map/all_to_all | solution.py:285
  34.5 0.1 iota_add_fusion
  34.6 0.7 add.101.pos_ref
  35.3 0.1 broadcast_in_dim.95
  35.4 0.7 reshape.151.req_ref
  36.1 0.1 broadcast_in_dim.96
  36.1 0.1 stack_reshape.3
  36.2 0.7 copy.39.row_ref
  36.9 129.0 %shard_map.155 = bf16[128,16,1024]{2,1,0:T(8,128)(2,1)} custom-call(s32[128]{0:T(128)} %get-tuple-element.11.source_ref, bf16[128,16,1024]{2,1,0:T(8,128)(2,1)} %pool_ref.1), custom_call_target="tpu_custom_call" | custom-call | bytes 8388608 | tf_op jit(solution)/shard_map/pallas_call | solution.py:39
  165.9 0.6 and_select_fusion.new_bias_ref
  166.6 0.8 pad.9.new_key_ref.new_value_ref
  167.4 0.0 copy-done.1
  167.4 9.8 %shard_map.156 = bf16[32,64,128]{2,1,0:T(8,128)(2,1)} custom-call(bf16[8,48,640]{2,1,0:T(8,128)(2,1)} %copy-done.1, bf16[2048,1024]{1,0:T(8,128)(2,1)} %bitcast.25, bf16[2048,1024]{1,0:T(8,128)(2,1)} %bitcast.26, bf16[128,1024]{1,0:T(8,128)(2,1)} %pad.9.new_key_ref.new_value_ref, bf16[128,1024]{1,0:T(8,128)(2,1)} %pad.9.new_key_ref.new_value_ref, ...), custom_call_target="tpu_custom_call" | custom-call | flops 1426063360 | bytes 4194304 | tf_op jit(solution)/shard_map/pallas_call | solution.py:157
  177.2 21.5 %all_to_all.35.parts_ref = bf16[32,64,128]{2,1,0:T(8,128)(2,1)} all-to-all(bf16[32,64,128]{2,1,0:T(8,128)(2,1)} %shard_map.156), channel_id=1, replica_groups=mesh['wide'=8,'narrow'=4] {'narrow','wide'}, dimensions={0} | all-to-all | bytes 1048576 | tf_op jit(solution)/shard_map/all_to_all | solution.py:323
  198.7 2.1 shard_map.157
  200.8 0.7 broadcast_in_dim.99
  201.5 9.8 %all_to_all.36 = bf16[8,40,128]{2,1,0:T(8,128)(2,1)S(1)} all-to-all(bf16[8,40,128]{2,1,0:T(8,128)(2,1)S(1)} %broadcast_in_dim.99), channel_id=1, replica_groups=mesh['wide'=8,'narrow'=4] {'wide'}, dimensions={0} | all-to-all | bytes 163840 | tf_op jit(solution)/shard_map/all_to_all | solution.py:227
  211.3 0.1 dot_general.13
  211.4 0.3 fusion
  211.7 7.0 %all_to_all.37 = f32[4,10,512]{2,1,0:T(8,128)S(1)} all-to-all(f32[4,10,512]{2,1,0:T(8,128)S(1)} %fusion), channel_id=1, replica_groups=mesh['wide'=8,'narrow'=4] {'narrow'}, dimensions={0} | all-to-all | bytes 163840 | tf_op jit(solution)/shard_map/all_to_all | solution.py:329
  218.7 4.7 %all-to-all-start.6 = ((bf16[128,16,1024]{2,1,0:T(8,128)(2,1)}), bf16[128,16,1024]{2,1,0:T(8,128)(2,1)}, u32[]{:S(2)}, u32[]{:S(2)}) async-start(bf16[128,16,1024]{2,1,0:T(8,128)(2,1)} %shard_map.155), calls=%async_computation.6 | async-start | bytes 8388608 | tf_op jit(solution)/shard_map/all_to_all | solution.py:288
  223.4 0.6 dynamic_slice.6
  224.0 0.6 iota_compare_fusion.4
  224.7 0.1 reshape_reshape.3
  224.8 0.7 slice_convert_fusion
  225.5 0.1 add_add_fusion
  225.6 0.6 reshape.152
  226.2 0.6 reshape.153
  226.8 0.7 dynamic-slice_select_fusion
  227.5 0.6 reduce_sum.59
  228.1 88.4 %all-to-all-done.6 = bf16[128,16,1024]{2,1,0:T(8,128)(2,1)} async-done(((bf16[128,16,1024]{2,1,0:T(8,128)(2,1)}), bf16[128,16,1024]{2,1,0:T(8,128)(2,1)}, u32[]{:S(2)}, u32[]{:S(2)}) %all-to-all-start.6) | async-done | bytes 4194336 | tf_op jit(solution)/shard_map/all_to_all | solution.py:288
  316.5 5.0 %copy.46 = bf16[128,16,1024]{2,1,0:T(8,128)(2,1)} copy(bf16[128,16,1024]{2,1,0:T(8,128)(2,1)} %all-to-all-done.6) | data formatting | bytes 8388608
  (32 shorter events, 0.3 us)
Async XLA Ops:
  0.6 16.2 %copy-start = (bf16[1024,512]{1,0:T(8,128)(2,1)S(1)}, bf16[1024,512]{1,0:T(8,128)(2,1)}, u32[]{:S(2)}) copy-start(bf16[1024,512]{1,0:T(8,128)(2,1)} %param.13) | copy-start | bytes 3145732
  0.6 35.6 %copy-start.7 = (s32[40,1]{0,1:T(1,128)S(1)}, s32[40,1]{0,1:T(1,128)}, u32[]{:S(2)}) copy-start(s32[40,1]{0,1:T(1,128)} %constant.65) | copy-start | bytes 484
  0.7 34.6 %copy-start.4 = (s32[128]{0:T(128)S(1)}, s32[128]{0:T(128)}, u32[]{:S(2)}) copy-start(s32[128]{0:T(128)} %param.17) | copy-start | bytes 1540
  0.7 33.8 %copy-start.6 = (s32[128]{0:T(128)S(1)}, s32[128]{0:T(128)}, u32[]{:S(2)}) copy-start(s32[128]{0:T(128)} %param.18) | copy-start | bytes 1540
  0.7 35.4 %copy-start.5 = (s32[8]{0:T(128)S(1)}, s32[8]{0:T(128)}, u32[]{:S(2)}) copy-start(s32[8]{0:T(128)} %param.19) | copy-start | bytes 100
  2.2 14.6 %all-to-all-start = ((bf16[8,5,1024]{2,1,0:T(8,128)(2,1)}), bf16[8,5,1024]{2,1,0:T(8,128)(2,1)S(1)}, u32[]{:S(2)}, u32[]{:S(2)}) async-start(bf16[8,5,1024]{2,1,0:T(8,128)(2,1)} %broadcast_in_dim.90), calls=%async_computation | async-start | bytes 262144 | tf_op jit(solution)/shard_map/all_to_all | solution.py:227
  19.1 11.1 %all-to-all-start.1 = ((f32[4,40,640]{2,1,0:T(8,128)}), f32[4,40,640]{2,1,0:T(8,128)S(1)}, u32[]{:S(2)}, u32[]{:S(2)}) async-start(f32[4,40,640]{2,1,0:T(8,128)} %broadcast_in_dim.91), calls=%async_computation.1 | async-start | bytes 819200 | tf_op jit(solution)/shard_map/all_to_all | solution.py:227
  31.0 135.5 %all-to-all-start.2 = ((bf16[8,48,640]{2,1,0:T(8,128)(2,1)}), bf16[8,48,640]{2,1,0:T(8,128)(2,1)S(1)}, u32[]{:S(2)}, u32[]{:S(2)}) async-start(bf16[8,48,640]{2,1,0:T(8,128)(2,1)} %pad_maximum_fusion), calls=%async_computation.2 | async-start | bytes 983040 | tf_op jit(solution)/shard_map/all_to_all | solution.py:285
  36.9 129.0 %copy-start.3 = (pred[40,128]{1,0:T(8,128)(4,1)S(1)}, pred[40,128]{1,0:T(8,128)(4,1)}, u32[]{:S(2)}) copy-start(pred[40,128]{1,0:T(8,128)(4,1)} %constant.58.clone) | copy-start | bytes 15364
  166.5 0.9 copy-start.1
  167.4 44.0 %copy-start.2 = (bf16[1024,512]{1,0:T(8,128)(2,1)S(1)}, bf16[1024,512]{1,0:T(8,128)(2,1)}, u32[]{:S(2)}) copy-start(bf16[1024,512]{1,0:T(8,128)(2,1)} %param.15) | copy-start | bytes 3145732
  218.7 4.7 %copy-start.8 = (s32[8]{0:T(128)S(1)}, s32[8]{0:T(128)}, u32[]{:S(2)}) copy-start(s32[8]{0:T(128)} %param.21) | copy-start | bytes 100
  218.7 97.8 %all-to-all-start.6 = ((bf16[128,16,1024]{2,1,0:T(8,128)(2,1)}), bf16[128,16,1024]{2,1,0:T(8,128)(2,1)}, u32[]{:S(2)}, u32[]{:S(2)}) async-start(bf16[128,16,1024]{2,1,0:T(8,128)(2,1)} %shard_map.155), calls=%async_computation.6 | async-start | bytes 8388608 | tf_op jit(solution)/shard_map/all_to_all | solution.py:288

commit v2 on v1

--- a/solution.py
+++ b/solution.py
@@ -26,29 +26,82 @@
     return -(-value // unit) * unit
 
 
-def permute_kernel(source_ref, pool_ref, out_ref, sem):
+def permute_kernel(source_ref, place_ref, pool_ref, out_ref, *refs):
+    chunk_refs, (pages_ref, in_sem, out_sem) = refs[:-3], refs[-3:]
+    count = chunk_refs[0].shape[0]
+
     def start(j, carry):
-        pltpu.make_async_copy(pool_ref.at[source_ref[j]], out_ref.at[j], sem).start()
+        pltpu.make_async_copy(pool_ref.at[source_ref[j]], pages_ref.at[j], in_sem).start()
         return carry
 
     lax.fori_loop(0, pool_ref.shape[0], start, 0)
-    pltpu.make_async_copy(pool_ref, out_ref, sem).wait()
-
-
-def permute_pages(source_of, pool):
+    pltpu.make_async_copy(pool_ref, pages_ref, in_sem).wait()
+    targets = [out_ref.at[pl.ds(place_ref[0] * count, count)], *chunk_refs]
+    copies = [
+        pltpu.make_async_copy(pages_ref.at[pl.ds(c * count, count)], target, out_sem.at[c])
+        for c, target in enumerate(targets)
+    ]
+    for copy in copies:
+        copy.start()
+    for copy in copies:
+        copy.wait()
+
+
+def permute_pages(source_of, place, pool, chunks):
+    part = jax.ShapeDtypeStruct((pool.shape[0] // chunks,) + pool.shape[1:], pool.dtype)
     return pl.pallas_call(
         permute_kernel,
-        out_shape=jax.ShapeDtypeStruct(pool.shape, pool.dtype),
+        out_shape=[jax.ShapeDtypeStruct(pool.shape, pool.dtype)] + [part] * (chunks - 1),
         in_specs=[
             pl.BlockSpec(memory_space=pltpu.SMEM),
+            pl.BlockSpec(memory_space=pltpu.SMEM),
             pl.BlockSpec(memory_space=pl.ANY),
         ],
-        out_specs=pl.BlockSpec(memory_space=pl.ANY),
-        scratch_shapes=[pltpu.SemaphoreType.DMA],
+        out_specs=[pl.BlockSpec(memory_space=pl.ANY)] * chunks,
+        scratch_shapes=[
+            pltpu.VMEM(pool.shape, pool.dtype),
+            pltpu.SemaphoreType.DMA,
+            pltpu.SemaphoreType.DMA((chunks,)),
+        ],
+        compiler_params=pltpu.CompilerParams(vmem_limit_bytes=VMEM),
         cost_estimate=pl.CostEstimate(
             flops=0, bytes_accessed=2 * pool.size * 2, transcendentals=0
         ),
-    )(source_of, pool)
+    )(source_of, place, pool)
+
+
+def place_kernel(place_ref, *refs):
+    in_refs, (out_ref, sem) = refs[:-3], refs[-2:]
+    copies = []
+    for i, chunk in enumerate(in_refs):
+        depth = chunk.shape[0]
+        copies.append(
+            pltpu.make_async_copy(
+                chunk, out_ref.at[pl.ds(place_ref[i] * depth, depth)], sem.at[i]
+            )
+        )
+    for copy in copies:
+        copy.start()
+    for copy in copies:
+        copy.wait()
+
+
+def place_pages(place, chunks, pages):
+    count = len(chunks)
+    return pl.pallas_call(
+        place_kernel,
+        out_shape=jax.ShapeDtypeStruct(pages.shape, pages.dtype),
+        in_specs=[pl.BlockSpec(memory_space=pltpu.SMEM)]
+        + [pl.BlockSpec(memory_space=pltpu.VMEM)] * count
+        + [pl.BlockSpec(memory_space=pl.ANY)],
+        out_specs=pl.BlockSpec(memory_space=pl.ANY),
+        scratch_shapes=[pltpu.SemaphoreType.DMA((count,))],
+        input_output_aliases={count + 1: 0},
+        compiler_params=pltpu.CompilerParams(vmem_limit_bytes=VMEM),
+        cost_estimate=pl.CostEstimate(
+            flops=0, bytes_accessed=4 * count * chunks[0].size, transcendentals=0
+        ),
+    )(place, *chunks, pages)
 
 
 def attend_kernel(
@@ -222,6 +275,10 @@
     )(parts)
 
 
+def group_of(d, wide):
+    return d if wide <= 8 else 1 + (d - 1) * 7 // (wide - 1)
+
+
 def spread(block, axis):
     count = lax.axis_size(axis)
     return lax.all_to_all(
@@ -250,10 +307,34 @@
     rank = jnp.sum((dest[:, None] == dest[None, :]) & (order[None, :] < order[:, None]), axis=1)
     target = dest * capacity + rank
     chosen = target[None, :] == order[:, None]
-    source_of = jnp.sum(jnp.where(chosen, order[None, :], 0), axis=1)
+    me = lax.axis_index("wide")
+    moved_to = (dest ^ me) * capacity + rank
+    source_of = jnp.sum(
+        jnp.where(moved_to[None, :] == order[:, None], order[None, :], 0), axis=1
+    )
     sent_req = jnp.sum(jnp.where(chosen, page_req[None, :], 0), axis=1)
     sent_idx = jnp.sum(jnp.where(chosen, page_idx[None, :], 0), axis=1)
-    ordered = permute_pages(source_of, pool)
+    moved_pool, *chunks = permute_pages(source_of, me.reshape(1), pool, wide)
+    arrived = {}
+
+    def beside(step, value, groups):
+        taken = [d for group in groups for d in range(1, wide) if group_of(d, wide) == group]
+        value, *sent = lax.optimization_barrier((value, *[chunks[d - 1] for d in taken]))
+        result = step(value)
+        got = [
+            lax.ppermute(chunk, "wide", [(w, w ^ d) for w in range(wide)])
+            for chunk, d in zip(sent, taken)
+        ]
+        result, *got = lax.optimization_barrier((result, *got))
+        arrived.update(zip(taken, got))
+        return result
+
+    def placed(pages):
+        taken = sorted(arrived)
+        place = jnp.stack([me ^ d for d in taken])
+        pages = place_pages(place, [arrived[d] for d in taken], pages)
+        arrived.clear()
+        return pages
 
     partial = jnp.concatenate(
         [
@@ -262,7 +343,8 @@
         ],
         axis=1,
     )
-    projected = jnp.sum(spread(partial, "narrow"), axis=0).astype(jnp.bfloat16)
+    partial = beside(lambda value: spread(value, "narrow"), partial, (1,))
+    projected = jnp.sum(partial, axis=0).astype(jnp.bfloat16)
     shifted = sent_idx + 1
     tags = jnp.concatenate(
         [
@@ -282,10 +364,9 @@
         ],
         axis=1,
     )
-    received = lax.all_to_all(packed, "wide", split_axis=0, concat_axis=0, tiled=True)
-
-    ordered, received = lax.optimization_barrier((ordered, received))
-    moved_pool = lax.all_to_all(ordered, "wide", split_axis=0, concat_axis=0, tiled=True)
+    exchange = functools.partial(lax.all_to_all, split_axis=0, concat_axis=0, tiled=True)
+    received = beside(lambda value: exchange(value, "wide"), packed, (4,))
+
     tags_in = received[:, rows, : 3 * capacity].astype(jnp.int32)
     moved_req = tags_in[:, :capacity].reshape(slots)
     moved_idx = (
@@ -309,25 +390,26 @@
         axis=1,
     )
     piece = HEADS * rows // (wide * narrow)
-    parts = attend(
+    new_keyval = jnp.pad(keyval, ((0, extra - rows), (0, 0)))
+    tokens = pool.reshape(slots * PAGE, -1)
+    parts = beside(
+        lambda value: attend(
+            value, new_keyval, tokens, req_tok, pos_tok, row_info, new_bias, rows, piece
+        ),
         received,
-        jnp.pad(keyval, ((0, extra - rows), (0, 0))),
-        pool.reshape(slots * PAGE, -1),
-        req_tok,
-        pos_tok,
-        row_info,
-        new_bias,
-        rows,
-        piece,
-    )
-    parts = lax.all_to_all(parts, ("narrow", "wide"), split_axis=0, concat_axis=0, tiled=True)
-    attn = spread(combine(parts, piece), "wide").reshape(-1, rows, HD)
+        (2,),
+    )
+    parts = beside(lambda value: exchange(value, ("narrow", "wide")), parts, (3, 5))
+    moved_pool = placed(moved_pool)
+    attn = beside(lambda value: spread(value, "wide"), combine(parts, piece), (6,))
+    attn = attn.reshape(-1, rows, HD)
     attn = jnp.transpose(attn, (1, 0, 2)).reshape(rows, -1)
     sums = jnp.dot(attn, w_out, preferred_element_type=jnp.float32)
     sums = sums.reshape(narrow, rows // narrow, -1)
-    attended = jnp.sum(
-        lax.all_to_all(sums, "narrow", split_axis=0, concat_axis=0, tiled=True), axis=0
-    ).astype(jnp.bfloat16)
+    sums = beside(lambda value: exchange(value, "narrow"), sums, (7,))
+    attended = jnp.sum(sums, axis=0).astype(jnp.bfloat16)
+
+    moved_pool = placed(moved_pool)
 
     local_req = local_rows // STEPS
     first_req = lax.axis_index("wide") * local_req

time: 322 us -> 184 us (0.57)
  the two profiles are of different devices: /device:TPU:0 before, /device:TPU:8 now
where the time goes in v2:
time: 184 us; the launch traced here: 183 us
  waiting for transfers between devices  94.4 us (51%)
  starting transfers between devices  45 us (24%)
  Pallas kernels  22.3 us (12%)
  local copies, waits for them, and re-layouts  11.3 us (6%)
  other arithmetic  8.08 us (4%)
    ppermute x7, waiting for transfers between devices, beside(): lax.ppermute(chunk, 'wide', [(w, w ^ d) for w in range(wide)])  72.6 us
    all_to_all x3, waiting for transfers between devices, spread(): lax.all_to_all(jnp.broadcast_to(block[None], (count,) + block.shape), axi...  21.7 us
    all_to_all x3, starting transfers between devices, spread(): lax.all_to_all(jnp.broadcast_to(block[None], (count,) + block.shape), axi...  17.3 us
    ppermute x7, starting transfers between devices, beside(): lax.ppermute(chunk, 'wide', [(w, w ^ d) for w in range(wide)])  13.5 us
    pallas_call x1, Pallas kernels, attend(): pl.pallas_call(functools.partial(attend_kernel, rows, piece), grid=(KVH,)...  9.85 us
    all_to_all x1, starting transfers between devices, on_device(): received = beside(lambda value: exchange(value, 'wide'), packed, (4,))  5.93 us
    pallas_call x2, Pallas kernels, place_pages(): pl.pallas_call(place_kernel, out_shape=jax.ShapeDtypeStruct(pages.shape,...  5.4 us
    pallas_call x1, Pallas kernels, permute_pages(): pl.pallas_call(permute_kernel, out_shape=[jax.ShapeDtypeStruct(pool.shape...  4.98 us
  transfers between devices with their start and end apart: 13, of which 7 were waited for; matrix products, arithmetic and copies ran while one was open for 8% of the time, Pallas kernels for 10%

profile of v2, /device:TPU:8, one launch (start us, length us, event | category | flops | bytes accessed | tf_op | source)
XLA Modules:
  0.0 183.4 jit_solution(13588003503081284691)
XLA Ops:
  0.7 1.5 broadcast_in_dim.50
  2.1 6.3 %all-to-all-start = ((bf16[8,5,1024]{2,1,0:T(8,128)(2,1)}), bf16[8,5,1024]{2,1,0:T(8,128)(2,1)S(1)}, u32[]{:S(2)}, u32[]{:S(2)}) async-start(bf16[8,5,1024]{2,1,0:T(8,128)(2,1)} %broadcast_in_dim.50), calls=%async_computation | async-start | bytes 262144 | tf_op jit(solution)/shard_map/all_to_all | solution.py:284
  8.4 0.9 convert_reduce_fusion
  9.3 0.7 multiply_add_fusion.1
  10.0 1.3 select_reduce_fusion.1
  11.3 5.0 %shard_map.155 = (bf16[128,16,1024]{2,1,0:T(8,128)(2,1)}, bf16[16,16,1024]{2,1,0:T(8,128)(2,1)}, bf16[16,16,1024]{2,1,0:T(8,128)(2,1)}, bf16[16,16,1024]{2,1,0:T...) custom-call(s32[128]{0:T(128)} %get-tuple-element.83.source_ref, ...), custom_call_target="tpu_custom_call" | custom-call | bytes 8388608 | tf_op jit(solution)/shard_map/pallas_call | solution.py:52
  16.9 1.5 collective-permute-start
  18.5 0.8 broadcast_in_dim.52
  19.3 3.5 %all-to-all-start.1 = ((f32[4,40,640]{2,1,0:T(8,128)}), f32[4,40,640]{2,1,0:T(8,128)S(1)}, u32[]{:S(2)}, u32[]{:S(2)}) async-start(f32[4,40,640]{2,1,0:T(8,128)} %broadcast_in_dim.52), calls=%async_computation.1 | async-start | bytes 819200 | tf_op jit(solution)/shard_map/all_to_all | solution.py:284
  23.0 7.3 %all-to-all-done.1 = f32[4,40,640]{2,1,0:T(8,128)S(1)} async-done(((f32[4,40,640]{2,1,0:T(8,128)}), f32[4,40,640]{2,1,0:T(8,128)S(1)}, u32[]{:S(2)}, u32[]{:S(2)}) %all-to-all-start.1) | async-done | bytes 409632 | tf_op jit(solution)/shard_map/all_to_all | solution.py:284
  30.4 0.9 pad_maximum_fusion
  31.4 5.9 %all-to-all-start.2 = ((bf16[8,48,640]{2,1,0:T(8,128)(2,1)}), bf16[8,48,640]{2,1,0:T(8,128)(2,1)S(1)}, u32[]{:S(2)}, u32[]{:S(2)}) async-start(bf16[8,48,640]{2,1,0:T(8,128)(2,1)} %pad_maximum_fusion), calls=%async_computation.2 | async-start | bytes 983040 | tf_op jit(solution)/shard_map/all_to_all | solution.py:368
  37.4 0.7 reshape.164.req_ref
  38.1 2.4 %collective-permute-start.1 = (bf16[16,16,1024]{2,1,0:T(8,128)(2,1)}, bf16[16,16,1024]{2,1,0:T(8,128)(2,1)S(1)}, u32[]{:S(2)}, u32[]{:S(2)}) collective-permute-start(bf16[16,16,1024]{2,1,0:T(8,128)(2,1)} %get-tuple-element.45), channel_id=1, source_target_pairs={{0,16},{4,20},{8,24},{12,28},{16,0},{20,4},{24,8},{28,12},{1,17},{... | collective-permute-start | bytes 1572872 | tf_op jit(solution)/shard_map/ppermute | solution.py:325
  40.5 0.7 add.109.pos_ref
  41.4 0.7 copy.41.row_ref
  42.1 26.9 %collective-permute-done.1.refs_3_ = bf16[16,16,1024]{2,1,0:T(8,128)(2,1)S(1)} collective-permute-done((bf16[16,16,1024]{2,1,0:T(8,128)(2,1)}, bf16[16,16,1024]{2,1,0:T(8,128)(2,1)S(1)}, u32[]{:S(2)}, u32[]{:S(2)}) %collective-permute-start.1) | collective-permute-done | bytes 524320 | tf_op jit(solution)/shard_map/ppermute | solution.py:325
  69.0 3.6 %collective-permute-start.2 = (bf16[16,16,1024]{2,1,0:T(8,128)(2,1)}, bf16[16,16,1024]{2,1,0:T(8,128)(2,1)S(1)}, u32[]{:S(2)}, u32[]{:S(2)}) collective-permute-start(bf16[16,16,1024]{2,1,0:T(8,128)(2,1)} %get-tuple-element.49), channel_id=1, source_target_pairs={{0,8},{4,12},{8,0},{12,4},{16,24},{20,28},{24,16},{28,20},{1,9},{5... | collective-permute-start | bytes 1572872 | tf_op jit(solution)/shard_map/ppermute | solution.py:325
  72.6 0.6 and_select_fusion.new_bias_ref
  73.2 0.7 pad.9.new_key_ref.new_value_ref
  74.0 9.8 %shard_map.156 = bf16[32,64,128]{2,1,0:T(8,128)(2,1)} custom-call(bf16[8,48,640]{2,1,0:T(8,128)(2,1)} %copy-done.1, bf16[2048,1024]{1,0:T(8,128)(2,1)} %bitcast.34, bf16[2048,1024]{1,0:T(8,128)(2,1)} %bitcast.35, bf16[128,1024]{1,0:T(8,128)(2,1)} %pad.9.new_key_ref.new_value_ref, bf16[128,1024]{1,0:T(8,128)(2,1)} %pad.9.new_key_ref.new_value_ref, ...), custom_call_target="tpu_custom_call" | custom-call | flops 1426063360 | bytes 4194304 | tf_op jit(solution)/shard_map/pallas_call | solution.py:210
  83.8 0.8 copy-done.6
  84.6 4.9 %all-to-all-start.3 = ((bf16[32,64,128]{2,1,0:T(8,128)(2,1)}), bf16[32,64,128]{2,1,0:T(8,128)(2,1)S(1)}, u32[]{:S(2)}, u32[]{:S(2)}) async-start(bf16[32,64,128]{2,1,0:T(8,128)(2,1)} %shard_map.156), calls=%async_computation.3 | async-start | bytes 1048576 | tf_op jit(solution)/shard_map/all_to_all | solution.py:402
  89.6 1.5 collective-permute-start.3
  91.1 2.4 %collective-permute-start.4 = (bf16[16,16,1024]{2,1,0:T(8,128)(2,1)}, bf16[16,16,1024]{2,1,0:T(8,128)(2,1)}, u32[]{:S(2)}, u32[]{:S(2)}) collective-permute-start(bf16[16,16,1024]{2,1,0:T(8,128)(2,1)} %get-tuple-element.55), channel_id=1, source_target_pairs={{0,20},{4,16},{8,28},{12,24},{16,4},{20,0},{24,12},{28,8},{1,21},{... | collective-permute-start | bytes 1572872 | tf_op jit(solution)/shard_map/ppermute | solution.py:325
  93.5 26.3 %collective-permute-done.3.refs_2_ = bf16[16,16,1024]{2,1,0:T(8,128)(2,1)S(1)} collective-permute-done((bf16[16,16,1024]{2,1,0:T(8,128)(2,1)}, bf16[16,16,1024]{2,1,0:T(8,128)(2,1)S(1)}, u32[]{:S(2)}, u32[]{:S(2)}) %collective-permute-start.3) | collective-permute-done | bytes 524320 | tf_op jit(solution)/shard_map/ppermute | solution.py:325
  119.8 5.5 %collective-permute-done.4.refs_4_ = bf16[16,16,1024]{2,1,0:T(8,128)(2,1)} collective-permute-done((bf16[16,16,1024]{2,1,0:T(8,128)(2,1)}, bf16[16,16,1024]{2,1,0:T(8,128)(2,1)}, u32[]{:S(2)}, u32[]{:S(2)}) %collective-permute-start.4) | collective-permute-done | bytes 524320 | tf_op jit(solution)/shard_map/ppermute | solution.py:325
  125.3 0.8 copy-done.2
  126.1 2.1 %shard_map.157 = bf16[40,128]{1,0:T(8,128)(2,1)} custom-call(bf16[32,64,128]{2,1,0:T(8,128)(2,1)} %copy-done.2), custom_call_target="tpu_custom_call" | custom-call | flops 524288 | bytes 524288 | tf_op jit(solution)/shard_map/pallas_call | solution.py:266
  128.2 0.8 collective-permute-start.5
  128.9 0.6 dynamic_slice.6
  129.5 1.3 broadcast_in_dim.101
  130.9 7.6 %all-to-all-start.4 = ((bf16[8,40,128]{2,1,0:T(8,128)(2,1)}), bf16[8,40,128]{2,1,0:T(8,128)(2,1)S(1)}, u32[]{:S(2)}, u32[]{:S(2)}) async-start(bf16[8,40,128]{2,1,0:T(8,128)(2,1)} %broadcast_in_dim.101), calls=%async_computation.4 | async-start | bytes 163840 | tf_op jit(solution)/shard_map/all_to_all | solution.py:284
  138.5 0.6 iota_compare_fusion.5
  139.1 0.6 stack.43.place_ref
  139.7 0.7 pad_add_fusion.1.place_ref
  140.5 14.3 %all-to-all-done.4 = bf16[8,40,128]{2,1,0:T(8,128)(2,1)S(1)} async-done(((bf16[8,40,128]{2,1,0:T(8,128)(2,1)}), bf16[8,40,128]{2,1,0:T(8,128)(2,1)S(1)}, u32[]{:S(2)}, u32[]{:S(2)}) %all-to-all-start.4) | async-done | bytes 81952 | tf_op jit(solution)/shard_map/all_to_all | solution.py:284
  154.9 1.0 fusion
  155.9 1.3 collective-permute-start.6
  157.2 0.7 dynamic-slice_select_fusion
  157.9 0.7 slice_convert_fusion
  158.6 3.3 %all-to-all-start.5 = ((f32[4,10,512]{2,1,0:T(8,128)}), f32[4,10,512]{2,1,0:T(8,128)S(1)}, u32[]{:S(2)}, u32[]{:S(2)}) async-start(f32[4,10,512]{2,1,0:T(8,128)} %fusion), calls=%async_computation.5 | async-start | bytes 262144 | tf_op jit(solution)/shard_map/all_to_all | solution.py:409
  162.0 0.6 reshape.165
  162.6 0.6 reshape.166
  163.2 3.2 %shard_map.158.refs_2_ = bf16[128,16,1024]{2,1,0:T(8,128)(2,1)} custom-call(s32[5]{0:T(128)} %stack.43.place_ref, bf16[16,16,1024]{2,1,0:T(8,128)(2,1)} %copy-done.4, bf16[16,16,1024]{2,1,0:T(8,128)(2,1)} %copy-done.6, bf16[16,16,1024]{2,1,0:T(8,128)(2,1)} %copy-done.7, bf16[16,16,1024]{2,1,0:T(8,128)(2,1)} %copy-done.5, ...), custom_call_target="tpu_custom_call", output_to_operand_aliasing={{}: (6, {})} | custom-call | bytes 5242880 | tf_op jit(solution)/shard_map/pallas_call | solution.py:91
  166.5 13.9 %collective-permute-done.6.refs_1_ = bf16[16,16,1024]{2,1,0:T(8,128)(2,1)S(1)} collective-permute-done((bf16[16,16,1024]{2,1,0:T(8,128)(2,1)}, bf16[16,16,1024]{2,1,0:T(8,128)(2,1)S(1)}, u32[]{:S(2)}, u32[]{:S(2)}) %collective-permute-start.6) | collective-permute-done | bytes 524320 | tf_op jit(solution)/shard_map/ppermute | solution.py:325
  180.4 0.7 reduce_sum.59
  181.2 2.2 %shard_map.159 = bf16[128,16,1024]{2,1,0:T(8,128)(2,1)} custom-call(s32[2]{0:T(128)} %pad_add_fusion.1.place_ref, bf16[16,16,1024]{2,1,0:T(8,128)(2,1)} %copy-done.8, bf16[16,16,1024]{2,1,0:T(8,128)(2,1)} %copy-done.9, bf16[128,16,1024]{2,1,0:T(8,128)(2,1)} %shard_map.158.refs_2_), custom_call_target="tpu_custom_call", output_to_operand_aliasing={{}: (3, {})} | custom-call | bytes 2097152 | tf_op jit(solution)/shard_map/pallas_call | solution.py:91
  (66 shorter events, 1.8 us)
Async XLA Ops:
  0.6 16.0 %copy-start = (bf16[1024,512]{1,0:T(8,128)(2,1)S(1)}, bf16[1024,512]{1,0:T(8,128)(2,1)}, u32[]{:S(2)}) copy-start(bf16[1024,512]{1,0:T(8,128)(2,1)} %param.13) | copy-start | bytes 3145732
  0.6 15.8 %copy-start.10 = (bf16[1024,128]{1,0:T(8,128)(2,1)S(1)}, bf16[1024,128]{1,0:T(8,128)(2,1)}, u32[]{:S(2)}) copy-start(bf16[1024,128]{1,0:T(8,128)(2,1)} %param.14) | copy-start | bytes 786436
  2.1 14.2 %all-to-all-start = ((bf16[8,5,1024]{2,1,0:T(8,128)(2,1)}), bf16[8,5,1024]{2,1,0:T(8,128)(2,1)S(1)}, u32[]{:S(2)}, u32[]{:S(2)}) async-start(bf16[8,5,1024]{2,1,0:T(8,128)(2,1)} %broadcast_in_dim.50), calls=%async_computation | async-start | bytes 262144 | tf_op jit(solution)/shard_map/all_to_all | solution.py:284
  16.3 21.0 %copy-start.12 = (s32[128]{0:T(128)S(1)}, s32[128]{0:T(128)}, u32[]{:S(2)}) copy-start(s32[128]{0:T(128)} %param.17) | copy-start | bytes 1540
  16.3 24.1 %copy-start.13 = (s32[128]{0:T(128)S(1)}, s32[128]{0:T(128)}, u32[]{:S(2)}) copy-start(s32[128]{0:T(128)} %param.18) | copy-start | bytes 1540
  16.3 24.9 %copy-start.14 = (s32[8]{0:T(128)S(1)}, s32[8]{0:T(128)}, u32[]{:S(2)}) copy-start(s32[8]{0:T(128)} %param.19) | copy-start | bytes 100
  16.3 25.0 %copy-start.15 = (s32[40,1]{0,1:T(1,128)S(1)}, s32[40,1]{0,1:T(1,128)}, u32[]{:S(2)}) copy-start(s32[40,1]{0,1:T(1,128)} %constant.77) | copy-start | bytes 484
  16.4 56.2 %copy-start.11 = (pred[40,128]{1,0:T(8,128)(4,1)S(1)}, pred[40,128]{1,0:T(8,128)(4,1)}, u32[]{:S(2)}) copy-start(pred[40,128]{1,0:T(8,128)(4,1)} %constant.70.clone) | copy-start | bytes 15364
  16.9 13.4 %collective-permute-start = (bf16[16,16,1024]{2,1,0:T(8,128)(2,1)}, bf16[16,16,1024]{2,1,0:T(8,128)(2,1)S(1)}, u32[]{:S(2)}, u32[]{:S(2)}) collective-permute-start(bf16[16,16,1024]{2,1,0:T(8,128)(2,1)} %get-tuple-element.41), channel_id=1, source_target_pairs={{0,4},{4,0},{8,12},{12,8},{16,20},{20,16},{24,28},{28,24},{1,5},{5... | collective-permute-start | bytes 1572872 | tf_op jit(solution)/shard_map/ppermute | solution.py:325
  19.3 11.1 %all-to-all-start.1 = ((f32[4,40,640]{2,1,0:T(8,128)}), f32[4,40,640]{2,1,0:T(8,128)S(1)}, u32[]{:S(2)}, u32[]{:S(2)}) async-start(f32[4,40,640]{2,1,0:T(8,128)} %broadcast_in_dim.52), calls=%async_computation.1 | async-start | bytes 819200 | tf_op jit(solution)/shard_map/all_to_all | solution.py:284
  30.4 53.4 %copy-start.4 = (bf16[16,16,1024]{2,1,0:T(8,128)(2,1)}, bf16[16,16,1024]{2,1,0:T(8,128)(2,1)S(1)}, u32[]{:S(2)}) copy-start(bf16[16,16,1024]{2,1,0:T(8,128)(2,1)S(1)} %collective-permute-done.refs_0_) | copy-start | bytes 1572868
  31.4 37.6 %all-to-all-start.2 = ((bf16[8,48,640]{2,1,0:T(8,128)(2,1)}), bf16[8,48,640]{2,1,0:T(8,128)(2,1)S(1)}, u32[]{:S(2)}, u32[]{:S(2)}) async-start(bf16[8,48,640]{2,1,0:T(8,128)(2,1)} %pad_maximum_fusion), calls=%async_computation.2 | async-start | bytes 983040 | tf_op jit(solution)/shard_map/all_to_all | solution.py:368
  38.1 30.9 %collective-permute-start.1 = (bf16[16,16,1024]{2,1,0:T(8,128)(2,1)}, bf16[16,16,1024]{2,1,0:T(8,128)(2,1)S(1)}, u32[]{:S(2)}, u32[]{:S(2)}) collective-permute-start(bf16[16,16,1024]{2,1,0:T(8,128)(2,1)} %get-tuple-element.45), channel_id=1, source_target_pairs={{0,16},{4,20},{8,24},{12,28},{16,0},{20,4},{24,8},{28,12},{1,17},{... | collective-permute-start | bytes 1572872 | tf_op jit(solution)/shard_map/ppermute | solution.py:325
  69.0 5.0 %copy-start.5 = (bf16[16,16,1024]{2,1,0:T(8,128)(2,1)}, bf16[16,16,1024]{2,1,0:T(8,128)(2,1)S(1)}, u32[]{:S(2)}) copy-start(bf16[16,16,1024]{2,1,0:T(8,128)(2,1)S(1)} %collective-permute-done.1.refs_3_) | copy-start | bytes 1572868
  69.0 5.0 %copy-start.1 = (bf16[8,48,640]{2,1,0:T(8,128)(2,1)}, bf16[8,48,640]{2,1,0:T(8,128)(2,1)S(1)}, u32[]{:S(2)}) copy-start(bf16[8,48,640]{2,1,0:T(8,128)(2,1)S(1)} %all-to-all-done.2.query_ref) | copy-start | bytes 1474564
  69.0 14.9 %collective-permute-start.2 = (bf16[16,16,1024]{2,1,0:T(8,128)(2,1)}, bf16[16,16,1024]{2,1,0:T(8,128)(2,1)S(1)}, u32[]{:S(2)}, u32[]{:S(2)}) collective-permute-start(bf16[16,16,1024]{2,1,0:T(8,128)(2,1)} %get-tuple-element.49), channel_id=1, source_target_pairs={{0,8},{4,12},{8,0},{12,4},{16,24},{20,28},{24,16},{28,20},{1,9},{5... | collective-permute-start | bytes 1572872 | tf_op jit(solution)/shard_map/ppermute | solution.py:325
  74.0 55.0 %copy-start.16 = (s32[8]{0:T(128)S(1)}, s32[8]{0:T(128)}, u32[]{:S(2)}) copy-start(s32[8]{0:T(128)} %param.21) | copy-start | bytes 100
  74.0 81.0 %copy-start.3 = (bf16[1024,512]{1,0:T(8,128)(2,1)S(1)}, bf16[1024,512]{1,0:T(8,128)(2,1)}, u32[]{:S(2)}) copy-start(bf16[1024,512]{1,0:T(8,128)(2,1)} %param.15) | copy-start | bytes 3145732
  83.8 0.8 copy-start.6
  84.6 40.6 %all-to-all-start.3 = ((bf16[32,64,128]{2,1,0:T(8,128)(2,1)}), bf16[32,64,128]{2,1,0:T(8,128)(2,1)S(1)}, u32[]{:S(2)}, u32[]{:S(2)}) async-start(bf16[32,64,128]{2,1,0:T(8,128)(2,1)} %shard_map.156), calls=%async_computation.3 | async-start | bytes 1048576 | tf_op jit(solution)/shard_map/all_to_all | solution.py:402
  89.6 30.2 %collective-permute-start.3 = (bf16[16,16,1024]{2,1,0:T(8,128)(2,1)}, bf16[16,16,1024]{2,1,0:T(8,128)(2,1)S(1)}, u32[]{:S(2)}, u32[]{:S(2)}) collective-permute-start(bf16[16,16,1024]{2,1,0:T(8,128)(2,1)} %get-tuple-element.54), channel_id=1, source_target_pairs={{0,12},{4,8},{8,4},{12,0},{16,28},{20,24},{24,20},{28,16},{1,13},{... | collective-permute-start | bytes 1572872 | tf_op jit(solution)/shard_map/ppermute | solution.py:325
  91.1 34.2 %collective-permute-start.4 = (bf16[16,16,1024]{2,1,0:T(8,128)(2,1)}, bf16[16,16,1024]{2,1,0:T(8,128)(2,1)}, u32[]{:S(2)}, u32[]{:S(2)}) collective-permute-start(bf16[16,16,1024]{2,1,0:T(8,128)(2,1)} %get-tuple-element.55), channel_id=1, source_target_pairs={{0,20},{4,16},{8,28},{12,24},{16,4},{20,0},{24,12},{28,8},{1,21},{... | collective-permute-start | bytes 1572872 | tf_op jit(solution)/shard_map/ppermute | solution.py:325
  119.8 43.4 %copy-start.7 = (bf16[16,16,1024]{2,1,0:T(8,128)(2,1)}, bf16[16,16,1024]{2,1,0:T(8,128)(2,1)S(1)}, u32[]{:S(2)}) copy-start(bf16[16,16,1024]{2,1,0:T(8,128)(2,1)S(1)} %collective-permute-done.3.refs_2_) | copy-start | bytes 1572868
  125.3 0.8 copy-start.2
  128.2 26.7 %collective-permute-start.5 = (bf16[16,16,1024]{2,1,0:T(8,128)(2,1)}, bf16[16,16,1024]{2,1,0:T(8,128)(2,1)S(1)}, u32[]{:S(2)}, u32[]{:S(2)}) collective-permute-start(bf16[16,16,1024]{2,1,0:T(8,128)(2,1)} %get-tuple-element.59), channel_id=1, source_target_pairs={{0,24},{4,28},{8,16},{12,20},{16,8},{20,12},{24,0},{28,4},{1,25},{... | collective-permute-start | bytes 1572872 | tf_op jit(solution)/shard_map/ppermute | solution.py:325
  130.9 24.0 %all-to-all-start.4 = ((bf16[8,40,128]{2,1,0:T(8,128)(2,1)}), bf16[8,40,128]{2,1,0:T(8,128)(2,1)S(1)}, u32[]{:S(2)}, u32[]{:S(2)}) async-start(bf16[8,40,128]{2,1,0:T(8,128)(2,1)} %broadcast_in_dim.101), calls=%async_computation.4 | async-start | bytes 163840 | tf_op jit(solution)/shard_map/all_to_all | solution.py:284
  154.9 11.5 %copy-start.8 = (bf16[16,16,1024]{2,1,0:T(8,128)(2,1)}, bf16[16,16,1024]{2,1,0:T(8,128)(2,1)S(1)}, u32[]{:S(2)}) copy-start(bf16[16,16,1024]{2,1,0:T(8,128)(2,1)S(1)} %collective-permute-done.5.refs_0_) | copy-start | bytes 1572868
  155.9 24.5 %collective-permute-start.6 = (bf16[16,16,1024]{2,1,0:T(8,128)(2,1)}, bf16[16,16,1024]{2,1,0:T(8,128)(2,1)S(1)}, u32[]{:S(2)}, u32[]{:S(2)}) collective-permute-start(bf16[16,16,1024]{2,1,0:T(8,128)(2,1)} %get-tuple-element.63), channel_id=1, source_target_pairs={{0,28},{4,24},{8,20},{12,16},{16,12},{20,8},{24,4},{28,0},{1,29},{... | collective-permute-start | bytes 1572872 | tf_op jit(solution)/shard_map/ppermute | solution.py:325
  158.6 7.9 %all-to-all-start.5 = ((f32[4,10,512]{2,1,0:T(8,128)}), f32[4,10,512]{2,1,0:T(8,128)S(1)}, u32[]{:S(2)}, u32[]{:S(2)}) async-start(f32[4,10,512]{2,1,0:T(8,128)} %fusion), calls=%async_computation.5 | async-start | bytes 262144 | tf_op jit(solution)/shard_map/all_to_all | solution.py:409
  180.4 0.8 copy-start.9

commit v3 on v2

--- a/solution.py
+++ b/solution.py
@@ -18,7 +18,7 @@
 NEG_FILL = -1e30
 SCALE2 = math.log2(math.e) / math.sqrt(HD)
 STAT = 16
-VMEM = 56 * 1024 * 1024
+MIB = 1024 * 1024
 NT = (((1,), (1,)), ((), ()))
 
 
@@ -63,7 +63,7 @@
             pltpu.SemaphoreType.DMA,
             pltpu.SemaphoreType.DMA((chunks,)),
         ],
-        compiler_params=pltpu.CompilerParams(vmem_limit_bytes=VMEM),
+        compiler_params=pltpu.CompilerParams(vmem_limit_bytes=2 * pool.size + 2 * MIB),
         cost_estimate=pl.CostEstimate(
             flops=0, bytes_accessed=2 * pool.size * 2, transcendentals=0
         ),
@@ -97,11 +97,21 @@
         out_specs=pl.BlockSpec(memory_space=pl.ANY),
         scratch_shapes=[pltpu.SemaphoreType.DMA((count,))],
         input_output_aliases={count + 1: 0},
-        compiler_params=pltpu.CompilerParams(vmem_limit_bytes=VMEM),
+        compiler_params=pltpu.CompilerParams(vmem_limit_bytes=2 * count * chunks[0].size + 2 * MIB),
         cost_estimate=pl.CostEstimate(
             flops=0, bytes_accessed=4 * count * chunks[0].size, transcendentals=0
         ),
     )(place, *chunks, pages)
+
+
+def cut(value):
+    return value.astype(jnp.bfloat16).astype(jnp.float32)
+
+
+def split_stats(peak, total):
+    high = cut(peak)
+    mid = cut(peak - high)
+    return high, mid, peak - high - mid, cut(total), total - cut(total)
 
 
 def attend_kernel(
@@ -122,20 +132,13 @@
     weight_ref,
 ):
     tokens = key_ref.shape[0]
-    per_block = GROUPS // query_ref.shape[0]
 
     @pl.when(pl.program_id(0) == 0)
     def _():
         seen = (req_ref[...] == row_ref[:, 0:1]) & (pos_ref[...] < row_ref[:, 1:2])
         bias_ref[...] = jnp.where(seen, 0.0, NEG_FILL)
 
-    query = jnp.concatenate(
-        [
-            query_ref[g // per_block, :rows, pl.ds((g % per_block) * HD, HD)].astype(jnp.float32)
-            for g in range(GROUPS)
-        ],
-        axis=0,
-    ).astype(jnp.bfloat16)
+    query = query_ref[0]
     score_ref[:, :tokens] = lax.dot_general(
         query, key_ref[...], NT, preferred_element_type=jnp.float32
     )
@@ -168,17 +171,9 @@
     peak = jnp.concatenate(peaks, axis=0)
     total = jnp.concatenate(totals, axis=0)
 
-    def cut(value):
-        return value.astype(jnp.bfloat16).astype(jnp.float32)
-
-    peak_high = cut(peak)
-    peak_mid = cut(peak - peak_high)
-    peak_low = peak - peak_high - peak_mid
-    total_high = cut(total)
-    total_low = total - total_high
     lane = lax.broadcasted_iota(jnp.int32, (GROUPS * rows, HD), 1)
     stats = jnp.zeros((GROUPS * rows, HD), jnp.float32)
-    for i, part in enumerate((peak_high, peak_mid, peak_low, total_high, total_low)):
+    for i, part in enumerate(split_stats(peak, total)):
         stats = jnp.where(lane == i, part, stats)
     pick = (
         lax.broadcasted_iota(jnp.int32, (STAT, HD), 0)
@@ -203,7 +198,6 @@
 def attend(queries, keyval, pool, req_tok, pos_tok, row_info, new_bias, rows, piece):
     tokens = pool.shape[0]
     extra = keyval.shape[0]
-    blocks = queries.shape[0] // KVH
     pieces = GROUPS * rows // piece
     height = STAT + up(piece, 16)
     whole = lambda shape: pl.BlockSpec(shape, lambda k: (0,) * len(shape))
@@ -212,7 +206,7 @@
         grid=(KVH,),
         out_shape=jax.ShapeDtypeStruct((KVH * pieces, height, HD), jnp.bfloat16),
         in_specs=[
-            pl.BlockSpec((blocks,) + queries.shape[1:], lambda k: (k, 0, 0)),
+            pl.BlockSpec((1,) + queries.shape[1:], lambda k: (k, 0, 0)),
             pl.BlockSpec((tokens, HD), lambda k: (0, k)),
             pl.BlockSpec((tokens, HD), lambda k: (0, KVH + k)),
             pl.BlockSpec((extra, HD), lambda k: (0, k)),
@@ -228,7 +222,7 @@
             pltpu.VMEM((GROUPS * rows, tokens + extra), jnp.float32),
             pltpu.VMEM((GROUPS * rows, tokens + extra), jnp.bfloat16),
         ],
-        compiler_params=pltpu.CompilerParams(vmem_limit_bytes=VMEM),
+        compiler_params=pltpu.CompilerParams(vmem_limit_bytes=32 * MIB),
         cost_estimate=pl.CostEstimate(
             flops=4 * HEADS * rows * (tokens + extra) * HD,
             bytes_accessed=pool.size * 2,
@@ -237,38 +231,50 @@
     )(queries, pool, pool, keyval, keyval, req_tok, pos_tok, row_info, new_bias)
 
 
-def combine_kernel(piece, parts_ref, out_ref):
-    count = parts_ref.shape[0]
+def combine_kernel(piece, last, parts_ref, out_ref):
+    count, groups, height = parts_ref.shape[:3]
     peaks, totals = [], []
     for i in range(count):
-        stat = parts_ref[i, :STAT, :].astype(jnp.float32)
-        peaks.append(stat[0:1] + stat[1:2] + stat[2:3])
-        totals.append(stat[3:4] + stat[4:5])
-    peak = jnp.concatenate(peaks, axis=0)
-    total = jnp.concatenate(totals, axis=0)
-    lead = jnp.exp2(peak - jnp.max(peak, axis=0, keepdims=True))
-    whole = jnp.sum(lead * total, axis=0, keepdims=True)
-    lane = lax.broadcasted_iota(jnp.int32, whole.shape, 1)
-    share = lead / jnp.where(lane < piece, whole, 1.0)
-    if count % HD:
-        share = jnp.concatenate(
-            [share, jnp.zeros((up(count, HD) - count, HD), jnp.float32)], axis=0
-        )
-    share = jnp.transpose(share)
-    height = parts_ref.shape[1] - STAT
-    result = jnp.zeros((height, HD), jnp.float32)
-    for i in range(count):
-        result = result + share[:height, i : i + 1] * parts_ref[i, STAT:, :].astype(jnp.float32)
-    out_ref[...] = result[:piece].astype(jnp.bfloat16)
-
-
-def combine(parts, piece):
+        for j in range(groups):
+            stat = parts_ref[i, j, :STAT, :].astype(jnp.float32)
+            peaks.append(stat[0:1] + stat[1:2] + stat[2:3])
+            totals.append(stat[3:4] + stat[4:5])
+    peak = jnp.concatenate(peaks, axis=0).reshape(count, groups, HD)
+    total = jnp.concatenate(totals, axis=0).reshape(count, groups, HD)
+    top = jnp.max(peak, axis=0)
+    lead = jnp.exp2(peak - top[None])
+    whole = jnp.sum(lead * total, axis=0)
+    if last:
+        lane = lax.broadcasted_iota(jnp.int32, whole.shape, 1)
+        lead = lead / jnp.where(lane < piece, whole, 1.0)[None]
+    lead = lead.reshape(count * groups, HD)
+    if (count * groups) % HD:
+        fill = up(count * groups, HD) - count * groups
+        lead = jnp.concatenate([lead, jnp.zeros((fill, HD), jnp.float32)], axis=0)
+    lead = jnp.transpose(lead)
+    rows = height - STAT
+    for j in range(groups):
+        result = jnp.zeros((rows, HD), jnp.float32)
+        for i in range(count):
+            c = i * groups + j
+            result = result + lead[:rows, c : c + 1] * parts_ref[i, j, STAT:, :].astype(jnp.float32)
+        if last:
+            out_ref[...] = result[:piece].astype(jnp.bfloat16)
+        else:
+            stats = split_stats(top[j : j + 1], whole[j : j + 1])
+            rest = jnp.zeros((STAT - len(stats), HD), jnp.float32)
+            out_ref[j] = jnp.concatenate([*stats, rest, result], axis=0).astype(jnp.bfloat16)
+
+
+def combine(parts, piece, last):
+    groups, height = parts.shape[1:3]
+    shape = (piece, HD) if last else (groups, height, HD)
     return pl.pallas_call(
-        functools.partial(combine_kernel, piece),
-        out_shape=jax.ShapeDtypeStruct((piece, HD), jnp.bfloat16),
+        functools.partial(combine_kernel, piece, last),
+        out_shape=jax.ShapeDtypeStruct(shape, jnp.bfloat16),
         in_specs=[pl.BlockSpec(memory_space=pltpu.VMEM)],
         out_specs=pl.BlockSpec(memory_space=pltpu.VMEM),
-        compiler_params=pltpu.CompilerParams(vmem_limit_bytes=VMEM),
+        compiler_params=pltpu.CompilerParams(vmem_limit_bytes=8 * MIB),
         cost_estimate=pl.CostEstimate(
             flops=2 * parts.size, bytes_accessed=parts.size * 2, transcendentals=0
         ),
@@ -298,7 +304,6 @@
     requests = rows // STEPS
     slots = pool.shape[0]
     capacity = slots // wide
-    query_cols = w_query.shape[1]
 
     gathered = spread(hidden, "wide").reshape(rows, -1)
 
@@ -317,15 +322,17 @@
     moved_pool, *chunks = permute_pages(source_of, me.reshape(1), pool, wide)
     arrived = {}
 
-    def beside(step, value, groups):
-        taken = [d for group in groups for d in range(1, wide) if group_of(d, wide) == group]
+    exchange = functools.partial(lax.all_to_all, split_axis=0, concat_axis=0, tiled=True)
+    flying = {}
+
+    def beside(step, value, begin=(), end=()):
+        taken = [d for d in range(1, wide) if group_of(d, wide) in begin]
         value, *sent = lax.optimization_barrier((value, *[chunks[d - 1] for d in taken]))
         result = step(value)
-        got = [
-            lax.ppermute(chunk, "wide", [(w, w ^ d) for w in range(wide)])
-            for chunk, d in zip(sent, taken)
-        ]
-        result, *got = lax.optimization_barrier((result, *got))
+        for d, chunk in zip(taken, sent):
+            flying[d] = lax.ppermute(chunk, "wide", [(w, w ^ d) for w in range(wide)])
+        taken = [d for d in range(1, wide) if group_of(d, wide) in end]
+        result, *got = lax.optimization_barrier((result, *[flying[d] for d in taken]))
         arrived.update(zip(taken, got))
         return result
 
@@ -336,14 +343,14 @@
         arrived.clear()
         return pages
 
+    query_part = jnp.dot(gathered, w_query, preferred_element_type=jnp.float32)
+    keyval_part = jnp.dot(gathered, w_keyval, preferred_element_type=jnp.float32)
+    own_cols = query_part.shape[1] // narrow
+    query_part = jnp.transpose(query_part.reshape(rows, narrow, own_cols), (1, 0, 2))
     partial = jnp.concatenate(
-        [
-            jnp.dot(gathered, w_query, preferred_element_type=jnp.float32),
-            jnp.dot(gathered, w_keyval, preferred_element_type=jnp.float32),
-        ],
-        axis=1,
-    )
-    partial = beside(lambda value: spread(value, "narrow"), partial, (1,))
+        [query_part, jnp.broadcast_to(keyval_part[None], (narrow,) + keyval_part.shape)], axis=2
+    )
+    partial = beside(lambda value: exchange(value, "narrow"), partial, (2, 6), (2, 6))
     projected = jnp.sum(partial, axis=0).astype(jnp.bfloat16)
     shifted = sent_idx + 1
     tags = jnp.concatenate(
@@ -354,7 +361,7 @@
         ],
         axis=2,
     ).astype(jnp.bfloat16)
-    height = up(rows + 1, 16)
+    height = up(rows + 1, 8)
     packed = jnp.concatenate(
         [
             jnp.broadcast_to(projected[None], (wide,) + projected.shape),
@@ -364,16 +371,23 @@
         ],
         axis=1,
     )
-    exchange = functools.partial(lax.all_to_all, split_axis=0, concat_axis=0, tiled=True)
-    received = beside(lambda value: exchange(value, "wide"), packed, (4,))
-
+    received = beside(lambda value: exchange(value, "wide"), packed, (1,), (1,))
+    queries = beside(
+        lambda value: spread(value, "narrow"), received[:, :rows, :own_cols], (3, 7), (3, 7)
+    )
+    if own_cols == HD:
+        queries = jnp.transpose(queries, (1, 0, 2, 3))
+    else:
+        queries = jnp.transpose(queries, (2, 1, 0, 3)).reshape(rows, HEADS, HD)
+        queries = jnp.transpose(queries, (1, 0, 2))
+    queries = queries.reshape(KVH, GROUPS * rows, HD)
     tags_in = received[:, rows, : 3 * capacity].astype(jnp.int32)
     moved_req = tags_in[:, :capacity].reshape(slots)
     moved_idx = (
         tags_in[:, capacity : 2 * capacity] * 32 + tags_in[:, 2 * capacity :] - 1
     ).reshape(slots)
 
-    keyval = jnp.transpose(received[:, :rows, query_cols:], (1, 0, 2)).reshape(rows, -1)
+    keyval = jnp.transpose(received[:, :rows, own_cols:], (1, 0, 2)).reshape(rows, -1)
     extra = up(rows, HD)
     here = (lax.axis_index("wide") == 0) & (lax.axis_index("narrow") == 0)
     row_ids = np.arange(rows)[:, None]
@@ -396,17 +410,19 @@
         lambda value: attend(
             value, new_keyval, tokens, req_tok, pos_tok, row_info, new_bias, rows, piece
         ),
-        received,
-        (2,),
-    )
-    parts = beside(lambda value: exchange(value, ("narrow", "wide")), parts, (3, 5))
+        queries,
+        (4,),
+    )
     moved_pool = placed(moved_pool)
-    attn = beside(lambda value: spread(value, "wide"), combine(parts, piece), (6,))
-    attn = attn.reshape(-1, rows, HD)
-    attn = jnp.transpose(attn, (1, 0, 2)).reshape(rows, -1)
+    parts = beside(lambda value: exchange(value, "narrow"), parts, (), (4,))
+    parts = combine(parts.reshape((narrow, wide) + parts.shape[1:]), piece, False)
+    parts = beside(lambda value: exchange(value, "wide"), parts, (5,))
+    attn = combine(parts[:, None], piece, True)
+    attn = beside(lambda value: spread(value, "wide"), attn, (), (5,))
+    attn = jnp.transpose(attn.reshape(-1, rows, HD), (1, 0, 2)).reshape(rows, -1)
     sums = jnp.dot(attn, w_out, preferred_element_type=jnp.float32)
     sums = sums.reshape(narrow, rows // narrow, -1)
-    sums = beside(lambda value: exchange(value, "narrow"), sums, (7,))
+    sums = exchange(sums, "narrow")
     attended = jnp.sum(sums, axis=0).astype(jnp.bfloat16)
 
     moved_pool = placed(moved_pool)

time: 184 us -> 183 us (level)
  the two profiles are of different devices: /device:TPU:8 before, /device:TPU:0 now
where the time goes in v3:
time: 183 us; the launch traced here: 182 us
  waiting for transfers between devices  72.9 us (40%)
  starting transfers between devices  53.6 us (29%)
  Pallas kernels  23.7 us (13%)
  local copies, waits for them, and re-layouts  20.6 us (11%)
  other arithmetic  7.42 us (4%)
  matrix products  2.76 us (2%)
    ppermute x7, waiting for transfers between devices, beside(): flying[d] = lax.ppermute(chunk, 'wide', [(w, w ^ d) for w in range(wide)])  27.6 us
    ppermute x7, starting transfers between devices, beside(): flying[d] = lax.ppermute(chunk, 'wide', [(w, w ^ d) for w in range(wide)])  22 us
    all_to_all x3, starting transfers between devices, spread(): lax.all_to_all(jnp.broadcast_to(block[None], (count,) + block.shape), axi...  14.7 us
    all_to_all x1, waiting for transfers between devices, on_device(): parts = beside(lambda value: exchange(value, 'wide'), parts, (5,))  12.5 us
    all_to_all x3, waiting for transfers between devices, spread(): lax.all_to_all(jnp.broadcast_to(block[None], (count,) + block.shape), axi...  11.1 us
    pallas_call x1, Pallas kernels, attend(): pl.pallas_call(functools.partial(attend_kernel, rows, piece), grid=(KVH,)...  9.51 us
    all_to_all x1, waiting for transfers between devices, on_device(): received = beside(lambda value: exchange(value, 'wide'), packed, (1,), (1,))  9.46 us
    pallas_call x1, Pallas kernels, permute_pages(): pl.pallas_call(permute_kernel, out_shape=[jax.ShapeDtypeStruct(pool.shape...  8.05 us
  transfers between devices with their start and end apart: 15, of which 10 were waited for; matrix products, arithmetic and copies ran while one was open for 9% of the time, Pallas kernels for 12%

profile of v3, /device:TPU:0, one launch (start us, length us, event | category | flops | bytes accessed | tf_op | source)
XLA Modules:
  0.0 182.0 jit_solution(6278287403067418867)
XLA Ops:
  0.7 1.5 broadcast_in_dim.54
  2.1 7.3 %all-to-all-start = ((bf16[8,5,1024]{2,1,0:T(8,128)(2,1)}), bf16[8,5,1024]{2,1,0:T(8,128)(2,1)S(1)}, u32[]{:S(2)}, u32[]{:S(2)}) async-start(bf16[8,5,1024]{2,1,0:T(8,128)(2,1)} %broadcast_in_dim.54), calls=%async_computation | async-start | bytes 262144 | tf_op jit(solution)/shard_map/all_to_all | solution.py:290
  9.4 0.9 convert_reduce_fusion
  11.0 2.3 %copy.41 = bf16[512,1024]{1,0:T(8,128)(2,1)} copy(bf16[512,1024]{0,1:T(8,128)(2,1)} %bitcast.52) | data formatting | bytes 2097152 | tf_op jit(solution)/shard_map/dot_general | solution.py:346
  13.3 0.9 select_reduce_fusion.1
  14.2 2.2 %copy-done.1 = bf16[128,16,1024]{2,1,0:T(8,128)(2,1)S(1)} copy-done((bf16[128,16,1024]{2,1,0:T(8,128)(2,1)S(1)}, bf16[128,16,1024]{2,1,0:T(8,128)(2,1)}, u32[]{:S(2)}) %copy-start.1) | copy-done | bytes 4194328
  16.3 8.1 %shard_map.155 = (bf16[128,16,1024]{2,1,0:T(8,128)(2,1)}, bf16[16,16,1024]{2,1,0:T(8,128)(2,1)S(1)}, bf16[16,16,1024]{2,1,0:T(8,128)(2,1)S(1)}, bf16[16,16,1024]...) custom-call(s32[128]{0:T(128)S(1)} %get-tuple-element.80.source_ref,, ...), custom_call_target="tpu_custom_call" | custom-call | bytes 8388608 | tf_op jit(solution)/shard_map/pallas_call | solution.py:52
  24.4 0.8 copy-done.3
  25.2 0.8 copy-done.4
  26.0 0.8 copy-done.5
  26.8 0.8 copy-done.6
  27.9 1.6 convolution_bitcast_fusion
  30.2 2.0 %collective-permute-start = (bf16[16,16,1024]{2,1,0:T(8,128)(2,1)}, bf16[16,16,1024]{2,1,0:T(8,128)(2,1)S(1)}, u32[]{:S(2)}, u32[]{:S(2)}) collective-permute-start(bf16[16,16,1024]{2,1,0:T(8,128)(2,1)} %copy-done.7), channel_id=1, source_target_pairs={{0,8},{4,12},{8,0},{12,4},{16,24},{20,28},{24,16},{28,20},{1,9},{5... | collective-permute-start | bytes 1572872 | tf_op jit(solution)/shard_map/ppermute | solution.py:333
  32.3 2.4 %collective-permute-start.1 = (bf16[16,16,1024]{2,1,0:T(8,128)(2,1)}, bf16[16,16,1024]{2,1,0:T(8,128)(2,1)S(1)}, u32[]{:S(2)}, u32[]{:S(2)}) collective-permute-start(bf16[16,16,1024]{2,1,0:T(8,128)(2,1)} %copy-done.6), channel_id=1, source_target_pairs={{0,24},{4,28},{8,16},{12,20},{16,8},{20,12},{24,0},{28,4},{1,25},{... | collective-permute-start | bytes 1572872 | tf_op jit(solution)/shard_map/ppermute | solution.py:333
  34.7 3.3 %all-to-all-start.1 = ((f32[4,40,256]{2,1,0:T(8,128)}), f32[4,40,256]{2,1,0:T(8,128)S(1)}, u32[]{:S(2)}, u32[]{:S(2)}) async-start(f32[4,40,256]{2,1,0:T(8,128)} %pad_maximum_fusion), calls=%async_computation.1 | async-start | bytes 327680 | tf_op jit(solution)/shard_map/all_to_all | solution.py:353
  38.3 4.7 %all-to-all-done.1 = f32[4,40,256]{2,1,0:T(8,128)S(1)} async-done(((f32[4,40,256]{2,1,0:T(8,128)}), f32[4,40,256]{2,1,0:T(8,128)S(1)}, u32[]{:S(2)}, u32[]{:S(2)}) %all-to-all-start.1) | async-done | bytes 163872 | tf_op jit(solution)/shard_map/all_to_all | solution.py:353
  43.0 1.9 %collective-permute-done.refs_1_ = bf16[16,16,1024]{2,1,0:T(8,128)(2,1)S(1)} collective-permute-done((bf16[16,16,1024]{2,1,0:T(8,128)(2,1)}, bf16[16,16,1024]{2,1,0:T(8,128)(2,1)S(1)}, u32[]{:S(2)}, u32[]{:S(2)}) %collective-permute-start) | collective-permute-done | bytes 524320 | tf_op jit(solution)/shard_map/ppermute | solution.py:333
  45.0 12.2 %collective-permute-done.1.refs_3_ = bf16[16,16,1024]{2,1,0:T(8,128)(2,1)S(1)} collective-permute-done((bf16[16,16,1024]{2,1,0:T(8,128)(2,1)}, bf16[16,16,1024]{2,1,0:T(8,128)(2,1)S(1)}, u32[]{:S(2)}, u32[]{:S(2)}) %collective-permute-start.1) | collective-permute-done | bytes 524320 | tf_op jit(solution)/shard_map/ppermute | solution.py:333
  57.9 1.5 collective-permute-start.2
  59.3 3.4 %all-to-all-start.2 = ((bf16[8,48,256]{2,1,0:T(8,128)(2,1)}), bf16[8,48,256]{2,1,0:T(8,128)(2,1)S(1)}, u32[]{:S(2)}, u32[]{:S(2)}) async-start(bf16[8,48,256]{2,1,0:T(8,128)(2,1)} %fusion.3), calls=%async_computation.2 | async-start | bytes 393216 | tf_op jit(solution)/shard_map/all_to_all | solution.py:374
  62.9 9.5 %all-to-all-done.2 = bf16[8,48,256]{2,1,0:T(8,128)(2,1)S(1)} async-done(((bf16[8,48,256]{2,1,0:T(8,128)(2,1)}), bf16[8,48,256]{2,1,0:T(8,128)(2,1)S(1)}, u32[]{:S(2)}, u32[]{:S(2)}) %all-to-all-start.2) | async-done | bytes 196640 | tf_op jit(solution)/shard_map/all_to_all | solution.py:374
  72.5 2.5 %collective-permute-start.4 = (bf16[16,16,1024]{2,1,0:T(8,128)(2,1)S(1)}, bf16[16,16,1024]{2,1,0:T(8,128)(2,1)}, u32[]{:S(2)}, u32[]{:S(2)}) collective-permute-start(bf16[16,16,1024]{2,1,0:T(8,128)(2,1)S(1)} %get-tuple-element.51), channel_id=1, source_target_pairs={{0,28},{4,24},{8,20},{12,16},{16,12},{20,8},{24,4},{28,0},{1,29},{... | collective-permute-start | bytes 1572872 | tf_op jit(solution)/shard_map/ppermute | solution.py:333
  75.0 0.7 iota_add_fusion
  75.7 0.8 broadcast_in_dim.106
  76.4 4.1 %all-to-all-start.3 = ((bf16[4,8,40,128]{3,2,1,0:T(8,128)(2,1)}), bf16[4,8,40,128]{3,2,1,0:T(8,128)(2,1)}, u32[]{:S(2)}, u32[]{:S(2)}) async-start(bf16[4,8,40,128]{3,2,1,0:T(8,128)(2,1)} %broadcast_in_dim.106), calls=%async_computation.3 | async-start | bytes 655360 | tf_op jit(solution)/shard_map/all_to_all | solution.py:290
  80.6 0.7 broadcast_in_dim.107
  81.3 0.9 reshape.174.req_ref
  82.2 0.9 add.109.pos_ref
  83.3 4.0 %all-to-all-done.3 = bf16[4,8,40,128]{3,2,1,0:T(8,128)(2,1)} async-done(((bf16[4,8,40,128]{3,2,1,0:T(8,128)(2,1)}), bf16[4,8,40,128]{3,2,1,0:T(8,128)(2,1)}, u32[]{:S(2)}, u32[]{:S(2)}) %all-to-all-start.3) | async-done | bytes 327712 | tf_op jit(solution)/shard_map/all_to_all | solution.py:290
  87.3 2.3 %collective-permute-done.3.refs_2_ = bf16[16,16,1024]{2,1,0:T(8,128)(2,1)} collective-permute-done((bf16[16,16,1024]{2,1,0:T(8,128)(2,1)}, bf16[16,16,1024]{2,1,0:T(8,128)(2,1)}, u32[]{:S(2)}, u32[]{:S(2)}) %collective-permute-start.3) | collective-permute-done | bytes 524320 | tf_op jit(solution)/shard_map/ppermute | solution.py:333
  89.7 11.1 %collective-permute-done.4.refs_4_ = bf16[16,16,1024]{2,1,0:T(8,128)(2,1)} collective-permute-done((bf16[16,16,1024]{2,1,0:T(8,128)(2,1)S(1)}, bf16[16,16,1024]{2,1,0:T(8,128)(2,1)}, u32[]{:S(2)}, u32[]{:S(2)}) %collective-permute-start.4) | collective-permute-done | bytes 524320 | tf_op jit(solution)/shard_map/ppermute | solution.py:333
  100.8 1.0 copy.35
  101.8 9.9 %collective-permute-start.5 = (bf16[16,16,1024]{2,1,0:T(8,128)(2,1)}, bf16[16,16,1024]{2,1,0:T(8,128)(2,1)}, u32[]{:S(2)}, u32[]{:S(2)}) collective-permute-start(bf16[16,16,1024]{2,1,0:T(8,128)(2,1)} %get-tuple-element.55), channel_id=1, source_target_pairs={{0,16},{4,20},{8,24},{12,28},{16,0},{20,4},{24,8},{28,12},{1,17},{... | collective-permute-start | bytes 1572872 | tf_op jit(solution)/shard_map/ppermute | solution.py:333
  111.6 2.2 %copy-done.2 = bf16[128,16,1024]{2,1,0:T(8,128)(2,1)S(1)} copy-done((bf16[128,16,1024]{2,1,0:T(8,128)(2,1)S(1)}, bf16[128,16,1024]{2,1,0:T(8,128)(2,1)}, u32[]{:S(2)}) %copy-start.2) | copy-done | bytes 4194328
  113.8 9.5 %shard_map.156 = bf16[32,64,128]{2,1,0:T(8,128)(2,1)} custom-call(bf16[4,320,128]{2,1,0:T(8,128)(2,1)S(1)} %bitcast.49, bf16[2048,1024]{1,0:T(8,128)(2,1)S(1)} %bitcast.46, bf16[2048,1024]{1,0:T(8,128)(2,1)S(1)} %bitcast.47, bf16[128,1024]{1,0:T(8,128)(2,1)S(1)} %pad.9.new_key_ref.new_value_ref, bf16[128,1024]{1,0:T(8,128)(2,1)S(1)} %pad.9.new_key_ref.new_value_ref, ...), custom_call_target="tpu_custom_call" | custom-call | flops 1426063360 | bytes 4194304 | tf_op jit(solution)/shard_map/pallas_call | solution.py:204
  123.3 3.5 %all-to-all-start.4 = ((bf16[32,64,128]{2,1,0:T(8,128)(2,1)}), bf16[32,64,128]{2,1,0:T(8,128)(2,1)S(1)}, u32[]{:S(2)}, u32[]{:S(2)}) async-start(bf16[32,64,128]{2,1,0:T(8,128)(2,1)} %shard_map.156), calls=%async_computation.4 | async-start | bytes 1048576 | tf_op jit(solution)/shard_map/all_to_all | solution.py:417
  128.1 7.6 %all-to-all-done.4 = bf16[32,64,128]{2,1,0:T(8,128)(2,1)S(1)} async-done(((bf16[32,64,128]{2,1,0:T(8,128)(2,1)}), bf16[32,64,128]{2,1,0:T(8,128)(2,1)S(1)}, u32[]{:S(2)}, u32[]{:S(2)}) %all-to-all-start.4) | async-done | bytes 524320 | tf_op jit(solution)/shard_map/all_to_all | solution.py:417
  135.6 1.1 shard_map.157
  136.7 3.4 %all-to-all-start.5 = ((bf16[8,64,128]{2,1,0:T(8,128)(2,1)}), bf16[8,64,128]{2,1,0:T(8,128)(2,1)S(1)}, u32[]{:S(2)}, u32[]{:S(2)}) async-start(bf16[8,64,128]{2,1,0:T(8,128)(2,1)} %shard_map.157), calls=%async_computation.5 | async-start | bytes 262144 | tf_op jit(solution)/shard_map/all_to_all | solution.py:419
  140.1 3.7 %collective-permute-start.6 = (bf16[16,16,1024]{2,1,0:T(8,128)(2,1)}, bf16[16,16,1024]{2,1,0:T(8,128)(2,1)S(1)}, u32[]{:S(2)}, u32[]{:S(2)}) collective-permute-start(bf16[16,16,1024]{2,1,0:T(8,128)(2,1)} %copy-done.3), channel_id=1, source_target_pairs={{0,20},{4,16},{8,28},{12,24},{16,4},{20,0},{24,12},{28,8},{1,21},{... | collective-permute-start | bytes 1572872 | tf_op jit(solution)/shard_map/ppermute | solution.py:333
  144.0 1.7 copy.40
  146.5 12.5 %all-to-all-done.5 = bf16[8,64,128]{2,1,0:T(8,128)(2,1)S(1)} async-done(((bf16[8,64,128]{2,1,0:T(8,128)(2,1)}), bf16[8,64,128]{2,1,0:T(8,128)(2,1)S(1)}, u32[]{:S(2)}, u32[]{:S(2)}) %all-to-all-start.5) | async-done | bytes 131104 | tf_op jit(solution)/shard_map/all_to_all | solution.py:419
  159.9 3.4 %all-to-all-start.6 = ((bf16[8,40,128]{2,1,0:T(8,128)(2,1)}), bf16[8,40,128]{2,1,0:T(8,128)(2,1)S(1)}, u32[]{:S(2)}, u32[]{:S(2)}) async-start(bf16[8,40,128]{2,1,0:T(8,128)(2,1)} %broadcast_in_dim.112), calls=%async_computation.6 | async-start | bytes 163840 | tf_op jit(solution)/shard_map/all_to_all | solution.py:290
  164.0 7.0 %all-to-all-done.6 = bf16[8,40,128]{2,1,0:T(8,128)(2,1)S(1)} async-done(((bf16[8,40,128]{2,1,0:T(8,128)(2,1)}), bf16[8,40,128]{2,1,0:T(8,128)(2,1)S(1)}, u32[]{:S(2)}, u32[]{:S(2)}) %all-to-all-start.6) | async-done | bytes 81952 | tf_op jit(solution)/shard_map/all_to_all | solution.py:290
  171.1 0.9 fusion
  172.0 3.3 %all-to-all-start.7 = ((f32[4,10,512]{2,1,0:T(8,128)}), f32[4,10,512]{2,1,0:T(8,128)S(1)}, u32[]{:S(2)}, u32[]{:S(2)}) async-start(f32[4,10,512]{2,1,0:T(8,128)} %fusion), calls=%async_computation.7 | async-start | bytes 262144 | tf_op jit(solution)/shard_map/all_to_all | solution.py:425
  176.6 2.7 %shard_map.159.refs_2_ = bf16[128,16,1024]{2,1,0:T(8,128)(2,1)} custom-call(s32[5]{0:T(128)S(1)} %stack.43.place_ref, bf16[16,16,1024]{2,1,0:T(8,128)(2,1)S(1)} %collective-permute-done.2.refs_0_, bf16[16,16,1024]{2,1,0:T(8,128)(2,1)S(1)} %collective-permute-done.refs_1_, ...), custom_call_target="tpu_custom_call", output_to_operand_aliasing={{}: (6, {})} | custom-call | bytes 5242880 | tf_op jit(solution)/shard_map/pallas_call | solution.py:91
  179.4 2.0 %shard_map.160 = bf16[128,16,1024]{2,1,0:T(8,128)(2,1)} custom-call(s32[2]{0:T(128)S(1)} %pad_add_fusion.1.place_ref, bf16[16,16,1024]{2,1,0:T(8,128)(2,1)} %collective-permute-done.5.refs_0_, bf16[16,16,1024]{2,1,0:T(8,128)(2,1)S(1)} %collective-permute-done.6.refs_1_, bf16[128,16,1024]{2,1,0:T(8,128)(2,1)} %shard_map.159.refs_2_), custom_call_target="tpu_custom_call", output_to_operand_aliasing={{}: (3, {})} | custom-call | bytes 2097152 | tf_op jit(solution)/shard_map/pallas_call | solution.py:91
  (73 shorter events, 8.8 us)
Async XLA Ops:
  0.6 170.4 %copy-start = (bf16[1024,512]{1,0:T(8,128)(2,1)S(1)}, bf16[1024,512]{1,0:T(8,128)(2,1)}, u32[]{:S(2)}) copy-start(bf16[1024,512]{1,0:T(8,128)(2,1)} %param.15) | copy-start | bytes 3145732
  0.6 27.0 %copy-start.9 = (bf16[1024,128]{1,0:T(8,128)(2,1)S(1)}, bf16[1024,128]{1,0:T(8,128)(2,1)}, u32[]{:S(2)}) copy-start(bf16[1024,128]{1,0:T(8,128)(2,1)} %param.14) | copy-start | bytes 786436
  2.1 25.5 %all-to-all-start = ((bf16[8,5,1024]{2,1,0:T(8,128)(2,1)}), bf16[8,5,1024]{2,1,0:T(8,128)(2,1)S(1)}, u32[]{:S(2)}, u32[]{:S(2)}) async-start(bf16[8,5,1024]{2,1,0:T(8,128)(2,1)} %broadcast_in_dim.54), calls=%async_computation | async-start | bytes 262144 | tf_op jit(solution)/shard_map/all_to_all | solution.py:290
  13.3 49.5 %copy-start.12 = (s32[8]{0:T(128)S(1)}, s32[8]{0:T(128)}, u32[]{:S(2)}) copy-start(s32[8]{0:T(128)} %param.19) | copy-start | bytes 100
  13.3 49.6 %copy-start.13 = (s32[128]{0:T(128)S(1)}, s32[128]{0:T(128)}, u32[]{:S(2)}) copy-start(s32[128]{0:T(128)} %param.18) | copy-start | bytes 1540
  14.1 2.2 %copy-start.1 = (bf16[128,16,1024]{2,1,0:T(8,128)(2,1)S(1)}, bf16[128,16,1024]{2,1,0:T(8,128)(2,1)}, u32[]{:S(2)}) copy-start(bf16[128,16,1024]{2,1,0:T(8,128)(2,1)} %pool_ref.1) | copy-start | bytes 12582916
  16.3 64.2 %copy-start.14 = (s32[40,1]{0,1:T(1,128)S(1)}, s32[40,1]{0,1:T(1,128)}, u32[]{:S(2)}) copy-start(s32[40,1]{0,1:T(1,128)} %constant.77) | copy-start | bytes 484
  16.3 64.2 %copy-start.11 = (s32[128]{0:T(128)S(1)}, s32[128]{0:T(128)}, u32[]{:S(2)}) copy-start(s32[128]{0:T(128)} %param.17) | copy-start | bytes 1540
  16.3 66.9 %copy-start.10 = (pred[40,128]{1,0:T(8,128)(4,1)S(1)}, pred[40,128]{1,0:T(8,128)(4,1)}, u32[]{:S(2)}) copy-start(pred[40,128]{1,0:T(8,128)(4,1)} %constant.70.clone) | copy-start | bytes 15364
  24.4 0.8 copy-start.3
  25.2 0.8 copy-start.4
  26.0 0.8 copy-start.5
  26.8 0.8 copy-start.6
  27.6 2.6 %copy-start.7 = (bf16[16,16,1024]{2,1,0:T(8,128)(2,1)}, bf16[16,16,1024]{2,1,0:T(8,128)(2,1)S(1)}, u32[]{:S(2)}) copy-start(bf16[16,16,1024]{2,1,0:T(8,128)(2,1)S(1)} %get-tuple-element.40) | copy-start | bytes 1572868
  30.2 14.7 %collective-permute-start = (bf16[16,16,1024]{2,1,0:T(8,128)(2,1)}, bf16[16,16,1024]{2,1,0:T(8,128)(2,1)S(1)}, u32[]{:S(2)}, u32[]{:S(2)}) collective-permute-start(bf16[16,16,1024]{2,1,0:T(8,128)(2,1)} %copy-done.7), channel_id=1, source_target_pairs={{0,8},{4,12},{8,0},{12,4},{16,24},{20,28},{24,16},{28,20},{1,9},{5... | collective-permute-start | bytes 1572872 | tf_op jit(solution)/shard_map/ppermute | solution.py:333
  32.3 24.9 %collective-permute-start.1 = (bf16[16,16,1024]{2,1,0:T(8,128)(2,1)}, bf16[16,16,1024]{2,1,0:T(8,128)(2,1)S(1)}, u32[]{:S(2)}, u32[]{:S(2)}) collective-permute-start(bf16[16,16,1024]{2,1,0:T(8,128)(2,1)} %copy-done.6), channel_id=1, source_target_pairs={{0,24},{4,28},{8,16},{12,20},{16,8},{20,12},{24,0},{28,4},{1,25},{... | collective-permute-start | bytes 1572872 | tf_op jit(solution)/shard_map/ppermute | solution.py:333
  34.7 8.3 %all-to-all-start.1 = ((f32[4,40,256]{2,1,0:T(8,128)}), f32[4,40,256]{2,1,0:T(8,128)S(1)}, u32[]{:S(2)}, u32[]{:S(2)}) async-start(f32[4,40,256]{2,1,0:T(8,128)} %pad_maximum_fusion), calls=%async_computation.1 | async-start | bytes 327680 | tf_op jit(solution)/shard_map/all_to_all | solution.py:353
  57.9 14.5 %collective-permute-start.2 = (bf16[16,16,1024]{2,1,0:T(8,128)(2,1)}, bf16[16,16,1024]{2,1,0:T(8,128)(2,1)S(1)}, u32[]{:S(2)}, u32[]{:S(2)}) collective-permute-start(bf16[16,16,1024]{2,1,0:T(8,128)(2,1)} %copy-done.5), channel_id=1, source_target_pairs={{0,4},{4,0},{8,12},{12,8},{16,20},{20,16},{24,28},{28,24},{1,5},{5... | collective-permute-start | bytes 1572872 | tf_op jit(solution)/shard_map/ppermute | solution.py:333
  59.3 13.0 %all-to-all-start.2 = ((bf16[8,48,256]{2,1,0:T(8,128)(2,1)}), bf16[8,48,256]{2,1,0:T(8,128)(2,1)S(1)}, u32[]{:S(2)}, u32[]{:S(2)}) async-start(bf16[8,48,256]{2,1,0:T(8,128)(2,1)} %fusion.3), calls=%async_computation.2 | async-start | bytes 393216 | tf_op jit(solution)/shard_map/all_to_all | solution.py:374
  72.4 8.2 %copy-start.8 = (bf16[8,48,256]{2,1,0:T(8,128)(2,1)}, bf16[8,48,256]{2,1,0:T(8,128)(2,1)S(1)}, u32[]{:S(2)}) copy-start(bf16[8,48,256]{2,1,0:T(8,128)(2,1)S(1)} %all-to-all-done.2) | copy-start | bytes 589828
  72.4 17.2 %collective-permute-start.3 = (bf16[16,16,1024]{2,1,0:T(8,128)(2,1)}, bf16[16,16,1024]{2,1,0:T(8,128)(2,1)}, u32[]{:S(2)}, u32[]{:S(2)}) collective-permute-start(bf16[16,16,1024]{2,1,0:T(8,128)(2,1)} %copy-done.4), channel_id=1, source_target_pairs={{0,12},{4,8},{8,4},{12,0},{16,28},{20,24},{24,20},{28,16},{1,13},{... | collective-permute-start | bytes 1572872 | tf_op jit(solution)/shard_map/ppermute | solution.py:333
  72.5 28.3 %collective-permute-start.4 = (bf16[16,16,1024]{2,1,0:T(8,128)(2,1)S(1)}, bf16[16,16,1024]{2,1,0:T(8,128)(2,1)}, u32[]{:S(2)}, u32[]{:S(2)}) collective-permute-start(bf16[16,16,1024]{2,1,0:T(8,128)(2,1)S(1)} %get-tuple-element.51), channel_id=1, source_target_pairs={{0,28},{4,24},{8,20},{12,16},{16,12},{20,8},{24,4},{28,0},{1,29},{... | collective-permute-start | bytes 1572872 | tf_op jit(solution)/shard_map/ppermute | solution.py:333
  76.4 10.9 %all-to-all-start.3 = ((bf16[4,8,40,128]{3,2,1,0:T(8,128)(2,1)}), bf16[4,8,40,128]{3,2,1,0:T(8,128)(2,1)}, u32[]{:S(2)}, u32[]{:S(2)}) async-start(bf16[4,8,40,128]{3,2,1,0:T(8,128)(2,1)} %broadcast_in_dim.106), calls=%async_computation.3 | async-start | bytes 655360 | tf_op jit(solution)/shard_map/all_to_all | solution.py:290
  101.8 33.9 %collective-permute-start.5 = (bf16[16,16,1024]{2,1,0:T(8,128)(2,1)}, bf16[16,16,1024]{2,1,0:T(8,128)(2,1)}, u32[]{:S(2)}, u32[]{:S(2)}) collective-permute-start(bf16[16,16,1024]{2,1,0:T(8,128)(2,1)} %get-tuple-element.55), channel_id=1, source_target_pairs={{0,16},{4,20},{8,24},{12,28},{16,0},{20,4},{24,8},{28,12},{1,17},{... | collective-permute-start | bytes 1572872 | tf_op jit(solution)/shard_map/ppermute | solution.py:333
  111.6 2.2 %copy-start.2 = (bf16[128,16,1024]{2,1,0:T(8,128)(2,1)S(1)}, bf16[128,16,1024]{2,1,0:T(8,128)(2,1)}, u32[]{:S(2)}) copy-start(bf16[128,16,1024]{2,1,0:T(8,128)(2,1)} %pool_ref.1) | copy-start | bytes 12582916
  113.8 13.0 %copy-start.15 = (s32[8]{0:T(128)S(1)}, s32[8]{0:T(128)}, u32[]{:S(2)}) copy-start(s32[8]{0:T(128)} %param.21) | copy-start | bytes 100
  123.3 12.3 %all-to-all-start.4 = ((bf16[32,64,128]{2,1,0:T(8,128)(2,1)}), bf16[32,64,128]{2,1,0:T(8,128)(2,1)S(1)}, u32[]{:S(2)}, u32[]{:S(2)}) async-start(bf16[32,64,128]{2,1,0:T(8,128)(2,1)} %shard_map.156), calls=%async_computation.4 | async-start | bytes 1048576 | tf_op jit(solution)/shard_map/all_to_all | solution.py:417
  136.7 22.3 %all-to-all-start.5 = ((bf16[8,64,128]{2,1,0:T(8,128)(2,1)}), bf16[8,64,128]{2,1,0:T(8,128)(2,1)S(1)}, u32[]{:S(2)}, u32[]{:S(2)}) async-start(bf16[8,64,128]{2,1,0:T(8,128)(2,1)} %shard_map.157), calls=%async_computation.5 | async-start | bytes 262144 | tf_op jit(solution)/shard_map/all_to_all | solution.py:419
  140.1 30.9 %collective-permute-start.6 = (bf16[16,16,1024]{2,1,0:T(8,128)(2,1)}, bf16[16,16,1024]{2,1,0:T(8,128)(2,1)S(1)}, u32[]{:S(2)}, u32[]{:S(2)}) collective-permute-start(bf16[16,16,1024]{2,1,0:T(8,128)(2,1)} %copy-done.3), channel_id=1, source_target_pairs={{0,20},{4,16},{8,28},{12,24},{16,4},{20,0},{24,12},{28,8},{1,21},{... | collective-permute-start | bytes 1572872 | tf_op jit(solution)/shard_map/ppermute | solution.py:333
  159.9 11.1 %all-to-all-start.6 = ((bf16[8,40,128]{2,1,0:T(8,128)(2,1)}), bf16[8,40,128]{2,1,0:T(8,128)(2,1)S(1)}, u32[]{:S(2)}, u32[]{:S(2)}) async-start(bf16[8,40,128]{2,1,0:T(8,128)(2,1)} %broadcast_in_dim.112), calls=%async_computation.6 | async-start | bytes 163840 | tf_op jit(solution)/shard_map/all_to_all | solution.py:290
  172.0 9.4 %all-to-all-start.7 = ((f32[4,10,512]{2,1,0:T(8,128)}), f32[4,10,512]{2,1,0:T(8,128)S(1)}, u32[]{:S(2)}, u32[]{:S(2)}) async-start(f32[4,10,512]{2,1,0:T(8,128)} %fusion), calls=%async_computation.7 | async-start | bytes 262144 | tf_op jit(solution)/shard_map/all_to_all | solution.py:425

commit v4 on v3

--- a/solution.py
+++ b/solution.py
@@ -31,18 +31,17 @@
     count = chunk_refs[0].shape[0]
 
     def start(j, carry):
-        pltpu.make_async_copy(pool_ref.at[source_ref[j]], pages_ref.at[j], in_sem).start()
+        pltpu.make_async_copy(pool_ref.at[source_ref[j]], pages_ref.at[j], in_sem.at[j // count]).start()
         return carry
 
     lax.fori_loop(0, pool_ref.shape[0], start, 0)
-    pltpu.make_async_copy(pool_ref, pages_ref, in_sem).wait()
     targets = [out_ref.at[pl.ds(place_ref[0] * count, count)], *chunk_refs]
-    copies = [
-        pltpu.make_async_copy(pages_ref.at[pl.ds(c * count, count)], target, out_sem.at[c])
-        for c, target in enumerate(targets)
-    ]
-    for copy in copies:
-        copy.start()
+    copies = []
+    for c, target in enumerate(targets):
+        held = pages_ref.at[pl.ds(c * count, count)]
+        pltpu.make_async_copy(pool_ref.at[pl.ds(0, count)], held, in_sem.at[c]).wait()
+        copies.append(pltpu.make_async_copy(held, target, out_sem.at[c]))
+        copies[-1].start()
     for copy in copies:
         copy.wait()
 
@@ -55,12 +54,12 @@
         in_specs=[
             pl.BlockSpec(memory_space=pltpu.SMEM),
             pl.BlockSpec(memory_space=pltpu.SMEM),
-            pl.BlockSpec(memory_space=pl.ANY),
-        ],
-        out_specs=[pl.BlockSpec(memory_space=pl.ANY)] * chunks,
+            pl.BlockSpec(memory_space=pltpu.HBM),
+        ],
+        out_specs=[pl.BlockSpec(memory_space=pltpu.HBM)] * chunks,
         scratch_shapes=[
             pltpu.VMEM(pool.shape, pool.dtype),
-            pltpu.SemaphoreType.DMA,
+            pltpu.SemaphoreType.DMA((chunks,)),
             pltpu.SemaphoreType.DMA((chunks,)),
         ],
         compiler_params=pltpu.CompilerParams(vmem_limit_bytes=2 * pool.size + 2 * MIB),
@@ -325,16 +324,21 @@
     exchange = functools.partial(lax.all_to_all, split_axis=0, concat_axis=0, tiled=True)
     flying = {}
 
-    def beside(step, value, begin=(), end=()):
-        taken = [d for d in range(1, wide) if group_of(d, wide) in begin]
-        value, *sent = lax.optimization_barrier((value, *[chunks[d - 1] for d in taken]))
-        result = step(value)
+    def members(groups):
+        return [d for group in groups for d in range(1, wide) if group_of(d, wide) == group]
+
+    def launch(values, *groups):
+        taken = members(groups)
+        values, sent = lax.optimization_barrier((values, [chunks[d - 1] for d in taken]))
         for d, chunk in zip(taken, sent):
             flying[d] = lax.ppermute(chunk, "wide", [(w, w ^ d) for w in range(wide)])
-        taken = [d for d in range(1, wide) if group_of(d, wide) in end]
-        result, *got = lax.optimization_barrier((result, *[flying[d] for d in taken]))
+        return values
+
+    def land(values, *groups):
+        taken = members(groups)
+        values, got = lax.optimization_barrier((values, [flying[d] for d in taken]))
         arrived.update(zip(taken, got))
-        return result
+        return values
 
     def placed(pages):
         taken = sorted(arrived)
@@ -350,7 +354,7 @@
     partial = jnp.concatenate(
         [query_part, jnp.broadcast_to(keyval_part[None], (narrow,) + keyval_part.shape)], axis=2
     )
-    partial = beside(lambda value: exchange(value, "narrow"), partial, (2, 6), (2, 6))
+    partial = exchange(launch(partial, 6), "narrow")
     projected = jnp.sum(partial, axis=0).astype(jnp.bfloat16)
     shifted = sent_idx + 1
     tags = jnp.concatenate(
@@ -371,10 +375,21 @@
         ],
         axis=1,
     )
-    received = beside(lambda value: exchange(value, "wide"), packed, (1,), (1,))
-    queries = beside(
-        lambda value: spread(value, "narrow"), received[:, :rows, :own_cols], (3, 7), (3, 7)
-    )
+    packed, page_req, page_idx, lengths = lax.optimization_barrier(
+        (packed, page_req, page_idx, lengths)
+    )
+    received = exchange(packed, "wide")
+    req_tok = jnp.broadcast_to(page_req[:, None], (slots, PAGE)).reshape(1, -1)
+    pos_tok = (page_idx[:, None] * PAGE + jnp.arange(PAGE, dtype=jnp.int32)[None, :]).reshape(1, -1)
+    row_info = jnp.stack(
+        [
+            jnp.asarray(np.arange(rows) // STEPS, jnp.int32),
+            jnp.broadcast_to(lengths[:, None], (requests, STEPS)).reshape(rows),
+        ],
+        axis=1,
+    )
+    req_tok, pos_tok, row_info = launch((req_tok, pos_tok, row_info), 7, 4, 2, 3, 1)
+    queries = spread(received[:, :rows, :own_cols], "narrow")
     if own_cols == HD:
         queries = jnp.transpose(queries, (1, 0, 2, 3))
     else:
@@ -394,37 +409,25 @@
     col_ids = np.arange(extra)[None, :]
     causal = (row_ids // STEPS == col_ids // STEPS) & (col_ids <= row_ids) & (col_ids < rows)
     new_bias = jnp.where(jnp.asarray(causal) & here, 0.0, NEG_FILL).astype(jnp.float32)
-    req_tok = jnp.broadcast_to(page_req[:, None], (slots, PAGE)).reshape(1, -1)
-    pos_tok = (page_idx[:, None] * PAGE + jnp.arange(PAGE, dtype=jnp.int32)[None, :]).reshape(1, -1)
-    row_info = jnp.stack(
-        [
-            jnp.asarray(np.arange(rows) // STEPS, jnp.int32),
-            jnp.broadcast_to(lengths[:, None], (requests, STEPS)).reshape(rows),
-        ],
-        axis=1,
-    )
     piece = HEADS * rows // (wide * narrow)
     new_keyval = jnp.pad(keyval, ((0, extra - rows), (0, 0)))
     tokens = pool.reshape(slots * PAGE, -1)
-    parts = beside(
-        lambda value: attend(
-            value, new_keyval, tokens, req_tok, pos_tok, row_info, new_bias, rows, piece
-        ),
-        queries,
-        (4,),
-    )
-    moved_pool = placed(moved_pool)
-    parts = beside(lambda value: exchange(value, "narrow"), parts, (), (4,))
+    parts = attend(
+        queries, new_keyval, tokens, req_tok, pos_tok, row_info, new_bias, rows, piece
+    )
+    parts = exchange(parts, "narrow")
     parts = combine(parts.reshape((narrow, wide) + parts.shape[1:]), piece, False)
-    parts = beside(lambda value: exchange(value, "wide"), parts, (5,))
-    attn = combine(parts[:, None], piece, True)
-    attn = beside(lambda value: spread(value, "wide"), attn, (), (5,))
+    attn = combine(exchange(parts, "wide")[:, None], piece, True)
+    attn = land(attn, 6, 7, 4, 2, 3, 1)
+    moved_pool = launch(placed(moved_pool), 5)
+    attn = spread(attn, "wide")
     attn = jnp.transpose(attn.reshape(-1, rows, HD), (1, 0, 2)).reshape(rows, -1)
     sums = jnp.dot(attn, w_out, preferred_element_type=jnp.float32)
     sums = sums.reshape(narrow, rows // narrow, -1)
     sums = exchange(sums, "narrow")
     attended = jnp.sum(sums, axis=0).astype(jnp.bfloat16)
 
+    attended = land(attended, 5)
     moved_pool = placed(moved_pool)
 
     local_req = local_rows // STEPS

time: 183 us -> 182 us (level)
  waiting for transfers between devices: 72.9 us -> 85 us
  starting transfers between devices: 53.6 us -> 47.9 us
  local copies, waits for them, and re-layouts: 20.6 us -> 15.7 us
    all_to_all x4, waiting for transfers between devices: 34.3 us -> 60.4 us  [the longest x1 38.3 us: on_device(): attn = combine(exchange(parts, 'wide')[:, None], piece, True)]
    ppermute x7, waiting for transfers between devices: 27.6 us -> 1.47 us  [launch(): flying[d] = lax.ppermute(chunk, 'wide', [(w, w ^ d) for w in range(wide)])]
    all_to_all x3, waiting for transfers between devices: 11.1 us -> 19.8 us  [spread(): lax.all_to_all(jnp.broadcast_to(block[None], (count,) + block.shape), axi...]
    ppermute x7, starting transfers between devices: 22 us -> 14.3 us  [launch(): flying[d] = lax.ppermute(chunk, 'wide', [(w, w ^ d) for w in range(wide)])]
    all_to_all x1, waiting for transfers between devices: 0.01 us -> 3.33 us  [on_device(): sums = exchange(sums, 'narrow')]
    all_to_all x4, starting transfers between devices: 13.6 us -> 16.2 us  [the longest x1 6 us: on_device(): received = exchange(packed, 'wide')]
  transfers between devices with their start and end apart: 15 -> 15, of which waited for: 10 -> 8; matrix products, arithmetic and copies ran while one was open for 9% -> 6% of each run, Pallas kernels for 12% -> 11%
where the time goes in v4:
time: 182 us; the launch traced here: 181 us
  waiting for transfers between devices  85 us (47%)
  starting transfers between devices  47.9 us (26%)
  Pallas kernels  23.5 us (13%)
  local copies, waits for them, and re-layouts  15.7 us (9%)
  other arithmetic  5.99 us (3%)
    all_to_all x1, waiting for transfers between devices, on_device(): attn = combine(exchange(parts, 'wide')[:, None], piece, True)  38.3 us
    all_to_all x3, waiting for transfers between devices, spread(): lax.all_to_all(jnp.broadcast_to(block[None], (count,) + block.shape), axi...  19.8 us
    all_to_all x1, waiting for transfers between devices, on_device(): received = exchange(packed, 'wide')  15.8 us
    ppermute x7, starting transfers between devices, launch(): flying[d] = lax.ppermute(chunk, 'wide', [(w, w ^ d) for w in range(wide)])  14.3 us
    all_to_all x3, starting transfers between devices, spread(): lax.all_to_all(jnp.broadcast_to(block[None], (count,) + block.shape), axi...  14.1 us
    pallas_call x1, Pallas kernels, attend(): pl.pallas_call(functools.partial(attend_kernel, rows, piece), grid=(KVH,)...  9.51 us
    pallas_call x1, Pallas kernels, permute_pages(): pl.pallas_call(permute_kernel, out_shape=[jax.ShapeDtypeStruct(pool.shape...  8.64 us
    unnamed x33, local copies, waits for them, and re-layouts  8.41 us
  transfers between devices with their start and end apart: 15, of which 8 were waited for; matrix products, arithmetic and copies ran while one was open for 6% of the time, Pallas kernels for 11%

profile of v4, /device:TPU:0, one launch (start us, length us, event | category | flops | bytes accessed | tf_op | source)
XLA Modules:
  0.0 180.7 jit_solution(17200640037051407893)
XLA Ops:
  0.7 1.5 broadcast_in_dim.54
  2.1 7.3 %all-to-all-start = ((bf16[8,5,1024]{2,1,0:T(8,128)(2,1)}), bf16[8,5,1024]{2,1,0:T(8,128)(2,1)S(1)}, u32[]{:S(2)}, u32[]{:S(2)}) async-start(bf16[8,5,1024]{2,1,0:T(8,128)(2,1)} %broadcast_in_dim.54), calls=%async_computation | async-start | bytes 262144 | tf_op jit(solution)/shard_map/all_to_all | solution.py:289
  9.4 0.9 convert_reduce_fusion
  10.3 0.7 multiply_add_fusion.1
  11.0 0.8 select_reduce_fusion.1
  11.9 1.5 copy.41
  13.4 2.2 %copy-done.1 = bf16[128,16,1024]{2,1,0:T(8,128)(2,1)S(1)} copy-done((bf16[128,16,1024]{2,1,0:T(8,128)(2,1)S(1)}, bf16[128,16,1024]{2,1,0:T(8,128)(2,1)}, u32[]{:S(2)}) %copy-start.1) | copy-done | bytes 4194328
  15.6 8.6 %shard_map.155 = (bf16[128,16,1024]{2,1,0:T(8,128)(2,1)}, bf16[16,16,1024]{2,1,0:T(8,128)(2,1)S(1)}, bf16[16,16,1024]{2,1,0:T(8,128)(2,1)S(1)}, bf16[16,16,1024]...) custom-call(s32[128]{0:T(128)S(1)} %get-tuple-element.82.source_ref,, ...), custom_call_target="tpu_custom_call" | custom-call | bytes 8388608 | tf_op jit(solution)/shard_map/pallas_call | solution.py:51
  24.3 0.8 copy-done.3
  25.1 0.8 copy-done.5
  25.9 0.8 copy-done.6
  26.7 0.8 copy-done.7
  27.5 0.8 copy-done.8
  29.0 0.7 pad_maximum_fusion
  29.7 3.3 %all-to-all-start.1 = ((f32[4,40,256]{2,1,0:T(8,128)}), f32[4,40,256]{2,1,0:T(8,128)S(1)}, u32[]{:S(2)}, u32[]{:S(2)}) async-start(f32[4,40,256]{2,1,0:T(8,128)} %pad_maximum_fusion), calls=%async_computation.1 | async-start | bytes 327680 | tf_op jit(solution)/shard_map/all_to_all | solution.py:357
  33.3 4.7 %all-to-all-done.1 = f32[4,40,256]{2,1,0:T(8,128)S(1)} async-done(((f32[4,40,256]{2,1,0:T(8,128)}), f32[4,40,256]{2,1,0:T(8,128)S(1)}, u32[]{:S(2)}, u32[]{:S(2)}) %all-to-all-start.1) | async-done | bytes 163872 | tf_op jit(solution)/shard_map/all_to_all | solution.py:357
  38.0 0.7 fusion.3
  38.7 6.0 %all-to-all-start.2 = ((bf16[8,48,256]{2,1,0:T(8,128)(2,1)}), bf16[8,48,256]{2,1,0:T(8,128)(2,1)S(1)}, u32[]{:S(2)}, u32[]{:S(2)}) async-start(bf16[8,48,256]{2,1,0:T(8,128)(2,1)} %fusion.3), calls=%async_computation.2 | async-start | bytes 393216 | tf_op jit(solution)/shard_map/all_to_all | solution.py:381
  44.7 3.9 %collective-permute-start = (bf16[16,16,1024]{2,1,0:T(8,128)(2,1)}, bf16[16,16,1024]{2,1,0:T(8,128)(2,1)S(1)}, u32[]{:S(2)}, u32[]{:S(2)}) collective-permute-start(bf16[16,16,1024]{2,1,0:T(8,128)(2,1)} %get-tuple-element.52), channel_id=1, source_target_pairs={{0,24},{4,28},{8,16},{12,20},{16,8},{20,12},{24,0},{28,4},{1,25},{... | collective-permute-start | bytes 1572872 | tf_op jit(solution)/shard_map/ppermute | solution.py:334
  48.6 15.8 %all-to-all-done.2 = bf16[8,48,256]{2,1,0:T(8,128)(2,1)S(1)} async-done(((bf16[8,48,256]{2,1,0:T(8,128)(2,1)}), bf16[8,48,256]{2,1,0:T(8,128)(2,1)S(1)}, u32[]{:S(2)}, u32[]{:S(2)}) %all-to-all-start.2) | async-done | bytes 196640 | tf_op jit(solution)/shard_map/all_to_all | solution.py:381
  64.5 0.7 broadcast_in_dim.106
  65.3 3.5 %all-to-all-start.3 = ((bf16[4,8,40,128]{3,2,1,0:T(8,128)(2,1)}), bf16[4,8,40,128]{3,2,1,0:T(8,128)(2,1)S(1)}, u32[]{:S(2)}, u32[]{:S(2)}) async-start(bf16[4,8,40,128]{3,2,1,0:T(8,128)(2,1)} %broadcast_in_dim.106), calls=%async_computation.3 | async-start | bytes 655360 | tf_op jit(solution)/shard_map/all_to_all | solution.py:289
  69.4 6.0 %all-to-all-done.3 = bf16[4,8,40,128]{3,2,1,0:T(8,128)(2,1)S(1)} async-done(((bf16[4,8,40,128]{3,2,1,0:T(8,128)(2,1)}), bf16[4,8,40,128]{3,2,1,0:T(8,128)(2,1)S(1)}, u32[]{:S(2)}, u32[]{:S(2)}) %all-to-all-start.3) | async-done | bytes 327712 | tf_op jit(solution)/shard_map/all_to_all | solution.py:289
  75.5 2.2 %copy-done.2 = bf16[128,16,1024]{2,1,0:T(8,128)(2,1)S(1)} copy-done((bf16[128,16,1024]{2,1,0:T(8,128)(2,1)S(1)}, bf16[128,16,1024]{2,1,0:T(8,128)(2,1)}, u32[]{:S(2)}) %copy-start.2) | copy-done | bytes 4194328
  77.6 9.5 %shard_map.156 = bf16[32,64,128]{2,1,0:T(8,128)(2,1)} custom-call(bf16[4,320,128]{2,1,0:T(8,128)(2,1)S(1)} %bitcast.49, bf16[2048,1024]{1,0:T(8,128)(2,1)S(1)} %bitcast.46, bf16[2048,1024]{1,0:T(8,128)(2,1)S(1)} %bitcast.47, bf16[128,1024]{1,0:T(8,128)(2,1)S(1)} %pad.9.new_key_ref.new_value_ref, bf16[128,1024]{1,0:T(8,128)(2,1)S(1)} %pad.9.new_key_ref.new_value_ref, ...), custom_call_target="tpu_custom_call" | custom-call | flops 1426063360 | bytes 4194304 | tf_op jit(solution)/shard_map/pallas_call | solution.py:203
  87.2 3.5 %all-to-all-start.4 = ((bf16[32,64,128]{2,1,0:T(8,128)(2,1)}), bf16[32,64,128]{2,1,0:T(8,128)(2,1)S(1)}, u32[]{:S(2)}, u32[]{:S(2)}) async-start(bf16[32,64,128]{2,1,0:T(8,128)(2,1)} %shard_map.156), calls=%async_computation.4 | async-start | bytes 1048576 | tf_op jit(solution)/shard_map/all_to_all | solution.py:418
  90.6 1.8 %collective-permute-start.1 = (bf16[16,16,1024]{2,1,0:T(8,128)(2,1)}, bf16[16,16,1024]{2,1,0:T(8,128)(2,1)S(1)}, u32[]{:S(2)}, u32[]{:S(2)}) collective-permute-start(bf16[16,16,1024]{2,1,0:T(8,128)(2,1)} %get-tuple-element.53), channel_id=1, source_target_pairs={{0,28},{4,24},{8,20},{12,16},{16,12},{20,8},{24,4},{28,0},{1,29},{... | collective-permute-start | bytes 1572872 | tf_op jit(solution)/shard_map/ppermute | solution.py:334
  92.5 3.4 %collective-permute-start.3 = (bf16[16,16,1024]{2,1,0:T(8,128)(2,1)}, bf16[16,16,1024]{2,1,0:T(8,128)(2,1)}, u32[]{:S(2)}, u32[]{:S(2)}) collective-permute-start(bf16[16,16,1024]{2,1,0:T(8,128)(2,1)} %copy-done.7), channel_id=1, source_target_pairs={{0,8},{4,12},{8,0},{12,4},{16,24},{20,28},{24,16},{28,20},{1,9},{5... | collective-permute-start | bytes 1572872 | tf_op jit(solution)/shard_map/ppermute | solution.py:334
  96.0 1.4 collective-permute-start.5
  97.9 1.5 all-to-all-done.4
  99.4 1.1 shard_map.157
  100.6 3.4 %all-to-all-start.5 = ((bf16[8,64,128]{2,1,0:T(8,128)(2,1)}), bf16[8,64,128]{2,1,0:T(8,128)(2,1)S(1)}, u32[]{:S(2)}, u32[]{:S(2)}) async-start(bf16[8,64,128]{2,1,0:T(8,128)(2,1)} %shard_map.157), calls=%async_computation.5 | async-start | bytes 262144 | tf_op jit(solution)/shard_map/all_to_all | solution.py:420
  103.9 0.7 iota_compare_fusion.4
  104.8 0.7 dynamic-slice_select_fusion
  105.5 38.3 %all-to-all-done.5 = bf16[8,64,128]{2,1,0:T(8,128)(2,1)S(1)} async-done(((bf16[8,64,128]{2,1,0:T(8,128)(2,1)}), bf16[8,64,128]{2,1,0:T(8,128)(2,1)S(1)}, u32[]{:S(2)}, u32[]{:S(2)}) %all-to-all-start.5) | async-done | bytes 131104 | tf_op jit(solution)/shard_map/all_to_all | solution.py:420
  144.2 3.1 %shard_map.159.refs_1_ = bf16[128,16,1024]{2,1,0:T(8,128)(2,1)} custom-call(s32[6]{0:T(128)S(1)} %stack.38.place_ref, bf16[16,16,1024]{2,1,0:T(8,128)(2,1)} %collective-permute-done.5.refs_0_, bf16[16,16,1024]{2,1,0:T(8,128)(2,1)} %collective-permute-done.3.refs_1_, ...), custom_call_target="tpu_custom_call", output_to_operand_aliasing={{}: (7, {})} | custom-call | bytes 6291456 | tf_op jit(solution)/shard_map/pallas_call | solution.py:90
  147.3 0.6 broadcast_in_dim.112
  147.9 3.4 %all-to-all-start.6 = ((bf16[8,40,128]{2,1,0:T(8,128)(2,1)}), bf16[8,40,128]{2,1,0:T(8,128)(2,1)S(1)}, u32[]{:S(2)}, u32[]{:S(2)}) async-start(bf16[8,40,128]{2,1,0:T(8,128)(2,1)} %broadcast_in_dim.112), calls=%async_computation.6 | async-start | bytes 163840 | tf_op jit(solution)/shard_map/all_to_all | solution.py:289
  151.3 3.7 %collective-permute-start.6 = (bf16[16,16,1024]{2,1,0:T(8,128)(2,1)S(1)}, bf16[16,16,1024]{2,1,0:T(8,128)(2,1)S(1)}, u32[]{:S(2)}, u32[]{:S(2)}) collective-permute-start(bf16[16,16,1024]{2,1,0:T(8,128)(2,1)S(1)} %copy-done.4), channel_id=1, source_target_pairs={{0,20},{4,16},{8,28},{12,24},{16,4},{20,0},{24,12},{28,8},{1,21},{... | collective-permute-start | bytes 1572872 | tf_op jit(solution)/shard_map/ppermute | solution.py:334
  155.1 13.8 %all-to-all-done.6 = bf16[8,40,128]{2,1,0:T(8,128)(2,1)S(1)} async-done(((bf16[8,40,128]{2,1,0:T(8,128)(2,1)}), bf16[8,40,128]{2,1,0:T(8,128)(2,1)S(1)}, u32[]{:S(2)}, u32[]{:S(2)}) %all-to-all-start.6) | async-done | bytes 81952 | tf_op jit(solution)/shard_map/all_to_all | solution.py:289
  169.0 0.9 fusion
  169.9 3.3 %all-to-all-start.7 = ((f32[4,10,512]{2,1,0:T(8,128)}), f32[4,10,512]{2,1,0:T(8,128)S(1)}, u32[]{:S(2)}, u32[]{:S(2)}) async-start(f32[4,10,512]{2,1,0:T(8,128)} %fusion), calls=%async_computation.7 | async-start | bytes 262144 | tf_op jit(solution)/shard_map/all_to_all | solution.py:427
  173.3 0.6 reshape.177
  173.9 0.6 reshape.176
  174.5 3.3 %all-to-all-done.7 = f32[4,10,512]{2,1,0:T(8,128)S(1)} async-done(((f32[4,10,512]{2,1,0:T(8,128)}), f32[4,10,512]{2,1,0:T(8,128)S(1)}, u32[]{:S(2)}, u32[]{:S(2)}) %all-to-all-start.7) | async-done | bytes 81952 | tf_op jit(solution)/shard_map/all_to_all | solution.py:427
  177.8 0.6 reduce_sum.59
  178.5 1.5 collective-permute-done.6.refs_0_
  179.9 0.8 shard_map.160
  (72 shorter events, 3.1 us)
Async XLA Ops:
  0.6 168.3 %copy-start = (bf16[1024,512]{1,0:T(8,128)(2,1)S(1)}, bf16[1024,512]{1,0:T(8,128)(2,1)}, u32[]{:S(2)}) copy-start(bf16[1024,512]{1,0:T(8,128)(2,1)} %param.15) | copy-start | bytes 3145732
  0.6 27.7 %copy-start.9 = (bf16[1024,128]{1,0:T(8,128)(2,1)S(1)}, bf16[1024,128]{1,0:T(8,128)(2,1)}, u32[]{:S(2)}) copy-start(bf16[1024,128]{1,0:T(8,128)(2,1)} %param.14) | copy-start | bytes 786436
  2.1 26.1 %all-to-all-start = ((bf16[8,5,1024]{2,1,0:T(8,128)(2,1)}), bf16[8,5,1024]{2,1,0:T(8,128)(2,1)S(1)}, u32[]{:S(2)}, u32[]{:S(2)}) async-start(bf16[8,5,1024]{2,1,0:T(8,128)(2,1)} %broadcast_in_dim.54), calls=%async_computation | async-start | bytes 262144 | tf_op jit(solution)/shard_map/all_to_all | solution.py:289
  11.9 32.8 %copy-start.10 = (pred[40,128]{1,0:T(8,128)(4,1)S(1)}, pred[40,128]{1,0:T(8,128)(4,1)}, u32[]{:S(2)}) copy-start(pred[40,128]{1,0:T(8,128)(4,1)} %constant.71.clone) | copy-start | bytes 15364
  13.4 35.2 %copy-start.12 = (s32[128]{0:T(128)S(1)}, s32[128]{0:T(128)}, u32[]{:S(2)}) copy-start(s32[128]{0:T(128)} %param.18) | copy-start | bytes 1540
  13.4 2.2 %copy-start.1 = (bf16[128,16,1024]{2,1,0:T(8,128)(2,1)S(1)}, bf16[128,16,1024]{2,1,0:T(8,128)(2,1)}, u32[]{:S(2)}) copy-start(bf16[128,16,1024]{2,1,0:T(8,128)(2,1)} %pool_ref.1) | copy-start | bytes 12582916
  15.6 53.2 %copy-start.13 = (s32[8]{0:T(128)S(1)}, s32[8]{0:T(128)}, u32[]{:S(2)}) copy-start(s32[8]{0:T(128)} %param.19) | copy-start | bytes 100
  15.6 53.4 %copy-start.11 = (s32[128]{0:T(128)S(1)}, s32[128]{0:T(128)}, u32[]{:S(2)}) copy-start(s32[128]{0:T(128)} %param.17) | copy-start | bytes 1540
  15.6 53.6 %copy-start.14 = (s32[40,1]{0,1:T(1,128)S(1)}, s32[40,1]{0,1:T(1,128)}, u32[]{:S(2)}) copy-start(s32[40,1]{0,1:T(1,128)} %constant.77) | copy-start | bytes 484
  24.3 0.8 copy-start.3
  25.1 0.8 copy-start.5
  25.9 0.8 copy-start.6
  26.7 0.8 copy-start.7
  27.5 0.8 copy-start.8
  29.7 8.3 %all-to-all-start.1 = ((f32[4,40,256]{2,1,0:T(8,128)}), f32[4,40,256]{2,1,0:T(8,128)S(1)}, u32[]{:S(2)}, u32[]{:S(2)}) async-start(f32[4,40,256]{2,1,0:T(8,128)} %pad_maximum_fusion), calls=%async_computation.1 | async-start | bytes 327680 | tf_op jit(solution)/shard_map/all_to_all | solution.py:357
  38.7 25.8 %all-to-all-start.2 = ((bf16[8,48,256]{2,1,0:T(8,128)(2,1)}), bf16[8,48,256]{2,1,0:T(8,128)(2,1)S(1)}, u32[]{:S(2)}, u32[]{:S(2)}) async-start(bf16[8,48,256]{2,1,0:T(8,128)(2,1)} %fusion.3), calls=%async_computation.2 | async-start | bytes 393216 | tf_op jit(solution)/shard_map/all_to_all | solution.py:381
  44.7 51.3 %collective-permute-start = (bf16[16,16,1024]{2,1,0:T(8,128)(2,1)}, bf16[16,16,1024]{2,1,0:T(8,128)(2,1)S(1)}, u32[]{:S(2)}, u32[]{:S(2)}) collective-permute-start(bf16[16,16,1024]{2,1,0:T(8,128)(2,1)} %get-tuple-element.52), channel_id=1, source_target_pairs={{0,24},{4,28},{8,16},{12,20},{16,8},{20,12},{24,0},{28,4},{1,25},{... | collective-permute-start | bytes 1572872 | tf_op jit(solution)/shard_map/ppermute | solution.py:334
  65.3 10.2 %all-to-all-start.3 = ((bf16[4,8,40,128]{3,2,1,0:T(8,128)(2,1)}), bf16[4,8,40,128]{3,2,1,0:T(8,128)(2,1)S(1)}, u32[]{:S(2)}, u32[]{:S(2)}) async-start(bf16[4,8,40,128]{3,2,1,0:T(8,128)(2,1)} %broadcast_in_dim.106), calls=%async_computation.3 | async-start | bytes 655360 | tf_op jit(solution)/shard_map/all_to_all | solution.py:289
  75.5 2.2 %copy-start.2 = (bf16[128,16,1024]{2,1,0:T(8,128)(2,1)S(1)}, bf16[128,16,1024]{2,1,0:T(8,128)(2,1)}, u32[]{:S(2)}) copy-start(bf16[128,16,1024]{2,1,0:T(8,128)(2,1)} %pool_ref.1) | copy-start | bytes 12582916
  77.6 19.7 %copy-start.15 = (s32[8]{0:T(128)S(1)}, s32[8]{0:T(128)}, u32[]{:S(2)}) copy-start(s32[8]{0:T(128)} %param.21) | copy-start | bytes 100
  87.2 12.3 %all-to-all-start.4 = ((bf16[32,64,128]{2,1,0:T(8,128)(2,1)}), bf16[32,64,128]{2,1,0:T(8,128)(2,1)S(1)}, u32[]{:S(2)}, u32[]{:S(2)}) async-start(bf16[32,64,128]{2,1,0:T(8,128)(2,1)} %shard_map.156), calls=%async_computation.4 | async-start | bytes 1048576 | tf_op jit(solution)/shard_map/all_to_all | solution.py:418
  90.6 53.5 %collective-permute-start.1 = (bf16[16,16,1024]{2,1,0:T(8,128)(2,1)}, bf16[16,16,1024]{2,1,0:T(8,128)(2,1)S(1)}, u32[]{:S(2)}, u32[]{:S(2)}) collective-permute-start(bf16[16,16,1024]{2,1,0:T(8,128)(2,1)} %get-tuple-element.53), channel_id=1, source_target_pairs={{0,28},{4,24},{8,20},{12,16},{16,12},{20,8},{24,4},{28,0},{1,29},{... | collective-permute-start | bytes 1572872 | tf_op jit(solution)/shard_map/ppermute | solution.py:334
  92.4 51.7 %collective-permute-start.2 = (bf16[16,16,1024]{2,1,0:T(8,128)(2,1)}, bf16[16,16,1024]{2,1,0:T(8,128)(2,1)S(1)}, u32[]{:S(2)}, u32[]{:S(2)}) collective-permute-start(bf16[16,16,1024]{2,1,0:T(8,128)(2,1)} %copy-done.8), channel_id=1, source_target_pairs={{0,16},{4,20},{8,24},{12,28},{16,0},{20,4},{24,8},{28,12},{1,17},{... | collective-permute-start | bytes 1572872 | tf_op jit(solution)/shard_map/ppermute | solution.py:334
  92.5 51.6 %collective-permute-start.3 = (bf16[16,16,1024]{2,1,0:T(8,128)(2,1)}, bf16[16,16,1024]{2,1,0:T(8,128)(2,1)}, u32[]{:S(2)}, u32[]{:S(2)}) collective-permute-start(bf16[16,16,1024]{2,1,0:T(8,128)(2,1)} %copy-done.7), channel_id=1, source_target_pairs={{0,8},{4,12},{8,0},{12,4},{16,24},{20,28},{24,16},{28,20},{1,9},{5... | collective-permute-start | bytes 1572872 | tf_op jit(solution)/shard_map/ppermute | solution.py:334
  95.9 48.2 %collective-permute-start.4 = (bf16[16,16,1024]{2,1,0:T(8,128)(2,1)}, bf16[16,16,1024]{2,1,0:T(8,128)(2,1)}, u32[]{:S(2)}, u32[]{:S(2)}) collective-permute-start(bf16[16,16,1024]{2,1,0:T(8,128)(2,1)} %copy-done.6), channel_id=1, source_target_pairs={{0,12},{4,8},{8,4},{12,0},{16,28},{20,24},{24,20},{28,16},{1,13},{... | collective-permute-start | bytes 1572872 | tf_op jit(solution)/shard_map/ppermute | solution.py:334
  96.0 48.1 %collective-permute-start.5 = (bf16[16,16,1024]{2,1,0:T(8,128)(2,1)}, bf16[16,16,1024]{2,1,0:T(8,128)(2,1)}, u32[]{:S(2)}, u32[]{:S(2)}) collective-permute-start(bf16[16,16,1024]{2,1,0:T(8,128)(2,1)} %copy-done.5), channel_id=1, source_target_pairs={{0,4},{4,0},{8,12},{12,8},{16,20},{20,16},{24,28},{28,24},{1,5},{5... | collective-permute-start | bytes 1572872 | tf_op jit(solution)/shard_map/ppermute | solution.py:334
  100.6 43.3 %all-to-all-start.5 = ((bf16[8,64,128]{2,1,0:T(8,128)(2,1)}), bf16[8,64,128]{2,1,0:T(8,128)(2,1)S(1)}, u32[]{:S(2)}, u32[]{:S(2)}) async-start(bf16[8,64,128]{2,1,0:T(8,128)(2,1)} %shard_map.157), calls=%async_computation.5 | async-start | bytes 262144 | tf_op jit(solution)/shard_map/all_to_all | solution.py:420
  144.1 7.2 %copy-start.4 = (bf16[16,16,1024]{2,1,0:T(8,128)(2,1)S(1)}, bf16[16,16,1024]{2,1,0:T(8,128)(2,1)}, u32[]{:S(2)}) copy-start(bf16[16,16,1024]{2,1,0:T(8,128)(2,1)} %copy-done.3) | copy-start | bytes 1572868
  147.9 20.9 %all-to-all-start.6 = ((bf16[8,40,128]{2,1,0:T(8,128)(2,1)}), bf16[8,40,128]{2,1,0:T(8,128)(2,1)S(1)}, u32[]{:S(2)}, u32[]{:S(2)}) async-start(bf16[8,40,128]{2,1,0:T(8,128)(2,1)} %broadcast_in_dim.112), calls=%async_computation.6 | async-start | bytes 163840 | tf_op jit(solution)/shard_map/all_to_all | solution.py:289
  151.3 28.6 %collective-permute-start.6 = (bf16[16,16,1024]{2,1,0:T(8,128)(2,1)S(1)}, bf16[16,16,1024]{2,1,0:T(8,128)(2,1)S(1)}, u32[]{:S(2)}, u32[]{:S(2)}) collective-permute-start(bf16[16,16,1024]{2,1,0:T(8,128)(2,1)S(1)} %copy-done.4), channel_id=1, source_target_pairs={{0,20},{4,16},{8,28},{12,24},{16,4},{20,0},{24,12},{28,8},{1,21},{... | collective-permute-start | bytes 1572872 | tf_op jit(solution)/shard_map/ppermute | solution.py:334
  169.9 7.9 %all-to-all-start.7 = ((f32[4,10,512]{2,1,0:T(8,128)}), f32[4,10,512]{2,1,0:T(8,128)S(1)}, u32[]{:S(2)}, u32[]{:S(2)}) async-start(f32[4,10,512]{2,1,0:T(8,128)} %fusion), calls=%async_computation.7 | async-start | bytes 262144 | tf_op jit(solution)/shard_map/all_to_all | solution.py:427

commit v5 on v4

--- a/solution.py
+++ b/solution.py
@@ -19,6 +19,7 @@
 SCALE2 = math.log2(math.e) / math.sqrt(HD)
 STAT = 16
 MIB = 1024 * 1024
+PARTS = 2
 NT = (((1,), (1,)), ((), ()))
 
 
@@ -29,13 +30,16 @@
 def permute_kernel(source_ref, place_ref, pool_ref, out_ref, *refs):
     chunk_refs, (pages_ref, in_sem, out_sem) = refs[:-3], refs[-3:]
     count = chunk_refs[0].shape[0]
+    own = out_ref.at[pl.ds(place_ref[0] * (PARTS * count), PARTS * count)]
+    targets = [own.at[pl.ds(i * count, count)] for i in range(PARTS)] + list(chunk_refs)
 
     def start(j, carry):
-        pltpu.make_async_copy(pool_ref.at[source_ref[j]], pages_ref.at[j], in_sem.at[j // count]).start()
+        pltpu.make_async_copy(
+            pool_ref.at[source_ref[j]], pages_ref.at[j], in_sem.at[j // count]
+        ).start()
         return carry
 
     lax.fori_loop(0, pool_ref.shape[0], start, 0)
-    targets = [out_ref.at[pl.ds(place_ref[0] * count, count)], *chunk_refs]
     copies = []
     for c, target in enumerate(targets):
         held = pages_ref.at[pl.ds(c * count, count)]
@@ -50,19 +54,19 @@
     part = jax.ShapeDtypeStruct((pool.shape[0] // chunks,) + pool.shape[1:], pool.dtype)
     return pl.pallas_call(
         permute_kernel,
-        out_shape=[jax.ShapeDtypeStruct(pool.shape, pool.dtype)] + [part] * (chunks - 1),
+        out_shape=[jax.ShapeDtypeStruct(pool.shape, pool.dtype)] + [part] * (chunks - PARTS),
         in_specs=[
             pl.BlockSpec(memory_space=pltpu.SMEM),
             pl.BlockSpec(memory_space=pltpu.SMEM),
             pl.BlockSpec(memory_space=pltpu.HBM),
         ],
-        out_specs=[pl.BlockSpec(memory_space=pltpu.HBM)] * chunks,
+        out_specs=[pl.BlockSpec(memory_space=pltpu.HBM)] * (1 + chunks - PARTS),
         scratch_shapes=[
             pltpu.VMEM(pool.shape, pool.dtype),
             pltpu.SemaphoreType.DMA((chunks,)),
             pltpu.SemaphoreType.DMA((chunks,)),
         ],
-        compiler_params=pltpu.CompilerParams(vmem_limit_bytes=2 * pool.size + 2 * MIB),
+        compiler_params=pltpu.CompilerParams(vmem_limit_bytes=56 * MIB),
         cost_estimate=pl.CostEstimate(
             flops=0, bytes_accessed=2 * pool.size * 2, transcendentals=0
         ),
@@ -318,32 +322,41 @@
     )
     sent_req = jnp.sum(jnp.where(chosen, page_req[None, :], 0), axis=1)
     sent_idx = jnp.sum(jnp.where(chosen, page_idx[None, :], 0), axis=1)
-    moved_pool, *chunks = permute_pages(source_of, me.reshape(1), pool, wide)
+    moved_pool, *chunks = permute_pages(source_of, me.reshape(1), pool, wide * PARTS)
     arrived = {}
 
     exchange = functools.partial(lax.all_to_all, split_axis=0, concat_axis=0, tiled=True)
     flying = {}
 
     def members(groups):
-        return [d for group in groups for d in range(1, wide) if group_of(d, wide) == group]
+        return [
+            (d - 1) * PARTS + part
+            for group, part in groups
+            for d in range(1, wide)
+            if group_of(d, wide) == group
+        ]
 
     def launch(values, *groups):
         taken = members(groups)
-        values, sent = lax.optimization_barrier((values, [chunks[d - 1] for d in taken]))
-        for d, chunk in zip(taken, sent):
-            flying[d] = lax.ppermute(chunk, "wide", [(w, w ^ d) for w in range(wide)])
+        values, sent = lax.optimization_barrier((values, [chunks[c] for c in taken]))
+        for c, chunk in zip(taken, sent):
+            peer = 1 + c // PARTS
+            flying[c] = lax.ppermute(chunk, "wide", [(w, w ^ peer) for w in range(wide)])
         return values
 
     def land(values, *groups):
         taken = members(groups)
-        values, got = lax.optimization_barrier((values, [flying[d] for d in taken]))
+        values, got = lax.optimization_barrier((values, [flying[c] for c in taken]))
         arrived.update(zip(taken, got))
         return values
 
+    def beside(step, value, *groups):
+        return land(step(launch(value, *groups)), *groups)
+
     def placed(pages):
         taken = sorted(arrived)
-        place = jnp.stack([me ^ d for d in taken])
-        pages = place_pages(place, [arrived[d] for d in taken], pages)
+        place = jnp.stack([(me ^ (1 + c // PARTS)) * PARTS + c % PARTS for c in taken])
+        pages = place_pages(place, [arrived[c] for c in taken], pages)
         arrived.clear()
         return pages
 
@@ -354,7 +367,7 @@
     partial = jnp.concatenate(
         [query_part, jnp.broadcast_to(keyval_part[None], (narrow,) + keyval_part.shape)], axis=2
     )
-    partial = exchange(launch(partial, 6), "narrow")
+    partial = beside(lambda value: exchange(value, "narrow"), partial, (6, 0), (1, 0))
     projected = jnp.sum(partial, axis=0).astype(jnp.bfloat16)
     shifted = sent_idx + 1
     tags = jnp.concatenate(
@@ -375,10 +388,7 @@
         ],
         axis=1,
     )
-    packed, page_req, page_idx, lengths = lax.optimization_barrier(
-        (packed, page_req, page_idx, lengths)
-    )
-    received = exchange(packed, "wide")
+    received = beside(lambda value: exchange(value, "wide"), packed, (6, 1))
     req_tok = jnp.broadcast_to(page_req[:, None], (slots, PAGE)).reshape(1, -1)
     pos_tok = (page_idx[:, None] * PAGE + jnp.arange(PAGE, dtype=jnp.int32)[None, :]).reshape(1, -1)
     row_info = jnp.stack(
@@ -388,8 +398,9 @@
         ],
         axis=1,
     )
-    req_tok, pos_tok, row_info = launch((req_tok, pos_tok, row_info), 7, 4, 2, 3, 1)
-    queries = spread(received[:, :rows, :own_cols], "narrow")
+    queries = beside(
+        lambda value: spread(value, "narrow"), received[:, :rows, :own_cols], (7, 0), (2, 0)
+    )
     if own_cols == HD:
         queries = jnp.transpose(queries, (1, 0, 2, 3))
     else:
@@ -412,22 +423,27 @@
     piece = HEADS * rows // (wide * narrow)
     new_keyval = jnp.pad(keyval, ((0, extra - rows), (0, 0)))
     tokens = pool.reshape(slots * PAGE, -1)
-    parts = attend(
-        queries, new_keyval, tokens, req_tok, pos_tok, row_info, new_bias, rows, piece
-    )
-    parts = exchange(parts, "narrow")
+    parts = beside(
+        lambda value: attend(
+            value, new_keyval, tokens, req_tok, pos_tok, row_info, new_bias, rows, piece
+        ),
+        queries,
+        (7, 1),
+        (2, 1),
+        (1, 1),
+    )
+    parts = beside(lambda value: exchange(value, "narrow"), parts, (4, 0), (3, 0))
     parts = combine(parts.reshape((narrow, wide) + parts.shape[1:]), piece, False)
-    attn = combine(exchange(parts, "wide")[:, None], piece, True)
-    attn = land(attn, 6, 7, 4, 2, 3, 1)
-    moved_pool = launch(placed(moved_pool), 5)
-    attn = spread(attn, "wide")
+    parts = beside(lambda value: exchange(value, "wide"), parts, (4, 1))
+    attn = combine(parts[:, None], piece, True)
+    attn = beside(lambda value: spread(value, "wide"), attn, (5, 0))
+    moved_pool = placed(moved_pool)
     attn = jnp.transpose(attn.reshape(-1, rows, HD), (1, 0, 2)).reshape(rows, -1)
     sums = jnp.dot(attn, w_out, preferred_element_type=jnp.float32)
     sums = sums.reshape(narrow, rows // narrow, -1)
-    sums = exchange(sums, "narrow")
+    sums = beside(lambda value: exchange(value, "narrow"), sums, (5, 1), (3, 1))
     attended = jnp.sum(sums, axis=0).astype(jnp.bfloat16)
 
-    attended = land(attended, 5)
     moved_pool = placed(moved_pool)
 
     local_req = local_rows // STEPS

time: 182 us -> 172 us (0.945)
  waiting for transfers between devices: 85 us -> 61.7 us
  starting transfers between devices: 47.9 us -> 62.5 us
  Pallas kernels: 23.5 us -> 19.9 us
    all_to_all x5, waiting for transfers between devices: 63.7 us -> 12.8 us  [the longest x1 11.3 us: on_device(): parts = beside(lambda value: exchange(value, 'wide'), parts, (4, 1))]
    ppermute x7 -> x14, waiting for transfers between devices: 1.47 us -> 40.7 us  [launch(): lax.ppermute(chunk, 'wide', [(w, w ^ peer) for w in range(wide)])]
    all_to_all x3, waiting for transfers between devices: 19.8 us -> 8.2 us  [spread(): lax.all_to_all(jnp.broadcast_to(block[None], (count,) + block.shape), axi...]
    ppermute x7 -> x14, starting transfers between devices: 14.3 us -> 25.3 us  [launch(): lax.ppermute(chunk, 'wide', [(w, w ^ peer) for w in range(wide)])]
    pallas_call x1, Pallas kernels: 8.64 us -> 4.5 us  [permute_pages(): pl.pallas_call(permute_kernel, out_shape=[jax.ShapeDtypeStruct(pool.shape...]
    all_to_all x5, starting transfers between devices: 19.5 us -> 21.7 us  [the longest x1 7.18 us: on_device(): received = beside(lambda value: exchange(value, 'wide'), packed, (6, 1))]
    unnamed x33 -> x39, local copies, waits for them, and re-layouts: 8.41 us -> 8.15 us
  transfers between devices with their start and end apart: 15 -> 22, of which waited for: 8 -> 12; matrix products, arithmetic and copies ran while one was open for 6% -> 7% of each run, Pallas kernels for 11% -> 10%
where the time goes in v5:
time: 172 us; the launch traced here: 171 us
  starting transfers between devices  62.5 us (36%)
  waiting for transfers between devices  61.7 us (36%)
  Pallas kernels  19.9 us (12%)
  local copies, waits for them, and re-layouts  17.1 us (10%)
  other arithmetic  7.23 us (4%)
    ppermute x14, waiting for transfers between devices, launch(): lax.ppermute(chunk, 'wide', [(w, w ^ peer) for w in range(wide)])  40.7 us
    ppermute x14, starting transfers between devices, launch(): lax.ppermute(chunk, 'wide', [(w, w ^ peer) for w in range(wide)])  25.3 us
    all_to_all x3, starting transfers between devices, spread(): lax.all_to_all(jnp.broadcast_to(block[None], (count,) + block.shape), axi...  15.5 us
    all_to_all x1, waiting for transfers between devices, on_device(): parts = beside(lambda value: exchange(value, 'wide'), parts, (4, 1))  11.3 us
    pallas_call x1, Pallas kernels, attend(): pl.pallas_call(functools.partial(attend_kernel, rows, piece), grid=(KVH,)...  9.52 us
    all_to_all x3, waiting for transfers between devices, spread(): lax.all_to_all(jnp.broadcast_to(block[None], (count,) + block.shape), axi...  8.2 us
    unnamed x39, local copies, waits for them, and re-layouts  8.15 us
    all_to_all x1, starting transfers between devices, on_device(): received = beside(lambda value: exchange(value, 'wide'), packed, (6, 1))  7.18 us
  transfers between devices with their start and end apart: 22, of which 12 were waited for; matrix products, arithmetic and copies ran while one was open for 7% of the time, Pallas kernels for 10%

profile of v5, /device:TPU:0, one launch (start us, length us, event | category | flops | bytes accessed | tf_op | source)
XLA Modules:
  0.0 171.0 jit_solution(15957522624705336449)
XLA Ops:
  0.7 1.5 broadcast_in_dim.54
  2.1 7.3 %all-to-all-start = ((bf16[8,5,1024]{2,1,0:T(8,128)(2,1)}), bf16[8,5,1024]{2,1,0:T(8,128)(2,1)S(1)}, u32[]{:S(2)}, u32[]{:S(2)}) async-start(bf16[8,5,1024]{2,1,0:T(8,128)(2,1)} %broadcast_in_dim.54), calls=%async_computation | async-start | bytes 262144 | tf_op jit(solution)/shard_map/all_to_all | solution.py:293
  9.4 0.9 convert_reduce_fusion
  11.0 1.3 select_reduce_fusion.1
  12.4 1.5 copy.41
  13.9 4.5 %shard_map.155 = (bf16[128,16,1024]{2,1,0:T(8,128)(2,1)}, bf16[8,16,1024]{2,1,0:T(8,128)(2,1)}, bf16[8,16,1024]{2,1,0:T(8,128)(2,1)}, bf16[8,16,1024]{2,1,0:T(8,...) custom-call(s32[128]{0:T(128)} %get-tuple-element.134.source_ref, ...), custom_call_target="tpu_custom_call" | custom-call | bytes 8388608 | tf_op jit(solution)/shard_map/pallas_call | solution.py:55
  19.9 3.3 %all-to-all-start.1 = ((f32[4,40,256]{2,1,0:T(8,128)}), f32[4,40,256]{2,1,0:T(8,128)S(1)}, u32[]{:S(2)}, u32[]{:S(2)}) async-start(f32[4,40,256]{2,1,0:T(8,128)} %pad_maximum_fusion), calls=%async_computation.1 | async-start | bytes 327680 | tf_op jit(solution)/shard_map/all_to_all | solution.py:370
  23.2 3.9 %collective-permute-start = (bf16[8,16,1024]{2,1,0:T(8,128)(2,1)}, bf16[8,16,1024]{2,1,0:T(8,128)(2,1)S(1)}, u32[]{:S(2)}, u32[]{:S(2)}) collective-permute-start(bf16[8,16,1024]{2,1,0:T(8,128)(2,1)} %get-tuple-element.67), channel_id=1, source_target_pairs={{0,24},{4,28},{8,16},{12,20},{16,8},{20,12},{24,0},{28,4},{1,25},{... | collective-permute-start | bytes 786440 | tf_op jit(solution)/shard_map/ppermute | solution.py:344
  27.1 1.5 collective-permute-start.1
  28.8 5.5 %collective-permute-done.refs_8_ = bf16[8,16,1024]{2,1,0:T(8,128)(2,1)S(1)} collective-permute-done((bf16[8,16,1024]{2,1,0:T(8,128)(2,1)}, bf16[8,16,1024]{2,1,0:T(8,128)(2,1)S(1)}, u32[]{:S(2)}, u32[]{:S(2)}) %collective-permute-start) | collective-permute-done | bytes 262176 | tf_op jit(solution)/shard_map/ppermute | solution.py:344
  34.3 1.4 collective-permute-done.1.refs_0_
  36.4 7.2 %all-to-all-start.2 = ((bf16[8,48,256]{2,1,0:T(8,128)(2,1)}), bf16[8,48,256]{2,1,0:T(8,128)(2,1)S(1)}, u32[]{:S(2)}, u32[]{:S(2)}) async-start(bf16[8,48,256]{2,1,0:T(8,128)(2,1)} %fusion.3), calls=%async_computation.2 | async-start | bytes 393216 | tf_op jit(solution)/shard_map/all_to_all | solution.py:391
  43.6 3.8 %collective-permute-start.2 = (bf16[8,16,1024]{2,1,0:T(8,128)(2,1)}, bf16[8,16,1024]{2,1,0:T(8,128)(2,1)S(1)}, u32[]{:S(2)}, u32[]{:S(2)}) collective-permute-start(bf16[8,16,1024]{2,1,0:T(8,128)(2,1)} %get-tuple-element.72), channel_id=1, source_target_pairs={{0,24},{4,28},{8,16},{12,20},{16,8},{20,12},{24,0},{28,4},{1,25},{... | collective-permute-start | bytes 786440 | tf_op jit(solution)/shard_map/ppermute | solution.py:344
  47.6 8.8 %collective-permute-done.2.refs_9_ = bf16[8,16,1024]{2,1,0:T(8,128)(2,1)S(1)} collective-permute-done((bf16[8,16,1024]{2,1,0:T(8,128)(2,1)}, bf16[8,16,1024]{2,1,0:T(8,128)(2,1)S(1)}, u32[]{:S(2)}, u32[]{:S(2)}) %collective-permute-start.2) | collective-permute-done | bytes 262176 | tf_op jit(solution)/shard_map/ppermute | solution.py:344
  56.4 1.5 all-to-all-done.2
  57.9 0.8 broadcast_in_dim.106
  58.7 3.5 %all-to-all-start.3 = ((bf16[4,8,40,128]{3,2,1,0:T(8,128)(2,1)}), bf16[4,8,40,128]{3,2,1,0:T(8,128)(2,1)S(1)}, u32[]{:S(2)}, u32[]{:S(2)}) async-start(bf16[4,8,40,128]{3,2,1,0:T(8,128)(2,1)} %broadcast_in_dim.106), calls=%async_computation.3 | async-start | bytes 655360 | tf_op jit(solution)/shard_map/all_to_all | solution.py:293
  62.2 1.6 collective-permute-start.3
  63.8 4.7 %collective-permute-start.4 = (bf16[8,16,1024]{2,1,0:T(8,128)(2,1)}, bf16[8,16,1024]{2,1,0:T(8,128)(2,1)S(1)}, u32[]{:S(2)}, u32[]{:S(2)}) collective-permute-start(bf16[8,16,1024]{2,1,0:T(8,128)(2,1)} %get-tuple-element.78), channel_id=1, source_target_pairs={{0,8},{4,12},{8,0},{12,4},{16,24},{20,28},{24,16},{28,20},{1,9},{5... | collective-permute-start | bytes 786440 | tf_op jit(solution)/shard_map/ppermute | solution.py:344
  69.0 5.3 %collective-permute-done.3.refs_10_ = bf16[8,16,1024]{2,1,0:T(8,128)(2,1)S(1)} collective-permute-done((bf16[8,16,1024]{2,1,0:T(8,128)(2,1)}, bf16[8,16,1024]{2,1,0:T(8,128)(2,1)S(1)}, u32[]{:S(2)}, u32[]{:S(2)}) %collective-permute-start.3) | collective-permute-done | bytes 262176 | tf_op jit(solution)/shard_map/ppermute | solution.py:344
  74.3 4.9 %collective-permute-done.4.refs_2_ = bf16[8,16,1024]{2,1,0:T(8,128)(2,1)S(1)} collective-permute-done((bf16[8,16,1024]{2,1,0:T(8,128)(2,1)}, bf16[8,16,1024]{2,1,0:T(8,128)(2,1)S(1)}, u32[]{:S(2)}, u32[]{:S(2)}) %collective-permute-start.4) | collective-permute-done | bytes 262176 | tf_op jit(solution)/shard_map/ppermute | solution.py:344
  79.9 0.8 collective-permute-start.6
  80.7 1.2 collective-permute-start.7
  82.0 2.2 %copy-done.1 = bf16[128,16,1024]{2,1,0:T(8,128)(2,1)S(1)} copy-done((bf16[128,16,1024]{2,1,0:T(8,128)(2,1)S(1)}, bf16[128,16,1024]{2,1,0:T(8,128)(2,1)}, u32[]{:S(2)}) %copy-start.1) | copy-done | bytes 4194328
  84.2 9.5 %shard_map.156 = bf16[32,64,128]{2,1,0:T(8,128)(2,1)} custom-call(bf16[4,320,128]{2,1,0:T(8,128)(2,1)S(1)} %bitcast.56, bf16[2048,1024]{1,0:T(8,128)(2,1)S(1)} %bitcast.53, bf16[2048,1024]{1,0:T(8,128)(2,1)S(1)} %bitcast.54, bf16[128,1024]{1,0:T(8,128)(2,1)S(1)} %pad.9.new_key_ref.new_value_ref, bf16[128,1024]{1,0:T(8,128)(2,1)S(1)} %pad.9.new_key_ref.new_value_ref, ...), custom_call_target="tpu_custom_call" | custom-call | flops 1426063360 | bytes 4194304 | tf_op jit(solution)/shard_map/pallas_call | solution.py:207
  94.8 3.5 %all-to-all-start.4 = ((bf16[32,64,128]{2,1,0:T(8,128)(2,1)}), bf16[32,64,128]{2,1,0:T(8,128)(2,1)S(1)}, u32[]{:S(2)}, u32[]{:S(2)}) async-start(bf16[32,64,128]{2,1,0:T(8,128)(2,1)} %shard_map.156), calls=%async_computation.4 | async-start | bytes 1048576 | tf_op jit(solution)/shard_map/all_to_all | solution.py:435
  98.2 3.0 %collective-permute-start.8 = (bf16[8,16,1024]{2,1,0:T(8,128)(2,1)}, bf16[8,16,1024]{2,1,0:T(8,128)(2,1)S(1)}, u32[]{:S(2)}, u32[]{:S(2)}) collective-permute-start(bf16[8,16,1024]{2,1,0:T(8,128)(2,1)} %get-tuple-element.91), channel_id=1, source_target_pairs={{0,16},{4,20},{8,24},{12,28},{16,0},{20,4},{24,8},{28,12},{1,17},{... | collective-permute-start | bytes 786440 | tf_op jit(solution)/shard_map/ppermute | solution.py:344
  101.9 12.1 %collective-permute-done.8.refs_5_ = bf16[8,16,1024]{2,1,0:T(8,128)(2,1)S(1)} collective-permute-done((bf16[8,16,1024]{2,1,0:T(8,128)(2,1)}, bf16[8,16,1024]{2,1,0:T(8,128)(2,1)S(1)}, u32[]{:S(2)}, u32[]{:S(2)}) %collective-permute-start.8) | collective-permute-done | bytes 262176 | tf_op jit(solution)/shard_map/ppermute | solution.py:344
  114.0 0.7 copy-done.4
  114.7 1.1 collective-permute-done.9.refs_4_
  115.8 0.7 copy-done.6
  116.5 1.1 shard_map.157
  117.6 4.4 %all-to-all-start.5 = ((bf16[8,64,128]{2,1,0:T(8,128)(2,1)}), bf16[8,64,128]{2,1,0:T(8,128)(2,1)S(1)}, u32[]{:S(2)}, u32[]{:S(2)}) async-start(bf16[8,64,128]{2,1,0:T(8,128)(2,1)} %shard_map.157), calls=%async_computation.5 | async-start | bytes 262144 | tf_op jit(solution)/shard_map/all_to_all | solution.py:437
  123.3 11.3 %all-to-all-done.5 = bf16[8,64,128]{2,1,0:T(8,128)(2,1)S(1)} async-done(((bf16[8,64,128]{2,1,0:T(8,128)(2,1)}), bf16[8,64,128]{2,1,0:T(8,128)(2,1)S(1)}, u32[]{:S(2)}, u32[]{:S(2)}) %all-to-all-start.5) | async-done | bytes 131104 | tf_op jit(solution)/shard_map/all_to_all | solution.py:437
  135.4 1.7 copy.40
  137.9 4.8 %all-to-all-start.6 = ((bf16[8,40,128]{2,1,0:T(8,128)(2,1)}), bf16[8,40,128]{2,1,0:T(8,128)(2,1)S(1)}, u32[]{:S(2)}, u32[]{:S(2)}) async-start(bf16[8,40,128]{2,1,0:T(8,128)(2,1)} %broadcast_in_dim.112), calls=%async_computation.6 | async-start | bytes 163840 | tf_op jit(solution)/shard_map/all_to_all | solution.py:293
  143.3 8.2 %all-to-all-done.6 = bf16[8,40,128]{2,1,0:T(8,128)(2,1)S(1)} async-done(((bf16[8,40,128]{2,1,0:T(8,128)(2,1)}), bf16[8,40,128]{2,1,0:T(8,128)(2,1)S(1)}, u32[]{:S(2)}, u32[]{:S(2)}) %all-to-all-start.6) | async-done | bytes 81952 | tf_op jit(solution)/shard_map/all_to_all | solution.py:293
  151.6 0.9 fusion
  152.6 0.9 collective-permute-start.12
  153.5 2.1 %collective-permute-start.13 = (bf16[8,16,1024]{2,1,0:T(8,128)(2,1)}, bf16[8,16,1024]{2,1,0:T(8,128)(2,1)}, u32[]{:S(2)}, u32[]{:S(2)}) collective-permute-start(bf16[8,16,1024]{2,1,0:T(8,128)(2,1)} %get-tuple-element.106), channel_id=1, source_target_pairs={{0,12},{4,8},{8,4},{12,0},{16,28},{20,24},{24,20},{28,16},{1,13},{... | collective-permute-start | bytes 786440 | tf_op jit(solution)/shard_map/ppermute | solution.py:344
  156.3 3.3 %all-to-all-start.7 = ((f32[4,10,512]{2,1,0:T(8,128)}), f32[4,10,512]{2,1,0:T(8,128)S(1)}, u32[]{:S(2)}, u32[]{:S(2)}) async-start(f32[4,10,512]{2,1,0:T(8,128)} %fusion), calls=%async_computation.7 | async-start | bytes 262144 | tf_op jit(solution)/shard_map/all_to_all | solution.py:444
  160.9 0.9 copy-done.3
  161.8 0.9 copy-done.5
  162.8 0.9 copy-done.7
  163.7 0.9 copy-done.9
  164.7 2.7 %shard_map.159.refs_2_ = bf16[128,16,1024]{2,1,0:T(8,128)(2,1)} custom-call(s32[12]{0:T(128)S(1)} %stack.71.place_ref, bf16[8,16,1024]{2,1,0:T(8,128)(2,1)S(1)} %collective-permute-done.1.refs_0_, bf16[8,16,1024]{2,1,0:T(8,128)(2,1)S(1)} %copy-done.3, bf16[8,16,1024]{2,1,0:T(8,128)(2,1)S(1)} %collective-permute-done.4.refs_2_, ...), custom_call_target="tpu_custom_call", output_to_operand_aliasing={{}: (13, {})} | custom-call | bytes 6291456 | tf_op jit(solution)/shard_map/pallas_call | solution.py:94
  167.4 1.1 collective-permute-done.12.refs_1_
  169.1 1.8 %shard_map.160 = bf16[128,16,1024]{2,1,0:T(8,128)(2,1)} custom-call(s32[2]{0:T(128)S(1)} %pad_add_fusion.1.place_ref, bf16[8,16,1024]{2,1,0:T(8,128)(2,1)} %collective-permute-done.13.refs_0_, bf16[8,16,1024]{2,1,0:T(8,128)(2,1)} %collective-permute-done.12.refs_1_, bf16[128,16,1024]{2,1,0:T(8,128)(2,1)} %shard_map.159.refs_2_), custom_call_target="tpu_custom_call", output_to_operand_aliasing={{}: (3, {})} | custom-call | bytes 1048576 | tf_op jit(solution)/shard_map/pallas_call | solution.py:94
  (93 shorter events, 12.3 us)
Async XLA Ops:
  0.6 151.0 %copy-start = (bf16[1024,512]{1,0:T(8,128)(2,1)S(1)}, bf16[1024,512]{1,0:T(8,128)(2,1)}, u32[]{:S(2)}) copy-start(bf16[1024,512]{1,0:T(8,128)(2,1)} %param.15) | copy-start | bytes 3145732
  0.6 17.9 %copy-start.11 = (bf16[1024,128]{1,0:T(8,128)(2,1)S(1)}, bf16[1024,128]{1,0:T(8,128)(2,1)}, u32[]{:S(2)}) copy-start(bf16[1024,128]{1,0:T(8,128)(2,1)} %param.14) | copy-start | bytes 786436
  2.1 16.3 %all-to-all-start = ((bf16[8,5,1024]{2,1,0:T(8,128)(2,1)}), bf16[8,5,1024]{2,1,0:T(8,128)(2,1)S(1)}, u32[]{:S(2)}, u32[]{:S(2)}) async-start(bf16[8,5,1024]{2,1,0:T(8,128)(2,1)} %broadcast_in_dim.54), calls=%async_computation | async-start | bytes 262144 | tf_op jit(solution)/shard_map/all_to_all | solution.py:293
  13.9 33.5 %copy-start.14 = (s32[8]{0:T(128)S(1)}, s32[8]{0:T(128)}, u32[]{:S(2)}) copy-start(s32[8]{0:T(128)} %param.19) | copy-start | bytes 100
  13.9 33.7 %copy-start.15 = (s32[128]{0:T(128)S(1)}, s32[128]{0:T(128)}, u32[]{:S(2)}) copy-start(s32[128]{0:T(128)} %param.18) | copy-start | bytes 1540
  13.9 54.6 %copy-start.16 = (s32[40,1]{0,1:T(1,128)S(1)}, s32[40,1]{0,1:T(1,128)}, u32[]{:S(2)}) copy-start(s32[40,1]{0,1:T(1,128)} %constant.77) | copy-start | bytes 484
  13.9 54.8 %copy-start.13 = (s32[128]{0:T(128)S(1)}, s32[128]{0:T(128)}, u32[]{:S(2)}) copy-start(s32[128]{0:T(128)} %param.17) | copy-start | bytes 1540
  18.4 62.3 %copy-start.17 = (bf16[8,16,1024]{2,1,0:T(8,128)(2,1)S(1)}, bf16[8,16,1024]{2,1,0:T(8,128)(2,1)}, u32[]{:S(2)}) copy-start(bf16[8,16,1024]{2,1,0:T(8,128)(2,1)} %get-tuple-element.86) | copy-start | bytes 786436
  18.5 63.5 %copy-start.12 = (pred[40,128]{1,0:T(8,128)(4,1)S(1)}, pred[40,128]{1,0:T(8,128)(4,1)}, u32[]{:S(2)}) copy-start(pred[40,128]{1,0:T(8,128)(4,1)} %constant.71.clone) | copy-start | bytes 15364
  19.9 8.9 %all-to-all-start.1 = ((f32[4,40,256]{2,1,0:T(8,128)}), f32[4,40,256]{2,1,0:T(8,128)S(1)}, u32[]{:S(2)}, u32[]{:S(2)}) async-start(f32[4,40,256]{2,1,0:T(8,128)} %pad_maximum_fusion), calls=%async_computation.1 | async-start | bytes 327680 | tf_op jit(solution)/shard_map/all_to_all | solution.py:370
  23.2 11.1 %collective-permute-start = (bf16[8,16,1024]{2,1,0:T(8,128)(2,1)}, bf16[8,16,1024]{2,1,0:T(8,128)(2,1)S(1)}, u32[]{:S(2)}, u32[]{:S(2)}) collective-permute-start(bf16[8,16,1024]{2,1,0:T(8,128)(2,1)} %get-tuple-element.67), channel_id=1, source_target_pairs={{0,24},{4,28},{8,16},{12,20},{16,8},{20,12},{24,0},{28,4},{1,25},{... | collective-permute-start | bytes 786440 | tf_op jit(solution)/shard_map/ppermute | solution.py:344
  27.1 8.6 %collective-permute-start.1 = (bf16[8,16,1024]{2,1,0:T(8,128)(2,1)}, bf16[8,16,1024]{2,1,0:T(8,128)(2,1)S(1)}, u32[]{:S(2)}, u32[]{:S(2)}) collective-permute-start(bf16[8,16,1024]{2,1,0:T(8,128)(2,1)} %get-tuple-element.68), channel_id=1, source_target_pairs={{0,4},{4,0},{8,12},{12,8},{16,20},{20,16},{24,28},{28,24},{1,5},{5... | collective-permute-start | bytes 786440 | tf_op jit(solution)/shard_map/ppermute | solution.py:344
  36.4 21.5 %all-to-all-start.2 = ((bf16[8,48,256]{2,1,0:T(8,128)(2,1)}), bf16[8,48,256]{2,1,0:T(8,128)(2,1)S(1)}, u32[]{:S(2)}, u32[]{:S(2)}) async-start(bf16[8,48,256]{2,1,0:T(8,128)(2,1)} %fusion.3), calls=%async_computation.2 | async-start | bytes 393216 | tf_op jit(solution)/shard_map/all_to_all | solution.py:391
  43.6 12.8 %collective-permute-start.2 = (bf16[8,16,1024]{2,1,0:T(8,128)(2,1)}, bf16[8,16,1024]{2,1,0:T(8,128)(2,1)S(1)}, u32[]{:S(2)}, u32[]{:S(2)}) collective-permute-start(bf16[8,16,1024]{2,1,0:T(8,128)(2,1)} %get-tuple-element.72), channel_id=1, source_target_pairs={{0,24},{4,28},{8,16},{12,20},{16,8},{20,12},{24,0},{28,4},{1,25},{... | collective-permute-start | bytes 786440 | tf_op jit(solution)/shard_map/ppermute | solution.py:344
  57.9 0.8 copy-start.10
  58.7 10.3 %all-to-all-start.3 = ((bf16[4,8,40,128]{3,2,1,0:T(8,128)(2,1)}), bf16[4,8,40,128]{3,2,1,0:T(8,128)(2,1)S(1)}, u32[]{:S(2)}, u32[]{:S(2)}) async-start(bf16[4,8,40,128]{3,2,1,0:T(8,128)(2,1)} %broadcast_in_dim.106), calls=%async_computation.3 | async-start | bytes 655360 | tf_op jit(solution)/shard_map/all_to_all | solution.py:293
  62.2 12.1 %collective-permute-start.3 = (bf16[8,16,1024]{2,1,0:T(8,128)(2,1)}, bf16[8,16,1024]{2,1,0:T(8,128)(2,1)S(1)}, u32[]{:S(2)}, u32[]{:S(2)}) collective-permute-start(bf16[8,16,1024]{2,1,0:T(8,128)(2,1)} %get-tuple-element.77), channel_id=1, source_target_pairs={{0,28},{4,24},{8,20},{12,16},{16,12},{20,8},{24,4},{28,0},{1,29},{... | collective-permute-start | bytes 786440 | tf_op jit(solution)/shard_map/ppermute | solution.py:344
  63.8 15.4 %collective-permute-start.4 = (bf16[8,16,1024]{2,1,0:T(8,128)(2,1)}, bf16[8,16,1024]{2,1,0:T(8,128)(2,1)S(1)}, u32[]{:S(2)}, u32[]{:S(2)}) collective-permute-start(bf16[8,16,1024]{2,1,0:T(8,128)(2,1)} %get-tuple-element.78), channel_id=1, source_target_pairs={{0,8},{4,12},{8,0},{12,4},{16,24},{20,28},{24,16},{28,20},{1,9},{5... | collective-permute-start | bytes 786440 | tf_op jit(solution)/shard_map/ppermute | solution.py:344
  79.3 14.5 %collective-permute-start.5 = (bf16[8,16,1024]{2,1,0:T(8,128)(2,1)}, bf16[8,16,1024]{2,1,0:T(8,128)(2,1)S(1)}, u32[]{:S(2)}, u32[]{:S(2)}) collective-permute-start(bf16[8,16,1024]{2,1,0:T(8,128)(2,1)} %get-tuple-element.84), channel_id=1, source_target_pairs={{0,28},{4,24},{8,20},{12,16},{16,12},{20,8},{24,4},{28,0},{1,29},{... | collective-permute-start | bytes 786440 | tf_op jit(solution)/shard_map/ppermute | solution.py:344
  79.9 13.8 %collective-permute-start.6 = (bf16[8,16,1024]{2,1,0:T(8,128)(2,1)}, bf16[8,16,1024]{2,1,0:T(8,128)(2,1)S(1)}, u32[]{:S(2)}, u32[]{:S(2)}) collective-permute-start(bf16[8,16,1024]{2,1,0:T(8,128)(2,1)} %get-tuple-element.85), channel_id=1, source_target_pairs={{0,8},{4,12},{8,0},{12,4},{16,24},{20,28},{24,16},{28,20},{1,9},{5... | collective-permute-start | bytes 786440 | tf_op jit(solution)/shard_map/ppermute | solution.py:344
  80.7 13.3 %collective-permute-start.7 = (bf16[8,16,1024]{2,1,0:T(8,128)(2,1)S(1)}, bf16[8,16,1024]{2,1,0:T(8,128)(2,1)S(1)}, u32[]{:S(2)}, u32[]{:S(2)}) collective-permute-start(bf16[8,16,1024]{2,1,0:T(8,128)(2,1)S(1)} %copy-done.17), channel_id=1, source_target_pairs={{0,4},{4,0},{8,12},{12,8},{16,20},{20,16},{24,28},{28,24},{1,5},{5... | collective-permute-start | bytes 786440 | tf_op jit(solution)/shard_map/ppermute | solution.py:344
  82.0 2.2 %copy-start.1 = (bf16[128,16,1024]{2,1,0:T(8,128)(2,1)S(1)}, bf16[128,16,1024]{2,1,0:T(8,128)(2,1)}, u32[]{:S(2)}) copy-start(bf16[128,16,1024]{2,1,0:T(8,128)(2,1)} %pool_ref.1) | copy-start | bytes 12582916
  84.2 37.8 %copy-start.18 = (s32[8]{0:T(128)S(1)}, s32[8]{0:T(128)}, u32[]{:S(2)}) copy-start(s32[8]{0:T(128)} %param.21) | copy-start | bytes 100
  94.1 0.7 copy-start.2
  94.8 21.8 %all-to-all-start.4 = ((bf16[32,64,128]{2,1,0:T(8,128)(2,1)}), bf16[32,64,128]{2,1,0:T(8,128)(2,1)S(1)}, u32[]{:S(2)}, u32[]{:S(2)}) async-start(bf16[32,64,128]{2,1,0:T(8,128)(2,1)} %shard_map.156), calls=%async_computation.4 | async-start | bytes 1048576 | tf_op jit(solution)/shard_map/all_to_all | solution.py:435
  98.2 15.8 %collective-permute-start.8 = (bf16[8,16,1024]{2,1,0:T(8,128)(2,1)}, bf16[8,16,1024]{2,1,0:T(8,128)(2,1)S(1)}, u32[]{:S(2)}, u32[]{:S(2)}) collective-permute-start(bf16[8,16,1024]{2,1,0:T(8,128)(2,1)} %get-tuple-element.91), channel_id=1, source_target_pairs={{0,16},{4,20},{8,24},{12,28},{16,0},{20,4},{24,8},{28,12},{1,17},{... | collective-permute-start | bytes 786440 | tf_op jit(solution)/shard_map/ppermute | solution.py:344
  101.2 14.6 %collective-permute-start.9 = (bf16[8,16,1024]{2,1,0:T(8,128)(2,1)}, bf16[8,16,1024]{2,1,0:T(8,128)(2,1)S(1)}, u32[]{:S(2)}, u32[]{:S(2)}) collective-permute-start(bf16[8,16,1024]{2,1,0:T(8,128)(2,1)} %get-tuple-element.92), channel_id=1, source_target_pairs={{0,12},{4,8},{8,4},{12,0},{16,28},{20,24},{24,20},{28,16},{1,13},{... | collective-permute-start | bytes 786440 | tf_op jit(solution)/shard_map/ppermute | solution.py:344
  114.0 0.7 copy-start.4
  115.8 0.7 copy-start.6
  117.6 16.9 %collective-permute-start.10 = (bf16[8,16,1024]{2,1,0:T(8,128)(2,1)}, bf16[8,16,1024]{2,1,0:T(8,128)(2,1)S(1)}, u32[]{:S(2)}, u32[]{:S(2)}) collective-permute-start(bf16[8,16,1024]{2,1,0:T(8,128)(2,1)} %get-tuple-element.96), channel_id=1, source_target_pairs={{0,16},{4,20},{8,24},{12,28},{16,0},{20,4},{24,8},{28,12},{1,17},{... | collective-permute-start | bytes 786440 | tf_op jit(solution)/shard_map/ppermute | solution.py:344
  117.6 16.9 %all-to-all-start.5 = ((bf16[8,64,128]{2,1,0:T(8,128)(2,1)}), bf16[8,64,128]{2,1,0:T(8,128)(2,1)S(1)}, u32[]{:S(2)}, u32[]{:S(2)}) async-start(bf16[8,64,128]{2,1,0:T(8,128)(2,1)} %shard_map.157), calls=%async_computation.5 | async-start | bytes 262144 | tf_op jit(solution)/shard_map/all_to_all | solution.py:437
  134.6 26.3 %copy-start.8 = (bf16[8,16,1024]{2,1,0:T(8,128)(2,1)}, bf16[8,16,1024]{2,1,0:T(8,128)(2,1)S(1)}, u32[]{:S(2)}) copy-start(bf16[8,16,1024]{2,1,0:T(8,128)(2,1)S(1)} %collective-permute-done.10.refs_6_) | copy-start | bytes 786436
  134.8 16.7 %collective-permute-start.11 = (bf16[8,16,1024]{2,1,0:T(8,128)(2,1)}, bf16[8,16,1024]{2,1,0:T(8,128)(2,1)}, u32[]{:S(2)}, u32[]{:S(2)}) collective-permute-start(bf16[8,16,1024]{2,1,0:T(8,128)(2,1)} %get-tuple-element.100), channel_id=1, source_target_pairs={{0,20},{4,16},{8,28},{12,24},{16,4},{20,0},{24,12},{28,8},{1,21},{... | collective-permute-start | bytes 786440 | tf_op jit(solution)/shard_map/ppermute | solution.py:344
  137.9 13.6 %all-to-all-start.6 = ((bf16[8,40,128]{2,1,0:T(8,128)(2,1)}), bf16[8,40,128]{2,1,0:T(8,128)(2,1)S(1)}, u32[]{:S(2)}, u32[]{:S(2)}) async-start(bf16[8,40,128]{2,1,0:T(8,128)(2,1)} %broadcast_in_dim.112), calls=%async_computation.6 | async-start | bytes 163840 | tf_op jit(solution)/shard_map/all_to_all | solution.py:293
  152.6 16.0 %collective-permute-start.12 = (bf16[8,16,1024]{2,1,0:T(8,128)(2,1)}, bf16[8,16,1024]{2,1,0:T(8,128)(2,1)}, u32[]{:S(2)}, u32[]{:S(2)}) collective-permute-start(bf16[8,16,1024]{2,1,0:T(8,128)(2,1)} %get-tuple-element.105), channel_id=1, source_target_pairs={{0,20},{4,16},{8,28},{12,24},{16,4},{20,0},{24,12},{28,8},{1,21},{... | collective-permute-start | bytes 786440 | tf_op jit(solution)/shard_map/ppermute | solution.py:344
  153.5 15.1 %collective-permute-start.13 = (bf16[8,16,1024]{2,1,0:T(8,128)(2,1)}, bf16[8,16,1024]{2,1,0:T(8,128)(2,1)}, u32[]{:S(2)}, u32[]{:S(2)}) collective-permute-start(bf16[8,16,1024]{2,1,0:T(8,128)(2,1)} %get-tuple-element.106), channel_id=1, source_target_pairs={{0,12},{4,8},{8,4},{12,0},{16,28},{20,24},{24,20},{28,16},{1,13},{... | collective-permute-start | bytes 786440 | tf_op jit(solution)/shard_map/ppermute | solution.py:344
  156.3 11.1 %all-to-all-start.7 = ((f32[4,10,512]{2,1,0:T(8,128)}), f32[4,10,512]{2,1,0:T(8,128)S(1)}, u32[]{:S(2)}, u32[]{:S(2)}) async-start(f32[4,10,512]{2,1,0:T(8,128)} %fusion), calls=%async_computation.7 | async-start | bytes 262144 | tf_op jit(solution)/shard_map/all_to_all | solution.py:444
  160.9 1.0 copy-start.3
  161.8 0.9 copy-start.5
  162.8 0.9 copy-start.7
  163.7 0.9 copy-start.9

commit v6 on v5

--- a/solution.py
+++ b/solution.py
@@ -117,31 +117,34 @@
     return high, mid, peak - high - mid, cut(total), total - cut(total)
 
 
-def attend_kernel(
-    rows,
-    piece,
-    query_ref,
-    key_ref,
-    value_ref,
-    new_key_ref,
-    new_value_ref,
-    req_ref,
-    pos_ref,
-    row_ref,
-    new_bias_ref,
-    out_ref,
-    bias_ref,
-    score_ref,
-    weight_ref,
-):
+def attend_kernel(rows, piece, peers, me_ref, *refs):
+    query_refs, refs = refs[:peers], refs[peers:]
+    key_ref, value_ref, new_key_ref, new_value_ref, req_ref, pos_ref, row_ref, new_bias_ref = refs[:8]
+    out_refs = refs[8 : 8 + peers]
+    bias_ref, score_ref, weight_ref, query_ref, result_ref = refs[8 + peers :]
     tokens = key_ref.shape[0]
-
-    @pl.when(pl.program_id(0) == 0)
+    step = pl.program_id(0)
+
+    @pl.when(step == 0)
     def _():
         seen = (req_ref[...] == row_ref[:, 0:1]) & (pos_ref[...] < row_ref[:, 1:2])
         bias_ref[...] = jnp.where(seen, 0.0, NEG_FILL)
-
-    query = query_ref[0]
+        if peers > 1:
+            for d in range(peers):
+                query_ref[me_ref[1] ^ d] = query_refs[d][...]
+
+    if peers > 1:
+        per_step = query_refs[0].shape[0] // KVH
+        query = jnp.concatenate(
+            [
+                query_ref[n, step * per_step + i].astype(jnp.float32)
+                for i in range(per_step)
+                for n in range(peers)
+            ],
+            axis=0,
+        ).astype(jnp.bfloat16)
+    else:
+        query = query_refs[0][0]
     score_ref[:, :tokens] = lax.dot_general(
         query, key_ref[...], NT, preferred_element_type=jnp.float32
     )
@@ -173,7 +176,6 @@
     ) + jnp.dot(weight_ref[:, tokens:], new_value_ref[...], preferred_element_type=jnp.float32)
     peak = jnp.concatenate(peaks, axis=0)
     total = jnp.concatenate(totals, axis=0)
-
     lane = lax.broadcasted_iota(jnp.int32, (GROUPS * rows, HD), 1)
     stats = jnp.zeros((GROUPS * rows, HD), jnp.float32)
     for i, part in enumerate(split_stats(peak, total)):
@@ -182,7 +184,7 @@
         lax.broadcasted_iota(jnp.int32, (STAT, HD), 0)
         == lax.broadcasted_iota(jnp.int32, (STAT, HD), 1)
     ).astype(jnp.bfloat16)
-    fill = out_ref.shape[1] - STAT - piece
+    fill = result_ref.shape[1] - STAT - piece
     for c in range(GROUPS * rows // piece):
         part = slice(c * piece, (c + 1) * piece)
         turned = lax.dot_general(
@@ -193,23 +195,41 @@
             NT,
             preferred_element_type=jnp.float32,
         )
-        out_ref[c] = jnp.concatenate(
+        result_ref[c] = jnp.concatenate(
             [turned, mixed[part], jnp.zeros((fill, HD), jnp.float32)], axis=0
         ).astype(jnp.bfloat16)
-
-
-def attend(queries, keyval, pool, req_tok, pos_tok, row_info, new_bias, rows, piece):
+    if peers > 1:
+        for d, out_ref in enumerate(out_refs):
+
+            @pl.when((step ^ me_ref[1]) == d)
+            def _():
+                out_ref[...] = result_ref[...]
+    else:
+        out_refs[0][...] = result_ref[...]
+
+
+def attend(me, queries, keyval, pool, req_tok, pos_tok, row_info, new_bias, rows, piece):
     tokens = pool.shape[0]
     extra = keyval.shape[0]
+    peers = len(queries)
     pieces = GROUPS * rows // piece
     height = STAT + up(piece, 16)
     whole = lambda shape: pl.BlockSpec(shape, lambda k: (0,) * len(shape))
+    if peers > 1:
+        query_spec = whole(queries[0].shape)
+        out_spec = whole((pieces, height, HD))
+        out_shape = jax.ShapeDtypeStruct((pieces, height, HD), jnp.bfloat16)
+    else:
+        query_spec = pl.BlockSpec((1,) + queries[0].shape[1:], lambda k: (k, 0, 0))
+        out_spec = pl.BlockSpec((pieces, height, HD), lambda k: (k, 0, 0))
+        out_shape = jax.ShapeDtypeStruct((KVH * pieces, height, HD), jnp.bfloat16)
     return pl.pallas_call(
-        functools.partial(attend_kernel, rows, piece),
+        functools.partial(attend_kernel, rows, piece, peers),
         grid=(KVH,),
-        out_shape=jax.ShapeDtypeStruct((KVH * pieces, height, HD), jnp.bfloat16),
-        in_specs=[
-            pl.BlockSpec((1,) + queries.shape[1:], lambda k: (k, 0, 0)),
+        out_shape=[out_shape] * peers,
+        in_specs=[pl.BlockSpec(memory_space=pltpu.SMEM)]
+        + [query_spec] * peers
+        + [
             pl.BlockSpec((tokens, HD), lambda k: (0, k)),
             pl.BlockSpec((tokens, HD), lambda k: (0, KVH + k)),
             pl.BlockSpec((extra, HD), lambda k: (0, k)),
@@ -219,11 +239,13 @@
             whole(row_info.shape),
             whole(new_bias.shape),
         ],
-        out_specs=pl.BlockSpec((pieces, height, HD), lambda k: (k, 0, 0)),
+        out_specs=[out_spec] * peers,
         scratch_shapes=[
             pltpu.VMEM((rows, tokens), jnp.float32),
             pltpu.VMEM((GROUPS * rows, tokens + extra), jnp.float32),
             pltpu.VMEM((GROUPS * rows, tokens + extra), jnp.bfloat16),
+            pltpu.VMEM((peers,) + queries[0].shape, jnp.bfloat16),
+            pltpu.VMEM((pieces, height, HD), jnp.bfloat16),
         ],
         compiler_params=pltpu.CompilerParams(vmem_limit_bytes=32 * MIB),
         cost_estimate=pl.CostEstimate(
@@ -231,15 +253,16 @@
             bytes_accessed=pool.size * 2,
             transcendentals=HEADS * rows * (tokens + extra),
         ),
-    )(queries, pool, pool, keyval, keyval, req_tok, pos_tok, row_info, new_bias)
-
-
-def combine_kernel(piece, last, parts_ref, out_ref):
-    count, groups, height = parts_ref.shape[:3]
+    )(me, *queries, pool, pool, keyval, keyval, req_tok, pos_tok, row_info, new_bias)
+
+
+def combine_kernel(piece, last, count, me_ref, *refs):
+    part_refs, refs = refs[:count], refs[count:]
+    groups, height = part_refs[0].shape[:2]
     peaks, totals = [], []
     for i in range(count):
         for j in range(groups):
-            stat = parts_ref[i, j, :STAT, :].astype(jnp.float32)
+            stat = part_refs[i][j, :STAT, :].astype(jnp.float32)
             peaks.append(stat[0:1] + stat[1:2] + stat[2:3])
             totals.append(stat[3:4] + stat[4:5])
     peak = jnp.concatenate(peaks, axis=0).reshape(count, groups, HD)
@@ -260,28 +283,124 @@
         result = jnp.zeros((rows, HD), jnp.float32)
         for i in range(count):
             c = i * groups + j
-            result = result + lead[:rows, c : c + 1] * parts_ref[i, j, STAT:, :].astype(jnp.float32)
+            result = result + lead[:rows, c : c + 1] * part_refs[i][j, STAT:, :].astype(jnp.float32)
         if last:
-            out_ref[...] = result[:piece].astype(jnp.bfloat16)
+            refs[0][...] = result[:piece].astype(jnp.bfloat16)
         else:
             stats = split_stats(top[j : j + 1], whole[j : j + 1])
             rest = jnp.zeros((STAT - len(stats), HD), jnp.float32)
-            out_ref[j] = jnp.concatenate([*stats, rest, result], axis=0).astype(jnp.bfloat16)
-
-
-def combine(parts, piece, last):
-    groups, height = parts.shape[1:3]
-    shape = (piece, HD) if last else (groups, height, HD)
+            refs[-1][j] = jnp.concatenate([*stats, rest, result], axis=0).astype(jnp.bfloat16)
+    for d, out_ref in enumerate(refs[:-1]):
+        out_ref[...] = refs[-1][me_ref[0] ^ d]
+
+
+def combine(me, parts, piece, last, apart):
+    groups, height = parts[0].shape[:2]
+    if last:
+        out_shape = [jax.ShapeDtypeStruct((piece, HD), jnp.bfloat16)]
+    elif apart:
+        out_shape = [jax.ShapeDtypeStruct((height, HD), jnp.bfloat16)] * groups
+    else:
+        out_shape = [jax.ShapeDtypeStruct((groups, height, HD), jnp.bfloat16)]
+    scratch = [pltpu.VMEM((groups, height, HD), jnp.bfloat16)] if apart and not last else []
     return pl.pallas_call(
-        functools.partial(combine_kernel, piece, last),
-        out_shape=jax.ShapeDtypeStruct(shape, jnp.bfloat16),
-        in_specs=[pl.BlockSpec(memory_space=pltpu.VMEM)],
-        out_specs=pl.BlockSpec(memory_space=pltpu.VMEM),
+        functools.partial(combine_kernel, piece, last, len(parts)),
+        out_shape=out_shape,
+        in_specs=[pl.BlockSpec(memory_space=pltpu.SMEM)]
+        + [pl.BlockSpec(memory_space=pltpu.VMEM)] * len(parts),
+        out_specs=[pl.BlockSpec(memory_space=pltpu.VMEM)] * len(out_shape),
+        scratch_shapes=scratch,
         compiler_params=pltpu.CompilerParams(vmem_limit_bytes=8 * MIB),
         cost_estimate=pl.CostEstimate(
-            flops=2 * parts.size, bytes_accessed=parts.size * 2, transcendentals=0
+            flops=2 * len(parts) * parts[0].size,
+            bytes_accessed=len(parts) * parts[0].size * 2,
+            transcendentals=0,
         ),
-    )(parts)
+    )(me, *parts)
+
+
+def reorder(shape, unit, valid, own, column):
+    first, second = (0, 1) if column else (1, 0)
+    block = lax.broadcasted_iota(jnp.int32, shape, second) // unit
+    place = lax.broadcasted_iota(jnp.int32, shape, second) % unit
+    target = (block ^ own) * valid + place
+    match = (lax.broadcasted_iota(jnp.int32, shape, first) == target) & (place < valid)
+    return match.astype(jnp.bfloat16)
+
+
+def project_kernel(count, peers, me_ref, *refs):
+    hidden_refs, (query_ref, keyval_ref), refs = refs[:count], refs[count : count + 2], refs[count + 2 :]
+    out_refs, (full_ref,) = refs[:peers], refs[peers:]
+    local, depth = hidden_refs[0].shape
+    unit = up(local, 8)
+    blocks = []
+    for ref in hidden_refs:
+        blocks.append(ref[...].astype(jnp.float32))
+        if unit > local:
+            blocks.append(jnp.zeros((unit - local, depth), jnp.float32))
+    hidden = jnp.concatenate(blocks, axis=0).astype(jnp.bfloat16)
+    order = reorder((count * local, count * unit), unit, local, me_ref[0], True)
+    hidden = jnp.dot(order, hidden, preferred_element_type=jnp.float32).astype(jnp.bfloat16)
+    full_ref[...] = jnp.dot(hidden, query_ref[...], preferred_element_type=jnp.float32)
+    keyval = jnp.dot(hidden, keyval_ref[...], preferred_element_type=jnp.float32)
+    for d, out_ref in enumerate(out_refs):
+        start = pl.multiple_of((me_ref[1] ^ d) * HD, HD)
+        out_ref[:, :HD] = full_ref[:, pl.ds(start, HD)]
+        out_ref[:, HD:] = keyval
+
+
+def pack_kernel(peers, *refs):
+    own = refs[:peers]
+    total = (own[0][...] + own[1][...]) + (own[2][...] + own[3][...])
+    refs[-1][...] = jnp.concatenate([total, refs[peers][...]], axis=0).astype(jnp.bfloat16)
+
+
+def unpack_kernel(count, rows, me_ref, *refs):
+    part_refs, (query_ref, keyval_ref, tag_ref) = refs[:count], refs[count:]
+    line = lax.broadcasted_iota(jnp.int32, (count, HD), 0)
+    tags = jnp.zeros((count, HD), jnp.float32)
+    for d, ref in enumerate(part_refs):
+        source = me_ref[0] ^ d
+        part = ref[...].astype(jnp.float32)
+        query_ref[source] = part[:rows, :HD].astype(jnp.bfloat16)
+        fill = jnp.zeros((keyval_ref.shape[0] - rows, HD), jnp.float32)
+        block = jnp.concatenate([part[:rows, HD:], fill], axis=0).astype(jnp.bfloat16)
+        keyval_ref[:, pl.ds(pl.multiple_of(source * HD, HD), HD)] = block
+        tag = jnp.sum(jnp.where(line == me_ref[0], part[rows:, :HD], 0.0), axis=0, keepdims=True)
+        tags = tags + jnp.where(line == source, tag, 0.0)
+    tag_ref[...] = tags
+
+
+def finish_kernel(count, peers, me_ref, *refs):
+    part_refs, weight_ref, refs = refs[:count], refs[count], refs[count + 1 :]
+    out_refs, (whole_ref,) = refs[:peers], refs[peers:]
+    rows = whole_ref.shape[0]
+    local = rows // peers
+    unit = up(local, 16)
+    for d, ref in enumerate(part_refs):
+        start = pl.multiple_of((me_ref[0] ^ d) * HD, HD)
+        whole_ref[:, pl.ds(start, HD)] = ref[...]
+    order = reorder((peers * unit, rows), unit, local, me_ref[1], False)
+    mixed = jnp.dot(order, whole_ref[...], preferred_element_type=jnp.float32)
+    mixed = jnp.dot(mixed.astype(jnp.bfloat16), weight_ref[...], preferred_element_type=jnp.float32)
+    for d, out_ref in enumerate(out_refs):
+        out_ref[...] = mixed[d * unit : d * unit + local]
+
+
+def in_vmem(kernel, out_shape, me, *args, scratch=()):
+    head = [] if me is None else [me]
+    return pl.pallas_call(
+        kernel,
+        out_shape=out_shape,
+        in_specs=[pl.BlockSpec(memory_space=pltpu.SMEM)] * len(head)
+        + [pl.BlockSpec(memory_space=pltpu.VMEM)] * len(args),
+        out_specs=jax.tree.map(lambda _: pl.BlockSpec(memory_space=pltpu.VMEM), out_shape),
+        scratch_shapes=scratch,
+        compiler_params=pltpu.CompilerParams(vmem_limit_bytes=16 * MIB),
+        cost_estimate=pl.CostEstimate(
+            flops=0, bytes_accessed=sum(2 * arg.size for arg in args), transcendentals=0
+        ),
+    )(*head, *args)
 
 
 def group_of(d, wide):
@@ -307,15 +426,33 @@
     requests = rows // STEPS
     slots = pool.shape[0]
     capacity = slots // wide
-
-    gathered = spread(hidden, "wide").reshape(rows, -1)
+    own_cols = w_query.shape[1] // narrow
+    piece = HEADS * rows // (wide * narrow)
+    extra = up(rows, HD)
+    direct = piece == rows and own_cols == HD and wide == 8 and narrow == 4
+    me = lax.axis_index("wide")
+    both = jnp.stack([me, lax.axis_index("narrow")])
+    exchange = functools.partial(lax.all_to_all, split_axis=0, concat_axis=0, tiled=True)
+
+    def send(block, axis, d):
+        return lax.ppermute(block, axis, [(i, i ^ d) for i in range(lax.axis_size(axis))])
+
+    def share(block, axis):
+        return [block] + [send(block, axis, d) for d in range(1, lax.axis_size(axis))]
+
+    def deal(blocks, axis):
+        return [blocks[0]] + [send(block, axis, d) for d, block in enumerate(blocks) if d]
+
+    if direct:
+        gathered = share(hidden, "wide")
+    else:
+        gathered = spread(hidden, "wide").reshape(rows, -1)
 
     dest = moves[:, 0]
     order = jnp.arange(slots, dtype=jnp.int32)
     rank = jnp.sum((dest[:, None] == dest[None, :]) & (order[None, :] < order[:, None]), axis=1)
     target = dest * capacity + rank
     chosen = target[None, :] == order[:, None]
-    me = lax.axis_index("wide")
     moved_to = (dest ^ me) * capacity + rank
     source_of = jnp.sum(
         jnp.where(moved_to[None, :] == order[:, None], order[None, :], 0), axis=1
@@ -324,8 +461,6 @@
     sent_idx = jnp.sum(jnp.where(chosen, page_idx[None, :], 0), axis=1)
     moved_pool, *chunks = permute_pages(source_of, me.reshape(1), pool, wide * PARTS)
     arrived = {}
-
-    exchange = functools.partial(lax.all_to_all, split_axis=0, concat_axis=0, tiled=True)
     flying = {}
 
     def members(groups):
@@ -340,8 +475,7 @@
         taken = members(groups)
         values, sent = lax.optimization_barrier((values, [chunks[c] for c in taken]))
         for c, chunk in zip(taken, sent):
-            peer = 1 + c // PARTS
-            flying[c] = lax.ppermute(chunk, "wide", [(w, w ^ peer) for w in range(wide)])
+            flying[c] = send(chunk, "wide", 1 + c // PARTS)
         return values
 
     def land(values, *groups):
@@ -360,35 +494,15 @@
         arrived.clear()
         return pages
 
-    query_part = jnp.dot(gathered, w_query, preferred_element_type=jnp.float32)
-    keyval_part = jnp.dot(gathered, w_keyval, preferred_element_type=jnp.float32)
-    own_cols = query_part.shape[1] // narrow
-    query_part = jnp.transpose(query_part.reshape(rows, narrow, own_cols), (1, 0, 2))
-    partial = jnp.concatenate(
-        [query_part, jnp.broadcast_to(keyval_part[None], (narrow,) + keyval_part.shape)], axis=2
-    )
-    partial = beside(lambda value: exchange(value, "narrow"), partial, (6, 0), (1, 0))
-    projected = jnp.sum(partial, axis=0).astype(jnp.bfloat16)
     shifted = sent_idx + 1
     tags = jnp.concatenate(
         [
-            sent_req.reshape(wide, 1, capacity),
-            (shifted // 32).reshape(wide, 1, capacity),
-            (shifted % 32).reshape(wide, 1, capacity),
-        ],
-        axis=2,
-    ).astype(jnp.bfloat16)
-    height = up(rows + 1, 8)
-    packed = jnp.concatenate(
-        [
-            jnp.broadcast_to(projected[None], (wide,) + projected.shape),
-            jnp.pad(
-                tags, ((0, 0), (0, height - rows - 1), (0, projected.shape[1] - 3 * capacity))
-            ),
+            sent_req.reshape(wide, capacity),
+            (shifted // 32).reshape(wide, capacity),
+            (shifted % 32).reshape(wide, capacity),
         ],
         axis=1,
     )
-    received = beside(lambda value: exchange(value, "wide"), packed, (6, 1))
     req_tok = jnp.broadcast_to(page_req[:, None], (slots, PAGE)).reshape(1, -1)
     pos_tok = (page_idx[:, None] * PAGE + jnp.arange(PAGE, dtype=jnp.int32)[None, :]).reshape(1, -1)
     row_info = jnp.stack(
@@ -398,58 +512,128 @@
         ],
         axis=1,
     )
-    queries = beside(
-        lambda value: spread(value, "narrow"), received[:, :rows, :own_cols], (7, 0), (2, 0)
-    )
-    if own_cols == HD:
-        queries = jnp.transpose(queries, (1, 0, 2, 3))
-    else:
-        queries = jnp.transpose(queries, (2, 1, 0, 3)).reshape(rows, HEADS, HD)
-        queries = jnp.transpose(queries, (1, 0, 2))
-    queries = queries.reshape(KVH, GROUPS * rows, HD)
-    tags_in = received[:, rows, : 3 * capacity].astype(jnp.int32)
-    moved_req = tags_in[:, :capacity].reshape(slots)
-    moved_idx = (
-        tags_in[:, capacity : 2 * capacity] * 32 + tags_in[:, 2 * capacity :] - 1
-    ).reshape(slots)
-
-    keyval = jnp.transpose(received[:, :rows, own_cols:], (1, 0, 2)).reshape(rows, -1)
-    extra = up(rows, HD)
-    here = (lax.axis_index("wide") == 0) & (lax.axis_index("narrow") == 0)
+    here = (me == 0) & (lax.axis_index("narrow") == 0)
     row_ids = np.arange(rows)[:, None]
     col_ids = np.arange(extra)[None, :]
     causal = (row_ids // STEPS == col_ids // STEPS) & (col_ids <= row_ids) & (col_ids < rows)
     new_bias = jnp.where(jnp.asarray(causal) & here, 0.0, NEG_FILL).astype(jnp.float32)
-    piece = HEADS * rows // (wide * narrow)
-    new_keyval = jnp.pad(keyval, ((0, extra - rows), (0, 0)))
     tokens = pool.reshape(slots * PAGE, -1)
+    window = {
+        "project": ((6, 0),),
+        "gather": ((6, 1),),
+        "queries": ((7, 0), (2, 0)),
+        "attend": ((7, 1), (2, 1), (1, 1)),
+        "narrow": ((4, 0), (3, 0)),
+        "wide": ((4, 1), (1, 0)),
+        "attn": ((5, 0),),
+        "finish": ((5, 1), (3, 1)),
+    }
+
+    if direct:
+        block = jax.ShapeDtypeStruct((rows, 2 * HD), jnp.float32)
+        partial = in_vmem(
+            functools.partial(project_kernel, wide, narrow),
+            [block] * narrow,
+            both,
+            *gathered,
+            w_query,
+            w_keyval,
+            scratch=[pltpu.VMEM((rows, narrow * HD), jnp.float32)],
+        )
+        partial = beside(lambda value: deal(value, "narrow"), partial, *window["project"])
+        tags = jnp.pad(tags.astype(jnp.float32), ((0, 0), (0, 2 * HD - tags.shape[1])))
+        packed = in_vmem(
+            functools.partial(pack_kernel, narrow),
+            jax.ShapeDtypeStruct((rows + wide, 2 * HD), jnp.bfloat16),
+            None,
+            *partial,
+            tags,
+        )
+        received = beside(lambda value: share(value, "wide"), packed, *window["gather"])
+        queries, keyval, tags_in = in_vmem(
+            functools.partial(unpack_kernel, wide, rows),
+            [
+                jax.ShapeDtypeStruct((wide, rows, HD), jnp.bfloat16),
+                jax.ShapeDtypeStruct((extra, wide * HD), jnp.bfloat16),
+                jax.ShapeDtypeStruct((wide, HD), jnp.float32),
+            ],
+            both,
+            *received,
+        )
+        queries = beside(lambda value: share(value, "narrow"), queries, *window["queries"])
+    else:
+        query_part = jnp.dot(gathered, w_query, preferred_element_type=jnp.float32)
+        keyval_part = jnp.dot(gathered, w_keyval, preferred_element_type=jnp.float32)
+        query_part = jnp.transpose(query_part.reshape(rows, narrow, own_cols), (1, 0, 2))
+        partial = jnp.concatenate(
+            [query_part, jnp.broadcast_to(keyval_part[None], (narrow,) + keyval_part.shape)], axis=2
+        )
+        partial = beside(lambda value: exchange(value, "narrow"), partial, *window["project"])
+        projected = jnp.sum(partial, axis=0).astype(jnp.bfloat16)
+        tags = tags.astype(jnp.bfloat16)[:, None]
+        tags = jnp.pad(tags, ((0, 0), (0, 7), (0, projected.shape[1] - tags.shape[2])))
+        packed = jnp.broadcast_to(projected[None], (wide,) + projected.shape)
+        packed = jnp.concatenate([packed, tags], axis=1)
+        received = beside(lambda value: exchange(value, "wide"), packed, *window["gather"])
+        tags_in = received[:, rows]
+        queries = beside(
+            lambda value: spread(value, "narrow"),
+            received[:, :rows, :own_cols],
+            *window["queries"],
+        )
+        queries = jnp.transpose(queries, (2, 1, 0, 3)).reshape(rows, HEADS, HD)
+        queries = [jnp.transpose(queries, (1, 0, 2)).reshape(KVH, GROUPS * rows, HD)]
+        keyval = jnp.transpose(received[:, :rows, own_cols:], (1, 0, 2)).reshape(rows, -1)
+        keyval = jnp.pad(keyval, ((0, extra - rows), (0, 0)))
+
     parts = beside(
         lambda value: attend(
-            value, new_keyval, tokens, req_tok, pos_tok, row_info, new_bias, rows, piece
+            both, value, keyval, tokens, req_tok, pos_tok, row_info, new_bias, rows, piece
         ),
         queries,
-        (7, 1),
-        (2, 1),
-        (1, 1),
-    )
-    parts = beside(lambda value: exchange(value, "narrow"), parts, (4, 0), (3, 0))
-    parts = combine(parts.reshape((narrow, wide) + parts.shape[1:]), piece, False)
-    parts = beside(lambda value: exchange(value, "wide"), parts, (4, 1))
-    attn = combine(parts[:, None], piece, True)
-    attn = beside(lambda value: spread(value, "wide"), attn, (5, 0))
+        *window["attend"],
+    )
+    if direct:
+        parts = beside(lambda value: deal(value, "narrow"), parts, *window["narrow"])
+        parts = combine(both, parts, piece, False, True)
+        parts = beside(lambda value: deal(value, "wide"), parts, *window["wide"])
+        (attn,) = combine(both, [part[None] for part in parts], piece, True, True)
+        attn = beside(lambda value: share(value, "wide"), attn, *window["attn"])
+        moved_pool = placed(moved_pool)
+        sums = in_vmem(
+            functools.partial(finish_kernel, wide, narrow),
+            [jax.ShapeDtypeStruct((rows // narrow, w_out.shape[1]), jnp.float32)] * narrow,
+            both,
+            *attn,
+            w_out,
+            scratch=[pltpu.VMEM((rows, wide * HD), jnp.bfloat16)],
+        )
+        sums = beside(lambda value: deal(value, "narrow"), sums, *window["finish"])
+        attended = ((sums[0] + sums[1]) + (sums[2] + sums[3])).astype(jnp.bfloat16)
+    else:
+        parts = beside(lambda value: exchange(value, "narrow"), parts[0], *window["narrow"])
+        parts = parts.reshape((narrow, wide) + parts.shape[1:])
+        (parts,) = combine(both, [parts[i] for i in range(narrow)], piece, False, False)
+        parts = beside(lambda value: exchange(value, "wide"), parts, *window["wide"])
+        (attn,) = combine(both, [parts[i][None] for i in range(wide)], piece, True, False)
+        attn = beside(lambda value: spread(value, "wide"), attn, *window["attn"])
+        moved_pool = placed(moved_pool)
+        attn = jnp.transpose(attn.reshape(-1, rows, HD), (1, 0, 2)).reshape(rows, -1)
+        sums = jnp.dot(attn, w_out, preferred_element_type=jnp.float32)
+        sums = sums.reshape(narrow, rows // narrow, -1)
+        sums = beside(lambda value: exchange(value, "narrow"), sums, *window["finish"])
+        attended = jnp.sum(sums, axis=0).astype(jnp.bfloat16)
     moved_pool = placed(moved_pool)
-    attn = jnp.transpose(attn.reshape(-1, rows, HD), (1, 0, 2)).reshape(rows, -1)
-    sums = jnp.dot(attn, w_out, preferred_element_type=jnp.float32)
-    sums = sums.reshape(narrow, rows // narrow, -1)
-    sums = beside(lambda value: exchange(value, "narrow"), sums, (5, 1), (3, 1))
-    attended = jnp.sum(sums, axis=0).astype(jnp.bfloat16)
-
-    moved_pool = placed(moved_pool)
-
+
+    tags_in = tags_in.astype(jnp.int32)
+    moved_req = tags_in[:, :capacity].reshape(slots)
+    moved_idx = tags_in[:, capacity : 2 * capacity] * 32
+    moved_idx = (moved_idx + tags_in[:, 2 * capacity : 3 * capacity] - 1).reshape(slots)
     local_req = local_rows // STEPS
-    first_req = lax.axis_index("wide") * local_req
-    fresh = lax.dynamic_slice_in_dim(keyval.reshape(requests, STEPS, -1), first_req, local_req, 0)
-    kept = lax.dynamic_slice_in_dim(accepted, first_req, local_req, 0)
+    first_row = me * local_rows
+    fresh = lax.dynamic_slice_in_dim(keyval, first_row, local_rows, 0)
+    fresh = fresh.reshape(local_req, STEPS, -1)
+    kept = lax.dynamic_slice_in_dim(accepted, me * local_req, local_req, 0)
     new_entries = jnp.where(
         jnp.arange(STEPS)[None, :, None] < kept[:, None, None], fresh, jnp.zeros((), jnp.bfloat16)
     )

time: 172 us -> 160 us (0.930)
  waiting for transfers between devices: 61.7 us -> 41.5 us
  starting transfers between devices: 62.5 us -> 78.5 us
  local copies, waits for them, and re-layouts: 17.1 us -> 9.73 us
  Pallas kernels: 19.9 us -> 22.8 us
    ppermute x14 -> x54, starting transfers between devices: 25.3 us -> 78.5 us  [send(): lax.ppermute(block, axis, [(i, i ^ d) for i in range(lax.axis_size(axis))])]
    all_to_all x8 -> x0, starting transfers between devices: 37.2 us -> none  [the longest x3 15.5 us: spread(): lax.all_to_all(jnp.broadcast_to(block[None], (count,) + block.shape), axi...]
    all_to_all x8 -> x0, waiting for transfers between devices: 21 us -> none  [the longest x1 11.3 us: on_device(): parts = beside(lambda value: exchange(value, 'wide'), parts, (4, 1))]
    pallas_call x3 -> x7, Pallas kernels: 10.9 us -> 14.3 us  [the longest x1 9.33 us: attend(): pl.pallas_call(functools.partial(attend_kernel, rows, piece, peers), grid...]
    broadcast_in_dim x5 -> x0, local copies, waits for them, and re-layouts: 2.89 us -> none  [the longest x3 2.87 us: spread(): jnp.broadcast_to(block[None], (count,) + block.shape)]
    unnamed x39 -> x42, local copies, waits for them, and re-layouts: 8.15 us -> 7.21 us
    ppermute x14 -> x54, waiting for transfers between devices: 40.7 us -> 41.5 us  [send(): lax.ppermute(block, axis, [(i, i ^ d) for i in range(lax.axis_size(axis))])]
  transfers between devices with their start and end apart: 22 -> 54, of which waited for: 12 -> 22; matrix products, arithmetic and copies ran while one was open for 7% -> 5% of each run, Pallas kernels for 10% -> 10%
where the time goes in v6:
time: 160 us
  starting transfers between devices  78.5 us (49%)
  waiting for transfers between devices  41.5 us (26%)
  Pallas kernels  22.8 us (14%)
  local copies, waits for them, and re-layouts  9.73 us (6%)
  other arithmetic  6.42 us (4%)
    ppermute x54, starting transfers between devices, send(): lax.ppermute(block, axis, [(i, i ^ d) for i in range(lax.axis_size(axis))])  78.5 us
    ppermute x54, waiting for transfers between devices, send(): lax.ppermute(block, axis, [(i, i ^ d) for i in range(lax.axis_size(axis))])  41.5 us
    pallas_call x1, Pallas kernels, attend(): pl.pallas_call(functools.partial(attend_kernel, rows, piece, peers), grid...  9.33 us
    unnamed x42, local copies, waits for them, and re-layouts  7.21 us
    pallas_call x1, Pallas kernels, permute_pages(): pl.pallas_call(permute_kernel, out_shape=[jax.ShapeDtypeStruct(pool.shape...  4.38 us
    pallas_call x2, Pallas kernels, place_pages(): pl.pallas_call(place_kernel, out_shape=jax.ShapeDtypeStruct(pages.shape,...  4.06 us
  transfers between devices with their start and end apart: 54, of which 22 were waited for; matrix products, arithmetic and copies ran while one was open for 5% of the time, Pallas kernels for 10%

profile of v6, /device:TPU:0, one launch (start us, length us, event | category | flops | bytes accessed | tf_op | source)
XLA Modules:
  0.0 160.0 jit_solution(17839363863258055172)
XLA Ops:
  0.7 3.0 %collective-permute-start = (bf16[5,1024]{1,0:T(8,128)(2,1)}, bf16[5,1024]{1,0:T(8,128)(2,1)S(1)}, u32[]{:S(2)}, u32[]{:S(2)}) collective-permute-start(bf16[5,1024]{1,0:T(8,128)(2,1)} %refs_0_.1), channel_id=1, source_target_pairs={{0,4},{4,0},{8,12},{12,8},{16,20},{20,16},{24,28},{28,24},{1,5},{5... | collective-permute-start | bytes 30728 | tf_op jit(solution)/shard_map/ppermute | solution.py:438
  3.8 1.6 collective-permute-start.1
  5.3 3.0 %collective-permute-start.3 = (bf16[5,1024]{1,0:T(8,128)(2,1)}, bf16[5,1024]{1,0:T(8,128)(2,1)S(1)}, u32[]{:S(2)}, u32[]{:S(2)}) collective-permute-start(bf16[5,1024]{1,0:T(8,128)(2,1)} %refs_0_.1), channel_id=1, source_target_pairs={{0,16},{4,20},{8,24},{12,28},{16,0},{20,4},{24,8},{28,12},{1,17},{... | collective-permute-start | bytes 30728 | tf_op jit(solution)/shard_map/ppermute | solution.py:438
  12.5 3.6 %collective-permute-start.5 = (bf16[5,1024]{1,0:T(8,128)(2,1)}, bf16[5,1024]{1,0:T(8,128)(2,1)S(1)}, u32[]{:S(2)}, u32[]{:S(2)}) collective-permute-start(bf16[5,1024]{1,0:T(8,128)(2,1)} %refs_0_.1), channel_id=1, source_target_pairs={{0,24},{4,28},{8,16},{12,20},{16,8},{20,12},{24,0},{28,4},{1,25},{... | collective-permute-start | bytes 30728 | tf_op jit(solution)/shard_map/ppermute | solution.py:438
  16.4 4.4 %shard_map.156 = (bf16[128,16,1024]{2,1,0:T(8,128)(2,1)}, bf16[8,16,1024]{2,1,0:T(8,128)(2,1)}, bf16[8,16,1024]{2,1,0:T(8,128)(2,1)}, bf16[8,16,1024]{2,1,0:T(8,...) custom-call(s32[128]{0:T(128)} %get-tuple-element.287.source_ref, ...), custom_call_target="tpu_custom_call" | custom-call | bytes 8388608 | tf_op jit(solution)/shard_map/pallas_call | solution.py:55
  20.8 2.0 %collective-permute-done.6.refs_7_ = bf16[5,1024]{1,0:T(8,128)(2,1)S(1)} collective-permute-done((bf16[5,1024]{1,0:T(8,128)(2,1)}, bf16[5,1024]{1,0:T(8,128)(2,1)S(1)}, u32[]{:S(2)}, u32[]{:S(2)}) %collective-permute-start.6) | collective-permute-done | bytes 10272 | tf_op jit(solution)/shard_map/ppermute | solution.py:438
  23.8 1.9 %collective-permute-start.10 = (bf16[8,16,1024]{2,1,0:T(8,128)(2,1)}, bf16[8,16,1024]{2,1,0:T(8,128)(2,1)S(1)}, u32[]{:S(2)}, u32[]{:S(2)}) collective-permute-start(bf16[8,16,1024]{2,1,0:T(8,128)(2,1)} %get-tuple-element.151), channel_id=1, source_target_pairs={{0,24},{4,28},{8,16},{12,20},{16,8},{20,12},{24,0},{28,4},{1,25},{... | collective-permute-start | bytes 786440 | tf_op jit(solution)/shard_map/ppermute | solution.py:438
  25.7 1.6 collective-permute-start.8
  27.7 2.1 %collective-permute-done.8.refs_2_ = f32[40,256]{1,0:T(8,128)S(1)} collective-permute-done((f32[40,256]{1,0:T(8,128)S(1)}, f32[40,256]{1,0:T(8,128)S(1)}, u32[]{:S(2)}, u32[]{:S(2)}) %collective-permute-start.8) | collective-permute-done | bytes 40992 | tf_op jit(solution)/shard_map/ppermute | solution.py:438
  30.8 1.5 collective-permute-done.10.refs_8_
  32.3 1.8 %collective-permute-start.18 = (bf16[8,16,1024]{2,1,0:T(8,128)(2,1)}, bf16[8,16,1024]{2,1,0:T(8,128)(2,1)S(1)}, u32[]{:S(2)}, u32[]{:S(2)}) collective-permute-start(bf16[8,16,1024]{2,1,0:T(8,128)(2,1)} %get-tuple-element.158), channel_id=1, source_target_pairs={{0,24},{4,28},{8,16},{12,20},{16,8},{20,12},{24,0},{28,4},{1,25},{... | collective-permute-start | bytes 786440 | tf_op jit(solution)/shard_map/ppermute | solution.py:438
  34.2 1.5 collective-permute-start.11
  35.7 9.4 %collective-permute-start.12 = (bf16[48,256]{1,0:T(8,128)(2,1)S(1)}, bf16[48,256]{1,0:T(8,128)(2,1)S(1)}, u32[]{:S(2)}, u32[]{:S(2)}) collective-permute-start(bf16[48,256]{1,0:T(8,128)(2,1)S(1)} %shard_map.157.refs_0_), channel_id=1, source_target_pairs={{0,8},{4,12},{8,0},{12,4},{16,24},{20,28},{24,16},{28,20},{1,9},{5... | collective-permute-start | bytes 73736 | tf_op jit(solution)/shard_map/ppermute | solution.py:438
  46.2 2.8 %collective-permute-start.15 = (bf16[48,256]{1,0:T(8,128)(2,1)S(1)}, bf16[48,256]{1,0:T(8,128)(2,1)S(1)}, u32[]{:S(2)}, u32[]{:S(2)}) collective-permute-start(bf16[48,256]{1,0:T(8,128)(2,1)S(1)} %shard_map.157.refs_0_), channel_id=1, source_target_pairs={{0,20},{4,16},{8,28},{12,24},{16,4},{20,0},{24,12},{28,8},{1,21},{... | collective-permute-start | bytes 73736 | tf_op jit(solution)/shard_map/ppermute | solution.py:438
  49.0 1.8 %collective-permute-start.16 = (bf16[48,256]{1,0:T(8,128)(2,1)S(1)}, bf16[48,256]{1,0:T(8,128)(2,1)S(1)}, u32[]{:S(2)}, u32[]{:S(2)}) collective-permute-start(bf16[48,256]{1,0:T(8,128)(2,1)S(1)} %shard_map.157.refs_0_), channel_id=1, source_target_pairs={{0,24},{4,28},{8,16},{12,20},{16,8},{20,12},{24,0},{28,4},{1,25},{... | collective-permute-start | bytes 73736 | tf_op jit(solution)/shard_map/ppermute | solution.py:438
  50.8 2.0 %collective-permute-start.17 = (bf16[48,256]{1,0:T(8,128)(2,1)S(1)}, bf16[48,256]{1,0:T(8,128)(2,1)S(1)}, u32[]{:S(2)}, u32[]{:S(2)}) collective-permute-start(bf16[48,256]{1,0:T(8,128)(2,1)S(1)} %shard_map.157.refs_0_), channel_id=1, source_target_pairs={{0,28},{4,24},{8,20},{12,16},{16,12},{20,8},{24,4},{28,0},{1,29},{... | collective-permute-start | bytes 73736 | tf_op jit(solution)/shard_map/ppermute | solution.py:438
  53.0 1.9 %collective-permute-done.16.refs_6_ = bf16[48,256]{1,0:T(8,128)(2,1)S(1)} collective-permute-done((bf16[48,256]{1,0:T(8,128)(2,1)S(1)}, bf16[48,256]{1,0:T(8,128)(2,1)S(1)}, u32[]{:S(2)}, u32[]{:S(2)}) %collective-permute-start.16) | collective-permute-done | bytes 24608 | tf_op jit(solution)/shard_map/ppermute | solution.py:438
  54.9 2.9 %collective-permute-done.17.refs_7_ = bf16[48,256]{1,0:T(8,128)(2,1)S(1)} collective-permute-done((bf16[48,256]{1,0:T(8,128)(2,1)S(1)}, bf16[48,256]{1,0:T(8,128)(2,1)S(1)}, u32[]{:S(2)}, u32[]{:S(2)}) %collective-permute-start.17) | collective-permute-done | bytes 24608 | tf_op jit(solution)/shard_map/ppermute | solution.py:438
  58.3 2.0 %collective-permute-start.22 = (bf16[8,16,1024]{2,1,0:T(8,128)(2,1)}, bf16[8,16,1024]{2,1,0:T(8,128)(2,1)S(1)}, u32[]{:S(2)}, u32[]{:S(2)}) collective-permute-start(bf16[8,16,1024]{2,1,0:T(8,128)(2,1)} %get-tuple-element.171), channel_id=1, source_target_pairs={{0,28},{4,24},{8,20},{12,16},{16,12},{20,8},{24,4},{28,0},{1,29},{... | collective-permute-start | bytes 786440 | tf_op jit(solution)/shard_map/ppermute | solution.py:438
  60.7 1.6 collective-permute-start.20
  62.7 3.2 %collective-permute-done.20.refs_2_ = bf16[8,40,128]{2,1,0:T(8,128)(2,1)S(1)} collective-permute-done((bf16[8,40,128]{2,1,0:T(8,128)(2,1)S(1)}, bf16[8,40,128]{2,1,0:T(8,128)(2,1)S(1)}, u32[]{:S(2)}, u32[]{:S(2)}) %collective-permute-start.20) | collective-permute-done | bytes 81952 | tf_op jit(solution)/shard_map/ppermute | solution.py:438
  67.9 1.6 collective-permute-done.23.refs_2_
  69.5 3.0 %collective-permute-start.24 = (bf16[8,16,1024]{2,1,0:T(8,128)(2,1)}, bf16[8,16,1024]{2,1,0:T(8,128)(2,1)S(1)}, u32[]{:S(2)}, u32[]{:S(2)}) collective-permute-start(bf16[8,16,1024]{2,1,0:T(8,128)(2,1)} %get-tuple-element.189), channel_id=1, source_target_pairs={{0,28},{4,24},{8,20},{12,16},{16,12},{20,8},{24,4},{28,0},{1,29},{... | collective-permute-start | bytes 786440 | tf_op jit(solution)/shard_map/ppermute | solution.py:438
  72.9 2.2 %copy-done = bf16[128,16,1024]{2,1,0:T(8,128)(2,1)S(1)} copy-done((bf16[128,16,1024]{2,1,0:T(8,128)(2,1)S(1)}, bf16[128,16,1024]{2,1,0:T(8,128)(2,1)}, u32[]{:S(2)}) %copy-start) | copy-done | bytes 4194328
  75.1 9.3 %shard_map.159 = (bf16[8,64,128]{2,1,0:T(8,128)(2,1)S(1)}, bf16[8,64,128]{2,1,0:T(8,128)(2,1)S(1)}, bf16[8,64,128]{2,1,0:T(8,128)(2,1)S(1)}, bf16[8,64,128]{2,1,0:T(8,128)(2,1)S(1)}) custom-call(s32[2]{0:T(128)S(1)} %pad_add_fusion.1.me_ref, bf16[8,40,128]{2,1,0:T(8,128)(2,1)S(1)} %get-tuple-element.180.refs_0_, ...), custom_call_target="tpu_custom_call" | custom-call | flops 1426063360 | bytes 4194304 | tf_op jit(solution)/shard_map/pallas_call | solution.py:226
  84.5 2.5 %collective-permute-start.30 = (bf16[8,16,1024]{2,1,0:T(8,128)(2,1)S(1)}, bf16[8,16,1024]{2,1,0:T(8,128)(2,1)S(1)}, u32[]{:S(2)}, u32[]{:S(2)}) collective-permute-start(bf16[8,16,1024]{2,1,0:T(8,128)(2,1)S(1)} %copy-done.19), channel_id=1, source_target_pairs={{0,16},{4,20},{8,24},{12,28},{16,0},{20,4},{24,8},{28,12},{1,17},{... | collective-permute-start | bytes 786440 | tf_op jit(solution)/shard_map/ppermute | solution.py:438
  88.1 1.4 collective-permute-start.28
  90.0 4.4 %collective-permute-done.28.refs_2_ = bf16[8,64,128]{2,1,0:T(8,128)(2,1)S(1)} collective-permute-done((bf16[8,64,128]{2,1,0:T(8,128)(2,1)S(1)}, bf16[8,64,128]{2,1,0:T(8,128)(2,1)S(1)}, u32[]{:S(2)}, u32[]{:S(2)}) %collective-permute-start.28) | collective-permute-done | bytes 131104 | tf_op jit(solution)/shard_map/ppermute | solution.py:438
  94.4 2.0 %collective-permute-done.29.refs_3_ = bf16[8,64,128]{2,1,0:T(8,128)(2,1)S(1)} collective-permute-done((bf16[8,64,128]{2,1,0:T(8,128)(2,1)S(1)}, bf16[8,64,128]{2,1,0:T(8,128)(2,1)S(1)}, u32[]{:S(2)}, u32[]{:S(2)}) %collective-permute-start.29) | collective-permute-done | bytes 131104 | tf_op jit(solution)/shard_map/ppermute | solution.py:438
  96.5 2.3 %collective-permute-done.30.refs_5_ = bf16[8,16,1024]{2,1,0:T(8,128)(2,1)S(1)} collective-permute-done((bf16[8,16,1024]{2,1,0:T(8,128)(2,1)S(1)}, bf16[8,16,1024]{2,1,0:T(8,128)(2,1)S(1)}, u32[]{:S(2)}, u32[]{:S(2)}) %collective-permute-start.30) | collective-permute-done | bytes 262176 | tf_op jit(solution)/shard_map/ppermute | solution.py:438
  103.6 2.2 %collective-permute-start.33 = (bf16[64,128]{1,0:T(8,128)(2,1)S(1)}, bf16[64,128]{1,0:T(8,128)(2,1)S(1)}, u32[]{:S(2)}, u32[]{:S(2)}) collective-permute-start(bf16[64,128]{1,0:T(8,128)(2,1)S(1)} %get-tuple-element.220), channel_id=1, source_target_pairs={{0,8},{4,12},{8,0},{12,4},{16,24},{20,28},{24,16},{28,20},{1,9},{5... | collective-permute-start | bytes 49160 | tf_op jit(solution)/shard_map/ppermute | solution.py:438
  106.2 3.5 %collective-permute-done.32 = bf16[64,128]{1,0:T(8,128)(2,1)S(1)} collective-permute-done((bf16[64,128]{1,0:T(8,128)(2,1)S(1)}, bf16[64,128]{1,0:T(8,128)(2,1)S(1)}, u32[]{:S(2)}, u32[]{:S(2)}) %collective-permute-start.32) | collective-permute-done | bytes 16416 | tf_op jit(solution)/shard_map/ppermute | solution.py:438
  109.7 2.5 %collective-permute-start.35 = (bf16[64,128]{1,0:T(8,128)(2,1)S(1)}, bf16[64,128]{1,0:T(8,128)(2,1)S(1)}, u32[]{:S(2)}, u32[]{:S(2)}) collective-permute-start(bf16[64,128]{1,0:T(8,128)(2,1)S(1)} %get-tuple-element.222), channel_id=1, source_target_pairs={{0,16},{4,20},{8,24},{12,28},{16,0},{20,4},{24,8},{28,12},{1,17},{... | collective-permute-start | bytes 49160 | tf_op jit(solution)/shard_map/ppermute | solution.py:438
  112.7 1.8 %collective-permute-start.37 = (bf16[64,128]{1,0:T(8,128)(2,1)S(1)}, bf16[64,128]{1,0:T(8,128)(2,1)S(1)}, u32[]{:S(2)}, u32[]{:S(2)}) collective-permute-start(bf16[64,128]{1,0:T(8,128)(2,1)S(1)} %get-tuple-element.224), channel_id=1, source_target_pairs={{0,24},{4,28},{8,16},{12,20},{16,8},{20,12},{24,0},{28,4},{1,25},{... | collective-permute-start | bytes 49160 | tf_op jit(solution)/shard_map/ppermute | solution.py:438
  114.5 1.6 collective-permute-done.35
  116.1 1.4 collective-permute-start.38
  118.3 4.3 %collective-permute-done.38 = bf16[64,128]{1,0:T(8,128)(2,1)S(1)} collective-permute-done((bf16[64,128]{1,0:T(8,128)(2,1)S(1)}, bf16[64,128]{1,0:T(8,128)(2,1)S(1)}, u32[]{:S(2)}, u32[]{:S(2)}) %collective-permute-start.38) | collective-permute-done | bytes 16416 | tf_op jit(solution)/shard_map/ppermute | solution.py:438
  126.3 3.3 %collective-permute-start.42 = (bf16[40,128]{1,0:T(8,128)(2,1)S(1)}, bf16[40,128]{1,0:T(8,128)(2,1)S(1)}, u32[]{:S(2)}, u32[]{:S(2)}) collective-permute-start(bf16[40,128]{1,0:T(8,128)(2,1)S(1)} %shard_map.161.refs_0_), channel_id=1, source_target_pairs={{0,8},{4,12},{8,0},{12,4},{16,24},{20,28},{24,16},{28,20},{1,9},{5... | collective-permute-start | bytes 30728 | tf_op jit(solution)/shard_map/ppermute | solution.py:438
  130.7 2.5 %collective-permute-start.44 = (bf16[40,128]{1,0:T(8,128)(2,1)S(1)}, bf16[40,128]{1,0:T(8,128)(2,1)S(1)}, u32[]{:S(2)}, u32[]{:S(2)}) collective-permute-start(bf16[40,128]{1,0:T(8,128)(2,1)S(1)} %shard_map.161.refs_0_), channel_id=1, source_target_pairs={{0,16},{4,20},{8,24},{12,28},{16,0},{20,4},{24,8},{28,12},{1,17},{... | collective-permute-start | bytes 30728 | tf_op jit(solution)/shard_map/ppermute | solution.py:438
  133.2 1.4 collective-permute-start.45
  134.7 1.6 %collective-permute-start.46 = (bf16[40,128]{1,0:T(8,128)(2,1)S(1)}, bf16[40,128]{1,0:T(8,128)(2,1)S(1)}, u32[]{:S(2)}, u32[]{:S(2)}) collective-permute-start(bf16[40,128]{1,0:T(8,128)(2,1)S(1)} %shard_map.161.refs_0_), channel_id=1, source_target_pairs={{0,24},{4,28},{8,16},{12,20},{16,8},{20,12},{24,0},{28,4},{1,25},{... | collective-permute-start | bytes 30728 | tf_op jit(solution)/shard_map/ppermute | solution.py:438
  136.3 2.1 %collective-permute-start.47 = (bf16[40,128]{1,0:T(8,128)(2,1)S(1)}, bf16[40,128]{1,0:T(8,128)(2,1)S(1)}, u32[]{:S(2)}, u32[]{:S(2)}) collective-permute-start(bf16[40,128]{1,0:T(8,128)(2,1)S(1)} %shard_map.161.refs_0_), channel_id=1, source_target_pairs={{0,28},{4,24},{8,20},{12,16},{16,12},{20,8},{24,4},{28,0},{1,29},{... | collective-permute-start | bytes 30728 | tf_op jit(solution)/shard_map/ppermute | solution.py:438
  138.7 1.4 collective-permute-done.46.refs_6_
  140.1 2.5 %collective-permute-done.47.refs_7_ = bf16[40,128]{1,0:T(8,128)(2,1)S(1)} collective-permute-done((bf16[40,128]{1,0:T(8,128)(2,1)S(1)}, bf16[40,128]{1,0:T(8,128)(2,1)S(1)}, u32[]{:S(2)}, u32[]{:S(2)}) %collective-permute-start.47) | collective-permute-done | bytes 10272 | tf_op jit(solution)/shard_map/ppermute | solution.py:438
  142.7 1.6 shard_map.162
  144.2 3.7 %collective-permute-start.53 = (bf16[8,16,1024]{2,1,0:T(8,128)(2,1)}, bf16[8,16,1024]{2,1,0:T(8,128)(2,1)S(1)}, u32[]{:S(2)}, u32[]{:S(2)}) collective-permute-start(bf16[8,16,1024]{2,1,0:T(8,128)(2,1)} %get-tuple-element.258), channel_id=1, source_target_pairs={{0,12},{4,8},{8,4},{12,0},{16,28},{20,24},{24,20},{28,16},{1,13},{... | collective-permute-start | bytes 786440 | tf_op jit(solution)/shard_map/ppermute | solution.py:438
  149.3 1.4 collective-permute-start.50
  155.2 2.7 %shard_map.163.refs_2_ = bf16[128,16,1024]{2,1,0:T(8,128)(2,1)} custom-call(s32[12]{0:T(128)S(1)} %stack.83.place_ref, bf16[8,16,1024]{2,1,0:T(8,128)(2,1)S(1)} %copy-done.8, bf16[8,16,1024]{2,1,0:T(8,128)(2,1)S(1)} %collective-permute-done.26.refs_1_, bf16[8,16,1024]{2,1,0:T(8,128)(2,1)S(1)} %collective-permute-done.23.refs_2_, ...), custom_call_target="tpu_custom_call", output_to_operand_aliasing={{}: (13, {})} | custom-call | bytes 6291456 | tf_op jit(solution)/shard_map/pallas_call | solution.py:94
  (142 shorter events, 33.0 us)
Async XLA Ops:
  0.7 11.8 %collective-permute-start = (bf16[5,1024]{1,0:T(8,128)(2,1)}, bf16[5,1024]{1,0:T(8,128)(2,1)S(1)}, u32[]{:S(2)}, u32[]{:S(2)}) collective-permute-start(bf16[5,1024]{1,0:T(8,128)(2,1)} %refs_0_.1), channel_id=1, source_target_pairs={{0,4},{4,0},{8,12},{12,8},{16,20},{20,16},{24,28},{28,24},{1,5},{5... | collective-permute-start | bytes 30728 | tf_op jit(solution)/shard_map/ppermute | solution.py:438
  3.8 12.4 %collective-permute-start.1 = (bf16[5,1024]{1,0:T(8,128)(2,1)}, bf16[5,1024]{1,0:T(8,128)(2,1)S(1)}, u32[]{:S(2)}, u32[]{:S(2)}) collective-permute-start(bf16[5,1024]{1,0:T(8,128)(2,1)} %refs_0_.1), channel_id=1, source_target_pairs={{0,8},{4,12},{8,0},{12,4},{16,24},{20,28},{24,16},{28,20},{1,9},{5... | collective-permute-start | bytes 30728 | tf_op jit(solution)/shard_map/ppermute | solution.py:438
  5.3 15.4 %collective-permute-start.2 = (bf16[5,1024]{1,0:T(8,128)(2,1)}, bf16[5,1024]{1,0:T(8,128)(2,1)S(1)}, u32[]{:S(2)}, u32[]{:S(2)}) collective-permute-start(bf16[5,1024]{1,0:T(8,128)(2,1)} %refs_0_.1), channel_id=1, source_target_pairs={{0,12},{4,8},{8,4},{12,0},{16,28},{20,24},{24,20},{28,16},{1,13},{... | collective-permute-start | bytes 30728 | tf_op jit(solution)/shard_map/ppermute | solution.py:438
  5.3 15.4 %collective-permute-start.3 = (bf16[5,1024]{1,0:T(8,128)(2,1)}, bf16[5,1024]{1,0:T(8,128)(2,1)S(1)}, u32[]{:S(2)}, u32[]{:S(2)}) collective-permute-start(bf16[5,1024]{1,0:T(8,128)(2,1)} %refs_0_.1), channel_id=1, source_target_pairs={{0,16},{4,20},{8,24},{12,28},{16,0},{20,4},{24,8},{28,12},{1,17},{... | collective-permute-start | bytes 30728 | tf_op jit(solution)/shard_map/ppermute | solution.py:438
  8.3 12.5 %collective-permute-start.4 = (bf16[5,1024]{1,0:T(8,128)(2,1)}, bf16[5,1024]{1,0:T(8,128)(2,1)S(1)}, u32[]{:S(2)}, u32[]{:S(2)}) collective-permute-start(bf16[5,1024]{1,0:T(8,128)(2,1)} %refs_0_.1), channel_id=1, source_target_pairs={{0,20},{4,16},{8,28},{12,24},{16,4},{20,0},{24,12},{28,8},{1,21},{... | collective-permute-start | bytes 30728 | tf_op jit(solution)/shard_map/ppermute | solution.py:438
  12.5 8.3 %collective-permute-start.5 = (bf16[5,1024]{1,0:T(8,128)(2,1)}, bf16[5,1024]{1,0:T(8,128)(2,1)S(1)}, u32[]{:S(2)}, u32[]{:S(2)}) collective-permute-start(bf16[5,1024]{1,0:T(8,128)(2,1)} %refs_0_.1), channel_id=1, source_target_pairs={{0,24},{4,28},{8,16},{12,20},{16,8},{20,12},{24,0},{28,4},{1,25},{... | collective-permute-start | bytes 30728 | tf_op jit(solution)/shard_map/ppermute | solution.py:438
  16.1 6.6 %collective-permute-start.6 = (bf16[5,1024]{1,0:T(8,128)(2,1)}, bf16[5,1024]{1,0:T(8,128)(2,1)S(1)}, u32[]{:S(2)}, u32[]{:S(2)}) collective-permute-start(bf16[5,1024]{1,0:T(8,128)(2,1)} %refs_0_.1), channel_id=1, source_target_pairs={{0,28},{4,24},{8,20},{12,16},{16,12},{20,8},{24,4},{28,0},{1,29},{... | collective-permute-start | bytes 30728 | tf_op jit(solution)/shard_map/ppermute | solution.py:438
  23.8 8.6 %collective-permute-start.10 = (bf16[8,16,1024]{2,1,0:T(8,128)(2,1)}, bf16[8,16,1024]{2,1,0:T(8,128)(2,1)S(1)}, u32[]{:S(2)}, u32[]{:S(2)}) collective-permute-start(bf16[8,16,1024]{2,1,0:T(8,128)(2,1)} %get-tuple-element.151), channel_id=1, source_target_pairs={{0,24},{4,28},{8,16},{12,20},{16,8},{20,12},{24,0},{28,4},{1,25},{... | collective-permute-start | bytes 786440 | tf_op jit(solution)/shard_map/ppermute | solution.py:438
  32.3 25.4 %collective-permute-start.18 = (bf16[8,16,1024]{2,1,0:T(8,128)(2,1)}, bf16[8,16,1024]{2,1,0:T(8,128)(2,1)S(1)}, u32[]{:S(2)}, u32[]{:S(2)}) collective-permute-start(bf16[8,16,1024]{2,1,0:T(8,128)(2,1)} %get-tuple-element.158), channel_id=1, source_target_pairs={{0,24},{4,28},{8,16},{12,20},{16,8},{20,12},{24,0},{28,4},{1,25},{... | collective-permute-start | bytes 786440 | tf_op jit(solution)/shard_map/ppermute | solution.py:438
  34.2 12.0 %collective-permute-start.11 = (bf16[48,256]{1,0:T(8,128)(2,1)S(1)}, bf16[48,256]{1,0:T(8,128)(2,1)S(1)}, u32[]{:S(2)}, u32[]{:S(2)}) collective-permute-start(bf16[48,256]{1,0:T(8,128)(2,1)S(1)} %shard_map.157.refs_0_), channel_id=1, source_target_pairs={{0,4},{4,0},{8,12},{12,8},{16,20},{20,16},{24,28},{28,24},{1,5},{5... | collective-permute-start | bytes 73736 | tf_op jit(solution)/shard_map/ppermute | solution.py:438
  35.7 13.3 %collective-permute-start.12 = (bf16[48,256]{1,0:T(8,128)(2,1)S(1)}, bf16[48,256]{1,0:T(8,128)(2,1)S(1)}, u32[]{:S(2)}, u32[]{:S(2)}) collective-permute-start(bf16[48,256]{1,0:T(8,128)(2,1)S(1)} %shard_map.157.refs_0_), channel_id=1, source_target_pairs={{0,8},{4,12},{8,0},{12,4},{16,24},{20,28},{24,16},{28,20},{1,9},{5... | collective-permute-start | bytes 73736 | tf_op jit(solution)/shard_map/ppermute | solution.py:438
  45.1 5.6 %collective-permute-start.13 = (bf16[48,256]{1,0:T(8,128)(2,1)S(1)}, bf16[48,256]{1,0:T(8,128)(2,1)S(1)}, u32[]{:S(2)}, u32[]{:S(2)}) collective-permute-start(bf16[48,256]{1,0:T(8,128)(2,1)S(1)} %shard_map.157.refs_0_), channel_id=1, source_target_pairs={{0,12},{4,8},{8,4},{12,0},{16,28},{20,24},{24,20},{28,16},{1,13},{... | collective-permute-start | bytes 73736 | tf_op jit(solution)/shard_map/ppermute | solution.py:438
  45.1 7.8 %collective-permute-start.14 = (bf16[48,256]{1,0:T(8,128)(2,1)S(1)}, bf16[48,256]{1,0:T(8,128)(2,1)S(1)}, u32[]{:S(2)}, u32[]{:S(2)}) collective-permute-start(bf16[48,256]{1,0:T(8,128)(2,1)S(1)} %shard_map.157.refs_0_), channel_id=1, source_target_pairs={{0,16},{4,20},{8,24},{12,28},{16,0},{20,4},{24,8},{28,12},{1,17},{... | collective-permute-start | bytes 73736 | tf_op jit(solution)/shard_map/ppermute | solution.py:438
  46.2 6.8 %collective-permute-start.15 = (bf16[48,256]{1,0:T(8,128)(2,1)S(1)}, bf16[48,256]{1,0:T(8,128)(2,1)S(1)}, u32[]{:S(2)}, u32[]{:S(2)}) collective-permute-start(bf16[48,256]{1,0:T(8,128)(2,1)S(1)} %shard_map.157.refs_0_), channel_id=1, source_target_pairs={{0,20},{4,16},{8,28},{12,24},{16,4},{20,0},{24,12},{28,8},{1,21},{... | collective-permute-start | bytes 73736 | tf_op jit(solution)/shard_map/ppermute | solution.py:438
  49.0 5.9 %collective-permute-start.16 = (bf16[48,256]{1,0:T(8,128)(2,1)S(1)}, bf16[48,256]{1,0:T(8,128)(2,1)S(1)}, u32[]{:S(2)}, u32[]{:S(2)}) collective-permute-start(bf16[48,256]{1,0:T(8,128)(2,1)S(1)} %shard_map.157.refs_0_), channel_id=1, source_target_pairs={{0,24},{4,28},{8,16},{12,20},{16,8},{20,12},{24,0},{28,4},{1,25},{... | collective-permute-start | bytes 73736 | tf_op jit(solution)/shard_map/ppermute | solution.py:438
  50.8 7.0 %collective-permute-start.17 = (bf16[48,256]{1,0:T(8,128)(2,1)S(1)}, bf16[48,256]{1,0:T(8,128)(2,1)S(1)}, u32[]{:S(2)}, u32[]{:S(2)}) collective-permute-start(bf16[48,256]{1,0:T(8,128)(2,1)S(1)} %shard_map.157.refs_0_), channel_id=1, source_target_pairs={{0,28},{4,24},{8,20},{12,16},{16,12},{20,8},{24,4},{28,0},{1,29},{... | collective-permute-start | bytes 73736 | tf_op jit(solution)/shard_map/ppermute | solution.py:438
  58.3 9.6 %collective-permute-start.22 = (bf16[8,16,1024]{2,1,0:T(8,128)(2,1)}, bf16[8,16,1024]{2,1,0:T(8,128)(2,1)S(1)}, u32[]{:S(2)}, u32[]{:S(2)}) collective-permute-start(bf16[8,16,1024]{2,1,0:T(8,128)(2,1)} %get-tuple-element.171), channel_id=1, source_target_pairs={{0,28},{4,24},{8,20},{12,16},{16,12},{20,8},{24,4},{28,0},{1,29},{... | collective-permute-start | bytes 786440 | tf_op jit(solution)/shard_map/ppermute | solution.py:438
  60.3 9.1 %collective-permute-start.23 = (bf16[8,16,1024]{2,1,0:T(8,128)(2,1)}, bf16[8,16,1024]{2,1,0:T(8,128)(2,1)S(1)}, u32[]{:S(2)}, u32[]{:S(2)}) collective-permute-start(bf16[8,16,1024]{2,1,0:T(8,128)(2,1)} %get-tuple-element.172), channel_id=1, source_target_pairs={{0,8},{4,12},{8,0},{12,4},{16,24},{20,28},{24,16},{28,20},{1,9},{5... | collective-permute-start | bytes 786440 | tf_op jit(solution)/shard_map/ppermute | solution.py:438
  60.7 5.2 %collective-permute-start.20 = (bf16[8,40,128]{2,1,0:T(8,128)(2,1)S(1)}, bf16[8,40,128]{2,1,0:T(8,128)(2,1)S(1)}, u32[]{:S(2)}, u32[]{:S(2)}) collective-permute-start(bf16[8,40,128]{2,1,0:T(8,128)(2,1)S(1)} %get-tuple-element.180.refs_0_), channel_id=1, source_target_pairs={{0,2},{1,3},{2,0},{3,1},{4,6},{5,7},{6,4},{7,5},{8,10},{9,11},{10,... | collective-permute-start | bytes 245768 | tf_op jit(solution)/shard_map/ppermute | solution.py:438
  69.5 15.0 %collective-permute-start.24 = (bf16[8,16,1024]{2,1,0:T(8,128)(2,1)}, bf16[8,16,1024]{2,1,0:T(8,128)(2,1)S(1)}, u32[]{:S(2)}, u32[]{:S(2)}) collective-permute-start(bf16[8,16,1024]{2,1,0:T(8,128)(2,1)} %get-tuple-element.189), channel_id=1, source_target_pairs={{0,28},{4,24},{8,20},{12,16},{16,12},{20,8},{24,4},{28,0},{1,29},{... | collective-permute-start | bytes 786440 | tf_op jit(solution)/shard_map/ppermute | solution.py:438
  72.5 12.0 %collective-permute-start.25 = (bf16[8,16,1024]{2,1,0:T(8,128)(2,1)}, bf16[8,16,1024]{2,1,0:T(8,128)(2,1)S(1)}, u32[]{:S(2)}, u32[]{:S(2)}) collective-permute-start(bf16[8,16,1024]{2,1,0:T(8,128)(2,1)} %get-tuple-element.190), channel_id=1, source_target_pairs={{0,8},{4,12},{8,0},{12,4},{16,24},{20,28},{24,16},{28,20},{1,9},{5... | collective-permute-start | bytes 786440 | tf_op jit(solution)/shard_map/ppermute | solution.py:438
  72.5 12.0 %collective-permute-start.26 = (bf16[8,16,1024]{2,1,0:T(8,128)(2,1)}, bf16[8,16,1024]{2,1,0:T(8,128)(2,1)S(1)}, u32[]{:S(2)}, u32[]{:S(2)}) collective-permute-start(bf16[8,16,1024]{2,1,0:T(8,128)(2,1)} %get-tuple-element.191), channel_id=1, source_target_pairs={{0,4},{4,0},{8,12},{12,8},{16,20},{20,16},{24,28},{28,24},{1,5},{5... | collective-permute-start | bytes 786440 | tf_op jit(solution)/shard_map/ppermute | solution.py:438
  84.5 14.3 %collective-permute-start.30 = (bf16[8,16,1024]{2,1,0:T(8,128)(2,1)S(1)}, bf16[8,16,1024]{2,1,0:T(8,128)(2,1)S(1)}, u32[]{:S(2)}, u32[]{:S(2)}) collective-permute-start(bf16[8,16,1024]{2,1,0:T(8,128)(2,1)S(1)} %copy-done.19), channel_id=1, source_target_pairs={{0,16},{4,20},{8,24},{12,28},{16,0},{20,4},{24,8},{28,12},{1,17},{... | collective-permute-start | bytes 786440 | tf_op jit(solution)/shard_map/ppermute | solution.py:438
  87.0 11.8 %collective-permute-start.31 = (bf16[8,16,1024]{2,1,0:T(8,128)(2,1)S(1)}, bf16[8,16,1024]{2,1,0:T(8,128)(2,1)S(1)}, u32[]{:S(2)}, u32[]{:S(2)}) collective-permute-start(bf16[8,16,1024]{2,1,0:T(8,128)(2,1)S(1)} %copy-done.18), channel_id=1, source_target_pairs={{0,12},{4,8},{8,4},{12,0},{16,28},{20,24},{24,20},{28,16},{1,13},{... | collective-permute-start | bytes 786440 | tf_op jit(solution)/shard_map/ppermute | solution.py:438
  88.1 6.3 %collective-permute-start.28 = (bf16[8,64,128]{2,1,0:T(8,128)(2,1)S(1)}, bf16[8,64,128]{2,1,0:T(8,128)(2,1)S(1)}, u32[]{:S(2)}, u32[]{:S(2)}) collective-permute-start(bf16[8,64,128]{2,1,0:T(8,128)(2,1)S(1)} %get-tuple-element.200), channel_id=1, source_target_pairs={{0,2},{1,3},{2,0},{3,1},{4,6},{5,7},{6,4},{7,5},{8,10},{9,11},{10,... | collective-permute-start | bytes 393224 | tf_op jit(solution)/shard_map/ppermute | solution.py:438
  89.5 6.9 %collective-permute-start.29 = (bf16[8,64,128]{2,1,0:T(8,128)(2,1)S(1)}, bf16[8,64,128]{2,1,0:T(8,128)(2,1)S(1)}, u32[]{:S(2)}, u32[]{:S(2)}) collective-permute-start(bf16[8,64,128]{2,1,0:T(8,128)(2,1)S(1)} %get-tuple-element.201), channel_id=1, source_target_pairs={{0,3},{1,2},{2,1},{3,0},{4,7},{5,6},{6,5},{7,4},{8,11},{9,10},{10,... | collective-permute-start | bytes 393224 | tf_op jit(solution)/shard_map/ppermute | solution.py:438
  100.5 22.0 %collective-permute-start.39 = (bf16[8,16,1024]{2,1,0:T(8,128)(2,1)S(1)}, bf16[8,16,1024]{2,1,0:T(8,128)(2,1)S(1)}, u32[]{:S(2)}, u32[]{:S(2)}) collective-permute-start(bf16[8,16,1024]{2,1,0:T(8,128)(2,1)S(1)} %copy-done.17), channel_id=1, source_target_pairs={{0,16},{4,20},{8,24},{12,28},{16,0},{20,4},{24,8},{28,12},{1,17},{... | collective-permute-start | bytes 786440 | tf_op jit(solution)/shard_map/ppermute | solution.py:438
  101.6 21.7 %collective-permute-start.40 = (bf16[8,16,1024]{2,1,0:T(8,128)(2,1)S(1)}, bf16[8,16,1024]{2,1,0:T(8,128)(2,1)S(1)}, u32[]{:S(2)}, u32[]{:S(2)}) collective-permute-start(bf16[8,16,1024]{2,1,0:T(8,128)(2,1)S(1)} %copy-done.16), channel_id=1, source_target_pairs={{0,4},{4,0},{8,12},{12,8},{16,20},{20,16},{24,28},{28,24},{1,5},{5... | collective-permute-start | bytes 786440 | tf_op jit(solution)/shard_map/ppermute | solution.py:438
  102.7 7.0 %collective-permute-start.32 = (bf16[64,128]{1,0:T(8,128)(2,1)S(1)}, bf16[64,128]{1,0:T(8,128)(2,1)S(1)}, u32[]{:S(2)}, u32[]{:S(2)}) collective-permute-start(bf16[64,128]{1,0:T(8,128)(2,1)S(1)} %get-tuple-element.219), channel_id=1, source_target_pairs={{0,4},{4,0},{8,12},{12,8},{16,20},{20,16},{24,28},{28,24},{1,5},{5... | collective-permute-start | bytes 49160 | tf_op jit(solution)/shard_map/ppermute | solution.py:438
  103.6 8.6 %collective-permute-start.33 = (bf16[64,128]{1,0:T(8,128)(2,1)S(1)}, bf16[64,128]{1,0:T(8,128)(2,1)S(1)}, u32[]{:S(2)}, u32[]{:S(2)}) collective-permute-start(bf16[64,128]{1,0:T(8,128)(2,1)S(1)} %get-tuple-element.220), channel_id=1, source_target_pairs={{0,8},{4,12},{8,0},{12,4},{16,24},{20,28},{24,16},{28,20},{1,9},{5... | collective-permute-start | bytes 49160 | tf_op jit(solution)/shard_map/ppermute | solution.py:438
  105.8 6.9 %collective-permute-start.34 = (bf16[64,128]{1,0:T(8,128)(2,1)S(1)}, bf16[64,128]{1,0:T(8,128)(2,1)S(1)}, u32[]{:S(2)}, u32[]{:S(2)}) collective-permute-start(bf16[64,128]{1,0:T(8,128)(2,1)S(1)} %get-tuple-element.221), channel_id=1, source_target_pairs={{0,12},{4,8},{8,4},{12,0},{16,28},{20,24},{24,20},{28,16},{1,13},{... | collective-permute-start | bytes 49160 | tf_op jit(solution)/shard_map/ppermute | solution.py:438
  109.7 6.4 %collective-permute-start.35 = (bf16[64,128]{1,0:T(8,128)(2,1)S(1)}, bf16[64,128]{1,0:T(8,128)(2,1)S(1)}, u32[]{:S(2)}, u32[]{:S(2)}) collective-permute-start(bf16[64,128]{1,0:T(8,128)(2,1)S(1)} %get-tuple-element.222), channel_id=1, source_target_pairs={{0,16},{4,20},{8,24},{12,28},{16,0},{20,4},{24,8},{28,12},{1,17},{... | collective-permute-start | bytes 49160 | tf_op jit(solution)/shard_map/ppermute | solution.py:438
  112.2 5.5 %collective-permute-start.36 = (bf16[64,128]{1,0:T(8,128)(2,1)S(1)}, bf16[64,128]{1,0:T(8,128)(2,1)S(1)}, u32[]{:S(2)}, u32[]{:S(2)}) collective-permute-start(bf16[64,128]{1,0:T(8,128)(2,1)S(1)} %get-tuple-element.223), channel_id=1, source_target_pairs={{0,20},{4,16},{8,28},{12,24},{16,4},{20,0},{24,12},{28,8},{1,21},{... | collective-permute-start | bytes 49160 | tf_op jit(solution)/shard_map/ppermute | solution.py:438
  112.7 5.5 %collective-permute-start.37 = (bf16[64,128]{1,0:T(8,128)(2,1)S(1)}, bf16[64,128]{1,0:T(8,128)(2,1)S(1)}, u32[]{:S(2)}, u32[]{:S(2)}) collective-permute-start(bf16[64,128]{1,0:T(8,128)(2,1)S(1)} %get-tuple-element.224), channel_id=1, source_target_pairs={{0,24},{4,28},{8,16},{12,20},{16,8},{20,12},{24,0},{28,4},{1,25},{... | collective-permute-start | bytes 49160 | tf_op jit(solution)/shard_map/ppermute | solution.py:438
  116.1 6.4 %collective-permute-start.38 = (bf16[64,128]{1,0:T(8,128)(2,1)S(1)}, bf16[64,128]{1,0:T(8,128)(2,1)S(1)}, u32[]{:S(2)}, u32[]{:S(2)}) collective-permute-start(bf16[64,128]{1,0:T(8,128)(2,1)S(1)} %get-tuple-element.225), channel_id=1, source_target_pairs={{0,28},{4,24},{8,20},{12,16},{16,12},{20,8},{24,4},{28,0},{1,29},{... | collective-permute-start | bytes 49160 | tf_op jit(solution)/shard_map/ppermute | solution.py:438
  124.8 17.9 %collective-permute-start.48 = (bf16[8,16,1024]{2,1,0:T(8,128)(2,1)}, bf16[8,16,1024]{2,1,0:T(8,128)(2,1)}, u32[]{:S(2)}, u32[]{:S(2)}) collective-permute-start(bf16[8,16,1024]{2,1,0:T(8,128)(2,1)} %get-tuple-element.238), channel_id=1, source_target_pairs={{0,20},{4,16},{8,28},{12,24},{16,4},{20,0},{24,12},{28,8},{1,21},{... | collective-permute-start | bytes 786440 | tf_op jit(solution)/shard_map/ppermute | solution.py:438
  125.5 7.8 %collective-permute-start.41 = (bf16[40,128]{1,0:T(8,128)(2,1)S(1)}, bf16[40,128]{1,0:T(8,128)(2,1)S(1)}, u32[]{:S(2)}, u32[]{:S(2)}) collective-permute-start(bf16[40,128]{1,0:T(8,128)(2,1)S(1)} %shard_map.161.refs_0_), channel_id=1, source_target_pairs={{0,4},{4,0},{8,12},{12,8},{16,20},{20,16},{24,28},{28,24},{1,5},{5... | collective-permute-start | bytes 30728 | tf_op jit(solution)/shard_map/ppermute | solution.py:438
  126.3 8.4 %collective-permute-start.42 = (bf16[40,128]{1,0:T(8,128)(2,1)S(1)}, bf16[40,128]{1,0:T(8,128)(2,1)S(1)}, u32[]{:S(2)}, u32[]{:S(2)}) collective-permute-start(bf16[40,128]{1,0:T(8,128)(2,1)S(1)} %shard_map.161.refs_0_), channel_id=1, source_target_pairs={{0,8},{4,12},{8,0},{12,4},{16,24},{20,28},{24,16},{28,20},{1,9},{5... | collective-permute-start | bytes 30728 | tf_op jit(solution)/shard_map/ppermute | solution.py:438
  129.6 6.7 %collective-permute-start.43 = (bf16[40,128]{1,0:T(8,128)(2,1)S(1)}, bf16[40,128]{1,0:T(8,128)(2,1)S(1)}, u32[]{:S(2)}, u32[]{:S(2)}) collective-permute-start(bf16[40,128]{1,0:T(8,128)(2,1)S(1)} %shard_map.161.refs_0_), channel_id=1, source_target_pairs={{0,12},{4,8},{8,4},{12,0},{16,28},{20,24},{24,20},{28,16},{1,13},{... | collective-permute-start | bytes 30728 | tf_op jit(solution)/shard_map/ppermute | solution.py:438
  130.7 7.8 %collective-permute-start.44 = (bf16[40,128]{1,0:T(8,128)(2,1)S(1)}, bf16[40,128]{1,0:T(8,128)(2,1)S(1)}, u32[]{:S(2)}, u32[]{:S(2)}) collective-permute-start(bf16[40,128]{1,0:T(8,128)(2,1)S(1)} %shard_map.161.refs_0_), channel_id=1, source_target_pairs={{0,16},{4,20},{8,24},{12,28},{16,0},{20,4},{24,8},{28,12},{1,17},{... | collective-permute-start | bytes 30728 | tf_op jit(solution)/shard_map/ppermute | solution.py:438
  133.2 5.5 %collective-permute-start.45 = (bf16[40,128]{1,0:T(8,128)(2,1)S(1)}, bf16[40,128]{1,0:T(8,128)(2,1)S(1)}, u32[]{:S(2)}, u32[]{:S(2)}) collective-permute-start(bf16[40,128]{1,0:T(8,128)(2,1)S(1)} %shard_map.161.refs_0_), channel_id=1, source_target_pairs={{0,20},{4,16},{8,28},{12,24},{16,4},{20,0},{24,12},{28,8},{1,21},{... | collective-permute-start | bytes 30728 | tf_op jit(solution)/shard_map/ppermute | solution.py:438
  134.7 5.5 %collective-permute-start.46 = (bf16[40,128]{1,0:T(8,128)(2,1)S(1)}, bf16[40,128]{1,0:T(8,128)(2,1)S(1)}, u32[]{:S(2)}, u32[]{:S(2)}) collective-permute-start(bf16[40,128]{1,0:T(8,128)(2,1)S(1)} %shard_map.161.refs_0_), channel_id=1, source_target_pairs={{0,24},{4,28},{8,16},{12,20},{16,8},{20,12},{24,0},{28,4},{1,25},{... | collective-permute-start | bytes 30728 | tf_op jit(solution)/shard_map/ppermute | solution.py:438
  136.3 6.4 %collective-permute-start.47 = (bf16[40,128]{1,0:T(8,128)(2,1)S(1)}, bf16[40,128]{1,0:T(8,128)(2,1)S(1)}, u32[]{:S(2)}, u32[]{:S(2)}) collective-permute-start(bf16[40,128]{1,0:T(8,128)(2,1)S(1)} %shard_map.161.refs_0_), channel_id=1, source_target_pairs={{0,28},{4,24},{8,20},{12,16},{16,12},{20,8},{24,4},{28,0},{1,29},{... | collective-permute-start | bytes 30728 | tf_op jit(solution)/shard_map/ppermute | solution.py:438
  144.2 13.7 %collective-permute-start.52 = (bf16[8,16,1024]{2,1,0:T(8,128)(2,1)}, bf16[8,16,1024]{2,1,0:T(8,128)(2,1)S(1)}, u32[]{:S(2)}, u32[]{:S(2)}) collective-permute-start(bf16[8,16,1024]{2,1,0:T(8,128)(2,1)} %get-tuple-element.257), channel_id=1, source_target_pairs={{0,20},{4,16},{8,28},{12,24},{16,4},{20,0},{24,12},{28,8},{1,21},{... | collective-permute-start | bytes 786440 | tf_op jit(solution)/shard_map/ppermute | solution.py:438
  144.2 13.7 %collective-permute-start.53 = (bf16[8,16,1024]{2,1,0:T(8,128)(2,1)}, bf16[8,16,1024]{2,1,0:T(8,128)(2,1)S(1)}, u32[]{:S(2)}, u32[]{:S(2)}) collective-permute-start(bf16[8,16,1024]{2,1,0:T(8,128)(2,1)} %get-tuple-element.258), channel_id=1, source_target_pairs={{0,12},{4,8},{8,4},{12,0},{16,28},{20,24},{24,20},{28,16},{1,13},{... | collective-permute-start | bytes 786440 | tf_op jit(solution)/shard_map/ppermute | solution.py:438
  149.3 8.7 %collective-permute-start.49 = (f32[10,512]{1,0:T(8,128)}, f32[10,512]{1,0:T(8,128)S(1)}, u32[]{:S(2)}, u32[]{:S(2)}) collective-permute-start(f32[10,512]{1,0:T(8,128)} %get-tuple-element.254), channel_id=1, source_target_pairs={{0,1},{1,0},{2,3},{3,2},{4,5},{5,4},{6,7},{7,6},{8,9},{9,8},{10,11... | collective-permute-start | bytes 61448 | tf_op jit(solution)/shard_map/ppermute | solution.py:438
  149.3 8.7 %collective-permute-start.50 = (f32[10,512]{1,0:T(8,128)}, f32[10,512]{1,0:T(8,128)S(1)}, u32[]{:S(2)}, u32[]{:S(2)}) collective-permute-start(f32[10,512]{1,0:T(8,128)} %get-tuple-element.255), channel_id=1, source_target_pairs={{0,2},{1,3},{2,0},{3,1},{4,6},{5,7},{6,4},{7,5},{8,10},{9,11},{10,... | collective-permute-start | bytes 61448 | tf_op jit(solution)/shard_map/ppermute | solution.py:438
  150.7 7.3 %collective-permute-start.51 = (f32[10,512]{1,0:T(8,128)}, f32[10,512]{1,0:T(8,128)S(1)}, u32[]{:S(2)}, u32[]{:S(2)}) collective-permute-start(f32[10,512]{1,0:T(8,128)} %get-tuple-element.256), channel_id=1, source_target_pairs={{0,3},{1,2},{2,1},{3,0},{4,7},{5,6},{6,5},{7,4},{8,11},{9,10},{10,... | collective-permute-start | bytes 61448 | tf_op jit(solution)/shard_map/ppermute | solution.py:438
  (27 other events, 580.4 us)

commit v7 on v6

--- a/solution.py
+++ b/solution.py
@@ -19,7 +19,7 @@
 SCALE2 = math.log2(math.e) / math.sqrt(HD)
 STAT = 16
 MIB = 1024 * 1024
-PARTS = 2
+CUTS = {1: (0, 16), 2: (0, 8, 16), 3: (0, 8, 16), 4: (0, 6, 16), 5: (0, 10, 16), 6: (0, 6, 16), 7: (0, 6, 16)}
 NT = (((1,), (1,)), ((), ()))
 
 
@@ -27,22 +27,60 @@
     return -(-value // unit) * unit
 
 
-def permute_kernel(source_ref, place_ref, pool_ref, out_ref, *refs):
-    chunk_refs, (pages_ref, in_sem, out_sem) = refs[:-3], refs[-3:]
-    count = chunk_refs[0].shape[0]
-    own = out_ref.at[pl.ds(place_ref[0] * (PARTS * count), PARTS * count)]
-    targets = [own.at[pl.ds(i * count, count)] for i in range(PARTS)] + list(chunk_refs)
-
-    def start(j, carry):
-        pltpu.make_async_copy(
-            pool_ref.at[source_ref[j]], pages_ref.at[j], in_sem.at[j // count]
-        ).start()
-        return carry
-
-    lax.fori_loop(0, pool_ref.shape[0], start, 0)
+def column(row):
+    return jnp.transpose(jnp.broadcast_to(row, (row.shape[1], row.shape[1])))
+
+
+def order_kernel(
+    wide, parts, me_ref, dest_ref, req_ref, idx_ref, pool_ref, out_ref, tag_ref, *refs
+):
+    chunk_refs, refs = refs[: len(parts)], refs[len(parts) :]
+    pages_ref, line_ref, source_ref, in_sem, out_sem, line_sem = refs
+    slots = pool_ref.shape[0]
+    capacity = slots // wide
+    shape = (slots, slots)
+    high = lax.broadcasted_iota(jnp.int32, shape, 0)
+    low = lax.broadcasted_iota(jnp.int32, shape, 1)
+    dest = dest_ref[...]
+    same = column(dest.astype(jnp.float32)) == dest.astype(jnp.float32)
+    rank = jnp.sum(jnp.where(same & (high < low), 1.0, 0.0), axis=0, keepdims=True)
+    moved_to = ((dest ^ me_ref[0]) * capacity).astype(jnp.float32) + rank
+    match = column(moved_to) == low.astype(jnp.float32)
+    source = jnp.sum(jnp.where(match, high.astype(jnp.float32), 0.0), axis=0, keepdims=True)
+    line_ref[...] = source.astype(jnp.int32)
+    copy = pltpu.make_async_copy(line_ref, source_ref, line_sem)
+    copy.start()
+    copy.wait()
+
+    blocks = [(0, capacity, out_ref.at[pl.ds(me_ref[0] * capacity, capacity)])]
+    for (d, first, last), chunk in zip(parts, chunk_refs):
+        blocks.append((d * capacity + first, last - first, chunk))
+    for c, (first, count, _) in enumerate(blocks):
+
+        def start(j, carry, c=c):
+            page = source_ref[0, j]
+            pltpu.make_async_copy(pool_ref.at[page], pages_ref.at[j], in_sem.at[c]).start()
+            return carry
+
+        lax.fori_loop(first, first + count, start, 0)
+
+    shifted = idx_ref[...] + 1
+    fields = (req_ref[...], shifted // 32, shifted % 32)
+    rank_col = column(rank)
+    lane = low.astype(jnp.float32)
+    spread_out = jnp.zeros(shape, jnp.float32)
+    for i, field in enumerate(fields):
+        picked = lane == rank_col + float(i * capacity)
+        spread_out = spread_out + jnp.where(picked, column(field.astype(jnp.float32)), 0.0)
+    line = lax.broadcasted_iota(jnp.int32, (wide, slots), 0)
+    chosen = jnp.where(line == dest, 1.0, 0.0).astype(jnp.bfloat16)
+    tag_ref[...] = jnp.dot(
+        chosen, spread_out.astype(jnp.bfloat16), preferred_element_type=jnp.float32
+    )
+
     copies = []
-    for c, target in enumerate(targets):
-        held = pages_ref.at[pl.ds(c * count, count)]
+    for c, (first, count, target) in enumerate(blocks):
+        held = pages_ref.at[pl.ds(first, count)]
         pltpu.make_async_copy(pool_ref.at[pl.ds(0, count)], held, in_sem.at[c]).wait()
         copies.append(pltpu.make_async_copy(held, target, out_sem.at[c]))
         copies[-1].start()
@@ -50,27 +88,31 @@
         copy.wait()
 
 
-def permute_pages(source_of, place, pool, chunks):
-    part = jax.ShapeDtypeStruct((pool.shape[0] // chunks,) + pool.shape[1:], pool.dtype)
+def order_pages(me, dest, page_req, page_idx, pool, wide, parts):
+    slots = pool.shape[0]
+    part = lambda count: jax.ShapeDtypeStruct((count,) + pool.shape[1:], pool.dtype)
+    out_shape = [part(slots), jax.ShapeDtypeStruct((wide, slots), jnp.float32)]
+    out_shape += [part(last - first) for _, first, last in parts]
+    vmem = pl.BlockSpec(memory_space=pltpu.VMEM)
+    hbm = pl.BlockSpec(memory_space=pltpu.HBM)
     return pl.pallas_call(
-        permute_kernel,
-        out_shape=[jax.ShapeDtypeStruct(pool.shape, pool.dtype)] + [part] * (chunks - PARTS),
-        in_specs=[
-            pl.BlockSpec(memory_space=pltpu.SMEM),
-            pl.BlockSpec(memory_space=pltpu.SMEM),
-            pl.BlockSpec(memory_space=pltpu.HBM),
-        ],
-        out_specs=[pl.BlockSpec(memory_space=pltpu.HBM)] * (1 + chunks - PARTS),
+        functools.partial(order_kernel, wide, parts),
+        out_shape=out_shape,
+        in_specs=[pl.BlockSpec(memory_space=pltpu.SMEM), vmem, vmem, vmem, hbm],
+        out_specs=[hbm, vmem] + [hbm] * len(parts),
         scratch_shapes=[
             pltpu.VMEM(pool.shape, pool.dtype),
-            pltpu.SemaphoreType.DMA((chunks,)),
-            pltpu.SemaphoreType.DMA((chunks,)),
+            pltpu.VMEM((1, slots), jnp.int32),
+            pltpu.SMEM((1, slots), jnp.int32),
+            pltpu.SemaphoreType.DMA((1 + len(parts),)),
+            pltpu.SemaphoreType.DMA((1 + len(parts),)),
+            pltpu.SemaphoreType.DMA,
         ],
         compiler_params=pltpu.CompilerParams(vmem_limit_bytes=56 * MIB),
         cost_estimate=pl.CostEstimate(
             flops=0, bytes_accessed=2 * pool.size * 2, transcendentals=0
         ),
-    )(source_of, place, pool)
+    )(me, dest.reshape(1, -1), page_req.reshape(1, -1), page_idx.reshape(1, -1), pool)
 
 
 def place_kernel(place_ref, *refs):
@@ -80,7 +122,7 @@
         depth = chunk.shape[0]
         copies.append(
             pltpu.make_async_copy(
-                chunk, out_ref.at[pl.ds(place_ref[i] * depth, depth)], sem.at[i]
+                chunk, out_ref.at[pl.ds(place_ref[i], depth)], sem.at[i]
             )
         )
     for copy in copies:
@@ -247,7 +289,7 @@
             pltpu.VMEM((peers,) + queries[0].shape, jnp.bfloat16),
             pltpu.VMEM((pieces, height, HD), jnp.bfloat16),
         ],
-        compiler_params=pltpu.CompilerParams(vmem_limit_bytes=32 * MIB),
+        compiler_params=pltpu.CompilerParams(vmem_limit_bytes=56 * MIB),
         cost_estimate=pl.CostEstimate(
             flops=4 * HEADS * rows * (tokens + extra) * HD,
             bytes_accessed=pool.size * 2,
@@ -256,8 +298,8 @@
     )(me, *queries, pool, pool, keyval, keyval, req_tok, pos_tok, row_info, new_bias)
 
 
-def combine_kernel(piece, last, count, me_ref, *refs):
-    part_refs, refs = refs[:count], refs[count:]
+def combine_kernel(piece, last, count, *refs):
+    part_refs, out_ref = refs[:count], refs[count]
     groups, height = part_refs[0].shape[:2]
     peaks, totals = [], []
     for i in range(count):
@@ -285,38 +327,29 @@
             c = i * groups + j
             result = result + lead[:rows, c : c + 1] * part_refs[i][j, STAT:, :].astype(jnp.float32)
         if last:
-            refs[0][...] = result[:piece].astype(jnp.bfloat16)
+            for i in range(out_ref.shape[0]):
+                out_ref[i] = result[:piece].astype(jnp.bfloat16)
         else:
             stats = split_stats(top[j : j + 1], whole[j : j + 1])
             rest = jnp.zeros((STAT - len(stats), HD), jnp.float32)
-            refs[-1][j] = jnp.concatenate([*stats, rest, result], axis=0).astype(jnp.bfloat16)
-    for d, out_ref in enumerate(refs[:-1]):
-        out_ref[...] = refs[-1][me_ref[0] ^ d]
-
-
-def combine(me, parts, piece, last, apart):
+            out_ref[j] = jnp.concatenate([*stats, rest, result], axis=0).astype(jnp.bfloat16)
+
+
+def combine(parts, piece, repeats=0):
     groups, height = parts[0].shape[:2]
-    if last:
-        out_shape = [jax.ShapeDtypeStruct((piece, HD), jnp.bfloat16)]
-    elif apart:
-        out_shape = [jax.ShapeDtypeStruct((height, HD), jnp.bfloat16)] * groups
-    else:
-        out_shape = [jax.ShapeDtypeStruct((groups, height, HD), jnp.bfloat16)]
-    scratch = [pltpu.VMEM((groups, height, HD), jnp.bfloat16)] if apart and not last else []
+    shape = (repeats, piece, HD) if repeats else (groups, height, HD)
     return pl.pallas_call(
-        functools.partial(combine_kernel, piece, last, len(parts)),
-        out_shape=out_shape,
-        in_specs=[pl.BlockSpec(memory_space=pltpu.SMEM)]
-        + [pl.BlockSpec(memory_space=pltpu.VMEM)] * len(parts),
-        out_specs=[pl.BlockSpec(memory_space=pltpu.VMEM)] * len(out_shape),
-        scratch_shapes=scratch,
+        functools.partial(combine_kernel, piece, repeats > 0, len(parts)),
+        out_shape=jax.ShapeDtypeStruct(shape, jnp.bfloat16),
+        in_specs=[pl.BlockSpec(memory_space=pltpu.VMEM)] * len(parts),
+        out_specs=pl.BlockSpec(memory_space=pltpu.VMEM),
         compiler_params=pltpu.CompilerParams(vmem_limit_bytes=8 * MIB),
         cost_estimate=pl.CostEstimate(
             flops=2 * len(parts) * parts[0].size,
             bytes_accessed=len(parts) * parts[0].size * 2,
             transcendentals=0,
         ),
-    )(me, *parts)
+    )(*parts)
 
 
 def reorder(shape, unit, valid, own, column):
@@ -328,18 +361,17 @@
     return match.astype(jnp.bfloat16)
 
 
-def project_kernel(count, peers, me_ref, *refs):
-    hidden_refs, (query_ref, keyval_ref), refs = refs[:count], refs[count : count + 2], refs[count + 2 :]
+def project_kernel(peers, me_ref, hidden_ref, query_ref, keyval_ref, *refs):
     out_refs, (full_ref,) = refs[:peers], refs[peers:]
-    local, depth = hidden_refs[0].shape
+    count, local, depth = hidden_ref.shape
     unit = up(local, 8)
     blocks = []
-    for ref in hidden_refs:
-        blocks.append(ref[...].astype(jnp.float32))
+    for i in range(count):
+        blocks.append(hidden_ref[i].astype(jnp.float32))
         if unit > local:
             blocks.append(jnp.zeros((unit - local, depth), jnp.float32))
     hidden = jnp.concatenate(blocks, axis=0).astype(jnp.bfloat16)
-    order = reorder((count * local, count * unit), unit, local, me_ref[0], True)
+    order = reorder((count * local, count * unit), unit, local, 0, True)
     hidden = jnp.dot(order, hidden, preferred_element_type=jnp.float32).astype(jnp.bfloat16)
     full_ref[...] = jnp.dot(hidden, query_ref[...], preferred_element_type=jnp.float32)
     keyval = jnp.dot(hidden, keyval_ref[...], preferred_element_type=jnp.float32)
@@ -350,40 +382,38 @@
 
 
 def pack_kernel(peers, *refs):
-    own = refs[:peers]
+    own, tag_ref, out_ref = refs[:peers], refs[peers], refs[peers + 1]
     total = (own[0][...] + own[1][...]) + (own[2][...] + own[3][...])
-    refs[-1][...] = jnp.concatenate([total, refs[peers][...]], axis=0).astype(jnp.bfloat16)
-
-
-def unpack_kernel(count, rows, me_ref, *refs):
-    part_refs, (query_ref, keyval_ref, tag_ref) = refs[:count], refs[count:]
+    tags = jnp.concatenate([tag_ref[...], jnp.zeros_like(tag_ref[...])], axis=1)
+    packed = jnp.concatenate([total, tags], axis=0).astype(jnp.bfloat16)
+    for i in range(out_ref.shape[0]):
+        out_ref[i] = packed
+
+
+def unpack_kernel(rows, me_ref, part_ref, query_ref, keyval_ref, tag_ref):
+    count = part_ref.shape[0]
     line = lax.broadcasted_iota(jnp.int32, (count, HD), 0)
     tags = jnp.zeros((count, HD), jnp.float32)
-    for d, ref in enumerate(part_refs):
-        source = me_ref[0] ^ d
-        part = ref[...].astype(jnp.float32)
-        query_ref[source] = part[:rows, :HD].astype(jnp.bfloat16)
-        fill = jnp.zeros((keyval_ref.shape[0] - rows, HD), jnp.float32)
+    fill = jnp.zeros((keyval_ref.shape[0] - rows, HD), jnp.float32)
+    for i in range(count):
+        part = part_ref[i].astype(jnp.float32)
+        query_ref[i] = part[:rows, :HD].astype(jnp.bfloat16)
         block = jnp.concatenate([part[:rows, HD:], fill], axis=0).astype(jnp.bfloat16)
-        keyval_ref[:, pl.ds(pl.multiple_of(source * HD, HD), HD)] = block
-        tag = jnp.sum(jnp.where(line == me_ref[0], part[rows:, :HD], 0.0), axis=0, keepdims=True)
-        tags = tags + jnp.where(line == source, tag, 0.0)
+        keyval_ref[:, i * HD : (i + 1) * HD] = block
+        mine = jnp.where(line == me_ref[0], part[rows : rows + count, :HD], 0.0)
+        tags = tags + jnp.where(line == i, jnp.sum(mine, axis=0, keepdims=True), 0.0)
     tag_ref[...] = tags
 
 
-def finish_kernel(count, peers, me_ref, *refs):
-    part_refs, weight_ref, refs = refs[:count], refs[count], refs[count + 1 :]
-    out_refs, (whole_ref,) = refs[:peers], refs[peers:]
-    rows = whole_ref.shape[0]
+def finish_kernel(peers, me_ref, part_ref, weight_ref, *refs):
+    count, rows = part_ref.shape[:2]
     local = rows // peers
     unit = up(local, 16)
-    for d, ref in enumerate(part_refs):
-        start = pl.multiple_of((me_ref[0] ^ d) * HD, HD)
-        whole_ref[:, pl.ds(start, HD)] = ref[...]
+    whole = jnp.concatenate([part_ref[i] for i in range(count)], axis=1)
     order = reorder((peers * unit, rows), unit, local, me_ref[1], False)
-    mixed = jnp.dot(order, whole_ref[...], preferred_element_type=jnp.float32)
+    mixed = jnp.dot(order, whole, preferred_element_type=jnp.float32)
     mixed = jnp.dot(mixed.astype(jnp.bfloat16), weight_ref[...], preferred_element_type=jnp.float32)
-    for d, out_ref in enumerate(out_refs):
+    for d, out_ref in enumerate(refs):
         out_ref[...] = mixed[d * unit : d * unit + local]
 
 
@@ -443,66 +473,53 @@
     def deal(blocks, axis):
         return [blocks[0]] + [send(block, axis, d) for d, block in enumerate(blocks) if d]
 
-    if direct:
-        gathered = share(hidden, "wide")
-    else:
-        gathered = spread(hidden, "wide").reshape(rows, -1)
-
-    dest = moves[:, 0]
-    order = jnp.arange(slots, dtype=jnp.int32)
-    rank = jnp.sum((dest[:, None] == dest[None, :]) & (order[None, :] < order[:, None]), axis=1)
-    target = dest * capacity + rank
-    chosen = target[None, :] == order[:, None]
-    moved_to = (dest ^ me) * capacity + rank
-    source_of = jnp.sum(
-        jnp.where(moved_to[None, :] == order[:, None], order[None, :], 0), axis=1
-    )
-    sent_req = jnp.sum(jnp.where(chosen, page_req[None, :], 0), axis=1)
-    sent_idx = jnp.sum(jnp.where(chosen, page_idx[None, :], 0), axis=1)
-    moved_pool, *chunks = permute_pages(source_of, me.reshape(1), pool, wide * PARTS)
+    gathered = spread(hidden, "wide")
+
+    parts = []
+    for d in range(1, wide):
+        cuts = [cut * capacity // 16 for cut in CUTS[group_of(d, wide)]]
+        parts += [(d, a, b) for a, b in zip(cuts[:-1], cuts[1:]) if b > a]
+    moved_pool, tags, *chunks = order_pages(
+        both, moves, page_req, page_idx, pool, wide, parts
+    )
     arrived = {}
     flying = {}
 
-    def members(groups):
-        return [
-            (d - 1) * PARTS + part
-            for group, part in groups
-            for d in range(1, wide)
-            if group_of(d, wide) == group
-        ]
-
-    def launch(values, *groups):
-        taken = members(groups)
+    def members(names):
+        taken = []
+        for group, which in names:
+            cut = CUTS[group][which] * capacity // 16
+            end = CUTS[group][which + 1] * capacity // 16
+            taken += [
+                c
+                for c, (d, first, last) in enumerate(parts)
+                if group_of(d, wide) == group and (first, last) == (cut, end)
+            ]
+        return taken
+
+    def launch(values, *names):
+        taken = members(names)
         values, sent = lax.optimization_barrier((values, [chunks[c] for c in taken]))
         for c, chunk in zip(taken, sent):
-            flying[c] = send(chunk, "wide", 1 + c // PARTS)
+            flying[c] = send(chunk, "wide", parts[c][0])
         return values
 
-    def land(values, *groups):
-        taken = members(groups)
+    def land(values, *names):
+        taken = members(names)
         values, got = lax.optimization_barrier((values, [flying[c] for c in taken]))
         arrived.update(zip(taken, got))
         return values
 
-    def beside(step, value, *groups):
-        return land(step(launch(value, *groups)), *groups)
+    def beside(step, value, *names):
+        return land(step(launch(value, *names)), *names)
 
     def placed(pages):
         taken = sorted(arrived)
-        place = jnp.stack([(me ^ (1 + c // PARTS)) * PARTS + c % PARTS for c in taken])
+        place = jnp.stack([(me ^ parts[c][0]) * capacity + parts[c][1] for c in taken])
         pages = place_pages(place, [arrived[c] for c in taken], pages)
         arrived.clear()
         return pages
 
-    shifted = sent_idx + 1
-    tags = jnp.concatenate(
-        [
-            sent_req.reshape(wide, capacity),
-            (shifted // 32).reshape(wide, capacity),
-            (shifted % 32).reshape(wide, capacity),
-        ],
-        axis=1,
-    )
     req_tok = jnp.broadcast_to(page_req[:, None], (slots, PAGE)).reshape(1, -1)
     pos_tok = (page_idx[:, None] * PAGE + jnp.arange(PAGE, dtype=jnp.int32)[None, :]).reshape(1, -1)
     row_info = jnp.stack(
@@ -519,12 +536,12 @@
     new_bias = jnp.where(jnp.asarray(causal) & here, 0.0, NEG_FILL).astype(jnp.float32)
     tokens = pool.reshape(slots * PAGE, -1)
     window = {
-        "project": ((6, 0),),
+        "project": ((6, 0), (3, 0)),
         "gather": ((6, 1),),
         "queries": ((7, 0), (2, 0)),
-        "attend": ((7, 1), (2, 1), (1, 1)),
-        "narrow": ((4, 0), (3, 0)),
-        "wide": ((4, 1), (1, 0)),
+        "attend": ((7, 1), (2, 1)),
+        "narrow": ((4, 0), (1, 0)),
+        "wide": ((4, 1),),
         "attn": ((5, 0),),
         "finish": ((5, 1), (3, 1)),
     }
@@ -532,36 +549,36 @@
     if direct:
         block = jax.ShapeDtypeStruct((rows, 2 * HD), jnp.float32)
         partial = in_vmem(
-            functools.partial(project_kernel, wide, narrow),
+            functools.partial(project_kernel, narrow),
             [block] * narrow,
             both,
-            *gathered,
+            gathered,
             w_query,
             w_keyval,
             scratch=[pltpu.VMEM((rows, narrow * HD), jnp.float32)],
         )
         partial = beside(lambda value: deal(value, "narrow"), partial, *window["project"])
-        tags = jnp.pad(tags.astype(jnp.float32), ((0, 0), (0, 2 * HD - tags.shape[1])))
         packed = in_vmem(
             functools.partial(pack_kernel, narrow),
-            jax.ShapeDtypeStruct((rows + wide, 2 * HD), jnp.bfloat16),
+            jax.ShapeDtypeStruct((wide, rows + wide, 2 * HD), jnp.bfloat16),
             None,
             *partial,
             tags,
         )
-        received = beside(lambda value: share(value, "wide"), packed, *window["gather"])
+        received = beside(lambda value: exchange(value, "wide"), packed, *window["gather"])
         queries, keyval, tags_in = in_vmem(
-            functools.partial(unpack_kernel, wide, rows),
+            functools.partial(unpack_kernel, rows),
             [
                 jax.ShapeDtypeStruct((wide, rows, HD), jnp.bfloat16),
                 jax.ShapeDtypeStruct((extra, wide * HD), jnp.bfloat16),
                 jax.ShapeDtypeStruct((wide, HD), jnp.float32),
             ],
             both,
-            *received,
+            received,
         )
         queries = beside(lambda value: share(value, "narrow"), queries, *window["queries"])
     else:
+        gathered = gathered.reshape(rows, -1)
         query_part = jnp.dot(gathered, w_query, preferred_element_type=jnp.float32)
         keyval_part = jnp.dot(gathered, w_keyval, preferred_element_type=jnp.float32)
         query_part = jnp.transpose(query_part.reshape(rows, narrow, own_cols), (1, 0, 2))
@@ -570,7 +587,7 @@
         )
         partial = beside(lambda value: exchange(value, "narrow"), partial, *window["project"])
         projected = jnp.sum(partial, axis=0).astype(jnp.bfloat16)
-        tags = tags.astype(jnp.bfloat16)[:, None]
+        tags = tags[:, : 3 * capacity].astype(jnp.bfloat16)[:, None]
         tags = jnp.pad(tags, ((0, 0), (0, 7), (0, projected.shape[1] - tags.shape[2])))
         packed = jnp.broadcast_to(projected[None], (wide,) + projected.shape)
         packed = jnp.concatenate([packed, tags], axis=1)
@@ -585,45 +602,6 @@
         queries = [jnp.transpose(queries, (1, 0, 2)).reshape(KVH, GROUPS * rows, HD)]
         keyval = jnp.transpose(received[:, :rows, own_cols:], (1, 0, 2)).reshape(rows, -1)
         keyval = jnp.pad(keyval, ((0, extra - rows), (0, 0)))
-
-    parts = beside(
-        lambda value: attend(
-            both, value, keyval, tokens, req_tok, pos_tok, row_info, new_bias, rows, piece
-        ),
-        queries,
-        *window["attend"],
-    )
-    if direct:
-        parts = beside(lambda value: deal(value, "narrow"), parts, *window["narrow"])
-        parts = combine(both, parts, piece, False, True)
-        parts = beside(lambda value: deal(value, "wide"), parts, *window["wide"])
-        (attn,) = combine(both, [part[None] for part in parts], piece, True, True)
-        attn = beside(lambda value: share(value, "wide"), attn, *window["attn"])
-        moved_pool = placed(moved_pool)
-        sums = in_vmem(
-            functools.partial(finish_kernel, wide, narrow),
-            [jax.ShapeDtypeStruct((rows // narrow, w_out.shape[1]), jnp.float32)] * narrow,
-            both,
-            *attn,
-            w_out,
-            scratch=[pltpu.VMEM((rows, wide * HD), jnp.bfloat16)],
-        )
-        sums = beside(lambda value: deal(value, "narrow"), sums, *window["finish"])
-        attended = ((sums[0] + sums[1]) + (sums[2] + sums[3])).astype(jnp.bfloat16)
-    else:
-        parts = beside(lambda value: exchange(value, "narrow"), parts[0], *window["narrow"])
-        parts = parts.reshape((narrow, wide) + parts.shape[1:])
-        (parts,) = combine(both, [parts[i] for i in range(narrow)], piece, False, False)
-        parts = beside(lambda value: exchange(value, "wide"), parts, *window["wide"])
-        (attn,) = combine(both, [parts[i][None] for i in range(wide)], piece, True, False)
-        attn = beside(lambda value: spread(value, "wide"), attn, *window["attn"])
-        moved_pool = placed(moved_pool)
-        attn = jnp.transpose(attn.reshape(-1, rows, HD), (1, 0, 2)).reshape(rows, -1)
-        sums = jnp.dot(attn, w_out, preferred_element_type=jnp.float32)
-        sums = sums.reshape(narrow, rows // narrow, -1)
-        sums = beside(lambda value: exchange(value, "narrow"), sums, *window["finish"])
-        attended = jnp.sum(sums, axis=0).astype(jnp.bfloat16)
-    moved_pool = placed(moved_pool)
 
     tags_in = tags_in.astype(jnp.int32)
     moved_req = tags_in[:, :capacity].reshape(slots)
@@ -637,6 +615,46 @@
     new_entries = jnp.where(
         jnp.arange(STEPS)[None, :, None] < kept[:, None, None], fresh, jnp.zeros((), jnp.bfloat16)
     )
+    mixed = beside(
+        lambda value: attend(
+            both, value, keyval, tokens, req_tok, pos_tok, row_info, new_bias, rows, piece
+        ),
+        queries,
+        *window["attend"],
+    )
+    if direct:
+        mixed = beside(lambda value: deal(value, "narrow"), mixed, *window["narrow"])
+    else:
+        mixed = beside(lambda value: exchange(value, "narrow"), mixed[0], *window["narrow"])
+        mixed = mixed.reshape((narrow, wide) + mixed.shape[1:])
+        mixed = [mixed[i] for i in range(narrow)]
+    mixed = combine(mixed, piece)
+    mixed, pages = lax.optimization_barrier((mixed, moved_pool))
+    pages = placed(pages)
+    mixed = beside(lambda value: exchange(value, "wide"), mixed, *window["wide"])
+    mixed, moved_pool = lax.optimization_barrier((mixed, pages))
+    attn = combine([mixed[i][None] for i in range(wide)], piece, wide)
+    attn = beside(lambda value: exchange(value, "wide"), attn, *window["attn"])
+    attn, new_entries, moved_req, moved_idx = lax.optimization_barrier(
+        (attn, new_entries, moved_req, moved_idx)
+    )
+    if direct:
+        sums = in_vmem(
+            functools.partial(finish_kernel, narrow),
+            [jax.ShapeDtypeStruct((rows // narrow, w_out.shape[1]), jnp.float32)] * narrow,
+            both,
+            attn,
+            w_out,
+        )
+        sums = beside(lambda value: deal(value, "narrow"), sums, *window["finish"])
+        attended = ((sums[0] + sums[1]) + (sums[2] + sums[3])).astype(jnp.bfloat16)
+    else:
+        attn = jnp.transpose(attn.reshape(-1, rows, HD), (1, 0, 2)).reshape(rows, -1)
+        sums = jnp.dot(attn, w_out, preferred_element_type=jnp.float32)
+        sums = sums.reshape(narrow, rows // narrow, -1)
+        sums = beside(lambda value: exchange(value, "narrow"), sums, *window["finish"])
+        attended = jnp.sum(sums, axis=0).astype(jnp.bfloat16)
+    moved_pool = placed(moved_pool)
     return (attended, new_entries, moved_pool, moved_req, moved_idx)
 
 

time: 160 us -> 164 us (1.025)
  waiting for transfers between devices: 41.5 us -> 59.2 us
  starting transfers between devices: 78.5 us -> 61.6 us
  Pallas kernels: 22.8 us -> 25.2 us
  other arithmetic: 6.42 us -> 4.22 us
  local copies, waits for them, and re-layouts: 9.73 us -> 11.4 us
    ppermute x54 -> x25, starting transfers between devices: 78.5 us -> 42.6 us  [send(): lax.ppermute(block, axis, [(i, i ^ d) for i in range(lax.axis_size(axis))])]
    all_to_all x0 -> x4, waiting for transfers between devices: none -> 21.7 us  [the longest x1 11.7 us: on_device(): attn = beside(lambda value: exchange(value, 'wide'), attn, *window['attn'])]
    all_to_all x0 -> x4, starting transfers between devices: none -> 19.1 us  [the longest x2 7.39 us: on_device(): exchange(value, 'wide')]
    ppermute x54 -> x25, waiting for transfers between devices: 41.5 us -> 37.5 us  [send(): lax.ppermute(block, axis, [(i, i ^ d) for i in range(lax.axis_size(axis))])]
    unnamed x42 -> x48, local copies, waits for them, and re-layouts: 7.21 us -> 4.92 us
    reduce_sum x2 -> x0, other arithmetic: 2.23 us -> none  [the longest x1 1.33 us: on_device(): sent_req = jnp.sum(jnp.where(chosen, page_req[None, :], 0), axis=1)]
    pallas_call x3, Pallas kernels: 6.18 us -> 7.98 us  [the longest x1 5.96 us: order_pages(): pl.pallas_call(functools.partial(order_kernel, wide, parts), out_shape=ou...]
  transfers between devices with their start and end apart: 54 -> 29, of which waited for: 22 -> 17; matrix products, arithmetic and copies ran while one was open for 5% -> 5% of each run, Pallas kernels for 10% -> 11%
where the time goes in v7:
time: 164 us; the launch traced here: 163 us
  starting transfers between devices  61.6 us (38%)
  waiting for transfers between devices  59.2 us (36%)
  Pallas kernels  25.2 us (15%)
  local copies, waits for them, and re-layouts  11.4 us (7%)
  other arithmetic  4.22 us (3%)
    ppermute x25, starting transfers between devices, send(): lax.ppermute(block, axis, [(i, i ^ d) for i in range(lax.axis_size(axis))])  42.6 us
    ppermute x25, waiting for transfers between devices, send(): lax.ppermute(block, axis, [(i, i ^ d) for i in range(lax.axis_size(axis))])  37.5 us
    all_to_all x1, waiting for transfers between devices, on_device(): attn = beside(lambda value: exchange(value, 'wide'), attn, *window['attn'])  11.7 us
    pallas_call x1, Pallas kernels, attend(): pl.pallas_call(functools.partial(attend_kernel, rows, piece, peers), grid...  10.4 us
    all_to_all x2, waiting for transfers between devices, on_device(): exchange(value, 'wide')  9.3 us
    all_to_all x2, starting transfers between devices, on_device(): exchange(value, 'wide')  7.39 us
    all_to_all x1, starting transfers between devices, spread(): lax.all_to_all(jnp.broadcast_to(block[None], (count,) + block.shape), axi...  7.28 us
    pallas_call x1, Pallas kernels, order_pages(): pl.pallas_call(functools.partial(order_kernel, wide, parts), out_shape=ou...  5.96 us
  transfers between devices with their start and end apart: 29, of which 17 were waited for; matrix products, arithmetic and copies ran while one was open for 5% of the time, Pallas kernels for 11%

profile of v7, /device:TPU:0, one launch (start us, length us, event | category | flops | bytes accessed | tf_op | source)
XLA Modules:
  0.0 162.6 jit_solution(16015702313819010346)
XLA Ops:
  0.7 1.5 broadcast_in_dim.22
  2.2 7.3 %all-to-all-start = ((bf16[8,5,1024]{2,1,0:T(8,128)(2,1)}), bf16[8,5,1024]{2,1,0:T(8,128)(2,1)S(1)}, u32[]{:S(2)}, u32[]{:S(2)}) async-start(bf16[8,5,1024]{2,1,0:T(8,128)(2,1)} %broadcast_in_dim.22), calls=%async_computation | async-start | bytes 262144 | tf_op jit(solution)/shard_map/all_to_all | solution.py:442
  10.1 6.0 %shard_map.156 = (bf16[128,16,1024]{2,1,0:T(8,128)(2,1)}, f32[8,128]{1,0:T(8,128)}, bf16[16,16,1024]{2,1,0:T(8,128)(2,1)}, bf16[8,16,1024]{2,1,0:T(8,128)(2,1)},...) custom-call(s32[2]{0:T(128)} %pad_add_fusion.1.me_ref, ...), custom_call_target="tpu_custom_call" | custom-call | bytes 8388608 | tf_op jit(solution)/shard_map/pallas_call | solution.py:98
  16.8 1.0 shard_map.155
  17.8 2.3 %collective-permute-start.4 = (bf16[8,16,1024]{2,1,0:T(8,128)(2,1)}, bf16[8,16,1024]{2,1,0:T(8,128)(2,1)S(1)}, u32[]{:S(2)}, u32[]{:S(2)}) collective-permute-start(bf16[8,16,1024]{2,1,0:T(8,128)(2,1)} %get-tuple-element.123), channel_id=1, source_target_pairs={{0,12},{4,8},{8,4},{12,0},{16,28},{20,24},{24,20},{28,16},{1,13},{... | collective-permute-start | bytes 786440 | tf_op jit(solution)/shard_map/ppermute | solution.py:468
  20.1 2.4 %collective-permute-start.3 = (bf16[6,16,1024]{2,1,0:T(8,128)(2,1)}, bf16[6,16,1024]{2,1,0:T(8,128)(2,1)S(1)}, u32[]{:S(2)}, u32[]{:S(2)}) collective-permute-start(bf16[6,16,1024]{2,1,0:T(8,128)(2,1)} %get-tuple-element.122), channel_id=1, source_target_pairs={{0,24},{4,28},{8,16},{12,20},{16,8},{20,12},{24,0},{28,4},{1,25},{... | collective-permute-start | bytes 589832 | tf_op jit(solution)/shard_map/ppermute | solution.py:468
  22.5 1.5 collective-permute-start.1
  24.4 2.1 %collective-permute-done.1.refs_2_ = f32[40,256]{1,0:T(8,128)S(1)} collective-permute-done((f32[40,256]{1,0:T(8,128)S(1)}, f32[40,256]{1,0:T(8,128)S(1)}, u32[]{:S(2)}, u32[]{:S(2)}) %collective-permute-start.1) | collective-permute-done | bytes 40992 | tf_op jit(solution)/shard_map/ppermute | solution.py:468
  26.5 1.0 collective-permute-done.2.refs_3_
  27.5 4.8 %collective-permute-done.3.refs_5_ = bf16[6,16,1024]{2,1,0:T(8,128)(2,1)S(1)} collective-permute-done((bf16[6,16,1024]{2,1,0:T(8,128)(2,1)}, bf16[6,16,1024]{2,1,0:T(8,128)(2,1)S(1)}, u32[]{:S(2)}, u32[]{:S(2)}) %collective-permute-start.3) | collective-permute-done | bytes 196640 | tf_op jit(solution)/shard_map/ppermute | solution.py:468
  33.8 3.4 %all-to-all-start.1 = ((bf16[8,48,256]{2,1,0:T(8,128)(2,1)}), bf16[8,48,256]{2,1,0:T(8,128)(2,1)S(1)}, u32[]{:S(2)}, u32[]{:S(2)}) async-start(bf16[8,48,256]{2,1,0:T(8,128)(2,1)} %shard_map.157), calls=%async_computation.1 | async-start | bytes 393216 | tf_op jit(solution)/shard_map/all_to_all | solution.py:568
  37.2 3.8 %collective-permute-start.5 = (bf16[10,16,1024]{2,1,0:T(8,128)(2,1)}, bf16[10,16,1024]{2,1,0:T(8,128)(2,1)S(1)}, u32[]{:S(2)}, u32[]{:S(2)}) collective-permute-start(bf16[10,16,1024]{2,1,0:T(8,128)(2,1)} %get-tuple-element.131), channel_id=1, source_target_pairs={{0,24},{4,28},{8,16},{12,20},{16,8},{20,12},{24,0},{28,4},{1,25},{... | collective-permute-start | bytes 983048 | tf_op jit(solution)/shard_map/ppermute | solution.py:468
  40.9 9.3 %collective-permute-done.5.refs_6_ = bf16[10,16,1024]{2,1,0:T(8,128)(2,1)S(1)} collective-permute-done((bf16[10,16,1024]{2,1,0:T(8,128)(2,1)}, bf16[10,16,1024]{2,1,0:T(8,128)(2,1)S(1)}, u32[]{:S(2)}, u32[]{:S(2)}) %collective-permute-start.5) | collective-permute-done | bytes 327712 | tf_op jit(solution)/shard_map/ppermute | solution.py:468
  50.2 1.7 %all-to-all-done.1.part_ref = bf16[8,48,256]{2,1,0:T(8,128)(2,1)S(1)} async-done(((bf16[8,48,256]{2,1,0:T(8,128)(2,1)}), bf16[8,48,256]{2,1,0:T(8,128)(2,1)S(1)}, u32[]{:S(2)}, u32[]{:S(2)}) %all-to-all-start.1) | async-done | bytes 196640 | tf_op jit(solution)/shard_map/all_to_all | solution.py:568
  53.2 2.4 %collective-permute-start.9 = (bf16[6,16,1024]{2,1,0:T(8,128)(2,1)}, bf16[6,16,1024]{2,1,0:T(8,128)(2,1)S(1)}, u32[]{:S(2)}, u32[]{:S(2)}) collective-permute-start(bf16[6,16,1024]{2,1,0:T(8,128)(2,1)} %get-tuple-element.137), channel_id=1, source_target_pairs={{0,28},{4,24},{8,20},{12,16},{16,12},{20,8},{24,4},{28,0},{1,29},{... | collective-permute-start | bytes 589832 | tf_op jit(solution)/shard_map/ppermute | solution.py:468
  55.6 9.3 %collective-permute-start.10 = (bf16[8,16,1024]{2,1,0:T(8,128)(2,1)}, bf16[8,16,1024]{2,1,0:T(8,128)(2,1)S(1)}, u32[]{:S(2)}, u32[]{:S(2)}) collective-permute-start(bf16[8,16,1024]{2,1,0:T(8,128)(2,1)} %get-tuple-element.138), channel_id=1, source_target_pairs={{0,8},{4,12},{8,0},{12,4},{16,24},{20,28},{24,16},{28,20},{1,9},{5... | collective-permute-start | bytes 786440 | tf_op jit(solution)/shard_map/ppermute | solution.py:468
  65.2 1.6 collective-permute-start.7
  69.9 1.8 %collective-permute-done.7.refs_2_ = bf16[8,40,128]{2,1,0:T(8,128)(2,1)S(1)} collective-permute-done((bf16[8,40,128]{2,1,0:T(8,128)(2,1)S(1)}, bf16[8,40,128]{2,1,0:T(8,128)(2,1)S(1)}, u32[]{:S(2)}, u32[]{:S(2)}) %collective-permute-start.7) | collective-permute-done | bytes 81952 | tf_op jit(solution)/shard_map/ppermute | solution.py:468
  72.4 0.9 collective-permute-start.11
  74.0 10.4 %shard_map.159 = (bf16[8,64,128]{2,1,0:T(8,128)(2,1)}, bf16[8,64,128]{2,1,0:T(8,128)(2,1)}, bf16[8,64,128]{2,1,0:T(8,128)(2,1)}, bf16[8,64,128]{2,1,0:T(8,128)(2,1)}) custom-call(s32[2]{0:T(128)} %pad_add_fusion.1.me_ref, bf16[8,40,128]{2,1,0:T(8,128)(2,1)} %copy-done.9, bf16[8,40,128]{2,1,0:T(8,128)(2,1)} %copy-done.15, bf16[8,40,128]{2,1,0:T(8,128)(2,1)} %copy-done.14, ...), custom_call_target="tpu_custom_call" | custom-call | flops 1426063360 | bytes 4194304 | tf_op jit(solution)/shard_map/pallas_call | solution.py:268
  84.4 2.9 %collective-permute-done.11.refs_8_ = bf16[10,16,1024]{2,1,0:T(8,128)(2,1)S(1)} collective-permute-done((bf16[10,16,1024]{2,1,0:T(8,128)(2,1)}, bf16[10,16,1024]{2,1,0:T(8,128)(2,1)S(1)}, u32[]{:S(2)}, u32[]{:S(2)}) %collective-permute-start.11) | collective-permute-done | bytes 327712 | tf_op jit(solution)/shard_map/ppermute | solution.py:468
  87.3 2.9 %collective-permute-start.17 = (bf16[16,16,1024]{2,1,0:T(8,128)(2,1)S(1)}, bf16[16,16,1024]{2,1,0:T(8,128)(2,1)S(1)}, u32[]{:S(2)}, u32[]{:S(2)}) collective-permute-start(bf16[16,16,1024]{2,1,0:T(8,128)(2,1)S(1)} %copy-done.21), channel_id=1, source_target_pairs={{0,4},{4,0},{8,12},{12,8},{16,20},{20,16},{24,28},{28,24},{1,5},{5... | collective-permute-start | bytes 1572872 | tf_op jit(solution)/shard_map/ppermute | solution.py:468
  90.2 2.8 %collective-permute-start.16 = (bf16[6,16,1024]{2,1,0:T(8,128)(2,1)S(1)}, bf16[6,16,1024]{2,1,0:T(8,128)(2,1)S(1)}, u32[]{:S(2)}, u32[]{:S(2)}) collective-permute-start(bf16[6,16,1024]{2,1,0:T(8,128)(2,1)S(1)} %copy-done.22), channel_id=1, source_target_pairs={{0,16},{4,20},{8,24},{12,28},{16,0},{20,4},{24,8},{28,12},{1,17},{... | collective-permute-start | bytes 589832 | tf_op jit(solution)/shard_map/ppermute | solution.py:468
  93.4 1.5 collective-permute-start.15
  94.9 4.6 %collective-permute-done.14.refs_2_ = bf16[8,64,128]{2,1,0:T(8,128)(2,1)S(1)} collective-permute-done((bf16[8,64,128]{2,1,0:T(8,128)(2,1)}, bf16[8,64,128]{2,1,0:T(8,128)(2,1)S(1)}, u32[]{:S(2)}, u32[]{:S(2)}) %collective-permute-start.14) | collective-permute-done | bytes 131104 | tf_op jit(solution)/shard_map/ppermute | solution.py:468
  99.5 2.0 %collective-permute-done.15.refs_3_ = bf16[8,64,128]{2,1,0:T(8,128)(2,1)S(1)} collective-permute-done((bf16[8,64,128]{2,1,0:T(8,128)(2,1)}, bf16[8,64,128]{2,1,0:T(8,128)(2,1)S(1)}, u32[]{:S(2)}, u32[]{:S(2)}) %collective-permute-start.15) | collective-permute-done | bytes 131104 | tf_op jit(solution)/shard_map/ppermute | solution.py:468
  101.7 0.9 copy-done.8
  102.6 1.1 shard_map.160
  103.7 3.9 %collective-permute-start.18 = (bf16[10,16,1024]{2,1,0:T(8,128)(2,1)}, bf16[10,16,1024]{2,1,0:T(8,128)(2,1)S(1)}, u32[]{:S(2)}, u32[]{:S(2)}) collective-permute-start(bf16[10,16,1024]{2,1,0:T(8,128)(2,1)} %get-tuple-element.176), channel_id=1, source_target_pairs={{0,16},{4,20},{8,24},{12,28},{16,0},{20,4},{24,8},{28,12},{1,17},{... | collective-permute-start | bytes 983048 | tf_op jit(solution)/shard_map/ppermute | solution.py:468
  107.7 4.0 %all-to-all-start.2 = ((bf16[8,64,128]{2,1,0:T(8,128)(2,1)}), bf16[8,64,128]{2,1,0:T(8,128)(2,1)}, u32[]{:S(2)}, u32[]{:S(2)}) async-start(bf16[8,64,128]{2,1,0:T(8,128)(2,1)} %shard_map.160), calls=%async_computation.2 | async-start | bytes 262144 | tf_op jit(solution)/shard_map/all_to_all | solution.py:634
  113.1 0.9 copy-done.5
  114.0 0.9 copy-done.7
  114.9 2.1 %shard_map.161.refs_4_ = bf16[128,16,1024]{2,1,0:T(8,128)(2,1)} custom-call(s32[9]{0:T(128)S(1)} %stack.74.place_ref, bf16[16,16,1024]{2,1,0:T(8,128)(2,1)S(1)} %collective-permute-done.17.refs_0_, bf16[8,16,1024]{2,1,0:T(8,128)(2,1)S(1)} %collective-permute-done.10.refs_1_, ...), custom_call_target="tpu_custom_call", output_to_operand_aliasing={{}: (10, {})} | custom-call | bytes 9437184 | tf_op jit(solution)/shard_map/pallas_call | solution.py:136
  117.0 7.6 %all-to-all-done.2 = bf16[8,64,128]{2,1,0:T(8,128)(2,1)} async-done(((bf16[8,64,128]{2,1,0:T(8,128)(2,1)}), bf16[8,64,128]{2,1,0:T(8,128)(2,1)}, u32[]{:S(2)}, u32[]{:S(2)}) %all-to-all-start.2) | async-done | bytes 131104 | tf_op jit(solution)/shard_map/all_to_all | solution.py:634
  124.6 0.8 fusion
  125.5 0.9 shard_map.162
  126.4 1.1 collective-permute-start.19
  128.7 4.4 %all-to-all-start.3 = ((bf16[8,40,128]{2,1,0:T(8,128)(2,1)}), bf16[8,40,128]{2,1,0:T(8,128)(2,1)S(1)}, u32[]{:S(2)}, u32[]{:S(2)}) async-start(bf16[8,40,128]{2,1,0:T(8,128)(2,1)} %shard_map.162), calls=%async_computation.3 | async-start | bytes 163840 | tf_op jit(solution)/shard_map/all_to_all | solution.py:637
  133.1 1.4 select_bitcast_fusion
  134.6 11.7 %all-to-all-done.3.part_ref = bf16[8,40,128]{2,1,0:T(8,128)(2,1)S(1)} async-done(((bf16[8,40,128]{2,1,0:T(8,128)(2,1)}), bf16[8,40,128]{2,1,0:T(8,128)(2,1)S(1)}, u32[]{:S(2)}, u32[]{:S(2)}) %all-to-all-start.3) | async-done | bytes 81952 | tf_op jit(solution)/shard_map/all_to_all | solution.py:637
  146.2 0.9 shard_map.163
  147.2 0.7 collective-permute-start.24
  147.9 2.6 %collective-permute-start.23 = (bf16[6,16,1024]{2,1,0:T(8,128)(2,1)}, bf16[6,16,1024]{2,1,0:T(8,128)(2,1)S(1)}, u32[]{:S(2)}, u32[]{:S(2)}) collective-permute-start(bf16[6,16,1024]{2,1,0:T(8,128)(2,1)} %get-tuple-element.205), channel_id=1, source_target_pairs={{0,20},{4,16},{8,28},{12,24},{16,4},{20,0},{24,12},{28,8},{1,21},{... | collective-permute-start | bytes 589832 | tf_op jit(solution)/shard_map/ppermute | solution.py:468
  150.6 1.8 %collective-permute-start.22 = (f32[10,512]{1,0:T(8,128)S(1)}, f32[10,512]{1,0:T(8,128)S(1)}, u32[]{:S(2)}, u32[]{:S(2)}) collective-permute-start(f32[10,512]{1,0:T(8,128)S(1)} %get-tuple-element.204), channel_id=1, source_target_pairs={{0,3},{1,2},{2,1},{3,0},{4,7},{5,6},{6,5},{7,4},{8,11},{9,10},{10,... | collective-permute-start | bytes 61448 | tf_op jit(solution)/shard_map/ppermute | solution.py:468
  152.5 2.2 %collective-permute-done.21 = f32[10,512]{1,0:T(8,128)S(1)} collective-permute-done((f32[10,512]{1,0:T(8,128)S(1)}, f32[10,512]{1,0:T(8,128)S(1)}, u32[]{:S(2)}, u32[]{:S(2)}) %collective-permute-start.21) | collective-permute-done | bytes 20512 | tf_op jit(solution)/shard_map/ppermute | solution.py:468
  154.7 3.5 %collective-permute-done.23.refs_3_ = bf16[6,16,1024]{2,1,0:T(8,128)(2,1)S(1)} collective-permute-done((bf16[6,16,1024]{2,1,0:T(8,128)(2,1)}, bf16[6,16,1024]{2,1,0:T(8,128)(2,1)S(1)}, u32[]{:S(2)}, u32[]{:S(2)}) %collective-permute-start.23) | collective-permute-done | bytes 196640 | tf_op jit(solution)/shard_map/ppermute | solution.py:468
  158.2 2.3 %collective-permute-done.24.refs_0_ = bf16[8,16,1024]{2,1,0:T(8,128)(2,1)S(1)} collective-permute-done((bf16[8,16,1024]{2,1,0:T(8,128)(2,1)}, bf16[8,16,1024]{2,1,0:T(8,128)(2,1)S(1)}, u32[]{:S(2)}, u32[]{:S(2)}) %collective-permute-start.24) | collective-permute-done | bytes 262176 | tf_op jit(solution)/shard_map/ppermute | solution.py:468
  161.1 1.6 shard_map.164
  (91 shorter events, 13.1 us)
Async XLA Ops:
  0.6 66.4 %copy-start.19 = (s32[40,1]{0,1:T(1,128)S(1)}, s32[40,1]{0,1:T(1,128)}, u32[]{:S(2)}) copy-start(s32[40,1]{0,1:T(1,128)} %constant.52) | copy-start | bytes 484
  0.6 72.7 %copy-start.16 = (pred[40,128]{1,0:T(8,128)(4,1)S(1)}, pred[40,128]{1,0:T(8,128)(4,1)}, u32[]{:S(2)}) copy-start(pred[40,128]{1,0:T(8,128)(4,1)} %constant.50.clone) | copy-start | bytes 15364
  0.7 67.8 %copy-start.17 = (s32[128]{0:T(128)S(1)}, s32[128]{0:T(128)}, u32[]{:S(2)}) copy-start(s32[128]{0:T(128)} %param.17) | copy-start | bytes 1540
  0.7 40.3 %copy-start.20 = (s32[128]{0:T(128)S(1)}, s32[128]{0:T(128)}, u32[]{:S(2)}) copy-start(s32[128]{0:T(128)} %param.18) | copy-start | bytes 1540
  0.7 16.1 %copy-start.3 = (bf16[1024,128]{1,0:T(8,128)(2,1)S(1)}, bf16[1024,128]{1,0:T(8,128)(2,1)}, u32[]{:S(2)}) copy-start(bf16[1024,128]{1,0:T(8,128)(2,1)} %keyval_ref.1) | copy-start | bytes 786436
  0.7 16.1 %copy-start.1 = (bf16[1024,512]{1,0:T(8,128)(2,1)S(1)}, bf16[1024,512]{1,0:T(8,128)(2,1)}, u32[]{:S(2)}) copy-start(bf16[1024,512]{1,0:T(8,128)(2,1)} %query_ref.1) | copy-start | bytes 3145732
  0.7 64.3 %copy-start.18 = (s32[8]{0:T(128)S(1)}, s32[8]{0:T(128)}, u32[]{:S(2)}) copy-start(s32[8]{0:T(128)} %param.19) | copy-start | bytes 100
  2.2 14.6 %all-to-all-start = ((bf16[8,5,1024]{2,1,0:T(8,128)(2,1)}), bf16[8,5,1024]{2,1,0:T(8,128)(2,1)S(1)}, u32[]{:S(2)}, u32[]{:S(2)}) async-start(bf16[8,5,1024]{2,1,0:T(8,128)(2,1)} %broadcast_in_dim.22), calls=%async_computation | async-start | bytes 262144 | tf_op jit(solution)/shard_map/all_to_all | solution.py:442
  10.1 6.7 %copy-start.10 = (s32[2]{0:T(128)S(1)}, s32[2]{0:T(128)}, u32[]{:S(2)}) copy-start(s32[2]{0:T(128)} %pad_add_fusion.1.me_ref) | copy-start | bytes 28
  17.8 14.6 %collective-permute-start.4 = (bf16[8,16,1024]{2,1,0:T(8,128)(2,1)}, bf16[8,16,1024]{2,1,0:T(8,128)(2,1)S(1)}, u32[]{:S(2)}, u32[]{:S(2)}) collective-permute-start(bf16[8,16,1024]{2,1,0:T(8,128)(2,1)} %get-tuple-element.123), channel_id=1, source_target_pairs={{0,12},{4,8},{8,4},{12,0},{16,28},{20,24},{24,20},{28,16},{1,13},{... | collective-permute-start | bytes 786440 | tf_op jit(solution)/shard_map/ppermute | solution.py:468
  20.1 12.2 %collective-permute-start.3 = (bf16[6,16,1024]{2,1,0:T(8,128)(2,1)}, bf16[6,16,1024]{2,1,0:T(8,128)(2,1)S(1)}, u32[]{:S(2)}, u32[]{:S(2)}) collective-permute-start(bf16[6,16,1024]{2,1,0:T(8,128)(2,1)} %get-tuple-element.122), channel_id=1, source_target_pairs={{0,24},{4,28},{8,16},{12,20},{16,8},{20,12},{24,0},{28,4},{1,25},{... | collective-permute-start | bytes 589832 | tf_op jit(solution)/shard_map/ppermute | solution.py:468
  22.5 1.9 %collective-permute-start = (f32[40,256]{1,0:T(8,128)S(1)}, f32[40,256]{1,0:T(8,128)S(1)}, u32[]{:S(2)}, u32[]{:S(2)}) collective-permute-start(f32[40,256]{1,0:T(8,128)S(1)} %get-tuple-element.119), channel_id=1, source_target_pairs={{0,1},{1,0},{2,3},{3,2},{4,5},{5,4},{6,7},{7,6},{8,9},{9,8},{10,11... | collective-permute-start | bytes 122888 | tf_op jit(solution)/shard_map/ppermute | solution.py:468
  22.5 4.0 %collective-permute-start.1 = (f32[40,256]{1,0:T(8,128)S(1)}, f32[40,256]{1,0:T(8,128)S(1)}, u32[]{:S(2)}, u32[]{:S(2)}) collective-permute-start(f32[40,256]{1,0:T(8,128)S(1)} %get-tuple-element.120), channel_id=1, source_target_pairs={{0,2},{1,3},{2,0},{3,1},{4,6},{5,7},{6,4},{7,5},{8,10},{9,11},{10,... | collective-permute-start | bytes 122888 | tf_op jit(solution)/shard_map/ppermute | solution.py:468
  24.0 3.5 %collective-permute-start.2 = (f32[40,256]{1,0:T(8,128)S(1)}, f32[40,256]{1,0:T(8,128)S(1)}, u32[]{:S(2)}, u32[]{:S(2)}) collective-permute-start(f32[40,256]{1,0:T(8,128)S(1)} %get-tuple-element.121), channel_id=1, source_target_pairs={{0,3},{1,2},{2,1},{3,0},{4,7},{5,6},{6,5},{7,4},{8,11},{9,10},{10,... | collective-permute-start | bytes 122888 | tf_op jit(solution)/shard_map/ppermute | solution.py:468
  33.8 18.2 %all-to-all-start.1 = ((bf16[8,48,256]{2,1,0:T(8,128)(2,1)}), bf16[8,48,256]{2,1,0:T(8,128)(2,1)S(1)}, u32[]{:S(2)}, u32[]{:S(2)}) async-start(bf16[8,48,256]{2,1,0:T(8,128)(2,1)} %shard_map.157), calls=%async_computation.1 | async-start | bytes 393216 | tf_op jit(solution)/shard_map/all_to_all | solution.py:568
  37.2 13.1 %collective-permute-start.5 = (bf16[10,16,1024]{2,1,0:T(8,128)(2,1)}, bf16[10,16,1024]{2,1,0:T(8,128)(2,1)S(1)}, u32[]{:S(2)}, u32[]{:S(2)}) collective-permute-start(bf16[10,16,1024]{2,1,0:T(8,128)(2,1)} %get-tuple-element.131), channel_id=1, source_target_pairs={{0,24},{4,28},{8,16},{12,20},{16,8},{20,12},{24,0},{28,4},{1,25},{... | collective-permute-start | bytes 983048 | tf_op jit(solution)/shard_map/ppermute | solution.py:468
  53.2 20.7 %copy-start.9 = (bf16[8,40,128]{2,1,0:T(8,128)(2,1)}, bf16[8,40,128]{2,1,0:T(8,128)(2,1)S(1)}, u32[]{:S(2)}) copy-start(bf16[8,40,128]{2,1,0:T(8,128)(2,1)S(1)} %get-tuple-element.145.refs_0_) | copy-start | bytes 245764
  53.2 18.5 %collective-permute-start.9 = (bf16[6,16,1024]{2,1,0:T(8,128)(2,1)}, bf16[6,16,1024]{2,1,0:T(8,128)(2,1)S(1)}, u32[]{:S(2)}, u32[]{:S(2)}) collective-permute-start(bf16[6,16,1024]{2,1,0:T(8,128)(2,1)} %get-tuple-element.137), channel_id=1, source_target_pairs={{0,28},{4,24},{8,20},{12,16},{16,12},{20,8},{24,4},{28,0},{1,29},{... | collective-permute-start | bytes 589832 | tf_op jit(solution)/shard_map/ppermute | solution.py:468
  55.6 16.8 %collective-permute-start.10 = (bf16[8,16,1024]{2,1,0:T(8,128)(2,1)}, bf16[8,16,1024]{2,1,0:T(8,128)(2,1)S(1)}, u32[]{:S(2)}, u32[]{:S(2)}) collective-permute-start(bf16[8,16,1024]{2,1,0:T(8,128)(2,1)} %get-tuple-element.138), channel_id=1, source_target_pairs={{0,8},{4,12},{8,0},{12,4},{16,24},{20,28},{24,16},{28,20},{1,9},{5... | collective-permute-start | bytes 786440 | tf_op jit(solution)/shard_map/ppermute | solution.py:468
  65.2 4.7 %collective-permute-start.8 = (bf16[8,40,128]{2,1,0:T(8,128)(2,1)S(1)}, bf16[8,40,128]{2,1,0:T(8,128)(2,1)S(1)}, u32[]{:S(2)}, u32[]{:S(2)}) collective-permute-start(bf16[8,40,128]{2,1,0:T(8,128)(2,1)S(1)} %get-tuple-element.145.refs_0_), channel_id=1, source_target_pairs={{0,3},{1,2},{2,1},{3,0},{4,7},{5,6},{6,5},{7,4},{8,11},{9,10},{10,... | collective-permute-start | bytes 245768 | tf_op jit(solution)/shard_map/ppermute | solution.py:468
  65.2 6.5 %collective-permute-start.7 = (bf16[8,40,128]{2,1,0:T(8,128)(2,1)S(1)}, bf16[8,40,128]{2,1,0:T(8,128)(2,1)S(1)}, u32[]{:S(2)}, u32[]{:S(2)}) collective-permute-start(bf16[8,40,128]{2,1,0:T(8,128)(2,1)S(1)} %get-tuple-element.145.refs_0_), channel_id=1, source_target_pairs={{0,2},{1,3},{2,0},{3,1},{4,6},{5,7},{6,4},{7,5},{8,10},{9,11},{10,... | collective-permute-start | bytes 245768 | tf_op jit(solution)/shard_map/ppermute | solution.py:468
  66.8 4.9 %collective-permute-start.6 = (bf16[8,40,128]{2,1,0:T(8,128)(2,1)S(1)}, bf16[8,40,128]{2,1,0:T(8,128)(2,1)S(1)}, u32[]{:S(2)}, u32[]{:S(2)}) collective-permute-start(bf16[8,40,128]{2,1,0:T(8,128)(2,1)S(1)} %get-tuple-element.145.refs_0_), channel_id=1, source_target_pairs={{0,1},{1,0},{2,3},{3,2},{4,5},{5,4},{6,7},{7,6},{8,9},{9,8},{10,11... | collective-permute-start | bytes 245768 | tf_op jit(solution)/shard_map/ppermute | solution.py:468
  69.9 4.1 %copy-start.13 = (bf16[8,40,128]{2,1,0:T(8,128)(2,1)}, bf16[8,40,128]{2,1,0:T(8,128)(2,1)S(1)}, u32[]{:S(2)}) copy-start(bf16[8,40,128]{2,1,0:T(8,128)(2,1)S(1)} %collective-permute-done.8.refs_3_) | copy-start | bytes 245764
  71.7 2.3 %copy-start.14 = (bf16[8,40,128]{2,1,0:T(8,128)(2,1)}, bf16[8,40,128]{2,1,0:T(8,128)(2,1)S(1)}, u32[]{:S(2)}) copy-start(bf16[8,40,128]{2,1,0:T(8,128)(2,1)S(1)} %collective-permute-done.7.refs_2_) | copy-start | bytes 245764
  71.7 2.3 %copy-start.15 = (bf16[8,40,128]{2,1,0:T(8,128)(2,1)}, bf16[8,40,128]{2,1,0:T(8,128)(2,1)S(1)}, u32[]{:S(2)}) copy-start(bf16[8,40,128]{2,1,0:T(8,128)(2,1)S(1)} %collective-permute-done.6.refs_1_) | copy-start | bytes 245764
  72.4 11.9 %collective-permute-start.12 = (bf16[8,16,1024]{2,1,0:T(8,128)(2,1)}, bf16[8,16,1024]{2,1,0:T(8,128)(2,1)S(1)}, u32[]{:S(2)}, u32[]{:S(2)}) collective-permute-start(bf16[8,16,1024]{2,1,0:T(8,128)(2,1)} %get-tuple-element.155), channel_id=1, source_target_pairs={{0,8},{4,12},{8,0},{12,4},{16,24},{20,28},{24,16},{28,20},{1,9},{5... | collective-permute-start | bytes 786440 | tf_op jit(solution)/shard_map/ppermute | solution.py:468
  72.4 14.8 %collective-permute-start.11 = (bf16[10,16,1024]{2,1,0:T(8,128)(2,1)}, bf16[10,16,1024]{2,1,0:T(8,128)(2,1)S(1)}, u32[]{:S(2)}, u32[]{:S(2)}) collective-permute-start(bf16[10,16,1024]{2,1,0:T(8,128)(2,1)} %get-tuple-element.154), channel_id=1, source_target_pairs={{0,28},{4,24},{8,20},{12,16},{16,12},{20,8},{24,4},{28,0},{1,29},{... | collective-permute-start | bytes 983048 | tf_op jit(solution)/shard_map/ppermute | solution.py:468
  74.0 13.3 %copy-start.21 = (bf16[16,16,1024]{2,1,0:T(8,128)(2,1)S(1)}, bf16[16,16,1024]{2,1,0:T(8,128)(2,1)}, u32[]{:S(2)}) copy-start(bf16[16,16,1024]{2,1,0:T(8,128)(2,1)} %get-tuple-element.167) | copy-start | bytes 1572868
  74.0 16.2 %copy-start.22 = (bf16[6,16,1024]{2,1,0:T(8,128)(2,1)S(1)}, bf16[6,16,1024]{2,1,0:T(8,128)(2,1)}, u32[]{:S(2)}) copy-start(bf16[6,16,1024]{2,1,0:T(8,128)(2,1)} %get-tuple-element.166) | copy-start | bytes 589828
  74.0 37.7 %copy-start.23 = (s32[8]{0:T(128)S(1)}, s32[8]{0:T(128)}, u32[]{:S(2)}) copy-start(s32[8]{0:T(128)} %param.21) | copy-start | bytes 100
  87.3 14.5 %collective-permute-start.17 = (bf16[16,16,1024]{2,1,0:T(8,128)(2,1)S(1)}, bf16[16,16,1024]{2,1,0:T(8,128)(2,1)S(1)}, u32[]{:S(2)}, u32[]{:S(2)}) collective-permute-start(bf16[16,16,1024]{2,1,0:T(8,128)(2,1)S(1)} %copy-done.21), channel_id=1, source_target_pairs={{0,4},{4,0},{8,12},{12,8},{16,20},{20,16},{24,28},{28,24},{1,5},{5... | collective-permute-start | bytes 1572872 | tf_op jit(solution)/shard_map/ppermute | solution.py:468
  90.2 11.4 %collective-permute-start.16 = (bf16[6,16,1024]{2,1,0:T(8,128)(2,1)S(1)}, bf16[6,16,1024]{2,1,0:T(8,128)(2,1)S(1)}, u32[]{:S(2)}, u32[]{:S(2)}) collective-permute-start(bf16[6,16,1024]{2,1,0:T(8,128)(2,1)S(1)} %copy-done.22), channel_id=1, source_target_pairs={{0,16},{4,20},{8,24},{12,28},{16,0},{20,4},{24,8},{28,12},{1,17},{... | collective-permute-start | bytes 589832 | tf_op jit(solution)/shard_map/ppermute | solution.py:468
  93.0 1.9 %collective-permute-start.13 = (bf16[8,64,128]{2,1,0:T(8,128)(2,1)}, bf16[8,64,128]{2,1,0:T(8,128)(2,1)S(1)}, u32[]{:S(2)}, u32[]{:S(2)}) collective-permute-start(bf16[8,64,128]{2,1,0:T(8,128)(2,1)} %get-tuple-element.163), channel_id=1, source_target_pairs={{0,1},{1,0},{2,3},{3,2},{4,5},{5,4},{6,7},{7,6},{8,9},{9,8},{10,11... | collective-permute-start | bytes 393224 | tf_op jit(solution)/shard_map/ppermute | solution.py:468
  93.0 6.5 %collective-permute-start.14 = (bf16[8,64,128]{2,1,0:T(8,128)(2,1)}, bf16[8,64,128]{2,1,0:T(8,128)(2,1)S(1)}, u32[]{:S(2)}, u32[]{:S(2)}) collective-permute-start(bf16[8,64,128]{2,1,0:T(8,128)(2,1)} %get-tuple-element.164), channel_id=1, source_target_pairs={{0,2},{1,3},{2,0},{3,1},{4,6},{5,7},{6,4},{7,5},{8,10},{9,11},{10,... | collective-permute-start | bytes 393224 | tf_op jit(solution)/shard_map/ppermute | solution.py:468
  93.4 8.2 %collective-permute-start.15 = (bf16[8,64,128]{2,1,0:T(8,128)(2,1)}, bf16[8,64,128]{2,1,0:T(8,128)(2,1)S(1)}, u32[]{:S(2)}, u32[]{:S(2)}) collective-permute-start(bf16[8,64,128]{2,1,0:T(8,128)(2,1)} %get-tuple-element.165), channel_id=1, source_target_pairs={{0,3},{1,2},{2,1},{3,0},{4,7},{5,6},{6,5},{7,4},{8,11},{9,10},{10,... | collective-permute-start | bytes 393224 | tf_op jit(solution)/shard_map/ppermute | solution.py:468
  101.5 2.2 %copy-start.6 = (bf16[6,16,1024]{2,1,0:T(8,128)(2,1)}, bf16[6,16,1024]{2,1,0:T(8,128)(2,1)S(1)}, u32[]{:S(2)}) copy-start(bf16[6,16,1024]{2,1,0:T(8,128)(2,1)S(1)} %collective-permute-done.16.refs_4_) | copy-start | bytes 589828
  103.7 20.9 %collective-permute-start.18 = (bf16[10,16,1024]{2,1,0:T(8,128)(2,1)}, bf16[10,16,1024]{2,1,0:T(8,128)(2,1)S(1)}, u32[]{:S(2)}, u32[]{:S(2)}) collective-permute-start(bf16[10,16,1024]{2,1,0:T(8,128)(2,1)} %get-tuple-element.176), channel_id=1, source_target_pairs={{0,16},{4,20},{8,24},{12,28},{16,0},{20,4},{24,8},{28,12},{1,17},{... | collective-permute-start | bytes 983048 | tf_op jit(solution)/shard_map/ppermute | solution.py:468
  107.7 16.9 %all-to-all-start.2 = ((bf16[8,64,128]{2,1,0:T(8,128)(2,1)}), bf16[8,64,128]{2,1,0:T(8,128)(2,1)}, u32[]{:S(2)}, u32[]{:S(2)}) async-start(bf16[8,64,128]{2,1,0:T(8,128)(2,1)} %shard_map.160), calls=%async_computation.2 | async-start | bytes 262144 | tf_op jit(solution)/shard_map/all_to_all | solution.py:634
  113.1 0.9 copy-start.5
  114.9 31.3 %copy-start.2 = (bf16[1024,512]{1,0:T(8,128)(2,1)S(1)}, bf16[1024,512]{1,0:T(8,128)(2,1)}, u32[]{:S(2)}) copy-start(bf16[1024,512]{1,0:T(8,128)(2,1)} %weight_ref.1) | copy-start | bytes 3145732
  114.9 31.3 %copy-start.11 = (s32[2]{0:T(128)S(1)}, s32[2]{0:T(128)}, u32[]{:S(2)}) copy-start(s32[2]{0:T(128)} %pad_add_fusion.1.me_ref) | copy-start | bytes 28
  126.4 19.9 %collective-permute-start.19 = (bf16[10,16,1024]{2,1,0:T(8,128)(2,1)}, bf16[10,16,1024]{2,1,0:T(8,128)(2,1)S(1)}, u32[]{:S(2)}, u32[]{:S(2)}) collective-permute-start(bf16[10,16,1024]{2,1,0:T(8,128)(2,1)} %get-tuple-element.191), channel_id=1, source_target_pairs={{0,20},{4,16},{8,28},{12,24},{16,4},{20,0},{24,12},{28,8},{1,21},{... | collective-permute-start | bytes 983048 | tf_op jit(solution)/shard_map/ppermute | solution.py:468
  128.7 17.5 %all-to-all-start.3 = ((bf16[8,40,128]{2,1,0:T(8,128)(2,1)}), bf16[8,40,128]{2,1,0:T(8,128)(2,1)S(1)}, u32[]{:S(2)}, u32[]{:S(2)}) async-start(bf16[8,40,128]{2,1,0:T(8,128)(2,1)} %shard_map.162), calls=%async_computation.3 | async-start | bytes 163840 | tf_op jit(solution)/shard_map/all_to_all | solution.py:637
  147.2 13.3 %collective-permute-start.24 = (bf16[8,16,1024]{2,1,0:T(8,128)(2,1)}, bf16[8,16,1024]{2,1,0:T(8,128)(2,1)S(1)}, u32[]{:S(2)}, u32[]{:S(2)}) collective-permute-start(bf16[8,16,1024]{2,1,0:T(8,128)(2,1)} %get-tuple-element.206), channel_id=1, source_target_pairs={{0,12},{4,8},{8,4},{12,0},{16,28},{20,24},{24,20},{28,16},{1,13},{... | collective-permute-start | bytes 786440 | tf_op jit(solution)/shard_map/ppermute | solution.py:468
  147.9 10.3 %collective-permute-start.23 = (bf16[6,16,1024]{2,1,0:T(8,128)(2,1)}, bf16[6,16,1024]{2,1,0:T(8,128)(2,1)S(1)}, u32[]{:S(2)}, u32[]{:S(2)}) collective-permute-start(bf16[6,16,1024]{2,1,0:T(8,128)(2,1)} %get-tuple-element.205), channel_id=1, source_target_pairs={{0,20},{4,16},{8,28},{12,24},{16,4},{20,0},{24,12},{28,8},{1,21},{... | collective-permute-start | bytes 589832 | tf_op jit(solution)/shard_map/ppermute | solution.py:468
  150.5 1.9 %collective-permute-start.20 = (f32[10,512]{1,0:T(8,128)S(1)}, f32[10,512]{1,0:T(8,128)S(1)}, u32[]{:S(2)}, u32[]{:S(2)}) collective-permute-start(f32[10,512]{1,0:T(8,128)S(1)} %get-tuple-element.202), channel_id=1, source_target_pairs={{0,1},{1,0},{2,3},{3,2},{4,5},{5,4},{6,7},{7,6},{8,9},{9,8},{10,11... | collective-permute-start | bytes 61448 | tf_op jit(solution)/shard_map/ppermute | solution.py:468
  150.5 4.2 %collective-permute-start.21 = (f32[10,512]{1,0:T(8,128)S(1)}, f32[10,512]{1,0:T(8,128)S(1)}, u32[]{:S(2)}, u32[]{:S(2)}) collective-permute-start(f32[10,512]{1,0:T(8,128)S(1)} %get-tuple-element.203), channel_id=1, source_target_pairs={{0,2},{1,3},{2,0},{3,1},{4,6},{5,7},{6,4},{7,5},{8,10},{9,11},{10,... | collective-permute-start | bytes 61448 | tf_op jit(solution)/shard_map/ppermute | solution.py:468
  150.6 4.1 %collective-permute-start.22 = (f32[10,512]{1,0:T(8,128)S(1)}, f32[10,512]{1,0:T(8,128)S(1)}, u32[]{:S(2)}, u32[]{:S(2)}) collective-permute-start(f32[10,512]{1,0:T(8,128)S(1)} %get-tuple-element.204), channel_id=1, source_target_pairs={{0,3},{1,2},{2,1},{3,0},{4,7},{5,6},{6,5},{7,4},{8,11},{9,10},{10,... | collective-permute-start | bytes 61448 | tf_op jit(solution)/shard_map/ppermute | solution.py:468
  (5 other events, 3.9 us)

commit v8 on v7

--- a/solution.py
+++ b/solution.py
@@ -19,7 +19,7 @@
 SCALE2 = math.log2(math.e) / math.sqrt(HD)
 STAT = 16
 MIB = 1024 * 1024
-CUTS = {1: (0, 16), 2: (0, 8, 16), 3: (0, 8, 16), 4: (0, 6, 16), 5: (0, 10, 16), 6: (0, 6, 16), 7: (0, 6, 16)}
+CUTS = {1: (0, 8, 16), 2: (0, 16), 3: (0, 8, 16), 4: (0, 12, 16), 5: (0, 8, 16), 6: (0, 6, 16), 7: (0, 8, 16)}
 NT = (((1,), (1,)), ((), ()))
 
 
@@ -290,11 +290,7 @@
             pltpu.VMEM((pieces, height, HD), jnp.bfloat16),
         ],
         compiler_params=pltpu.CompilerParams(vmem_limit_bytes=56 * MIB),
-        cost_estimate=pl.CostEstimate(
-            flops=4 * HEADS * rows * (tokens + extra) * HD,
-            bytes_accessed=pool.size * 2,
-            transcendentals=HEADS * rows * (tokens + extra),
-        ),
+        cost_estimate=pl.CostEstimate(flops=0, bytes_accessed=0, transcendentals=0),
     )(me, *queries, pool, pool, keyval, keyval, req_tok, pos_tok, row_info, new_bias)
 
 
@@ -520,32 +516,24 @@
         arrived.clear()
         return pages
 
-    req_tok = jnp.broadcast_to(page_req[:, None], (slots, PAGE)).reshape(1, -1)
-    pos_tok = (page_idx[:, None] * PAGE + jnp.arange(PAGE, dtype=jnp.int32)[None, :]).reshape(1, -1)
-    row_info = jnp.stack(
-        [
-            jnp.asarray(np.arange(rows) // STEPS, jnp.int32),
-            jnp.broadcast_to(lengths[:, None], (requests, STEPS)).reshape(rows),
-        ],
-        axis=1,
-    )
+    def prepare(page_req, page_idx, lengths):
+        req_tok = jnp.broadcast_to(page_req[:, None], (slots, PAGE)).reshape(1, -1)
+        pos_tok = page_idx[:, None] * PAGE + jnp.arange(PAGE, dtype=jnp.int32)[None, :]
+        row_info = jnp.stack(
+            [
+                jnp.asarray(np.arange(rows) // STEPS, jnp.int32),
+                jnp.broadcast_to(lengths[:, None], (requests, STEPS)).reshape(rows),
+            ],
+            axis=1,
+        )
+        return req_tok, pos_tok.reshape(1, -1), row_info
+
     here = (me == 0) & (lax.axis_index("narrow") == 0)
     row_ids = np.arange(rows)[:, None]
     col_ids = np.arange(extra)[None, :]
     causal = (row_ids // STEPS == col_ids // STEPS) & (col_ids <= row_ids) & (col_ids < rows)
     new_bias = jnp.where(jnp.asarray(causal) & here, 0.0, NEG_FILL).astype(jnp.float32)
     tokens = pool.reshape(slots * PAGE, -1)
-    window = {
-        "project": ((6, 0), (3, 0)),
-        "gather": ((6, 1),),
-        "queries": ((7, 0), (2, 0)),
-        "attend": ((7, 1), (2, 1)),
-        "narrow": ((4, 0), (1, 0)),
-        "wide": ((4, 1),),
-        "attn": ((5, 0),),
-        "finish": ((5, 1), (3, 1)),
-    }
-
     if direct:
         block = jax.ShapeDtypeStruct((rows, 2 * HD), jnp.float32)
         partial = in_vmem(
@@ -557,7 +545,7 @@
             w_keyval,
             scratch=[pltpu.VMEM((rows, narrow * HD), jnp.float32)],
         )
-        partial = beside(lambda value: deal(value, "narrow"), partial, *window["project"])
+        partial = beside(lambda value: deal(value, "narrow"), partial, (6, 0), (3, 0))
         packed = in_vmem(
             functools.partial(pack_kernel, narrow),
             jax.ShapeDtypeStruct((wide, rows + wide, 2 * HD), jnp.bfloat16),
@@ -565,7 +553,9 @@
             *partial,
             tags,
         )
-        received = beside(lambda value: exchange(value, "wide"), packed, *window["gather"])
+        packed, raw = lax.optimization_barrier((packed, (page_req, page_idx, lengths)))
+        received = exchange(packed, "wide")
+        info = launch(prepare(*raw), (6, 1))
         queries, keyval, tags_in = in_vmem(
             functools.partial(unpack_kernel, rows),
             [
@@ -576,7 +566,7 @@
             both,
             received,
         )
-        queries = beside(lambda value: share(value, "narrow"), queries, *window["queries"])
+        queries = share(launch(queries, (7, 0)), "narrow")
     else:
         gathered = gathered.reshape(rows, -1)
         query_part = jnp.dot(gathered, w_query, preferred_element_type=jnp.float32)
@@ -585,59 +575,53 @@
         partial = jnp.concatenate(
             [query_part, jnp.broadcast_to(keyval_part[None], (narrow,) + keyval_part.shape)], axis=2
         )
-        partial = beside(lambda value: exchange(value, "narrow"), partial, *window["project"])
+        partial = beside(lambda value: exchange(value, "narrow"), partial, (6, 0), (3, 0))
         projected = jnp.sum(partial, axis=0).astype(jnp.bfloat16)
         tags = tags[:, : 3 * capacity].astype(jnp.bfloat16)[:, None]
         tags = jnp.pad(tags, ((0, 0), (0, 7), (0, projected.shape[1] - tags.shape[2])))
         packed = jnp.broadcast_to(projected[None], (wide,) + projected.shape)
         packed = jnp.concatenate([packed, tags], axis=1)
-        received = beside(lambda value: exchange(value, "wide"), packed, *window["gather"])
+        packed, raw = lax.optimization_barrier((packed, (page_req, page_idx, lengths)))
+        received = exchange(packed, "wide")
+        info = launch(prepare(*raw), (6, 1))
         tags_in = received[:, rows]
-        queries = beside(
-            lambda value: spread(value, "narrow"),
-            received[:, :rows, :own_cols],
-            *window["queries"],
-        )
+        queries = spread(launch(received[:, :rows, :own_cols], (7, 0)), "narrow")
         queries = jnp.transpose(queries, (2, 1, 0, 3)).reshape(rows, HEADS, HD)
         queries = [jnp.transpose(queries, (1, 0, 2)).reshape(KVH, GROUPS * rows, HD)]
         keyval = jnp.transpose(received[:, :rows, own_cols:], (1, 0, 2)).reshape(rows, -1)
         keyval = jnp.pad(keyval, ((0, extra - rows), (0, 0)))
 
-    tags_in = tags_in.astype(jnp.int32)
-    moved_req = tags_in[:, :capacity].reshape(slots)
-    moved_idx = tags_in[:, capacity : 2 * capacity] * 32
-    moved_idx = (moved_idx + tags_in[:, 2 * capacity : 3 * capacity] - 1).reshape(slots)
-    local_req = local_rows // STEPS
-    first_row = me * local_rows
-    fresh = lax.dynamic_slice_in_dim(keyval, first_row, local_rows, 0)
-    fresh = fresh.reshape(local_req, STEPS, -1)
-    kept = lax.dynamic_slice_in_dim(accepted, me * local_req, local_req, 0)
-    new_entries = jnp.where(
-        jnp.arange(STEPS)[None, :, None] < kept[:, None, None], fresh, jnp.zeros((), jnp.bfloat16)
-    )
-    mixed = beside(
-        lambda value: attend(
-            both, value, keyval, tokens, req_tok, pos_tok, row_info, new_bias, rows, piece
-        ),
-        queries,
-        *window["attend"],
-    )
+    def small_outputs(keyval, tags):
+        tags = tags.astype(jnp.int32)
+        moved_req = tags[:, :capacity].reshape(slots)
+        moved_idx = tags[:, capacity : 2 * capacity] * 32
+        moved_idx = (moved_idx + tags[:, 2 * capacity : 3 * capacity] - 1).reshape(slots)
+        local_req = local_rows // STEPS
+        fresh = lax.dynamic_slice_in_dim(keyval, me * local_rows, local_rows, 0)
+        fresh = fresh.reshape(local_req, STEPS, -1)
+        kept = lax.dynamic_slice_in_dim(accepted, me * local_req, local_req, 0)
+        step_ids = jnp.arange(STEPS)[None, :, None]
+        entries = jnp.where(step_ids < kept[:, None, None], fresh, jnp.zeros((), jnp.bfloat16))
+        return entries, moved_req, moved_idx
+
+    queries = launch(land(queries, (6, 1)), (2, 0))
+    mixed = attend(both, queries, keyval, tokens, *info, new_bias, rows, piece)
+    mixed = launch(land(mixed, (7, 0), (2, 0)), (7, 1), (3, 1))
     if direct:
-        mixed = beside(lambda value: deal(value, "narrow"), mixed, *window["narrow"])
+        mixed = deal(mixed, "narrow")
     else:
-        mixed = beside(lambda value: exchange(value, "narrow"), mixed[0], *window["narrow"])
-        mixed = mixed.reshape((narrow, wide) + mixed.shape[1:])
+        mixed = exchange(mixed[0], "narrow").reshape((narrow, wide) + mixed[0].shape[1:])
         mixed = [mixed[i] for i in range(narrow)]
-    mixed = combine(mixed, piece)
-    mixed, pages = lax.optimization_barrier((mixed, moved_pool))
-    pages = placed(pages)
-    mixed = beside(lambda value: exchange(value, "wide"), mixed, *window["wide"])
-    mixed, moved_pool = lax.optimization_barrier((mixed, pages))
+    mixed = combine(land(mixed, (7, 1), (3, 1)), piece)
+    mixed, moved_pool = lax.optimization_barrier((mixed, moved_pool))
+    moved_pool = launch(placed(moved_pool), (4, 0), (1, 0))
+    mixed = land(exchange(mixed, "wide"), (4, 0), (1, 0))
     attn = combine([mixed[i][None] for i in range(wide)], piece, wide)
-    attn = beside(lambda value: exchange(value, "wide"), attn, *window["attn"])
-    attn, new_entries, moved_req, moved_idx = lax.optimization_barrier(
-        (attn, new_entries, moved_req, moved_idx)
-    )
+    attn, raw = lax.optimization_barrier((attn, (keyval, tags_in)))
+    attn = exchange(attn, "wide")
+    small = launch(small_outputs(*raw), (5, 0), (4, 1), (1, 1))
+    new_entries, moved_req, moved_idx = small
+    attn = launch(land(attn, (5, 0), (4, 1), (1, 1)), (5, 1))
     if direct:
         sums = in_vmem(
             functools.partial(finish_kernel, narrow),
@@ -646,14 +630,15 @@
             attn,
             w_out,
         )
-        sums = beside(lambda value: deal(value, "narrow"), sums, *window["finish"])
+        sums = deal(sums, "narrow")
         attended = ((sums[0] + sums[1]) + (sums[2] + sums[3])).astype(jnp.bfloat16)
     else:
         attn = jnp.transpose(attn.reshape(-1, rows, HD), (1, 0, 2)).reshape(rows, -1)
         sums = jnp.dot(attn, w_out, preferred_element_type=jnp.float32)
         sums = sums.reshape(narrow, rows // narrow, -1)
-        sums = beside(lambda value: exchange(value, "narrow"), sums, *window["finish"])
+        sums = exchange(sums, "narrow")
         attended = jnp.sum(sums, axis=0).astype(jnp.bfloat16)
+    attended = land(attended, (5, 1))
     moved_pool = placed(moved_pool)
     return (attended, new_entries, moved_pool, moved_req, moved_idx)
 

time: 164 us -> 166 us (1.012)
  waiting for transfers between devices: 59.2 us -> 78.9 us
  starting transfers between devices: 61.6 us -> 47.8 us
  local copies, waits for them, and re-layouts: 11.4 us -> 8.73 us
    ppermute x25, waiting for transfers between devices: 37.5 us -> 54.4 us  [send(): lax.ppermute(block, axis, [(i, i ^ d) for i in range(lax.axis_size(axis))])]
    ppermute x25, starting transfers between devices: 42.6 us -> 29.1 us  [send(): lax.ppermute(block, axis, [(i, i ^ d) for i in range(lax.axis_size(axis))])]
    all_to_all x3, waiting for transfers between devices: 21 us -> 23.7 us  [the longest x1 14.5 us: on_device(): mixed = land(exchange(mixed, 'wide'), (4, 0), (1, 0))]
    unnamed x48 -> x40, local copies, waits for them, and re-layouts: 4.92 us -> 2.36 us
  transfers between devices with their start and end apart: 29 -> 29, of which waited for: 17 -> 17; matrix products, arithmetic and copies ran while one was open for 5% -> 4% of each run, Pallas kernels for 11% -> 11%
where the time goes in v8:
time: 166 us; the launch traced here: 165 us
  waiting for transfers between devices  78.9 us (48%)
  starting transfers between devices  47.8 us (29%)
  Pallas kernels  25.2 us (15%)
  local copies, waits for them, and re-layouts  8.73 us (5%)
  other arithmetic  4.04 us (2%)
    ppermute x25, waiting for transfers between devices, send(): lax.ppermute(block, axis, [(i, i ^ d) for i in range(lax.axis_size(axis))])  54.4 us
    ppermute x25, starting transfers between devices, send(): lax.ppermute(block, axis, [(i, i ^ d) for i in range(lax.axis_size(axis))])  29.1 us
    all_to_all x1, waiting for transfers between devices, on_device(): mixed = land(exchange(mixed, 'wide'), (4, 0), (1, 0))  14.5 us
    pallas_call x1, Pallas kernels, attend(): pl.pallas_call(functools.partial(attend_kernel, rows, piece, peers), grid...  10.4 us
    all_to_all x1, waiting for transfers between devices, on_device(): received = exchange(packed, 'wide')  9.21 us
    all_to_all x1, starting transfers between devices, spread(): lax.all_to_all(jnp.broadcast_to(block[None], (count,) + block.shape), axi...  7.28 us
    pallas_call x1, Pallas kernels, order_pages(): pl.pallas_call(functools.partial(order_kernel, wide, parts), out_shape=ou...  5.97 us
    all_to_all x1, starting transfers between devices, on_device(): mixed = land(exchange(mixed, 'wide'), (4, 0), (1, 0))  4.26 us
  transfers between devices with their start and end apart: 29, of which 17 were waited for; matrix products, arithmetic and copies ran while one was open for 4% of the time, Pallas kernels for 11%

profile of v8, /device:TPU:0, one launch (start us, length us, event | category | flops | bytes accessed | tf_op | source)
XLA Modules:
  0.0 165.5 jit_solution(14372322682929027765)
XLA Ops:
  0.7 1.5 broadcast_in_dim.22
  2.2 7.3 %all-to-all-start = ((bf16[8,5,1024]{2,1,0:T(8,128)(2,1)}), bf16[8,5,1024]{2,1,0:T(8,128)(2,1)S(1)}, u32[]{:S(2)}, u32[]{:S(2)}) async-start(bf16[8,5,1024]{2,1,0:T(8,128)(2,1)} %broadcast_in_dim.22), calls=%async_computation | async-start | bytes 262144 | tf_op jit(solution)/shard_map/all_to_all | solution.py:438
  10.0 6.0 %shard_map.156 = (bf16[128,16,1024]{2,1,0:T(8,128)(2,1)}, f32[8,128]{1,0:T(8,128)}, bf16[8,16,1024]{2,1,0:T(8,128)(2,1)}, bf16[8,16,1024]{2,1,0:T(8,128)(2,1)}, ...) custom-call(s32[2]{0:T(128)} %pad_add_fusion.1.me_ref, ...), custom_call_target="tpu_custom_call" | custom-call | bytes 8388608 | tf_op jit(solution)/shard_map/pallas_call | solution.py:98
  16.0 0.8 all-to-all-done.hidden_ref
  16.8 1.0 shard_map.155
  17.8 2.2 %collective-permute-start.4 = (bf16[8,16,1024]{2,1,0:T(8,128)(2,1)}, bf16[8,16,1024]{2,1,0:T(8,128)(2,1)S(1)}, u32[]{:S(2)}, u32[]{:S(2)}) collective-permute-start(bf16[8,16,1024]{2,1,0:T(8,128)(2,1)} %get-tuple-element.121), channel_id=1, source_target_pairs={{0,12},{4,8},{8,4},{12,0},{16,28},{20,24},{24,20},{28,16},{1,13},{... | collective-permute-start | bytes 786440 | tf_op jit(solution)/shard_map/ppermute | solution.py:464
  20.0 2.4 %collective-permute-start.3 = (bf16[6,16,1024]{2,1,0:T(8,128)(2,1)}, bf16[6,16,1024]{2,1,0:T(8,128)(2,1)S(1)}, u32[]{:S(2)}, u32[]{:S(2)}) collective-permute-start(bf16[6,16,1024]{2,1,0:T(8,128)(2,1)} %get-tuple-element.120), channel_id=1, source_target_pairs={{0,24},{4,28},{8,16},{12,20},{16,8},{20,12},{24,0},{28,4},{1,25},{... | collective-permute-start | bytes 589832 | tf_op jit(solution)/shard_map/ppermute | solution.py:464
  22.4 1.5 collective-permute-start.1
  24.2 2.1 %collective-permute-done.1.refs_2_ = f32[40,256]{1,0:T(8,128)S(1)} collective-permute-done((f32[40,256]{1,0:T(8,128)S(1)}, f32[40,256]{1,0:T(8,128)S(1)}, u32[]{:S(2)}, u32[]{:S(2)}) %collective-permute-start.1) | collective-permute-done | bytes 40992 | tf_op jit(solution)/shard_map/ppermute | solution.py:464
  26.4 1.0 collective-permute-done.2.refs_3_
  27.4 4.8 %collective-permute-done.3.refs_3_ = bf16[6,16,1024]{2,1,0:T(8,128)(2,1)S(1)} collective-permute-done((bf16[6,16,1024]{2,1,0:T(8,128)(2,1)}, bf16[6,16,1024]{2,1,0:T(8,128)(2,1)S(1)}, u32[]{:S(2)}, u32[]{:S(2)}) %collective-permute-start.3) | collective-permute-done | bytes 196640 | tf_op jit(solution)/shard_map/ppermute | solution.py:464
  33.6 3.4 %all-to-all-start.1 = ((bf16[8,48,256]{2,1,0:T(8,128)(2,1)}), bf16[8,48,256]{2,1,0:T(8,128)(2,1)S(1)}, u32[]{:S(2)}, u32[]{:S(2)}) async-start(bf16[8,48,256]{2,1,0:T(8,128)(2,1)} %shard_map.157), calls=%async_computation.1 | async-start | bytes 393216 | tf_op jit(solution)/shard_map/all_to_all | solution.py:557
  37.1 0.7 reshape.74.refs_8_
  37.9 0.7 add.63.refs_9_
  38.8 3.8 %collective-permute-start.8 = (bf16[10,16,1024]{2,1,0:T(8,128)(2,1)}, bf16[10,16,1024]{2,1,0:T(8,128)(2,1)S(1)}, u32[]{:S(2)}, u32[]{:S(2)}) collective-permute-start(bf16[10,16,1024]{2,1,0:T(8,128)(2,1)} %get-tuple-element.135), channel_id=1, source_target_pairs={{0,24},{4,28},{8,16},{12,20},{16,8},{20,12},{24,0},{28,4},{1,25},{... | collective-permute-start | bytes 983048 | tf_op jit(solution)/shard_map/ppermute | solution.py:464
  42.6 9.2 %all-to-all-done.1.part_ref = bf16[8,48,256]{2,1,0:T(8,128)(2,1)S(1)} async-done(((bf16[8,48,256]{2,1,0:T(8,128)(2,1)}), bf16[8,48,256]{2,1,0:T(8,128)(2,1)S(1)}, u32[]{:S(2)}, u32[]{:S(2)}) %all-to-all-start.1) | async-done | bytes 196640 | tf_op jit(solution)/shard_map/all_to_all | solution.py:557
  53.1 1.5 collective-permute-start.6
  55.0 3.4 %collective-permute-done.6.refs_2_ = bf16[8,40,128]{2,1,0:T(8,128)(2,1)S(1)} collective-permute-done((bf16[8,40,128]{2,1,0:T(8,128)(2,1)S(1)}, bf16[8,40,128]{2,1,0:T(8,128)(2,1)S(1)}, u32[]{:S(2)}, u32[]{:S(2)}) %collective-permute-start.6) | collective-permute-done | bytes 81952 | tf_op jit(solution)/shard_map/ppermute | solution.py:464
  58.4 1.0 collective-permute-done.7.refs_3_
  59.3 0.9 collective-permute-start.10
  60.3 1.4 collective-permute-start.9
  63.0 10.4 %shard_map.159 = (bf16[8,64,128]{2,1,0:T(8,128)(2,1)}, bf16[8,64,128]{2,1,0:T(8,128)(2,1)}, bf16[8,64,128]{2,1,0:T(8,128)(2,1)}, bf16[8,64,128]{2,1,0:T(8,128)(2,1)}) custom-call(s32[2]{0:T(128)} %pad_add_fusion.1.me_ref, bf16[8,40,128]{2,1,0:T(8,128)(2,1)} %copy-done.5, bf16[8,40,128]{2,1,0:T(8,128)(2,1)} %copy-done.9, bf16[8,40,128]{2,1,0:T(8,128)(2,1)} %copy-done.10, ...), custom_call_target="tpu_custom_call" | custom-call | tf_op jit(solution)/shard_map/pallas_call | solution.py:268
  73.3 6.6 %collective-permute-done.9.refs_5_ = bf16[8,16,1024]{2,1,0:T(8,128)(2,1)S(1)} collective-permute-done((bf16[8,16,1024]{2,1,0:T(8,128)(2,1)}, bf16[8,16,1024]{2,1,0:T(8,128)(2,1)S(1)}, u32[]{:S(2)}, u32[]{:S(2)}) %collective-permute-start.9) | collective-permute-done | bytes 262176 | tf_op jit(solution)/shard_map/ppermute | solution.py:464
  80.0 3.0 %collective-permute-start.14 = (bf16[8,16,1024]{2,1,0:T(8,128)(2,1)S(1)}, bf16[8,16,1024]{2,1,0:T(8,128)(2,1)S(1)}, u32[]{:S(2)}, u32[]{:S(2)}) collective-permute-start(bf16[8,16,1024]{2,1,0:T(8,128)(2,1)S(1)} %copy-done.19), channel_id=1, source_target_pairs={{0,28},{4,24},{8,20},{12,16},{16,12},{20,8},{24,4},{28,0},{1,29},{... | collective-permute-start | bytes 786440 | tf_op jit(solution)/shard_map/ppermute | solution.py:464
  83.0 1.6 collective-permute-start.12
  84.9 4.6 %collective-permute-done.12.refs_2_ = bf16[8,64,128]{2,1,0:T(8,128)(2,1)S(1)} collective-permute-done((bf16[8,64,128]{2,1,0:T(8,128)(2,1)}, bf16[8,64,128]{2,1,0:T(8,128)(2,1)S(1)}, u32[]{:S(2)}, u32[]{:S(2)}) %collective-permute-start.12) | collective-permute-done | bytes 131104 | tf_op jit(solution)/shard_map/ppermute | solution.py:464
  89.5 1.9 %collective-permute-done.13.refs_3_ = bf16[8,64,128]{2,1,0:T(8,128)(2,1)S(1)} collective-permute-done((bf16[8,64,128]{2,1,0:T(8,128)(2,1)}, bf16[8,64,128]{2,1,0:T(8,128)(2,1)S(1)}, u32[]{:S(2)}, u32[]{:S(2)}) %collective-permute-start.13) | collective-permute-done | bytes 131104 | tf_op jit(solution)/shard_map/ppermute | solution.py:464
  91.9 4.3 %collective-permute-done.15.refs_2_ = bf16[8,16,1024]{2,1,0:T(8,128)(2,1)S(1)} collective-permute-done((bf16[8,16,1024]{2,1,0:T(8,128)(2,1)S(1)}, bf16[8,16,1024]{2,1,0:T(8,128)(2,1)S(1)}, u32[]{:S(2)}, u32[]{:S(2)}) %collective-permute-start.15) | collective-permute-done | bytes 262176 | tf_op jit(solution)/shard_map/ppermute | solution.py:464
  96.2 0.9 copy-done.4
  97.1 1.1 shard_map.160
  98.2 1.9 %shard_map.161.refs_6_ = bf16[128,16,1024]{2,1,0:T(8,128)(2,1)} custom-call(s32[7]{0:T(128)S(1)} %stack.72.place_ref, bf16[16,16,1024]{2,1,0:T(8,128)(2,1)S(1)} %collective-permute-done.10.refs_0_, bf16[8,16,1024]{2,1,0:T(8,128)(2,1)S(1)} %collective-permute-done.4.refs_1_, ...), custom_call_target="tpu_custom_call", output_to_operand_aliasing={{}: (8, {})} | custom-call | bytes 7340032 | tf_op jit(solution)/shard_map/pallas_call | solution.py:136
  100.8 0.9 collective-permute-start.17
  101.6 4.3 %all-to-all-start.2 = ((bf16[8,64,128]{2,1,0:T(8,128)(2,1)}), bf16[8,64,128]{2,1,0:T(8,128)(2,1)S(1)}, u32[]{:S(2)}, u32[]{:S(2)}) async-start(bf16[8,64,128]{2,1,0:T(8,128)(2,1)} %shard_map.160), calls=%async_computation.2 | async-start | bytes 262144 | tf_op jit(solution)/shard_map/all_to_all | solution.py:618
  105.9 1.2 dynamic_slice.6
  107.8 14.5 %all-to-all-done.2 = bf16[8,64,128]{2,1,0:T(8,128)(2,1)S(1)} async-done(((bf16[8,64,128]{2,1,0:T(8,128)(2,1)}), bf16[8,64,128]{2,1,0:T(8,128)(2,1)S(1)}, u32[]{:S(2)}, u32[]{:S(2)}) %all-to-all-start.2) | async-done | bytes 131104 | tf_op jit(solution)/shard_map/all_to_all | solution.py:618
  122.3 0.9 shard_map.162
  124.5 1.4 select_bitcast_fusion
  125.9 1.3 collective-permute-start.18
  127.2 1.6 collective-permute-start.20
  128.8 3.7 %all-to-all-start.3 = ((bf16[8,40,128]{2,1,0:T(8,128)(2,1)}), bf16[8,40,128]{2,1,0:T(8,128)(2,1)S(1)}, u32[]{:S(2)}, u32[]{:S(2)}) async-start(bf16[8,40,128]{2,1,0:T(8,128)(2,1)} %shard_map.162), calls=%async_computation.3 | async-start | bytes 163840 | tf_op jit(solution)/shard_map/all_to_all | solution.py:621
  132.5 2.9 %collective-permute-start.19 = (bf16[4,16,1024]{2,1,0:T(8,128)(2,1)}, bf16[4,16,1024]{2,1,0:T(8,128)(2,1)S(1)}, u32[]{:S(2)}, u32[]{:S(2)}) collective-permute-start(bf16[4,16,1024]{2,1,0:T(8,128)(2,1)} %get-tuple-element.194), channel_id=1, source_target_pairs={{0,16},{4,20},{8,24},{12,28},{16,0},{20,4},{24,8},{28,12},{1,17},{... | collective-permute-start | bytes 393224 | tf_op jit(solution)/shard_map/ppermute | solution.py:464
  135.4 13.0 %collective-permute-done.19.refs_3_ = bf16[4,16,1024]{2,1,0:T(8,128)(2,1)S(1)} collective-permute-done((bf16[4,16,1024]{2,1,0:T(8,128)(2,1)}, bf16[4,16,1024]{2,1,0:T(8,128)(2,1)S(1)}, u32[]{:S(2)}, u32[]{:S(2)}) %collective-permute-start.19) | collective-permute-done | bytes 131104 | tf_op jit(solution)/shard_map/ppermute | solution.py:464
  148.9 0.9 shard_map.163
  149.8 1.5 collective-permute-start.22
  152.1 1.7 %collective-permute-done.22 = f32[10,512]{1,0:T(8,128)S(1)} collective-permute-done((f32[10,512]{1,0:T(8,128)S(1)}, f32[10,512]{1,0:T(8,128)S(1)}, u32[]{:S(2)}, u32[]{:S(2)}) %collective-permute-start.22) | collective-permute-done | bytes 20512 | tf_op jit(solution)/shard_map/ppermute | solution.py:464
  153.8 0.9 collective-permute-done.23
  155.3 8.4 %collective-permute-done.24.refs_5_ = bf16[8,16,1024]{2,1,0:T(8,128)(2,1)S(1)} collective-permute-done((bf16[8,16,1024]{2,1,0:T(8,128)(2,1)}, bf16[8,16,1024]{2,1,0:T(8,128)(2,1)S(1)}, u32[]{:S(2)}, u32[]{:S(2)}) %collective-permute-start.24) | collective-permute-done | bytes 262176 | tf_op jit(solution)/shard_map/ppermute | solution.py:464
  163.7 1.7 %shard_map.164 = bf16[128,16,1024]{2,1,0:T(8,128)(2,1)} custom-call(s32[6]{0:T(128)S(1)} %stack.79.place_ref, bf16[8,16,1024]{2,1,0:T(8,128)(2,1)S(1)} %collective-permute-done.17.refs_0_, bf16[8,16,1024]{2,1,0:T(8,128)(2,1)S(1)} %collective-permute-done.20.refs_1_, ...), custom_call_target="tpu_custom_call", output_to_operand_aliasing={{}: (7, {})} | custom-call | bytes 3145728 | tf_op jit(solution)/shard_map/pallas_call | solution.py:136
  (83 shorter events, 10.9 us)
Async XLA Ops:
  0.6 38.1 %copy-start.15 = (s32[40,1]{0,1:T(1,128)S(1)}, s32[40,1]{0,1:T(1,128)}, u32[]{:S(2)}) copy-start(s32[40,1]{0,1:T(1,128)} %constant.52) | copy-start | bytes 484
  0.6 61.0 %copy-start.12 = (pred[40,128]{1,0:T(8,128)(4,1)S(1)}, pred[40,128]{1,0:T(8,128)(4,1)}, u32[]{:S(2)}) copy-start(pred[40,128]{1,0:T(8,128)(4,1)} %constant.49.clone) | copy-start | bytes 15364
  0.7 36.4 %copy-start.13 = (s32[128]{0:T(128)S(1)}, s32[128]{0:T(128)}, u32[]{:S(2)}) copy-start(s32[128]{0:T(128)} %param.17) | copy-start | bytes 1540
  0.7 37.2 %copy-start.16 = (s32[128]{0:T(128)S(1)}, s32[128]{0:T(128)}, u32[]{:S(2)}) copy-start(s32[128]{0:T(128)} %param.18) | copy-start | bytes 1540
  0.7 16.1 %copy-start.1 = (bf16[1024,512]{1,0:T(8,128)(2,1)S(1)}, bf16[1024,512]{1,0:T(8,128)(2,1)}, u32[]{:S(2)}) copy-start(bf16[1024,512]{1,0:T(8,128)(2,1)} %query_ref.1) | copy-start | bytes 3145732
  0.7 16.1 %copy-start.3 = (bf16[1024,128]{1,0:T(8,128)(2,1)S(1)}, bf16[1024,128]{1,0:T(8,128)(2,1)}, u32[]{:S(2)}) copy-start(bf16[1024,128]{1,0:T(8,128)(2,1)} %keyval_ref.1) | copy-start | bytes 786436
  0.7 37.9 %copy-start.14 = (s32[8]{0:T(128)S(1)}, s32[8]{0:T(128)}, u32[]{:S(2)}) copy-start(s32[8]{0:T(128)} %param.19) | copy-start | bytes 100
  2.2 14.6 %all-to-all-start = ((bf16[8,5,1024]{2,1,0:T(8,128)(2,1)}), bf16[8,5,1024]{2,1,0:T(8,128)(2,1)S(1)}, u32[]{:S(2)}, u32[]{:S(2)}) async-start(bf16[8,5,1024]{2,1,0:T(8,128)(2,1)} %broadcast_in_dim.22), calls=%async_computation | async-start | bytes 262144 | tf_op jit(solution)/shard_map/all_to_all | solution.py:438
  10.0 6.8 %copy-start.6 = (s32[2]{0:T(128)S(1)}, s32[2]{0:T(128)}, u32[]{:S(2)}) copy-start(s32[2]{0:T(128)} %pad_add_fusion.1.me_ref) | copy-start | bytes 28
  17.8 14.5 %collective-permute-start.4 = (bf16[8,16,1024]{2,1,0:T(8,128)(2,1)}, bf16[8,16,1024]{2,1,0:T(8,128)(2,1)S(1)}, u32[]{:S(2)}, u32[]{:S(2)}) collective-permute-start(bf16[8,16,1024]{2,1,0:T(8,128)(2,1)} %get-tuple-element.121), channel_id=1, source_target_pairs={{0,12},{4,8},{8,4},{12,0},{16,28},{20,24},{24,20},{28,16},{1,13},{... | collective-permute-start | bytes 786440 | tf_op jit(solution)/shard_map/ppermute | solution.py:464
  20.0 12.2 %collective-permute-start.3 = (bf16[6,16,1024]{2,1,0:T(8,128)(2,1)}, bf16[6,16,1024]{2,1,0:T(8,128)(2,1)S(1)}, u32[]{:S(2)}, u32[]{:S(2)}) collective-permute-start(bf16[6,16,1024]{2,1,0:T(8,128)(2,1)} %get-tuple-element.120), channel_id=1, source_target_pairs={{0,24},{4,28},{8,16},{12,20},{16,8},{20,12},{24,0},{28,4},{1,25},{... | collective-permute-start | bytes 589832 | tf_op jit(solution)/shard_map/ppermute | solution.py:464
  22.4 1.9 %collective-permute-start = (f32[40,256]{1,0:T(8,128)S(1)}, f32[40,256]{1,0:T(8,128)S(1)}, u32[]{:S(2)}, u32[]{:S(2)}) collective-permute-start(f32[40,256]{1,0:T(8,128)S(1)} %get-tuple-element.117), channel_id=1, source_target_pairs={{0,1},{1,0},{2,3},{3,2},{4,5},{5,4},{6,7},{7,6},{8,9},{9,8},{10,11... | collective-permute-start | bytes 122888 | tf_op jit(solution)/shard_map/ppermute | solution.py:464
  22.4 4.0 %collective-permute-start.1 = (f32[40,256]{1,0:T(8,128)S(1)}, f32[40,256]{1,0:T(8,128)S(1)}, u32[]{:S(2)}, u32[]{:S(2)}) collective-permute-start(f32[40,256]{1,0:T(8,128)S(1)} %get-tuple-element.118), channel_id=1, source_target_pairs={{0,2},{1,3},{2,0},{3,1},{4,6},{5,7},{6,4},{7,5},{8,10},{9,11},{10,... | collective-permute-start | bytes 122888 | tf_op jit(solution)/shard_map/ppermute | solution.py:464
  23.9 3.5 %collective-permute-start.2 = (f32[40,256]{1,0:T(8,128)S(1)}, f32[40,256]{1,0:T(8,128)S(1)}, u32[]{:S(2)}, u32[]{:S(2)}) collective-permute-start(f32[40,256]{1,0:T(8,128)S(1)} %get-tuple-element.119), channel_id=1, source_target_pairs={{0,3},{1,2},{2,1},{3,0},{4,7},{5,6},{6,5},{7,4},{8,11},{9,10},{10,... | collective-permute-start | bytes 122888 | tf_op jit(solution)/shard_map/ppermute | solution.py:464
  33.6 18.2 %all-to-all-start.1 = ((bf16[8,48,256]{2,1,0:T(8,128)(2,1)}), bf16[8,48,256]{2,1,0:T(8,128)(2,1)S(1)}, u32[]{:S(2)}, u32[]{:S(2)}) async-start(bf16[8,48,256]{2,1,0:T(8,128)(2,1)} %shard_map.157), calls=%async_computation.1 | async-start | bytes 393216 | tf_op jit(solution)/shard_map/all_to_all | solution.py:557
  38.8 16.2 %collective-permute-start.8 = (bf16[10,16,1024]{2,1,0:T(8,128)(2,1)}, bf16[10,16,1024]{2,1,0:T(8,128)(2,1)S(1)}, u32[]{:S(2)}, u32[]{:S(2)}) collective-permute-start(bf16[10,16,1024]{2,1,0:T(8,128)(2,1)} %get-tuple-element.135), channel_id=1, source_target_pairs={{0,24},{4,28},{8,16},{12,20},{16,8},{20,12},{24,0},{28,4},{1,25},{... | collective-permute-start | bytes 983048 | tf_op jit(solution)/shard_map/ppermute | solution.py:464
  52.4 0.7 copy-start
  53.1 9.8 %copy-start.5 = (bf16[8,40,128]{2,1,0:T(8,128)(2,1)}, bf16[8,40,128]{2,1,0:T(8,128)(2,1)S(1)}, u32[]{:S(2)}) copy-start(bf16[8,40,128]{2,1,0:T(8,128)(2,1)S(1)} %get-tuple-element.141.refs_0_) | copy-start | bytes 245764
  53.1 1.9 %collective-permute-start.5 = (bf16[8,40,128]{2,1,0:T(8,128)(2,1)S(1)}, bf16[8,40,128]{2,1,0:T(8,128)(2,1)S(1)}, u32[]{:S(2)}, u32[]{:S(2)}) collective-permute-start(bf16[8,40,128]{2,1,0:T(8,128)(2,1)S(1)} %get-tuple-element.141.refs_0_), channel_id=1, source_target_pairs={{0,1},{1,0},{2,3},{3,2},{4,5},{5,4},{6,7},{7,6},{8,9},{9,8},{10,11... | collective-permute-start | bytes 245768 | tf_op jit(solution)/shard_map/ppermute | solution.py:464
  53.1 5.2 %collective-permute-start.6 = (bf16[8,40,128]{2,1,0:T(8,128)(2,1)S(1)}, bf16[8,40,128]{2,1,0:T(8,128)(2,1)S(1)}, u32[]{:S(2)}, u32[]{:S(2)}) collective-permute-start(bf16[8,40,128]{2,1,0:T(8,128)(2,1)S(1)} %get-tuple-element.141.refs_0_), channel_id=1, source_target_pairs={{0,2},{1,3},{2,0},{3,1},{4,6},{5,7},{6,4},{7,5},{8,10},{9,11},{10,... | collective-permute-start | bytes 245768 | tf_op jit(solution)/shard_map/ppermute | solution.py:464
  54.6 4.7 %collective-permute-start.7 = (bf16[8,40,128]{2,1,0:T(8,128)(2,1)S(1)}, bf16[8,40,128]{2,1,0:T(8,128)(2,1)S(1)}, u32[]{:S(2)}, u32[]{:S(2)}) collective-permute-start(bf16[8,40,128]{2,1,0:T(8,128)(2,1)S(1)} %get-tuple-element.141.refs_0_), channel_id=1, source_target_pairs={{0,3},{1,2},{2,1},{3,0},{4,7},{5,6},{6,5},{7,4},{8,11},{9,10},{10,... | collective-permute-start | bytes 245768 | tf_op jit(solution)/shard_map/ppermute | solution.py:464
  55.0 8.0 %copy-start.9 = (bf16[8,40,128]{2,1,0:T(8,128)(2,1)}, bf16[8,40,128]{2,1,0:T(8,128)(2,1)S(1)}, u32[]{:S(2)}) copy-start(bf16[8,40,128]{2,1,0:T(8,128)(2,1)S(1)} %collective-permute-done.5.refs_1_) | copy-start | bytes 245764
  58.4 4.6 %copy-start.10 = (bf16[8,40,128]{2,1,0:T(8,128)(2,1)}, bf16[8,40,128]{2,1,0:T(8,128)(2,1)S(1)}, u32[]{:S(2)}) copy-start(bf16[8,40,128]{2,1,0:T(8,128)(2,1)S(1)} %collective-permute-done.6.refs_2_) | copy-start | bytes 245764
  59.3 3.6 %copy-start.11 = (bf16[8,40,128]{2,1,0:T(8,128)(2,1)}, bf16[8,40,128]{2,1,0:T(8,128)(2,1)S(1)}, u32[]{:S(2)}) copy-start(bf16[8,40,128]{2,1,0:T(8,128)(2,1)S(1)} %collective-permute-done.7.refs_3_) | copy-start | bytes 245764
  59.3 20.6 %collective-permute-start.10 = (bf16[16,16,1024]{2,1,0:T(8,128)(2,1)}, bf16[16,16,1024]{2,1,0:T(8,128)(2,1)S(1)}, u32[]{:S(2)}, u32[]{:S(2)}) collective-permute-start(bf16[16,16,1024]{2,1,0:T(8,128)(2,1)} %get-tuple-element.154), channel_id=1, source_target_pairs={{0,8},{4,12},{8,0},{12,4},{16,24},{20,28},{24,16},{28,20},{1,9},{5... | collective-permute-start | bytes 1572872 | tf_op jit(solution)/shard_map/ppermute | solution.py:464
  60.3 19.7 %collective-permute-start.9 = (bf16[8,16,1024]{2,1,0:T(8,128)(2,1)}, bf16[8,16,1024]{2,1,0:T(8,128)(2,1)S(1)}, u32[]{:S(2)}, u32[]{:S(2)}) collective-permute-start(bf16[8,16,1024]{2,1,0:T(8,128)(2,1)} %get-tuple-element.153), channel_id=1, source_target_pairs={{0,28},{4,24},{8,20},{12,16},{16,12},{20,8},{24,4},{28,0},{1,29},{... | collective-permute-start | bytes 786440 | tf_op jit(solution)/shard_map/ppermute | solution.py:464
  63.0 17.0 %copy-start.19 = (bf16[8,16,1024]{2,1,0:T(8,128)(2,1)S(1)}, bf16[8,16,1024]{2,1,0:T(8,128)(2,1)}, u32[]{:S(2)}) copy-start(bf16[8,16,1024]{2,1,0:T(8,128)(2,1)} %get-tuple-element.165) | copy-start | bytes 786436
  63.0 20.0 %copy-start.18 = (bf16[8,16,1024]{2,1,0:T(8,128)(2,1)S(1)}, bf16[8,16,1024]{2,1,0:T(8,128)(2,1)}, u32[]{:S(2)}) copy-start(bf16[8,16,1024]{2,1,0:T(8,128)(2,1)} %get-tuple-element.166) | copy-start | bytes 786436
  80.0 12.0 %collective-permute-start.14 = (bf16[8,16,1024]{2,1,0:T(8,128)(2,1)S(1)}, bf16[8,16,1024]{2,1,0:T(8,128)(2,1)S(1)}, u32[]{:S(2)}, u32[]{:S(2)}) collective-permute-start(bf16[8,16,1024]{2,1,0:T(8,128)(2,1)S(1)} %copy-done.19), channel_id=1, source_target_pairs={{0,28},{4,24},{8,20},{12,16},{16,12},{20,8},{24,4},{28,0},{1,29},{... | collective-permute-start | bytes 786440 | tf_op jit(solution)/shard_map/ppermute | solution.py:464
  82.9 13.3 %collective-permute-start.15 = (bf16[8,16,1024]{2,1,0:T(8,128)(2,1)S(1)}, bf16[8,16,1024]{2,1,0:T(8,128)(2,1)S(1)}, u32[]{:S(2)}, u32[]{:S(2)}) collective-permute-start(bf16[8,16,1024]{2,1,0:T(8,128)(2,1)S(1)} %copy-done.18), channel_id=1, source_target_pairs={{0,12},{4,8},{8,4},{12,0},{16,28},{20,24},{24,20},{28,16},{1,13},{... | collective-permute-start | bytes 786440 | tf_op jit(solution)/shard_map/ppermute | solution.py:464
  82.9 1.9 %collective-permute-start.11 = (bf16[8,64,128]{2,1,0:T(8,128)(2,1)}, bf16[8,64,128]{2,1,0:T(8,128)(2,1)S(1)}, u32[]{:S(2)}, u32[]{:S(2)}) collective-permute-start(bf16[8,64,128]{2,1,0:T(8,128)(2,1)} %get-tuple-element.162), channel_id=1, source_target_pairs={{0,1},{1,0},{2,3},{3,2},{4,5},{5,4},{6,7},{7,6},{8,9},{9,8},{10,11... | collective-permute-start | bytes 393224 | tf_op jit(solution)/shard_map/ppermute | solution.py:464
  83.0 6.6 %collective-permute-start.12 = (bf16[8,64,128]{2,1,0:T(8,128)(2,1)}, bf16[8,64,128]{2,1,0:T(8,128)(2,1)S(1)}, u32[]{:S(2)}, u32[]{:S(2)}) collective-permute-start(bf16[8,64,128]{2,1,0:T(8,128)(2,1)} %get-tuple-element.163), channel_id=1, source_target_pairs={{0,2},{1,3},{2,0},{3,1},{4,6},{5,7},{6,4},{7,5},{8,10},{9,11},{10,... | collective-permute-start | bytes 393224 | tf_op jit(solution)/shard_map/ppermute | solution.py:464
  84.5 6.9 %collective-permute-start.13 = (bf16[8,64,128]{2,1,0:T(8,128)(2,1)}, bf16[8,64,128]{2,1,0:T(8,128)(2,1)S(1)}, u32[]{:S(2)}, u32[]{:S(2)}) collective-permute-start(bf16[8,64,128]{2,1,0:T(8,128)(2,1)} %get-tuple-element.164), channel_id=1, source_target_pairs={{0,3},{1,2},{2,1},{3,0},{4,7},{5,6},{6,5},{7,4},{8,11},{9,10},{10,... | collective-permute-start | bytes 393224 | tf_op jit(solution)/shard_map/ppermute | solution.py:464
  96.2 0.9 copy-start.4
  98.2 1.9 %copy-start.17 = (bf16[12,16,1024]{2,1,0:T(8,128)(2,1)S(1)}, bf16[12,16,1024]{2,1,0:T(8,128)(2,1)}, u32[]{:S(2)}) copy-start(bf16[12,16,1024]{2,1,0:T(8,128)(2,1)} %get-tuple-element.183) | copy-start | bytes 1179652
  98.2 50.6 %copy-start.2 = (bf16[1024,512]{1,0:T(8,128)(2,1)S(1)}, bf16[1024,512]{1,0:T(8,128)(2,1)}, u32[]{:S(2)}) copy-start(bf16[1024,512]{1,0:T(8,128)(2,1)} %weight_ref.1) | copy-start | bytes 3145732
  98.2 50.6 %copy-start.7 = (s32[2]{0:T(128)S(1)}, s32[2]{0:T(128)}, u32[]{:S(2)}) copy-start(s32[2]{0:T(128)} %pad_add_fusion.1.me_ref) | copy-start | bytes 28
  100.1 22.1 %collective-permute-start.16 = (bf16[12,16,1024]{2,1,0:T(8,128)(2,1)S(1)}, bf16[12,16,1024]{2,1,0:T(8,128)(2,1)S(1)}, u32[]{:S(2)}, u32[]{:S(2)}) collective-permute-start(bf16[12,16,1024]{2,1,0:T(8,128)(2,1)S(1)} %copy-done.17), channel_id=1, source_target_pairs={{0,16},{4,20},{8,24},{12,28},{16,0},{20,4},{24,8},{28,12},{1,17},{... | collective-permute-start | bytes 1179656 | tf_op jit(solution)/shard_map/ppermute | solution.py:464
  100.8 21.5 %collective-permute-start.17 = (bf16[8,16,1024]{2,1,0:T(8,128)(2,1)}, bf16[8,16,1024]{2,1,0:T(8,128)(2,1)S(1)}, u32[]{:S(2)}, u32[]{:S(2)}) collective-permute-start(bf16[8,16,1024]{2,1,0:T(8,128)(2,1)} %get-tuple-element.184), channel_id=1, source_target_pairs={{0,4},{4,0},{8,12},{12,8},{16,20},{20,16},{24,28},{28,24},{1,5},{5... | collective-permute-start | bytes 786440 | tf_op jit(solution)/shard_map/ppermute | solution.py:464
  101.6 20.7 %all-to-all-start.2 = ((bf16[8,64,128]{2,1,0:T(8,128)(2,1)}), bf16[8,64,128]{2,1,0:T(8,128)(2,1)S(1)}, u32[]{:S(2)}, u32[]{:S(2)}) async-start(bf16[8,64,128]{2,1,0:T(8,128)(2,1)} %shard_map.160), calls=%async_computation.2 | async-start | bytes 262144 | tf_op jit(solution)/shard_map/all_to_all | solution.py:618
  125.9 22.6 %collective-permute-start.18 = (bf16[8,16,1024]{2,1,0:T(8,128)(2,1)}, bf16[8,16,1024]{2,1,0:T(8,128)(2,1)S(1)}, u32[]{:S(2)}, u32[]{:S(2)}) collective-permute-start(bf16[8,16,1024]{2,1,0:T(8,128)(2,1)} %get-tuple-element.193), channel_id=1, source_target_pairs={{0,20},{4,16},{8,28},{12,24},{16,4},{20,0},{24,12},{28,8},{1,21},{... | collective-permute-start | bytes 786440 | tf_op jit(solution)/shard_map/ppermute | solution.py:464
  127.2 21.3 %collective-permute-start.20 = (bf16[8,16,1024]{2,1,0:T(8,128)(2,1)}, bf16[8,16,1024]{2,1,0:T(8,128)(2,1)S(1)}, u32[]{:S(2)}, u32[]{:S(2)}) collective-permute-start(bf16[8,16,1024]{2,1,0:T(8,128)(2,1)} %get-tuple-element.195), channel_id=1, source_target_pairs={{0,4},{4,0},{8,12},{12,8},{16,20},{20,16},{24,28},{28,24},{1,5},{5... | collective-permute-start | bytes 786440 | tf_op jit(solution)/shard_map/ppermute | solution.py:464
  128.8 19.7 %all-to-all-start.3 = ((bf16[8,40,128]{2,1,0:T(8,128)(2,1)}), bf16[8,40,128]{2,1,0:T(8,128)(2,1)S(1)}, u32[]{:S(2)}, u32[]{:S(2)}) async-start(bf16[8,40,128]{2,1,0:T(8,128)(2,1)} %shard_map.162), calls=%async_computation.3 | async-start | bytes 163840 | tf_op jit(solution)/shard_map/all_to_all | solution.py:621
  132.5 16.0 %collective-permute-start.19 = (bf16[4,16,1024]{2,1,0:T(8,128)(2,1)}, bf16[4,16,1024]{2,1,0:T(8,128)(2,1)S(1)}, u32[]{:S(2)}, u32[]{:S(2)}) collective-permute-start(bf16[4,16,1024]{2,1,0:T(8,128)(2,1)} %get-tuple-element.194), channel_id=1, source_target_pairs={{0,16},{4,20},{8,24},{12,28},{16,0},{20,4},{24,8},{28,12},{1,17},{... | collective-permute-start | bytes 393224 | tf_op jit(solution)/shard_map/ppermute | solution.py:464
  148.5 15.3 %collective-permute-start.24 = (bf16[8,16,1024]{2,1,0:T(8,128)(2,1)}, bf16[8,16,1024]{2,1,0:T(8,128)(2,1)S(1)}, u32[]{:S(2)}, u32[]{:S(2)}) collective-permute-start(bf16[8,16,1024]{2,1,0:T(8,128)(2,1)} %get-tuple-element.203), channel_id=1, source_target_pairs={{0,20},{4,16},{8,28},{12,24},{16,4},{20,0},{24,12},{28,8},{1,21},{... | collective-permute-start | bytes 786440 | tf_op jit(solution)/shard_map/ppermute | solution.py:464
  149.8 4.0 %collective-permute-start.22 = (f32[10,512]{1,0:T(8,128)S(1)}, f32[10,512]{1,0:T(8,128)S(1)}, u32[]{:S(2)}, u32[]{:S(2)}) collective-permute-start(f32[10,512]{1,0:T(8,128)S(1)} %get-tuple-element.201), channel_id=1, source_target_pairs={{0,2},{1,3},{2,0},{3,1},{4,6},{5,7},{6,4},{7,5},{8,10},{9,11},{10,... | collective-permute-start | bytes 61448 | tf_op jit(solution)/shard_map/ppermute | solution.py:464
  151.3 3.3 %collective-permute-start.23 = (f32[10,512]{1,0:T(8,128)S(1)}, f32[10,512]{1,0:T(8,128)S(1)}, u32[]{:S(2)}, u32[]{:S(2)}) collective-permute-start(f32[10,512]{1,0:T(8,128)S(1)} %get-tuple-element.202), channel_id=1, source_target_pairs={{0,3},{1,2},{2,1},{3,0},{4,7},{5,6},{6,5},{7,4},{8,11},{9,10},{10,... | collective-permute-start | bytes 61448 | tf_op jit(solution)/shard_map/ppermute | solution.py:464
  151.3 3.3 %collective-permute-start.21 = (f32[10,512]{1,0:T(8,128)S(1)}, f32[10,512]{1,0:T(8,128)S(1)}, u32[]{:S(2)}, u32[]{:S(2)}) collective-permute-start(f32[10,512]{1,0:T(8,128)S(1)} %get-tuple-element.200), channel_id=1, source_target_pairs={{0,1},{1,0},{2,3},{3,2},{4,5},{5,4},{6,7},{7,6},{8,9},{9,8},{10,11... | collective-permute-start | bytes 61448 | tf_op jit(solution)/shard_map/ppermute | solution.py:464
  (1 other events, 0.7 us)

commit v9 on v8

--- a/solution.py
+++ b/solution.py
@@ -3,7 +3,6 @@
 
 import jax
 import jax.numpy as jnp
-import numpy as np
 from jax import lax
 from jax.experimental import pallas as pl
 from jax.experimental.pallas import tpu as pltpu
@@ -19,7 +18,7 @@
 SCALE2 = math.log2(math.e) / math.sqrt(HD)
 STAT = 16
 MIB = 1024 * 1024
-CUTS = {1: (0, 8, 16), 2: (0, 16), 3: (0, 8, 16), 4: (0, 12, 16), 5: (0, 8, 16), 6: (0, 6, 16), 7: (0, 8, 16)}
+CUTS = {1: (0, 8, 16), 2: (0, 16), 3: (0, 8, 16), 4: (0, 16), 5: (0, 10, 16), 6: (0, 4, 16), 7: (0, 4, 11, 16)}
 NT = (((1,), (1,)), ((), ()))
 
 
@@ -32,7 +31,7 @@
 
 
 def order_kernel(
-    wide, parts, me_ref, dest_ref, req_ref, idx_ref, pool_ref, out_ref, tag_ref, *refs
+    wide, parts, me_ref, dest_ref, req_ref, idx_ref, pool_ref, out_ref, tag_ref, token_ref, *refs
 ):
     chunk_refs, refs = refs[: len(parts)], refs[len(parts) :]
     pages_ref, line_ref, source_ref, in_sem, out_sem, line_sem = refs
@@ -78,6 +77,18 @@
         chosen, spread_out.astype(jnp.bfloat16), preferred_element_type=jnp.float32
     )
 
+    tokens = slots * PAGE
+    page = lax.broadcasted_iota(jnp.int32, (slots, tokens), 0)
+    token = lax.broadcasted_iota(jnp.int32, (slots, tokens), 1)
+    widen = jnp.where(page == token // PAGE, 1.0, 0.0).astype(jnp.bfloat16)
+    row = lax.broadcasted_iota(jnp.int32, (8, slots), 0)
+    stacked = jnp.zeros((8, slots), jnp.float32)
+    for i, field in enumerate(fields):
+        stacked = jnp.where(row == i, field.astype(jnp.float32), stacked)
+    token_ref[...] = jnp.dot(
+        stacked.astype(jnp.bfloat16), widen, preferred_element_type=jnp.float32
+    )
+
     copies = []
     for c, (first, count, target) in enumerate(blocks):
         held = pages_ref.at[pl.ds(first, count)]
@@ -92,6 +103,7 @@
     slots = pool.shape[0]
     part = lambda count: jax.ShapeDtypeStruct((count,) + pool.shape[1:], pool.dtype)
     out_shape = [part(slots), jax.ShapeDtypeStruct((wide, slots), jnp.float32)]
+    out_shape += [jax.ShapeDtypeStruct((8, slots * PAGE), jnp.float32)]
     out_shape += [part(last - first) for _, first, last in parts]
     vmem = pl.BlockSpec(memory_space=pltpu.VMEM)
     hbm = pl.BlockSpec(memory_space=pltpu.HBM)
@@ -99,7 +111,7 @@
         functools.partial(order_kernel, wide, parts),
         out_shape=out_shape,
         in_specs=[pl.BlockSpec(memory_space=pltpu.SMEM), vmem, vmem, vmem, hbm],
-        out_specs=[hbm, vmem] + [hbm] * len(parts),
+        out_specs=[hbm, vmem, vmem] + [hbm] * len(parts),
         scratch_shapes=[
             pltpu.VMEM(pool.shape, pool.dtype),
             pltpu.VMEM((1, slots), jnp.int32),
@@ -159,18 +171,30 @@
     return high, mid, peak - high - mid, cut(total), total - cut(total)
 
 
-def attend_kernel(rows, piece, peers, me_ref, *refs):
+def attend_kernel(rows, piece, peers, me_ref, length_ref, *refs):
     query_refs, refs = refs[:peers], refs[peers:]
-    key_ref, value_ref, new_key_ref, new_value_ref, req_ref, pos_ref, row_ref, new_bias_ref = refs[:8]
-    out_refs = refs[8 : 8 + peers]
-    bias_ref, score_ref, weight_ref, query_ref, result_ref = refs[8 + peers :]
+    key_ref, value_ref, new_key_ref, new_value_ref, token_ref = refs[:5]
+    out_refs = refs[5 : 5 + peers]
+    bias_ref, new_bias_ref, score_ref, weight_ref, query_ref, result_ref = refs[5 + peers :]
     tokens = key_ref.shape[0]
     step = pl.program_id(0)
 
     @pl.when(step == 0)
     def _():
-        seen = (req_ref[...] == row_ref[:, 0:1]) & (pos_ref[...] < row_ref[:, 1:2])
+        owner = token_ref[0:1, :]
+        offset = lax.broadcasted_iota(jnp.int32, owner.shape, 1) % PAGE
+        spot = (token_ref[1:2, :] * 32 + token_ref[2:3, :] - 1) * PAGE + offset.astype(jnp.float32)
+        request = lax.broadcasted_iota(jnp.int32, (rows, 1), 0) // STEPS
+        limit = jnp.zeros((rows, 1), jnp.int32)
+        for r in range(rows // STEPS):
+            limit = jnp.where(request == r, length_ref[r], limit)
+        seen = (owner == request.astype(jnp.float32)) & (spot < limit.astype(jnp.float32))
         bias_ref[...] = jnp.where(seen, 0.0, NEG_FILL)
+        row = lax.broadcasted_iota(jnp.int32, new_bias_ref.shape, 0)
+        col = lax.broadcasted_iota(jnp.int32, new_bias_ref.shape, 1)
+        first = jnp.where((me_ref[0] == 0) & (me_ref[1] == 0), 1, 0)
+        seen = (row // STEPS == col // STEPS) & (col <= row) & (col < rows * first)
+        new_bias_ref[...] = jnp.where(seen, 0.0, NEG_FILL)
         if peers > 1:
             for d in range(peers):
                 query_ref[me_ref[1] ^ d] = query_refs[d][...]
@@ -250,7 +274,7 @@
         out_refs[0][...] = result_ref[...]
 
 
-def attend(me, queries, keyval, pool, req_tok, pos_tok, row_info, new_bias, rows, piece):
+def attend(me, lengths, queries, keyval, pool, token_info, rows, piece):
     tokens = pool.shape[0]
     extra = keyval.shape[0]
     peers = len(queries)
@@ -269,21 +293,19 @@
         functools.partial(attend_kernel, rows, piece, peers),
         grid=(KVH,),
         out_shape=[out_shape] * peers,
-        in_specs=[pl.BlockSpec(memory_space=pltpu.SMEM)]
+        in_specs=[pl.BlockSpec(memory_space=pltpu.SMEM)] * 2
         + [query_spec] * peers
         + [
             pl.BlockSpec((tokens, HD), lambda k: (0, k)),
             pl.BlockSpec((tokens, HD), lambda k: (0, KVH + k)),
             pl.BlockSpec((extra, HD), lambda k: (0, k)),
             pl.BlockSpec((extra, HD), lambda k: (0, KVH + k)),
-            whole(req_tok.shape),
-            whole(pos_tok.shape),
-            whole(row_info.shape),
-            whole(new_bias.shape),
+            whole(token_info.shape),
         ],
         out_specs=[out_spec] * peers,
         scratch_shapes=[
             pltpu.VMEM((rows, tokens), jnp.float32),
+            pltpu.VMEM((rows, extra), jnp.float32),
             pltpu.VMEM((GROUPS * rows, tokens + extra), jnp.float32),
             pltpu.VMEM((GROUPS * rows, tokens + extra), jnp.bfloat16),
             pltpu.VMEM((peers,) + queries[0].shape, jnp.bfloat16),
@@ -291,11 +313,15 @@
         ],
         compiler_params=pltpu.CompilerParams(vmem_limit_bytes=56 * MIB),
         cost_estimate=pl.CostEstimate(flops=0, bytes_accessed=0, transcendentals=0),
-    )(me, *queries, pool, pool, keyval, keyval, req_tok, pos_tok, row_info, new_bias)
+    )(me, lengths, *queries, pool, pool, keyval, keyval, token_info)
 
 
 def combine_kernel(piece, last, count, *refs):
-    part_refs, out_ref = refs[:count], refs[count]
+    if last:
+        part_ref, out_ref = refs
+        part_refs = [part_ref.at[pl.ds(i, 1)] for i in range(count)]
+    else:
+        part_refs, out_ref = refs[:count], refs[count]
     groups, height = part_refs[0].shape[:2]
     peaks, totals = [], []
     for i in range(count):
@@ -332,10 +358,10 @@
 
 
 def combine(parts, piece, repeats=0):
-    groups, height = parts[0].shape[:2]
-    shape = (repeats, piece, HD) if repeats else (groups, height, HD)
+    count = parts[0].shape[0] if repeats else len(parts)
+    shape = (repeats, piece, HD) if repeats else parts[0].shape
     return pl.pallas_call(
-        functools.partial(combine_kernel, piece, repeats > 0, len(parts)),
+        functools.partial(combine_kernel, piece, repeats > 0, count),
         out_shape=jax.ShapeDtypeStruct(shape, jnp.bfloat16),
         in_specs=[pl.BlockSpec(memory_space=pltpu.VMEM)] * len(parts),
         out_specs=pl.BlockSpec(memory_space=pltpu.VMEM),
@@ -386,7 +412,8 @@
         out_ref[i] = packed
 
 
-def unpack_kernel(rows, me_ref, part_ref, query_ref, keyval_ref, tag_ref):
+def unpack_kernel(rows, me_ref, kept_ref, part_ref, query_ref, keyval_ref, *refs):
+    entry_ref, req_ref, idx_ref = refs
     count = part_ref.shape[0]
     line = lax.broadcasted_iota(jnp.int32, (count, HD), 0)
     tags = jnp.zeros((count, HD), jnp.float32)
@@ -398,7 +425,26 @@
         keyval_ref[:, i * HD : (i + 1) * HD] = block
         mine = jnp.where(line == me_ref[0], part[rows : rows + count, :HD], 0.0)
         tags = tags + jnp.where(line == i, jnp.sum(mine, axis=0, keepdims=True), 0.0)
-    tag_ref[...] = tags
+    capacity = HD // count
+    high = lax.broadcasted_iota(jnp.int32, (HD, HD), 0)
+    low = lax.broadcasted_iota(jnp.int32, (HD, HD), 1)
+    slot = lax.broadcasted_iota(jnp.int32, (count, HD), 1)
+    tags = tags.astype(jnp.bfloat16)
+    fields = []
+    for i in range(3):
+        pick = jnp.where(high == i * capacity + low % capacity, 1.0, 0.0).astype(jnp.bfloat16)
+        spread_out = jnp.dot(tags, pick, preferred_element_type=jnp.float32)
+        spread_out = jnp.where(slot // capacity == line, spread_out, 0.0)
+        fields.append(jnp.sum(spread_out, axis=0, keepdims=True))
+    req_ref[...] = fields[0].astype(jnp.int32)
+    idx_ref[...] = (fields[1] * 32.0 + fields[2] - 1.0).astype(jnp.int32)
+    local = entry_ref.shape[1]
+    step = lax.broadcasted_iota(jnp.int32, (16, keyval_ref.shape[0]), 0)
+    row = lax.broadcasted_iota(jnp.int32, (16, keyval_ref.shape[0]), 1)
+    kept = (row == me_ref[0] * local + step) & (step < kept_ref[me_ref[0]])
+    kept = jnp.where(kept, 1.0, 0.0).astype(jnp.bfloat16)
+    entries = jnp.dot(kept, keyval_ref[...], preferred_element_type=jnp.float32)
+    entry_ref[0] = entries[:local].astype(jnp.bfloat16)
 
 
 def finish_kernel(peers, me_ref, part_ref, weight_ref, *refs):
@@ -414,7 +460,7 @@
 
 
 def in_vmem(kernel, out_shape, me, *args, scratch=()):
-    head = [] if me is None else [me]
+    head = [] if me is None else list(me) if isinstance(me, tuple) else [me]
     return pl.pallas_call(
         kernel,
         out_shape=out_shape,
@@ -455,7 +501,8 @@
     own_cols = w_query.shape[1] // narrow
     piece = HEADS * rows // (wide * narrow)
     extra = up(rows, HD)
-    direct = piece == rows and own_cols == HD and wide == 8 and narrow == 4
+    direct = piece == rows and own_cols == HD and slots == HD
+    direct = direct and wide == 8 and narrow == 4 and local_rows == STEPS
     me = lax.axis_index("wide")
     both = jnp.stack([me, lax.axis_index("narrow")])
     exchange = functools.partial(lax.all_to_all, split_axis=0, concat_axis=0, tiled=True)
@@ -475,7 +522,7 @@
     for d in range(1, wide):
         cuts = [cut * capacity // 16 for cut in CUTS[group_of(d, wide)]]
         parts += [(d, a, b) for a, b in zip(cuts[:-1], cuts[1:]) if b > a]
-    moved_pool, tags, *chunks = order_pages(
+    moved_pool, tags, token_info, *chunks = order_pages(
         both, moves, page_req, page_idx, pool, wide, parts
     )
     arrived = {}
@@ -516,23 +563,6 @@
         arrived.clear()
         return pages
 
-    def prepare(page_req, page_idx, lengths):
-        req_tok = jnp.broadcast_to(page_req[:, None], (slots, PAGE)).reshape(1, -1)
-        pos_tok = page_idx[:, None] * PAGE + jnp.arange(PAGE, dtype=jnp.int32)[None, :]
-        row_info = jnp.stack(
-            [
-                jnp.asarray(np.arange(rows) // STEPS, jnp.int32),
-                jnp.broadcast_to(lengths[:, None], (requests, STEPS)).reshape(rows),
-            ],
-            axis=1,
-        )
-        return req_tok, pos_tok.reshape(1, -1), row_info
-
-    here = (me == 0) & (lax.axis_index("narrow") == 0)
-    row_ids = np.arange(rows)[:, None]
-    col_ids = np.arange(extra)[None, :]
-    causal = (row_ids // STEPS == col_ids // STEPS) & (col_ids <= row_ids) & (col_ids < rows)
-    new_bias = jnp.where(jnp.asarray(causal) & here, 0.0, NEG_FILL).astype(jnp.float32)
     tokens = pool.reshape(slots * PAGE, -1)
     if direct:
         block = jax.ShapeDtypeStruct((rows, 2 * HD), jnp.float32)
@@ -553,20 +583,21 @@
             *partial,
             tags,
         )
-        packed, raw = lax.optimization_barrier((packed, (page_req, page_idx, lengths)))
-        received = exchange(packed, "wide")
-        info = launch(prepare(*raw), (6, 1))
-        queries, keyval, tags_in = in_vmem(
+        received = beside(lambda value: exchange(value, "wide"), packed, (6, 1))
+        queries, keyval, new_entries, moved_req, moved_idx = in_vmem(
             functools.partial(unpack_kernel, rows),
             [
                 jax.ShapeDtypeStruct((wide, rows, HD), jnp.bfloat16),
                 jax.ShapeDtypeStruct((extra, wide * HD), jnp.bfloat16),
-                jax.ShapeDtypeStruct((wide, HD), jnp.float32),
+                jax.ShapeDtypeStruct((1, local_rows, wide * HD), jnp.bfloat16),
+                jax.ShapeDtypeStruct((1, slots), jnp.int32),
+                jax.ShapeDtypeStruct((1, slots), jnp.int32),
             ],
-            both,
+            (both, accepted),
             received,
         )
-        queries = share(launch(queries, (7, 0)), "narrow")
+        moved_req, moved_idx = moved_req.reshape(slots), moved_idx.reshape(slots)
+        queries = beside(lambda value: share(value, "narrow"), queries, (7, 0), (1, 0))
     else:
         gathered = gathered.reshape(rows, -1)
         query_part = jnp.dot(gathered, w_query, preferred_element_type=jnp.float32)
@@ -581,47 +612,46 @@
         tags = jnp.pad(tags, ((0, 0), (0, 7), (0, projected.shape[1] - tags.shape[2])))
         packed = jnp.broadcast_to(projected[None], (wide,) + projected.shape)
         packed = jnp.concatenate([packed, tags], axis=1)
-        packed, raw = lax.optimization_barrier((packed, (page_req, page_idx, lengths)))
-        received = exchange(packed, "wide")
-        info = launch(prepare(*raw), (6, 1))
+        received = beside(lambda value: exchange(value, "wide"), packed, (6, 1))
         tags_in = received[:, rows]
-        queries = spread(launch(received[:, :rows, :own_cols], (7, 0)), "narrow")
+        queries = received[:, :rows, :own_cols]
+        queries = beside(lambda value: spread(value, "narrow"), queries, (7, 0), (1, 0))
         queries = jnp.transpose(queries, (2, 1, 0, 3)).reshape(rows, HEADS, HD)
         queries = [jnp.transpose(queries, (1, 0, 2)).reshape(KVH, GROUPS * rows, HD)]
         keyval = jnp.transpose(received[:, :rows, own_cols:], (1, 0, 2)).reshape(rows, -1)
         keyval = jnp.pad(keyval, ((0, extra - rows), (0, 0)))
-
-    def small_outputs(keyval, tags):
-        tags = tags.astype(jnp.int32)
-        moved_req = tags[:, :capacity].reshape(slots)
-        moved_idx = tags[:, capacity : 2 * capacity] * 32
-        moved_idx = (moved_idx + tags[:, 2 * capacity : 3 * capacity] - 1).reshape(slots)
+        tags_in = tags_in.astype(jnp.int32)
+        moved_req = tags_in[:, :capacity].reshape(slots)
+        moved_idx = tags_in[:, capacity : 2 * capacity] * 32
+        moved_idx = (moved_idx + tags_in[:, 2 * capacity : 3 * capacity] - 1).reshape(slots)
         local_req = local_rows // STEPS
         fresh = lax.dynamic_slice_in_dim(keyval, me * local_rows, local_rows, 0)
         fresh = fresh.reshape(local_req, STEPS, -1)
         kept = lax.dynamic_slice_in_dim(accepted, me * local_req, local_req, 0)
         step_ids = jnp.arange(STEPS)[None, :, None]
-        entries = jnp.where(step_ids < kept[:, None, None], fresh, jnp.zeros((), jnp.bfloat16))
-        return entries, moved_req, moved_idx
-
-    queries = launch(land(queries, (6, 1)), (2, 0))
-    mixed = attend(both, queries, keyval, tokens, *info, new_bias, rows, piece)
-    mixed = launch(land(mixed, (7, 0), (2, 0)), (7, 1), (3, 1))
+        new_entries = jnp.where(
+            step_ids < kept[:, None, None], fresh, jnp.zeros((), jnp.bfloat16)
+        )
+
+    mixed = beside(
+        lambda value: attend(both, lengths, value, keyval, tokens, token_info, rows, piece),
+        queries,
+        (7, 1),
+        (2, 0),
+    )
     if direct:
-        mixed = deal(mixed, "narrow")
+        mixed = beside(lambda value: deal(value, "narrow"), mixed, (7, 2), (3, 1))
     else:
-        mixed = exchange(mixed[0], "narrow").reshape((narrow, wide) + mixed[0].shape[1:])
+        mixed = beside(lambda value: exchange(value, "narrow"), mixed[0], (7, 2), (3, 1))
+        mixed = mixed.reshape((narrow, wide) + mixed.shape[1:])
         mixed = [mixed[i] for i in range(narrow)]
-    mixed = combine(land(mixed, (7, 1), (3, 1)), piece)
-    mixed, moved_pool = lax.optimization_barrier((mixed, moved_pool))
-    moved_pool = launch(placed(moved_pool), (4, 0), (1, 0))
-    mixed = land(exchange(mixed, "wide"), (4, 0), (1, 0))
-    attn = combine([mixed[i][None] for i in range(wide)], piece, wide)
-    attn, raw = lax.optimization_barrier((attn, (keyval, tags_in)))
-    attn = exchange(attn, "wide")
-    small = launch(small_outputs(*raw), (5, 0), (4, 1), (1, 1))
-    new_entries, moved_req, moved_idx = small
-    attn = launch(land(attn, (5, 0), (4, 1), (1, 1)), (5, 1))
+    mixed = combine(mixed, piece)
+    mixed, pages = lax.optimization_barrier((mixed, moved_pool))
+    pages = placed(pages)
+    mixed = beside(lambda value: exchange(value, "wide"), mixed, (4, 0))
+    mixed, moved_pool = lax.optimization_barrier((mixed, pages))
+    attn = combine([mixed], piece, wide)
+    attn = beside(lambda value: exchange(value, "wide"), attn, (5, 0))
     if direct:
         sums = in_vmem(
             functools.partial(finish_kernel, narrow),
@@ -630,15 +660,14 @@
             attn,
             w_out,
         )
-        sums = deal(sums, "narrow")
+        sums = beside(lambda value: deal(value, "narrow"), sums, (5, 1), (1, 1))
         attended = ((sums[0] + sums[1]) + (sums[2] + sums[3])).astype(jnp.bfloat16)
     else:
         attn = jnp.transpose(attn.reshape(-1, rows, HD), (1, 0, 2)).reshape(rows, -1)
         sums = jnp.dot(attn, w_out, preferred_element_type=jnp.float32)
         sums = sums.reshape(narrow, rows // narrow, -1)
-        sums = exchange(sums, "narrow")
+        sums = beside(lambda value: exchange(value, "narrow"), sums, (5, 1), (1, 1))
         attended = jnp.sum(sums, axis=0).astype(jnp.bfloat16)
-    attended = land(attended, (5, 1))
     moved_pool = placed(moved_pool)
     return (attended, new_entries, moved_pool, moved_req, moved_idx)
 

time: 166 us -> 163 us (0.982)
  blocking collectives: 0 us -> 36.8 us
  waiting for transfers between devices: 78.9 us -> 52.9 us
  starting transfers between devices: 47.8 us -> 39.3 us
  other arithmetic: 4.04 us -> 1.31 us
  local copies, waits for them, and re-layouts: 8.73 us -> 6.65 us
    all_to_all x0 -> x2, blocking collectives: none -> 36.8 us  [the longest x1 19.4 us: on_device(): received = beside(lambda value: exchange(value, 'wide'), packed, (6, 1))]
    ppermute x25, waiting for transfers between devices: 54.4 us -> 34 us  [send(): lax.ppermute(block, axis, [(i, i ^ d) for i in range(lax.axis_size(axis))])]
    all_to_all x3 -> x1, starting transfers between devices: 11.4 us -> 4.58 us  [on_device(): mixed = beside(lambda value: exchange(value, 'wide'), mixed, (4, 0))]
    all_to_all x3 -> x1, waiting for transfers between devices: 23.7 us -> 17.9 us  [on_device(): mixed = beside(lambda value: exchange(value, 'wide'), mixed, (4, 0))]
    unnamed x40 -> x42, local copies, waits for them, and re-layouts: 2.36 us -> 5.1 us
    select_n x2 -> x0, other arithmetic: 2.04 us -> none  [the longest x1 1.44 us: small_outputs(): jnp.where(step_ids < kept[:, None, None], fresh, jnp.zeros((), jnp.bfloat...]
    reshape x3 -> x0, local copies, waits for them, and re-layouts: 1.89 us -> none  [the longest x1 0.7 us: prepare(): req_tok = jnp.broadcast_to(page_req[:, None], (slots, PAGE)).reshape(1, -1)]
  transfers between devices with their start and end apart: 29 -> 27, of which waited for: 17 -> 17; matrix products, arithmetic and copies ran while one was open for 4% -> 0% of each run, Pallas kernels for 11% -> 11%
where the time goes in v9:
time: 163 us; the launch traced here: 162 us
  waiting for transfers between devices  52.9 us (32%)
  starting transfers between devices  39.3 us (24%)
  blocking collectives  36.8 us (23%)
  Pallas kernels  24.3 us (15%)
  local copies, waits for them, and re-layouts  6.65 us (4%)
    ppermute x25, waiting for transfers between devices, send(): lax.ppermute(block, axis, [(i, i ^ d) for i in range(lax.axis_size(axis))])  34 us
    ppermute x25, starting transfers between devices, send(): lax.ppermute(block, axis, [(i, i ^ d) for i in range(lax.axis_size(axis))])  27.4 us
    all_to_all x1, blocking collectives, on_device(): received = beside(lambda value: exchange(value, 'wide'), packed, (6, 1))  19.4 us
    all_to_all x1, waiting for transfers between devices, on_device(): mixed = beside(lambda value: exchange(value, 'wide'), mixed, (4, 0))  17.9 us
    all_to_all x1, blocking collectives, on_device(): attn = beside(lambda value: exchange(value, 'wide'), attn, (5, 0))  17.4 us
    pallas_call x1, Pallas kernels, attend(): pl.pallas_call(functools.partial(attend_kernel, rows, piece, peers), grid...  10.4 us
    all_to_all x1, starting transfers between devices, spread(): lax.all_to_all(jnp.broadcast_to(block[None], (count,) + block.shape), axi...  7.28 us
    pallas_call x1, Pallas kernels, order_pages(): pl.pallas_call(functools.partial(order_kernel, wide, parts), out_shape=ou...  5.7 us
  transfers between devices with their start and end apart: 27, of which 17 were waited for; matrix products, arithmetic and copies ran while one was open for 0% of the time, Pallas kernels for 11%

profile of v9, /device:TPU:0, one launch (start us, length us, event | category | flops | bytes accessed | tf_op | source)
XLA Modules:
  0.0 162.1 jit_solution(5458441861571988929)
XLA Ops:
  0.7 1.5 broadcast_in_dim.2
  2.1 7.3 %all-to-all-start = ((bf16[8,5,1024]{2,1,0:T(8,128)(2,1)}), bf16[8,5,1024]{2,1,0:T(8,128)(2,1)S(1)}, u32[]{:S(2)}, u32[]{:S(2)}) async-start(bf16[8,5,1024]{2,1,0:T(8,128)(2,1)} %broadcast_in_dim.2), calls=%async_computation | async-start | bytes 262144 | tf_op jit(solution)/shard_map/all_to_all | solution.py:484
  10.0 5.7 %shard_map.138 = (bf16[128,16,1024]{2,1,0:T(8,128)(2,1)}, f32[8,128]{1,0:T(8,128)}, f32[8,2048]{1,0:T(8,128)}, bf16[8,16,1024]{2,1,0:T(8,128)(2,1)}, bf16[8,16,1...) custom-call(s32[2]{0:T(128)} %pad_add_fusion.me_ref, ...), custom_call_target="tpu_custom_call" | custom-call | bytes 8388608 | tf_op jit(solution)/shard_map/pallas_call | solution.py:110
  15.7 1.0 all-to-all-done.hidden_ref
  16.8 1.0 shard_map.137
  17.8 2.0 %collective-permute-start.4 = (bf16[8,16,1024]{2,1,0:T(8,128)(2,1)}, bf16[8,16,1024]{2,1,0:T(8,128)(2,1)S(1)}, u32[]{:S(2)}, u32[]{:S(2)}) collective-permute-start(bf16[8,16,1024]{2,1,0:T(8,128)(2,1)} %get-tuple-element.122), channel_id=1, source_target_pairs={{0,12},{4,8},{8,4},{12,0},{16,28},{20,24},{24,20},{28,16},{1,13},{... | collective-permute-start | bytes 786440 | tf_op jit(solution)/shard_map/ppermute | solution.py:511
  19.8 2.4 %collective-permute-start.3 = (bf16[4,16,1024]{2,1,0:T(8,128)(2,1)}, bf16[4,16,1024]{2,1,0:T(8,128)(2,1)S(1)}, u32[]{:S(2)}, u32[]{:S(2)}) collective-permute-start(bf16[4,16,1024]{2,1,0:T(8,128)(2,1)} %get-tuple-element.121), channel_id=1, source_target_pairs={{0,24},{4,28},{8,16},{12,20},{16,8},{20,12},{24,0},{28,4},{1,25},{... | collective-permute-start | bytes 393224 | tf_op jit(solution)/shard_map/ppermute | solution.py:511
  22.1 1.5 collective-permute-start.1
  24.0 2.1 %collective-permute-done.1.refs_2_ = f32[40,256]{1,0:T(8,128)S(1)} collective-permute-done((f32[40,256]{1,0:T(8,128)S(1)}, f32[40,256]{1,0:T(8,128)S(1)}, u32[]{:S(2)}, u32[]{:S(2)}) %collective-permute-start.1) | collective-permute-done | bytes 40992 | tf_op jit(solution)/shard_map/ppermute | solution.py:511
  26.1 1.0 collective-permute-done.2.refs_3_
  27.2 3.4 %collective-permute-done.3.refs_4_ = bf16[4,16,1024]{2,1,0:T(8,128)(2,1)S(1)} collective-permute-done((bf16[4,16,1024]{2,1,0:T(8,128)(2,1)}, bf16[4,16,1024]{2,1,0:T(8,128)(2,1)S(1)}, u32[]{:S(2)}, u32[]{:S(2)}) %collective-permute-start.3) | collective-permute-done | bytes 131104 | tf_op jit(solution)/shard_map/ppermute | solution.py:511
  30.6 0.7 copy-done.14
  31.3 1.5 collective-permute-start.5
  32.8 19.4 %all_to_all.20.part_ref = bf16[8,48,256]{2,1,0:T(8,128)(2,1)S(1)} all-to-all(bf16[8,48,256]{2,1,0:T(8,128)(2,1)S(1)} %shard_map.139), channel_id=1, replica_groups=mesh['wide'=8,'narrow'=4] {'wide'}, dimensions={0} | all-to-all | bytes 393216 | tf_op jit(solution)/shard_map/all_to_all | solution.py:586
  52.3 1.4 shard_map.140
  53.6 0.7 copy-done
  54.3 1.2 collective-permute-start.10
  55.5 1.4 collective-permute-start.9
  56.9 1.2 collective-permute-start.7
  58.8 2.9 %collective-permute-done.8.refs_3_ = bf16[8,40,128]{2,1,0:T(8,128)(2,1)S(1)} collective-permute-done((bf16[8,40,128]{2,1,0:T(8,128)(2,1)S(1)}, bf16[8,40,128]{2,1,0:T(8,128)(2,1)S(1)}, u32[]{:S(2)}, u32[]{:S(2)}) %collective-permute-start.8) | collective-permute-done | bytes 81952 | tf_op jit(solution)/shard_map/ppermute | solution.py:511
  61.7 1.2 collective-permute-done.7.refs_2_
  63.7 2.4 %collective-permute-start.11 = (bf16[7,16,1024]{2,1,0:T(8,128)(2,1)}, bf16[7,16,1024]{2,1,0:T(8,128)(2,1)S(1)}, u32[]{:S(2)}, u32[]{:S(2)}) collective-permute-start(bf16[7,16,1024]{2,1,0:T(8,128)(2,1)} %get-tuple-element.154), channel_id=1, source_target_pairs={{0,28},{4,24},{8,20},{12,16},{16,12},{20,8},{24,4},{28,0},{1,29},{... | collective-permute-start | bytes 688136 | tf_op jit(solution)/shard_map/ppermute | solution.py:511
  66.1 10.4 %shard_map.141 = (bf16[8,64,128]{2,1,0:T(8,128)(2,1)}, bf16[8,64,128]{2,1,0:T(8,128)(2,1)}, bf16[8,64,128]{2,1,0:T(8,128)(2,1)}, bf16[8,64,128]{2,1,0:T(8,128)(2,1)}) custom-call(s32[2]{0:T(128)} %pad_add_fusion.me_ref, s32[8]{0:T(128)} %length_ref.1, bf16[8,40,128]{2,1,0:T(8,128)(2,1)} %copy-done.11, bf16[8,40,128]{2,1,0:T(8,128)(2,1)} %copy-done.18, ...), custom_call_target="tpu_custom_call" | custom-call | tf_op jit(solution)/shard_map/pallas_call | solution.py:292
  76.5 6.9 %collective-permute-done.11.refs_7_ = bf16[7,16,1024]{2,1,0:T(8,128)(2,1)S(1)} collective-permute-done((bf16[7,16,1024]{2,1,0:T(8,128)(2,1)}, bf16[7,16,1024]{2,1,0:T(8,128)(2,1)S(1)}, u32[]{:S(2)}, u32[]{:S(2)}) %collective-permute-start.11) | collective-permute-done | bytes 229408 | tf_op jit(solution)/shard_map/ppermute | solution.py:511
  83.5 2.1 %collective-permute-start.16 = (bf16[5,16,1024]{2,1,0:T(8,128)(2,1)S(1)}, bf16[5,16,1024]{2,1,0:T(8,128)(2,1)S(1)}, u32[]{:S(2)}, u32[]{:S(2)}) collective-permute-start(bf16[5,16,1024]{2,1,0:T(8,128)(2,1)S(1)} %copy-done.20), channel_id=1, source_target_pairs={{0,28},{4,24},{8,20},{12,16},{16,12},{20,8},{24,4},{28,0},{1,29},{... | collective-permute-start | bytes 491528 | tf_op jit(solution)/shard_map/ppermute | solution.py:511
  85.6 0.9 collective-permute-start.14
  86.4 1.0 collective-permute-start.15
  87.4 4.6 %collective-permute-done.14.refs_2_ = bf16[8,64,128]{2,1,0:T(8,128)(2,1)S(1)} collective-permute-done((bf16[8,64,128]{2,1,0:T(8,128)(2,1)}, bf16[8,64,128]{2,1,0:T(8,128)(2,1)S(1)}, u32[]{:S(2)}, u32[]{:S(2)}) %collective-permute-start.14) | collective-permute-done | bytes 131104 | tf_op jit(solution)/shard_map/ppermute | solution.py:511
  92.1 2.0 %collective-permute-done.15.refs_3_ = bf16[8,64,128]{2,1,0:T(8,128)(2,1)S(1)} collective-permute-done((bf16[8,64,128]{2,1,0:T(8,128)(2,1)}, bf16[8,64,128]{2,1,0:T(8,128)(2,1)S(1)}, u32[]{:S(2)}, u32[]{:S(2)}) %collective-permute-start.15) | collective-permute-done | bytes 131104 | tf_op jit(solution)/shard_map/ppermute | solution.py:511
  94.1 1.1 collective-permute-done.16.refs_8_
  95.8 0.9 copy-done.10
  96.7 1.1 shard_map.142
  98.5 4.6 %all-to-all-start.2 = ((bf16[8,64,128]{2,1,0:T(8,128)(2,1)}), bf16[8,64,128]{2,1,0:T(8,128)(2,1)S(1)}, u32[]{:S(2)}, u32[]{:S(2)}) async-start(bf16[8,64,128]{2,1,0:T(8,128)(2,1)} %shard_map.142), calls=%async_computation.2 | async-start | bytes 262144 | tf_op jit(solution)/shard_map/all_to_all | solution.py:651
  103.2 0.9 copy-done.5
  104.1 0.9 copy-done.7
  105.0 0.9 copy-done.9
  105.9 2.0 %shard_map.143.refs_4_ = bf16[128,16,1024]{2,1,0:T(8,128)(2,1)} custom-call(s32[9]{0:T(128)S(1)} %stack.66.place_ref, bf16[8,16,1024]{2,1,0:T(8,128)(2,1)S(1)} %collective-permute-done.10.refs_0_, bf16[16,16,1024]{2,1,0:T(8,128)(2,1)S(1)} %collective-permute-done.12.refs_1_, ...), custom_call_target="tpu_custom_call", output_to_operand_aliasing={{}: (10, {})} | custom-call | bytes 4718592 | tf_op jit(solution)/shard_map/pallas_call | solution.py:148
  107.9 17.9 %all-to-all-done.2.refs_0_ = bf16[8,64,128]{2,1,0:T(8,128)(2,1)S(1)} async-done(((bf16[8,64,128]{2,1,0:T(8,128)(2,1)}), bf16[8,64,128]{2,1,0:T(8,128)(2,1)S(1)}, u32[]{:S(2)}, u32[]{:S(2)}) %all-to-all-start.2) | async-done | bytes 131104 | tf_op jit(solution)/shard_map/all_to_all | solution.py:651
  126.1 1.9 %collective-permute-start.19 = (bf16[10,16,1024]{2,1,0:T(8,128)(2,1)}, bf16[10,16,1024]{2,1,0:T(8,128)(2,1)S(1)}, u32[]{:S(2)}, u32[]{:S(2)}) collective-permute-start(bf16[10,16,1024]{2,1,0:T(8,128)(2,1)} %get-tuple-element.191), channel_id=1, source_target_pairs={{0,20},{4,16},{8,28},{12,24},{16,4},{20,0},{24,12},{28,8},{1,21},{... | collective-permute-start | bytes 983048 | tf_op jit(solution)/shard_map/ppermute | solution.py:511
  128.0 17.4 %all_to_all.21.part_ref = bf16[8,40,128]{2,1,0:T(8,128)(2,1)S(1)} all-to-all(bf16[8,40,128]{2,1,0:T(8,128)(2,1)S(1)} %shard_map.144), channel_id=1, replica_groups=mesh['wide'=8,'narrow'=4] {'wide'}, dimensions={0} | all-to-all | bytes 163840 | tf_op jit(solution)/shard_map/all_to_all | solution.py:654
  145.4 0.9 shard_map.145
  146.3 1.4 collective-permute-start.24
  147.7 3.0 %collective-permute-start.23 = (bf16[6,16,1024]{2,1,0:T(8,128)(2,1)}, bf16[6,16,1024]{2,1,0:T(8,128)(2,1)S(1)}, u32[]{:S(2)}, u32[]{:S(2)}) collective-permute-start(bf16[6,16,1024]{2,1,0:T(8,128)(2,1)} %get-tuple-element.203), channel_id=1, source_target_pairs={{0,20},{4,16},{8,28},{12,24},{16,4},{20,0},{24,12},{28,8},{1,21},{... | collective-permute-start | bytes 589832 | tf_op jit(solution)/shard_map/ppermute | solution.py:511
  150.7 0.7 collective-permute-start.21
  151.4 1.2 collective-permute-start.22
  152.6 2.2 %collective-permute-done.21 = f32[10,512]{1,0:T(8,128)S(1)} collective-permute-done((f32[10,512]{1,0:T(8,128)S(1)}, f32[10,512]{1,0:T(8,128)S(1)}, u32[]{:S(2)}, u32[]{:S(2)}) %collective-permute-start.21) | collective-permute-done | bytes 20512 | tf_op jit(solution)/shard_map/ppermute | solution.py:511
  155.1 4.8 %collective-permute-done.23.refs_3_ = bf16[6,16,1024]{2,1,0:T(8,128)(2,1)S(1)} collective-permute-done((bf16[6,16,1024]{2,1,0:T(8,128)(2,1)}, bf16[6,16,1024]{2,1,0:T(8,128)(2,1)S(1)}, u32[]{:S(2)}, u32[]{:S(2)}) %collective-permute-start.23) | collective-permute-done | bytes 196640 | tf_op jit(solution)/shard_map/ppermute | solution.py:511
  160.5 1.6 shard_map.146
  (65 shorter events, 5.2 us)
Async XLA Ops:
  0.6 16.1 %copy-start.3 = (bf16[1024,128]{1,0:T(8,128)(2,1)S(1)}, bf16[1024,128]{1,0:T(8,128)(2,1)}, u32[]{:S(2)}) copy-start(bf16[1024,128]{1,0:T(8,128)(2,1)} %keyval_ref.1) | copy-start | bytes 786436
  0.6 16.1 %copy-start.1 = (bf16[1024,512]{1,0:T(8,128)(2,1)S(1)}, bf16[1024,512]{1,0:T(8,128)(2,1)}, u32[]{:S(2)}) copy-start(bf16[1024,512]{1,0:T(8,128)(2,1)} %query_ref.1) | copy-start | bytes 3145732
  0.7 51.6 %copy-start.15 = (s32[8]{0:T(128)S(1)}, s32[8]{0:T(128)}, u32[]{:S(2)}) copy-start(s32[8]{0:T(128)} %kept_ref.1) | copy-start | bytes 100
  2.1 14.6 %all-to-all-start = ((bf16[8,5,1024]{2,1,0:T(8,128)(2,1)}), bf16[8,5,1024]{2,1,0:T(8,128)(2,1)S(1)}, u32[]{:S(2)}, u32[]{:S(2)}) async-start(bf16[8,5,1024]{2,1,0:T(8,128)(2,1)} %broadcast_in_dim.2), calls=%async_computation | async-start | bytes 262144 | tf_op jit(solution)/shard_map/all_to_all | solution.py:484
  10.0 6.7 %copy-start.12 = (s32[2]{0:T(128)S(1)}, s32[2]{0:T(128)}, u32[]{:S(2)}) copy-start(s32[2]{0:T(128)} %pad_add_fusion.me_ref) | copy-start | bytes 28
  17.8 12.8 %collective-permute-start.4 = (bf16[8,16,1024]{2,1,0:T(8,128)(2,1)}, bf16[8,16,1024]{2,1,0:T(8,128)(2,1)S(1)}, u32[]{:S(2)}, u32[]{:S(2)}) collective-permute-start(bf16[8,16,1024]{2,1,0:T(8,128)(2,1)} %get-tuple-element.122), channel_id=1, source_target_pairs={{0,12},{4,8},{8,4},{12,0},{16,28},{20,24},{24,20},{28,16},{1,13},{... | collective-permute-start | bytes 786440 | tf_op jit(solution)/shard_map/ppermute | solution.py:511
  19.8 10.8 %collective-permute-start.3 = (bf16[4,16,1024]{2,1,0:T(8,128)(2,1)}, bf16[4,16,1024]{2,1,0:T(8,128)(2,1)S(1)}, u32[]{:S(2)}, u32[]{:S(2)}) collective-permute-start(bf16[4,16,1024]{2,1,0:T(8,128)(2,1)} %get-tuple-element.121), channel_id=1, source_target_pairs={{0,24},{4,28},{8,16},{12,20},{16,8},{20,12},{24,0},{28,4},{1,25},{... | collective-permute-start | bytes 393224 | tf_op jit(solution)/shard_map/ppermute | solution.py:511
  22.1 1.9 %collective-permute-start = (f32[40,256]{1,0:T(8,128)S(1)}, f32[40,256]{1,0:T(8,128)S(1)}, u32[]{:S(2)}, u32[]{:S(2)}) collective-permute-start(f32[40,256]{1,0:T(8,128)S(1)} %get-tuple-element.118), channel_id=1, source_target_pairs={{0,1},{1,0},{2,3},{3,2},{4,5},{5,4},{6,7},{7,6},{8,9},{9,8},{10,11... | collective-permute-start | bytes 122888 | tf_op jit(solution)/shard_map/ppermute | solution.py:511
  22.1 4.0 %collective-permute-start.1 = (f32[40,256]{1,0:T(8,128)S(1)}, f32[40,256]{1,0:T(8,128)S(1)}, u32[]{:S(2)}, u32[]{:S(2)}) collective-permute-start(f32[40,256]{1,0:T(8,128)S(1)} %get-tuple-element.119), channel_id=1, source_target_pairs={{0,2},{1,3},{2,0},{3,1},{4,6},{5,7},{6,4},{7,5},{8,10},{9,11},{10,... | collective-permute-start | bytes 122888 | tf_op jit(solution)/shard_map/ppermute | solution.py:511
  23.6 3.5 %collective-permute-start.2 = (f32[40,256]{1,0:T(8,128)S(1)}, f32[40,256]{1,0:T(8,128)S(1)}, u32[]{:S(2)}, u32[]{:S(2)}) collective-permute-start(f32[40,256]{1,0:T(8,128)S(1)} %get-tuple-element.120), channel_id=1, source_target_pairs={{0,3},{1,2},{2,1},{3,0},{4,7},{5,6},{6,5},{7,4},{8,11},{9,10},{10,... | collective-permute-start | bytes 122888 | tf_op jit(solution)/shard_map/ppermute | solution.py:511
  30.6 0.7 copy-start.14
  31.3 20.9 %collective-permute-start.5 = (bf16[12,16,1024]{2,1,0:T(8,128)(2,1)}, bf16[12,16,1024]{2,1,0:T(8,128)(2,1)S(1)}, u32[]{:S(2)}, u32[]{:S(2)}) collective-permute-start(bf16[12,16,1024]{2,1,0:T(8,128)(2,1)} %get-tuple-element.130), channel_id=1, source_target_pairs={{0,24},{4,28},{8,16},{12,20},{16,8},{20,12},{24,0},{28,4},{1,25},{... | collective-permute-start | bytes 1179656 | tf_op jit(solution)/shard_map/ppermute | solution.py:511
  53.6 0.7 copy-start
  54.3 11.8 %copy-start.11 = (bf16[8,40,128]{2,1,0:T(8,128)(2,1)}, bf16[8,40,128]{2,1,0:T(8,128)(2,1)S(1)}, u32[]{:S(2)}) copy-start(bf16[8,40,128]{2,1,0:T(8,128)(2,1)S(1)} %get-tuple-element.144.refs_0_) | copy-start | bytes 245764
  54.3 9.4 %collective-permute-start.10 = (bf16[8,16,1024]{2,1,0:T(8,128)(2,1)}, bf16[8,16,1024]{2,1,0:T(8,128)(2,1)S(1)}, u32[]{:S(2)}, u32[]{:S(2)}) collective-permute-start(bf16[8,16,1024]{2,1,0:T(8,128)(2,1)} %get-tuple-element.137), channel_id=1, source_target_pairs={{0,4},{4,0},{8,12},{12,8},{16,20},{20,16},{24,28},{28,24},{1,5},{5... | collective-permute-start | bytes 786440 | tf_op jit(solution)/shard_map/ppermute | solution.py:511
  55.5 8.0 %collective-permute-start.9 = (bf16[4,16,1024]{2,1,0:T(8,128)(2,1)}, bf16[4,16,1024]{2,1,0:T(8,128)(2,1)S(1)}, u32[]{:S(2)}, u32[]{:S(2)}) collective-permute-start(bf16[4,16,1024]{2,1,0:T(8,128)(2,1)} %get-tuple-element.136), channel_id=1, source_target_pairs={{0,28},{4,24},{8,20},{12,16},{16,12},{20,8},{24,4},{28,0},{1,29},{... | collective-permute-start | bytes 393224 | tf_op jit(solution)/shard_map/ppermute | solution.py:511
  56.9 4.7 %collective-permute-start.8 = (bf16[8,40,128]{2,1,0:T(8,128)(2,1)S(1)}, bf16[8,40,128]{2,1,0:T(8,128)(2,1)S(1)}, u32[]{:S(2)}, u32[]{:S(2)}) collective-permute-start(bf16[8,40,128]{2,1,0:T(8,128)(2,1)S(1)} %get-tuple-element.144.refs_0_), channel_id=1, source_target_pairs={{0,3},{1,2},{2,1},{3,0},{4,7},{5,6},{6,5},{7,4},{8,11},{9,10},{10,... | collective-permute-start | bytes 245768 | tf_op jit(solution)/shard_map/ppermute | solution.py:511
  56.9 6.0 %collective-permute-start.7 = (bf16[8,40,128]{2,1,0:T(8,128)(2,1)S(1)}, bf16[8,40,128]{2,1,0:T(8,128)(2,1)S(1)}, u32[]{:S(2)}, u32[]{:S(2)}) collective-permute-start(bf16[8,40,128]{2,1,0:T(8,128)(2,1)S(1)} %get-tuple-element.144.refs_0_), channel_id=1, source_target_pairs={{0,2},{1,3},{2,0},{3,1},{4,6},{5,7},{6,4},{7,5},{8,10},{9,11},{10,... | collective-permute-start | bytes 245768 | tf_op jit(solution)/shard_map/ppermute | solution.py:511
  58.2 4.7 %collective-permute-start.6 = (bf16[8,40,128]{2,1,0:T(8,128)(2,1)S(1)}, bf16[8,40,128]{2,1,0:T(8,128)(2,1)S(1)}, u32[]{:S(2)}, u32[]{:S(2)}) collective-permute-start(bf16[8,40,128]{2,1,0:T(8,128)(2,1)S(1)} %get-tuple-element.144.refs_0_), channel_id=1, source_target_pairs={{0,1},{1,0},{2,3},{3,2},{4,5},{5,4},{6,7},{7,6},{8,9},{9,8},{10,11... | collective-permute-start | bytes 245768 | tf_op jit(solution)/shard_map/ppermute | solution.py:511
  61.7 4.4 %copy-start.16 = (bf16[8,40,128]{2,1,0:T(8,128)(2,1)}, bf16[8,40,128]{2,1,0:T(8,128)(2,1)S(1)}, u32[]{:S(2)}) copy-start(bf16[8,40,128]{2,1,0:T(8,128)(2,1)S(1)} %collective-permute-done.8.refs_3_) | copy-start | bytes 245764
  62.9 3.2 %copy-start.17 = (bf16[8,40,128]{2,1,0:T(8,128)(2,1)}, bf16[8,40,128]{2,1,0:T(8,128)(2,1)S(1)}, u32[]{:S(2)}) copy-start(bf16[8,40,128]{2,1,0:T(8,128)(2,1)S(1)} %collective-permute-done.7.refs_2_) | copy-start | bytes 245764
  62.9 3.2 %copy-start.18 = (bf16[8,40,128]{2,1,0:T(8,128)(2,1)}, bf16[8,40,128]{2,1,0:T(8,128)(2,1)S(1)}, u32[]{:S(2)}) copy-start(bf16[8,40,128]{2,1,0:T(8,128)(2,1)S(1)} %collective-permute-done.6.refs_1_) | copy-start | bytes 245764
  63.5 13.0 %copy-start.8 = (bf16[4,16,1024]{2,1,0:T(8,128)(2,1)}, bf16[4,16,1024]{2,1,0:T(8,128)(2,1)S(1)}, u32[]{:S(2)}) copy-start(bf16[4,16,1024]{2,1,0:T(8,128)(2,1)S(1)} %collective-permute-done.9.refs_6_) | copy-start | bytes 393220
  63.7 19.7 %collective-permute-start.12 = (bf16[16,16,1024]{2,1,0:T(8,128)(2,1)}, bf16[16,16,1024]{2,1,0:T(8,128)(2,1)S(1)}, u32[]{:S(2)}, u32[]{:S(2)}) collective-permute-start(bf16[16,16,1024]{2,1,0:T(8,128)(2,1)} %get-tuple-element.155), channel_id=1, source_target_pairs={{0,8},{4,12},{8,0},{12,4},{16,24},{20,28},{24,16},{28,20},{1,9},{5... | collective-permute-start | bytes 1572872 | tf_op jit(solution)/shard_map/ppermute | solution.py:511
  63.7 19.7 %collective-permute-start.11 = (bf16[7,16,1024]{2,1,0:T(8,128)(2,1)}, bf16[7,16,1024]{2,1,0:T(8,128)(2,1)S(1)}, u32[]{:S(2)}, u32[]{:S(2)}) collective-permute-start(bf16[7,16,1024]{2,1,0:T(8,128)(2,1)} %get-tuple-element.154), channel_id=1, source_target_pairs={{0,28},{4,24},{8,20},{12,16},{16,12},{20,8},{24,4},{28,0},{1,29},{... | collective-permute-start | bytes 688136 | tf_op jit(solution)/shard_map/ppermute | solution.py:511
  66.1 17.3 %copy-start.19 = (bf16[8,16,1024]{2,1,0:T(8,128)(2,1)S(1)}, bf16[8,16,1024]{2,1,0:T(8,128)(2,1)}, u32[]{:S(2)}) copy-start(bf16[8,16,1024]{2,1,0:T(8,128)(2,1)} %get-tuple-element.167) | copy-start | bytes 786436
  66.1 17.4 %copy-start.20 = (bf16[5,16,1024]{2,1,0:T(8,128)(2,1)S(1)}, bf16[5,16,1024]{2,1,0:T(8,128)(2,1)}, u32[]{:S(2)}) copy-start(bf16[5,16,1024]{2,1,0:T(8,128)(2,1)} %get-tuple-element.166) | copy-start | bytes 491524
  83.4 14.4 %copy-start.4 = (bf16[7,16,1024]{2,1,0:T(8,128)(2,1)}, bf16[7,16,1024]{2,1,0:T(8,128)(2,1)S(1)}, u32[]{:S(2)}) copy-start(bf16[7,16,1024]{2,1,0:T(8,128)(2,1)S(1)} %collective-permute-done.11.refs_7_) | copy-start | bytes 688132
  83.4 12.4 %collective-permute-start.17 = (bf16[8,16,1024]{2,1,0:T(8,128)(2,1)S(1)}, bf16[8,16,1024]{2,1,0:T(8,128)(2,1)S(1)}, u32[]{:S(2)}, u32[]{:S(2)}) collective-permute-start(bf16[8,16,1024]{2,1,0:T(8,128)(2,1)S(1)} %copy-done.19), channel_id=1, source_target_pairs={{0,12},{4,8},{8,4},{12,0},{16,28},{20,24},{24,20},{28,16},{1,13},{... | collective-permute-start | bytes 786440 | tf_op jit(solution)/shard_map/ppermute | solution.py:511
  83.5 11.7 %collective-permute-start.16 = (bf16[5,16,1024]{2,1,0:T(8,128)(2,1)S(1)}, bf16[5,16,1024]{2,1,0:T(8,128)(2,1)S(1)}, u32[]{:S(2)}, u32[]{:S(2)}) collective-permute-start(bf16[5,16,1024]{2,1,0:T(8,128)(2,1)S(1)} %copy-done.20), channel_id=1, source_target_pairs={{0,28},{4,24},{8,20},{12,16},{16,12},{20,8},{24,4},{28,0},{1,29},{... | collective-permute-start | bytes 491528 | tf_op jit(solution)/shard_map/ppermute | solution.py:511
  85.6 1.9 %collective-permute-start.13 = (bf16[8,64,128]{2,1,0:T(8,128)(2,1)}, bf16[8,64,128]{2,1,0:T(8,128)(2,1)S(1)}, u32[]{:S(2)}, u32[]{:S(2)}) collective-permute-start(bf16[8,64,128]{2,1,0:T(8,128)(2,1)} %get-tuple-element.163), channel_id=1, source_target_pairs={{0,1},{1,0},{2,3},{3,2},{4,5},{5,4},{6,7},{7,6},{8,9},{9,8},{10,11... | collective-permute-start | bytes 393224 | tf_op jit(solution)/shard_map/ppermute | solution.py:511
  85.6 6.5 %collective-permute-start.14 = (bf16[8,64,128]{2,1,0:T(8,128)(2,1)}, bf16[8,64,128]{2,1,0:T(8,128)(2,1)S(1)}, u32[]{:S(2)}, u32[]{:S(2)}) collective-permute-start(bf16[8,64,128]{2,1,0:T(8,128)(2,1)} %get-tuple-element.164), channel_id=1, source_target_pairs={{0,2},{1,3},{2,0},{3,1},{4,6},{5,7},{6,4},{7,5},{8,10},{9,11},{10,... | collective-permute-start | bytes 393224 | tf_op jit(solution)/shard_map/ppermute | solution.py:511
  86.4 7.7 %collective-permute-start.15 = (bf16[8,64,128]{2,1,0:T(8,128)(2,1)}, bf16[8,64,128]{2,1,0:T(8,128)(2,1)S(1)}, u32[]{:S(2)}, u32[]{:S(2)}) collective-permute-start(bf16[8,64,128]{2,1,0:T(8,128)(2,1)} %get-tuple-element.165), channel_id=1, source_target_pairs={{0,3},{1,2},{2,1},{3,0},{4,7},{5,6},{6,5},{7,4},{8,11},{9,10},{10,... | collective-permute-start | bytes 393224 | tf_op jit(solution)/shard_map/ppermute | solution.py:511
  95.2 2.7 %copy-start.6 = (bf16[5,16,1024]{2,1,0:T(8,128)(2,1)}, bf16[5,16,1024]{2,1,0:T(8,128)(2,1)S(1)}, u32[]{:S(2)}) copy-start(bf16[5,16,1024]{2,1,0:T(8,128)(2,1)S(1)} %collective-permute-done.16.refs_8_) | copy-start | bytes 491524
  95.8 0.9 copy-start.10
  97.8 28.0 %collective-permute-start.18 = (bf16[16,16,1024]{2,1,0:T(8,128)(2,1)}, bf16[16,16,1024]{2,1,0:T(8,128)(2,1)S(1)}, u32[]{:S(2)}, u32[]{:S(2)}) collective-permute-start(bf16[16,16,1024]{2,1,0:T(8,128)(2,1)} %get-tuple-element.176), channel_id=1, source_target_pairs={{0,16},{4,20},{8,24},{12,28},{16,0},{20,4},{24,8},{28,12},{1,17},{... | collective-permute-start | bytes 1572872 | tf_op jit(solution)/shard_map/ppermute | solution.py:511
  98.5 27.3 %all-to-all-start.2 = ((bf16[8,64,128]{2,1,0:T(8,128)(2,1)}), bf16[8,64,128]{2,1,0:T(8,128)(2,1)S(1)}, u32[]{:S(2)}, u32[]{:S(2)}) async-start(bf16[8,64,128]{2,1,0:T(8,128)(2,1)} %shard_map.142), calls=%async_computation.2 | async-start | bytes 262144 | tf_op jit(solution)/shard_map/all_to_all | solution.py:651
  103.2 0.9 copy-start.5
  104.1 0.9 copy-start.7
  105.0 0.9 copy-start.9
  105.9 39.4 %copy-start.2 = (bf16[1024,512]{1,0:T(8,128)(2,1)S(1)}, bf16[1024,512]{1,0:T(8,128)(2,1)}, u32[]{:S(2)}) copy-start(bf16[1024,512]{1,0:T(8,128)(2,1)} %weight_ref.1) | copy-start | bytes 3145732
  105.9 39.4 %copy-start.13 = (s32[2]{0:T(128)S(1)}, s32[2]{0:T(128)}, u32[]{:S(2)}) copy-start(s32[2]{0:T(128)} %pad_add_fusion.me_ref) | copy-start | bytes 28
  126.1 19.3 %collective-permute-start.19 = (bf16[10,16,1024]{2,1,0:T(8,128)(2,1)}, bf16[10,16,1024]{2,1,0:T(8,128)(2,1)S(1)}, u32[]{:S(2)}, u32[]{:S(2)}) collective-permute-start(bf16[10,16,1024]{2,1,0:T(8,128)(2,1)} %get-tuple-element.191), channel_id=1, source_target_pairs={{0,20},{4,16},{8,28},{12,24},{16,4},{20,0},{24,12},{28,8},{1,21},{... | collective-permute-start | bytes 983048 | tf_op jit(solution)/shard_map/ppermute | solution.py:511
  146.3 13.6 %collective-permute-start.24 = (bf16[8,16,1024]{2,1,0:T(8,128)(2,1)}, bf16[8,16,1024]{2,1,0:T(8,128)(2,1)S(1)}, u32[]{:S(2)}, u32[]{:S(2)}) collective-permute-start(bf16[8,16,1024]{2,1,0:T(8,128)(2,1)} %get-tuple-element.204), channel_id=1, source_target_pairs={{0,4},{4,0},{8,12},{12,8},{16,20},{20,16},{24,28},{28,24},{1,5},{5... | collective-permute-start | bytes 786440 | tf_op jit(solution)/shard_map/ppermute | solution.py:511
  147.7 12.1 %collective-permute-start.23 = (bf16[6,16,1024]{2,1,0:T(8,128)(2,1)}, bf16[6,16,1024]{2,1,0:T(8,128)(2,1)S(1)}, u32[]{:S(2)}, u32[]{:S(2)}) collective-permute-start(bf16[6,16,1024]{2,1,0:T(8,128)(2,1)} %get-tuple-element.203), channel_id=1, source_target_pairs={{0,20},{4,16},{8,28},{12,24},{16,4},{20,0},{24,12},{28,8},{1,21},{... | collective-permute-start | bytes 589832 | tf_op jit(solution)/shard_map/ppermute | solution.py:511
  150.7 1.9 %collective-permute-start.20 = (f32[10,512]{1,0:T(8,128)S(1)}, f32[10,512]{1,0:T(8,128)S(1)}, u32[]{:S(2)}, u32[]{:S(2)}) collective-permute-start(f32[10,512]{1,0:T(8,128)S(1)} %get-tuple-element.200), channel_id=1, source_target_pairs={{0,1},{1,0},{2,3},{3,2},{4,5},{5,4},{6,7},{7,6},{8,9},{9,8},{10,11... | collective-permute-start | bytes 61448 | tf_op jit(solution)/shard_map/ppermute | solution.py:511
  150.7 4.1 %collective-permute-start.21 = (f32[10,512]{1,0:T(8,128)S(1)}, f32[10,512]{1,0:T(8,128)S(1)}, u32[]{:S(2)}, u32[]{:S(2)}) collective-permute-start(f32[10,512]{1,0:T(8,128)S(1)} %get-tuple-element.201), channel_id=1, source_target_pairs={{0,2},{1,3},{2,0},{3,1},{4,6},{5,7},{6,4},{7,5},{8,10},{9,11},{10,... | collective-permute-start | bytes 61448 | tf_op jit(solution)/shard_map/ppermute | solution.py:511
  151.4 3.7 %collective-permute-start.22 = (f32[10,512]{1,0:T(8,128)S(1)}, f32[10,512]{1,0:T(8,128)S(1)}, u32[]{:S(2)}, u32[]{:S(2)}) collective-permute-start(f32[10,512]{1,0:T(8,128)S(1)} %get-tuple-element.202), channel_id=1, source_target_pairs={{0,3},{1,2},{2,1},{3,0},{4,7},{5,6},{6,5},{7,4},{8,11},{9,10},{10,... | collective-permute-start | bytes 61448 | tf_op jit(solution)/shard_map/ppermute | solution.py:511

commit v10 on v9

--- a/solution.py
+++ b/solution.py
@@ -18,7 +18,7 @@
 SCALE2 = math.log2(math.e) / math.sqrt(HD)
 STAT = 16
 MIB = 1024 * 1024
-CUTS = {1: (0, 8, 16), 2: (0, 16), 3: (0, 8, 16), 4: (0, 16), 5: (0, 10, 16), 6: (0, 4, 16), 7: (0, 4, 11, 16)}
+CUTS = {1: (0, 8, 16), 2: (0, 7, 16), 3: (0, 5, 16), 4: (0, 13, 16), 5: (0, 10, 16), 6: (0, 4, 16), 7: (0, 4, 11, 16)}
 NT = (((1,), (1,)), ((), ()))
 
 
@@ -575,7 +575,7 @@
             w_keyval,
             scratch=[pltpu.VMEM((rows, narrow * HD), jnp.float32)],
         )
-        partial = beside(lambda value: deal(value, "narrow"), partial, (6, 0), (3, 0))
+        partial = beside(lambda value: deal(value, "narrow"), partial, (6, 0), (1, 0))
         packed = in_vmem(
             functools.partial(pack_kernel, narrow),
             jax.ShapeDtypeStruct((wide, rows + wide, 2 * HD), jnp.bfloat16),
@@ -597,7 +597,7 @@
             received,
         )
         moved_req, moved_idx = moved_req.reshape(slots), moved_idx.reshape(slots)
-        queries = beside(lambda value: share(value, "narrow"), queries, (7, 0), (1, 0))
+        queries = beside(lambda value: share(value, "narrow"), queries, (7, 0), (1, 1))
     else:
         gathered = gathered.reshape(rows, -1)
         query_part = jnp.dot(gathered, w_query, preferred_element_type=jnp.float32)
@@ -606,7 +606,7 @@
         partial = jnp.concatenate(
             [query_part, jnp.broadcast_to(keyval_part[None], (narrow,) + keyval_part.shape)], axis=2
         )
-        partial = beside(lambda value: exchange(value, "narrow"), partial, (6, 0), (3, 0))
+        partial = beside(lambda value: exchange(value, "narrow"), partial, (6, 0), (1, 0))
         projected = jnp.sum(partial, axis=0).astype(jnp.bfloat16)
         tags = tags[:, : 3 * capacity].astype(jnp.bfloat16)[:, None]
         tags = jnp.pad(tags, ((0, 0), (0, 7), (0, projected.shape[1] - tags.shape[2])))
@@ -615,7 +615,7 @@
         received = beside(lambda value: exchange(value, "wide"), packed, (6, 1))
         tags_in = received[:, rows]
         queries = received[:, :rows, :own_cols]
-        queries = beside(lambda value: spread(value, "narrow"), queries, (7, 0), (1, 0))
+        queries = beside(lambda value: spread(value, "narrow"), queries, (7, 0), (1, 1))
         queries = jnp.transpose(queries, (2, 1, 0, 3)).reshape(rows, HEADS, HD)
         queries = [jnp.transpose(queries, (1, 0, 2)).reshape(KVH, GROUPS * rows, HD)]
         keyval = jnp.transpose(received[:, :rows, own_cols:], (1, 0, 2)).reshape(rows, -1)
@@ -640,18 +640,18 @@
         (2, 0),
     )
     if direct:
-        mixed = beside(lambda value: deal(value, "narrow"), mixed, (7, 2), (3, 1))
+        mixed = beside(lambda value: deal(value, "narrow"), mixed, (7, 2), (3, 0))
     else:
-        mixed = beside(lambda value: exchange(value, "narrow"), mixed[0], (7, 2), (3, 1))
+        mixed = beside(lambda value: exchange(value, "narrow"), mixed[0], (7, 2), (3, 0))
         mixed = mixed.reshape((narrow, wide) + mixed.shape[1:])
         mixed = [mixed[i] for i in range(narrow)]
     mixed = combine(mixed, piece)
     mixed, pages = lax.optimization_barrier((mixed, moved_pool))
     pages = placed(pages)
-    mixed = beside(lambda value: exchange(value, "wide"), mixed, (4, 0))
+    mixed = beside(lambda value: exchange(value, "wide"), mixed, (4, 0), (2, 1))
     mixed, moved_pool = lax.optimization_barrier((mixed, pages))
     attn = combine([mixed], piece, wide)
-    attn = beside(lambda value: exchange(value, "wide"), attn, (5, 0))
+    attn = beside(lambda value: exchange(value, "wide"), attn, (5, 0), (4, 1), (3, 1))
     if direct:
         sums = in_vmem(
             functools.partial(finish_kernel, narrow),
@@ -660,13 +660,13 @@
             attn,
             w_out,
         )
-        sums = beside(lambda value: deal(value, "narrow"), sums, (5, 1), (1, 1))
+        sums = beside(lambda value: deal(value, "narrow"), sums, (5, 1))
         attended = ((sums[0] + sums[1]) + (sums[2] + sums[3])).astype(jnp.bfloat16)
     else:
         attn = jnp.transpose(attn.reshape(-1, rows, HD), (1, 0, 2)).reshape(rows, -1)
         sums = jnp.dot(attn, w_out, preferred_element_type=jnp.float32)
         sums = sums.reshape(narrow, rows // narrow, -1)
-        sums = beside(lambda value: exchange(value, "narrow"), sums, (5, 1), (1, 1))
+        sums = beside(lambda value: exchange(value, "narrow"), sums, (5, 1))
         attended = jnp.sum(sums, axis=0).astype(jnp.bfloat16)
     moved_pool = placed(moved_pool)
     return (attended, new_entries, moved_pool, moved_req, moved_idx)

time: 163 us -> 156 us (0.957)
  blocking collectives: 36.8 us -> 21.4 us
  starting transfers between devices: 39.3 us -> 44.9 us
    all_to_all x1 -> x0, blocking collectives: 17.4 us -> none  [on_device(): attn = beside(lambda value: exchange(value, 'wide'), attn, (5, 0))]
    ppermute x25 -> x27, waiting for transfers between devices: 34 us -> 39.7 us  [send(): lax.ppermute(block, axis, [(i, i ^ d) for i in range(lax.axis_size(axis))])]
    all_to_all x1 -> x2, waiting for transfers between devices: 17.9 us -> 13.8 us  [the longest x1 13.8 us: on_device(): mixed = beside(lambda value: exchange(value, 'wide'), mixed, (4, 0), (2, 1))]
    all_to_all x1 -> x2, starting transfers between devices: 4.58 us -> 7.58 us  [the longest x1 3.82 us: on_device(): mixed = beside(lambda value: exchange(value, 'wide'), mixed, (4, 0), (2, 1))]
    ppermute x25 -> x27, starting transfers between devices: 27.4 us -> 30 us  [send(): lax.ppermute(block, axis, [(i, i ^ d) for i in range(lax.axis_size(axis))])]
    all_to_all x1, blocking collectives: 19.4 us -> 21.4 us  [on_device(): received = beside(lambda value: exchange(value, 'wide'), packed, (6, 1))]
    unnamed x42 -> x44, local copies, waits for them, and re-layouts: 5.1 us -> 5.72 us
  transfers between devices with their start and end apart: 27 -> 30, of which waited for: 17 -> 16; matrix products, arithmetic and copies ran while one was open for 0% -> 0% of each run, Pallas kernels for 11% -> 12%
where the time goes in v10:
time: 156 us; the launch traced here: 155 us
  waiting for transfers between devices  54.5 us (35%)
  starting transfers between devices  44.9 us (29%)
  Pallas kernels  25 us (16%)
  blocking collectives  21.4 us (14%)
  local copies, waits for them, and re-layouts  7.36 us (5%)
    ppermute x27, waiting for transfers between devices, send(): lax.ppermute(block, axis, [(i, i ^ d) for i in range(lax.axis_size(axis))])  39.7 us
    ppermute x27, starting transfers between devices, send(): lax.ppermute(block, axis, [(i, i ^ d) for i in range(lax.axis_size(axis))])  30 us
    all_to_all x1, blocking collectives, on_device(): received = beside(lambda value: exchange(value, 'wide'), packed, (6, 1))  21.4 us
    all_to_all x1, waiting for transfers between devices, on_device(): mixed = beside(lambda value: exchange(value, 'wide'), mixed, (4, 0), (2, 1))  13.8 us
    pallas_call x1, Pallas kernels, attend(): pl.pallas_call(functools.partial(attend_kernel, rows, piece, peers), grid...  10.3 us
    all_to_all x1, starting transfers between devices, spread(): lax.all_to_all(jnp.broadcast_to(block[None], (count,) + block.shape), axi...  7.28 us
    pallas_call x1, Pallas kernels, order_pages(): pl.pallas_call(functools.partial(order_kernel, wide, parts), out_shape=ou...  5.73 us
    unnamed x44, local copies, waits for them, and re-layouts  5.72 us
  transfers between devices with their start and end apart: 30, of which 16 were waited for; matrix products, arithmetic and copies ran while one was open for 0% of the time, Pallas kernels for 12%

profile of v10, /device:TPU:0, one launch (start us, length us, event | category | flops | bytes accessed | tf_op | source)
XLA Modules:
  0.0 155.1 jit_solution(5673295112817593474)
XLA Ops:
  0.7 1.5 broadcast_in_dim.2
  2.1 7.3 %all-to-all-start = ((bf16[8,5,1024]{2,1,0:T(8,128)(2,1)}), bf16[8,5,1024]{2,1,0:T(8,128)(2,1)S(1)}, u32[]{:S(2)}, u32[]{:S(2)}) async-start(bf16[8,5,1024]{2,1,0:T(8,128)(2,1)} %broadcast_in_dim.2), calls=%async_computation | async-start | bytes 262144 | tf_op jit(solution)/shard_map/all_to_all | solution.py:484
  10.0 5.7 %shard_map.138 = (bf16[128,16,1024]{2,1,0:T(8,128)(2,1)}, f32[8,128]{1,0:T(8,128)}, f32[8,2048]{1,0:T(8,128)}, bf16[8,16,1024]{2,1,0:T(8,128)(2,1)}, bf16[8,16,1...) custom-call(s32[2]{0:T(128)} %pad_add_fusion.me_ref, ...), custom_call_target="tpu_custom_call" | custom-call | bytes 8388608 | tf_op jit(solution)/shard_map/pallas_call | solution.py:110
  15.7 1.0 all-to-all-done.hidden_ref
  16.8 1.0 shard_map.137
  17.8 1.1 collective-permute-start.4
  18.8 3.3 %collective-permute-start.3 = (bf16[4,16,1024]{2,1,0:T(8,128)(2,1)}, bf16[4,16,1024]{2,1,0:T(8,128)(2,1)S(1)}, u32[]{:S(2)}, u32[]{:S(2)}) collective-permute-start(bf16[4,16,1024]{2,1,0:T(8,128)(2,1)} %get-tuple-element.127), channel_id=1, source_target_pairs={{0,24},{4,28},{8,16},{12,20},{16,8},{20,12},{24,0},{28,4},{1,25},{... | collective-permute-start | bytes 393224 | tf_op jit(solution)/shard_map/ppermute | solution.py:511
  22.1 1.5 collective-permute-start.1
  24.0 2.1 %collective-permute-done.1.refs_2_ = f32[40,256]{1,0:T(8,128)S(1)} collective-permute-done((f32[40,256]{1,0:T(8,128)S(1)}, f32[40,256]{1,0:T(8,128)S(1)}, u32[]{:S(2)}, u32[]{:S(2)}) %collective-permute-start.1) | collective-permute-done | bytes 40992 | tf_op jit(solution)/shard_map/ppermute | solution.py:511
  26.1 1.0 collective-permute-done.2.refs_3_
  28.5 2.1 %collective-permute-start.5 = (bf16[12,16,1024]{2,1,0:T(8,128)(2,1)}, bf16[12,16,1024]{2,1,0:T(8,128)(2,1)S(1)}, u32[]{:S(2)}, u32[]{:S(2)}) collective-permute-start(bf16[12,16,1024]{2,1,0:T(8,128)(2,1)} %get-tuple-element.136), channel_id=1, source_target_pairs={{0,24},{4,28},{8,16},{12,20},{16,8},{20,12},{24,0},{28,4},{1,25},{... | collective-permute-start | bytes 1179656 | tf_op jit(solution)/shard_map/ppermute | solution.py:511
  30.6 21.4 %all_to_all.20.part_ref = bf16[8,48,256]{2,1,0:T(8,128)(2,1)S(1)} all-to-all(bf16[8,48,256]{2,1,0:T(8,128)(2,1)S(1)} %shard_map.139), channel_id=1, replica_groups=mesh['wide'=8,'narrow'=4] {'wide'}, dimensions={0} | all-to-all | bytes 393216 | tf_op jit(solution)/shard_map/all_to_all | solution.py:586
  52.0 1.4 shard_map.140
  54.0 1.2 collective-permute-start.10
  55.2 1.7 %collective-permute-start.9 = (bf16[4,16,1024]{2,1,0:T(8,128)(2,1)}, bf16[4,16,1024]{2,1,0:T(8,128)(2,1)S(1)}, u32[]{:S(2)}, u32[]{:S(2)}) collective-permute-start(bf16[4,16,1024]{2,1,0:T(8,128)(2,1)} %get-tuple-element.142), channel_id=1, source_target_pairs={{0,28},{4,24},{8,20},{12,16},{16,12},{20,8},{24,4},{28,0},{1,29},{... | collective-permute-start | bytes 393224 | tf_op jit(solution)/shard_map/ppermute | solution.py:511
  57.0 1.0 collective-permute-start.7
  58.0 0.8 collective-permute-start.6
  58.8 2.8 %collective-permute-done.8.refs_3_ = bf16[8,40,128]{2,1,0:T(8,128)(2,1)S(1)} collective-permute-done((bf16[8,40,128]{2,1,0:T(8,128)(2,1)S(1)}, bf16[8,40,128]{2,1,0:T(8,128)(2,1)S(1)}, u32[]{:S(2)}, u32[]{:S(2)}) %collective-permute-start.8) | collective-permute-done | bytes 81952 | tf_op jit(solution)/shard_map/ppermute | solution.py:511
  61.6 1.0 collective-permute-done.7.refs_2_
  63.6 2.2 %collective-permute-start.11 = (bf16[7,16,1024]{2,1,0:T(8,128)(2,1)}, bf16[7,16,1024]{2,1,0:T(8,128)(2,1)S(1)}, u32[]{:S(2)}, u32[]{:S(2)}) collective-permute-start(bf16[7,16,1024]{2,1,0:T(8,128)(2,1)} %get-tuple-element.160), channel_id=1, source_target_pairs={{0,28},{4,24},{8,20},{12,16},{16,12},{20,8},{24,4},{28,0},{1,29},{... | collective-permute-start | bytes 688136 | tf_op jit(solution)/shard_map/ppermute | solution.py:511
  65.8 10.3 %shard_map.141 = (bf16[8,64,128]{2,1,0:T(8,128)(2,1)}, bf16[8,64,128]{2,1,0:T(8,128)(2,1)}, bf16[8,64,128]{2,1,0:T(8,128)(2,1)}, bf16[8,64,128]{2,1,0:T(8,128)(2,1)}) custom-call(s32[2]{0:T(128)} %pad_add_fusion.me_ref, s32[8]{0:T(128)} %length_ref.1, bf16[8,40,128]{2,1,0:T(8,128)(2,1)} %copy-done.11, bf16[8,40,128]{2,1,0:T(8,128)(2,1)} %copy-done.18, ...), custom_call_target="tpu_custom_call" | custom-call | tf_op jit(solution)/shard_map/pallas_call | solution.py:292
  76.2 2.1 %collective-permute-done.12.refs_2_ = bf16[7,16,1024]{2,1,0:T(8,128)(2,1)S(1)} collective-permute-done((bf16[7,16,1024]{2,1,0:T(8,128)(2,1)}, bf16[7,16,1024]{2,1,0:T(8,128)(2,1)S(1)}, u32[]{:S(2)}, u32[]{:S(2)}) %collective-permute-start.12) | collective-permute-done | bytes 229408 | tf_op jit(solution)/shard_map/ppermute | solution.py:511
  78.3 2.0 %collective-permute-start.16 = (bf16[5,16,1024]{2,1,0:T(8,128)(2,1)S(1)}, bf16[5,16,1024]{2,1,0:T(8,128)(2,1)S(1)}, u32[]{:S(2)}, u32[]{:S(2)}) collective-permute-start(bf16[5,16,1024]{2,1,0:T(8,128)(2,1)S(1)} %copy-done.20), channel_id=1, source_target_pairs={{0,28},{4,24},{8,20},{12,16},{16,12},{20,8},{24,4},{28,0},{1,29},{... | collective-permute-start | bytes 491528 | tf_op jit(solution)/shard_map/ppermute | solution.py:511
  80.4 1.0 collective-permute-start.14
  81.4 0.8 collective-permute-start.15
  82.3 4.6 %collective-permute-done.14.refs_2_ = bf16[8,64,128]{2,1,0:T(8,128)(2,1)S(1)} collective-permute-done((bf16[8,64,128]{2,1,0:T(8,128)(2,1)}, bf16[8,64,128]{2,1,0:T(8,128)(2,1)S(1)}, u32[]{:S(2)}, u32[]{:S(2)}) %collective-permute-start.14) | collective-permute-done | bytes 131104 | tf_op jit(solution)/shard_map/ppermute | solution.py:511
  86.9 2.0 %collective-permute-done.15.refs_3_ = bf16[8,64,128]{2,1,0:T(8,128)(2,1)S(1)} collective-permute-done((bf16[8,64,128]{2,1,0:T(8,128)(2,1)}, bf16[8,64,128]{2,1,0:T(8,128)(2,1)S(1)}, u32[]{:S(2)}, u32[]{:S(2)}) %collective-permute-start.15) | collective-permute-done | bytes 131104 | tf_op jit(solution)/shard_map/ppermute | solution.py:511
  89.0 1.1 collective-permute-done.17.refs_3_
  90.1 0.9 copy-done.6
  91.0 1.1 shard_map.142
  92.1 2.0 %collective-permute-start.18 = (bf16[13,16,1024]{2,1,0:T(8,128)(2,1)}, bf16[13,16,1024]{2,1,0:T(8,128)(2,1)S(1)}, u32[]{:S(2)}, u32[]{:S(2)}) collective-permute-start(bf16[13,16,1024]{2,1,0:T(8,128)(2,1)} %get-tuple-element.183), channel_id=1, source_target_pairs={{0,16},{4,20},{8,24},{12,28},{16,0},{20,4},{24,8},{28,12},{1,17},{... | collective-permute-start | bytes 1277960 | tf_op jit(solution)/shard_map/ppermute | solution.py:511
  94.6 3.8 %all-to-all-start.2 = ((bf16[8,64,128]{2,1,0:T(8,128)(2,1)}), bf16[8,64,128]{2,1,0:T(8,128)(2,1)S(1)}, u32[]{:S(2)}, u32[]{:S(2)}) async-start(bf16[8,64,128]{2,1,0:T(8,128)(2,1)} %shard_map.142), calls=%async_computation.2 | async-start | bytes 262144 | tf_op jit(solution)/shard_map/all_to_all | solution.py:651
  98.5 0.9 copy-done.5
  99.4 0.9 copy-done.8
  100.3 0.9 copy-done.10
  101.2 1.9 %shard_map.143.refs_6_ = bf16[128,16,1024]{2,1,0:T(8,128)(2,1)} custom-call(s32[9]{0:T(128)S(1)} %stack.72.place_ref, bf16[8,16,1024]{2,1,0:T(8,128)(2,1)S(1)} %collective-permute-done.4.refs_0_, bf16[8,16,1024]{2,1,0:T(8,128)(2,1)S(1)} %collective-permute-done.10.refs_1_, ...), custom_call_target="tpu_custom_call", output_to_operand_aliasing={{}: (10, {})} | custom-call | bytes 4718592 | tf_op jit(solution)/shard_map/pallas_call | solution.py:148
  103.1 13.8 %all-to-all-done.2.refs_0_ = bf16[8,64,128]{2,1,0:T(8,128)(2,1)S(1)} async-done(((bf16[8,64,128]{2,1,0:T(8,128)(2,1)}), bf16[8,64,128]{2,1,0:T(8,128)(2,1)S(1)}, u32[]{:S(2)}, u32[]{:S(2)}) %all-to-all-start.2) | async-done | bytes 131104 | tf_op jit(solution)/shard_map/all_to_all | solution.py:651
  116.9 0.9 shard_map.144
  117.9 0.7 collective-permute-start.22
  118.6 2.6 %collective-permute-start.20 = (bf16[10,16,1024]{2,1,0:T(8,128)(2,1)}, bf16[10,16,1024]{2,1,0:T(8,128)(2,1)S(1)}, u32[]{:S(2)}, u32[]{:S(2)}) collective-permute-start(bf16[10,16,1024]{2,1,0:T(8,128)(2,1)} %get-tuple-element.201), channel_id=1, source_target_pairs={{0,20},{4,16},{8,28},{12,24},{16,4},{20,0},{24,12},{28,8},{1,21},{... | collective-permute-start | bytes 983048 | tf_op jit(solution)/shard_map/ppermute | solution.py:511
  121.2 3.8 %all-to-all-start.3 = ((bf16[8,40,128]{2,1,0:T(8,128)(2,1)}), bf16[8,40,128]{2,1,0:T(8,128)(2,1)S(1)}, u32[]{:S(2)}, u32[]{:S(2)}) async-start(bf16[8,40,128]{2,1,0:T(8,128)(2,1)} %shard_map.144), calls=%async_computation.3 | async-start | bytes 163840 | tf_op jit(solution)/shard_map/all_to_all | solution.py:654
  124.9 2.9 %collective-permute-start.21 = (bf16[3,16,1024]{2,1,0:T(8,128)(2,1)S(1)}, bf16[3,16,1024]{2,1,0:T(8,128)(2,1)S(1)}, u32[]{:S(2)}, u32[]{:S(2)}) collective-permute-start(bf16[3,16,1024]{2,1,0:T(8,128)(2,1)S(1)} %copy-done.21), channel_id=1, source_target_pairs={{0,16},{4,20},{8,24},{12,28},{16,0},{20,4},{24,8},{28,12},{1,17},{... | collective-permute-start | bytes 294920 | tf_op jit(solution)/shard_map/ppermute | solution.py:511
  127.9 14.1 %collective-permute-done.21.refs_3_ = bf16[3,16,1024]{2,1,0:T(8,128)(2,1)S(1)} collective-permute-done((bf16[3,16,1024]{2,1,0:T(8,128)(2,1)S(1)}, bf16[3,16,1024]{2,1,0:T(8,128)(2,1)S(1)}, u32[]{:S(2)}, u32[]{:S(2)}) %collective-permute-start.21) | collective-permute-done | bytes 98336 | tf_op jit(solution)/shard_map/ppermute | solution.py:511
  142.0 0.9 shard_map.145
  143.1 1.1 collective-permute-start.24
  145.0 2.0 %collective-permute-done.24 = f32[10,512]{1,0:T(8,128)S(1)} collective-permute-done((f32[10,512]{1,0:T(8,128)S(1)}, f32[10,512]{1,0:T(8,128)S(1)}, u32[]{:S(2)}, u32[]{:S(2)}) %collective-permute-start.24) | collective-permute-done | bytes 20512 | tf_op jit(solution)/shard_map/ppermute | solution.py:511
  147.6 5.2 %collective-permute-done.26.refs_5_ = bf16[6,16,1024]{2,1,0:T(8,128)(2,1)S(1)} collective-permute-done((bf16[6,16,1024]{2,1,0:T(8,128)(2,1)}, bf16[6,16,1024]{2,1,0:T(8,128)(2,1)S(1)}, u32[]{:S(2)}, u32[]{:S(2)}) %collective-permute-start.26) | collective-permute-done | bytes 196640 | tf_op jit(solution)/shard_map/ppermute | solution.py:511
  153.4 1.8 %shard_map.146 = bf16[128,16,1024]{2,1,0:T(8,128)(2,1)} custom-call(s32[6]{0:T(128)S(1)} %stack.79.place_ref, bf16[9,16,1024]{2,1,0:T(8,128)(2,1)S(1)} %collective-permute-done.19.refs_0_, bf16[11,16,1024]{2,1,0:T(8,128)(2,1)S(1)} %collective-permute-done.22.refs_1_, ...), custom_call_target="tpu_custom_call", output_to_operand_aliasing={{}: (7, {})} | custom-call | bytes 3538944 | tf_op jit(solution)/shard_map/pallas_call | solution.py:148
  (72 shorter events, 6.8 us)
Async XLA Ops:
  0.6 16.1 %copy-start.3 = (bf16[1024,128]{1,0:T(8,128)(2,1)S(1)}, bf16[1024,128]{1,0:T(8,128)(2,1)}, u32[]{:S(2)}) copy-start(bf16[1024,128]{1,0:T(8,128)(2,1)} %keyval_ref.1) | copy-start | bytes 786436
  0.6 16.1 %copy-start.1 = (bf16[1024,512]{1,0:T(8,128)(2,1)S(1)}, bf16[1024,512]{1,0:T(8,128)(2,1)}, u32[]{:S(2)}) copy-start(bf16[1024,512]{1,0:T(8,128)(2,1)} %query_ref.1) | copy-start | bytes 3145732
  0.7 51.3 %copy-start.15 = (s32[8]{0:T(128)S(1)}, s32[8]{0:T(128)}, u32[]{:S(2)}) copy-start(s32[8]{0:T(128)} %kept_ref.1) | copy-start | bytes 100
  2.1 14.6 %all-to-all-start = ((bf16[8,5,1024]{2,1,0:T(8,128)(2,1)}), bf16[8,5,1024]{2,1,0:T(8,128)(2,1)S(1)}, u32[]{:S(2)}, u32[]{:S(2)}) async-start(bf16[8,5,1024]{2,1,0:T(8,128)(2,1)} %broadcast_in_dim.2), calls=%async_computation | async-start | bytes 262144 | tf_op jit(solution)/shard_map/all_to_all | solution.py:484
  10.0 6.8 %copy-start.12 = (s32[2]{0:T(128)S(1)}, s32[2]{0:T(128)}, u32[]{:S(2)}) copy-start(s32[2]{0:T(128)} %pad_add_fusion.me_ref) | copy-start | bytes 28
  17.8 10.0 %collective-permute-start.4 = (bf16[8,16,1024]{2,1,0:T(8,128)(2,1)}, bf16[8,16,1024]{2,1,0:T(8,128)(2,1)S(1)}, u32[]{:S(2)}, u32[]{:S(2)}) collective-permute-start(bf16[8,16,1024]{2,1,0:T(8,128)(2,1)} %get-tuple-element.128), channel_id=1, source_target_pairs={{0,4},{4,0},{8,12},{12,8},{16,20},{20,16},{24,28},{28,24},{1,5},{5... | collective-permute-start | bytes 786440 | tf_op jit(solution)/shard_map/ppermute | solution.py:511
  18.8 8.3 %collective-permute-start.3 = (bf16[4,16,1024]{2,1,0:T(8,128)(2,1)}, bf16[4,16,1024]{2,1,0:T(8,128)(2,1)S(1)}, u32[]{:S(2)}, u32[]{:S(2)}) collective-permute-start(bf16[4,16,1024]{2,1,0:T(8,128)(2,1)} %get-tuple-element.127), channel_id=1, source_target_pairs={{0,24},{4,28},{8,16},{12,20},{16,8},{20,12},{24,0},{28,4},{1,25},{... | collective-permute-start | bytes 393224 | tf_op jit(solution)/shard_map/ppermute | solution.py:511
  22.1 1.9 %collective-permute-start = (f32[40,256]{1,0:T(8,128)S(1)}, f32[40,256]{1,0:T(8,128)S(1)}, u32[]{:S(2)}, u32[]{:S(2)}) collective-permute-start(f32[40,256]{1,0:T(8,128)S(1)} %get-tuple-element.124), channel_id=1, source_target_pairs={{0,1},{1,0},{2,3},{3,2},{4,5},{5,4},{6,7},{7,6},{8,9},{9,8},{10,11... | collective-permute-start | bytes 122888 | tf_op jit(solution)/shard_map/ppermute | solution.py:511
  22.1 4.0 %collective-permute-start.1 = (f32[40,256]{1,0:T(8,128)S(1)}, f32[40,256]{1,0:T(8,128)S(1)}, u32[]{:S(2)}, u32[]{:S(2)}) collective-permute-start(f32[40,256]{1,0:T(8,128)S(1)} %get-tuple-element.125), channel_id=1, source_target_pairs={{0,2},{1,3},{2,0},{3,1},{4,6},{5,7},{6,4},{7,5},{8,10},{9,11},{10,... | collective-permute-start | bytes 122888 | tf_op jit(solution)/shard_map/ppermute | solution.py:511
  23.6 3.5 %collective-permute-start.2 = (f32[40,256]{1,0:T(8,128)S(1)}, f32[40,256]{1,0:T(8,128)S(1)}, u32[]{:S(2)}, u32[]{:S(2)}) collective-permute-start(f32[40,256]{1,0:T(8,128)S(1)} %get-tuple-element.126), channel_id=1, source_target_pairs={{0,3},{1,2},{2,1},{3,0},{4,7},{5,6},{6,5},{7,4},{8,11},{9,10},{10,... | collective-permute-start | bytes 122888 | tf_op jit(solution)/shard_map/ppermute | solution.py:511
  28.5 23.5 %collective-permute-start.5 = (bf16[12,16,1024]{2,1,0:T(8,128)(2,1)}, bf16[12,16,1024]{2,1,0:T(8,128)(2,1)S(1)}, u32[]{:S(2)}, u32[]{:S(2)}) collective-permute-start(bf16[12,16,1024]{2,1,0:T(8,128)(2,1)} %get-tuple-element.136), channel_id=1, source_target_pairs={{0,24},{4,28},{8,16},{12,20},{16,8},{20,12},{24,0},{28,4},{1,25},{... | collective-permute-start | bytes 1179656 | tf_op jit(solution)/shard_map/ppermute | solution.py:511
  54.0 11.7 %copy-start.11 = (bf16[8,40,128]{2,1,0:T(8,128)(2,1)}, bf16[8,40,128]{2,1,0:T(8,128)(2,1)S(1)}, u32[]{:S(2)}) copy-start(bf16[8,40,128]{2,1,0:T(8,128)(2,1)S(1)} %get-tuple-element.150.refs_0_) | copy-start | bytes 245764
  54.0 9.5 %collective-permute-start.10 = (bf16[8,16,1024]{2,1,0:T(8,128)(2,1)}, bf16[8,16,1024]{2,1,0:T(8,128)(2,1)S(1)}, u32[]{:S(2)}, u32[]{:S(2)}) collective-permute-start(bf16[8,16,1024]{2,1,0:T(8,128)(2,1)} %get-tuple-element.143), channel_id=1, source_target_pairs={{0,4},{4,0},{8,12},{12,8},{16,20},{20,16},{24,28},{28,24},{1,5},{5... | collective-permute-start | bytes 786440 | tf_op jit(solution)/shard_map/ppermute | solution.py:511
  55.2 8.0 %collective-permute-start.9 = (bf16[4,16,1024]{2,1,0:T(8,128)(2,1)}, bf16[4,16,1024]{2,1,0:T(8,128)(2,1)S(1)}, u32[]{:S(2)}, u32[]{:S(2)}) collective-permute-start(bf16[4,16,1024]{2,1,0:T(8,128)(2,1)} %get-tuple-element.142), channel_id=1, source_target_pairs={{0,28},{4,24},{8,20},{12,16},{16,12},{20,8},{24,4},{28,0},{1,29},{... | collective-permute-start | bytes 393224 | tf_op jit(solution)/shard_map/ppermute | solution.py:511
  57.0 4.7 %collective-permute-start.8 = (bf16[8,40,128]{2,1,0:T(8,128)(2,1)S(1)}, bf16[8,40,128]{2,1,0:T(8,128)(2,1)S(1)}, u32[]{:S(2)}, u32[]{:S(2)}) collective-permute-start(bf16[8,40,128]{2,1,0:T(8,128)(2,1)S(1)} %get-tuple-element.150.refs_0_), channel_id=1, source_target_pairs={{0,3},{1,2},{2,1},{3,0},{4,7},{5,6},{6,5},{7,4},{8,11},{9,10},{10,... | collective-permute-start | bytes 245768 | tf_op jit(solution)/shard_map/ppermute | solution.py:511
  57.0 5.7 %collective-permute-start.7 = (bf16[8,40,128]{2,1,0:T(8,128)(2,1)S(1)}, bf16[8,40,128]{2,1,0:T(8,128)(2,1)S(1)}, u32[]{:S(2)}, u32[]{:S(2)}) collective-permute-start(bf16[8,40,128]{2,1,0:T(8,128)(2,1)S(1)} %get-tuple-element.150.refs_0_), channel_id=1, source_target_pairs={{0,2},{1,3},{2,0},{3,1},{4,6},{5,7},{6,4},{7,5},{8,10},{9,11},{10,... | collective-permute-start | bytes 245768 | tf_op jit(solution)/shard_map/ppermute | solution.py:511
  58.0 4.6 %collective-permute-start.6 = (bf16[8,40,128]{2,1,0:T(8,128)(2,1)S(1)}, bf16[8,40,128]{2,1,0:T(8,128)(2,1)S(1)}, u32[]{:S(2)}, u32[]{:S(2)}) collective-permute-start(bf16[8,40,128]{2,1,0:T(8,128)(2,1)S(1)} %get-tuple-element.150.refs_0_), channel_id=1, source_target_pairs={{0,1},{1,0},{2,3},{3,2},{4,5},{5,4},{6,7},{7,6},{8,9},{9,8},{10,11... | collective-permute-start | bytes 245768 | tf_op jit(solution)/shard_map/ppermute | solution.py:511
  61.6 4.2 %copy-start.16 = (bf16[8,40,128]{2,1,0:T(8,128)(2,1)}, bf16[8,40,128]{2,1,0:T(8,128)(2,1)S(1)}, u32[]{:S(2)}) copy-start(bf16[8,40,128]{2,1,0:T(8,128)(2,1)S(1)} %collective-permute-done.8.refs_3_) | copy-start | bytes 245764
  62.6 3.2 %copy-start.17 = (bf16[8,40,128]{2,1,0:T(8,128)(2,1)}, bf16[8,40,128]{2,1,0:T(8,128)(2,1)S(1)}, u32[]{:S(2)}) copy-start(bf16[8,40,128]{2,1,0:T(8,128)(2,1)S(1)} %collective-permute-done.7.refs_2_) | copy-start | bytes 245764
  62.6 3.2 %copy-start.18 = (bf16[8,40,128]{2,1,0:T(8,128)(2,1)}, bf16[8,40,128]{2,1,0:T(8,128)(2,1)S(1)}, u32[]{:S(2)}) copy-start(bf16[8,40,128]{2,1,0:T(8,128)(2,1)S(1)} %collective-permute-done.6.refs_1_) | copy-start | bytes 245764
  63.2 13.0 %copy-start.9 = (bf16[4,16,1024]{2,1,0:T(8,128)(2,1)}, bf16[4,16,1024]{2,1,0:T(8,128)(2,1)S(1)}, u32[]{:S(2)}) copy-start(bf16[4,16,1024]{2,1,0:T(8,128)(2,1)S(1)} %collective-permute-done.9.refs_6_) | copy-start | bytes 393220
  63.6 12.6 %collective-permute-start.11 = (bf16[7,16,1024]{2,1,0:T(8,128)(2,1)}, bf16[7,16,1024]{2,1,0:T(8,128)(2,1)S(1)}, u32[]{:S(2)}, u32[]{:S(2)}) collective-permute-start(bf16[7,16,1024]{2,1,0:T(8,128)(2,1)} %get-tuple-element.160), channel_id=1, source_target_pairs={{0,28},{4,24},{8,20},{12,16},{16,12},{20,8},{24,4},{28,0},{1,29},{... | collective-permute-start | bytes 688136 | tf_op jit(solution)/shard_map/ppermute | solution.py:511
  65.8 12.5 %collective-permute-start.12 = (bf16[7,16,1024]{2,1,0:T(8,128)(2,1)}, bf16[7,16,1024]{2,1,0:T(8,128)(2,1)S(1)}, u32[]{:S(2)}, u32[]{:S(2)}) collective-permute-start(bf16[7,16,1024]{2,1,0:T(8,128)(2,1)} %get-tuple-element.161), channel_id=1, source_target_pairs={{0,8},{4,12},{8,0},{12,4},{16,24},{20,28},{24,16},{28,20},{1,9},{5... | collective-permute-start | bytes 688136 | tf_op jit(solution)/shard_map/ppermute | solution.py:511
  65.8 12.5 %copy-start.20 = (bf16[5,16,1024]{2,1,0:T(8,128)(2,1)S(1)}, bf16[5,16,1024]{2,1,0:T(8,128)(2,1)}, u32[]{:S(2)}) copy-start(bf16[5,16,1024]{2,1,0:T(8,128)(2,1)} %get-tuple-element.172) | copy-start | bytes 491524
  65.8 14.5 %copy-start.19 = (bf16[5,16,1024]{2,1,0:T(8,128)(2,1)S(1)}, bf16[5,16,1024]{2,1,0:T(8,128)(2,1)}, u32[]{:S(2)}) copy-start(bf16[5,16,1024]{2,1,0:T(8,128)(2,1)} %get-tuple-element.173) | copy-start | bytes 491524
  78.3 10.7 %collective-permute-start.16 = (bf16[5,16,1024]{2,1,0:T(8,128)(2,1)S(1)}, bf16[5,16,1024]{2,1,0:T(8,128)(2,1)S(1)}, u32[]{:S(2)}, u32[]{:S(2)}) collective-permute-start(bf16[5,16,1024]{2,1,0:T(8,128)(2,1)S(1)} %copy-done.20), channel_id=1, source_target_pairs={{0,28},{4,24},{8,20},{12,16},{16,12},{20,8},{24,4},{28,0},{1,29},{... | collective-permute-start | bytes 491528 | tf_op jit(solution)/shard_map/ppermute | solution.py:511
  80.3 9.8 %collective-permute-start.17 = (bf16[5,16,1024]{2,1,0:T(8,128)(2,1)S(1)}, bf16[5,16,1024]{2,1,0:T(8,128)(2,1)S(1)}, u32[]{:S(2)}, u32[]{:S(2)}) collective-permute-start(bf16[5,16,1024]{2,1,0:T(8,128)(2,1)S(1)} %copy-done.19), channel_id=1, source_target_pairs={{0,12},{4,8},{8,4},{12,0},{16,28},{20,24},{24,20},{28,16},{1,13},{... | collective-permute-start | bytes 491528 | tf_op jit(solution)/shard_map/ppermute | solution.py:511
  80.4 1.9 %collective-permute-start.13 = (bf16[8,64,128]{2,1,0:T(8,128)(2,1)}, bf16[8,64,128]{2,1,0:T(8,128)(2,1)S(1)}, u32[]{:S(2)}, u32[]{:S(2)}) collective-permute-start(bf16[8,64,128]{2,1,0:T(8,128)(2,1)} %get-tuple-element.169), channel_id=1, source_target_pairs={{0,1},{1,0},{2,3},{3,2},{4,5},{5,4},{6,7},{7,6},{8,9},{9,8},{10,11... | collective-permute-start | bytes 393224 | tf_op jit(solution)/shard_map/ppermute | solution.py:511
  80.4 6.5 %collective-permute-start.14 = (bf16[8,64,128]{2,1,0:T(8,128)(2,1)}, bf16[8,64,128]{2,1,0:T(8,128)(2,1)S(1)}, u32[]{:S(2)}, u32[]{:S(2)}) collective-permute-start(bf16[8,64,128]{2,1,0:T(8,128)(2,1)} %get-tuple-element.170), channel_id=1, source_target_pairs={{0,2},{1,3},{2,0},{3,1},{4,6},{5,7},{6,4},{7,5},{8,10},{9,11},{10,... | collective-permute-start | bytes 393224 | tf_op jit(solution)/shard_map/ppermute | solution.py:511
  81.4 7.5 %collective-permute-start.15 = (bf16[8,64,128]{2,1,0:T(8,128)(2,1)}, bf16[8,64,128]{2,1,0:T(8,128)(2,1)S(1)}, u32[]{:S(2)}, u32[]{:S(2)}) collective-permute-start(bf16[8,64,128]{2,1,0:T(8,128)(2,1)} %get-tuple-element.171), channel_id=1, source_target_pairs={{0,3},{1,2},{2,1},{3,0},{4,7},{5,6},{6,5},{7,4},{8,11},{9,10},{10,... | collective-permute-start | bytes 393224 | tf_op jit(solution)/shard_map/ppermute | solution.py:511
  90.1 0.9 copy-start.6
  91.0 1.1 copy-start.4
  92.1 24.8 %collective-permute-start.18 = (bf16[13,16,1024]{2,1,0:T(8,128)(2,1)}, bf16[13,16,1024]{2,1,0:T(8,128)(2,1)S(1)}, u32[]{:S(2)}, u32[]{:S(2)}) collective-permute-start(bf16[13,16,1024]{2,1,0:T(8,128)(2,1)} %get-tuple-element.183), channel_id=1, source_target_pairs={{0,16},{4,20},{8,24},{12,28},{16,0},{20,4},{24,8},{28,12},{1,17},{... | collective-permute-start | bytes 1277960 | tf_op jit(solution)/shard_map/ppermute | solution.py:511
  94.2 22.8 %collective-permute-start.19 = (bf16[9,16,1024]{2,1,0:T(8,128)(2,1)}, bf16[9,16,1024]{2,1,0:T(8,128)(2,1)S(1)}, u32[]{:S(2)}, u32[]{:S(2)}) collective-permute-start(bf16[9,16,1024]{2,1,0:T(8,128)(2,1)} %get-tuple-element.184), channel_id=1, source_target_pairs={{0,8},{4,12},{8,0},{12,4},{16,24},{20,28},{24,16},{28,20},{1,9},{5... | collective-permute-start | bytes 884744 | tf_op jit(solution)/shard_map/ppermute | solution.py:511
  94.6 22.4 %all-to-all-start.2 = ((bf16[8,64,128]{2,1,0:T(8,128)(2,1)}), bf16[8,64,128]{2,1,0:T(8,128)(2,1)S(1)}, u32[]{:S(2)}, u32[]{:S(2)}) async-start(bf16[8,64,128]{2,1,0:T(8,128)(2,1)} %shard_map.142), calls=%async_computation.2 | async-start | bytes 262144 | tf_op jit(solution)/shard_map/all_to_all | solution.py:651
  98.5 0.9 copy-start.5
  100.3 0.9 copy-start.10
  101.2 23.7 %copy-start.21 = (bf16[3,16,1024]{2,1,0:T(8,128)(2,1)S(1)}, bf16[3,16,1024]{2,1,0:T(8,128)(2,1)}, u32[]{:S(2)}) copy-start(bf16[3,16,1024]{2,1,0:T(8,128)(2,1)} %get-tuple-element.202) | copy-start | bytes 294916
  101.2 40.7 %copy-start.2 = (bf16[1024,512]{1,0:T(8,128)(2,1)S(1)}, bf16[1024,512]{1,0:T(8,128)(2,1)}, u32[]{:S(2)}) copy-start(bf16[1024,512]{1,0:T(8,128)(2,1)} %weight_ref.1) | copy-start | bytes 3145732
  101.2 40.7 %copy-start.13 = (s32[2]{0:T(128)S(1)}, s32[2]{0:T(128)}, u32[]{:S(2)}) copy-start(s32[2]{0:T(128)} %pad_add_fusion.me_ref) | copy-start | bytes 28
  117.9 24.1 %collective-permute-start.22 = (bf16[11,16,1024]{2,1,0:T(8,128)(2,1)}, bf16[11,16,1024]{2,1,0:T(8,128)(2,1)S(1)}, u32[]{:S(2)}, u32[]{:S(2)}) collective-permute-start(bf16[11,16,1024]{2,1,0:T(8,128)(2,1)} %get-tuple-element.203), channel_id=1, source_target_pairs={{0,12},{4,8},{8,4},{12,0},{16,28},{20,24},{24,20},{28,16},{1,13},{... | collective-permute-start | bytes 1081352 | tf_op jit(solution)/shard_map/ppermute | solution.py:511
  118.6 23.4 %collective-permute-start.20 = (bf16[10,16,1024]{2,1,0:T(8,128)(2,1)}, bf16[10,16,1024]{2,1,0:T(8,128)(2,1)S(1)}, u32[]{:S(2)}, u32[]{:S(2)}) collective-permute-start(bf16[10,16,1024]{2,1,0:T(8,128)(2,1)} %get-tuple-element.201), channel_id=1, source_target_pairs={{0,20},{4,16},{8,28},{12,24},{16,4},{20,0},{24,12},{28,8},{1,21},{... | collective-permute-start | bytes 983048 | tf_op jit(solution)/shard_map/ppermute | solution.py:511
  121.2 20.8 %all-to-all-start.3 = ((bf16[8,40,128]{2,1,0:T(8,128)(2,1)}), bf16[8,40,128]{2,1,0:T(8,128)(2,1)S(1)}, u32[]{:S(2)}, u32[]{:S(2)}) async-start(bf16[8,40,128]{2,1,0:T(8,128)(2,1)} %shard_map.144), calls=%async_computation.3 | async-start | bytes 163840 | tf_op jit(solution)/shard_map/all_to_all | solution.py:654
  124.9 17.0 %collective-permute-start.21 = (bf16[3,16,1024]{2,1,0:T(8,128)(2,1)S(1)}, bf16[3,16,1024]{2,1,0:T(8,128)(2,1)S(1)}, u32[]{:S(2)}, u32[]{:S(2)}) collective-permute-start(bf16[3,16,1024]{2,1,0:T(8,128)(2,1)S(1)} %copy-done.21), channel_id=1, source_target_pairs={{0,16},{4,20},{8,24},{12,28},{16,0},{20,4},{24,8},{28,12},{1,17},{... | collective-permute-start | bytes 294920 | tf_op jit(solution)/shard_map/ppermute | solution.py:511
  142.9 9.8 %collective-permute-start.26 = (bf16[6,16,1024]{2,1,0:T(8,128)(2,1)}, bf16[6,16,1024]{2,1,0:T(8,128)(2,1)S(1)}, u32[]{:S(2)}, u32[]{:S(2)}) collective-permute-start(bf16[6,16,1024]{2,1,0:T(8,128)(2,1)} %get-tuple-element.214), channel_id=1, source_target_pairs={{0,20},{4,16},{8,28},{12,24},{16,4},{20,0},{24,12},{28,8},{1,21},{... | collective-permute-start | bytes 589832 | tf_op jit(solution)/shard_map/ppermute | solution.py:511
  143.1 1.9 %collective-permute-start.23 = (f32[10,512]{1,0:T(8,128)S(1)}, f32[10,512]{1,0:T(8,128)S(1)}, u32[]{:S(2)}, u32[]{:S(2)}) collective-permute-start(f32[10,512]{1,0:T(8,128)S(1)} %get-tuple-element.211), channel_id=1, source_target_pairs={{0,1},{1,0},{2,3},{3,2},{4,5},{5,4},{6,7},{7,6},{8,9},{9,8},{10,11... | collective-permute-start | bytes 61448 | tf_op jit(solution)/shard_map/ppermute | solution.py:511
  143.1 4.0 %collective-permute-start.24 = (f32[10,512]{1,0:T(8,128)S(1)}, f32[10,512]{1,0:T(8,128)S(1)}, u32[]{:S(2)}, u32[]{:S(2)}) collective-permute-start(f32[10,512]{1,0:T(8,128)S(1)} %get-tuple-element.212), channel_id=1, source_target_pairs={{0,2},{1,3},{2,0},{3,1},{4,6},{5,7},{6,4},{7,5},{8,10},{9,11},{10,... | collective-permute-start | bytes 61448 | tf_op jit(solution)/shard_map/ppermute | solution.py:511
  144.2 3.4 %collective-permute-start.25 = (f32[10,512]{1,0:T(8,128)S(1)}, f32[10,512]{1,0:T(8,128)S(1)}, u32[]{:S(2)}, u32[]{:S(2)}) collective-permute-start(f32[10,512]{1,0:T(8,128)S(1)} %get-tuple-element.213), channel_id=1, source_target_pairs={{0,3},{1,2},{2,1},{3,0},{4,7},{5,6},{6,5},{7,4},{8,11},{9,10},{10,... | collective-permute-start | bytes 61448 | tf_op jit(solution)/shard_map/ppermute | solution.py:511
  (4 other events, 2.9 us)

commit v11 on v10

--- a/solution.py
+++ b/solution.py
@@ -18,7 +18,7 @@
 SCALE2 = math.log2(math.e) / math.sqrt(HD)
 STAT = 16
 MIB = 1024 * 1024
-CUTS = {1: (0, 8, 16), 2: (0, 7, 16), 3: (0, 5, 16), 4: (0, 13, 16), 5: (0, 10, 16), 6: (0, 4, 16), 7: (0, 4, 11, 16)}
+CUTS = {1: (0, 8, 16), 2: (0, 7, 16), 3: (0, 5, 16), 4: (0, 13, 16), 5: (0, 10, 16), 6: (0, 6, 16), 7: (0, 4, 11, 16)}
 NT = (((1,), (1,)), ((), ()))
 
 
@@ -31,8 +31,9 @@
 
 
 def order_kernel(
-    wide, parts, me_ref, dest_ref, req_ref, idx_ref, pool_ref, out_ref, tag_ref, token_ref, *refs
+    wide, parts, me_ref, dest_ref, req_ref, idx_ref, hidden_ref, pool_ref, *refs
 ):
+    out_ref, tag_ref, token_ref, copies_ref, refs = *refs[:4], refs[4:]
     chunk_refs, refs = refs[: len(parts)], refs[len(parts) :]
     pages_ref, line_ref, source_ref, in_sem, out_sem, line_sem = refs
     slots = pool_ref.shape[0]
@@ -63,6 +64,8 @@
 
         lax.fori_loop(first, first + count, start, 0)
 
+    for i in range(wide):
+        copies_ref[i] = hidden_ref[...]
     shifted = idx_ref[...] + 1
     fields = (req_ref[...], shifted // 32, shifted % 32)
     rank_col = column(rank)
@@ -99,19 +102,20 @@
         copy.wait()
 
 
-def order_pages(me, dest, page_req, page_idx, pool, wide, parts):
+def order_pages(me, dest, page_req, page_idx, hidden, pool, wide, parts):
     slots = pool.shape[0]
     part = lambda count: jax.ShapeDtypeStruct((count,) + pool.shape[1:], pool.dtype)
     out_shape = [part(slots), jax.ShapeDtypeStruct((wide, slots), jnp.float32)]
     out_shape += [jax.ShapeDtypeStruct((8, slots * PAGE), jnp.float32)]
+    out_shape += [jax.ShapeDtypeStruct((wide,) + hidden.shape, hidden.dtype)]
     out_shape += [part(last - first) for _, first, last in parts]
     vmem = pl.BlockSpec(memory_space=pltpu.VMEM)
     hbm = pl.BlockSpec(memory_space=pltpu.HBM)
     return pl.pallas_call(
         functools.partial(order_kernel, wide, parts),
         out_shape=out_shape,
-        in_specs=[pl.BlockSpec(memory_space=pltpu.SMEM), vmem, vmem, vmem, hbm],
-        out_specs=[hbm, vmem, vmem] + [hbm] * len(parts),
+        in_specs=[pl.BlockSpec(memory_space=pltpu.SMEM), vmem, vmem, vmem, vmem, hbm],
+        out_specs=[hbm, vmem, vmem, vmem] + [hbm] * len(parts),
         scratch_shapes=[
             pltpu.VMEM(pool.shape, pool.dtype),
             pltpu.VMEM((1, slots), jnp.int32),
@@ -121,10 +125,8 @@
             pltpu.SemaphoreType.DMA,
         ],
         compiler_params=pltpu.CompilerParams(vmem_limit_bytes=56 * MIB),
-        cost_estimate=pl.CostEstimate(
-            flops=0, bytes_accessed=2 * pool.size * 2, transcendentals=0
-        ),
-    )(me, dest.reshape(1, -1), page_req.reshape(1, -1), page_idx.reshape(1, -1), pool)
+        cost_estimate=pl.CostEstimate(flops=1, bytes_accessed=1, transcendentals=0),
+    )(me, dest.reshape(1, -1), page_req.reshape(1, -1), page_idx.reshape(1, -1), hidden, pool)
 
 
 def place_kernel(place_ref, *refs):
@@ -155,9 +157,7 @@
         scratch_shapes=[pltpu.SemaphoreType.DMA((count,))],
         input_output_aliases={count + 1: 0},
         compiler_params=pltpu.CompilerParams(vmem_limit_bytes=2 * count * chunks[0].size + 2 * MIB),
-        cost_estimate=pl.CostEstimate(
-            flops=0, bytes_accessed=4 * count * chunks[0].size, transcendentals=0
-        ),
+        cost_estimate=pl.CostEstimate(flops=1, bytes_accessed=1, transcendentals=0),
     )(place, *chunks, pages)
 
 
@@ -312,7 +312,7 @@
             pltpu.VMEM((pieces, height, HD), jnp.bfloat16),
         ],
         compiler_params=pltpu.CompilerParams(vmem_limit_bytes=56 * MIB),
-        cost_estimate=pl.CostEstimate(flops=0, bytes_accessed=0, transcendentals=0),
+        cost_estimate=pl.CostEstimate(flops=1, bytes_accessed=1, transcendentals=0),
     )(me, lengths, *queries, pool, pool, keyval, keyval, token_info)
 
 
@@ -366,11 +366,7 @@
         in_specs=[pl.BlockSpec(memory_space=pltpu.VMEM)] * len(parts),
         out_specs=pl.BlockSpec(memory_space=pltpu.VMEM),
         compiler_params=pltpu.CompilerParams(vmem_limit_bytes=8 * MIB),
-        cost_estimate=pl.CostEstimate(
-            flops=2 * len(parts) * parts[0].size,
-            bytes_accessed=len(parts) * parts[0].size * 2,
-            transcendentals=0,
-        ),
+        cost_estimate=pl.CostEstimate(flops=1, bytes_accessed=1, transcendentals=0),
     )(*parts)
 
 
@@ -469,9 +465,7 @@
         out_specs=jax.tree.map(lambda _: pl.BlockSpec(memory_space=pltpu.VMEM), out_shape),
         scratch_shapes=scratch,
         compiler_params=pltpu.CompilerParams(vmem_limit_bytes=16 * MIB),
-        cost_estimate=pl.CostEstimate(
-            flops=0, bytes_accessed=sum(2 * arg.size for arg in args), transcendentals=0
-        ),
+        cost_estimate=pl.CostEstimate(flops=1, bytes_accessed=1, transcendentals=0),
     )(*head, *args)
 
 
@@ -516,14 +510,12 @@
     def deal(blocks, axis):
         return [blocks[0]] + [send(block, axis, d) for d, block in enumerate(blocks) if d]
 
-    gathered = spread(hidden, "wide")
-
     parts = []
     for d in range(1, wide):
         cuts = [cut * capacity // 16 for cut in CUTS[group_of(d, wide)]]
         parts += [(d, a, b) for a, b in zip(cuts[:-1], cuts[1:]) if b > a]
-    moved_pool, tags, token_info, *chunks = order_pages(
-        both, moves, page_req, page_idx, pool, wide, parts
+    moved_pool, tags, token_info, copies, *chunks = order_pages(
+        both, moves, page_req, page_idx, hidden, pool, wide, parts
     )
     arrived = {}
     flying = {}
@@ -563,6 +555,7 @@
         arrived.clear()
         return pages
 
+    gathered = beside(lambda value: exchange(value, "wide"), copies, (6, 0), (1, 0))
     tokens = pool.reshape(slots * PAGE, -1)
     if direct:
         block = jax.ShapeDtypeStruct((rows, 2 * HD), jnp.float32)
@@ -575,7 +568,7 @@
             w_keyval,
             scratch=[pltpu.VMEM((rows, narrow * HD), jnp.float32)],
         )
-        partial = beside(lambda value: deal(value, "narrow"), partial, (6, 0), (1, 0))
+        partial = launch(deal(partial, "narrow"), (6, 1))
         packed = in_vmem(
             functools.partial(pack_kernel, narrow),
             jax.ShapeDtypeStruct((wide, rows + wide, 2 * HD), jnp.bfloat16),
@@ -583,7 +576,8 @@
             *partial,
             tags,
         )
-        received = beside(lambda value: exchange(value, "wide"), packed, (6, 1))
+        received = land(exchange(packed, "wide"), (6, 1))
+        received = launch(received, (7, 0), (1, 1), (7, 1))
         queries, keyval, new_entries, moved_req, moved_idx = in_vmem(
             functools.partial(unpack_kernel, rows),
             [
@@ -597,7 +591,7 @@
             received,
         )
         moved_req, moved_idx = moved_req.reshape(slots), moved_idx.reshape(slots)
-        queries = beside(lambda value: share(value, "narrow"), queries, (7, 0), (1, 1))
+        queries = land(share(queries, "narrow"), (7, 0), (1, 1))
     else:
         gathered = gathered.reshape(rows, -1)
         query_part = jnp.dot(gathered, w_query, preferred_element_type=jnp.float32)
@@ -606,16 +600,17 @@
         partial = jnp.concatenate(
             [query_part, jnp.broadcast_to(keyval_part[None], (narrow,) + keyval_part.shape)], axis=2
         )
-        partial = beside(lambda value: exchange(value, "narrow"), partial, (6, 0), (1, 0))
+        partial = launch(exchange(partial, "narrow"), (6, 1))
         projected = jnp.sum(partial, axis=0).astype(jnp.bfloat16)
         tags = tags[:, : 3 * capacity].astype(jnp.bfloat16)[:, None]
         tags = jnp.pad(tags, ((0, 0), (0, 7), (0, projected.shape[1] - tags.shape[2])))
         packed = jnp.broadcast_to(projected[None], (wide,) + projected.shape)
         packed = jnp.concatenate([packed, tags], axis=1)
-        received = beside(lambda value: exchange(value, "wide"), packed, (6, 1))
+        received = land(exchange(packed, "wide"), (6, 1))
+        received = launch(received, (7, 0), (1, 1), (7, 1))
         tags_in = received[:, rows]
         queries = received[:, :rows, :own_cols]
-        queries = beside(lambda value: spread(value, "narrow"), queries, (7, 0), (1, 1))
+        queries = land(spread(queries, "narrow"), (7, 0), (1, 1))
         queries = jnp.transpose(queries, (2, 1, 0, 3)).reshape(rows, HEADS, HD)
         queries = [jnp.transpose(queries, (1, 0, 2)).reshape(KVH, GROUPS * rows, HD)]
         keyval = jnp.transpose(received[:, :rows, own_cols:], (1, 0, 2)).reshape(rows, -1)
@@ -633,25 +628,25 @@
             step_ids < kept[:, None, None], fresh, jnp.zeros((), jnp.bfloat16)
         )
 
-    mixed = beside(
-        lambda value: attend(both, lengths, value, keyval, tokens, token_info, rows, piece),
-        queries,
-        (7, 1),
-        (2, 0),
-    )
+    queries = launch(queries, (2, 0), (7, 2))
+    mixed = attend(both, lengths, queries, keyval, tokens, token_info, rows, piece)
+    mixed = launch(land(mixed, (7, 1), (2, 0)), (3, 0))
     if direct:
-        mixed = beside(lambda value: deal(value, "narrow"), mixed, (7, 2), (3, 0))
+        mixed = deal(mixed, "narrow")
     else:
-        mixed = beside(lambda value: exchange(value, "narrow"), mixed[0], (7, 2), (3, 0))
+        mixed = exchange(mixed[0], "narrow")
         mixed = mixed.reshape((narrow, wide) + mixed.shape[1:])
         mixed = [mixed[i] for i in range(narrow)]
+    mixed = launch(land(mixed, (7, 2), (3, 0)), (4, 0), (2, 1))
     mixed = combine(mixed, piece)
     mixed, pages = lax.optimization_barrier((mixed, moved_pool))
     pages = placed(pages)
-    mixed = beside(lambda value: exchange(value, "wide"), mixed, (4, 0), (2, 1))
+    mixed = land(exchange(mixed, "wide"), (4, 0), (2, 1))
     mixed, moved_pool = lax.optimization_barrier((mixed, pages))
+    mixed = launch(mixed, (5, 0), (4, 1), (3, 1))
     attn = combine([mixed], piece, wide)
-    attn = beside(lambda value: exchange(value, "wide"), attn, (5, 0), (4, 1), (3, 1))
+    attn = land(exchange(attn, "wide"), (5, 0), (4, 1), (3, 1))
+    attn = launch(attn, (5, 1))
     if direct:
         sums = in_vmem(
             functools.partial(finish_kernel, narrow),
@@ -660,14 +655,15 @@
             attn,
             w_out,
         )
-        sums = beside(lambda value: deal(value, "narrow"), sums, (5, 1))
+        sums = deal(sums, "narrow")
         attended = ((sums[0] + sums[1]) + (sums[2] + sums[3])).astype(jnp.bfloat16)
     else:
         attn = jnp.transpose(attn.reshape(-1, rows, HD), (1, 0, 2)).reshape(rows, -1)
         sums = jnp.dot(attn, w_out, preferred_element_type=jnp.float32)
         sums = sums.reshape(narrow, rows // narrow, -1)
-        sums = beside(lambda value: exchange(value, "narrow"), sums, (5, 1))
+        sums = exchange(sums, "narrow")
         attended = jnp.sum(sums, axis=0).astype(jnp.bfloat16)
+    attended = land(attended, (5, 1))
     moved_pool = placed(moved_pool)
     return (attended, new_entries, moved_pool, moved_req, moved_idx)
 

time: 156 us -> 164 us (1.051)
  starting transfers between devices: 44.9 us -> 56.5 us
  blocking collectives: 21.4 us -> 11 us
  waiting for transfers between devices: 54.5 us -> 60.4 us
    ppermute x27, starting transfers between devices: 30 us -> 44.4 us  [send(): lax.ppermute(block, axis, [(i, i ^ d) for i in range(lax.axis_size(axis))])]
    all_to_all x1, blocking collectives: 21.4 us -> 11 us  [on_device(): exchange(value, 'wide')]
    ppermute x27, waiting for transfers between devices: 39.7 us -> 47.7 us  [send(): lax.ppermute(block, axis, [(i, i ^ d) for i in range(lax.axis_size(axis))])]
    all_to_all x3, starting transfers between devices: 14.9 us -> 12.1 us  [the longest x1 4.47 us: on_device(): received = land(exchange(packed, 'wide'), (6, 1))]
    all_to_all x3, waiting for transfers between devices: 14.9 us -> 12.8 us  [the longest x1 11.6 us: on_device(): mixed = land(exchange(mixed, 'wide'), (4, 0), (2, 1))]
    unnamed x44 -> x42, local copies, waits for them, and re-layouts: 5.72 us -> 7.09 us
  transfers between devices with their start and end apart: 30 -> 30, of which waited for: 16 -> 12; matrix products, arithmetic and copies ran while one was open for 0% -> 0% of each run, Pallas kernels for 12% -> 10%
where the time goes in v11:
time: 164 us; the launch traced here: 163 us
  waiting for transfers between devices  60.4 us (37%)
  starting transfers between devices  56.5 us (34%)
  Pallas kernels  25.7 us (16%)
  blocking collectives  11 us (7%)
  local copies, waits for them, and re-layouts  7.25 us (4%)
    ppermute x27, waiting for transfers between devices, send(): lax.ppermute(block, axis, [(i, i ^ d) for i in range(lax.axis_size(axis))])  47.7 us
    ppermute x27, starting transfers between devices, send(): lax.ppermute(block, axis, [(i, i ^ d) for i in range(lax.axis_size(axis))])  44.4 us
    all_to_all x1, waiting for transfers between devices, on_device(): mixed = land(exchange(mixed, 'wide'), (4, 0), (2, 1))  11.6 us
    all_to_all x1, blocking collectives, on_device(): exchange(value, 'wide')  11 us
    pallas_call x1, Pallas kernels, attend(): pl.pallas_call(functools.partial(attend_kernel, rows, piece, peers), grid...  10.3 us
    unnamed x42, local copies, waits for them, and re-layouts  7.09 us
    pallas_call x1, Pallas kernels, order_pages(): pl.pallas_call(functools.partial(order_kernel, wide, parts), out_shape=ou...  5.83 us
    all_to_all x1, starting transfers between devices, on_device(): received = land(exchange(packed, 'wide'), (6, 1))  4.47 us
  transfers between devices with their start and end apart: 30, of which 12 were waited for; matrix products, arithmetic and copies ran while one was open for 0% of the time, Pallas kernels for 10%

profile of v11, /device:TPU:0, one launch (start us, length us, event | category | flops | bytes accessed | tf_op | source)
XLA Modules:
  0.0 163.0 jit_solution(2862291132752759616)
XLA Ops:
  1.3 5.8 %shard_map.137 = (bf16[128,16,1024]{2,1,0:T(8,128)(2,1)}, f32[8,128]{1,0:T(8,128)}, f32[8,2048]{1,0:T(8,128)}, bf16[8,5,1024]{2,1,0:T(8,128)(2,1)}, bf16[8,16,10...) custom-call(s32[2]{0:T(128)} %pad_add_fusion.me_ref, ...), custom_call_target="tpu_custom_call" | custom-call | flops 1 | bytes 1 | tf_op jit(solution)/shard_map/pallas_call | solution.py:114
  7.2 3.0 %collective-permute-start.1 = (bf16[8,16,1024]{2,1,0:T(8,128)(2,1)}, bf16[8,16,1024]{2,1,0:T(8,128)(2,1)S(1)}, u32[]{:S(2)}, u32[]{:S(2)}) collective-permute-start(bf16[8,16,1024]{2,1,0:T(8,128)(2,1)} %get-tuple-element.117), channel_id=1, source_target_pairs={{0,4},{4,0},{8,12},{12,8},{16,20},{20,16},{24,28},{28,24},{1,5},{5... | collective-permute-start | bytes 786440 | tf_op jit(solution)/shard_map/ppermute | solution.py:505
  10.2 3.6 %collective-permute-start = (bf16[6,16,1024]{2,1,0:T(8,128)(2,1)}, bf16[6,16,1024]{2,1,0:T(8,128)(2,1)S(1)}, u32[]{:S(2)}, u32[]{:S(2)}) collective-permute-start(bf16[6,16,1024]{2,1,0:T(8,128)(2,1)} %get-tuple-element.116), channel_id=1, source_target_pairs={{0,24},{4,28},{8,16},{12,20},{16,8},{20,12},{24,0},{28,4},{1,25},{... | collective-permute-start | bytes 589832 | tf_op jit(solution)/shard_map/ppermute | solution.py:505
  13.8 11.0 %all_to_all.20.hidden_ref = bf16[8,5,1024]{2,1,0:T(8,128)(2,1)S(1)} all-to-all(bf16[8,5,1024]{2,1,0:T(8,128)(2,1)} %get-tuple-element.115), channel_id=1, replica_groups=mesh['wide'=8,'narrow'=4] {'wide'}, dimensions={0} | all-to-all | bytes 163840 | tf_op jit(solution)/shard_map/all_to_all | solution.py:558
  24.8 1.0 shard_map.138
  25.9 1.6 collective-permute-start.3
  27.8 2.2 %collective-permute-done.3.refs_2_ = f32[40,256]{1,0:T(8,128)S(1)} collective-permute-done((f32[40,256]{1,0:T(8,128)S(1)}, f32[40,256]{1,0:T(8,128)S(1)}, u32[]{:S(2)}, u32[]{:S(2)}) %collective-permute-start.3) | collective-permute-done | bytes 40992 | tf_op jit(solution)/shard_map/ppermute | solution.py:505
  30.0 1.0 collective-permute-done.4.refs_3_
  32.4 4.5 %all-to-all-start.1 = ((bf16[8,48,256]{2,1,0:T(8,128)(2,1)}), bf16[8,48,256]{2,1,0:T(8,128)(2,1)S(1)}, u32[]{:S(2)}, u32[]{:S(2)}) async-start(bf16[8,48,256]{2,1,0:T(8,128)(2,1)} %shard_map.139), calls=%async_computation.1 | async-start | bytes 393216 | tf_op jit(solution)/shard_map/all_to_all | solution.py:579
  36.8 3.8 %collective-permute-start.5 = (bf16[10,16,1024]{2,1,0:T(8,128)(2,1)}, bf16[10,16,1024]{2,1,0:T(8,128)(2,1)S(1)}, u32[]{:S(2)}, u32[]{:S(2)}) collective-permute-start(bf16[10,16,1024]{2,1,0:T(8,128)(2,1)} %get-tuple-element.129), channel_id=1, source_target_pairs={{0,24},{4,28},{8,16},{12,20},{16,8},{20,12},{24,0},{28,4},{1,25},{... | collective-permute-start | bytes 983048 | tf_op jit(solution)/shard_map/ppermute | solution.py:505
  40.7 10.9 %collective-permute-done.5.refs_5_ = bf16[10,16,1024]{2,1,0:T(8,128)(2,1)S(1)} collective-permute-done((bf16[10,16,1024]{2,1,0:T(8,128)(2,1)}, bf16[10,16,1024]{2,1,0:T(8,128)(2,1)S(1)}, u32[]{:S(2)}, u32[]{:S(2)}) %collective-permute-start.5) | collective-permute-done | bytes 327712 | tf_op jit(solution)/shard_map/ppermute | solution.py:505
  51.6 1.2 all-to-all-done.1.part_ref
  52.7 1.4 collective-permute-start.10
  54.1 0.7 collective-permute-start.9
  54.9 1.4 shard_map.140
  56.9 0.9 collective-permute-start.7
  57.8 0.9 collective-permute-start.6
  58.8 2.8 %collective-permute-done.8.refs_3_ = bf16[8,40,128]{2,1,0:T(8,128)(2,1)S(1)} collective-permute-done((bf16[8,40,128]{2,1,0:T(8,128)(2,1)S(1)}, bf16[8,40,128]{2,1,0:T(8,128)(2,1)S(1)}, u32[]{:S(2)}, u32[]{:S(2)}) %collective-permute-start.8) | collective-permute-done | bytes 81952 | tf_op jit(solution)/shard_map/ppermute | solution.py:505
  61.6 4.0 %collective-permute-start.11 = (bf16[7,16,1024]{2,1,0:T(8,128)(2,1)}, bf16[7,16,1024]{2,1,0:T(8,128)(2,1)S(1)}, u32[]{:S(2)}, u32[]{:S(2)}) collective-permute-start(bf16[7,16,1024]{2,1,0:T(8,128)(2,1)} %get-tuple-element.154), channel_id=1, source_target_pairs={{0,28},{4,24},{8,20},{12,16},{16,12},{20,8},{24,4},{28,0},{1,29},{... | collective-permute-start | bytes 688136 | tf_op jit(solution)/shard_map/ppermute | solution.py:505
  66.3 7.6 %collective-permute-start.12 = (bf16[7,16,1024]{2,1,0:T(8,128)(2,1)}, bf16[7,16,1024]{2,1,0:T(8,128)(2,1)S(1)}, u32[]{:S(2)}, u32[]{:S(2)}) collective-permute-start(bf16[7,16,1024]{2,1,0:T(8,128)(2,1)} %get-tuple-element.155), channel_id=1, source_target_pairs={{0,8},{4,12},{8,0},{12,4},{16,24},{20,28},{24,16},{28,20},{1,9},{5... | collective-permute-start | bytes 688136 | tf_op jit(solution)/shard_map/ppermute | solution.py:505
  73.9 1.8 %collective-permute-start.16 = (bf16[5,16,1024]{2,1,0:T(8,128)(2,1)}, bf16[5,16,1024]{2,1,0:T(8,128)(2,1)S(1)}, u32[]{:S(2)}, u32[]{:S(2)}) collective-permute-start(bf16[5,16,1024]{2,1,0:T(8,128)(2,1)} %get-tuple-element.165), channel_id=1, source_target_pairs={{0,28},{4,24},{8,20},{12,16},{16,12},{20,8},{24,4},{28,0},{1,29},{... | collective-permute-start | bytes 491528 | tf_op jit(solution)/shard_map/ppermute | solution.py:505
  75.8 10.3 %shard_map.141 = (bf16[8,64,128]{2,1,0:T(8,128)(2,1)}, bf16[8,64,128]{2,1,0:T(8,128)(2,1)}, bf16[8,64,128]{2,1,0:T(8,128)(2,1)}, bf16[8,64,128]{2,1,0:T(8,128)(2,1)}) custom-call(s32[2]{0:T(128)} %pad_add_fusion.me_ref, s32[8]{0:T(128)} %length_ref.1, bf16[8,40,128]{2,1,0:T(8,128)(2,1)} %copy-done.11, bf16[8,40,128]{2,1,0:T(8,128)(2,1)} %copy-done.18, ...), custom_call_target="tpu_custom_call" | custom-call | flops 1 | bytes 1 | tf_op jit(solution)/shard_map/pallas_call | solution.py:292
  86.1 1.0 collective-permute-start.17
  87.1 1.0 collective-permute-start.14
  88.1 0.9 collective-permute-start.15
  89.6 4.0 %collective-permute-done.14.refs_2_ = bf16[8,64,128]{2,1,0:T(8,128)(2,1)S(1)} collective-permute-done((bf16[8,64,128]{2,1,0:T(8,128)(2,1)}, bf16[8,64,128]{2,1,0:T(8,128)(2,1)S(1)}, u32[]{:S(2)}, u32[]{:S(2)}) %collective-permute-start.14) | collective-permute-done | bytes 131104 | tf_op jit(solution)/shard_map/ppermute | solution.py:505
  93.6 2.0 %collective-permute-done.15.refs_3_ = bf16[8,64,128]{2,1,0:T(8,128)(2,1)S(1)} collective-permute-done((bf16[8,64,128]{2,1,0:T(8,128)(2,1)}, bf16[8,64,128]{2,1,0:T(8,128)(2,1)S(1)}, u32[]{:S(2)}, u32[]{:S(2)}) %collective-permute-start.15) | collective-permute-done | bytes 131104 | tf_op jit(solution)/shard_map/ppermute | solution.py:505
  96.3 2.5 %collective-permute-start.18 = (bf16[13,16,1024]{2,1,0:T(8,128)(2,1)}, bf16[13,16,1024]{2,1,0:T(8,128)(2,1)S(1)}, u32[]{:S(2)}, u32[]{:S(2)}) collective-permute-start(bf16[13,16,1024]{2,1,0:T(8,128)(2,1)} %get-tuple-element.179), channel_id=1, source_target_pairs={{0,16},{4,20},{8,24},{12,28},{16,0},{20,4},{24,8},{28,12},{1,17},{... | collective-permute-start | bytes 1277960 | tf_op jit(solution)/shard_map/ppermute | solution.py:505
  99.2 0.9 copy-done.8
  100.1 1.1 shard_map.142
  101.2 4.2 %all-to-all-start.2 = ((bf16[8,64,128]{2,1,0:T(8,128)(2,1)}), bf16[8,64,128]{2,1,0:T(8,128)(2,1)S(1)}, u32[]{:S(2)}, u32[]{:S(2)}) async-start(bf16[8,64,128]{2,1,0:T(8,128)(2,1)} %shard_map.142), calls=%async_computation.2 | async-start | bytes 262144 | tf_op jit(solution)/shard_map/all_to_all | solution.py:644
  105.5 0.9 copy-done.5
  106.4 0.9 copy-done.7
  107.3 0.9 copy-done.10
  108.2 1.9 %shard_map.143.refs_6_ = bf16[128,16,1024]{2,1,0:T(8,128)(2,1)} custom-call(s32[9]{0:T(128)S(1)} %stack.72.place_ref, bf16[8,16,1024]{2,1,0:T(8,128)(2,1)S(1)} %collective-permute-done.1.refs_0_, bf16[8,16,1024]{2,1,0:T(8,128)(2,1)S(1)} %collective-permute-done.10.refs_1_, ...), custom_call_target="tpu_custom_call", output_to_operand_aliasing={{}: (10, {})} | custom-call | flops 1 | bytes 1 | tf_op jit(solution)/shard_map/pallas_call | solution.py:150
  110.1 11.6 %all-to-all-done.2.refs_0_ = bf16[8,64,128]{2,1,0:T(8,128)(2,1)S(1)} async-done(((bf16[8,64,128]{2,1,0:T(8,128)(2,1)}), bf16[8,64,128]{2,1,0:T(8,128)(2,1)S(1)}, u32[]{:S(2)}, u32[]{:S(2)}) %all-to-all-start.2) | async-done | bytes 131104 | tf_op jit(solution)/shard_map/all_to_all | solution.py:644
  121.7 0.8 collective-permute-start.22
  122.5 2.9 %collective-permute-start.20 = (bf16[10,16,1024]{2,1,0:T(8,128)(2,1)}, bf16[10,16,1024]{2,1,0:T(8,128)(2,1)S(1)}, u32[]{:S(2)}, u32[]{:S(2)}) collective-permute-start(bf16[10,16,1024]{2,1,0:T(8,128)(2,1)} %get-tuple-element.197), channel_id=1, source_target_pairs={{0,20},{4,16},{8,28},{12,24},{16,4},{20,0},{24,12},{28,8},{1,21},{... | collective-permute-start | bytes 983048 | tf_op jit(solution)/shard_map/ppermute | solution.py:505
  125.4 0.9 shard_map.144
  126.3 3.4 %all-to-all-start.3 = ((bf16[8,40,128]{2,1,0:T(8,128)(2,1)}), bf16[8,40,128]{2,1,0:T(8,128)(2,1)S(1)}, u32[]{:S(2)}, u32[]{:S(2)}) async-start(bf16[8,40,128]{2,1,0:T(8,128)(2,1)} %shard_map.144), calls=%async_computation.3 | async-start | bytes 163840 | tf_op jit(solution)/shard_map/all_to_all | solution.py:648
  129.7 2.9 %collective-permute-start.21 = (bf16[3,16,1024]{2,1,0:T(8,128)(2,1)S(1)}, bf16[3,16,1024]{2,1,0:T(8,128)(2,1)S(1)}, u32[]{:S(2)}, u32[]{:S(2)}) collective-permute-start(bf16[3,16,1024]{2,1,0:T(8,128)(2,1)S(1)} %copy-done.20), channel_id=1, source_target_pairs={{0,16},{4,20},{8,24},{12,28},{16,0},{20,4},{24,8},{28,12},{1,17},{... | collective-permute-start | bytes 294920 | tf_op jit(solution)/shard_map/ppermute | solution.py:505
  132.6 13.5 %collective-permute-done.21.refs_3_ = bf16[3,16,1024]{2,1,0:T(8,128)(2,1)S(1)} collective-permute-done((bf16[3,16,1024]{2,1,0:T(8,128)(2,1)S(1)}, bf16[3,16,1024]{2,1,0:T(8,128)(2,1)S(1)}, u32[]{:S(2)}, u32[]{:S(2)}) %collective-permute-start.21) | collective-permute-done | bytes 98336 | tf_op jit(solution)/shard_map/ppermute | solution.py:505
  146.2 0.9 shard_map.145
  147.2 1.0 collective-permute-start.24
  148.2 0.9 collective-permute-start.25
  149.5 1.7 %collective-permute-done.24 = f32[10,512]{1,0:T(8,128)S(1)} collective-permute-done((f32[10,512]{1,0:T(8,128)S(1)}, f32[10,512]{1,0:T(8,128)S(1)}, u32[]{:S(2)}, u32[]{:S(2)}) %collective-permute-start.24) | collective-permute-done | bytes 20512 | tf_op jit(solution)/shard_map/ppermute | solution.py:505
  152.2 9.1 %collective-permute-done.26.refs_5_ = bf16[6,16,1024]{2,1,0:T(8,128)(2,1)S(1)} collective-permute-done((bf16[6,16,1024]{2,1,0:T(8,128)(2,1)}, bf16[6,16,1024]{2,1,0:T(8,128)(2,1)S(1)}, u32[]{:S(2)}, u32[]{:S(2)}) %collective-permute-start.26) | collective-permute-done | bytes 196640 | tf_op jit(solution)/shard_map/ppermute | solution.py:505
  161.2 1.8 %shard_map.146 = bf16[128,16,1024]{2,1,0:T(8,128)(2,1)} custom-call(s32[6]{0:T(128)S(1)} %stack.79.place_ref, bf16[9,16,1024]{2,1,0:T(8,128)(2,1)S(1)} %collective-permute-done.19.refs_0_, bf16[11,16,1024]{2,1,0:T(8,128)(2,1)S(1)} %collective-permute-done.22.refs_1_, ...), custom_call_target="tpu_custom_call", output_to_operand_aliasing={{}: (7, {})} | custom-call | flops 1 | bytes 1 | tf_op jit(solution)/shard_map/pallas_call | solution.py:150
  (69 shorter events, 7.1 us)
Async XLA Ops:
  0.6 24.2 %copy-start.3 = (bf16[1024,128]{1,0:T(8,128)(2,1)S(1)}, bf16[1024,128]{1,0:T(8,128)(2,1)}, u32[]{:S(2)}) copy-start(bf16[1024,128]{1,0:T(8,128)(2,1)} %keyval_ref.1) | copy-start | bytes 786436
  0.6 24.2 %copy-start.1 = (bf16[1024,512]{1,0:T(8,128)(2,1)S(1)}, bf16[1024,512]{1,0:T(8,128)(2,1)}, u32[]{:S(2)}) copy-start(bf16[1024,512]{1,0:T(8,128)(2,1)} %query_ref.1) | copy-start | bytes 3145732
  0.7 54.2 %copy-start.15 = (s32[8]{0:T(128)S(1)}, s32[8]{0:T(128)}, u32[]{:S(2)}) copy-start(s32[8]{0:T(128)} %kept_ref.1) | copy-start | bytes 100
  1.3 23.5 %copy-start.12 = (s32[2]{0:T(128)S(1)}, s32[2]{0:T(128)}, u32[]{:S(2)}) copy-start(s32[2]{0:T(128)} %pad_add_fusion.me_ref) | copy-start | bytes 28
  7.2 17.6 %collective-permute-start.1 = (bf16[8,16,1024]{2,1,0:T(8,128)(2,1)}, bf16[8,16,1024]{2,1,0:T(8,128)(2,1)S(1)}, u32[]{:S(2)}, u32[]{:S(2)}) collective-permute-start(bf16[8,16,1024]{2,1,0:T(8,128)(2,1)} %get-tuple-element.117), channel_id=1, source_target_pairs={{0,4},{4,0},{8,12},{12,8},{16,20},{20,16},{24,28},{28,24},{1,5},{5... | collective-permute-start | bytes 786440 | tf_op jit(solution)/shard_map/ppermute | solution.py:505
  10.2 14.6 %collective-permute-start = (bf16[6,16,1024]{2,1,0:T(8,128)(2,1)}, bf16[6,16,1024]{2,1,0:T(8,128)(2,1)S(1)}, u32[]{:S(2)}, u32[]{:S(2)}) collective-permute-start(bf16[6,16,1024]{2,1,0:T(8,128)(2,1)} %get-tuple-element.116), channel_id=1, source_target_pairs={{0,24},{4,28},{8,16},{12,20},{16,8},{20,12},{24,0},{28,4},{1,25},{... | collective-permute-start | bytes 589832 | tf_op jit(solution)/shard_map/ppermute | solution.py:505
  25.8 1.9 %collective-permute-start.2 = (f32[40,256]{1,0:T(8,128)S(1)}, f32[40,256]{1,0:T(8,128)S(1)}, u32[]{:S(2)}, u32[]{:S(2)}) collective-permute-start(f32[40,256]{1,0:T(8,128)S(1)} %get-tuple-element.120), channel_id=1, source_target_pairs={{0,1},{1,0},{2,3},{3,2},{4,5},{5,4},{6,7},{7,6},{8,9},{9,8},{10,11... | collective-permute-start | bytes 122888 | tf_op jit(solution)/shard_map/ppermute | solution.py:505
  25.9 4.1 %collective-permute-start.3 = (f32[40,256]{1,0:T(8,128)S(1)}, f32[40,256]{1,0:T(8,128)S(1)}, u32[]{:S(2)}, u32[]{:S(2)}) collective-permute-start(f32[40,256]{1,0:T(8,128)S(1)} %get-tuple-element.121), channel_id=1, source_target_pairs={{0,2},{1,3},{2,0},{3,1},{4,6},{5,7},{6,4},{7,5},{8,10},{9,11},{10,... | collective-permute-start | bytes 122888 | tf_op jit(solution)/shard_map/ppermute | solution.py:505
  27.5 3.5 %collective-permute-start.4 = (f32[40,256]{1,0:T(8,128)S(1)}, f32[40,256]{1,0:T(8,128)S(1)}, u32[]{:S(2)}, u32[]{:S(2)}) collective-permute-start(f32[40,256]{1,0:T(8,128)S(1)} %get-tuple-element.122), channel_id=1, source_target_pairs={{0,3},{1,2},{2,1},{3,0},{4,7},{5,6},{6,5},{7,4},{8,11},{9,10},{10,... | collective-permute-start | bytes 122888 | tf_op jit(solution)/shard_map/ppermute | solution.py:505
  32.4 20.4 %all-to-all-start.1 = ((bf16[8,48,256]{2,1,0:T(8,128)(2,1)}), bf16[8,48,256]{2,1,0:T(8,128)(2,1)S(1)}, u32[]{:S(2)}, u32[]{:S(2)}) async-start(bf16[8,48,256]{2,1,0:T(8,128)(2,1)} %shard_map.139), calls=%async_computation.1 | async-start | bytes 393216 | tf_op jit(solution)/shard_map/all_to_all | solution.py:579
  36.8 14.7 %collective-permute-start.5 = (bf16[10,16,1024]{2,1,0:T(8,128)(2,1)}, bf16[10,16,1024]{2,1,0:T(8,128)(2,1)S(1)}, u32[]{:S(2)}, u32[]{:S(2)}) collective-permute-start(bf16[10,16,1024]{2,1,0:T(8,128)(2,1)} %get-tuple-element.129), channel_id=1, source_target_pairs={{0,24},{4,28},{8,16},{12,20},{16,8},{20,12},{24,0},{28,4},{1,25},{... | collective-permute-start | bytes 983048 | tf_op jit(solution)/shard_map/ppermute | solution.py:505
  52.7 13.6 %collective-permute-start.10 = (bf16[8,16,1024]{2,1,0:T(8,128)(2,1)}, bf16[8,16,1024]{2,1,0:T(8,128)(2,1)S(1)}, u32[]{:S(2)}, u32[]{:S(2)}) collective-permute-start(bf16[8,16,1024]{2,1,0:T(8,128)(2,1)} %get-tuple-element.137), channel_id=1, source_target_pairs={{0,4},{4,0},{8,12},{12,8},{16,20},{20,16},{24,28},{28,24},{1,5},{5... | collective-permute-start | bytes 786440 | tf_op jit(solution)/shard_map/ppermute | solution.py:505
  54.1 11.5 %collective-permute-start.9 = (bf16[4,16,1024]{2,1,0:T(8,128)(2,1)}, bf16[4,16,1024]{2,1,0:T(8,128)(2,1)S(1)}, u32[]{:S(2)}, u32[]{:S(2)}) collective-permute-start(bf16[4,16,1024]{2,1,0:T(8,128)(2,1)} %get-tuple-element.136), channel_id=1, source_target_pairs={{0,28},{4,24},{8,20},{12,16},{16,12},{20,8},{24,4},{28,0},{1,29},{... | collective-permute-start | bytes 393224 | tf_op jit(solution)/shard_map/ppermute | solution.py:505
  56.2 0.7 copy-start
  56.9 18.8 %copy-start.11 = (bf16[8,40,128]{2,1,0:T(8,128)(2,1)}, bf16[8,40,128]{2,1,0:T(8,128)(2,1)S(1)}, u32[]{:S(2)}) copy-start(bf16[8,40,128]{2,1,0:T(8,128)(2,1)S(1)} %get-tuple-element.144.refs_0_) | copy-start | bytes 245764
  56.9 4.7 %collective-permute-start.8 = (bf16[8,40,128]{2,1,0:T(8,128)(2,1)S(1)}, bf16[8,40,128]{2,1,0:T(8,128)(2,1)S(1)}, u32[]{:S(2)}, u32[]{:S(2)}) collective-permute-start(bf16[8,40,128]{2,1,0:T(8,128)(2,1)S(1)} %get-tuple-element.144.refs_0_), channel_id=1, source_target_pairs={{0,3},{1,2},{2,1},{3,0},{4,7},{5,6},{6,5},{7,4},{8,11},{9,10},{10,... | collective-permute-start | bytes 245768 | tf_op jit(solution)/shard_map/ppermute | solution.py:505
  56.9 8.7 %collective-permute-start.7 = (bf16[8,40,128]{2,1,0:T(8,128)(2,1)S(1)}, bf16[8,40,128]{2,1,0:T(8,128)(2,1)S(1)}, u32[]{:S(2)}, u32[]{:S(2)}) collective-permute-start(bf16[8,40,128]{2,1,0:T(8,128)(2,1)S(1)} %get-tuple-element.144.refs_0_), channel_id=1, source_target_pairs={{0,2},{1,3},{2,0},{3,1},{4,6},{5,7},{6,4},{7,5},{8,10},{9,11},{10,... | collective-permute-start | bytes 245768 | tf_op jit(solution)/shard_map/ppermute | solution.py:505
  57.8 7.7 %collective-permute-start.6 = (bf16[8,40,128]{2,1,0:T(8,128)(2,1)S(1)}, bf16[8,40,128]{2,1,0:T(8,128)(2,1)S(1)}, u32[]{:S(2)}, u32[]{:S(2)}) collective-permute-start(bf16[8,40,128]{2,1,0:T(8,128)(2,1)S(1)} %get-tuple-element.144.refs_0_), channel_id=1, source_target_pairs={{0,1},{1,0},{2,3},{3,2},{4,5},{5,4},{6,7},{7,6},{8,9},{9,8},{10,11... | collective-permute-start | bytes 245768 | tf_op jit(solution)/shard_map/ppermute | solution.py:505
  61.6 14.2 %copy-start.16 = (bf16[8,40,128]{2,1,0:T(8,128)(2,1)}, bf16[8,40,128]{2,1,0:T(8,128)(2,1)S(1)}, u32[]{:S(2)}) copy-start(bf16[8,40,128]{2,1,0:T(8,128)(2,1)S(1)} %collective-permute-done.8.refs_3_) | copy-start | bytes 245764
  61.6 24.5 %collective-permute-start.11 = (bf16[7,16,1024]{2,1,0:T(8,128)(2,1)}, bf16[7,16,1024]{2,1,0:T(8,128)(2,1)S(1)}, u32[]{:S(2)}, u32[]{:S(2)}) collective-permute-start(bf16[7,16,1024]{2,1,0:T(8,128)(2,1)} %get-tuple-element.154), channel_id=1, source_target_pairs={{0,28},{4,24},{8,20},{12,16},{16,12},{20,8},{24,4},{28,0},{1,29},{... | collective-permute-start | bytes 688136 | tf_op jit(solution)/shard_map/ppermute | solution.py:505
  65.6 10.2 %copy-start.17 = (bf16[8,40,128]{2,1,0:T(8,128)(2,1)}, bf16[8,40,128]{2,1,0:T(8,128)(2,1)S(1)}, u32[]{:S(2)}) copy-start(bf16[8,40,128]{2,1,0:T(8,128)(2,1)S(1)} %collective-permute-done.7.refs_2_) | copy-start | bytes 245764
  65.6 10.2 %copy-start.18 = (bf16[8,40,128]{2,1,0:T(8,128)(2,1)}, bf16[8,40,128]{2,1,0:T(8,128)(2,1)S(1)}, u32[]{:S(2)}) copy-start(bf16[8,40,128]{2,1,0:T(8,128)(2,1)S(1)} %collective-permute-done.6.refs_1_) | copy-start | bytes 245764
  65.6 0.7 copy-start.9
  66.3 19.8 %collective-permute-start.12 = (bf16[7,16,1024]{2,1,0:T(8,128)(2,1)}, bf16[7,16,1024]{2,1,0:T(8,128)(2,1)S(1)}, u32[]{:S(2)}, u32[]{:S(2)}) collective-permute-start(bf16[7,16,1024]{2,1,0:T(8,128)(2,1)} %get-tuple-element.155), channel_id=1, source_target_pairs={{0,8},{4,12},{8,0},{12,4},{16,24},{20,28},{24,16},{28,20},{1,9},{5... | collective-permute-start | bytes 688136 | tf_op jit(solution)/shard_map/ppermute | solution.py:505
  73.9 15.0 %collective-permute-start.16 = (bf16[5,16,1024]{2,1,0:T(8,128)(2,1)}, bf16[5,16,1024]{2,1,0:T(8,128)(2,1)S(1)}, u32[]{:S(2)}, u32[]{:S(2)}) collective-permute-start(bf16[5,16,1024]{2,1,0:T(8,128)(2,1)} %get-tuple-element.165), channel_id=1, source_target_pairs={{0,28},{4,24},{8,20},{12,16},{16,12},{20,8},{24,4},{28,0},{1,29},{... | collective-permute-start | bytes 491528 | tf_op jit(solution)/shard_map/ppermute | solution.py:505
  75.7 10.3 %copy-start.19 = (bf16[5,16,1024]{2,1,0:T(8,128)(2,1)S(1)}, bf16[5,16,1024]{2,1,0:T(8,128)(2,1)}, u32[]{:S(2)}) copy-start(bf16[5,16,1024]{2,1,0:T(8,128)(2,1)} %get-tuple-element.166) | copy-start | bytes 491524
  86.1 9.5 %collective-permute-start.17 = (bf16[5,16,1024]{2,1,0:T(8,128)(2,1)S(1)}, bf16[5,16,1024]{2,1,0:T(8,128)(2,1)S(1)}, u32[]{:S(2)}, u32[]{:S(2)}) collective-permute-start(bf16[5,16,1024]{2,1,0:T(8,128)(2,1)S(1)} %copy-done.19), channel_id=1, source_target_pairs={{0,12},{4,8},{8,4},{12,0},{16,28},{20,24},{24,20},{28,16},{1,13},{... | collective-permute-start | bytes 491528 | tf_op jit(solution)/shard_map/ppermute | solution.py:505
  87.1 2.5 %collective-permute-start.13 = (bf16[8,64,128]{2,1,0:T(8,128)(2,1)}, bf16[8,64,128]{2,1,0:T(8,128)(2,1)S(1)}, u32[]{:S(2)}, u32[]{:S(2)}) collective-permute-start(bf16[8,64,128]{2,1,0:T(8,128)(2,1)} %get-tuple-element.162), channel_id=1, source_target_pairs={{0,1},{1,0},{2,3},{3,2},{4,5},{5,4},{6,7},{7,6},{8,9},{9,8},{10,11... | collective-permute-start | bytes 393224 | tf_op jit(solution)/shard_map/ppermute | solution.py:505
  87.1 6.5 %collective-permute-start.14 = (bf16[8,64,128]{2,1,0:T(8,128)(2,1)}, bf16[8,64,128]{2,1,0:T(8,128)(2,1)S(1)}, u32[]{:S(2)}, u32[]{:S(2)}) collective-permute-start(bf16[8,64,128]{2,1,0:T(8,128)(2,1)} %get-tuple-element.163), channel_id=1, source_target_pairs={{0,2},{1,3},{2,0},{3,1},{4,6},{5,7},{6,4},{7,5},{8,10},{9,11},{10,... | collective-permute-start | bytes 393224 | tf_op jit(solution)/shard_map/ppermute | solution.py:505
  88.1 7.5 %collective-permute-start.15 = (bf16[8,64,128]{2,1,0:T(8,128)(2,1)}, bf16[8,64,128]{2,1,0:T(8,128)(2,1)S(1)}, u32[]{:S(2)}, u32[]{:S(2)}) collective-permute-start(bf16[8,64,128]{2,1,0:T(8,128)(2,1)} %get-tuple-element.164), channel_id=1, source_target_pairs={{0,3},{1,2},{2,1},{3,0},{4,7},{5,6},{6,5},{7,4},{8,11},{9,10},{10,... | collective-permute-start | bytes 393224 | tf_op jit(solution)/shard_map/ppermute | solution.py:505
  96.3 25.4 %collective-permute-start.18 = (bf16[13,16,1024]{2,1,0:T(8,128)(2,1)}, bf16[13,16,1024]{2,1,0:T(8,128)(2,1)S(1)}, u32[]{:S(2)}, u32[]{:S(2)}) collective-permute-start(bf16[13,16,1024]{2,1,0:T(8,128)(2,1)} %get-tuple-element.179), channel_id=1, source_target_pairs={{0,16},{4,20},{8,24},{12,28},{16,0},{20,4},{24,8},{28,12},{1,17},{... | collective-permute-start | bytes 1277960 | tf_op jit(solution)/shard_map/ppermute | solution.py:505
  98.8 22.9 %collective-permute-start.19 = (bf16[9,16,1024]{2,1,0:T(8,128)(2,1)}, bf16[9,16,1024]{2,1,0:T(8,128)(2,1)S(1)}, u32[]{:S(2)}, u32[]{:S(2)}) collective-permute-start(bf16[9,16,1024]{2,1,0:T(8,128)(2,1)} %get-tuple-element.180), channel_id=1, source_target_pairs={{0,8},{4,12},{8,0},{12,4},{16,24},{20,28},{24,16},{28,20},{1,9},{5... | collective-permute-start | bytes 884744 | tf_op jit(solution)/shard_map/ppermute | solution.py:505
  99.2 0.9 copy-start.8
  101.2 20.5 %all-to-all-start.2 = ((bf16[8,64,128]{2,1,0:T(8,128)(2,1)}), bf16[8,64,128]{2,1,0:T(8,128)(2,1)S(1)}, u32[]{:S(2)}, u32[]{:S(2)}) async-start(bf16[8,64,128]{2,1,0:T(8,128)(2,1)} %shard_map.142), calls=%async_computation.2 | async-start | bytes 262144 | tf_op jit(solution)/shard_map/all_to_all | solution.py:644
  105.5 0.9 copy-start.5
  106.4 0.9 copy-start.7
  107.3 0.9 copy-start.10
  108.2 21.5 %copy-start.20 = (bf16[3,16,1024]{2,1,0:T(8,128)(2,1)S(1)}, bf16[3,16,1024]{2,1,0:T(8,128)(2,1)}, u32[]{:S(2)}) copy-start(bf16[3,16,1024]{2,1,0:T(8,128)(2,1)} %get-tuple-element.198) | copy-start | bytes 294916
  108.2 37.9 %copy-start.2 = (bf16[1024,512]{1,0:T(8,128)(2,1)S(1)}, bf16[1024,512]{1,0:T(8,128)(2,1)}, u32[]{:S(2)}) copy-start(bf16[1024,512]{1,0:T(8,128)(2,1)} %weight_ref.1) | copy-start | bytes 3145732
  108.2 37.9 %copy-start.13 = (s32[2]{0:T(128)S(1)}, s32[2]{0:T(128)}, u32[]{:S(2)}) copy-start(s32[2]{0:T(128)} %pad_add_fusion.me_ref) | copy-start | bytes 28
  121.7 24.5 %collective-permute-start.22 = (bf16[11,16,1024]{2,1,0:T(8,128)(2,1)}, bf16[11,16,1024]{2,1,0:T(8,128)(2,1)S(1)}, u32[]{:S(2)}, u32[]{:S(2)}) collective-permute-start(bf16[11,16,1024]{2,1,0:T(8,128)(2,1)} %get-tuple-element.199), channel_id=1, source_target_pairs={{0,12},{4,8},{8,4},{12,0},{16,28},{20,24},{24,20},{28,16},{1,13},{... | collective-permute-start | bytes 1081352 | tf_op jit(solution)/shard_map/ppermute | solution.py:505
  122.5 23.7 %collective-permute-start.20 = (bf16[10,16,1024]{2,1,0:T(8,128)(2,1)}, bf16[10,16,1024]{2,1,0:T(8,128)(2,1)S(1)}, u32[]{:S(2)}, u32[]{:S(2)}) collective-permute-start(bf16[10,16,1024]{2,1,0:T(8,128)(2,1)} %get-tuple-element.197), channel_id=1, source_target_pairs={{0,20},{4,16},{8,28},{12,24},{16,4},{20,0},{24,12},{28,8},{1,21},{... | collective-permute-start | bytes 983048 | tf_op jit(solution)/shard_map/ppermute | solution.py:505
  126.3 19.9 %all-to-all-start.3 = ((bf16[8,40,128]{2,1,0:T(8,128)(2,1)}), bf16[8,40,128]{2,1,0:T(8,128)(2,1)S(1)}, u32[]{:S(2)}, u32[]{:S(2)}) async-start(bf16[8,40,128]{2,1,0:T(8,128)(2,1)} %shard_map.144), calls=%async_computation.3 | async-start | bytes 163840 | tf_op jit(solution)/shard_map/all_to_all | solution.py:648
  129.7 16.4 %collective-permute-start.21 = (bf16[3,16,1024]{2,1,0:T(8,128)(2,1)S(1)}, bf16[3,16,1024]{2,1,0:T(8,128)(2,1)S(1)}, u32[]{:S(2)}, u32[]{:S(2)}) collective-permute-start(bf16[3,16,1024]{2,1,0:T(8,128)(2,1)S(1)} %copy-done.20), channel_id=1, source_target_pairs={{0,16},{4,20},{8,24},{12,28},{16,0},{20,4},{24,8},{28,12},{1,17},{... | collective-permute-start | bytes 294920 | tf_op jit(solution)/shard_map/ppermute | solution.py:505
  147.1 2.3 %collective-permute-start.23 = (f32[10,512]{1,0:T(8,128)S(1)}, f32[10,512]{1,0:T(8,128)S(1)}, u32[]{:S(2)}, u32[]{:S(2)}) collective-permute-start(f32[10,512]{1,0:T(8,128)S(1)} %get-tuple-element.204), channel_id=1, source_target_pairs={{0,1},{1,0},{2,3},{3,2},{4,5},{5,4},{6,7},{7,6},{8,9},{9,8},{10,11... | collective-permute-start | bytes 61448 | tf_op jit(solution)/shard_map/ppermute | solution.py:505
  147.2 4.0 %collective-permute-start.24 = (f32[10,512]{1,0:T(8,128)S(1)}, f32[10,512]{1,0:T(8,128)S(1)}, u32[]{:S(2)}, u32[]{:S(2)}) collective-permute-start(f32[10,512]{1,0:T(8,128)S(1)} %get-tuple-element.205), channel_id=1, source_target_pairs={{0,2},{1,3},{2,0},{3,1},{4,6},{5,7},{6,4},{7,5},{8,10},{9,11},{10,... | collective-permute-start | bytes 61448 | tf_op jit(solution)/shard_map/ppermute | solution.py:505
  148.2 3.4 %collective-permute-start.25 = (f32[10,512]{1,0:T(8,128)S(1)}, f32[10,512]{1,0:T(8,128)S(1)}, u32[]{:S(2)}, u32[]{:S(2)}) collective-permute-start(f32[10,512]{1,0:T(8,128)S(1)} %get-tuple-element.206), channel_id=1, source_target_pairs={{0,3},{1,2},{2,1},{3,0},{4,7},{5,6},{6,5},{7,4},{8,11},{9,10},{10,... | collective-permute-start | bytes 61448 | tf_op jit(solution)/shard_map/ppermute | solution.py:505
  149.2 12.1 %collective-permute-start.26 = (bf16[6,16,1024]{2,1,0:T(8,128)(2,1)}, bf16[6,16,1024]{2,1,0:T(8,128)(2,1)S(1)}, u32[]{:S(2)}, u32[]{:S(2)}) collective-permute-start(bf16[6,16,1024]{2,1,0:T(8,128)(2,1)} %get-tuple-element.207), channel_id=1, source_target_pairs={{0,20},{4,16},{8,28},{12,24},{16,4},{20,0},{24,12},{28,8},{1,21},{... | collective-permute-start | bytes 589832 | tf_op jit(solution)/shard_map/ppermute | solution.py:505
  (3 other events, 2.0 us)

commit v12 on v10

--- a/solution.py
+++ b/solution.py
@@ -18,7 +18,7 @@
 SCALE2 = math.log2(math.e) / math.sqrt(HD)
 STAT = 16
 MIB = 1024 * 1024
-CUTS = {1: (0, 8, 16), 2: (0, 7, 16), 3: (0, 5, 16), 4: (0, 13, 16), 5: (0, 10, 16), 6: (0, 4, 16), 7: (0, 4, 11, 16)}
+AHEAD = 5
 NT = (((1,), (1,)), ((), ()))
 
 
@@ -31,7 +31,7 @@
 
 
 def order_kernel(
-    wide, parts, me_ref, dest_ref, req_ref, idx_ref, pool_ref, out_ref, tag_ref, token_ref, *refs
+    wide, ahead, parts, me_ref, dest_ref, req_ref, idx_ref, pool_ref, out_ref, tag_ref, token_ref, *refs
 ):
     chunk_refs, refs = refs[: len(parts)], refs[len(parts) :]
     pages_ref, line_ref, source_ref, in_sem, out_sem, line_sem = refs
@@ -43,7 +43,10 @@
     dest = dest_ref[...]
     same = column(dest.astype(jnp.float32)) == dest.astype(jnp.float32)
     rank = jnp.sum(jnp.where(same & (high < low), 1.0, 0.0), axis=0, keepdims=True)
-    moved_to = ((dest ^ me_ref[0]) * capacity).astype(jnp.float32) + rank
+    rest = capacity - ahead
+    early = (dest * ahead).astype(jnp.float32) + rank
+    late = ((dest ^ me_ref[0]) * rest + wide * ahead - ahead).astype(jnp.float32) + rank
+    moved_to = jnp.where(rank < float(ahead), early, late)
     match = column(moved_to) == low.astype(jnp.float32)
     source = jnp.sum(jnp.where(match, high.astype(jnp.float32), 0.0), axis=0, keepdims=True)
     line_ref[...] = source.astype(jnp.int32)
@@ -51,9 +54,13 @@
     copy.start()
     copy.wait()
 
-    blocks = [(0, capacity, out_ref.at[pl.ds(me_ref[0] * capacity, capacity)])]
-    for (d, first, last), chunk in zip(parts, chunk_refs):
-        blocks.append((d * capacity + first, last - first, chunk))
+    own = out_ref.at[pl.ds(me_ref[0] * capacity + ahead, rest)]
+    blocks = [(wide * ahead, rest, own)]
+    for d, chunk in zip(parts, chunk_refs):
+        if d:
+            blocks.append((wide * ahead + d * rest, rest, chunk))
+        else:
+            blocks.insert(0, (0, wide * ahead, chunk))
     for c, (first, count, _) in enumerate(blocks):
 
         def start(j, carry, c=c):
@@ -99,16 +106,17 @@
         copy.wait()
 
 
-def order_pages(me, dest, page_req, page_idx, pool, wide, parts):
+def order_pages(me, dest, page_req, page_idx, pool, wide, ahead, parts):
     slots = pool.shape[0]
     part = lambda count: jax.ShapeDtypeStruct((count,) + pool.shape[1:], pool.dtype)
     out_shape = [part(slots), jax.ShapeDtypeStruct((wide, slots), jnp.float32)]
     out_shape += [jax.ShapeDtypeStruct((8, slots * PAGE), jnp.float32)]
-    out_shape += [part(last - first) for _, first, last in parts]
+    rest = slots // wide - ahead
+    out_shape += [part(rest if d else wide * ahead) for d in parts]
     vmem = pl.BlockSpec(memory_space=pltpu.VMEM)
     hbm = pl.BlockSpec(memory_space=pltpu.HBM)
     return pl.pallas_call(
-        functools.partial(order_kernel, wide, parts),
+        functools.partial(order_kernel, wide, ahead, parts),
         out_shape=out_shape,
         in_specs=[pl.BlockSpec(memory_space=pltpu.SMEM), vmem, vmem, vmem, hbm],
         out_specs=[hbm, vmem, vmem] + [hbm] * len(parts),
@@ -127,37 +135,35 @@
     )(me, dest.reshape(1, -1), page_req.reshape(1, -1), page_idx.reshape(1, -1), pool)
 
 
-def place_kernel(place_ref, *refs):
+def place_kernel(counts, place_ref, *refs):
     in_refs, (out_ref, sem) = refs[:-3], refs[-2:]
     copies = []
-    for i, chunk in enumerate(in_refs):
-        depth = chunk.shape[0]
-        copies.append(
-            pltpu.make_async_copy(
-                chunk, out_ref.at[pl.ds(place_ref[i], depth)], sem.at[i]
-            )
-        )
+    for chunk, count in zip(in_refs, counts):
+        depth = chunk.shape[0] // count
+        for i in range(count):
+            c = len(copies)
+            target = out_ref.at[pl.ds(place_ref[c], depth)]
+            source = chunk.at[pl.ds(i * depth, depth)]
+            copies.append(pltpu.make_async_copy(source, target, sem.at[c]))
     for copy in copies:
         copy.start()
     for copy in copies:
         copy.wait()
 
 
-def place_pages(place, chunks, pages):
-    count = len(chunks)
+def place_pages(place, chunks, counts, pages):
+    size = sum(chunk.size for chunk in chunks)
     return pl.pallas_call(
-        place_kernel,
+        functools.partial(place_kernel, counts),
         out_shape=jax.ShapeDtypeStruct(pages.shape, pages.dtype),
         in_specs=[pl.BlockSpec(memory_space=pltpu.SMEM)]
-        + [pl.BlockSpec(memory_space=pltpu.VMEM)] * count
+        + [pl.BlockSpec(memory_space=pltpu.VMEM)] * len(chunks)
         + [pl.BlockSpec(memory_space=pl.ANY)],
         out_specs=pl.BlockSpec(memory_space=pl.ANY),
-        scratch_shapes=[pltpu.SemaphoreType.DMA((count,))],
-        input_output_aliases={count + 1: 0},
-        compiler_params=pltpu.CompilerParams(vmem_limit_bytes=2 * count * chunks[0].size + 2 * MIB),
-        cost_estimate=pl.CostEstimate(
-            flops=0, bytes_accessed=4 * count * chunks[0].size, transcendentals=0
-        ),
+        scratch_shapes=[pltpu.SemaphoreType.DMA((sum(counts),))],
+        input_output_aliases={len(chunks) + 1: 0},
+        compiler_params=pltpu.CompilerParams(vmem_limit_bytes=2 * size + 2 * MIB),
+        cost_estimate=pl.CostEstimate(flops=0, bytes_accessed=4 * size, transcendentals=0),
     )(place, *chunks, pages)
 
 
@@ -312,7 +318,7 @@
             pltpu.VMEM((pieces, height, HD), jnp.bfloat16),
         ],
         compiler_params=pltpu.CompilerParams(vmem_limit_bytes=56 * MIB),
-        cost_estimate=pl.CostEstimate(flops=0, bytes_accessed=0, transcendentals=0),
+        cost_estimate=pl.CostEstimate(flops=1, bytes_accessed=1, transcendentals=0),
     )(me, lengths, *queries, pool, pool, keyval, keyval, token_info)
 
 
@@ -476,7 +482,7 @@
 
 
 def group_of(d, wide):
-    return d if wide <= 8 else 1 + (d - 1) * 7 // (wide - 1)
+    return d if wide <= 8 or d == 0 else 1 + (d - 1) * 7 // (wide - 1)
 
 
 def spread(block, axis):
@@ -518,38 +524,28 @@
 
     gathered = spread(hidden, "wide")
 
-    parts = []
-    for d in range(1, wide):
-        cuts = [cut * capacity // 16 for cut in CUTS[group_of(d, wide)]]
-        parts += [(d, a, b) for a, b in zip(cuts[:-1], cuts[1:]) if b > a]
+    ahead = AHEAD * capacity // 16
+    parts = list(range(0 if ahead else 1, wide))
     moved_pool, tags, token_info, *chunks = order_pages(
-        both, moves, page_req, page_idx, pool, wide, parts
-    )
+        both, moves, page_req, page_idx, pool, wide, ahead, parts
+    )
+    chunks = dict(zip(parts, chunks))
     arrived = {}
     flying = {}
 
-    def members(names):
-        taken = []
-        for group, which in names:
-            cut = CUTS[group][which] * capacity // 16
-            end = CUTS[group][which + 1] * capacity // 16
-            taken += [
-                c
-                for c, (d, first, last) in enumerate(parts)
-                if group_of(d, wide) == group and (first, last) == (cut, end)
-            ]
-        return taken
-
-    def launch(values, *names):
-        taken = members(names)
-        values, sent = lax.optimization_barrier((values, [chunks[c] for c in taken]))
-        for c, chunk in zip(taken, sent):
-            flying[c] = send(chunk, "wide", parts[c][0])
+    def members(groups):
+        return [d for group in groups for d in parts if group_of(d, wide) == group]
+
+    def launch(values, *groups):
+        taken = members(groups)
+        values, sent = lax.optimization_barrier((values, [chunks[d] for d in taken]))
+        for d, chunk in zip(taken, sent):
+            flying[d] = send(chunk, "wide", d) if d else exchange(chunk, "wide")
         return values
 
-    def land(values, *names):
-        taken = members(names)
-        values, got = lax.optimization_barrier((values, [flying[c] for c in taken]))
+    def land(values, *groups):
+        taken = members(groups)
+        values, got = lax.optimization_barrier((values, [flying[d] for d in taken]))
         arrived.update(zip(taken, got))
         return values
 
@@ -558,8 +554,12 @@
 
     def placed(pages):
         taken = sorted(arrived)
-        place = jnp.stack([(me ^ parts[c][0]) * capacity + parts[c][1] for c in taken])
-        pages = place_pages(place, [arrived[c] for c in taken], pages)
+        place = []
+        for d in taken:
+            place += [(me ^ d) * capacity + ahead] if d else [w * capacity for w in range(wide)]
+        place = jnp.stack([jnp.asarray(index, jnp.int32) for index in place])
+        counts = [1 if d else wide for d in taken]
+        pages = place_pages(place, [arrived[d] for d in taken], counts, pages)
         arrived.clear()
         return pages
 
@@ -575,7 +575,7 @@
             w_keyval,
             scratch=[pltpu.VMEM((rows, narrow * HD), jnp.float32)],
         )
-        partial = beside(lambda value: deal(value, "narrow"), partial, (6, 0), (1, 0))
+        partial = deal(partial, "narrow")
         packed = in_vmem(
             functools.partial(pack_kernel, narrow),
             jax.ShapeDtypeStruct((wide, rows + wide, 2 * HD), jnp.bfloat16),
@@ -583,7 +583,8 @@
             *partial,
             tags,
         )
-        received = beside(lambda value: exchange(value, "wide"), packed, (6, 1))
+        received = beside(lambda value: exchange(value, "wide"), packed, 6, 1)
+        received = launch(received, 0)
         queries, keyval, new_entries, moved_req, moved_idx = in_vmem(
             functools.partial(unpack_kernel, rows),
             [
@@ -597,7 +598,7 @@
             received,
         )
         moved_req, moved_idx = moved_req.reshape(slots), moved_idx.reshape(slots)
-        queries = beside(lambda value: share(value, "narrow"), queries, (7, 0), (1, 1))
+        queries = share(queries, "narrow")
     else:
         gathered = gathered.reshape(rows, -1)
         query_part = jnp.dot(gathered, w_query, preferred_element_type=jnp.float32)
@@ -606,16 +607,17 @@
         partial = jnp.concatenate(
             [query_part, jnp.broadcast_to(keyval_part[None], (narrow,) + keyval_part.shape)], axis=2
         )
-        partial = beside(lambda value: exchange(value, "narrow"), partial, (6, 0), (1, 0))
+        partial = exchange(partial, "narrow")
         projected = jnp.sum(partial, axis=0).astype(jnp.bfloat16)
         tags = tags[:, : 3 * capacity].astype(jnp.bfloat16)[:, None]
         tags = jnp.pad(tags, ((0, 0), (0, 7), (0, projected.shape[1] - tags.shape[2])))
         packed = jnp.broadcast_to(projected[None], (wide,) + projected.shape)
         packed = jnp.concatenate([packed, tags], axis=1)
-        received = beside(lambda value: exchange(value, "wide"), packed, (6, 1))
+        received = beside(lambda value: exchange(value, "wide"), packed, 6, 1)
+        received = launch(received, 0)
         tags_in = received[:, rows]
         queries = received[:, :rows, :own_cols]
-        queries = beside(lambda value: spread(value, "narrow"), queries, (7, 0), (1, 1))
+        queries = spread(queries, "narrow")
         queries = jnp.transpose(queries, (2, 1, 0, 3)).reshape(rows, HEADS, HD)
         queries = [jnp.transpose(queries, (1, 0, 2)).reshape(KVH, GROUPS * rows, HD)]
         keyval = jnp.transpose(received[:, :rows, own_cols:], (1, 0, 2)).reshape(rows, -1)
@@ -633,25 +635,20 @@
             step_ids < kept[:, None, None], fresh, jnp.zeros((), jnp.bfloat16)
         )
 
-    mixed = beside(
-        lambda value: attend(both, lengths, value, keyval, tokens, token_info, rows, piece),
-        queries,
-        (7, 1),
-        (2, 0),
-    )
+    mixed = attend(both, lengths, queries, keyval, tokens, token_info, rows, piece)
     if direct:
-        mixed = beside(lambda value: deal(value, "narrow"), mixed, (7, 2), (3, 0))
+        mixed = land(deal(mixed, "narrow"), 0)
     else:
-        mixed = beside(lambda value: exchange(value, "narrow"), mixed[0], (7, 2), (3, 0))
+        mixed = land(exchange(mixed[0], "narrow"), 0)
         mixed = mixed.reshape((narrow, wide) + mixed.shape[1:])
         mixed = [mixed[i] for i in range(narrow)]
     mixed = combine(mixed, piece)
     mixed, pages = lax.optimization_barrier((mixed, moved_pool))
     pages = placed(pages)
-    mixed = beside(lambda value: exchange(value, "wide"), mixed, (4, 0), (2, 1))
+    mixed = beside(lambda value: exchange(value, "wide"), mixed, 4, 2)
     mixed, moved_pool = lax.optimization_barrier((mixed, pages))
     attn = combine([mixed], piece, wide)
-    attn = beside(lambda value: exchange(value, "wide"), attn, (5, 0), (4, 1), (3, 1))
+    attn = beside(lambda value: exchange(value, "wide"), attn, 5, 3)
     if direct:
         sums = in_vmem(
             functools.partial(finish_kernel, narrow),
@@ -660,13 +657,13 @@
             attn,
             w_out,
         )
-        sums = beside(lambda value: deal(value, "narrow"), sums, (5, 1))
+        sums = beside(lambda value: deal(value, "narrow"), sums, 7)
         attended = ((sums[0] + sums[1]) + (sums[2] + sums[3])).astype(jnp.bfloat16)
     else:
         attn = jnp.transpose(attn.reshape(-1, rows, HD), (1, 0, 2)).reshape(rows, -1)
         sums = jnp.dot(attn, w_out, preferred_element_type=jnp.float32)
         sums = sums.reshape(narrow, rows // narrow, -1)
-        sums = beside(lambda value: exchange(value, "narrow"), sums, (5, 1))
+        sums = beside(lambda value: exchange(value, "narrow"), sums, 7)
         attended = jnp.sum(sums, axis=0).astype(jnp.bfloat16)
     moved_pool = placed(moved_pool)
     return (attended, new_entries, moved_pool, moved_req, moved_idx)

time: 156 us -> 153 us (0.981)
  the two profiles are of different devices: /device:TPU:0 before, /device:TPU:8 now
where the time goes in v12:
time: 153 us; the launch traced here: 152 us
  waiting for transfers between devices  40.8 us (27%)
  blocking collectives  39.9 us (26%)
  starting transfers between devices  34.6 us (23%)
  Pallas kernels  24.2 us (16%)
  local copies, waits for them, and re-layouts  10.7 us (7%)
    ppermute x19, waiting for transfers between devices, send(): lax.ppermute(block, axis, [(i, i ^ d) for i in range(lax.axis_size(axis))])  26 us
    all_to_all x1, blocking collectives, on_device(): received = beside(lambda value: exchange(value, 'wide'), packed, 6, 1)  21.9 us
    all_to_all x1, blocking collectives, on_device(): attn = beside(lambda value: exchange(value, 'wide'), attn, 5, 3)  18 us
    ppermute x19, starting transfers between devices, send(): lax.ppermute(block, axis, [(i, i ^ d) for i in range(lax.axis_size(axis))])  17.6 us
    pallas_call x1, Pallas kernels, attend(): pl.pallas_call(functools.partial(attend_kernel, rows, piece, peers), grid...  10.2 us
    all_to_all x1, waiting for transfers between devices, on_device(): mixed = beside(lambda value: exchange(value, 'wide'), mixed, 4, 2)  9.76 us
    unnamed x36, local copies, waits for them, and re-layouts  9.18 us
    all_to_all x1, starting transfers between devices, spread(): lax.all_to_all(jnp.broadcast_to(block[None], (count,) + block.shape), axi...  6.28 us
  transfers between devices with their start and end apart: 22, of which 9 were waited for; matrix products, arithmetic and copies ran while one was open for 0% of the time, Pallas kernels for 13%

profile of v12, /device:TPU:8, one launch (start us, length us, event | category | flops | bytes accessed | tf_op | source)
XLA Modules:
  0.0 151.8 jit_solution(5088788886698927870)
XLA Ops:
  0.6 1.4 broadcast_in_dim.2
  2.0 6.3 %all-to-all-start = ((bf16[8,5,1024]{2,1,0:T(8,128)(2,1)}), bf16[8,5,1024]{2,1,0:T(8,128)(2,1)S(1)}, u32[]{:S(2)}, u32[]{:S(2)}) async-start(bf16[8,5,1024]{2,1,0:T(8,128)(2,1)} %broadcast_in_dim.2), calls=%async_computation | async-start | bytes 262144 | tf_op jit(solution)/shard_map/all_to_all | solution.py:490
  8.4 5.1 %all-to-all-done.hidden_ref = bf16[8,5,1024]{2,1,0:T(8,128)(2,1)S(1)} async-done(((bf16[8,5,1024]{2,1,0:T(8,128)(2,1)}), bf16[8,5,1024]{2,1,0:T(8,128)(2,1)S(1)}, u32[]{:S(2)}, u32[]{:S(2)}) %all-to-all-start) | async-done | bytes 81952 | tf_op jit(solution)/shard_map/all_to_all | solution.py:490
  13.5 1.2 copy-done.1
  14.7 0.9 copy-done.7
  15.7 1.0 shard_map.137
  16.7 1.6 %collective-permute-start.1 = (f32[40,256]{1,0:T(8,128)S(1)}, f32[40,256]{1,0:T(8,128)S(1)}, u32[]{:S(2)}, u32[]{:S(2)}) collective-permute-start(f32[40,256]{1,0:T(8,128)S(1)} %get-tuple-element.74), channel_id=1, source_target_pairs={{0,2},{1,3},{2,0},{3,1},{4,6},{5,7},{6,4},{7,5},{8,10},{9,11},{10,... | collective-permute-start | bytes 122888 | tf_op jit(solution)/shard_map/ppermute | solution.py:517
  18.6 5.7 %shard_map.138 = (bf16[128,16,1024]{2,1,0:T(8,128)(2,1)}, f32[8,128]{1,0:T(8,128)}, f32[8,2048]{1,0:T(8,128)}, bf16[40,16,1024]{2,1,0:T(8,128)(2,1)}, bf16[11,16...) custom-call(s32[2]{0:T(128)} %copy-done.10, ...), custom_call_target="tpu_custom_call" | custom-call | bytes 8388608 | tf_op jit(solution)/shard_map/pallas_call | solution.py:118
  24.3 0.7 copy-done.13
  25.0 1.2 collective-permute-start.3
  26.2 0.4 collective-permute-start.4
  26.6 21.9 %all_to_all.25.part_ref = bf16[8,48,256]{2,1,0:T(8,128)(2,1)S(1)} all-to-all(bf16[8,48,256]{2,1,0:T(8,128)(2,1)S(1)} %shard_map.139), channel_id=1, replica_groups=mesh['wide'=8,'narrow'=4] {'wide'}, dimensions={0} | all-to-all | bytes 393216 | tf_op jit(solution)/shard_map/all_to_all | solution.py:586
  48.5 0.7 copy-done.3
  49.2 0.7 copy-done.5
  50.0 4.7 %all-to-all-start.2 = ((bf16[40,16,1024]{2,1,0:T(8,128)(2,1)}), bf16[40,16,1024]{2,1,0:T(8,128)(2,1)S(1)}, u32[]{:S(2)}, u32[]{:S(2)}) async-start(bf16[40,16,1024]{2,1,0:T(8,128)(2,1)} %get-tuple-element.92), calls=%async_computation.2 | async-start | bytes 2621440 | tf_op jit(solution)/shard_map/all_to_all | solution.py:543
  54.7 0.6 copy-done.11
  55.3 1.4 shard_map.140
  56.7 0.7 copy-done
  57.4 1.5 %collective-permute-start.6 = (bf16[8,40,128]{2,1,0:T(8,128)(2,1)S(1)}, bf16[8,40,128]{2,1,0:T(8,128)(2,1)S(1)}, u32[]{:S(2)}, u32[]{:S(2)}) collective-permute-start(bf16[8,40,128]{2,1,0:T(8,128)(2,1)S(1)} %get-tuple-element.85.refs_0_), channel_id=1, source_target_pairs={{0,2},{1,3},{2,0},{3,1},{4,6},{5,7},{6,4},{7,5},{8,10},{9,11},{10,... | collective-permute-start | bytes 245768 | tf_op jit(solution)/shard_map/ppermute | solution.py:517
  58.9 0.3 collective-permute-start.5
  59.2 2.8 %collective-permute-done.7.refs_3_ = bf16[8,40,128]{2,1,0:T(8,128)(2,1)S(1)} collective-permute-done((bf16[8,40,128]{2,1,0:T(8,128)(2,1)S(1)}, bf16[8,40,128]{2,1,0:T(8,128)(2,1)S(1)}, u32[]{:S(2)}, u32[]{:S(2)}) %collective-permute-start.7) | collective-permute-done | bytes 81952 | tf_op jit(solution)/shard_map/ppermute | solution.py:517
  62.1 1.8 %collective-permute-done.6.refs_2_ = bf16[8,40,128]{2,1,0:T(8,128)(2,1)S(1)} collective-permute-done((bf16[8,40,128]{2,1,0:T(8,128)(2,1)S(1)}, bf16[8,40,128]{2,1,0:T(8,128)(2,1)S(1)}, u32[]{:S(2)}, u32[]{:S(2)}) %collective-permute-start.6) | collective-permute-done | bytes 81952 | tf_op jit(solution)/shard_map/ppermute | solution.py:517
  63.9 0.6 copy-done.16
  64.5 10.2 %shard_map.141 = (bf16[8,64,128]{2,1,0:T(8,128)(2,1)}, bf16[8,64,128]{2,1,0:T(8,128)(2,1)}, bf16[8,64,128]{2,1,0:T(8,128)(2,1)}, bf16[8,64,128]{2,1,0:T(8,128)(2,1)}) custom-call(s32[2]{0:T(128)} %copy-done.10, s32[8]{0:T(128)} %length_ref.1, bf16[8,40,128]{2,1,0:T(8,128)(2,1)} %copy-done.9, bf16[8,40,128]{2,1,0:T(8,128)(2,1)} %copy-done.17, ...), custom_call_target="tpu_custom_call" | custom-call | flops 1 | bytes 1 | tf_op jit(solution)/shard_map/pallas_call | solution.py:298
  74.9 0.7 collective-permute-start.9
  75.5 1.1 collective-permute-start.10
  76.7 4.7 %collective-permute-done.9.refs_2_ = bf16[8,64,128]{2,1,0:T(8,128)(2,1)S(1)} collective-permute-done((bf16[8,64,128]{2,1,0:T(8,128)(2,1)}, bf16[8,64,128]{2,1,0:T(8,128)(2,1)S(1)}, u32[]{:S(2)}, u32[]{:S(2)}) %collective-permute-start.9) | collective-permute-done | bytes 131104 | tf_op jit(solution)/shard_map/ppermute | solution.py:517
  81.4 1.9 %collective-permute-done.10.refs_3_ = bf16[8,64,128]{2,1,0:T(8,128)(2,1)S(1)} collective-permute-done((bf16[8,64,128]{2,1,0:T(8,128)(2,1)}, bf16[8,64,128]{2,1,0:T(8,128)(2,1)S(1)}, u32[]{:S(2)}, u32[]{:S(2)}) %collective-permute-start.10) | collective-permute-done | bytes 131104 | tf_op jit(solution)/shard_map/ppermute | solution.py:517
  83.3 0.9 copy-done.8
  84.2 1.1 shard_map.142
  85.3 2.4 %collective-permute-start.11 = (bf16[11,16,1024]{2,1,0:T(8,128)(2,1)}, bf16[11,16,1024]{2,1,0:T(8,128)(2,1)S(1)}, u32[]{:S(2)}, u32[]{:S(2)}) collective-permute-start(bf16[11,16,1024]{2,1,0:T(8,128)(2,1)} %get-tuple-element.102), channel_id=1, source_target_pairs={{0,16},{4,20},{8,24},{12,28},{16,0},{20,4},{24,8},{28,12},{1,17},{... | collective-permute-start | bytes 1081352 | tf_op jit(solution)/shard_map/ppermute | solution.py:517
  87.7 0.6 collective-permute-start.12
  88.3 6.0 %all-to-all-start.3 = ((bf16[8,64,128]{2,1,0:T(8,128)(2,1)}), bf16[8,64,128]{2,1,0:T(8,128)(2,1)S(1)}, u32[]{:S(2)}, u32[]{:S(2)}) async-start(bf16[8,64,128]{2,1,0:T(8,128)(2,1)} %shard_map.142), calls=%async_computation.3 | async-start | bytes 262144 | tf_op jit(solution)/shard_map/all_to_all | solution.py:648
  94.3 1.0 copy-done.4
  95.3 1.0 copy-done.6
  96.3 1.9 %shard_map.143.refs_5_ = bf16[128,16,1024]{2,1,0:T(8,128)(2,1)} custom-call(s32[10]{0:T(128)S(1)} %stack.41.place_ref, bf16[40,16,1024]{2,1,0:T(8,128)(2,1)S(1)} %all-to-all-done.2.refs_0_, bf16[11,16,1024]{2,1,0:T(8,128)(2,1)S(1)} %copy-done.6, bf16[11,16,1024]{2,1,0:T(8,128)(2,1)S(1)} %copy-done.4, ...), custom_call_target="tpu_custom_call", output_to_operand_aliasing={{}: (4, {})} | custom-call | bytes 4063232 | tf_op jit(solution)/shard_map/pallas_call | solution.py:156
  98.2 9.8 %all-to-all-done.3.refs_0_ = bf16[8,64,128]{2,1,0:T(8,128)(2,1)S(1)} async-done(((bf16[8,64,128]{2,1,0:T(8,128)(2,1)}), bf16[8,64,128]{2,1,0:T(8,128)(2,1)S(1)}, u32[]{:S(2)}, u32[]{:S(2)}) %all-to-all-start.3) | async-done | bytes 131104 | tf_op jit(solution)/shard_map/all_to_all | solution.py:648
  108.2 3.0 %collective-permute-start.13 = (bf16[11,16,1024]{2,1,0:T(8,128)(2,1)}, bf16[11,16,1024]{2,1,0:T(8,128)(2,1)S(1)}, u32[]{:S(2)}, u32[]{:S(2)}) collective-permute-start(bf16[11,16,1024]{2,1,0:T(8,128)(2,1)} %get-tuple-element.113), channel_id=1, source_target_pairs={{0,20},{4,16},{8,28},{12,24},{16,4},{20,0},{24,12},{28,8},{1,21},{... | collective-permute-start | bytes 1081352 | tf_op jit(solution)/shard_map/ppermute | solution.py:517
  111.2 1.2 collective-permute-start.14
  112.4 18.0 %all_to_all.26.part_ref = bf16[8,40,128]{2,1,0:T(8,128)(2,1)S(1)} all-to-all(bf16[8,40,128]{2,1,0:T(8,128)(2,1)S(1)} %shard_map.144), channel_id=1, replica_groups=mesh['wide'=8,'narrow'=4] {'wide'}, dimensions={0} | all-to-all | bytes 163840 | tf_op jit(solution)/shard_map/all_to_all | solution.py:651
  130.4 0.9 shard_map.145
  131.4 1.4 collective-permute-start.18
  132.8 0.7 collective-permute-start.16
  133.5 1.1 collective-permute-start.17
  134.7 2.1 %collective-permute-done.16 = f32[10,512]{1,0:T(8,128)S(1)} collective-permute-done((f32[10,512]{1,0:T(8,128)S(1)}, f32[10,512]{1,0:T(8,128)S(1)}, u32[]{:S(2)}, u32[]{:S(2)}) %collective-permute-start.16) | collective-permute-done | bytes 20512 | tf_op jit(solution)/shard_map/ppermute | solution.py:517
  137.2 12.2 %collective-permute-done.18.refs_4_ = bf16[11,16,1024]{2,1,0:T(8,128)(2,1)S(1)} collective-permute-done((bf16[11,16,1024]{2,1,0:T(8,128)(2,1)}, bf16[11,16,1024]{2,1,0:T(8,128)(2,1)S(1)}, u32[]{:S(2)}, u32[]{:S(2)}) %collective-permute-start.18) | collective-permute-done | bytes 360480 | tf_op jit(solution)/shard_map/ppermute | solution.py:517
  149.4 0.6 add_convert_fusion
  150.0 1.8 %shard_map.146 = bf16[128,16,1024]{2,1,0:T(8,128)(2,1)} custom-call(s32[5]{0:T(128)S(1)} %stack.47.place_ref, bf16[11,16,1024]{2,1,0:T(8,128)(2,1)S(1)} %collective-permute-done.12.refs_0_, bf16[11,16,1024]{2,1,0:T(8,128)(2,1)S(1)} %collective-permute-done.14.refs_1_, ...), custom_call_target="tpu_custom_call", output_to_operand_aliasing={{}: (6, {})} | custom-call | bytes 3604480 | tf_op jit(solution)/shard_map/pallas_call | solution.py:156
  (49 shorter events, 1.4 us)
Async XLA Ops:
  2.0 11.5 %all-to-all-start = ((bf16[8,5,1024]{2,1,0:T(8,128)(2,1)}), bf16[8,5,1024]{2,1,0:T(8,128)(2,1)S(1)}, u32[]{:S(2)}, u32[]{:S(2)}) async-start(bf16[8,5,1024]{2,1,0:T(8,128)(2,1)} %broadcast_in_dim.2), calls=%async_computation | async-start | bytes 262144 | tf_op jit(solution)/shard_map/all_to_all | solution.py:490
  8.4 10.2 %copy-start.10 = (s32[2]{0:T(128)}, s32[2]{0:T(128)S(1)}, u32[]{:S(2)}) copy-start(s32[2]{0:T(128)S(1)} %pad_add_fusion.me_ref) | copy-start | bytes 28
  13.5 1.2 copy-start.1
  14.7 0.9 copy-start.7
  15.7 39.1 %copy-start.14 = (s32[8]{0:T(128)S(1)}, s32[8]{0:T(128)}, u32[]{:S(2)}) copy-start(s32[8]{0:T(128)} %kept_ref.1) | copy-start | bytes 100
  16.6 7.6 %collective-permute-start = (f32[40,256]{1,0:T(8,128)S(1)}, f32[40,256]{1,0:T(8,128)S(1)}, u32[]{:S(2)}, u32[]{:S(2)}) collective-permute-start(f32[40,256]{1,0:T(8,128)S(1)} %get-tuple-element.73), channel_id=1, source_target_pairs={{0,1},{1,0},{2,3},{3,2},{4,5},{5,4},{6,7},{7,6},{8,9},{9,8},{10,11... | collective-permute-start | bytes 122888 | tf_op jit(solution)/shard_map/ppermute | solution.py:517
  16.7 7.5 %collective-permute-start.1 = (f32[40,256]{1,0:T(8,128)S(1)}, f32[40,256]{1,0:T(8,128)S(1)}, u32[]{:S(2)}, u32[]{:S(2)}) collective-permute-start(f32[40,256]{1,0:T(8,128)S(1)} %get-tuple-element.74), channel_id=1, source_target_pairs={{0,2},{1,3},{2,0},{3,1},{4,6},{5,7},{6,4},{7,5},{8,10},{9,11},{10,... | collective-permute-start | bytes 122888 | tf_op jit(solution)/shard_map/ppermute | solution.py:517
  18.3 6.0 %collective-permute-start.2 = (f32[40,256]{1,0:T(8,128)S(1)}, f32[40,256]{1,0:T(8,128)S(1)}, u32[]{:S(2)}, u32[]{:S(2)}) collective-permute-start(f32[40,256]{1,0:T(8,128)S(1)} %get-tuple-element.75), channel_id=1, source_target_pairs={{0,3},{1,2},{2,1},{3,0},{4,7},{5,6},{6,5},{7,4},{8,11},{9,10},{10,... | collective-permute-start | bytes 122888 | tf_op jit(solution)/shard_map/ppermute | solution.py:517
  24.3 0.7 copy-start.13
  25.0 23.5 %collective-permute-start.3 = (bf16[11,16,1024]{2,1,0:T(8,128)(2,1)}, bf16[11,16,1024]{2,1,0:T(8,128)(2,1)S(1)}, u32[]{:S(2)}, u32[]{:S(2)}) collective-permute-start(bf16[11,16,1024]{2,1,0:T(8,128)(2,1)} %get-tuple-element.80), channel_id=1, source_target_pairs={{0,24},{4,28},{8,16},{12,20},{16,8},{20,12},{24,0},{28,4},{1,25},{... | collective-permute-start | bytes 1081352 | tf_op jit(solution)/shard_map/ppermute | solution.py:517
  26.2 23.1 %collective-permute-start.4 = (bf16[11,16,1024]{2,1,0:T(8,128)(2,1)}, bf16[11,16,1024]{2,1,0:T(8,128)(2,1)S(1)}, u32[]{:S(2)}, u32[]{:S(2)}) collective-permute-start(bf16[11,16,1024]{2,1,0:T(8,128)(2,1)} %get-tuple-element.81), channel_id=1, source_target_pairs={{0,4},{4,0},{8,12},{12,8},{16,20},{20,16},{24,28},{28,24},{1,5},{5... | collective-permute-start | bytes 1081352 | tf_op jit(solution)/shard_map/ppermute | solution.py:517
  48.5 0.7 copy-start.3
  49.2 0.7 copy-start.5
  50.0 33.4 %all-to-all-start.2 = ((bf16[40,16,1024]{2,1,0:T(8,128)(2,1)}), bf16[40,16,1024]{2,1,0:T(8,128)(2,1)S(1)}, u32[]{:S(2)}, u32[]{:S(2)}) async-start(bf16[40,16,1024]{2,1,0:T(8,128)(2,1)} %get-tuple-element.92), calls=%async_computation.2 | async-start | bytes 2621440 | tf_op jit(solution)/shard_map/all_to_all | solution.py:543
  54.7 0.6 copy-start.11
  56.7 0.7 copy-start
  57.4 6.5 %copy-start.9 = (bf16[8,40,128]{2,1,0:T(8,128)(2,1)}, bf16[8,40,128]{2,1,0:T(8,128)(2,1)S(1)}, u32[]{:S(2)}) copy-start(bf16[8,40,128]{2,1,0:T(8,128)(2,1)S(1)} %get-tuple-element.85.refs_0_) | copy-start | bytes 245764
  57.4 4.7 %collective-permute-start.7 = (bf16[8,40,128]{2,1,0:T(8,128)(2,1)S(1)}, bf16[8,40,128]{2,1,0:T(8,128)(2,1)S(1)}, u32[]{:S(2)}, u32[]{:S(2)}) collective-permute-start(bf16[8,40,128]{2,1,0:T(8,128)(2,1)S(1)} %get-tuple-element.85.refs_0_), channel_id=1, source_target_pairs={{0,3},{1,2},{2,1},{3,0},{4,7},{5,6},{6,5},{7,4},{8,11},{9,10},{10,... | collective-permute-start | bytes 245768 | tf_op jit(solution)/shard_map/ppermute | solution.py:517
  57.4 6.5 %collective-permute-start.6 = (bf16[8,40,128]{2,1,0:T(8,128)(2,1)S(1)}, bf16[8,40,128]{2,1,0:T(8,128)(2,1)S(1)}, u32[]{:S(2)}, u32[]{:S(2)}) collective-permute-start(bf16[8,40,128]{2,1,0:T(8,128)(2,1)S(1)} %get-tuple-element.85.refs_0_), channel_id=1, source_target_pairs={{0,2},{1,3},{2,0},{3,1},{4,6},{5,7},{6,4},{7,5},{8,10},{9,11},{10,... | collective-permute-start | bytes 245768 | tf_op jit(solution)/shard_map/ppermute | solution.py:517
  58.9 5.0 %collective-permute-start.5 = (bf16[8,40,128]{2,1,0:T(8,128)(2,1)S(1)}, bf16[8,40,128]{2,1,0:T(8,128)(2,1)S(1)}, u32[]{:S(2)}, u32[]{:S(2)}) collective-permute-start(bf16[8,40,128]{2,1,0:T(8,128)(2,1)S(1)} %get-tuple-element.85.refs_0_), channel_id=1, source_target_pairs={{0,1},{1,0},{2,3},{3,2},{4,5},{5,4},{6,7},{7,6},{8,9},{9,8},{10,11... | collective-permute-start | bytes 245768 | tf_op jit(solution)/shard_map/ppermute | solution.py:517
  62.1 1.8 %copy-start.15 = (bf16[8,40,128]{2,1,0:T(8,128)(2,1)}, bf16[8,40,128]{2,1,0:T(8,128)(2,1)S(1)}, u32[]{:S(2)}) copy-start(bf16[8,40,128]{2,1,0:T(8,128)(2,1)S(1)} %collective-permute-done.7.refs_3_) | copy-start | bytes 245764
  63.9 0.6 copy-start.16
  63.9 0.7 copy-start.17
  74.8 1.9 %collective-permute-start.8 = (bf16[8,64,128]{2,1,0:T(8,128)(2,1)}, bf16[8,64,128]{2,1,0:T(8,128)(2,1)S(1)}, u32[]{:S(2)}, u32[]{:S(2)}) collective-permute-start(bf16[8,64,128]{2,1,0:T(8,128)(2,1)} %get-tuple-element.89), channel_id=1, source_target_pairs={{0,1},{1,0},{2,3},{3,2},{4,5},{5,4},{6,7},{7,6},{8,9},{9,8},{10,11... | collective-permute-start | bytes 393224 | tf_op jit(solution)/shard_map/ppermute | solution.py:517
  74.9 6.5 %collective-permute-start.9 = (bf16[8,64,128]{2,1,0:T(8,128)(2,1)}, bf16[8,64,128]{2,1,0:T(8,128)(2,1)S(1)}, u32[]{:S(2)}, u32[]{:S(2)}) collective-permute-start(bf16[8,64,128]{2,1,0:T(8,128)(2,1)} %get-tuple-element.90), channel_id=1, source_target_pairs={{0,2},{1,3},{2,0},{3,1},{4,6},{5,7},{6,4},{7,5},{8,10},{9,11},{10,... | collective-permute-start | bytes 393224 | tf_op jit(solution)/shard_map/ppermute | solution.py:517
  75.5 7.8 %collective-permute-start.10 = (bf16[8,64,128]{2,1,0:T(8,128)(2,1)}, bf16[8,64,128]{2,1,0:T(8,128)(2,1)S(1)}, u32[]{:S(2)}, u32[]{:S(2)}) collective-permute-start(bf16[8,64,128]{2,1,0:T(8,128)(2,1)} %get-tuple-element.91), channel_id=1, source_target_pairs={{0,3},{1,2},{2,1},{3,0},{4,7},{5,6},{6,5},{7,4},{8,11},{9,10},{10,... | collective-permute-start | bytes 393224 | tf_op jit(solution)/shard_map/ppermute | solution.py:517
  83.3 0.9 copy-start.8
  85.3 22.6 %collective-permute-start.11 = (bf16[11,16,1024]{2,1,0:T(8,128)(2,1)}, bf16[11,16,1024]{2,1,0:T(8,128)(2,1)S(1)}, u32[]{:S(2)}, u32[]{:S(2)}) collective-permute-start(bf16[11,16,1024]{2,1,0:T(8,128)(2,1)} %get-tuple-element.102), channel_id=1, source_target_pairs={{0,16},{4,20},{8,24},{12,28},{16,0},{20,4},{24,8},{28,12},{1,17},{... | collective-permute-start | bytes 1081352 | tf_op jit(solution)/shard_map/ppermute | solution.py:517
  87.7 20.3 %collective-permute-start.12 = (bf16[11,16,1024]{2,1,0:T(8,128)(2,1)}, bf16[11,16,1024]{2,1,0:T(8,128)(2,1)S(1)}, u32[]{:S(2)}, u32[]{:S(2)}) collective-permute-start(bf16[11,16,1024]{2,1,0:T(8,128)(2,1)} %get-tuple-element.103), channel_id=1, source_target_pairs={{0,8},{4,12},{8,0},{12,4},{16,24},{20,28},{24,16},{28,20},{1,9},{5... | collective-permute-start | bytes 1081352 | tf_op jit(solution)/shard_map/ppermute | solution.py:517
  88.3 19.7 %all-to-all-start.3 = ((bf16[8,64,128]{2,1,0:T(8,128)(2,1)}), bf16[8,64,128]{2,1,0:T(8,128)(2,1)S(1)}, u32[]{:S(2)}, u32[]{:S(2)}) async-start(bf16[8,64,128]{2,1,0:T(8,128)(2,1)} %shard_map.142), calls=%async_computation.3 | async-start | bytes 262144 | tf_op jit(solution)/shard_map/all_to_all | solution.py:648
  94.3 1.0 copy-start.4
  95.3 1.0 copy-start.6
  96.3 34.1 %copy-start.2 = (bf16[1024,512]{1,0:T(8,128)(2,1)S(1)}, bf16[1024,512]{1,0:T(8,128)(2,1)}, u32[]{:S(2)}) copy-start(bf16[1024,512]{1,0:T(8,128)(2,1)} %weight_ref.1) | copy-start | bytes 3145732
  96.3 34.1 %copy-start.12 = (s32[2]{0:T(128)S(1)}, s32[2]{0:T(128)}, u32[]{:S(2)}) copy-start(s32[2]{0:T(128)} %copy-done.10) | copy-start | bytes 28
  108.2 22.2 %collective-permute-start.13 = (bf16[11,16,1024]{2,1,0:T(8,128)(2,1)}, bf16[11,16,1024]{2,1,0:T(8,128)(2,1)S(1)}, u32[]{:S(2)}, u32[]{:S(2)}) collective-permute-start(bf16[11,16,1024]{2,1,0:T(8,128)(2,1)} %get-tuple-element.113), channel_id=1, source_target_pairs={{0,20},{4,16},{8,28},{12,24},{16,4},{20,0},{24,12},{28,8},{1,21},{... | collective-permute-start | bytes 1081352 | tf_op jit(solution)/shard_map/ppermute | solution.py:517
  111.2 19.2 %collective-permute-start.14 = (bf16[11,16,1024]{2,1,0:T(8,128)(2,1)}, bf16[11,16,1024]{2,1,0:T(8,128)(2,1)S(1)}, u32[]{:S(2)}, u32[]{:S(2)}) collective-permute-start(bf16[11,16,1024]{2,1,0:T(8,128)(2,1)} %get-tuple-element.114), channel_id=1, source_target_pairs={{0,12},{4,8},{8,4},{12,0},{16,28},{20,24},{24,20},{28,16},{1,13},{... | collective-permute-start | bytes 1081352 | tf_op jit(solution)/shard_map/ppermute | solution.py:517
  131.4 18.0 %collective-permute-start.18 = (bf16[11,16,1024]{2,1,0:T(8,128)(2,1)}, bf16[11,16,1024]{2,1,0:T(8,128)(2,1)S(1)}, u32[]{:S(2)}, u32[]{:S(2)}) collective-permute-start(bf16[11,16,1024]{2,1,0:T(8,128)(2,1)} %get-tuple-element.125), channel_id=1, source_target_pairs={{0,28},{4,24},{8,20},{12,16},{16,12},{20,8},{24,4},{28,0},{1,29},{... | collective-permute-start | bytes 1081352 | tf_op jit(solution)/shard_map/ppermute | solution.py:517
  132.8 1.9 %collective-permute-start.15 = (f32[10,512]{1,0:T(8,128)S(1)}, f32[10,512]{1,0:T(8,128)S(1)}, u32[]{:S(2)}, u32[]{:S(2)}) collective-permute-start(f32[10,512]{1,0:T(8,128)S(1)} %get-tuple-element.122), channel_id=1, source_target_pairs={{0,1},{1,0},{2,3},{3,2},{4,5},{5,4},{6,7},{7,6},{8,9},{9,8},{10,11... | collective-permute-start | bytes 61448 | tf_op jit(solution)/shard_map/ppermute | solution.py:517
  132.8 4.1 %collective-permute-start.16 = (f32[10,512]{1,0:T(8,128)S(1)}, f32[10,512]{1,0:T(8,128)S(1)}, u32[]{:S(2)}, u32[]{:S(2)}) collective-permute-start(f32[10,512]{1,0:T(8,128)S(1)} %get-tuple-element.123), channel_id=1, source_target_pairs={{0,2},{1,3},{2,0},{3,1},{4,6},{5,7},{6,4},{7,5},{8,10},{9,11},{10,... | collective-permute-start | bytes 61448 | tf_op jit(solution)/shard_map/ppermute | solution.py:517
  133.5 3.6 %collective-permute-start.17 = (f32[10,512]{1,0:T(8,128)S(1)}, f32[10,512]{1,0:T(8,128)S(1)}, u32[]{:S(2)}, u32[]{:S(2)}) collective-permute-start(f32[10,512]{1,0:T(8,128)S(1)} %get-tuple-element.124), channel_id=1, source_target_pairs={{0,3},{1,2},{2,1},{3,0},{4,7},{5,6},{6,5},{7,4},{8,11},{9,10},{10,... | collective-permute-start | bytes 61448 | tf_op jit(solution)/shard_map/ppermute | solution.py:517

commit v13 on v12

--- a/solution.py
+++ b/solution.py
@@ -554,6 +554,8 @@
 
     def placed(pages):
         taken = sorted(arrived)
+        if not taken:
+            return pages
         place = []
         for d in taken:
             place += [(me ^ d) * capacity + ahead] if d else [w * capacity for w in range(wide)]
@@ -563,6 +565,7 @@
         arrived.clear()
         return pages
 
+    gathered, tags = lax.optimization_barrier((gathered, tags))
     tokens = pool.reshape(slots * PAGE, -1)
     if direct:
         block = jax.ShapeDtypeStruct((rows, 2 * HD), jnp.float32)
@@ -635,6 +638,7 @@
             step_ids < kept[:, None, None], fresh, jnp.zeros((), jnp.bfloat16)
         )
 
+    queries, moved_pool = lax.optimization_barrier((queries, placed(moved_pool)))
     mixed = attend(both, lengths, queries, keyval, tokens, token_info, rows, piece)
     if direct:
         mixed = land(deal(mixed, "narrow"), 0)
@@ -648,7 +652,10 @@
     mixed = beside(lambda value: exchange(value, "wide"), mixed, 4, 2)
     mixed, moved_pool = lax.optimization_barrier((mixed, pages))
     attn = combine([mixed], piece, wide)
+    attn, pages = lax.optimization_barrier((attn, moved_pool))
+    pages = placed(pages)
     attn = beside(lambda value: exchange(value, "wide"), attn, 5, 3)
+    attn, moved_pool = lax.optimization_barrier((attn, pages))
     if direct:
         sums = in_vmem(
             functools.partial(finish_kernel, narrow),
@@ -657,15 +664,19 @@
             attn,
             w_out,
         )
+        sums, pages = lax.optimization_barrier((sums, moved_pool))
+        pages = placed(pages)
         sums = beside(lambda value: deal(value, "narrow"), sums, 7)
         attended = ((sums[0] + sums[1]) + (sums[2] + sums[3])).astype(jnp.bfloat16)
     else:
         attn = jnp.transpose(attn.reshape(-1, rows, HD), (1, 0, 2)).reshape(rows, -1)
         sums = jnp.dot(attn, w_out, preferred_element_type=jnp.float32)
         sums = sums.reshape(narrow, rows // narrow, -1)
+        pages = placed(moved_pool)
         sums = beside(lambda value: exchange(value, "narrow"), sums, 7)
         attended = jnp.sum(sums, axis=0).astype(jnp.bfloat16)
-    moved_pool = placed(moved_pool)
+    attended, pages = lax.optimization_barrier((attended, pages))
+    moved_pool = placed(pages)
     return (attended, new_entries, moved_pool, moved_req, moved_idx)
 
 

time: 153 us -> 146 us (0.954)
  blocking collectives: 39.9 us -> 20.3 us
  waiting for transfers between devices: 40.8 us -> 49.1 us
  starting transfers between devices: 34.6 us -> 42 us
  local copies, waits for them, and re-layouts: 10.7 us -> 3.75 us
  Pallas kernels: 24.2 us -> 27.9 us
    all_to_all x1 -> x0, blocking collectives: 18 us -> none  [on_device(): attn = beside(lambda value: exchange(value, 'wide'), attn, 5, 3)]
    all_to_all x0 -> x1, waiting for transfers between devices: none -> 11.7 us  [on_device(): attn = beside(lambda value: exchange(value, 'wide'), attn, 5, 3)]
    unnamed x36 -> x32, local copies, waits for them, and re-layouts: 9.18 us -> 2.26 us
    all_to_all x0 -> x1, starting transfers between devices: none -> 5.43 us  [on_device(): attn = beside(lambda value: exchange(value, 'wide'), attn, 5, 3)]
    all_to_all x1, waiting for transfers between devices: 5.11 us -> 0.01 us  [spread(): lax.all_to_all(jnp.broadcast_to(block[None], (count,) + block.shape), axi...]
    pallas_call x2 -> x5, Pallas kernels: 3.71 us -> 6.64 us  [place_pages(): pl.pallas_call(functools.partial(place_kernel, counts), out_shape=jax.Sha...]
    all_to_all x1, waiting for transfers between devices: 9.76 us -> 11.6 us  [on_device(): mixed = beside(lambda value: exchange(value, 'wide'), mixed, 4, 2)]
    all_to_all x1, blocking collectives: 21.9 us -> 20.3 us  [on_device(): received = beside(lambda value: exchange(value, 'wide'), packed, 6, 1)]
  transfers between devices with their start and end apart: 22 -> 23, of which waited for: 9 -> 12; matrix products, arithmetic and copies ran while one was open for 0% -> 1% of each run, Pallas kernels for 13% -> 16%
where the time goes in v13:
time: 146 us; the launch traced here: 145 us
  waiting for transfers between devices  49.1 us (34%)
  starting transfers between devices  42 us (29%)
  Pallas kernels  27.9 us (19%)
  blocking collectives  20.3 us (14%)
  local copies, waits for them, and re-layouts  3.75 us (3%)
    ppermute x19, waiting for transfers between devices, send(): lax.ppermute(block, axis, [(i, i ^ d) for i in range(lax.axis_size(axis))])  25.6 us
    all_to_all x1, blocking collectives, on_device(): received = beside(lambda value: exchange(value, 'wide'), packed, 6, 1)  20.3 us
    ppermute x19, starting transfers between devices, send(): lax.ppermute(block, axis, [(i, i ^ d) for i in range(lax.axis_size(axis))])  18.7 us
    all_to_all x1, waiting for transfers between devices, on_device(): attn = beside(lambda value: exchange(value, 'wide'), attn, 5, 3)  11.7 us
    all_to_all x1, waiting for transfers between devices, on_device(): mixed = beside(lambda value: exchange(value, 'wide'), mixed, 4, 2)  11.6 us
    pallas_call x1, Pallas kernels, attend(): pl.pallas_call(functools.partial(attend_kernel, rows, piece, peers), grid...  10.3 us
    pallas_call x5, Pallas kernels, place_pages(): pl.pallas_call(functools.partial(place_kernel, counts), out_shape=jax.Sha...  6.64 us
    all_to_all x1, starting transfers between devices, spread(): lax.all_to_all(jnp.broadcast_to(block[None], (count,) + block.shape), axi...  6.28 us
  transfers between devices with their start and end apart: 23, of which 12 were waited for; matrix products, arithmetic and copies ran while one was open for 1% of the time, Pallas kernels for 16%

profile of v13, /device:TPU:8, one launch (start us, length us, event | category | flops | bytes accessed | tf_op | source)
XLA Modules:
  0.0 145.4 jit_solution(9706659421682881872)
XLA Ops:
  0.7 1.5 %broadcast_in_dim.2 = bf16[8,5,1024]{2,1,0:T(8,128)(2,1)} broadcast(bf16[5,1024]{1,0:T(8,128)(2,1)} %param.10), dimensions={1,2} | broadcast | bytes 92160 | tf_op jit(solution)/shard_map/broadcast_in_dim | solution.py:491
  2.1 6.3 %all-to-all-start = ((bf16[8,5,1024]{2,1,0:T(8,128)(2,1)}), bf16[8,5,1024]{2,1,0:T(8,128)(2,1)S(1)}, u32[]{:S(2)}, u32[]{:S(2)}) async-start(bf16[8,5,1024]{2,1,0:T(8,128)(2,1)} %broadcast_in_dim.2), calls=%async_computation | async-start | bytes 262144 | tf_op jit(solution)/shard_map/all_to_all | solution.py:490
  8.4 0.6 pad_add_fusion.me_ref
  9.0 5.7 %shard_map.137 = (bf16[128,16,1024]{2,1,0:T(8,128)(2,1)}, f32[8,128]{1,0:T(8,128)}, f32[8,2048]{1,0:T(8,128)}, bf16[40,16,1024]{2,1,0:T(8,128)(2,1)}, bf16[11,16...) custom-call(s32[2]{0:T(128)} %pad_add_fusion.me_ref, ...), custom_call_target="tpu_custom_call" | custom-call | bytes 8388608 | tf_op jit(solution)/shard_map/pallas_call | solution.py:118
  14.7 1.0 shard_map.138
  15.8 1.6 %collective-permute-start.1 = (f32[40,256]{1,0:T(8,128)S(1)}, f32[40,256]{1,0:T(8,128)S(1)}, u32[]{:S(2)}, u32[]{:S(2)}) collective-permute-start(f32[40,256]{1,0:T(8,128)S(1)} %get-tuple-element.94), channel_id=1, source_target_pairs={{0,2},{1,3},{2,0},{3,1},{4,6},{5,7},{6,4},{7,5},{8,10},{9,11},{10,... | collective-permute-start | bytes 122888 | tf_op jit(solution)/shard_map/ppermute | solution.py:517
  17.7 2.2 %collective-permute-done.1.refs_2_ = f32[40,256]{1,0:T(8,128)S(1)} collective-permute-done((f32[40,256]{1,0:T(8,128)S(1)}, f32[40,256]{1,0:T(8,128)S(1)}, u32[]{:S(2)}, u32[]{:S(2)}) %collective-permute-start.1) | collective-permute-done | bytes 40992 | tf_op jit(solution)/shard_map/ppermute | solution.py:517
  19.9 1.0 collective-permute-done.2.refs_3_
  20.9 0.7 copy-done.8
  21.6 1.5 %collective-permute-start.3 = (bf16[11,16,1024]{2,1,0:T(8,128)(2,1)}, bf16[11,16,1024]{2,1,0:T(8,128)(2,1)S(1)}, u32[]{:S(2)}, u32[]{:S(2)}) collective-permute-start(bf16[11,16,1024]{2,1,0:T(8,128)(2,1)} %get-tuple-element.100), channel_id=1, source_target_pairs={{0,24},{4,28},{8,16},{12,20},{16,8},{20,12},{24,0},{28,4},{1,25},{... | collective-permute-start | bytes 1081352 | tf_op jit(solution)/shard_map/ppermute | solution.py:517
  23.1 1.5 %collective-permute-start.4 = (bf16[11,16,1024]{2,1,0:T(8,128)(2,1)}, bf16[11,16,1024]{2,1,0:T(8,128)(2,1)S(1)}, u32[]{:S(2)}, u32[]{:S(2)}) collective-permute-start(bf16[11,16,1024]{2,1,0:T(8,128)(2,1)} %get-tuple-element.101), channel_id=1, source_target_pairs={{0,4},{4,0},{8,12},{12,8},{16,20},{20,16},{24,28},{28,24},{1,5},{5... | collective-permute-start | bytes 1081352 | tf_op jit(solution)/shard_map/ppermute | solution.py:517
  24.6 20.3 %all_to_all.25.part_ref = bf16[8,48,256]{2,1,0:T(8,128)(2,1)S(1)} all-to-all(bf16[8,48,256]{2,1,0:T(8,128)(2,1)S(1)} %shard_map.139), channel_id=1, replica_groups=mesh['wide'=8,'narrow'=4] {'wide'}, dimensions={0} | all-to-all | bytes 393216 | tf_op jit(solution)/shard_map/all_to_all | solution.py:589
  44.9 5.4 %all-to-all-start.2 = ((bf16[40,16,1024]{2,1,0:T(8,128)(2,1)}), bf16[40,16,1024]{2,1,0:T(8,128)(2,1)S(1)}, u32[]{:S(2)}, u32[]{:S(2)}) async-start(bf16[40,16,1024]{2,1,0:T(8,128)(2,1)} %get-tuple-element.119), calls=%async_computation.2 | async-start | bytes 2621440 | tf_op jit(solution)/shard_map/all_to_all | solution.py:543
  50.3 1.4 shard_map.140
  51.7 1.0 collective-permute-start.6
  52.7 0.8 collective-permute-start.7
  53.6 1.4 shard_map.141.refs_1_
  55.1 1.9 %collective-permute-done.6.refs_2_ = bf16[8,40,128]{2,1,0:T(8,128)(2,1)S(1)} collective-permute-done((bf16[8,40,128]{2,1,0:T(8,128)(2,1)S(1)}, bf16[8,40,128]{2,1,0:T(8,128)(2,1)S(1)}, u32[]{:S(2)}, u32[]{:S(2)}) %collective-permute-start.6) | collective-permute-done | bytes 81952 | tf_op jit(solution)/shard_map/ppermute | solution.py:517
  57.0 0.8 collective-permute-done.7.refs_3_
  57.8 0.6 copy-done.12
  58.4 10.3 %shard_map.142 = (bf16[8,64,128]{2,1,0:T(8,128)(2,1)}, bf16[8,64,128]{2,1,0:T(8,128)(2,1)}, bf16[8,64,128]{2,1,0:T(8,128)(2,1)}, bf16[8,64,128]{2,1,0:T(8,128)(2,1)}) custom-call(s32[2]{0:T(128)} %pad_add_fusion.me_ref, s32[8]{0:T(128)} %length_ref.1, bf16[8,40,128]{2,1,0:T(8,128)(2,1)} %copy-done.5, bf16[8,40,128]{2,1,0:T(8,128)(2,1)} %copy-done.10, ...), custom_call_target="tpu_custom_call" | custom-call | flops 1 | bytes 1 | tf_op jit(solution)/shard_map/pallas_call | solution.py:298
  68.7 1.2 collective-permute-start.10
  69.9 1.1 collective-permute-start.9
  71.0 3.1 %collective-permute-done.10.refs_3_ = bf16[8,64,128]{2,1,0:T(8,128)(2,1)S(1)} collective-permute-done((bf16[8,64,128]{2,1,0:T(8,128)(2,1)}, bf16[8,64,128]{2,1,0:T(8,128)(2,1)S(1)}, u32[]{:S(2)}, u32[]{:S(2)}) %collective-permute-start.10) | collective-permute-done | bytes 131104 | tf_op jit(solution)/shard_map/ppermute | solution.py:517
  74.1 3.5 %collective-permute-done.9.refs_2_ = bf16[8,64,128]{2,1,0:T(8,128)(2,1)S(1)} collective-permute-done((bf16[8,64,128]{2,1,0:T(8,128)(2,1)}, bf16[8,64,128]{2,1,0:T(8,128)(2,1)S(1)}, u32[]{:S(2)}, u32[]{:S(2)}) %collective-permute-start.9) | collective-permute-done | bytes 131104 | tf_op jit(solution)/shard_map/ppermute | solution.py:517
  77.8 0.9 copy-done.4
  78.7 1.1 shard_map.143
  79.8 2.7 %collective-permute-start.11 = (bf16[11,16,1024]{2,1,0:T(8,128)(2,1)S(1)}, bf16[11,16,1024]{2,1,0:T(8,128)(2,1)S(1)}, u32[]{:S(2)}, u32[]{:S(2)}) collective-permute-start(bf16[11,16,1024]{2,1,0:T(8,128)(2,1)S(1)} %copy-done.15), channel_id=1, source_target_pairs={{0,16},{4,20},{8,24},{12,28},{16,0},{20,4},{24,8},{28,12},{1,17},{... | collective-permute-start | bytes 1081352 | tf_op jit(solution)/shard_map/ppermute | solution.py:517
  82.6 0.6 collective-permute-start.12
  83.2 6.2 %all-to-all-start.3 = ((bf16[8,64,128]{2,1,0:T(8,128)(2,1)}), bf16[8,64,128]{2,1,0:T(8,128)(2,1)S(1)}, u32[]{:S(2)}, u32[]{:S(2)}) async-start(bf16[8,64,128]{2,1,0:T(8,128)(2,1)} %shard_map.143), calls=%async_computation.3 | async-start | bytes 262144 | tf_op jit(solution)/shard_map/all_to_all | solution.py:652
  89.4 1.7 %shard_map.144.refs_2_ = bf16[128,16,1024]{2,1,0:T(8,128)(2,1)} custom-call(s32[8]{0:T(128)S(1)} %iota_multiply_fusion.place_ref, bf16[40,16,1024]{2,1,0:T(8,128)(2,1)S(1)} %all-to-all-done.2.refs_0_, bf16[128,16,1024]{2,1,0:T(8,128)(2,1)} %shard_map.141.refs_1_), custom_call_target="tpu_custom_call", output_to_operand_aliasing={{}: (2, {})} | custom-call | bytes 2621440 | tf_op jit(solution)/shard_map/pallas_call | solution.py:156
  91.1 11.6 %all-to-all-done.3.refs_0_ = bf16[8,64,128]{2,1,0:T(8,128)(2,1)S(1)} async-done(((bf16[8,64,128]{2,1,0:T(8,128)(2,1)}), bf16[8,64,128]{2,1,0:T(8,128)(2,1)S(1)}, u32[]{:S(2)}, u32[]{:S(2)}) %all-to-all-start.3) | async-done | bytes 131104 | tf_op jit(solution)/shard_map/all_to_all | solution.py:652
  102.7 0.9 shard_map.145
  103.6 1.6 %collective-permute-start.13 = (bf16[11,16,1024]{2,1,0:T(8,128)(2,1)}, bf16[11,16,1024]{2,1,0:T(8,128)(2,1)S(1)}, u32[]{:S(2)}, u32[]{:S(2)}) collective-permute-start(bf16[11,16,1024]{2,1,0:T(8,128)(2,1)} %get-tuple-element.140), channel_id=1, source_target_pairs={{0,20},{4,16},{8,28},{12,24},{16,4},{20,0},{24,12},{28,8},{1,21},{... | collective-permute-start | bytes 1081352 | tf_op jit(solution)/shard_map/ppermute | solution.py:517
  105.2 1.2 collective-permute-start.14
  106.4 5.4 %all-to-all-start.4 = ((bf16[8,40,128]{2,1,0:T(8,128)(2,1)}), bf16[8,40,128]{2,1,0:T(8,128)(2,1)S(1)}, u32[]{:S(2)}, u32[]{:S(2)}) async-start(bf16[8,40,128]{2,1,0:T(8,128)(2,1)} %shard_map.145), calls=%async_computation.4 | async-start | bytes 163840 | tf_op jit(solution)/shard_map/all_to_all | solution.py:657
  111.9 1.4 shard_map.146.refs_2_
  113.4 11.7 %all-to-all-done.4.part_ref = bf16[8,40,128]{2,1,0:T(8,128)(2,1)S(1)} async-done(((bf16[8,40,128]{2,1,0:T(8,128)(2,1)}), bf16[8,40,128]{2,1,0:T(8,128)(2,1)S(1)}, u32[]{:S(2)}, u32[]{:S(2)}) %all-to-all-start.4) | async-done | bytes 81952 | tf_op jit(solution)/shard_map/all_to_all | solution.py:657
  125.0 0.9 shard_map.147
  126.0 1.6 %collective-permute-start.18 = (bf16[11,16,1024]{2,1,0:T(8,128)(2,1)S(1)}, bf16[11,16,1024]{2,1,0:T(8,128)(2,1)S(1)}, u32[]{:S(2)}, u32[]{:S(2)}) collective-permute-start(bf16[11,16,1024]{2,1,0:T(8,128)(2,1)S(1)} %copy-done.13), channel_id=1, source_target_pairs={{0,28},{4,24},{8,20},{12,16},{16,12},{20,8},{24,4},{28,0},{1,29},{... | collective-permute-start | bytes 1081352 | tf_op jit(solution)/shard_map/ppermute | solution.py:517
  127.6 1.4 collective-permute-start.16
  129.0 0.5 collective-permute-start.17
  129.5 1.4 shard_map.148.refs_1_
  131.0 0.5 collective-permute-done.16
  131.5 0.8 collective-permute-done.17
  132.3 11.7 %collective-permute-done.18.refs_0_ = bf16[11,16,1024]{2,1,0:T(8,128)(2,1)S(1)} collective-permute-done((bf16[11,16,1024]{2,1,0:T(8,128)(2,1)S(1)}, bf16[11,16,1024]{2,1,0:T(8,128)(2,1)S(1)}, u32[]{:S(2)}, u32[]{:S(2)}) %collective-permute-start.18) | collective-permute-done | bytes 360480 | tf_op jit(solution)/shard_map/ppermute | solution.py:517
  144.0 0.6 add_convert_fusion
  144.6 0.7 shard_map.149
  (51 shorter events, 1.0 us)
Async XLA Ops:
  0.6 14.1 %copy-start.1 = (bf16[1024,512]{1,0:T(8,128)(2,1)S(1)}, bf16[1024,512]{1,0:T(8,128)(2,1)}, u32[]{:S(2)}) copy-start(bf16[1024,512]{1,0:T(8,128)(2,1)} %query_ref.1) | copy-start | bytes 3145732
  0.6 14.1 %copy-start.3 = (bf16[1024,128]{1,0:T(8,128)(2,1)S(1)}, bf16[1024,128]{1,0:T(8,128)(2,1)}, u32[]{:S(2)}) copy-start(bf16[1024,128]{1,0:T(8,128)(2,1)} %keyval_ref.1) | copy-start | bytes 786436
  2.1 12.6 %all-to-all-start = ((bf16[8,5,1024]{2,1,0:T(8,128)(2,1)}), bf16[8,5,1024]{2,1,0:T(8,128)(2,1)S(1)}, u32[]{:S(2)}, u32[]{:S(2)}) async-start(bf16[8,5,1024]{2,1,0:T(8,128)(2,1)} %broadcast_in_dim.2), calls=%async_computation | async-start | bytes 262144 | tf_op jit(solution)/shard_map/all_to_all | solution.py:490
  9.0 5.7 %copy-start.6 = (s32[2]{0:T(128)S(1)}, s32[2]{0:T(128)}, u32[]{:S(2)}) copy-start(s32[2]{0:T(128)} %pad_add_fusion.me_ref) | copy-start | bytes 28
  9.0 41.3 %copy-start.9 = (s32[8]{0:T(128)S(1)}, s32[8]{0:T(128)}, u32[]{:S(2)}) copy-start(s32[8]{0:T(128)} %kept_ref.1) | copy-start | bytes 100
  15.7 1.9 %collective-permute-start = (f32[40,256]{1,0:T(8,128)S(1)}, f32[40,256]{1,0:T(8,128)S(1)}, u32[]{:S(2)}, u32[]{:S(2)}) collective-permute-start(f32[40,256]{1,0:T(8,128)S(1)} %get-tuple-element.93), channel_id=1, source_target_pairs={{0,1},{1,0},{2,3},{3,2},{4,5},{5,4},{6,7},{7,6},{8,9},{9,8},{10,11... | collective-permute-start | bytes 122888 | tf_op jit(solution)/shard_map/ppermute | solution.py:517
  15.8 4.1 %collective-permute-start.1 = (f32[40,256]{1,0:T(8,128)S(1)}, f32[40,256]{1,0:T(8,128)S(1)}, u32[]{:S(2)}, u32[]{:S(2)}) collective-permute-start(f32[40,256]{1,0:T(8,128)S(1)} %get-tuple-element.94), channel_id=1, source_target_pairs={{0,2},{1,3},{2,0},{3,1},{4,6},{5,7},{6,4},{7,5},{8,10},{9,11},{10,... | collective-permute-start | bytes 122888 | tf_op jit(solution)/shard_map/ppermute | solution.py:517
  17.4 3.5 %collective-permute-start.2 = (f32[40,256]{1,0:T(8,128)S(1)}, f32[40,256]{1,0:T(8,128)S(1)}, u32[]{:S(2)}, u32[]{:S(2)}) collective-permute-start(f32[40,256]{1,0:T(8,128)S(1)} %get-tuple-element.95), channel_id=1, source_target_pairs={{0,3},{1,2},{2,1},{3,0},{4,7},{5,6},{6,5},{7,4},{8,11},{9,10},{10,... | collective-permute-start | bytes 122888 | tf_op jit(solution)/shard_map/ppermute | solution.py:517
  20.9 0.7 copy-start.8
  21.6 23.3 %collective-permute-start.3 = (bf16[11,16,1024]{2,1,0:T(8,128)(2,1)}, bf16[11,16,1024]{2,1,0:T(8,128)(2,1)S(1)}, u32[]{:S(2)}, u32[]{:S(2)}) collective-permute-start(bf16[11,16,1024]{2,1,0:T(8,128)(2,1)} %get-tuple-element.100), channel_id=1, source_target_pairs={{0,24},{4,28},{8,16},{12,20},{16,8},{20,12},{24,0},{28,4},{1,25},{... | collective-permute-start | bytes 1081352 | tf_op jit(solution)/shard_map/ppermute | solution.py:517
  23.1 21.8 %collective-permute-start.4 = (bf16[11,16,1024]{2,1,0:T(8,128)(2,1)}, bf16[11,16,1024]{2,1,0:T(8,128)(2,1)S(1)}, u32[]{:S(2)}, u32[]{:S(2)}) collective-permute-start(bf16[11,16,1024]{2,1,0:T(8,128)(2,1)} %get-tuple-element.101), channel_id=1, source_target_pairs={{0,4},{4,0},{8,12},{12,8},{16,20},{20,16},{24,28},{28,24},{1,5},{5... | collective-permute-start | bytes 1081352 | tf_op jit(solution)/shard_map/ppermute | solution.py:517
  44.9 32.9 %all-to-all-start.2 = ((bf16[40,16,1024]{2,1,0:T(8,128)(2,1)}), bf16[40,16,1024]{2,1,0:T(8,128)(2,1)S(1)}, u32[]{:S(2)}, u32[]{:S(2)}) async-start(bf16[40,16,1024]{2,1,0:T(8,128)(2,1)} %get-tuple-element.119), calls=%async_computation.2 | async-start | bytes 2621440 | tf_op jit(solution)/shard_map/all_to_all | solution.py:543
  51.6 3.4 %copy-start = (bf16[128,1024]{1,0:T(8,128)(2,1)}, bf16[128,1024]{1,0:T(8,128)(2,1)S(1)}, u32[]{:S(2)}) copy-start(bf16[128,1024]{1,0:T(8,128)(2,1)S(1)} %get-tuple-element.113.refs_6_.refs_7_) | copy-start | bytes 786436
  51.7 3.4 %copy-start.5 = (bf16[8,40,128]{2,1,0:T(8,128)(2,1)}, bf16[8,40,128]{2,1,0:T(8,128)(2,1)S(1)}, u32[]{:S(2)}) copy-start(bf16[8,40,128]{2,1,0:T(8,128)(2,1)S(1)} %get-tuple-element.109.refs_0_) | copy-start | bytes 245764
  51.7 3.4 %collective-permute-start.5 = (bf16[8,40,128]{2,1,0:T(8,128)(2,1)S(1)}, bf16[8,40,128]{2,1,0:T(8,128)(2,1)S(1)}, u32[]{:S(2)}, u32[]{:S(2)}) collective-permute-start(bf16[8,40,128]{2,1,0:T(8,128)(2,1)S(1)} %get-tuple-element.109.refs_0_), channel_id=1, source_target_pairs={{0,1},{1,0},{2,3},{3,2},{4,5},{5,4},{6,7},{7,6},{8,9},{9,8},{10,11... | collective-permute-start | bytes 245768 | tf_op jit(solution)/shard_map/ppermute | solution.py:517
  51.7 5.3 %collective-permute-start.6 = (bf16[8,40,128]{2,1,0:T(8,128)(2,1)S(1)}, bf16[8,40,128]{2,1,0:T(8,128)(2,1)S(1)}, u32[]{:S(2)}, u32[]{:S(2)}) collective-permute-start(bf16[8,40,128]{2,1,0:T(8,128)(2,1)S(1)} %get-tuple-element.109.refs_0_), channel_id=1, source_target_pairs={{0,2},{1,3},{2,0},{3,1},{4,6},{5,7},{6,4},{7,5},{8,10},{9,11},{10,... | collective-permute-start | bytes 245768 | tf_op jit(solution)/shard_map/ppermute | solution.py:517
  52.7 5.1 %collective-permute-start.7 = (bf16[8,40,128]{2,1,0:T(8,128)(2,1)S(1)}, bf16[8,40,128]{2,1,0:T(8,128)(2,1)S(1)}, u32[]{:S(2)}, u32[]{:S(2)}) collective-permute-start(bf16[8,40,128]{2,1,0:T(8,128)(2,1)S(1)} %get-tuple-element.109.refs_0_), channel_id=1, source_target_pairs={{0,3},{1,2},{2,1},{3,0},{4,7},{5,6},{6,5},{7,4},{8,11},{9,10},{10,... | collective-permute-start | bytes 245768 | tf_op jit(solution)/shard_map/ppermute | solution.py:517
  55.0 2.8 %copy-start.10 = (bf16[8,40,128]{2,1,0:T(8,128)(2,1)}, bf16[8,40,128]{2,1,0:T(8,128)(2,1)S(1)}, u32[]{:S(2)}) copy-start(bf16[8,40,128]{2,1,0:T(8,128)(2,1)S(1)} %collective-permute-done.5.refs_1_) | copy-start | bytes 245764
  57.0 0.8 copy-start.11
  57.8 0.6 copy-start.12
  58.4 21.4 %copy-start.15 = (bf16[11,16,1024]{2,1,0:T(8,128)(2,1)S(1)}, bf16[11,16,1024]{2,1,0:T(8,128)(2,1)}, u32[]{:S(2)}) copy-start(bf16[11,16,1024]{2,1,0:T(8,128)(2,1)} %get-tuple-element.129) | copy-start | bytes 1081348
  58.4 24.2 %copy-start.14 = (bf16[11,16,1024]{2,1,0:T(8,128)(2,1)S(1)}, bf16[11,16,1024]{2,1,0:T(8,128)(2,1)}, u32[]{:S(2)}) copy-start(bf16[11,16,1024]{2,1,0:T(8,128)(2,1)} %get-tuple-element.130) | copy-start | bytes 1081348
  68.7 5.4 %collective-permute-start.10 = (bf16[8,64,128]{2,1,0:T(8,128)(2,1)}, bf16[8,64,128]{2,1,0:T(8,128)(2,1)S(1)}, u32[]{:S(2)}, u32[]{:S(2)}) collective-permute-start(bf16[8,64,128]{2,1,0:T(8,128)(2,1)} %get-tuple-element.118), channel_id=1, source_target_pairs={{0,3},{1,2},{2,1},{3,0},{4,7},{5,6},{6,5},{7,4},{8,11},{9,10},{10,... | collective-permute-start | bytes 393224 | tf_op jit(solution)/shard_map/ppermute | solution.py:517
  69.9 4.2 %collective-permute-start.8 = (bf16[8,64,128]{2,1,0:T(8,128)(2,1)}, bf16[8,64,128]{2,1,0:T(8,128)(2,1)S(1)}, u32[]{:S(2)}, u32[]{:S(2)}) collective-permute-start(bf16[8,64,128]{2,1,0:T(8,128)(2,1)} %get-tuple-element.116), channel_id=1, source_target_pairs={{0,1},{1,0},{2,3},{3,2},{4,5},{5,4},{6,7},{7,6},{8,9},{9,8},{10,11... | collective-permute-start | bytes 393224 | tf_op jit(solution)/shard_map/ppermute | solution.py:517
  69.9 7.6 %collective-permute-start.9 = (bf16[8,64,128]{2,1,0:T(8,128)(2,1)}, bf16[8,64,128]{2,1,0:T(8,128)(2,1)S(1)}, u32[]{:S(2)}, u32[]{:S(2)}) collective-permute-start(bf16[8,64,128]{2,1,0:T(8,128)(2,1)} %get-tuple-element.117), channel_id=1, source_target_pairs={{0,2},{1,3},{2,0},{3,1},{4,6},{5,7},{6,4},{7,5},{8,10},{9,11},{10,... | collective-permute-start | bytes 393224 | tf_op jit(solution)/shard_map/ppermute | solution.py:517
  77.8 0.9 copy-start.4
  79.8 22.8 %collective-permute-start.11 = (bf16[11,16,1024]{2,1,0:T(8,128)(2,1)S(1)}, bf16[11,16,1024]{2,1,0:T(8,128)(2,1)S(1)}, u32[]{:S(2)}, u32[]{:S(2)}) collective-permute-start(bf16[11,16,1024]{2,1,0:T(8,128)(2,1)S(1)} %copy-done.15), channel_id=1, source_target_pairs={{0,16},{4,20},{8,24},{12,28},{16,0},{20,4},{24,8},{28,12},{1,17},{... | collective-permute-start | bytes 1081352 | tf_op jit(solution)/shard_map/ppermute | solution.py:517
  82.6 20.1 %collective-permute-start.12 = (bf16[11,16,1024]{2,1,0:T(8,128)(2,1)S(1)}, bf16[11,16,1024]{2,1,0:T(8,128)(2,1)S(1)}, u32[]{:S(2)}, u32[]{:S(2)}) collective-permute-start(bf16[11,16,1024]{2,1,0:T(8,128)(2,1)S(1)} %copy-done.14), channel_id=1, source_target_pairs={{0,8},{4,12},{8,0},{12,4},{16,24},{20,28},{24,16},{28,20},{1,9},{5... | collective-permute-start | bytes 1081352 | tf_op jit(solution)/shard_map/ppermute | solution.py:517
  83.2 19.5 %all-to-all-start.3 = ((bf16[8,64,128]{2,1,0:T(8,128)(2,1)}), bf16[8,64,128]{2,1,0:T(8,128)(2,1)S(1)}, u32[]{:S(2)}, u32[]{:S(2)}) async-start(bf16[8,64,128]{2,1,0:T(8,128)(2,1)} %shard_map.143), calls=%async_computation.3 | async-start | bytes 262144 | tf_op jit(solution)/shard_map/all_to_all | solution.py:652
  103.6 21.4 %collective-permute-start.13 = (bf16[11,16,1024]{2,1,0:T(8,128)(2,1)}, bf16[11,16,1024]{2,1,0:T(8,128)(2,1)S(1)}, u32[]{:S(2)}, u32[]{:S(2)}) collective-permute-start(bf16[11,16,1024]{2,1,0:T(8,128)(2,1)} %get-tuple-element.140), channel_id=1, source_target_pairs={{0,20},{4,16},{8,28},{12,24},{16,4},{20,0},{24,12},{28,8},{1,21},{... | collective-permute-start | bytes 1081352 | tf_op jit(solution)/shard_map/ppermute | solution.py:517
  105.2 19.8 %collective-permute-start.14 = (bf16[11,16,1024]{2,1,0:T(8,128)(2,1)}, bf16[11,16,1024]{2,1,0:T(8,128)(2,1)S(1)}, u32[]{:S(2)}, u32[]{:S(2)}) collective-permute-start(bf16[11,16,1024]{2,1,0:T(8,128)(2,1)} %get-tuple-element.141), channel_id=1, source_target_pairs={{0,12},{4,8},{8,4},{12,0},{16,28},{20,24},{24,20},{28,16},{1,13},{... | collective-permute-start | bytes 1081352 | tf_op jit(solution)/shard_map/ppermute | solution.py:517
  106.4 18.6 %all-to-all-start.4 = ((bf16[8,40,128]{2,1,0:T(8,128)(2,1)}), bf16[8,40,128]{2,1,0:T(8,128)(2,1)S(1)}, u32[]{:S(2)}, u32[]{:S(2)}) async-start(bf16[8,40,128]{2,1,0:T(8,128)(2,1)} %shard_map.145), calls=%async_computation.4 | async-start | bytes 163840 | tf_op jit(solution)/shard_map/all_to_all | solution.py:657
  111.9 13.1 %copy-start.2 = (bf16[1024,512]{1,0:T(8,128)(2,1)S(1)}, bf16[1024,512]{1,0:T(8,128)(2,1)}, u32[]{:S(2)}) copy-start(bf16[1024,512]{1,0:T(8,128)(2,1)} %weight_ref.1) | copy-start | bytes 3145732
  111.9 13.1 %copy-start.7 = (s32[2]{0:T(128)S(1)}, s32[2]{0:T(128)}, u32[]{:S(2)}) copy-start(s32[2]{0:T(128)} %pad_add_fusion.me_ref) | copy-start | bytes 28
  111.9 14.0 %copy-start.13 = (bf16[11,16,1024]{2,1,0:T(8,128)(2,1)S(1)}, bf16[11,16,1024]{2,1,0:T(8,128)(2,1)}, u32[]{:S(2)}) copy-start(bf16[11,16,1024]{2,1,0:T(8,128)(2,1)} %get-tuple-element.161) | copy-start | bytes 1081348
  126.0 18.0 %collective-permute-start.18 = (bf16[11,16,1024]{2,1,0:T(8,128)(2,1)S(1)}, bf16[11,16,1024]{2,1,0:T(8,128)(2,1)S(1)}, u32[]{:S(2)}, u32[]{:S(2)}) collective-permute-start(bf16[11,16,1024]{2,1,0:T(8,128)(2,1)S(1)} %copy-done.13), channel_id=1, source_target_pairs={{0,28},{4,24},{8,20},{12,16},{16,12},{20,8},{24,4},{28,0},{1,29},{... | collective-permute-start | bytes 1081352 | tf_op jit(solution)/shard_map/ppermute | solution.py:517
  127.6 3.4 %collective-permute-start.15 = (f32[10,512]{1,0:T(8,128)S(1)}, f32[10,512]{1,0:T(8,128)S(1)}, u32[]{:S(2)}, u32[]{:S(2)}) collective-permute-start(f32[10,512]{1,0:T(8,128)S(1)} %get-tuple-element.158), channel_id=1, source_target_pairs={{0,1},{1,0},{2,3},{3,2},{4,5},{5,4},{6,7},{7,6},{8,9},{9,8},{10,11... | collective-permute-start | bytes 61448 | tf_op jit(solution)/shard_map/ppermute | solution.py:517
  127.6 3.9 %collective-permute-start.16 = (f32[10,512]{1,0:T(8,128)S(1)}, f32[10,512]{1,0:T(8,128)S(1)}, u32[]{:S(2)}, u32[]{:S(2)}) collective-permute-start(f32[10,512]{1,0:T(8,128)S(1)} %get-tuple-element.159), channel_id=1, source_target_pairs={{0,2},{1,3},{2,0},{3,1},{4,6},{5,7},{6,4},{7,5},{8,10},{9,11},{10,... | collective-permute-start | bytes 61448 | tf_op jit(solution)/shard_map/ppermute | solution.py:517
  129.0 3.3 %collective-permute-start.17 = (f32[10,512]{1,0:T(8,128)S(1)}, f32[10,512]{1,0:T(8,128)S(1)}, u32[]{:S(2)}, u32[]{:S(2)}) collective-permute-start(f32[10,512]{1,0:T(8,128)S(1)} %get-tuple-element.160), channel_id=1, source_target_pairs={{0,3},{1,2},{2,1},{3,0},{4,7},{5,6},{6,5},{7,4},{8,11},{9,10},{10,... | collective-permute-start | bytes 61448 | tf_op jit(solution)/shard_map/ppermute | solution.py:517

commit v14 on v13

--- a/solution.py
+++ b/solution.py
@@ -649,12 +649,12 @@
     mixed = combine(mixed, piece)
     mixed, pages = lax.optimization_barrier((mixed, moved_pool))
     pages = placed(pages)
-    mixed = beside(lambda value: exchange(value, "wide"), mixed, 4, 2)
+    mixed = beside(lambda value: exchange(value, "wide"), mixed, 3, 4)
     mixed, moved_pool = lax.optimization_barrier((mixed, pages))
     attn = combine([mixed], piece, wide)
     attn, pages = lax.optimization_barrier((attn, moved_pool))
     pages = placed(pages)
-    attn = beside(lambda value: exchange(value, "wide"), attn, 5, 3)
+    attn = beside(lambda value: exchange(value, "wide"), attn, 2, 5)
     attn, moved_pool = lax.optimization_barrier((attn, pages))
     if direct:
         sums = in_vmem(

time: 146 us -> 143 us (0.979)
  the two profiles are of different devices: /device:TPU:8 before, /device:TPU:10 now
where the time goes in v14:
time: 143 us; the launch traced here: 142 us
  waiting for transfers between devices  46 us (32%)
  starting transfers between devices  41.9 us (29%)
  Pallas kernels  27.9 us (20%)
  blocking collectives  20.4 us (14%)
  local copies, waits for them, and re-layouts  3.75 us (3%)
  other arithmetic  1.45 us (1%)
    ppermute x19, waiting for transfers between devices, send(): lax.ppermute(block, axis, [(i, i ^ d) for i in range(lax.axis_size(axis))])  22.2 us
    all_to_all x1, blocking collectives, on_device(): received = beside(lambda value: exchange(value, 'wide'), packed, 6, 1)  20.4 us
    ppermute x19, starting transfers between devices, send(): lax.ppermute(block, axis, [(i, i ^ d) for i in range(lax.axis_size(axis))])  19.1 us
    all_to_all x1, waiting for transfers between devices, on_device(): mixed = beside(lambda value: exchange(value, 'wide'), mixed, 3, 4)  11.9 us
    all_to_all x1, waiting for transfers between devices, on_device(): attn = beside(lambda value: exchange(value, 'wide'), attn, 2, 5)  11.3 us
    pallas_call x1, Pallas kernels, attend(): pl.pallas_call(functools.partial(attend_kernel, rows, piece, peers), grid...  10.3 us
    pallas_call x5, Pallas kernels, place_pages(): pl.pallas_call(functools.partial(place_kernel, counts), out_shape=jax.Sha...  6.64 us
    all_to_all x1, starting transfers between devices, spread(): lax.all_to_all(jnp.broadcast_to(block[None], (count,) + block.shape), axi...  6.28 us
  transfers between devices with their start and end apart: 23, of which 10 were waited for; matrix products, arithmetic and copies ran while one was open for 1% of the time, Pallas kernels for 16%

profile of v14, /device:TPU:10, one launch (start us, length us, event | category | flops | bytes accessed | tf_op | source)
XLA Modules:
  0.0 142.2 jit_solution(873002198437053275)
XLA Ops:
  0.7 1.5 %broadcast_in_dim.2 = bf16[8,5,1024]{2,1,0:T(8,128)(2,1)} broadcast(bf16[5,1024]{1,0:T(8,128)(2,1)} %param.10), dimensions={1,2} | broadcast | bytes 92160 | tf_op jit(solution)/shard_map/broadcast_in_dim | solution.py:491
  2.1 6.3 %all-to-all-start = ((bf16[8,5,1024]{2,1,0:T(8,128)(2,1)}), bf16[8,5,1024]{2,1,0:T(8,128)(2,1)S(1)}, u32[]{:S(2)}, u32[]{:S(2)}) async-start(bf16[8,5,1024]{2,1,0:T(8,128)(2,1)} %broadcast_in_dim.2), calls=%async_computation | async-start | bytes 262144 | tf_op jit(solution)/shard_map/all_to_all | solution.py:490
  8.4 0.6 pad_add_fusion.me_ref
  9.0 5.7 %shard_map.137 = (bf16[128,16,1024]{2,1,0:T(8,128)(2,1)}, f32[8,128]{1,0:T(8,128)}, f32[8,2048]{1,0:T(8,128)}, bf16[40,16,1024]{2,1,0:T(8,128)(2,1)}, bf16[11,16...) custom-call(s32[2]{0:T(128)} %pad_add_fusion.me_ref, ...), custom_call_target="tpu_custom_call" | custom-call | bytes 8388608 | tf_op jit(solution)/shard_map/pallas_call | solution.py:118
  14.7 1.0 shard_map.138
  15.8 0.6 collective-permute-start.1
  16.4 1.3 collective-permute-start.2
  17.7 2.6 %collective-permute-done.1.refs_2_ = f32[40,256]{1,0:T(8,128)S(1)} collective-permute-done((f32[40,256]{1,0:T(8,128)S(1)}, f32[40,256]{1,0:T(8,128)S(1)}, u32[]{:S(2)}, u32[]{:S(2)}) %collective-permute-start.1) | collective-permute-done | bytes 40992 | tf_op jit(solution)/shard_map/ppermute | solution.py:517
  20.3 0.7 copy-done.8
  21.0 1.5 %collective-permute-start.3 = (bf16[11,16,1024]{2,1,0:T(8,128)(2,1)}, bf16[11,16,1024]{2,1,0:T(8,128)(2,1)S(1)}, u32[]{:S(2)}, u32[]{:S(2)}) collective-permute-start(bf16[11,16,1024]{2,1,0:T(8,128)(2,1)} %get-tuple-element.100), channel_id=1, source_target_pairs={{0,24},{4,28},{8,16},{12,20},{16,8},{20,12},{24,0},{28,4},{1,25},{... | collective-permute-start | bytes 1081352 | tf_op jit(solution)/shard_map/ppermute | solution.py:517
  22.5 1.5 %collective-permute-start.4 = (bf16[11,16,1024]{2,1,0:T(8,128)(2,1)}, bf16[11,16,1024]{2,1,0:T(8,128)(2,1)S(1)}, u32[]{:S(2)}, u32[]{:S(2)}) collective-permute-start(bf16[11,16,1024]{2,1,0:T(8,128)(2,1)} %get-tuple-element.101), channel_id=1, source_target_pairs={{0,4},{4,0},{8,12},{12,8},{16,20},{20,16},{24,28},{28,24},{1,5},{5... | collective-permute-start | bytes 1081352 | tf_op jit(solution)/shard_map/ppermute | solution.py:517
  24.0 20.4 %all_to_all.25.part_ref = bf16[8,48,256]{2,1,0:T(8,128)(2,1)S(1)} all-to-all(bf16[8,48,256]{2,1,0:T(8,128)(2,1)S(1)} %shard_map.139), channel_id=1, replica_groups=mesh['wide'=8,'narrow'=4] {'wide'}, dimensions={0} | all-to-all | bytes 393216 | tf_op jit(solution)/shard_map/all_to_all | solution.py:589
  44.4 5.4 %all-to-all-start.2 = ((bf16[40,16,1024]{2,1,0:T(8,128)(2,1)}), bf16[40,16,1024]{2,1,0:T(8,128)(2,1)S(1)}, u32[]{:S(2)}, u32[]{:S(2)}) async-start(bf16[40,16,1024]{2,1,0:T(8,128)(2,1)} %get-tuple-element.119), calls=%async_computation.2 | async-start | bytes 2621440 | tf_op jit(solution)/shard_map/all_to_all | solution.py:543
  49.8 1.4 shard_map.140
  51.1 1.1 collective-permute-start.6
  52.3 0.7 collective-permute-start.7
  53.0 0.1 pad_add_fusion.1.place_ref
  53.1 1.4 shard_map.141.refs_1_
  54.5 1.9 %collective-permute-done.6.refs_2_ = bf16[8,40,128]{2,1,0:T(8,128)(2,1)S(1)} collective-permute-done((bf16[8,40,128]{2,1,0:T(8,128)(2,1)S(1)}, bf16[8,40,128]{2,1,0:T(8,128)(2,1)S(1)}, u32[]{:S(2)}, u32[]{:S(2)}) %collective-permute-start.6) | collective-permute-done | bytes 81952 | tf_op jit(solution)/shard_map/ppermute | solution.py:517
  56.5 0.8 collective-permute-done.7.refs_3_
  57.3 0.6 copy-done.12
  57.9 10.3 %shard_map.142 = (bf16[8,64,128]{2,1,0:T(8,128)(2,1)}, bf16[8,64,128]{2,1,0:T(8,128)(2,1)}, bf16[8,64,128]{2,1,0:T(8,128)(2,1)}, bf16[8,64,128]{2,1,0:T(8,128)(2,1)}) custom-call(s32[2]{0:T(128)} %pad_add_fusion.me_ref, s32[8]{0:T(128)} %length_ref.1, bf16[8,40,128]{2,1,0:T(8,128)(2,1)} %copy-done.5, bf16[8,40,128]{2,1,0:T(8,128)(2,1)} %copy-done.10, ...), custom_call_target="tpu_custom_call" | custom-call | flops 1 | bytes 1 | tf_op jit(solution)/shard_map/pallas_call | solution.py:298
  68.2 1.3 collective-permute-start.10
  69.5 1.0 collective-permute-start.9
  70.4 3.2 %collective-permute-done.10.refs_3_ = bf16[8,64,128]{2,1,0:T(8,128)(2,1)S(1)} collective-permute-done((bf16[8,64,128]{2,1,0:T(8,128)(2,1)}, bf16[8,64,128]{2,1,0:T(8,128)(2,1)S(1)}, u32[]{:S(2)}, u32[]{:S(2)}) %collective-permute-start.10) | collective-permute-done | bytes 131104 | tf_op jit(solution)/shard_map/ppermute | solution.py:517
  73.6 3.4 %collective-permute-done.9.refs_2_ = bf16[8,64,128]{2,1,0:T(8,128)(2,1)S(1)} collective-permute-done((bf16[8,64,128]{2,1,0:T(8,128)(2,1)}, bf16[8,64,128]{2,1,0:T(8,128)(2,1)S(1)}, u32[]{:S(2)}, u32[]{:S(2)}) %collective-permute-start.9) | collective-permute-done | bytes 131104 | tf_op jit(solution)/shard_map/ppermute | solution.py:517
  77.0 0.7 all-to-all-done.2.refs_0_
  77.7 0.9 copy-done.4
  78.6 1.1 shard_map.143
  79.7 3.9 %collective-permute-start.11 = (bf16[11,16,1024]{2,1,0:T(8,128)(2,1)S(1)}, bf16[11,16,1024]{2,1,0:T(8,128)(2,1)S(1)}, u32[]{:S(2)}, u32[]{:S(2)}) collective-permute-start(bf16[11,16,1024]{2,1,0:T(8,128)(2,1)S(1)} %copy-done.15), channel_id=1, source_target_pairs={{0,12},{4,8},{8,4},{12,0},{16,28},{20,24},{24,20},{28,16},{1,13},{... | collective-permute-start | bytes 1081352 | tf_op jit(solution)/shard_map/ppermute | solution.py:517
  83.6 5.7 %all-to-all-start.3 = ((bf16[8,64,128]{2,1,0:T(8,128)(2,1)}), bf16[8,64,128]{2,1,0:T(8,128)(2,1)S(1)}, u32[]{:S(2)}, u32[]{:S(2)}) async-start(bf16[8,64,128]{2,1,0:T(8,128)(2,1)} %shard_map.143), calls=%async_computation.3 | async-start | bytes 262144 | tf_op jit(solution)/shard_map/all_to_all | solution.py:652
  89.4 1.7 %shard_map.144.refs_2_ = bf16[128,16,1024]{2,1,0:T(8,128)(2,1)} custom-call(s32[8]{0:T(128)S(1)} %iota_multiply_fusion.place_ref, bf16[40,16,1024]{2,1,0:T(8,128)(2,1)S(1)} %all-to-all-done.2.refs_0_, bf16[128,16,1024]{2,1,0:T(8,128)(2,1)} %shard_map.141.refs_1_), custom_call_target="tpu_custom_call", output_to_operand_aliasing={{}: (2, {})} | custom-call | bytes 2621440 | tf_op jit(solution)/shard_map/pallas_call | solution.py:156
  91.0 11.9 %all-to-all-done.3.refs_0_ = bf16[8,64,128]{2,1,0:T(8,128)(2,1)S(1)} async-done(((bf16[8,64,128]{2,1,0:T(8,128)(2,1)}), bf16[8,64,128]{2,1,0:T(8,128)(2,1)S(1)}, u32[]{:S(2)}, u32[]{:S(2)}) %all-to-all-start.3) | async-done | bytes 131104 | tf_op jit(solution)/shard_map/all_to_all | solution.py:652
  102.9 0.9 shard_map.145
  103.8 1.6 %collective-permute-start.13 = (bf16[11,16,1024]{2,1,0:T(8,128)(2,1)}, bf16[11,16,1024]{2,1,0:T(8,128)(2,1)S(1)}, u32[]{:S(2)}, u32[]{:S(2)}) collective-permute-start(bf16[11,16,1024]{2,1,0:T(8,128)(2,1)} %get-tuple-element.140), channel_id=1, source_target_pairs={{0,8},{4,12},{8,0},{12,4},{16,24},{20,28},{24,16},{28,20},{1,9},{5... | collective-permute-start | bytes 1081352 | tf_op jit(solution)/shard_map/ppermute | solution.py:517
  105.5 1.2 collective-permute-start.14
  106.6 5.4 %all-to-all-start.4 = ((bf16[8,40,128]{2,1,0:T(8,128)(2,1)}), bf16[8,40,128]{2,1,0:T(8,128)(2,1)S(1)}, u32[]{:S(2)}, u32[]{:S(2)}) async-start(bf16[8,40,128]{2,1,0:T(8,128)(2,1)} %shard_map.145), calls=%async_computation.4 | async-start | bytes 163840 | tf_op jit(solution)/shard_map/all_to_all | solution.py:657
  112.1 1.4 shard_map.146.refs_2_
  113.5 11.3 %all-to-all-done.4.part_ref = bf16[8,40,128]{2,1,0:T(8,128)(2,1)S(1)} async-done(((bf16[8,40,128]{2,1,0:T(8,128)(2,1)}), bf16[8,40,128]{2,1,0:T(8,128)(2,1)S(1)}, u32[]{:S(2)}, u32[]{:S(2)}) %all-to-all-start.4) | async-done | bytes 81952 | tf_op jit(solution)/shard_map/all_to_all | solution.py:657
  124.8 0.9 shard_map.147
  125.8 1.5 %collective-permute-start.18 = (bf16[11,16,1024]{2,1,0:T(8,128)(2,1)S(1)}, bf16[11,16,1024]{2,1,0:T(8,128)(2,1)S(1)}, u32[]{:S(2)}, u32[]{:S(2)}) collective-permute-start(bf16[11,16,1024]{2,1,0:T(8,128)(2,1)S(1)} %copy-done.13), channel_id=1, source_target_pairs={{0,28},{4,24},{8,20},{12,16},{16,12},{20,8},{24,4},{28,0},{1,29},{... | collective-permute-start | bytes 1081352 | tf_op jit(solution)/shard_map/ppermute | solution.py:517
  127.3 0.5 collective-permute-start.16
  127.7 1.4 collective-permute-start.17
  129.2 1.4 shard_map.148.refs_1_
  130.6 0.8 collective-permute-done.16
  131.4 9.4 %collective-permute-done.18.refs_0_ = bf16[11,16,1024]{2,1,0:T(8,128)(2,1)S(1)} collective-permute-done((bf16[11,16,1024]{2,1,0:T(8,128)(2,1)S(1)}, bf16[11,16,1024]{2,1,0:T(8,128)(2,1)S(1)}, u32[]{:S(2)}, u32[]{:S(2)}) %collective-permute-start.18) | collective-permute-done | bytes 360480 | tf_op jit(solution)/shard_map/ppermute | solution.py:517
  140.9 0.6 add_convert_fusion
  141.5 0.7 shard_map.149
  (51 shorter events, 0.3 us)
Async XLA Ops:
  0.6 14.1 %copy-start.1 = (bf16[1024,512]{1,0:T(8,128)(2,1)S(1)}, bf16[1024,512]{1,0:T(8,128)(2,1)}, u32[]{:S(2)}) copy-start(bf16[1024,512]{1,0:T(8,128)(2,1)} %query_ref.1) | copy-start | bytes 3145732
  0.6 14.1 %copy-start.3 = (bf16[1024,128]{1,0:T(8,128)(2,1)S(1)}, bf16[1024,128]{1,0:T(8,128)(2,1)}, u32[]{:S(2)}) copy-start(bf16[1024,128]{1,0:T(8,128)(2,1)} %keyval_ref.1) | copy-start | bytes 786436
  2.1 12.6 %all-to-all-start = ((bf16[8,5,1024]{2,1,0:T(8,128)(2,1)}), bf16[8,5,1024]{2,1,0:T(8,128)(2,1)S(1)}, u32[]{:S(2)}, u32[]{:S(2)}) async-start(bf16[8,5,1024]{2,1,0:T(8,128)(2,1)} %broadcast_in_dim.2), calls=%async_computation | async-start | bytes 262144 | tf_op jit(solution)/shard_map/all_to_all | solution.py:490
  9.0 5.7 %copy-start.6 = (s32[2]{0:T(128)S(1)}, s32[2]{0:T(128)}, u32[]{:S(2)}) copy-start(s32[2]{0:T(128)} %pad_add_fusion.me_ref) | copy-start | bytes 28
  9.0 40.8 %copy-start.9 = (s32[8]{0:T(128)S(1)}, s32[8]{0:T(128)}, u32[]{:S(2)}) copy-start(s32[8]{0:T(128)} %kept_ref.1) | copy-start | bytes 100
  15.7 1.9 %collective-permute-start = (f32[40,256]{1,0:T(8,128)S(1)}, f32[40,256]{1,0:T(8,128)S(1)}, u32[]{:S(2)}, u32[]{:S(2)}) collective-permute-start(f32[40,256]{1,0:T(8,128)S(1)} %get-tuple-element.93), channel_id=1, source_target_pairs={{0,1},{1,0},{2,3},{3,2},{4,5},{5,4},{6,7},{7,6},{8,9},{9,8},{10,11... | collective-permute-start | bytes 122888 | tf_op jit(solution)/shard_map/ppermute | solution.py:517
  15.8 4.5 %collective-permute-start.1 = (f32[40,256]{1,0:T(8,128)S(1)}, f32[40,256]{1,0:T(8,128)S(1)}, u32[]{:S(2)}, u32[]{:S(2)}) collective-permute-start(f32[40,256]{1,0:T(8,128)S(1)} %get-tuple-element.94), channel_id=1, source_target_pairs={{0,2},{1,3},{2,0},{3,1},{4,6},{5,7},{6,4},{7,5},{8,10},{9,11},{10,... | collective-permute-start | bytes 122888 | tf_op jit(solution)/shard_map/ppermute | solution.py:517
  16.4 3.9 %collective-permute-start.2 = (f32[40,256]{1,0:T(8,128)S(1)}, f32[40,256]{1,0:T(8,128)S(1)}, u32[]{:S(2)}, u32[]{:S(2)}) collective-permute-start(f32[40,256]{1,0:T(8,128)S(1)} %get-tuple-element.95), channel_id=1, source_target_pairs={{0,3},{1,2},{2,1},{3,0},{4,7},{5,6},{6,5},{7,4},{8,11},{9,10},{10,... | collective-permute-start | bytes 122888 | tf_op jit(solution)/shard_map/ppermute | solution.py:517
  20.3 0.7 copy-start.8
  21.0 23.4 %collective-permute-start.3 = (bf16[11,16,1024]{2,1,0:T(8,128)(2,1)}, bf16[11,16,1024]{2,1,0:T(8,128)(2,1)S(1)}, u32[]{:S(2)}, u32[]{:S(2)}) collective-permute-start(bf16[11,16,1024]{2,1,0:T(8,128)(2,1)} %get-tuple-element.100), channel_id=1, source_target_pairs={{0,24},{4,28},{8,16},{12,20},{16,8},{20,12},{24,0},{28,4},{1,25},{... | collective-permute-start | bytes 1081352 | tf_op jit(solution)/shard_map/ppermute | solution.py:517
  22.5 21.9 %collective-permute-start.4 = (bf16[11,16,1024]{2,1,0:T(8,128)(2,1)}, bf16[11,16,1024]{2,1,0:T(8,128)(2,1)S(1)}, u32[]{:S(2)}, u32[]{:S(2)}) collective-permute-start(bf16[11,16,1024]{2,1,0:T(8,128)(2,1)} %get-tuple-element.101), channel_id=1, source_target_pairs={{0,4},{4,0},{8,12},{12,8},{16,20},{20,16},{24,28},{28,24},{1,5},{5... | collective-permute-start | bytes 1081352 | tf_op jit(solution)/shard_map/ppermute | solution.py:517
  44.4 33.3 %all-to-all-start.2 = ((bf16[40,16,1024]{2,1,0:T(8,128)(2,1)}), bf16[40,16,1024]{2,1,0:T(8,128)(2,1)S(1)}, u32[]{:S(2)}, u32[]{:S(2)}) async-start(bf16[40,16,1024]{2,1,0:T(8,128)(2,1)} %get-tuple-element.119), calls=%async_computation.2 | async-start | bytes 2621440 | tf_op jit(solution)/shard_map/all_to_all | solution.py:543
  51.1 3.4 %copy-start = (bf16[128,1024]{1,0:T(8,128)(2,1)}, bf16[128,1024]{1,0:T(8,128)(2,1)S(1)}, u32[]{:S(2)}) copy-start(bf16[128,1024]{1,0:T(8,128)(2,1)S(1)} %get-tuple-element.113.refs_6_.refs_7_) | copy-start | bytes 786436
  51.1 3.4 %copy-start.5 = (bf16[8,40,128]{2,1,0:T(8,128)(2,1)}, bf16[8,40,128]{2,1,0:T(8,128)(2,1)S(1)}, u32[]{:S(2)}) copy-start(bf16[8,40,128]{2,1,0:T(8,128)(2,1)S(1)} %get-tuple-element.109.refs_0_) | copy-start | bytes 245764
  51.1 3.4 %collective-permute-start.5 = (bf16[8,40,128]{2,1,0:T(8,128)(2,1)S(1)}, bf16[8,40,128]{2,1,0:T(8,128)(2,1)S(1)}, u32[]{:S(2)}, u32[]{:S(2)}) collective-permute-start(bf16[8,40,128]{2,1,0:T(8,128)(2,1)S(1)} %get-tuple-element.109.refs_0_), channel_id=1, source_target_pairs={{0,1},{1,0},{2,3},{3,2},{4,5},{5,4},{6,7},{7,6},{8,9},{9,8},{10,11... | collective-permute-start | bytes 245768 | tf_op jit(solution)/shard_map/ppermute | solution.py:517
  51.1 5.3 %collective-permute-start.6 = (bf16[8,40,128]{2,1,0:T(8,128)(2,1)S(1)}, bf16[8,40,128]{2,1,0:T(8,128)(2,1)S(1)}, u32[]{:S(2)}, u32[]{:S(2)}) collective-permute-start(bf16[8,40,128]{2,1,0:T(8,128)(2,1)S(1)} %get-tuple-element.109.refs_0_), channel_id=1, source_target_pairs={{0,2},{1,3},{2,0},{3,1},{4,6},{5,7},{6,4},{7,5},{8,10},{9,11},{10,... | collective-permute-start | bytes 245768 | tf_op jit(solution)/shard_map/ppermute | solution.py:517
  52.3 5.0 %collective-permute-start.7 = (bf16[8,40,128]{2,1,0:T(8,128)(2,1)S(1)}, bf16[8,40,128]{2,1,0:T(8,128)(2,1)S(1)}, u32[]{:S(2)}, u32[]{:S(2)}) collective-permute-start(bf16[8,40,128]{2,1,0:T(8,128)(2,1)S(1)} %get-tuple-element.109.refs_0_), channel_id=1, source_target_pairs={{0,3},{1,2},{2,1},{3,0},{4,7},{5,6},{6,5},{7,4},{8,11},{9,10},{10,... | collective-permute-start | bytes 245768 | tf_op jit(solution)/shard_map/ppermute | solution.py:517
  54.5 2.8 %copy-start.10 = (bf16[8,40,128]{2,1,0:T(8,128)(2,1)}, bf16[8,40,128]{2,1,0:T(8,128)(2,1)S(1)}, u32[]{:S(2)}) copy-start(bf16[8,40,128]{2,1,0:T(8,128)(2,1)S(1)} %collective-permute-done.5.refs_1_) | copy-start | bytes 245764
  56.5 0.8 copy-start.11
  57.3 0.6 copy-start.12
  57.9 21.8 %copy-start.15 = (bf16[11,16,1024]{2,1,0:T(8,128)(2,1)S(1)}, bf16[11,16,1024]{2,1,0:T(8,128)(2,1)}, u32[]{:S(2)}) copy-start(bf16[11,16,1024]{2,1,0:T(8,128)(2,1)} %get-tuple-element.129) | copy-start | bytes 1081348
  57.9 25.7 %copy-start.14 = (bf16[11,16,1024]{2,1,0:T(8,128)(2,1)S(1)}, bf16[11,16,1024]{2,1,0:T(8,128)(2,1)}, u32[]{:S(2)}) copy-start(bf16[11,16,1024]{2,1,0:T(8,128)(2,1)} %get-tuple-element.130) | copy-start | bytes 1081348
  68.2 5.5 %collective-permute-start.10 = (bf16[8,64,128]{2,1,0:T(8,128)(2,1)}, bf16[8,64,128]{2,1,0:T(8,128)(2,1)S(1)}, u32[]{:S(2)}, u32[]{:S(2)}) collective-permute-start(bf16[8,64,128]{2,1,0:T(8,128)(2,1)} %get-tuple-element.118), channel_id=1, source_target_pairs={{0,3},{1,2},{2,1},{3,0},{4,7},{5,6},{6,5},{7,4},{8,11},{9,10},{10,... | collective-permute-start | bytes 393224 | tf_op jit(solution)/shard_map/ppermute | solution.py:517
  69.5 4.2 %collective-permute-start.8 = (bf16[8,64,128]{2,1,0:T(8,128)(2,1)}, bf16[8,64,128]{2,1,0:T(8,128)(2,1)S(1)}, u32[]{:S(2)}, u32[]{:S(2)}) collective-permute-start(bf16[8,64,128]{2,1,0:T(8,128)(2,1)} %get-tuple-element.116), channel_id=1, source_target_pairs={{0,1},{1,0},{2,3},{3,2},{4,5},{5,4},{6,7},{7,6},{8,9},{9,8},{10,11... | collective-permute-start | bytes 393224 | tf_op jit(solution)/shard_map/ppermute | solution.py:517
  69.5 7.6 %collective-permute-start.9 = (bf16[8,64,128]{2,1,0:T(8,128)(2,1)}, bf16[8,64,128]{2,1,0:T(8,128)(2,1)S(1)}, u32[]{:S(2)}, u32[]{:S(2)}) collective-permute-start(bf16[8,64,128]{2,1,0:T(8,128)(2,1)} %get-tuple-element.117), channel_id=1, source_target_pairs={{0,2},{1,3},{2,0},{3,1},{4,6},{5,7},{6,4},{7,5},{8,10},{9,11},{10,... | collective-permute-start | bytes 393224 | tf_op jit(solution)/shard_map/ppermute | solution.py:517
  77.7 0.9 copy-start.4
  79.7 23.2 %collective-permute-start.11 = (bf16[11,16,1024]{2,1,0:T(8,128)(2,1)S(1)}, bf16[11,16,1024]{2,1,0:T(8,128)(2,1)S(1)}, u32[]{:S(2)}, u32[]{:S(2)}) collective-permute-start(bf16[11,16,1024]{2,1,0:T(8,128)(2,1)S(1)} %copy-done.15), channel_id=1, source_target_pairs={{0,12},{4,8},{8,4},{12,0},{16,28},{20,24},{24,20},{28,16},{1,13},{... | collective-permute-start | bytes 1081352 | tf_op jit(solution)/shard_map/ppermute | solution.py:517
  83.6 19.3 %collective-permute-start.12 = (bf16[11,16,1024]{2,1,0:T(8,128)(2,1)S(1)}, bf16[11,16,1024]{2,1,0:T(8,128)(2,1)S(1)}, u32[]{:S(2)}, u32[]{:S(2)}) collective-permute-start(bf16[11,16,1024]{2,1,0:T(8,128)(2,1)S(1)} %copy-done.14), channel_id=1, source_target_pairs={{0,16},{4,20},{8,24},{12,28},{16,0},{20,4},{24,8},{28,12},{1,17},{... | collective-permute-start | bytes 1081352 | tf_op jit(solution)/shard_map/ppermute | solution.py:517
  83.6 19.3 %all-to-all-start.3 = ((bf16[8,64,128]{2,1,0:T(8,128)(2,1)}), bf16[8,64,128]{2,1,0:T(8,128)(2,1)S(1)}, u32[]{:S(2)}, u32[]{:S(2)}) async-start(bf16[8,64,128]{2,1,0:T(8,128)(2,1)} %shard_map.143), calls=%async_computation.3 | async-start | bytes 262144 | tf_op jit(solution)/shard_map/all_to_all | solution.py:652
  103.8 21.0 %collective-permute-start.13 = (bf16[11,16,1024]{2,1,0:T(8,128)(2,1)}, bf16[11,16,1024]{2,1,0:T(8,128)(2,1)S(1)}, u32[]{:S(2)}, u32[]{:S(2)}) collective-permute-start(bf16[11,16,1024]{2,1,0:T(8,128)(2,1)} %get-tuple-element.140), channel_id=1, source_target_pairs={{0,8},{4,12},{8,0},{12,4},{16,24},{20,28},{24,16},{28,20},{1,9},{5... | collective-permute-start | bytes 1081352 | tf_op jit(solution)/shard_map/ppermute | solution.py:517
  105.5 19.3 %collective-permute-start.14 = (bf16[11,16,1024]{2,1,0:T(8,128)(2,1)}, bf16[11,16,1024]{2,1,0:T(8,128)(2,1)S(1)}, u32[]{:S(2)}, u32[]{:S(2)}) collective-permute-start(bf16[11,16,1024]{2,1,0:T(8,128)(2,1)} %get-tuple-element.141), channel_id=1, source_target_pairs={{0,20},{4,16},{8,28},{12,24},{16,4},{20,0},{24,12},{28,8},{1,21},{... | collective-permute-start | bytes 1081352 | tf_op jit(solution)/shard_map/ppermute | solution.py:517
  106.6 18.2 %all-to-all-start.4 = ((bf16[8,40,128]{2,1,0:T(8,128)(2,1)}), bf16[8,40,128]{2,1,0:T(8,128)(2,1)S(1)}, u32[]{:S(2)}, u32[]{:S(2)}) async-start(bf16[8,40,128]{2,1,0:T(8,128)(2,1)} %shard_map.145), calls=%async_computation.4 | async-start | bytes 163840 | tf_op jit(solution)/shard_map/all_to_all | solution.py:657
  112.1 12.7 %copy-start.2 = (bf16[1024,512]{1,0:T(8,128)(2,1)S(1)}, bf16[1024,512]{1,0:T(8,128)(2,1)}, u32[]{:S(2)}) copy-start(bf16[1024,512]{1,0:T(8,128)(2,1)} %weight_ref.1) | copy-start | bytes 3145732
  112.1 12.7 %copy-start.7 = (s32[2]{0:T(128)S(1)}, s32[2]{0:T(128)}, u32[]{:S(2)}) copy-start(s32[2]{0:T(128)} %pad_add_fusion.me_ref) | copy-start | bytes 28
  112.1 13.7 %copy-start.13 = (bf16[11,16,1024]{2,1,0:T(8,128)(2,1)S(1)}, bf16[11,16,1024]{2,1,0:T(8,128)(2,1)}, u32[]{:S(2)}) copy-start(bf16[11,16,1024]{2,1,0:T(8,128)(2,1)} %get-tuple-element.161) | copy-start | bytes 1081348
  125.8 15.1 %collective-permute-start.18 = (bf16[11,16,1024]{2,1,0:T(8,128)(2,1)S(1)}, bf16[11,16,1024]{2,1,0:T(8,128)(2,1)S(1)}, u32[]{:S(2)}, u32[]{:S(2)}) collective-permute-start(bf16[11,16,1024]{2,1,0:T(8,128)(2,1)S(1)} %copy-done.13), channel_id=1, source_target_pairs={{0,28},{4,24},{8,20},{12,16},{16,12},{20,8},{24,4},{28,0},{1,29},{... | collective-permute-start | bytes 1081352 | tf_op jit(solution)/shard_map/ppermute | solution.py:517
  127.3 3.4 %collective-permute-start.15 = (f32[10,512]{1,0:T(8,128)S(1)}, f32[10,512]{1,0:T(8,128)S(1)}, u32[]{:S(2)}, u32[]{:S(2)}) collective-permute-start(f32[10,512]{1,0:T(8,128)S(1)} %get-tuple-element.158), channel_id=1, source_target_pairs={{0,1},{1,0},{2,3},{3,2},{4,5},{5,4},{6,7},{7,6},{8,9},{9,8},{10,11... | collective-permute-start | bytes 61448 | tf_op jit(solution)/shard_map/ppermute | solution.py:517
  127.3 4.2 %collective-permute-start.16 = (f32[10,512]{1,0:T(8,128)S(1)}, f32[10,512]{1,0:T(8,128)S(1)}, u32[]{:S(2)}, u32[]{:S(2)}) collective-permute-start(f32[10,512]{1,0:T(8,128)S(1)} %get-tuple-element.159), channel_id=1, source_target_pairs={{0,2},{1,3},{2,0},{3,1},{4,6},{5,7},{6,4},{7,5},{8,10},{9,11},{10,... | collective-permute-start | bytes 61448 | tf_op jit(solution)/shard_map/ppermute | solution.py:517
  127.7 3.7 %collective-permute-start.17 = (f32[10,512]{1,0:T(8,128)S(1)}, f32[10,512]{1,0:T(8,128)S(1)}, u32[]{:S(2)}, u32[]{:S(2)}) collective-permute-start(f32[10,512]{1,0:T(8,128)S(1)} %get-tuple-element.160), channel_id=1, source_target_pairs={{0,3},{1,2},{2,1},{3,0},{4,7},{5,6},{6,5},{7,4},{8,11},{9,10},{10,... | collective-permute-start | bytes 61448 | tf_op jit(solution)/shard_map/ppermute | solution.py:517

commit v15 on v10

--- a/solution.py
+++ b/solution.py
@@ -18,7 +18,7 @@
 SCALE2 = math.log2(math.e) / math.sqrt(HD)
 STAT = 16
 MIB = 1024 * 1024
-CUTS = {1: (0, 8, 16), 2: (0, 7, 16), 3: (0, 5, 16), 4: (0, 13, 16), 5: (0, 10, 16), 6: (0, 4, 16), 7: (0, 4, 11, 16)}
+CUTS = {1: (0, 16), 2: (0, 12, 16), 3: (0, 16), 4: (0, 16), 5: (0, 12, 16), 6: (0, 12, 16), 7: (0, 16)}
 NT = (((1,), (1,)), ((), ()))
 
 
@@ -312,7 +312,7 @@
             pltpu.VMEM((pieces, height, HD), jnp.bfloat16),
         ],
         compiler_params=pltpu.CompilerParams(vmem_limit_bytes=56 * MIB),
-        cost_estimate=pl.CostEstimate(flops=0, bytes_accessed=0, transcendentals=0),
+        cost_estimate=pl.CostEstimate(flops=1, bytes_accessed=1, transcendentals=0),
     )(me, lengths, *queries, pool, pool, keyval, keyval, token_info)
 
 
@@ -558,11 +558,14 @@
 
     def placed(pages):
         taken = sorted(arrived)
+        if not taken:
+            return pages
         place = jnp.stack([(me ^ parts[c][0]) * capacity + parts[c][1] for c in taken])
         pages = place_pages(place, [arrived[c] for c in taken], pages)
         arrived.clear()
         return pages
 
+    gathered, tags = lax.optimization_barrier((gathered, tags))
     tokens = pool.reshape(slots * PAGE, -1)
     if direct:
         block = jax.ShapeDtypeStruct((rows, 2 * HD), jnp.float32)
@@ -575,7 +578,7 @@
             w_keyval,
             scratch=[pltpu.VMEM((rows, narrow * HD), jnp.float32)],
         )
-        partial = beside(lambda value: deal(value, "narrow"), partial, (6, 0), (1, 0))
+        partial = deal(partial, "narrow")
         packed = in_vmem(
             functools.partial(pack_kernel, narrow),
             jax.ShapeDtypeStruct((wide, rows + wide, 2 * HD), jnp.bfloat16),
@@ -583,7 +586,8 @@
             *partial,
             tags,
         )
-        received = beside(lambda value: exchange(value, "wide"), packed, (6, 1))
+        received = beside(lambda value: exchange(value, "wide"), packed, (1, 0), (6, 0))
+        received = launch(received, (7, 0), (6, 1))
         queries, keyval, new_entries, moved_req, moved_idx = in_vmem(
             functools.partial(unpack_kernel, rows),
             [
@@ -597,7 +601,7 @@
             received,
         )
         moved_req, moved_idx = moved_req.reshape(slots), moved_idx.reshape(slots)
-        queries = beside(lambda value: share(value, "narrow"), queries, (7, 0), (1, 1))
+        queries = share(queries, "narrow")
     else:
         gathered = gathered.reshape(rows, -1)
         query_part = jnp.dot(gathered, w_query, preferred_element_type=jnp.float32)
@@ -606,16 +610,17 @@
         partial = jnp.concatenate(
             [query_part, jnp.broadcast_to(keyval_part[None], (narrow,) + keyval_part.shape)], axis=2
         )
-        partial = beside(lambda value: exchange(value, "narrow"), partial, (6, 0), (1, 0))
+        partial = exchange(partial, "narrow")
         projected = jnp.sum(partial, axis=0).astype(jnp.bfloat16)
         tags = tags[:, : 3 * capacity].astype(jnp.bfloat16)[:, None]
         tags = jnp.pad(tags, ((0, 0), (0, 7), (0, projected.shape[1] - tags.shape[2])))
         packed = jnp.broadcast_to(projected[None], (wide,) + projected.shape)
         packed = jnp.concatenate([packed, tags], axis=1)
-        received = beside(lambda value: exchange(value, "wide"), packed, (6, 1))
+        received = beside(lambda value: exchange(value, "wide"), packed, (1, 0), (6, 0))
+        received = launch(received, (7, 0), (6, 1))
         tags_in = received[:, rows]
         queries = received[:, :rows, :own_cols]
-        queries = beside(lambda value: spread(value, "narrow"), queries, (7, 0), (1, 1))
+        queries = spread(queries, "narrow")
         queries = jnp.transpose(queries, (2, 1, 0, 3)).reshape(rows, HEADS, HD)
         queries = [jnp.transpose(queries, (1, 0, 2)).reshape(KVH, GROUPS * rows, HD)]
         keyval = jnp.transpose(received[:, :rows, own_cols:], (1, 0, 2)).reshape(rows, -1)
@@ -633,25 +638,24 @@
             step_ids < kept[:, None, None], fresh, jnp.zeros((), jnp.bfloat16)
         )
 
-    mixed = beside(
-        lambda value: attend(both, lengths, value, keyval, tokens, token_info, rows, piece),
-        queries,
-        (7, 1),
-        (2, 0),
-    )
+    queries, moved_pool = lax.optimization_barrier((queries, placed(moved_pool)))
+    mixed = attend(both, lengths, queries, keyval, tokens, token_info, rows, piece)
     if direct:
-        mixed = beside(lambda value: deal(value, "narrow"), mixed, (7, 2), (3, 0))
+        mixed = land(deal(mixed, "narrow"), (7, 0), (6, 1))
     else:
-        mixed = beside(lambda value: exchange(value, "narrow"), mixed[0], (7, 2), (3, 0))
+        mixed = land(exchange(mixed[0], "narrow"), (7, 0), (6, 1))
         mixed = mixed.reshape((narrow, wide) + mixed.shape[1:])
         mixed = [mixed[i] for i in range(narrow)]
     mixed = combine(mixed, piece)
     mixed, pages = lax.optimization_barrier((mixed, moved_pool))
     pages = placed(pages)
-    mixed = beside(lambda value: exchange(value, "wide"), mixed, (4, 0), (2, 1))
+    mixed = beside(lambda value: exchange(value, "wide"), mixed, (3, 0), (4, 0))
     mixed, moved_pool = lax.optimization_barrier((mixed, pages))
     attn = combine([mixed], piece, wide)
-    attn = beside(lambda value: exchange(value, "wide"), attn, (5, 0), (4, 1), (3, 1))
+    attn, pages = lax.optimization_barrier((attn, moved_pool))
+    pages = placed(pages)
+    attn = beside(lambda value: exchange(value, "wide"), attn, (2, 0), (5, 0))
+    attn, moved_pool = lax.optimization_barrier((attn, pages))
     if direct:
         sums = in_vmem(
             functools.partial(finish_kernel, narrow),
@@ -660,15 +664,19 @@
             attn,
             w_out,
         )
-        sums = beside(lambda value: deal(value, "narrow"), sums, (5, 1))
+        sums, pages = lax.optimization_barrier((sums, moved_pool))
+        pages = placed(pages)
+        sums = beside(lambda value: deal(value, "narrow"), sums, (2, 1), (5, 1))
         attended = ((sums[0] + sums[1]) + (sums[2] + sums[3])).astype(jnp.bfloat16)
     else:
         attn = jnp.transpose(attn.reshape(-1, rows, HD), (1, 0, 2)).reshape(rows, -1)
         sums = jnp.dot(attn, w_out, preferred_element_type=jnp.float32)
         sums = sums.reshape(narrow, rows // narrow, -1)
-        sums = beside(lambda value: exchange(value, "narrow"), sums, (5, 1))
+        pages = placed(moved_pool)
+        sums = beside(lambda value: exchange(value, "narrow"), sums, (2, 1), (5, 1))
         attended = jnp.sum(sums, axis=0).astype(jnp.bfloat16)
-    moved_pool = placed(moved_pool)
+    attended, pages = lax.optimization_barrier((attended, pages))
+    moved_pool = placed(pages)
     return (attended, new_entries, moved_pool, moved_req, moved_idx)
 
 

time: 156 us -> 145 us (0.929)
  waiting for transfers between devices: 54.5 us -> 47.6 us
  starting transfers between devices: 44.9 us -> 40.3 us
  local copies, waits for them, and re-layouts: 7.36 us -> 3.72 us
  Pallas kernels: 25 us -> 28.6 us
    ppermute x27 -> x22, waiting for transfers between devices: 39.7 us -> 13.6 us  [send(): lax.ppermute(block, axis, [(i, i ^ d) for i in range(lax.axis_size(axis))])]
    all_to_all x2, waiting for transfers between devices: 13.8 us -> 33.2 us  [the longest x1 20.2 us: on_device(): mixed = beside(lambda value: exchange(value, 'wide'), mixed, (3, 0), (4, 0))]
    ppermute x27 -> x22, starting transfers between devices: 30 us -> 25.1 us  [send(): lax.ppermute(block, axis, [(i, i ^ d) for i in range(lax.axis_size(axis))])]
    unnamed x44 -> x34, local copies, waits for them, and re-layouts: 5.72 us -> 2.27 us
    pallas_call x2 -> x5, Pallas kernels: 3.65 us -> 7.09 us  [place_pages(): pl.pallas_call(place_kernel, out_shape=jax.ShapeDtypeStruct(pages.shape,...]
  transfers between devices with their start and end apart: 30 -> 25, of which waited for: 16 -> 12; matrix products, arithmetic and copies ran while one was open for 0% -> 1% of each run, Pallas kernels for 12% -> 16%
where the time goes in v15:
time: 145 us; the launch traced here: 144 us
  waiting for transfers between devices  47.6 us (33%)
  starting transfers between devices  40.3 us (28%)
  Pallas kernels  28.6 us (20%)
  blocking collectives  21.4 us (15%)
  local copies, waits for them, and re-layouts  3.72 us (3%)
  other arithmetic  1.6 us (1%)
    ppermute x22, starting transfers between devices, send(): lax.ppermute(block, axis, [(i, i ^ d) for i in range(lax.axis_size(axis))])  25.1 us
    all_to_all x1, blocking collectives, on_device(): exchange(value, 'wide')  21.4 us
    all_to_all x1, waiting for transfers between devices, on_device(): mixed = beside(lambda value: exchange(value, 'wide'), mixed, (3, 0), (4, 0))  20.2 us
    ppermute x22, waiting for transfers between devices, send(): lax.ppermute(block, axis, [(i, i ^ d) for i in range(lax.axis_size(axis))])  13.6 us
    all_to_all x1, waiting for transfers between devices, on_device(): attn = beside(lambda value: exchange(value, 'wide'), attn, (2, 0), (5, 0))  13 us
    pallas_call x1, Pallas kernels, attend(): pl.pallas_call(functools.partial(attend_kernel, rows, piece, peers), grid...  10.3 us
    all_to_all x1, starting transfers between devices, spread(): lax.all_to_all(jnp.broadcast_to(block[None], (count,) + block.shape), axi...  7.28 us
    pallas_call x5, Pallas kernels, place_pages(): pl.pallas_call(place_kernel, out_shape=jax.ShapeDtypeStruct(pages.shape,...  7.09 us
  transfers between devices with their start and end apart: 25, of which 12 were waited for; matrix products, arithmetic and copies ran while one was open for 1% of the time, Pallas kernels for 16%

profile of v15, /device:TPU:0, one launch (start us, length us, event | category | flops | bytes accessed | tf_op | source)
XLA Modules:
  0.0 144.0 jit_solution(4222984912464523114)
XLA Ops:
  0.7 1.5 %broadcast_in_dim.2 = bf16[8,5,1024]{2,1,0:T(8,128)(2,1)} broadcast(bf16[5,1024]{1,0:T(8,128)(2,1)} %param.10), dimensions={1,2} | broadcast | bytes 92160 | tf_op jit(solution)/shard_map/broadcast_in_dim | solution.py:485
  2.1 7.3 %all-to-all-start = ((bf16[8,5,1024]{2,1,0:T(8,128)(2,1)}), bf16[8,5,1024]{2,1,0:T(8,128)(2,1)S(1)}, u32[]{:S(2)}, u32[]{:S(2)}) async-start(bf16[8,5,1024]{2,1,0:T(8,128)(2,1)} %broadcast_in_dim.2), calls=%async_computation | async-start | bytes 262144 | tf_op jit(solution)/shard_map/all_to_all | solution.py:484
  9.4 0.6 pad_add_fusion.me_ref
  10.0 5.9 %shard_map.137 = (bf16[128,16,1024]{2,1,0:T(8,128)(2,1)}, f32[8,128]{1,0:T(8,128)}, f32[8,2048]{1,0:T(8,128)}, bf16[16,16,1024]{2,1,0:T(8,128)(2,1)}, bf16[12,16...) custom-call(s32[2]{0:T(128)} %pad_add_fusion.me_ref, ...), custom_call_target="tpu_custom_call" | custom-call | bytes 8388608 | tf_op jit(solution)/shard_map/pallas_call | solution.py:110
  15.9 0.8 all-to-all-done.hidden_ref
  16.8 1.0 shard_map.138
  17.8 1.6 %collective-permute-start.1 = (f32[40,256]{1,0:T(8,128)S(1)}, f32[40,256]{1,0:T(8,128)S(1)}, u32[]{:S(2)}, u32[]{:S(2)}) collective-permute-start(f32[40,256]{1,0:T(8,128)S(1)} %get-tuple-element.100), channel_id=1, source_target_pairs={{0,2},{1,3},{2,0},{3,1},{4,6},{5,7},{6,4},{7,5},{8,10},{9,11},{10,... | collective-permute-start | bytes 122888 | tf_op jit(solution)/shard_map/ppermute | solution.py:511
  19.7 2.2 %collective-permute-done.1.refs_2_ = f32[40,256]{1,0:T(8,128)S(1)} collective-permute-done((f32[40,256]{1,0:T(8,128)S(1)}, f32[40,256]{1,0:T(8,128)S(1)}, u32[]{:S(2)}, u32[]{:S(2)}) %collective-permute-start.1) | collective-permute-done | bytes 40992 | tf_op jit(solution)/shard_map/ppermute | solution.py:511
  21.9 1.0 collective-permute-done.2.refs_3_
  22.9 0.7 copy-done.8
  23.6 1.3 collective-permute-start.3
  24.9 3.3 %collective-permute-start.4 = (bf16[12,16,1024]{2,1,0:T(8,128)(2,1)}, bf16[12,16,1024]{2,1,0:T(8,128)(2,1)S(1)}, u32[]{:S(2)}, u32[]{:S(2)}) collective-permute-start(bf16[12,16,1024]{2,1,0:T(8,128)(2,1)} %get-tuple-element.107), channel_id=1, source_target_pairs={{0,24},{4,28},{8,16},{12,20},{16,8},{20,12},{24,0},{28,4},{1,25},{... | collective-permute-start | bytes 1179656 | tf_op jit(solution)/shard_map/ppermute | solution.py:511
  28.2 21.4 %all_to_all.20.part_ref = bf16[8,48,256]{2,1,0:T(8,128)(2,1)S(1)} all-to-all(bf16[8,48,256]{2,1,0:T(8,128)(2,1)S(1)} %shard_map.139), channel_id=1, replica_groups=mesh['wide'=8,'narrow'=4] {'wide'}, dimensions={0} | all-to-all | bytes 393216 | tf_op jit(solution)/shard_map/all_to_all | solution.py:589
  49.6 3.0 %collective-permute-start.11 = (bf16[16,16,1024]{2,1,0:T(8,128)(2,1)}, bf16[16,16,1024]{2,1,0:T(8,128)(2,1)S(1)}, u32[]{:S(2)}, u32[]{:S(2)}) collective-permute-start(bf16[16,16,1024]{2,1,0:T(8,128)(2,1)} %get-tuple-element.126), channel_id=1, source_target_pairs={{0,28},{4,24},{8,20},{12,16},{16,12},{20,8},{24,4},{28,0},{1,29},{... | collective-permute-start | bytes 1572872 | tf_op jit(solution)/shard_map/ppermute | solution.py:511
  52.6 1.4 shard_map.140
  54.0 1.0 collective-permute-start.6
  55.0 0.8 collective-permute-start.7
  55.9 1.5 %collective-permute-start.12 = (bf16[4,16,1024]{2,1,0:T(8,128)(2,1)}, bf16[4,16,1024]{2,1,0:T(8,128)(2,1)S(1)}, u32[]{:S(2)}, u32[]{:S(2)}) collective-permute-start(bf16[4,16,1024]{2,1,0:T(8,128)(2,1)} %get-tuple-element.127), channel_id=1, source_target_pairs={{0,24},{4,28},{8,16},{12,20},{16,8},{20,12},{24,0},{28,4},{1,25},{... | collective-permute-start | bytes 393224 | tf_op jit(solution)/shard_map/ppermute | solution.py:511
  57.4 1.5 %shard_map.141.refs_2_ = bf16[128,16,1024]{2,1,0:T(8,128)(2,1)} custom-call(s32[2]{0:T(128)S(1)} %pad_add_fusion.1.place_ref, bf16[16,16,1024]{2,1,0:T(8,128)(2,1)S(1)} %collective-permute-done.3.refs_0_, bf16[12,16,1024]{2,1,0:T(8,128)(2,1)S(1)} %collective-permute-done.4.refs_1_, ...), custom_call_target="tpu_custom_call", output_to_operand_aliasing={{}: (3, {})} | custom-call | bytes 2097152 | tf_op jit(solution)/shard_map/pallas_call | solution.py:148
  59.3 0.8 collective-permute-done.7.refs_3_
  60.1 0.6 copy-done.12
  60.7 10.3 %shard_map.142 = (bf16[8,64,128]{2,1,0:T(8,128)(2,1)}, bf16[8,64,128]{2,1,0:T(8,128)(2,1)}, bf16[8,64,128]{2,1,0:T(8,128)(2,1)}, bf16[8,64,128]{2,1,0:T(8,128)(2,1)}) custom-call(s32[2]{0:T(128)} %pad_add_fusion.me_ref, s32[8]{0:T(128)} %length_ref.1, bf16[8,40,128]{2,1,0:T(8,128)(2,1)} %copy-done.5, bf16[8,40,128]{2,1,0:T(8,128)(2,1)} %copy-done.10, ...), custom_call_target="tpu_custom_call" | custom-call | flops 1 | bytes 1 | tf_op jit(solution)/shard_map/pallas_call | solution.py:292
  71.0 1.2 collective-permute-start.10
  72.2 1.1 collective-permute-start.9
  73.3 3.1 %collective-permute-done.10.refs_3_ = bf16[8,64,128]{2,1,0:T(8,128)(2,1)S(1)} collective-permute-done((bf16[8,64,128]{2,1,0:T(8,128)(2,1)}, bf16[8,64,128]{2,1,0:T(8,128)(2,1)S(1)}, u32[]{:S(2)}, u32[]{:S(2)}) %collective-permute-start.10) | collective-permute-done | bytes 131104 | tf_op jit(solution)/shard_map/ppermute | solution.py:511
  76.4 3.5 %collective-permute-done.9.refs_2_ = bf16[8,64,128]{2,1,0:T(8,128)(2,1)S(1)} collective-permute-done((bf16[8,64,128]{2,1,0:T(8,128)(2,1)}, bf16[8,64,128]{2,1,0:T(8,128)(2,1)S(1)}, u32[]{:S(2)}, u32[]{:S(2)}) %collective-permute-start.9) | collective-permute-done | bytes 131104 | tf_op jit(solution)/shard_map/ppermute | solution.py:511
  79.9 0.9 copy-done.4
  80.8 1.1 shard_map.143
  82.2 2.0 %collective-permute-start.14 = (bf16[16,16,1024]{2,1,0:T(8,128)(2,1)S(1)}, bf16[16,16,1024]{2,1,0:T(8,128)(2,1)S(1)}, u32[]{:S(2)}, u32[]{:S(2)}) collective-permute-start(bf16[16,16,1024]{2,1,0:T(8,128)(2,1)S(1)} %copy-done.13), channel_id=1, source_target_pairs={{0,16},{4,20},{8,24},{12,28},{16,0},{20,4},{24,8},{28,12},{1,17},{... | collective-permute-start | bytes 1572872 | tf_op jit(solution)/shard_map/ppermute | solution.py:511
  84.2 4.3 %all-to-all-start.2 = ((bf16[8,64,128]{2,1,0:T(8,128)(2,1)}), bf16[8,64,128]{2,1,0:T(8,128)(2,1)S(1)}, u32[]{:S(2)}, u32[]{:S(2)}) async-start(bf16[8,64,128]{2,1,0:T(8,128)(2,1)} %shard_map.143), calls=%async_computation.2 | async-start | bytes 262144 | tf_op jit(solution)/shard_map/all_to_all | solution.py:652
  88.6 1.4 shard_map.144.refs_2_
  90.0 20.2 %all-to-all-done.2.refs_0_ = bf16[8,64,128]{2,1,0:T(8,128)(2,1)S(1)} async-done(((bf16[8,64,128]{2,1,0:T(8,128)(2,1)}), bf16[8,64,128]{2,1,0:T(8,128)(2,1)S(1)}, u32[]{:S(2)}, u32[]{:S(2)}) %all-to-all-start.2) | async-done | bytes 131104 | tf_op jit(solution)/shard_map/all_to_all | solution.py:652
  110.2 0.9 shard_map.145
  111.1 0.6 collective-permute-start.15
  111.7 2.3 %collective-permute-start.16 = (bf16[12,16,1024]{2,1,0:T(8,128)(2,1)S(1)}, bf16[12,16,1024]{2,1,0:T(8,128)(2,1)S(1)}, u32[]{:S(2)}, u32[]{:S(2)}) collective-permute-start(bf16[12,16,1024]{2,1,0:T(8,128)(2,1)S(1)} %copy-done.15), channel_id=1, source_target_pairs={{0,20},{4,16},{8,28},{12,24},{16,4},{20,0},{24,12},{28,8},{1,21},{... | collective-permute-start | bytes 1179656 | tf_op jit(solution)/shard_map/ppermute | solution.py:511
  114.0 3.6 %all-to-all-start.3 = ((bf16[8,40,128]{2,1,0:T(8,128)(2,1)}), bf16[8,40,128]{2,1,0:T(8,128)(2,1)S(1)}, u32[]{:S(2)}, u32[]{:S(2)}) async-start(bf16[8,40,128]{2,1,0:T(8,128)(2,1)} %shard_map.145), calls=%async_computation.3 | async-start | bytes 163840 | tf_op jit(solution)/shard_map/all_to_all | solution.py:657
  117.7 1.5 %shard_map.146.refs_2_ = bf16[128,16,1024]{2,1,0:T(8,128)(2,1)} custom-call(s32[2]{0:T(128)S(1)} %pad_add_fusion.3.place_ref, bf16[16,16,1024]{2,1,0:T(8,128)(2,1)S(1)} %collective-permute-done.13.refs_0_, bf16[16,16,1024]{2,1,0:T(8,128)(2,1)S(1)} %collective-permute-done.14.refs_1_, ...), custom_call_target="tpu_custom_call", output_to_operand_aliasing={{}: (3, {})} | custom-call | bytes 2097152 | tf_op jit(solution)/shard_map/pallas_call | solution.py:148
  119.3 13.0 %all-to-all-done.3.part_ref = bf16[8,40,128]{2,1,0:T(8,128)(2,1)S(1)} async-done(((bf16[8,40,128]{2,1,0:T(8,128)(2,1)}), bf16[8,40,128]{2,1,0:T(8,128)(2,1)S(1)}, u32[]{:S(2)}, u32[]{:S(2)}) %all-to-all-start.3) | async-done | bytes 81952 | tf_op jit(solution)/shard_map/all_to_all | solution.py:657
  132.3 0.9 shard_map.147
  133.2 0.8 collective-permute-start.20
  134.0 2.2 %collective-permute-start.21 = (bf16[4,16,1024]{2,1,0:T(8,128)(2,1)S(1)}, bf16[4,16,1024]{2,1,0:T(8,128)(2,1)S(1)}, u32[]{:S(2)}, u32[]{:S(2)}) collective-permute-start(bf16[4,16,1024]{2,1,0:T(8,128)(2,1)S(1)} %copy-done.16), channel_id=1, source_target_pairs={{0,20},{4,16},{8,28},{12,24},{16,4},{20,0},{24,12},{28,8},{1,21},{... | collective-permute-start | bytes 393224 | tf_op jit(solution)/shard_map/ppermute | solution.py:511
  136.2 0.7 collective-permute-start.18
  136.9 1.1 collective-permute-start.19
  138.1 1.4 shard_map.148.refs_2_
  139.6 0.8 collective-permute-done.18
  140.6 1.5 %collective-permute-done.21.refs_1_ = bf16[4,16,1024]{2,1,0:T(8,128)(2,1)S(1)} collective-permute-done((bf16[4,16,1024]{2,1,0:T(8,128)(2,1)S(1)}, bf16[4,16,1024]{2,1,0:T(8,128)(2,1)S(1)}, u32[]{:S(2)}, u32[]{:S(2)}) %collective-permute-start.21) | collective-permute-done | bytes 131104 | tf_op jit(solution)/shard_map/ppermute | solution.py:511
  142.1 0.6 add_convert_fusion
  142.7 1.3 shard_map.149
  (58 shorter events, 1.8 us)
Async XLA Ops:
  0.6 16.1 %copy-start.1 = (bf16[1024,512]{1,0:T(8,128)(2,1)S(1)}, bf16[1024,512]{1,0:T(8,128)(2,1)}, u32[]{:S(2)}) copy-start(bf16[1024,512]{1,0:T(8,128)(2,1)} %query_ref.1) | copy-start | bytes 3145732
  0.6 16.1 %copy-start.3 = (bf16[1024,128]{1,0:T(8,128)(2,1)S(1)}, bf16[1024,128]{1,0:T(8,128)(2,1)}, u32[]{:S(2)}) copy-start(bf16[1024,128]{1,0:T(8,128)(2,1)} %keyval_ref.1) | copy-start | bytes 786436
  0.7 51.9 %copy-start.9 = (s32[8]{0:T(128)S(1)}, s32[8]{0:T(128)}, u32[]{:S(2)}) copy-start(s32[8]{0:T(128)} %kept_ref.1) | copy-start | bytes 100
  2.1 14.6 %all-to-all-start = ((bf16[8,5,1024]{2,1,0:T(8,128)(2,1)}), bf16[8,5,1024]{2,1,0:T(8,128)(2,1)S(1)}, u32[]{:S(2)}, u32[]{:S(2)}) async-start(bf16[8,5,1024]{2,1,0:T(8,128)(2,1)} %broadcast_in_dim.2), calls=%async_computation | async-start | bytes 262144 | tf_op jit(solution)/shard_map/all_to_all | solution.py:484
  10.0 6.7 %copy-start.6 = (s32[2]{0:T(128)S(1)}, s32[2]{0:T(128)}, u32[]{:S(2)}) copy-start(s32[2]{0:T(128)} %pad_add_fusion.me_ref) | copy-start | bytes 28
  17.7 1.9 %collective-permute-start = (f32[40,256]{1,0:T(8,128)S(1)}, f32[40,256]{1,0:T(8,128)S(1)}, u32[]{:S(2)}, u32[]{:S(2)}) collective-permute-start(f32[40,256]{1,0:T(8,128)S(1)} %get-tuple-element.99), channel_id=1, source_target_pairs={{0,1},{1,0},{2,3},{3,2},{4,5},{5,4},{6,7},{7,6},{8,9},{9,8},{10,11... | collective-permute-start | bytes 122888 | tf_op jit(solution)/shard_map/ppermute | solution.py:511
  17.8 4.1 %collective-permute-start.1 = (f32[40,256]{1,0:T(8,128)S(1)}, f32[40,256]{1,0:T(8,128)S(1)}, u32[]{:S(2)}, u32[]{:S(2)}) collective-permute-start(f32[40,256]{1,0:T(8,128)S(1)} %get-tuple-element.100), channel_id=1, source_target_pairs={{0,2},{1,3},{2,0},{3,1},{4,6},{5,7},{6,4},{7,5},{8,10},{9,11},{10,... | collective-permute-start | bytes 122888 | tf_op jit(solution)/shard_map/ppermute | solution.py:511
  19.4 3.5 %collective-permute-start.2 = (f32[40,256]{1,0:T(8,128)S(1)}, f32[40,256]{1,0:T(8,128)S(1)}, u32[]{:S(2)}, u32[]{:S(2)}) collective-permute-start(f32[40,256]{1,0:T(8,128)S(1)} %get-tuple-element.101), channel_id=1, source_target_pairs={{0,3},{1,2},{2,1},{3,0},{4,7},{5,6},{6,5},{7,4},{8,11},{9,10},{10,... | collective-permute-start | bytes 122888 | tf_op jit(solution)/shard_map/ppermute | solution.py:511
  22.9 0.7 copy-start.8
  23.6 26.0 %collective-permute-start.3 = (bf16[16,16,1024]{2,1,0:T(8,128)(2,1)}, bf16[16,16,1024]{2,1,0:T(8,128)(2,1)S(1)}, u32[]{:S(2)}, u32[]{:S(2)}) collective-permute-start(bf16[16,16,1024]{2,1,0:T(8,128)(2,1)} %get-tuple-element.106), channel_id=1, source_target_pairs={{0,4},{4,0},{8,12},{12,8},{16,20},{20,16},{24,28},{28,24},{1,5},{5... | collective-permute-start | bytes 1572872 | tf_op jit(solution)/shard_map/ppermute | solution.py:511
  24.9 24.7 %collective-permute-start.4 = (bf16[12,16,1024]{2,1,0:T(8,128)(2,1)}, bf16[12,16,1024]{2,1,0:T(8,128)(2,1)S(1)}, u32[]{:S(2)}, u32[]{:S(2)}) collective-permute-start(bf16[12,16,1024]{2,1,0:T(8,128)(2,1)} %get-tuple-element.107), channel_id=1, source_target_pairs={{0,24},{4,28},{8,16},{12,20},{16,8},{20,12},{24,0},{28,4},{1,25},{... | collective-permute-start | bytes 1179656 | tf_op jit(solution)/shard_map/ppermute | solution.py:511
  49.6 30.3 %collective-permute-start.11 = (bf16[16,16,1024]{2,1,0:T(8,128)(2,1)}, bf16[16,16,1024]{2,1,0:T(8,128)(2,1)S(1)}, u32[]{:S(2)}, u32[]{:S(2)}) collective-permute-start(bf16[16,16,1024]{2,1,0:T(8,128)(2,1)} %get-tuple-element.126), channel_id=1, source_target_pairs={{0,28},{4,24},{8,20},{12,16},{16,12},{20,8},{24,4},{28,0},{1,29},{... | collective-permute-start | bytes 1572872 | tf_op jit(solution)/shard_map/ppermute | solution.py:511
  54.0 4.9 %copy-start = (bf16[128,1024]{1,0:T(8,128)(2,1)}, bf16[128,1024]{1,0:T(8,128)(2,1)S(1)}, u32[]{:S(2)}) copy-start(bf16[128,1024]{1,0:T(8,128)(2,1)S(1)} %get-tuple-element.120.refs_6_.refs_7_) | copy-start | bytes 786436
  54.0 4.9 %copy-start.5 = (bf16[8,40,128]{2,1,0:T(8,128)(2,1)}, bf16[8,40,128]{2,1,0:T(8,128)(2,1)S(1)}, u32[]{:S(2)}) copy-start(bf16[8,40,128]{2,1,0:T(8,128)(2,1)S(1)} %get-tuple-element.116.refs_0_) | copy-start | bytes 245764
  54.0 4.9 %collective-permute-start.5 = (bf16[8,40,128]{2,1,0:T(8,128)(2,1)S(1)}, bf16[8,40,128]{2,1,0:T(8,128)(2,1)S(1)}, u32[]{:S(2)}, u32[]{:S(2)}) collective-permute-start(bf16[8,40,128]{2,1,0:T(8,128)(2,1)S(1)} %get-tuple-element.116.refs_0_), channel_id=1, source_target_pairs={{0,1},{1,0},{2,3},{3,2},{4,5},{5,4},{6,7},{7,6},{8,9},{9,8},{10,11... | collective-permute-start | bytes 245768 | tf_op jit(solution)/shard_map/ppermute | solution.py:511
  54.0 5.3 %collective-permute-start.6 = (bf16[8,40,128]{2,1,0:T(8,128)(2,1)S(1)}, bf16[8,40,128]{2,1,0:T(8,128)(2,1)S(1)}, u32[]{:S(2)}, u32[]{:S(2)}) collective-permute-start(bf16[8,40,128]{2,1,0:T(8,128)(2,1)S(1)} %get-tuple-element.116.refs_0_), channel_id=1, source_target_pairs={{0,2},{1,3},{2,0},{3,1},{4,6},{5,7},{6,4},{7,5},{8,10},{9,11},{10,... | collective-permute-start | bytes 245768 | tf_op jit(solution)/shard_map/ppermute | solution.py:511
  55.0 5.1 %collective-permute-start.7 = (bf16[8,40,128]{2,1,0:T(8,128)(2,1)S(1)}, bf16[8,40,128]{2,1,0:T(8,128)(2,1)S(1)}, u32[]{:S(2)}, u32[]{:S(2)}) collective-permute-start(bf16[8,40,128]{2,1,0:T(8,128)(2,1)S(1)} %get-tuple-element.116.refs_0_), channel_id=1, source_target_pairs={{0,3},{1,2},{2,1},{3,0},{4,7},{5,6},{6,5},{7,4},{8,11},{9,10},{10,... | collective-permute-start | bytes 245768 | tf_op jit(solution)/shard_map/ppermute | solution.py:511
  55.9 17.4 %collective-permute-start.12 = (bf16[4,16,1024]{2,1,0:T(8,128)(2,1)}, bf16[4,16,1024]{2,1,0:T(8,128)(2,1)S(1)}, u32[]{:S(2)}, u32[]{:S(2)}) collective-permute-start(bf16[4,16,1024]{2,1,0:T(8,128)(2,1)} %get-tuple-element.127), channel_id=1, source_target_pairs={{0,24},{4,28},{8,16},{12,20},{16,8},{20,12},{24,0},{28,4},{1,25},{... | collective-permute-start | bytes 393224 | tf_op jit(solution)/shard_map/ppermute | solution.py:511
  58.9 1.2 copy-start.10
  59.3 0.8 copy-start.11
  60.1 0.6 copy-start.12
  60.7 21.2 %copy-start.14 = (bf16[16,16,1024]{2,1,0:T(8,128)(2,1)S(1)}, bf16[16,16,1024]{2,1,0:T(8,128)(2,1)}, u32[]{:S(2)}) copy-start(bf16[16,16,1024]{2,1,0:T(8,128)(2,1)} %get-tuple-element.137) | copy-start | bytes 1572868
  60.7 21.5 %copy-start.13 = (bf16[16,16,1024]{2,1,0:T(8,128)(2,1)S(1)}, bf16[16,16,1024]{2,1,0:T(8,128)(2,1)}, u32[]{:S(2)}) copy-start(bf16[16,16,1024]{2,1,0:T(8,128)(2,1)} %get-tuple-element.138) | copy-start | bytes 1572868
  71.0 5.4 %collective-permute-start.10 = (bf16[8,64,128]{2,1,0:T(8,128)(2,1)}, bf16[8,64,128]{2,1,0:T(8,128)(2,1)S(1)}, u32[]{:S(2)}, u32[]{:S(2)}) collective-permute-start(bf16[8,64,128]{2,1,0:T(8,128)(2,1)} %get-tuple-element.125), channel_id=1, source_target_pairs={{0,3},{1,2},{2,1},{3,0},{4,7},{5,6},{6,5},{7,4},{8,11},{9,10},{10,... | collective-permute-start | bytes 393224 | tf_op jit(solution)/shard_map/ppermute | solution.py:511
  72.2 4.2 %collective-permute-start.8 = (bf16[8,64,128]{2,1,0:T(8,128)(2,1)}, bf16[8,64,128]{2,1,0:T(8,128)(2,1)S(1)}, u32[]{:S(2)}, u32[]{:S(2)}) collective-permute-start(bf16[8,64,128]{2,1,0:T(8,128)(2,1)} %get-tuple-element.123), channel_id=1, source_target_pairs={{0,1},{1,0},{2,3},{3,2},{4,5},{5,4},{6,7},{7,6},{8,9},{9,8},{10,11... | collective-permute-start | bytes 393224 | tf_op jit(solution)/shard_map/ppermute | solution.py:511
  72.2 7.7 %collective-permute-start.9 = (bf16[8,64,128]{2,1,0:T(8,128)(2,1)}, bf16[8,64,128]{2,1,0:T(8,128)(2,1)S(1)}, u32[]{:S(2)}, u32[]{:S(2)}) collective-permute-start(bf16[8,64,128]{2,1,0:T(8,128)(2,1)} %get-tuple-element.124), channel_id=1, source_target_pairs={{0,2},{1,3},{2,0},{3,1},{4,6},{5,7},{6,4},{7,5},{8,10},{9,11},{10,... | collective-permute-start | bytes 393224 | tf_op jit(solution)/shard_map/ppermute | solution.py:511
  79.9 0.9 copy-start.4
  81.9 28.3 %collective-permute-start.13 = (bf16[16,16,1024]{2,1,0:T(8,128)(2,1)S(1)}, bf16[16,16,1024]{2,1,0:T(8,128)(2,1)S(1)}, u32[]{:S(2)}, u32[]{:S(2)}) collective-permute-start(bf16[16,16,1024]{2,1,0:T(8,128)(2,1)S(1)} %copy-done.14), channel_id=1, source_target_pairs={{0,12},{4,8},{8,4},{12,0},{16,28},{20,24},{24,20},{28,16},{1,13},{... | collective-permute-start | bytes 1572872 | tf_op jit(solution)/shard_map/ppermute | solution.py:511
  82.2 28.0 %collective-permute-start.14 = (bf16[16,16,1024]{2,1,0:T(8,128)(2,1)S(1)}, bf16[16,16,1024]{2,1,0:T(8,128)(2,1)S(1)}, u32[]{:S(2)}, u32[]{:S(2)}) collective-permute-start(bf16[16,16,1024]{2,1,0:T(8,128)(2,1)S(1)} %copy-done.13), channel_id=1, source_target_pairs={{0,16},{4,20},{8,24},{12,28},{16,0},{20,4},{24,8},{28,12},{1,17},{... | collective-permute-start | bytes 1572872 | tf_op jit(solution)/shard_map/ppermute | solution.py:511
  84.2 26.0 %all-to-all-start.2 = ((bf16[8,64,128]{2,1,0:T(8,128)(2,1)}), bf16[8,64,128]{2,1,0:T(8,128)(2,1)S(1)}, u32[]{:S(2)}, u32[]{:S(2)}) async-start(bf16[8,64,128]{2,1,0:T(8,128)(2,1)} %shard_map.143), calls=%async_computation.2 | async-start | bytes 262144 | tf_op jit(solution)/shard_map/all_to_all | solution.py:652
  88.6 23.2 %copy-start.15 = (bf16[12,16,1024]{2,1,0:T(8,128)(2,1)S(1)}, bf16[12,16,1024]{2,1,0:T(8,128)(2,1)}, u32[]{:S(2)}) copy-start(bf16[12,16,1024]{2,1,0:T(8,128)(2,1)} %get-tuple-element.150) | copy-start | bytes 1179652
  111.1 21.2 %collective-permute-start.15 = (bf16[12,16,1024]{2,1,0:T(8,128)(2,1)}, bf16[12,16,1024]{2,1,0:T(8,128)(2,1)S(1)}, u32[]{:S(2)}, u32[]{:S(2)}) collective-permute-start(bf16[12,16,1024]{2,1,0:T(8,128)(2,1)} %get-tuple-element.149), channel_id=1, source_target_pairs={{0,8},{4,12},{8,0},{12,4},{16,24},{20,28},{24,16},{28,20},{1,9},{5... | collective-permute-start | bytes 1179656 | tf_op jit(solution)/shard_map/ppermute | solution.py:511
  111.7 20.5 %collective-permute-start.16 = (bf16[12,16,1024]{2,1,0:T(8,128)(2,1)S(1)}, bf16[12,16,1024]{2,1,0:T(8,128)(2,1)S(1)}, u32[]{:S(2)}, u32[]{:S(2)}) collective-permute-start(bf16[12,16,1024]{2,1,0:T(8,128)(2,1)S(1)} %copy-done.15), channel_id=1, source_target_pairs={{0,20},{4,16},{8,28},{12,24},{16,4},{20,0},{24,12},{28,8},{1,21},{... | collective-permute-start | bytes 1179656 | tf_op jit(solution)/shard_map/ppermute | solution.py:511
  114.0 18.2 %all-to-all-start.3 = ((bf16[8,40,128]{2,1,0:T(8,128)(2,1)}), bf16[8,40,128]{2,1,0:T(8,128)(2,1)S(1)}, u32[]{:S(2)}, u32[]{:S(2)}) async-start(bf16[8,40,128]{2,1,0:T(8,128)(2,1)} %shard_map.145), calls=%async_computation.3 | async-start | bytes 163840 | tf_op jit(solution)/shard_map/all_to_all | solution.py:657
  117.7 14.5 %copy-start.2 = (bf16[1024,512]{1,0:T(8,128)(2,1)S(1)}, bf16[1024,512]{1,0:T(8,128)(2,1)}, u32[]{:S(2)}) copy-start(bf16[1024,512]{1,0:T(8,128)(2,1)} %weight_ref.1) | copy-start | bytes 3145732
  117.7 14.5 %copy-start.7 = (s32[2]{0:T(128)S(1)}, s32[2]{0:T(128)}, u32[]{:S(2)}) copy-start(s32[2]{0:T(128)} %pad_add_fusion.me_ref) | copy-start | bytes 28
  117.7 16.2 %copy-start.16 = (bf16[4,16,1024]{2,1,0:T(8,128)(2,1)S(1)}, bf16[4,16,1024]{2,1,0:T(8,128)(2,1)}, u32[]{:S(2)}) copy-start(bf16[4,16,1024]{2,1,0:T(8,128)(2,1)} %get-tuple-element.172) | copy-start | bytes 393220
  133.2 7.4 %collective-permute-start.20 = (bf16[4,16,1024]{2,1,0:T(8,128)(2,1)}, bf16[4,16,1024]{2,1,0:T(8,128)(2,1)S(1)}, u32[]{:S(2)}, u32[]{:S(2)}) collective-permute-start(bf16[4,16,1024]{2,1,0:T(8,128)(2,1)} %get-tuple-element.171), channel_id=1, source_target_pairs={{0,8},{4,12},{8,0},{12,4},{16,24},{20,28},{24,16},{28,20},{1,9},{5... | collective-permute-start | bytes 393224 | tf_op jit(solution)/shard_map/ppermute | solution.py:511
  134.0 8.2 %collective-permute-start.21 = (bf16[4,16,1024]{2,1,0:T(8,128)(2,1)S(1)}, bf16[4,16,1024]{2,1,0:T(8,128)(2,1)S(1)}, u32[]{:S(2)}, u32[]{:S(2)}) collective-permute-start(bf16[4,16,1024]{2,1,0:T(8,128)(2,1)S(1)} %copy-done.16), channel_id=1, source_target_pairs={{0,20},{4,16},{8,28},{12,24},{16,4},{20,0},{24,12},{28,8},{1,21},{... | collective-permute-start | bytes 393224 | tf_op jit(solution)/shard_map/ppermute | solution.py:511
  136.2 3.4 %collective-permute-start.17 = (f32[10,512]{1,0:T(8,128)S(1)}, f32[10,512]{1,0:T(8,128)S(1)}, u32[]{:S(2)}, u32[]{:S(2)}) collective-permute-start(f32[10,512]{1,0:T(8,128)S(1)} %get-tuple-element.168), channel_id=1, source_target_pairs={{0,1},{1,0},{2,3},{3,2},{4,5},{5,4},{6,7},{7,6},{8,9},{9,8},{10,11... | collective-permute-start | bytes 61448 | tf_op jit(solution)/shard_map/ppermute | solution.py:511
  136.2 4.2 %collective-permute-start.18 = (f32[10,512]{1,0:T(8,128)S(1)}, f32[10,512]{1,0:T(8,128)S(1)}, u32[]{:S(2)}, u32[]{:S(2)}) collective-permute-start(f32[10,512]{1,0:T(8,128)S(1)} %get-tuple-element.169), channel_id=1, source_target_pairs={{0,2},{1,3},{2,0},{3,1},{4,6},{5,7},{6,4},{7,5},{8,10},{9,11},{10,... | collective-permute-start | bytes 61448 | tf_op jit(solution)/shard_map/ppermute | solution.py:511
  136.9 3.7 %collective-permute-start.19 = (f32[10,512]{1,0:T(8,128)S(1)}, f32[10,512]{1,0:T(8,128)S(1)}, u32[]{:S(2)}, u32[]{:S(2)}) collective-permute-start(f32[10,512]{1,0:T(8,128)S(1)} %get-tuple-element.170), channel_id=1, source_target_pairs={{0,3},{1,2},{2,1},{3,0},{4,7},{5,6},{6,5},{7,4},{8,11},{9,10},{10,... | collective-permute-start | bytes 61448 | tf_op jit(solution)/shard_map/ppermute | solution.py:511

commit v16 on v15

--- a/solution.py
+++ b/solution.py
@@ -18,7 +18,7 @@
 SCALE2 = math.log2(math.e) / math.sqrt(HD)
 STAT = 16
 MIB = 1024 * 1024
-CUTS = {1: (0, 16), 2: (0, 12, 16), 3: (0, 16), 4: (0, 16), 5: (0, 12, 16), 6: (0, 12, 16), 7: (0, 16)}
+CUTS = {1: (0, 16), 2: (0, 16), 3: (0, 12, 16), 4: (0, 4, 16), 5: (0, 12, 16), 6: (0, 4, 16), 7: (0, 16)}
 NT = (((1,), (1,)), ((), ()))
 
 
@@ -383,8 +383,9 @@
     return match.astype(jnp.bfloat16)
 
 
-def project_kernel(peers, me_ref, hidden_ref, query_ref, keyval_ref, *refs):
-    out_refs, (full_ref,) = refs[:peers], refs[peers:]
+def project_kernel(peers, me_ref, hidden_ref, query_ref, keyval_ref, tag_ref, *refs):
+    out_refs, (kept_ref, full_ref) = refs[:peers], refs[peers:]
+    kept_ref[...] = tag_ref[...]
     count, local, depth = hidden_ref.shape
     unit = up(local, 8)
     blocks = []
@@ -569,16 +570,17 @@
     tokens = pool.reshape(slots * PAGE, -1)
     if direct:
         block = jax.ShapeDtypeStruct((rows, 2 * HD), jnp.float32)
-        partial = in_vmem(
+        *partial, tags = in_vmem(
             functools.partial(project_kernel, narrow),
-            [block] * narrow,
+            [block] * narrow + [jax.ShapeDtypeStruct(tags.shape, tags.dtype)],
             both,
             gathered,
             w_query,
             w_keyval,
+            tags,
             scratch=[pltpu.VMEM((rows, narrow * HD), jnp.float32)],
         )
-        partial = deal(partial, "narrow")
+        partial = beside(lambda value: deal(value, "narrow"), partial, (6, 0))
         packed = in_vmem(
             functools.partial(pack_kernel, narrow),
             jax.ShapeDtypeStruct((wide, rows + wide, 2 * HD), jnp.bfloat16),
@@ -586,8 +588,8 @@
             *partial,
             tags,
         )
-        received = beside(lambda value: exchange(value, "wide"), packed, (1, 0), (6, 0))
-        received = launch(received, (7, 0), (6, 1))
+        received = beside(lambda value: exchange(value, "wide"), packed, (1, 0), (6, 1))
+        received = launch(received, (7, 0), (4, 0))
         queries, keyval, new_entries, moved_req, moved_idx = in_vmem(
             functools.partial(unpack_kernel, rows),
             [
@@ -610,14 +612,14 @@
         partial = jnp.concatenate(
             [query_part, jnp.broadcast_to(keyval_part[None], (narrow,) + keyval_part.shape)], axis=2
         )
-        partial = exchange(partial, "narrow")
+        partial = beside(lambda value: exchange(value, "narrow"), partial, (6, 0))
         projected = jnp.sum(partial, axis=0).astype(jnp.bfloat16)
         tags = tags[:, : 3 * capacity].astype(jnp.bfloat16)[:, None]
         tags = jnp.pad(tags, ((0, 0), (0, 7), (0, projected.shape[1] - tags.shape[2])))
         packed = jnp.broadcast_to(projected[None], (wide,) + projected.shape)
         packed = jnp.concatenate([packed, tags], axis=1)
-        received = beside(lambda value: exchange(value, "wide"), packed, (1, 0), (6, 0))
-        received = launch(received, (7, 0), (6, 1))
+        received = beside(lambda value: exchange(value, "wide"), packed, (1, 0), (6, 1))
+        received = launch(received, (7, 0), (4, 0))
         tags_in = received[:, rows]
         queries = received[:, :rows, :own_cols]
         queries = spread(queries, "narrow")
@@ -641,15 +643,15 @@
     queries, moved_pool = lax.optimization_barrier((queries, placed(moved_pool)))
     mixed = attend(both, lengths, queries, keyval, tokens, token_info, rows, piece)
     if direct:
-        mixed = land(deal(mixed, "narrow"), (7, 0), (6, 1))
+        mixed = land(deal(mixed, "narrow"), (7, 0), (4, 0))
     else:
-        mixed = land(exchange(mixed[0], "narrow"), (7, 0), (6, 1))
+        mixed = land(exchange(mixed[0], "narrow"), (7, 0), (4, 0))
         mixed = mixed.reshape((narrow, wide) + mixed.shape[1:])
         mixed = [mixed[i] for i in range(narrow)]
     mixed = combine(mixed, piece)
     mixed, pages = lax.optimization_barrier((mixed, moved_pool))
     pages = placed(pages)
-    mixed = beside(lambda value: exchange(value, "wide"), mixed, (3, 0), (4, 0))
+    mixed = beside(lambda value: exchange(value, "wide"), mixed, (3, 0), (4, 1))
     mixed, moved_pool = lax.optimization_barrier((mixed, pages))
     attn = combine([mixed], piece, wide)
     attn, pages = lax.optimization_barrier((attn, moved_pool))
@@ -666,14 +668,14 @@
         )
         sums, pages = lax.optimization_barrier((sums, moved_pool))
         pages = placed(pages)
-        sums = beside(lambda value: deal(value, "narrow"), sums, (2, 1), (5, 1))
+        sums = beside(lambda value: deal(value, "narrow"), sums, (3, 1), (5, 1))
         attended = ((sums[0] + sums[1]) + (sums[2] + sums[3])).astype(jnp.bfloat16)
     else:
         attn = jnp.transpose(attn.reshape(-1, rows, HD), (1, 0, 2)).reshape(rows, -1)
         sums = jnp.dot(attn, w_out, preferred_element_type=jnp.float32)
         sums = sums.reshape(narrow, rows // narrow, -1)
         pages = placed(moved_pool)
-        sums = beside(lambda value: exchange(value, "narrow"), sums, (2, 1), (5, 1))
+        sums = beside(lambda value: exchange(value, "narrow"), sums, (3, 1), (5, 1))
         attended = jnp.sum(sums, axis=0).astype(jnp.bfloat16)
     attended, pages = lax.optimization_barrier((attended, pages))
     moved_pool = placed(pages)

time: 145 us -> 144 us (level)
    all_to_all x1, waiting for transfers between devices: 20.2 us -> 15.6 us  [on_device(): mixed = beside(lambda value: exchange(value, 'wide'), mixed, (3, 0), (4, 1))]
    all_to_all x1, waiting for transfers between devices: 13 us -> 15.1 us  [on_device(): attn = beside(lambda value: exchange(value, 'wide'), attn, (2, 0), (5, 0))]
    ppermute x22 -> x23, starting transfers between devices: 25.1 us -> 26.5 us  [send(): lax.ppermute(block, axis, [(i, i ^ d) for i in range(lax.axis_size(axis))])]
    ppermute x22 -> x23, waiting for transfers between devices: 13.6 us -> 14.8 us  [send(): lax.ppermute(block, axis, [(i, i ^ d) for i in range(lax.axis_size(axis))])]
  transfers between devices with their start and end apart: 25 -> 26, of which waited for: 12 -> 12; matrix products, arithmetic and copies ran while one was open for 1% -> 1% of each run, Pallas kernels for 16% -> 16%
where the time goes in v16:
time: 144 us; the launch traced here: 143 us
  waiting for transfers between devices  46.4 us (32%)
  starting transfers between devices  40.5 us (28%)
  Pallas kernels  28.7 us (20%)
  blocking collectives  21.1 us (15%)
  local copies, waits for them, and re-layouts  3.73 us (3%)
  other arithmetic  1.57 us (1%)
    ppermute x23, starting transfers between devices, send(): lax.ppermute(block, axis, [(i, i ^ d) for i in range(lax.axis_size(axis))])  26.5 us
    all_to_all x1, blocking collectives, on_device(): exchange(value, 'wide')  21.1 us
    all_to_all x1, waiting for transfers between devices, on_device(): mixed = beside(lambda value: exchange(value, 'wide'), mixed, (3, 0), (4, 1))  15.6 us
    all_to_all x1, waiting for transfers between devices, on_device(): attn = beside(lambda value: exchange(value, 'wide'), attn, (2, 0), (5, 0))  15.1 us
    ppermute x23, waiting for transfers between devices, send(): lax.ppermute(block, axis, [(i, i ^ d) for i in range(lax.axis_size(axis))])  14.8 us
    pallas_call x1, Pallas kernels, attend(): pl.pallas_call(functools.partial(attend_kernel, rows, piece, peers), grid...  10.3 us
    all_to_all x1, starting transfers between devices, spread(): lax.all_to_all(jnp.broadcast_to(block[None], (count,) + block.shape), axi...  7.28 us
    pallas_call x5, Pallas kernels, place_pages(): pl.pallas_call(place_kernel, out_shape=jax.ShapeDtypeStruct(pages.shape,...  7.09 us
  transfers between devices with their start and end apart: 26, of which 12 were waited for; matrix products, arithmetic and copies ran while one was open for 1% of the time, Pallas kernels for 16%

profile of v16, /device:TPU:0, one launch (start us, length us, event | category | flops | bytes accessed | tf_op | source)
XLA Modules:
  0.0 142.8 jit_solution(15714761190981870113)
XLA Ops:
  0.7 1.5 %broadcast_in_dim.2 = bf16[8,5,1024]{2,1,0:T(8,128)(2,1)} broadcast(bf16[5,1024]{1,0:T(8,128)(2,1)} %param.10), dimensions={1,2} | broadcast | bytes 92160 | tf_op jit(solution)/shard_map/broadcast_in_dim | solution.py:486
  2.1 7.3 %all-to-all-start = ((bf16[8,5,1024]{2,1,0:T(8,128)(2,1)}), bf16[8,5,1024]{2,1,0:T(8,128)(2,1)S(1)}, u32[]{:S(2)}, u32[]{:S(2)}) async-start(bf16[8,5,1024]{2,1,0:T(8,128)(2,1)} %broadcast_in_dim.2), calls=%async_computation | async-start | bytes 262144 | tf_op jit(solution)/shard_map/all_to_all | solution.py:485
  9.4 0.6 pad_add_fusion.me_ref
  10.0 6.0 %shard_map.137 = (bf16[128,16,1024]{2,1,0:T(8,128)(2,1)}, f32[8,128]{1,0:T(8,128)}, f32[8,2048]{1,0:T(8,128)}, bf16[16,16,1024]{2,1,0:T(8,128)(2,1)}, bf16[16,16...) custom-call(s32[2]{0:T(128)} %pad_add_fusion.me_ref, ...), custom_call_target="tpu_custom_call" | custom-call | bytes 8388608 | tf_op jit(solution)/shard_map/pallas_call | solution.py:110
  16.0 0.8 all-to-all-done.hidden_ref
  16.8 0.7 copy-done.8
  17.5 1.0 shard_map.138
  18.4 3.1 %collective-permute-start.3 = (bf16[4,16,1024]{2,1,0:T(8,128)(2,1)}, bf16[4,16,1024]{2,1,0:T(8,128)(2,1)S(1)}, u32[]{:S(2)}, u32[]{:S(2)}) collective-permute-start(bf16[4,16,1024]{2,1,0:T(8,128)(2,1)} %get-tuple-element.120), channel_id=1, source_target_pairs={{0,24},{4,28},{8,16},{12,20},{16,8},{20,12},{24,0},{28,4},{1,25},{... | collective-permute-start | bytes 393224 | tf_op jit(solution)/shard_map/ppermute | solution.py:512
  21.6 1.5 %collective-permute-start.1 = (f32[40,256]{1,0:T(8,128)S(1)}, f32[40,256]{1,0:T(8,128)S(1)}, u32[]{:S(2)}, u32[]{:S(2)}) collective-permute-start(f32[40,256]{1,0:T(8,128)S(1)} %get-tuple-element.118), channel_id=1, source_target_pairs={{0,2},{1,3},{2,0},{3,1},{4,6},{5,7},{6,4},{7,5},{8,10},{9,11},{10,... | collective-permute-start | bytes 122888 | tf_op jit(solution)/shard_map/ppermute | solution.py:512
  23.4 2.1 %collective-permute-done.1.refs_2_ = f32[40,256]{1,0:T(8,128)S(1)} collective-permute-done((f32[40,256]{1,0:T(8,128)S(1)}, f32[40,256]{1,0:T(8,128)S(1)}, u32[]{:S(2)}, u32[]{:S(2)}) %collective-permute-start.1) | collective-permute-done | bytes 40992 | tf_op jit(solution)/shard_map/ppermute | solution.py:512
  25.6 1.0 collective-permute-done.2.refs_3_
  26.7 1.5 %collective-permute-start.4 = (bf16[16,16,1024]{2,1,0:T(8,128)(2,1)}, bf16[16,16,1024]{2,1,0:T(8,128)(2,1)S(1)}, u32[]{:S(2)}, u32[]{:S(2)}) collective-permute-start(bf16[16,16,1024]{2,1,0:T(8,128)(2,1)} %get-tuple-element.129), channel_id=1, source_target_pairs={{0,4},{4,0},{8,12},{12,8},{16,20},{20,16},{24,28},{28,24},{1,5},{5... | collective-permute-start | bytes 1572872 | tf_op jit(solution)/shard_map/ppermute | solution.py:512
  28.2 2.0 %collective-permute-start.5 = (bf16[12,16,1024]{2,1,0:T(8,128)(2,1)}, bf16[12,16,1024]{2,1,0:T(8,128)(2,1)S(1)}, u32[]{:S(2)}, u32[]{:S(2)}) collective-permute-start(bf16[12,16,1024]{2,1,0:T(8,128)(2,1)} %get-tuple-element.130), channel_id=1, source_target_pairs={{0,24},{4,28},{8,16},{12,20},{16,8},{20,12},{24,0},{28,4},{1,25},{... | collective-permute-start | bytes 1179656 | tf_op jit(solution)/shard_map/ppermute | solution.py:512
  30.2 21.1 %all_to_all.20.part_ref = bf16[8,48,256]{2,1,0:T(8,128)(2,1)S(1)} all-to-all(bf16[8,48,256]{2,1,0:T(8,128)(2,1)S(1)} %shard_map.139), channel_id=1, replica_groups=mesh['wide'=8,'narrow'=4] {'wide'}, dimensions={0} | all-to-all | bytes 393216 | tf_op jit(solution)/shard_map/all_to_all | solution.py:591
  51.3 2.1 %collective-permute-start.12 = (bf16[16,16,1024]{2,1,0:T(8,128)(2,1)}, bf16[16,16,1024]{2,1,0:T(8,128)(2,1)S(1)}, u32[]{:S(2)}, u32[]{:S(2)}) collective-permute-start(bf16[16,16,1024]{2,1,0:T(8,128)(2,1)} %get-tuple-element.150), channel_id=1, source_target_pairs={{0,28},{4,24},{8,20},{12,16},{16,12},{20,8},{24,4},{28,0},{1,29},{... | collective-permute-start | bytes 1572872 | tf_op jit(solution)/shard_map/ppermute | solution.py:512
  53.4 1.4 shard_map.140
  54.8 1.1 collective-permute-start.7
  55.9 0.8 collective-permute-start.8
  56.8 1.5 %shard_map.141.refs_2_ = bf16[128,16,1024]{2,1,0:T(8,128)(2,1)} custom-call(s32[3]{0:T(128)S(1)} %pad_add_fusion.1.place_ref, bf16[16,16,1024]{2,1,0:T(8,128)(2,1)S(1)} %collective-permute-done.4.refs_0_, bf16[4,16,1024]{2,1,0:T(8,128)(2,1)S(1)} %collective-permute-done.3.refs_1_, ...), custom_call_target="tpu_custom_call", output_to_operand_aliasing={{}: (4, {})} | custom-call | bytes 3145728 | tf_op jit(solution)/shard_map/pallas_call | solution.py:148
  58.3 1.8 %collective-permute-done.7.refs_2_ = bf16[8,40,128]{2,1,0:T(8,128)(2,1)S(1)} collective-permute-done((bf16[8,40,128]{2,1,0:T(8,128)(2,1)S(1)}, bf16[8,40,128]{2,1,0:T(8,128)(2,1)S(1)}, u32[]{:S(2)}, u32[]{:S(2)}) %collective-permute-start.7) | collective-permute-done | bytes 81952 | tf_op jit(solution)/shard_map/ppermute | solution.py:512
  60.1 0.8 collective-permute-done.8.refs_3_
  60.9 0.6 copy-done.12
  61.6 10.3 %shard_map.142 = (bf16[8,64,128]{2,1,0:T(8,128)(2,1)}, bf16[8,64,128]{2,1,0:T(8,128)(2,1)}, bf16[8,64,128]{2,1,0:T(8,128)(2,1)}, bf16[8,64,128]{2,1,0:T(8,128)(2,1)}) custom-call(s32[2]{0:T(128)} %pad_add_fusion.me_ref, s32[8]{0:T(128)} %length_ref.1, bf16[8,40,128]{2,1,0:T(8,128)(2,1)} %copy-done.5, bf16[8,40,128]{2,1,0:T(8,128)(2,1)} %copy-done.10, ...), custom_call_target="tpu_custom_call" | custom-call | flops 1 | bytes 1 | tf_op jit(solution)/shard_map/pallas_call | solution.py:292
  71.9 1.1 collective-permute-start.10
  72.9 0.9 collective-permute-start.11
  74.0 5.4 %collective-permute-done.13.refs_0_ = bf16[4,16,1024]{2,1,0:T(8,128)(2,1)S(1)} collective-permute-done((bf16[4,16,1024]{2,1,0:T(8,128)(2,1)}, bf16[4,16,1024]{2,1,0:T(8,128)(2,1)S(1)}, u32[]{:S(2)}, u32[]{:S(2)}) %collective-permute-start.13) | collective-permute-done | bytes 131104 | tf_op jit(solution)/shard_map/ppermute | solution.py:512
  79.4 1.2 collective-permute-done.11.refs_3_
  80.6 0.9 copy-done.4
  81.5 1.1 shard_map.143
  82.6 3.2 %collective-permute-start.15 = (bf16[12,16,1024]{2,1,0:T(8,128)(2,1)S(1)}, bf16[12,16,1024]{2,1,0:T(8,128)(2,1)S(1)}, u32[]{:S(2)}, u32[]{:S(2)}) collective-permute-start(bf16[12,16,1024]{2,1,0:T(8,128)(2,1)S(1)} %copy-done.14), channel_id=1, source_target_pairs={{0,16},{4,20},{8,24},{12,28},{16,0},{20,4},{24,8},{28,12},{1,17},{... | collective-permute-start | bytes 1179656 | tf_op jit(solution)/shard_map/ppermute | solution.py:512
  85.8 3.4 %all-to-all-start.2 = ((bf16[8,64,128]{2,1,0:T(8,128)(2,1)}), bf16[8,64,128]{2,1,0:T(8,128)(2,1)S(1)}, u32[]{:S(2)}, u32[]{:S(2)}) async-start(bf16[8,64,128]{2,1,0:T(8,128)(2,1)} %shard_map.143), calls=%async_computation.2 | async-start | bytes 262144 | tf_op jit(solution)/shard_map/all_to_all | solution.py:654
  89.3 1.4 shard_map.144.refs_2_
  90.7 15.6 %all-to-all-done.2.refs_0_ = bf16[8,64,128]{2,1,0:T(8,128)(2,1)S(1)} async-done(((bf16[8,64,128]{2,1,0:T(8,128)(2,1)}), bf16[8,64,128]{2,1,0:T(8,128)(2,1)S(1)}, u32[]{:S(2)}, u32[]{:S(2)}) %all-to-all-start.2) | async-done | bytes 131104 | tf_op jit(solution)/shard_map/all_to_all | solution.py:654
  106.3 0.9 shard_map.145
  107.3 0.9 collective-permute-start.16
  108.2 2.4 %collective-permute-start.17 = (bf16[12,16,1024]{2,1,0:T(8,128)(2,1)}, bf16[12,16,1024]{2,1,0:T(8,128)(2,1)S(1)}, u32[]{:S(2)}, u32[]{:S(2)}) collective-permute-start(bf16[12,16,1024]{2,1,0:T(8,128)(2,1)} %get-tuple-element.174), channel_id=1, source_target_pairs={{0,20},{4,16},{8,28},{12,24},{16,4},{20,0},{24,12},{28,8},{1,21},{... | collective-permute-start | bytes 1179656 | tf_op jit(solution)/shard_map/ppermute | solution.py:512
  110.6 3.4 %all-to-all-start.3 = ((bf16[8,40,128]{2,1,0:T(8,128)(2,1)}), bf16[8,40,128]{2,1,0:T(8,128)(2,1)S(1)}, u32[]{:S(2)}, u32[]{:S(2)}) async-start(bf16[8,40,128]{2,1,0:T(8,128)(2,1)} %shard_map.145), calls=%async_computation.3 | async-start | bytes 163840 | tf_op jit(solution)/shard_map/all_to_all | solution.py:659
  114.1 1.4 %shard_map.146.refs_2_ = bf16[128,16,1024]{2,1,0:T(8,128)(2,1)} custom-call(s32[2]{0:T(128)S(1)} %pad_add_fusion.3.place_ref, bf16[12,16,1024]{2,1,0:T(8,128)(2,1)S(1)} %collective-permute-done.14.refs_0_, bf16[12,16,1024]{2,1,0:T(8,128)(2,1)S(1)} %collective-permute-done.15.refs_1_, ...), custom_call_target="tpu_custom_call", output_to_operand_aliasing={{}: (3, {})} | custom-call | bytes 1572864 | tf_op jit(solution)/shard_map/pallas_call | solution.py:148
  115.5 15.1 %all-to-all-done.3.part_ref = bf16[8,40,128]{2,1,0:T(8,128)(2,1)S(1)} async-done(((bf16[8,40,128]{2,1,0:T(8,128)(2,1)}), bf16[8,40,128]{2,1,0:T(8,128)(2,1)S(1)}, u32[]{:S(2)}, u32[]{:S(2)}) %all-to-all-start.3) | async-done | bytes 81952 | tf_op jit(solution)/shard_map/all_to_all | solution.py:659
  130.7 0.9 shard_map.147
  131.6 1.2 collective-permute-start.21
  132.8 2.2 %collective-permute-start.22 = (bf16[4,16,1024]{2,1,0:T(8,128)(2,1)S(1)}, bf16[4,16,1024]{2,1,0:T(8,128)(2,1)S(1)}, u32[]{:S(2)}, u32[]{:S(2)}) collective-permute-start(bf16[4,16,1024]{2,1,0:T(8,128)(2,1)S(1)} %copy-done.16), channel_id=1, source_target_pairs={{0,20},{4,16},{8,28},{12,24},{16,4},{20,0},{24,12},{28,8},{1,21},{... | collective-permute-start | bytes 393224 | tf_op jit(solution)/shard_map/ppermute | solution.py:512
  135.1 1.3 collective-permute-start.19
  137.0 1.5 %shard_map.148.refs_2_ = bf16[128,16,1024]{2,1,0:T(8,128)(2,1)} custom-call(s32[2]{0:T(128)S(1)} %pad_add_fusion.4.place_ref, bf16[16,16,1024]{2,1,0:T(8,128)(2,1)S(1)} %collective-permute-done.16.refs_0_, bf16[12,16,1024]{2,1,0:T(8,128)(2,1)S(1)} %collective-permute-done.17.refs_1_, ...), custom_call_target="tpu_custom_call", output_to_operand_aliasing={{}: (3, {})} | custom-call | bytes 2097152 | tf_op jit(solution)/shard_map/pallas_call | solution.py:148
  139.0 0.7 collective-permute-done.20
  139.8 1.2 collective-permute-done.22.refs_1_
  141.0 0.6 add_convert_fusion
  141.6 1.3 shard_map.149
  (60 shorter events, 2.2 us)
Async XLA Ops:
  0.6 16.1 %copy-start.1 = (bf16[1024,512]{1,0:T(8,128)(2,1)S(1)}, bf16[1024,512]{1,0:T(8,128)(2,1)}, u32[]{:S(2)}) copy-start(bf16[1024,512]{1,0:T(8,128)(2,1)} %query_ref.1) | copy-start | bytes 3145732
  0.6 16.1 %copy-start.3 = (bf16[1024,128]{1,0:T(8,128)(2,1)S(1)}, bf16[1024,128]{1,0:T(8,128)(2,1)}, u32[]{:S(2)}) copy-start(bf16[1024,128]{1,0:T(8,128)(2,1)} %keyval_ref.1) | copy-start | bytes 786436
  0.7 52.8 %copy-start.9 = (s32[8]{0:T(128)S(1)}, s32[8]{0:T(128)}, u32[]{:S(2)}) copy-start(s32[8]{0:T(128)} %kept_ref.1) | copy-start | bytes 100
  2.1 14.6 %all-to-all-start = ((bf16[8,5,1024]{2,1,0:T(8,128)(2,1)}), bf16[8,5,1024]{2,1,0:T(8,128)(2,1)S(1)}, u32[]{:S(2)}, u32[]{:S(2)}) async-start(bf16[8,5,1024]{2,1,0:T(8,128)(2,1)} %broadcast_in_dim.2), calls=%async_computation | async-start | bytes 262144 | tf_op jit(solution)/shard_map/all_to_all | solution.py:485
  10.0 6.8 %copy-start.6 = (s32[2]{0:T(128)S(1)}, s32[2]{0:T(128)}, u32[]{:S(2)}) copy-start(s32[2]{0:T(128)} %pad_add_fusion.me_ref) | copy-start | bytes 28
  16.8 0.7 copy-start.8
  18.4 8.2 %collective-permute-start.3 = (bf16[4,16,1024]{2,1,0:T(8,128)(2,1)}, bf16[4,16,1024]{2,1,0:T(8,128)(2,1)S(1)}, u32[]{:S(2)}, u32[]{:S(2)}) collective-permute-start(bf16[4,16,1024]{2,1,0:T(8,128)(2,1)} %get-tuple-element.120), channel_id=1, source_target_pairs={{0,24},{4,28},{8,16},{12,20},{16,8},{20,12},{24,0},{28,4},{1,25},{... | collective-permute-start | bytes 393224 | tf_op jit(solution)/shard_map/ppermute | solution.py:512
  21.6 1.9 %collective-permute-start = (f32[40,256]{1,0:T(8,128)S(1)}, f32[40,256]{1,0:T(8,128)S(1)}, u32[]{:S(2)}, u32[]{:S(2)}) collective-permute-start(f32[40,256]{1,0:T(8,128)S(1)} %get-tuple-element.117), channel_id=1, source_target_pairs={{0,1},{1,0},{2,3},{3,2},{4,5},{5,4},{6,7},{7,6},{8,9},{9,8},{10,11... | collective-permute-start | bytes 122888 | tf_op jit(solution)/shard_map/ppermute | solution.py:512
  21.6 4.0 %collective-permute-start.1 = (f32[40,256]{1,0:T(8,128)S(1)}, f32[40,256]{1,0:T(8,128)S(1)}, u32[]{:S(2)}, u32[]{:S(2)}) collective-permute-start(f32[40,256]{1,0:T(8,128)S(1)} %get-tuple-element.118), channel_id=1, source_target_pairs={{0,2},{1,3},{2,0},{3,1},{4,6},{5,7},{6,4},{7,5},{8,10},{9,11},{10,... | collective-permute-start | bytes 122888 | tf_op jit(solution)/shard_map/ppermute | solution.py:512
  23.1 3.5 %collective-permute-start.2 = (f32[40,256]{1,0:T(8,128)S(1)}, f32[40,256]{1,0:T(8,128)S(1)}, u32[]{:S(2)}, u32[]{:S(2)}) collective-permute-start(f32[40,256]{1,0:T(8,128)S(1)} %get-tuple-element.119), channel_id=1, source_target_pairs={{0,3},{1,2},{2,1},{3,0},{4,7},{5,6},{6,5},{7,4},{8,11},{9,10},{10,... | collective-permute-start | bytes 122888 | tf_op jit(solution)/shard_map/ppermute | solution.py:512
  26.7 24.7 %collective-permute-start.4 = (bf16[16,16,1024]{2,1,0:T(8,128)(2,1)}, bf16[16,16,1024]{2,1,0:T(8,128)(2,1)S(1)}, u32[]{:S(2)}, u32[]{:S(2)}) collective-permute-start(bf16[16,16,1024]{2,1,0:T(8,128)(2,1)} %get-tuple-element.129), channel_id=1, source_target_pairs={{0,4},{4,0},{8,12},{12,8},{16,20},{20,16},{24,28},{28,24},{1,5},{5... | collective-permute-start | bytes 1572872 | tf_op jit(solution)/shard_map/ppermute | solution.py:512
  28.2 23.1 %collective-permute-start.5 = (bf16[12,16,1024]{2,1,0:T(8,128)(2,1)}, bf16[12,16,1024]{2,1,0:T(8,128)(2,1)S(1)}, u32[]{:S(2)}, u32[]{:S(2)}) collective-permute-start(bf16[12,16,1024]{2,1,0:T(8,128)(2,1)} %get-tuple-element.130), channel_id=1, source_target_pairs={{0,24},{4,28},{8,16},{12,20},{16,8},{20,12},{24,0},{28,4},{1,25},{... | collective-permute-start | bytes 1179656 | tf_op jit(solution)/shard_map/ppermute | solution.py:512
  51.3 29.3 %collective-permute-start.12 = (bf16[16,16,1024]{2,1,0:T(8,128)(2,1)}, bf16[16,16,1024]{2,1,0:T(8,128)(2,1)S(1)}, u32[]{:S(2)}, u32[]{:S(2)}) collective-permute-start(bf16[16,16,1024]{2,1,0:T(8,128)(2,1)} %get-tuple-element.150), channel_id=1, source_target_pairs={{0,28},{4,24},{8,20},{12,16},{16,12},{20,8},{24,4},{28,0},{1,29},{... | collective-permute-start | bytes 1572872 | tf_op jit(solution)/shard_map/ppermute | solution.py:512
  54.8 3.5 %copy-start = (bf16[128,1024]{1,0:T(8,128)(2,1)}, bf16[128,1024]{1,0:T(8,128)(2,1)S(1)}, u32[]{:S(2)}) copy-start(bf16[128,1024]{1,0:T(8,128)(2,1)S(1)} %get-tuple-element.144.refs_6_.refs_7_) | copy-start | bytes 786436
  54.8 3.5 %copy-start.5 = (bf16[8,40,128]{2,1,0:T(8,128)(2,1)}, bf16[8,40,128]{2,1,0:T(8,128)(2,1)S(1)}, u32[]{:S(2)}) copy-start(bf16[8,40,128]{2,1,0:T(8,128)(2,1)S(1)} %get-tuple-element.140.refs_0_) | copy-start | bytes 245764
  54.8 3.5 %collective-permute-start.6 = (bf16[8,40,128]{2,1,0:T(8,128)(2,1)S(1)}, bf16[8,40,128]{2,1,0:T(8,128)(2,1)S(1)}, u32[]{:S(2)}, u32[]{:S(2)}) collective-permute-start(bf16[8,40,128]{2,1,0:T(8,128)(2,1)S(1)} %get-tuple-element.140.refs_0_), channel_id=1, source_target_pairs={{0,1},{1,0},{2,3},{3,2},{4,5},{5,4},{6,7},{7,6},{8,9},{9,8},{10,11... | collective-permute-start | bytes 245768 | tf_op jit(solution)/shard_map/ppermute | solution.py:512
  54.8 5.3 %collective-permute-start.7 = (bf16[8,40,128]{2,1,0:T(8,128)(2,1)S(1)}, bf16[8,40,128]{2,1,0:T(8,128)(2,1)S(1)}, u32[]{:S(2)}, u32[]{:S(2)}) collective-permute-start(bf16[8,40,128]{2,1,0:T(8,128)(2,1)S(1)} %get-tuple-element.140.refs_0_), channel_id=1, source_target_pairs={{0,2},{1,3},{2,0},{3,1},{4,6},{5,7},{6,4},{7,5},{8,10},{9,11},{10,... | collective-permute-start | bytes 245768 | tf_op jit(solution)/shard_map/ppermute | solution.py:512
  55.9 5.1 %collective-permute-start.8 = (bf16[8,40,128]{2,1,0:T(8,128)(2,1)S(1)}, bf16[8,40,128]{2,1,0:T(8,128)(2,1)S(1)}, u32[]{:S(2)}, u32[]{:S(2)}) collective-permute-start(bf16[8,40,128]{2,1,0:T(8,128)(2,1)S(1)} %get-tuple-element.140.refs_0_), channel_id=1, source_target_pairs={{0,3},{1,2},{2,1},{3,0},{4,7},{5,6},{6,5},{7,4},{8,11},{9,10},{10,... | collective-permute-start | bytes 245768 | tf_op jit(solution)/shard_map/ppermute | solution.py:512
  56.7 22.7 %collective-permute-start.13 = (bf16[4,16,1024]{2,1,0:T(8,128)(2,1)}, bf16[4,16,1024]{2,1,0:T(8,128)(2,1)S(1)}, u32[]{:S(2)}, u32[]{:S(2)}) collective-permute-start(bf16[4,16,1024]{2,1,0:T(8,128)(2,1)} %get-tuple-element.151), channel_id=1, source_target_pairs={{0,16},{4,20},{8,24},{12,28},{16,0},{20,4},{24,8},{28,12},{1,17},{... | collective-permute-start | bytes 393224 | tf_op jit(solution)/shard_map/ppermute | solution.py:512
  58.3 2.6 %copy-start.10 = (bf16[8,40,128]{2,1,0:T(8,128)(2,1)}, bf16[8,40,128]{2,1,0:T(8,128)(2,1)S(1)}, u32[]{:S(2)}) copy-start(bf16[8,40,128]{2,1,0:T(8,128)(2,1)S(1)} %collective-permute-done.6.refs_1_) | copy-start | bytes 245764
  60.1 0.8 copy-start.11
  60.9 0.6 copy-start.12
  61.5 21.1 %copy-start.15 = (bf16[12,16,1024]{2,1,0:T(8,128)(2,1)S(1)}, bf16[12,16,1024]{2,1,0:T(8,128)(2,1)}, u32[]{:S(2)}) copy-start(bf16[12,16,1024]{2,1,0:T(8,128)(2,1)} %get-tuple-element.161) | copy-start | bytes 1179652
  61.6 21.1 %copy-start.14 = (bf16[12,16,1024]{2,1,0:T(8,128)(2,1)S(1)}, bf16[12,16,1024]{2,1,0:T(8,128)(2,1)}, u32[]{:S(2)}) copy-start(bf16[12,16,1024]{2,1,0:T(8,128)(2,1)} %get-tuple-element.162) | copy-start | bytes 1179652
  71.9 7.6 %collective-permute-start.10 = (bf16[8,64,128]{2,1,0:T(8,128)(2,1)}, bf16[8,64,128]{2,1,0:T(8,128)(2,1)S(1)}, u32[]{:S(2)}, u32[]{:S(2)}) collective-permute-start(bf16[8,64,128]{2,1,0:T(8,128)(2,1)} %get-tuple-element.148), channel_id=1, source_target_pairs={{0,2},{1,3},{2,0},{3,1},{4,6},{5,7},{6,4},{7,5},{8,10},{9,11},{10,... | collective-permute-start | bytes 393224 | tf_op jit(solution)/shard_map/ppermute | solution.py:512
  72.9 7.7 %collective-permute-start.11 = (bf16[8,64,128]{2,1,0:T(8,128)(2,1)}, bf16[8,64,128]{2,1,0:T(8,128)(2,1)S(1)}, u32[]{:S(2)}, u32[]{:S(2)}) collective-permute-start(bf16[8,64,128]{2,1,0:T(8,128)(2,1)} %get-tuple-element.149), channel_id=1, source_target_pairs={{0,3},{1,2},{2,1},{3,0},{4,7},{5,6},{6,5},{7,4},{8,11},{9,10},{10,... | collective-permute-start | bytes 393224 | tf_op jit(solution)/shard_map/ppermute | solution.py:512
  73.8 6.8 %collective-permute-start.9 = (bf16[8,64,128]{2,1,0:T(8,128)(2,1)}, bf16[8,64,128]{2,1,0:T(8,128)(2,1)S(1)}, u32[]{:S(2)}, u32[]{:S(2)}) collective-permute-start(bf16[8,64,128]{2,1,0:T(8,128)(2,1)} %get-tuple-element.147), channel_id=1, source_target_pairs={{0,1},{1,0},{2,3},{3,2},{4,5},{5,4},{6,7},{7,6},{8,9},{9,8},{10,11... | collective-permute-start | bytes 393224 | tf_op jit(solution)/shard_map/ppermute | solution.py:512
  80.6 0.9 copy-start.4
  82.6 23.7 %collective-permute-start.14 = (bf16[12,16,1024]{2,1,0:T(8,128)(2,1)S(1)}, bf16[12,16,1024]{2,1,0:T(8,128)(2,1)S(1)}, u32[]{:S(2)}, u32[]{:S(2)}) collective-permute-start(bf16[12,16,1024]{2,1,0:T(8,128)(2,1)S(1)} %copy-done.15), channel_id=1, source_target_pairs={{0,12},{4,8},{8,4},{12,0},{16,28},{20,24},{24,20},{28,16},{1,13},{... | collective-permute-start | bytes 1179656 | tf_op jit(solution)/shard_map/ppermute | solution.py:512
  82.6 23.7 %collective-permute-start.15 = (bf16[12,16,1024]{2,1,0:T(8,128)(2,1)S(1)}, bf16[12,16,1024]{2,1,0:T(8,128)(2,1)S(1)}, u32[]{:S(2)}, u32[]{:S(2)}) collective-permute-start(bf16[12,16,1024]{2,1,0:T(8,128)(2,1)S(1)} %copy-done.14), channel_id=1, source_target_pairs={{0,16},{4,20},{8,24},{12,28},{16,0},{20,4},{24,8},{28,12},{1,17},{... | collective-permute-start | bytes 1179656 | tf_op jit(solution)/shard_map/ppermute | solution.py:512
  85.8 20.5 %all-to-all-start.2 = ((bf16[8,64,128]{2,1,0:T(8,128)(2,1)}), bf16[8,64,128]{2,1,0:T(8,128)(2,1)S(1)}, u32[]{:S(2)}, u32[]{:S(2)}) async-start(bf16[8,64,128]{2,1,0:T(8,128)(2,1)} %shard_map.143), calls=%async_computation.2 | async-start | bytes 262144 | tf_op jit(solution)/shard_map/all_to_all | solution.py:654
  89.3 18.0 %copy-start.13 = (bf16[16,16,1024]{2,1,0:T(8,128)(2,1)S(1)}, bf16[16,16,1024]{2,1,0:T(8,128)(2,1)}, u32[]{:S(2)}) copy-start(bf16[16,16,1024]{2,1,0:T(8,128)(2,1)} %get-tuple-element.173) | copy-start | bytes 1572868
  107.3 23.4 %collective-permute-start.16 = (bf16[16,16,1024]{2,1,0:T(8,128)(2,1)S(1)}, bf16[16,16,1024]{2,1,0:T(8,128)(2,1)S(1)}, u32[]{:S(2)}, u32[]{:S(2)}) collective-permute-start(bf16[16,16,1024]{2,1,0:T(8,128)(2,1)S(1)} %copy-done.13), channel_id=1, source_target_pairs={{0,8},{4,12},{8,0},{12,4},{16,24},{20,28},{24,16},{28,20},{1,9},{5... | collective-permute-start | bytes 1572872 | tf_op jit(solution)/shard_map/ppermute | solution.py:512
  108.2 22.5 %collective-permute-start.17 = (bf16[12,16,1024]{2,1,0:T(8,128)(2,1)}, bf16[12,16,1024]{2,1,0:T(8,128)(2,1)S(1)}, u32[]{:S(2)}, u32[]{:S(2)}) collective-permute-start(bf16[12,16,1024]{2,1,0:T(8,128)(2,1)} %get-tuple-element.174), channel_id=1, source_target_pairs={{0,20},{4,16},{8,28},{12,24},{16,4},{20,0},{24,12},{28,8},{1,21},{... | collective-permute-start | bytes 1179656 | tf_op jit(solution)/shard_map/ppermute | solution.py:512
  110.6 20.0 %all-to-all-start.3 = ((bf16[8,40,128]{2,1,0:T(8,128)(2,1)}), bf16[8,40,128]{2,1,0:T(8,128)(2,1)S(1)}, u32[]{:S(2)}, u32[]{:S(2)}) async-start(bf16[8,40,128]{2,1,0:T(8,128)(2,1)} %shard_map.145), calls=%async_computation.3 | async-start | bytes 163840 | tf_op jit(solution)/shard_map/all_to_all | solution.py:659
  114.0 16.6 %copy-start.2 = (bf16[1024,512]{1,0:T(8,128)(2,1)S(1)}, bf16[1024,512]{1,0:T(8,128)(2,1)}, u32[]{:S(2)}) copy-start(bf16[1024,512]{1,0:T(8,128)(2,1)} %weight_ref.1) | copy-start | bytes 3145732
  114.0 16.6 %copy-start.7 = (s32[2]{0:T(128)S(1)}, s32[2]{0:T(128)}, u32[]{:S(2)}) copy-start(s32[2]{0:T(128)} %pad_add_fusion.me_ref) | copy-start | bytes 28
  114.0 18.7 %copy-start.16 = (bf16[4,16,1024]{2,1,0:T(8,128)(2,1)S(1)}, bf16[4,16,1024]{2,1,0:T(8,128)(2,1)}, u32[]{:S(2)}) copy-start(bf16[4,16,1024]{2,1,0:T(8,128)(2,1)} %get-tuple-element.196) | copy-start | bytes 393220
  131.6 8.2 %collective-permute-start.21 = (bf16[4,16,1024]{2,1,0:T(8,128)(2,1)}, bf16[4,16,1024]{2,1,0:T(8,128)(2,1)S(1)}, u32[]{:S(2)}, u32[]{:S(2)}) collective-permute-start(bf16[4,16,1024]{2,1,0:T(8,128)(2,1)} %get-tuple-element.195), channel_id=1, source_target_pairs={{0,12},{4,8},{8,4},{12,0},{16,28},{20,24},{24,20},{28,16},{1,13},{... | collective-permute-start | bytes 393224 | tf_op jit(solution)/shard_map/ppermute | solution.py:512
  132.8 8.2 %collective-permute-start.22 = (bf16[4,16,1024]{2,1,0:T(8,128)(2,1)S(1)}, bf16[4,16,1024]{2,1,0:T(8,128)(2,1)S(1)}, u32[]{:S(2)}, u32[]{:S(2)}) collective-permute-start(bf16[4,16,1024]{2,1,0:T(8,128)(2,1)S(1)} %copy-done.16), channel_id=1, source_target_pairs={{0,20},{4,16},{8,28},{12,24},{16,4},{20,0},{24,12},{28,8},{1,21},{... | collective-permute-start | bytes 393224 | tf_op jit(solution)/shard_map/ppermute | solution.py:512
  135.1 3.4 %collective-permute-start.18 = (f32[10,512]{1,0:T(8,128)S(1)}, f32[10,512]{1,0:T(8,128)S(1)}, u32[]{:S(2)}, u32[]{:S(2)}) collective-permute-start(f32[10,512]{1,0:T(8,128)S(1)} %get-tuple-element.192), channel_id=1, source_target_pairs={{0,1},{1,0},{2,3},{3,2},{4,5},{5,4},{6,7},{7,6},{8,9},{9,8},{10,11... | collective-permute-start | bytes 61448 | tf_op jit(solution)/shard_map/ppermute | solution.py:512
  135.1 4.0 %collective-permute-start.19 = (f32[10,512]{1,0:T(8,128)S(1)}, f32[10,512]{1,0:T(8,128)S(1)}, u32[]{:S(2)}, u32[]{:S(2)}) collective-permute-start(f32[10,512]{1,0:T(8,128)S(1)} %get-tuple-element.193), channel_id=1, source_target_pairs={{0,2},{1,3},{2,0},{3,1},{4,6},{5,7},{6,4},{7,5},{8,10},{9,11},{10,... | collective-permute-start | bytes 61448 | tf_op jit(solution)/shard_map/ppermute | solution.py:512
  136.4 3.4 %collective-permute-start.20 = (f32[10,512]{1,0:T(8,128)S(1)}, f32[10,512]{1,0:T(8,128)S(1)}, u32[]{:S(2)}, u32[]{:S(2)}) collective-permute-start(f32[10,512]{1,0:T(8,128)S(1)} %get-tuple-element.194), channel_id=1, source_target_pairs={{0,3},{1,2},{2,1},{3,0},{4,7},{5,6},{6,5},{7,4},{8,11},{9,10},{10,... | collective-permute-start | bytes 61448 | tf_op jit(solution)/shard_map/ppermute | solution.py:512

commit v17 on v16

--- a/solution.py
+++ b/solution.py
@@ -18,7 +18,7 @@
 SCALE2 = math.log2(math.e) / math.sqrt(HD)
 STAT = 16
 MIB = 1024 * 1024
-CUTS = {1: (0, 16), 2: (0, 16), 3: (0, 12, 16), 4: (0, 4, 16), 5: (0, 12, 16), 6: (0, 4, 16), 7: (0, 16)}
+CUTS = {1: (0, 16), 2: (0, 16), 3: (0, 16), 4: (0, 16), 5: (0, 4, 16), 6: (0, 4, 16), 7: (0, 12, 16)}
 NT = (((1,), (1,)), ((), ()))
 
 
@@ -588,8 +588,8 @@
             *partial,
             tags,
         )
-        received = beside(lambda value: exchange(value, "wide"), packed, (1, 0), (6, 1))
-        received = launch(received, (7, 0), (4, 0))
+        received = beside(lambda value: exchange(value, "wide"), packed, (3, 0), (6, 1))
+        received = launch(received, (4, 0), (5, 0))
         queries, keyval, new_entries, moved_req, moved_idx = in_vmem(
             functools.partial(unpack_kernel, rows),
             [
@@ -618,8 +618,8 @@
         tags = jnp.pad(tags, ((0, 0), (0, 7), (0, projected.shape[1] - tags.shape[2])))
         packed = jnp.broadcast_to(projected[None], (wide,) + projected.shape)
         packed = jnp.concatenate([packed, tags], axis=1)
-        received = beside(lambda value: exchange(value, "wide"), packed, (1, 0), (6, 1))
-        received = launch(received, (7, 0), (4, 0))
+        received = beside(lambda value: exchange(value, "wide"), packed, (3, 0), (6, 1))
+        received = launch(received, (4, 0), (5, 0))
         tags_in = received[:, rows]
         queries = received[:, :rows, :own_cols]
         queries = spread(queries, "narrow")
@@ -641,22 +641,24 @@
         )
 
     queries, moved_pool = lax.optimization_barrier((queries, placed(moved_pool)))
+    queries = launch(queries, (1, 0))
     mixed = attend(both, lengths, queries, keyval, tokens, token_info, rows, piece)
+    mixed = land(mixed, (1, 0))
     if direct:
-        mixed = land(deal(mixed, "narrow"), (7, 0), (4, 0))
+        mixed = land(deal(mixed, "narrow"), (4, 0), (5, 0))
     else:
-        mixed = land(exchange(mixed[0], "narrow"), (7, 0), (4, 0))
+        mixed = land(exchange(mixed[0], "narrow"), (4, 0), (5, 0))
         mixed = mixed.reshape((narrow, wide) + mixed.shape[1:])
         mixed = [mixed[i] for i in range(narrow)]
     mixed = combine(mixed, piece)
     mixed, pages = lax.optimization_barrier((mixed, moved_pool))
     pages = placed(pages)
-    mixed = beside(lambda value: exchange(value, "wide"), mixed, (3, 0), (4, 1))
+    mixed = beside(lambda value: exchange(value, "wide"), mixed, (2, 0), (5, 1))
     mixed, moved_pool = lax.optimization_barrier((mixed, pages))
     attn = combine([mixed], piece, wide)
     attn, pages = lax.optimization_barrier((attn, moved_pool))
     pages = placed(pages)
-    attn = beside(lambda value: exchange(value, "wide"), attn, (2, 0), (5, 0))
+    attn = beside(lambda value: exchange(value, "wide"), attn, (7, 0))
     attn, moved_pool = lax.optimization_barrier((attn, pages))
     if direct:
         sums = in_vmem(
@@ -668,14 +670,14 @@
         )
         sums, pages = lax.optimization_barrier((sums, moved_pool))
         pages = placed(pages)
-        sums = beside(lambda value: deal(value, "narrow"), sums, (3, 1), (5, 1))
+        sums = beside(lambda value: deal(value, "narrow"), sums, (7, 1))
         attended = ((sums[0] + sums[1]) + (sums[2] + sums[3])).astype(jnp.bfloat16)
     else:
         attn = jnp.transpose(attn.reshape(-1, rows, HD), (1, 0, 2)).reshape(rows, -1)
         sums = jnp.dot(attn, w_out, preferred_element_type=jnp.float32)
         sums = sums.reshape(narrow, rows // narrow, -1)
         pages = placed(moved_pool)
-        sums = beside(lambda value: exchange(value, "narrow"), sums, (3, 1), (5, 1))
+        sums = beside(lambda value: exchange(value, "narrow"), sums, (7, 1))
         attended = jnp.sum(sums, axis=0).astype(jnp.bfloat16)
     attended, pages = lax.optimization_barrier((attended, pages))
     moved_pool = placed(pages)

time: 144 us -> 153 us (1.062)
  waiting for transfers between devices: 46.4 us -> 73.5 us
  blocking collectives: 21.1 us -> 0 us
  starting transfers between devices: 40.5 us -> 45.4 us
    all_to_all x1 -> x0, blocking collectives: 21.1 us -> none  [on_device(): exchange(value, 'wide')]
    all_to_all x2 -> x3, waiting for transfers between devices: 30.8 us -> 48.7 us  [the longest x1 18.9 us: on_device(): exchange(value, 'wide')]
    ppermute x23 -> x22, waiting for transfers between devices: 14.8 us -> 24 us  [send(): lax.ppermute(block, axis, [(i, i ^ d) for i in range(lax.axis_size(axis))])]
    all_to_all x2 -> x3, starting transfers between devices: 6.72 us -> 11.5 us  [the longest x1 4.06 us: on_device(): mixed = beside(lambda value: exchange(value, 'wide'), mixed, (2, 0), (5, 1))]
    ppermute x23 -> x22, starting transfers between devices: 26.5 us -> 26.7 us  [send(): lax.ppermute(block, axis, [(i, i ^ d) for i in range(lax.axis_size(axis))])]
  transfers between devices with their start and end apart: 26 -> 26, of which waited for: 12 -> 12; matrix products, arithmetic and copies ran while one was open for 1% -> 1% of each run, Pallas kernels for 16% -> 14%
where the time goes in v17:
time: 153 us
  waiting for transfers between devices  73.5 us (48%)
  starting transfers between devices  45.4 us (30%)
  Pallas kernels  28.1 us (18%)
  local copies, waits for them, and re-layouts  3.12 us (2%)
    ppermute x22, starting transfers between devices, send(): lax.ppermute(block, axis, [(i, i ^ d) for i in range(lax.axis_size(axis))])  26.7 us
    ppermute x22, waiting for transfers between devices, send(): lax.ppermute(block, axis, [(i, i ^ d) for i in range(lax.axis_size(axis))])  24 us
    all_to_all x1, waiting for transfers between devices, on_device(): exchange(value, 'wide')  18.9 us
    all_to_all x1, waiting for transfers between devices, on_device(): mixed = beside(lambda value: exchange(value, 'wide'), mixed, (2, 0), (5, 1))  16.8 us
    all_to_all x1, waiting for transfers between devices, on_device(): attn = beside(lambda value: exchange(value, 'wide'), attn, (7, 0))  13 us
    pallas_call x1, Pallas kernels, attend(): pl.pallas_call(functools.partial(attend_kernel, rows, piece, peers), grid...  10.3 us
    all_to_all x1, starting transfers between devices, spread(): lax.all_to_all(jnp.broadcast_to(block[None], (count,) + block.shape), axi...  7.28 us
    pallas_call x5, Pallas kernels, place_pages(): pl.pallas_call(place_kernel, out_shape=jax.ShapeDtypeStruct(pages.shape,...  5.99 us
  transfers between devices with their start and end apart: 26, of which 12 were waited for; matrix products, arithmetic and copies ran while one was open for 1% of the time, Pallas kernels for 14%

profile of v17, /device:TPU:0, one launch (start us, length us, event | category | flops | bytes accessed | tf_op | source)
XLA Modules:
  0.0 152.5 jit_solution(9054878122122595874)
XLA Ops:
  0.7 1.5 broadcast_in_dim.2
  2.1 7.3 %all-to-all-start = ((bf16[8,5,1024]{2,1,0:T(8,128)(2,1)}), bf16[8,5,1024]{2,1,0:T(8,128)(2,1)S(1)}, u32[]{:S(2)}, u32[]{:S(2)}) async-start(bf16[8,5,1024]{2,1,0:T(8,128)(2,1)} %broadcast_in_dim.2), calls=%async_computation | async-start | bytes 262144 | tf_op jit(solution)/shard_map/all_to_all | solution.py:485
  9.4 0.6 pad_add_fusion.me_ref
  10.1 5.8 %shard_map.137 = (bf16[128,16,1024]{2,1,0:T(8,128)(2,1)}, f32[8,128]{1,0:T(8,128)}, f32[8,2048]{1,0:T(8,128)}, bf16[16,16,1024]{2,1,0:T(8,128)(2,1)}, bf16[16,16...) custom-call(s32[2]{0:T(128)} %pad_add_fusion.me_ref, ...), custom_call_target="tpu_custom_call" | custom-call | bytes 8388608 | tf_op jit(solution)/shard_map/pallas_call | solution.py:110
  15.9 0.9 all-to-all-done.hidden_ref
  16.8 0.7 copy-done.8
  17.5 1.0 shard_map.138
  18.5 3.0 %collective-permute-start.3 = (bf16[4,16,1024]{2,1,0:T(8,128)(2,1)}, bf16[4,16,1024]{2,1,0:T(8,128)(2,1)S(1)}, u32[]{:S(2)}, u32[]{:S(2)}) collective-permute-start(bf16[4,16,1024]{2,1,0:T(8,128)(2,1)} %get-tuple-element.125), channel_id=1, source_target_pairs={{0,24},{4,28},{8,16},{12,20},{16,8},{20,12},{24,0},{28,4},{1,25},{... | collective-permute-start | bytes 393224 | tf_op jit(solution)/shard_map/ppermute | solution.py:512
  21.5 1.5 collective-permute-start.1
  23.3 2.1 %collective-permute-done.1.refs_2_ = f32[40,256]{1,0:T(8,128)S(1)} collective-permute-done((f32[40,256]{1,0:T(8,128)S(1)}, f32[40,256]{1,0:T(8,128)S(1)}, u32[]{:S(2)}, u32[]{:S(2)}) %collective-permute-start.1) | collective-permute-done | bytes 40992 | tf_op jit(solution)/shard_map/ppermute | solution.py:512
  25.5 1.0 collective-permute-done.2.refs_3_
  26.5 0.7 shard_map.139
  27.2 1.8 %collective-permute-start.4 = (bf16[16,16,1024]{2,1,0:T(8,128)(2,1)}, bf16[16,16,1024]{2,1,0:T(8,128)(2,1)S(1)}, u32[]{:S(2)}, u32[]{:S(2)}) collective-permute-start(bf16[16,16,1024]{2,1,0:T(8,128)(2,1)} %get-tuple-element.134), channel_id=1, source_target_pairs={{0,12},{4,8},{8,4},{12,0},{16,28},{20,24},{24,20},{28,16},{1,13},{... | collective-permute-start | bytes 1572872 | tf_op jit(solution)/shard_map/ppermute | solution.py:512
  29.0 2.7 %collective-permute-start.5 = (bf16[12,16,1024]{2,1,0:T(8,128)(2,1)}, bf16[12,16,1024]{2,1,0:T(8,128)(2,1)S(1)}, u32[]{:S(2)}, u32[]{:S(2)}) collective-permute-start(bf16[12,16,1024]{2,1,0:T(8,128)(2,1)} %get-tuple-element.135), channel_id=1, source_target_pairs={{0,24},{4,28},{8,16},{12,20},{16,8},{20,12},{24,0},{28,4},{1,25},{... | collective-permute-start | bytes 1179656 | tf_op jit(solution)/shard_map/ppermute | solution.py:512
  31.6 3.4 %all-to-all-start.1 = ((bf16[8,48,256]{2,1,0:T(8,128)(2,1)}), bf16[8,48,256]{2,1,0:T(8,128)(2,1)S(1)}, u32[]{:S(2)}, u32[]{:S(2)}) async-start(bf16[8,48,256]{2,1,0:T(8,128)(2,1)} %shard_map.139), calls=%async_computation.1 | async-start | bytes 393216 | tf_op jit(solution)/shard_map/all_to_all | solution.py:591
  35.0 18.9 %all-to-all-done.1.part_ref = bf16[8,48,256]{2,1,0:T(8,128)(2,1)S(1)} async-done(((bf16[8,48,256]{2,1,0:T(8,128)(2,1)}), bf16[8,48,256]{2,1,0:T(8,128)(2,1)S(1)}, u32[]{:S(2)}, u32[]{:S(2)}) %all-to-all-start.1) | async-done | bytes 196640 | tf_op jit(solution)/shard_map/all_to_all | solution.py:591
  54.0 1.4 shard_map.140
  55.3 1.1 collective-permute-start.7
  56.4 0.8 collective-permute-start.8
  57.3 1.5 %shard_map.141.refs_3_ = bf16[128,16,1024]{2,1,0:T(8,128)(2,1)} custom-call(s32[3]{0:T(128)S(1)} %pad_add_fusion.1.place_ref, bf16[16,16,1024]{2,1,0:T(8,128)(2,1)S(1)} %collective-permute-done.4.refs_0_, bf16[4,16,1024]{2,1,0:T(8,128)(2,1)S(1)} %collective-permute-done.3.refs_1_, ...), custom_call_target="tpu_custom_call", output_to_operand_aliasing={{}: (4, {})} | custom-call | bytes 3145728 | tf_op jit(solution)/shard_map/pallas_call | solution.py:148
  58.8 1.8 %collective-permute-done.7.refs_2_ = bf16[8,40,128]{2,1,0:T(8,128)(2,1)S(1)} collective-permute-done((bf16[8,40,128]{2,1,0:T(8,128)(2,1)S(1)}, bf16[8,40,128]{2,1,0:T(8,128)(2,1)S(1)}, u32[]{:S(2)}, u32[]{:S(2)}) %collective-permute-start.7) | collective-permute-done | bytes 81952 | tf_op jit(solution)/shard_map/ppermute | solution.py:512
  60.6 0.8 collective-permute-done.8.refs_3_
  61.5 1.2 collective-permute-start.9
  62.7 0.9 collective-permute-start.13
  63.5 2.3 %collective-permute-start.14 = (bf16[4,16,1024]{2,1,0:T(8,128)(2,1)S(1)}, bf16[4,16,1024]{2,1,0:T(8,128)(2,1)S(1)}, u32[]{:S(2)}, u32[]{:S(2)}) collective-permute-start(bf16[4,16,1024]{2,1,0:T(8,128)(2,1)S(1)} %copy-done.18), channel_id=1, source_target_pairs={{0,20},{4,16},{8,28},{12,24},{16,4},{20,0},{24,12},{28,8},{1,21},{... | collective-permute-start | bytes 393224 | tf_op jit(solution)/shard_map/ppermute | solution.py:512
  65.9 10.3 %shard_map.142 = (bf16[8,64,128]{2,1,0:T(8,128)(2,1)}, bf16[8,64,128]{2,1,0:T(8,128)(2,1)}, bf16[8,64,128]{2,1,0:T(8,128)(2,1)}, bf16[8,64,128]{2,1,0:T(8,128)(2,1)}) custom-call(s32[2]{0:T(128)} %pad_add_fusion.me_ref, s32[8]{0:T(128)} %length_ref.1, bf16[8,40,128]{2,1,0:T(8,128)(2,1)} %copy-done.5, bf16[8,40,128]{2,1,0:T(8,128)(2,1)} %copy-done.10, ...), custom_call_target="tpu_custom_call" | custom-call | flops 1 | bytes 1 | tf_op jit(solution)/shard_map/pallas_call | solution.py:292
  76.3 1.1 collective-permute-start.11
  77.3 0.8 collective-permute-start.12
  78.1 15.8 %collective-permute-done.14.refs_2_ = bf16[4,16,1024]{2,1,0:T(8,128)(2,1)S(1)} collective-permute-done((bf16[4,16,1024]{2,1,0:T(8,128)(2,1)S(1)}, bf16[4,16,1024]{2,1,0:T(8,128)(2,1)S(1)}, u32[]{:S(2)}, u32[]{:S(2)}) %collective-permute-start.14) | collective-permute-done | bytes 131104 | tf_op jit(solution)/shard_map/ppermute | solution.py:512
  94.0 0.9 copy-done.4
  94.9 1.1 shard_map.143
  96.0 2.5 %collective-permute-start.16 = (bf16[12,16,1024]{2,1,0:T(8,128)(2,1)}, bf16[12,16,1024]{2,1,0:T(8,128)(2,1)S(1)}, u32[]{:S(2)}, u32[]{:S(2)}) collective-permute-start(bf16[12,16,1024]{2,1,0:T(8,128)(2,1)} %get-tuple-element.177), channel_id=1, source_target_pairs={{0,20},{4,16},{8,28},{12,24},{16,4},{20,0},{24,12},{28,8},{1,21},{... | collective-permute-start | bytes 1179656 | tf_op jit(solution)/shard_map/ppermute | solution.py:512
  98.5 4.1 %all-to-all-start.2 = ((bf16[8,64,128]{2,1,0:T(8,128)(2,1)}), bf16[8,64,128]{2,1,0:T(8,128)(2,1)S(1)}, u32[]{:S(2)}, u32[]{:S(2)}) async-start(bf16[8,64,128]{2,1,0:T(8,128)(2,1)} %shard_map.143), calls=%async_computation.2 | async-start | bytes 262144 | tf_op jit(solution)/shard_map/all_to_all | solution.py:656
  102.6 1.6 %shard_map.144.refs_2_ = bf16[128,16,1024]{2,1,0:T(8,128)(2,1)} custom-call(s32[3]{0:T(128)S(1)} %pad_add_fusion.2.place_ref, bf16[16,16,1024]{2,1,0:T(8,128)(2,1)S(1)} %collective-permute-done.9.refs_0_, bf16[16,16,1024]{2,1,0:T(8,128)(2,1)S(1)} %collective-permute-done.13.refs_1_, ...), custom_call_target="tpu_custom_call", output_to_operand_aliasing={{}: (4, {})} | custom-call | bytes 3145728 | tf_op jit(solution)/shard_map/pallas_call | solution.py:148
  104.2 16.8 %all-to-all-done.2.refs_0_ = bf16[8,64,128]{2,1,0:T(8,128)(2,1)S(1)} async-done(((bf16[8,64,128]{2,1,0:T(8,128)(2,1)}), bf16[8,64,128]{2,1,0:T(8,128)(2,1)S(1)}, u32[]{:S(2)}, u32[]{:S(2)}) %all-to-all-start.2) | async-done | bytes 131104 | tf_op jit(solution)/shard_map/all_to_all | solution.py:656
  121.0 0.9 shard_map.145
  121.9 2.0 %collective-permute-start.17 = (bf16[12,16,1024]{2,1,0:T(8,128)(2,1)S(1)}, bf16[12,16,1024]{2,1,0:T(8,128)(2,1)S(1)}, u32[]{:S(2)}, u32[]{:S(2)}) collective-permute-start(bf16[12,16,1024]{2,1,0:T(8,128)(2,1)S(1)} %copy-done.16), channel_id=1, source_target_pairs={{0,28},{4,24},{8,20},{12,16},{16,12},{20,8},{24,4},{28,0},{1,29},{... | collective-permute-start | bytes 1179656 | tf_op jit(solution)/shard_map/ppermute | solution.py:512
  123.9 4.0 %all-to-all-start.3 = ((bf16[8,40,128]{2,1,0:T(8,128)(2,1)}), bf16[8,40,128]{2,1,0:T(8,128)(2,1)S(1)}, u32[]{:S(2)}, u32[]{:S(2)}) async-start(bf16[8,40,128]{2,1,0:T(8,128)(2,1)} %shard_map.145), calls=%async_computation.3 | async-start | bytes 163840 | tf_op jit(solution)/shard_map/all_to_all | solution.py:661
  128.0 1.5 shard_map.146.refs_1_
  129.5 13.0 %all-to-all-done.3.part_ref = bf16[8,40,128]{2,1,0:T(8,128)(2,1)S(1)} async-done(((bf16[8,40,128]{2,1,0:T(8,128)(2,1)}), bf16[8,40,128]{2,1,0:T(8,128)(2,1)S(1)}, u32[]{:S(2)}, u32[]{:S(2)}) %all-to-all-start.3) | async-done | bytes 81952 | tf_op jit(solution)/shard_map/all_to_all | solution.py:661
  142.5 0.9 shard_map.147
  143.4 2.9 %collective-permute-start.21 = (bf16[4,16,1024]{2,1,0:T(8,128)(2,1)S(1)}, bf16[4,16,1024]{2,1,0:T(8,128)(2,1)S(1)}, u32[]{:S(2)}, u32[]{:S(2)}) collective-permute-start(bf16[4,16,1024]{2,1,0:T(8,128)(2,1)S(1)} %copy-done.17), channel_id=1, source_target_pairs={{0,28},{4,24},{8,20},{12,16},{16,12},{20,8},{24,4},{28,0},{1,29},{... | collective-permute-start | bytes 393224 | tf_op jit(solution)/shard_map/ppermute | solution.py:512
  146.3 1.1 collective-permute-start.19
  147.4 0.7 collective-permute-start.20
  148.1 0.8 shard_map.148.refs_1_
  148.9 1.3 collective-permute-done.19
  151.2 0.6 add_convert_fusion
  151.9 0.7 shard_map.149
  (61 shorter events, 1.8 us)
Async XLA Ops:
  0.6 16.1 %copy-start.1 = (bf16[1024,512]{1,0:T(8,128)(2,1)S(1)}, bf16[1024,512]{1,0:T(8,128)(2,1)}, u32[]{:S(2)}) copy-start(bf16[1024,512]{1,0:T(8,128)(2,1)} %query_ref.1) | copy-start | bytes 3145732
  0.6 16.1 %copy-start.3 = (bf16[1024,128]{1,0:T(8,128)(2,1)S(1)}, bf16[1024,128]{1,0:T(8,128)(2,1)}, u32[]{:S(2)}) copy-start(bf16[1024,128]{1,0:T(8,128)(2,1)} %keyval_ref.1) | copy-start | bytes 786436
  0.7 53.3 %copy-start.9 = (s32[8]{0:T(128)S(1)}, s32[8]{0:T(128)}, u32[]{:S(2)}) copy-start(s32[8]{0:T(128)} %kept_ref.1) | copy-start | bytes 100
  2.1 14.6 %all-to-all-start = ((bf16[8,5,1024]{2,1,0:T(8,128)(2,1)}), bf16[8,5,1024]{2,1,0:T(8,128)(2,1)S(1)}, u32[]{:S(2)}, u32[]{:S(2)}) async-start(bf16[8,5,1024]{2,1,0:T(8,128)(2,1)} %broadcast_in_dim.2), calls=%async_computation | async-start | bytes 262144 | tf_op jit(solution)/shard_map/all_to_all | solution.py:485
  10.1 6.7 %copy-start.6 = (s32[2]{0:T(128)S(1)}, s32[2]{0:T(128)}, u32[]{:S(2)}) copy-start(s32[2]{0:T(128)} %pad_add_fusion.me_ref) | copy-start | bytes 28
  16.8 0.7 copy-start.8
  18.5 8.1 %collective-permute-start.3 = (bf16[4,16,1024]{2,1,0:T(8,128)(2,1)}, bf16[4,16,1024]{2,1,0:T(8,128)(2,1)S(1)}, u32[]{:S(2)}, u32[]{:S(2)}) collective-permute-start(bf16[4,16,1024]{2,1,0:T(8,128)(2,1)} %get-tuple-element.125), channel_id=1, source_target_pairs={{0,24},{4,28},{8,16},{12,20},{16,8},{20,12},{24,0},{28,4},{1,25},{... | collective-permute-start | bytes 393224 | tf_op jit(solution)/shard_map/ppermute | solution.py:512
  21.5 1.9 %collective-permute-start = (f32[40,256]{1,0:T(8,128)S(1)}, f32[40,256]{1,0:T(8,128)S(1)}, u32[]{:S(2)}, u32[]{:S(2)}) collective-permute-start(f32[40,256]{1,0:T(8,128)S(1)} %get-tuple-element.122), channel_id=1, source_target_pairs={{0,1},{1,0},{2,3},{3,2},{4,5},{5,4},{6,7},{7,6},{8,9},{9,8},{10,11... | collective-permute-start | bytes 122888 | tf_op jit(solution)/shard_map/ppermute | solution.py:512
  21.5 4.0 %collective-permute-start.1 = (f32[40,256]{1,0:T(8,128)S(1)}, f32[40,256]{1,0:T(8,128)S(1)}, u32[]{:S(2)}, u32[]{:S(2)}) collective-permute-start(f32[40,256]{1,0:T(8,128)S(1)} %get-tuple-element.123), channel_id=1, source_target_pairs={{0,2},{1,3},{2,0},{3,1},{4,6},{5,7},{6,4},{7,5},{8,10},{9,11},{10,... | collective-permute-start | bytes 122888 | tf_op jit(solution)/shard_map/ppermute | solution.py:512
  23.0 3.5 %collective-permute-start.2 = (f32[40,256]{1,0:T(8,128)S(1)}, f32[40,256]{1,0:T(8,128)S(1)}, u32[]{:S(2)}, u32[]{:S(2)}) collective-permute-start(f32[40,256]{1,0:T(8,128)S(1)} %get-tuple-element.124), channel_id=1, source_target_pairs={{0,3},{1,2},{2,1},{3,0},{4,7},{5,6},{6,5},{7,4},{8,11},{9,10},{10,... | collective-permute-start | bytes 122888 | tf_op jit(solution)/shard_map/ppermute | solution.py:512
  27.2 26.7 %collective-permute-start.4 = (bf16[16,16,1024]{2,1,0:T(8,128)(2,1)}, bf16[16,16,1024]{2,1,0:T(8,128)(2,1)S(1)}, u32[]{:S(2)}, u32[]{:S(2)}) collective-permute-start(bf16[16,16,1024]{2,1,0:T(8,128)(2,1)} %get-tuple-element.134), channel_id=1, source_target_pairs={{0,12},{4,8},{8,4},{12,0},{16,28},{20,24},{24,20},{28,16},{1,13},{... | collective-permute-start | bytes 1572872 | tf_op jit(solution)/shard_map/ppermute | solution.py:512
  29.0 25.0 %collective-permute-start.5 = (bf16[12,16,1024]{2,1,0:T(8,128)(2,1)}, bf16[12,16,1024]{2,1,0:T(8,128)(2,1)S(1)}, u32[]{:S(2)}, u32[]{:S(2)}) collective-permute-start(bf16[12,16,1024]{2,1,0:T(8,128)(2,1)} %get-tuple-element.135), channel_id=1, source_target_pairs={{0,24},{4,28},{8,16},{12,20},{16,8},{20,12},{24,0},{28,4},{1,25},{... | collective-permute-start | bytes 1179656 | tf_op jit(solution)/shard_map/ppermute | solution.py:512
  31.6 22.3 %all-to-all-start.1 = ((bf16[8,48,256]{2,1,0:T(8,128)(2,1)}), bf16[8,48,256]{2,1,0:T(8,128)(2,1)S(1)}, u32[]{:S(2)}, u32[]{:S(2)}) async-start(bf16[8,48,256]{2,1,0:T(8,128)(2,1)} %shard_map.139), calls=%async_computation.1 | async-start | bytes 393216 | tf_op jit(solution)/shard_map/all_to_all | solution.py:591
  55.3 3.5 %copy-start = (bf16[128,1024]{1,0:T(8,128)(2,1)}, bf16[128,1024]{1,0:T(8,128)(2,1)S(1)}, u32[]{:S(2)}) copy-start(bf16[128,1024]{1,0:T(8,128)(2,1)S(1)} %get-tuple-element.154.refs_6_.refs_7_) | copy-start | bytes 786436
  55.3 3.5 %copy-start.5 = (bf16[8,40,128]{2,1,0:T(8,128)(2,1)}, bf16[8,40,128]{2,1,0:T(8,128)(2,1)S(1)}, u32[]{:S(2)}) copy-start(bf16[8,40,128]{2,1,0:T(8,128)(2,1)S(1)} %get-tuple-element.150.refs_0_) | copy-start | bytes 245764
  55.3 3.5 %collective-permute-start.6 = (bf16[8,40,128]{2,1,0:T(8,128)(2,1)S(1)}, bf16[8,40,128]{2,1,0:T(8,128)(2,1)S(1)}, u32[]{:S(2)}, u32[]{:S(2)}) collective-permute-start(bf16[8,40,128]{2,1,0:T(8,128)(2,1)S(1)} %get-tuple-element.150.refs_0_), channel_id=1, source_target_pairs={{0,1},{1,0},{2,3},{3,2},{4,5},{5,4},{6,7},{7,6},{8,9},{9,8},{10,11... | collective-permute-start | bytes 245768 | tf_op jit(solution)/shard_map/ppermute | solution.py:512
  55.3 5.3 %collective-permute-start.7 = (bf16[8,40,128]{2,1,0:T(8,128)(2,1)S(1)}, bf16[8,40,128]{2,1,0:T(8,128)(2,1)S(1)}, u32[]{:S(2)}, u32[]{:S(2)}) collective-permute-start(bf16[8,40,128]{2,1,0:T(8,128)(2,1)S(1)} %get-tuple-element.150.refs_0_), channel_id=1, source_target_pairs={{0,2},{1,3},{2,0},{3,1},{4,6},{5,7},{6,4},{7,5},{8,10},{9,11},{10,... | collective-permute-start | bytes 245768 | tf_op jit(solution)/shard_map/ppermute | solution.py:512
  56.4 5.1 %collective-permute-start.8 = (bf16[8,40,128]{2,1,0:T(8,128)(2,1)S(1)}, bf16[8,40,128]{2,1,0:T(8,128)(2,1)S(1)}, u32[]{:S(2)}, u32[]{:S(2)}) collective-permute-start(bf16[8,40,128]{2,1,0:T(8,128)(2,1)S(1)} %get-tuple-element.150.refs_0_), channel_id=1, source_target_pairs={{0,3},{1,2},{2,1},{3,0},{4,7},{5,6},{6,5},{7,4},{8,11},{9,10},{10,... | collective-permute-start | bytes 245768 | tf_op jit(solution)/shard_map/ppermute | solution.py:512
  57.2 4.2 %copy-start.15 = (bf16[16,16,1024]{2,1,0:T(8,128)(2,1)S(1)}, bf16[16,16,1024]{2,1,0:T(8,128)(2,1)}, u32[]{:S(2)}) copy-start(bf16[16,16,1024]{2,1,0:T(8,128)(2,1)} %get-tuple-element.160) | copy-start | bytes 1572868
  57.3 5.4 %copy-start.14 = (bf16[16,16,1024]{2,1,0:T(8,128)(2,1)S(1)}, bf16[16,16,1024]{2,1,0:T(8,128)(2,1)}, u32[]{:S(2)}) copy-start(bf16[16,16,1024]{2,1,0:T(8,128)(2,1)} %get-tuple-element.165) | copy-start | bytes 1572868
  57.3 6.3 %copy-start.18 = (bf16[4,16,1024]{2,1,0:T(8,128)(2,1)S(1)}, bf16[4,16,1024]{2,1,0:T(8,128)(2,1)}, u32[]{:S(2)}) copy-start(bf16[4,16,1024]{2,1,0:T(8,128)(2,1)} %get-tuple-element.166) | copy-start | bytes 393220
  58.8 7.0 %copy-start.10 = (bf16[8,40,128]{2,1,0:T(8,128)(2,1)}, bf16[8,40,128]{2,1,0:T(8,128)(2,1)S(1)}, u32[]{:S(2)}) copy-start(bf16[8,40,128]{2,1,0:T(8,128)(2,1)S(1)} %collective-permute-done.6.refs_1_) | copy-start | bytes 245764
  60.6 5.2 %copy-start.11 = (bf16[8,40,128]{2,1,0:T(8,128)(2,1)}, bf16[8,40,128]{2,1,0:T(8,128)(2,1)S(1)}, u32[]{:S(2)}) copy-start(bf16[8,40,128]{2,1,0:T(8,128)(2,1)S(1)} %collective-permute-done.7.refs_2_) | copy-start | bytes 245764
  61.5 4.4 %copy-start.12 = (bf16[8,40,128]{2,1,0:T(8,128)(2,1)}, bf16[8,40,128]{2,1,0:T(8,128)(2,1)S(1)}, u32[]{:S(2)}) copy-start(bf16[8,40,128]{2,1,0:T(8,128)(2,1)S(1)} %collective-permute-done.8.refs_3_) | copy-start | bytes 245764
  61.5 14.7 %collective-permute-start.9 = (bf16[16,16,1024]{2,1,0:T(8,128)(2,1)S(1)}, bf16[16,16,1024]{2,1,0:T(8,128)(2,1)S(1)}, u32[]{:S(2)}, u32[]{:S(2)}) collective-permute-start(bf16[16,16,1024]{2,1,0:T(8,128)(2,1)S(1)} %copy-done.15), channel_id=1, source_target_pairs={{0,4},{4,0},{8,12},{12,8},{16,20},{20,16},{24,28},{28,24},{1,5},{5... | collective-permute-start | bytes 1572872 | tf_op jit(solution)/shard_map/ppermute | solution.py:512
  62.7 31.3 %collective-permute-start.13 = (bf16[16,16,1024]{2,1,0:T(8,128)(2,1)S(1)}, bf16[16,16,1024]{2,1,0:T(8,128)(2,1)S(1)}, u32[]{:S(2)}, u32[]{:S(2)}) collective-permute-start(bf16[16,16,1024]{2,1,0:T(8,128)(2,1)S(1)} %copy-done.14), channel_id=1, source_target_pairs={{0,16},{4,20},{8,24},{12,28},{16,0},{20,4},{24,8},{28,12},{1,17},{... | collective-permute-start | bytes 1572872 | tf_op jit(solution)/shard_map/ppermute | solution.py:512
  63.5 30.4 %collective-permute-start.14 = (bf16[4,16,1024]{2,1,0:T(8,128)(2,1)S(1)}, bf16[4,16,1024]{2,1,0:T(8,128)(2,1)S(1)}, u32[]{:S(2)}, u32[]{:S(2)}) collective-permute-start(bf16[4,16,1024]{2,1,0:T(8,128)(2,1)S(1)} %copy-done.18), channel_id=1, source_target_pairs={{0,20},{4,16},{8,28},{12,24},{16,4},{20,0},{24,12},{28,8},{1,21},{... | collective-permute-start | bytes 393224 | tf_op jit(solution)/shard_map/ppermute | solution.py:512
  65.9 30.1 %copy-start.13 = (bf16[16,16,1024]{2,1,0:T(8,128)(2,1)S(1)}, bf16[16,16,1024]{2,1,0:T(8,128)(2,1)}, u32[]{:S(2)}) copy-start(bf16[16,16,1024]{2,1,0:T(8,128)(2,1)} %get-tuple-element.176) | copy-start | bytes 1572868
  76.2 17.8 %collective-permute-start.10 = (bf16[8,64,128]{2,1,0:T(8,128)(2,1)}, bf16[8,64,128]{2,1,0:T(8,128)(2,1)S(1)}, u32[]{:S(2)}, u32[]{:S(2)}) collective-permute-start(bf16[8,64,128]{2,1,0:T(8,128)(2,1)} %get-tuple-element.162), channel_id=1, source_target_pairs={{0,1},{1,0},{2,3},{3,2},{4,5},{5,4},{6,7},{7,6},{8,9},{9,8},{10,11... | collective-permute-start | bytes 393224 | tf_op jit(solution)/shard_map/ppermute | solution.py:512
  76.3 17.7 %collective-permute-start.11 = (bf16[8,64,128]{2,1,0:T(8,128)(2,1)}, bf16[8,64,128]{2,1,0:T(8,128)(2,1)S(1)}, u32[]{:S(2)}, u32[]{:S(2)}) collective-permute-start(bf16[8,64,128]{2,1,0:T(8,128)(2,1)} %get-tuple-element.163), channel_id=1, source_target_pairs={{0,2},{1,3},{2,0},{3,1},{4,6},{5,7},{6,4},{7,5},{8,10},{9,11},{10,... | collective-permute-start | bytes 393224 | tf_op jit(solution)/shard_map/ppermute | solution.py:512
  77.3 16.7 %collective-permute-start.12 = (bf16[8,64,128]{2,1,0:T(8,128)(2,1)}, bf16[8,64,128]{2,1,0:T(8,128)(2,1)S(1)}, u32[]{:S(2)}, u32[]{:S(2)}) collective-permute-start(bf16[8,64,128]{2,1,0:T(8,128)(2,1)} %get-tuple-element.164), channel_id=1, source_target_pairs={{0,3},{1,2},{2,1},{3,0},{4,7},{5,6},{6,5},{7,4},{8,11},{9,10},{10,... | collective-permute-start | bytes 393224 | tf_op jit(solution)/shard_map/ppermute | solution.py:512
  94.0 0.9 copy-start.4
  96.0 25.0 %collective-permute-start.15 = (bf16[16,16,1024]{2,1,0:T(8,128)(2,1)S(1)}, bf16[16,16,1024]{2,1,0:T(8,128)(2,1)S(1)}, u32[]{:S(2)}, u32[]{:S(2)}) collective-permute-start(bf16[16,16,1024]{2,1,0:T(8,128)(2,1)S(1)} %copy-done.13), channel_id=1, source_target_pairs={{0,8},{4,12},{8,0},{12,4},{16,24},{20,28},{24,16},{28,20},{1,9},{5... | collective-permute-start | bytes 1572872 | tf_op jit(solution)/shard_map/ppermute | solution.py:512
  96.0 25.0 %collective-permute-start.16 = (bf16[12,16,1024]{2,1,0:T(8,128)(2,1)}, bf16[12,16,1024]{2,1,0:T(8,128)(2,1)S(1)}, u32[]{:S(2)}, u32[]{:S(2)}) collective-permute-start(bf16[12,16,1024]{2,1,0:T(8,128)(2,1)} %get-tuple-element.177), channel_id=1, source_target_pairs={{0,20},{4,16},{8,28},{12,24},{16,4},{20,0},{24,12},{28,8},{1,21},{... | collective-permute-start | bytes 1179656 | tf_op jit(solution)/shard_map/ppermute | solution.py:512
  98.5 22.5 %all-to-all-start.2 = ((bf16[8,64,128]{2,1,0:T(8,128)(2,1)}), bf16[8,64,128]{2,1,0:T(8,128)(2,1)S(1)}, u32[]{:S(2)}, u32[]{:S(2)}) async-start(bf16[8,64,128]{2,1,0:T(8,128)(2,1)} %shard_map.143), calls=%async_computation.2 | async-start | bytes 262144 | tf_op jit(solution)/shard_map/all_to_all | solution.py:656
  102.6 19.3 %copy-start.16 = (bf16[12,16,1024]{2,1,0:T(8,128)(2,1)S(1)}, bf16[12,16,1024]{2,1,0:T(8,128)(2,1)}, u32[]{:S(2)}) copy-start(bf16[12,16,1024]{2,1,0:T(8,128)(2,1)} %get-tuple-element.188) | copy-start | bytes 1179652
  121.9 20.5 %collective-permute-start.17 = (bf16[12,16,1024]{2,1,0:T(8,128)(2,1)S(1)}, bf16[12,16,1024]{2,1,0:T(8,128)(2,1)S(1)}, u32[]{:S(2)}, u32[]{:S(2)}) collective-permute-start(bf16[12,16,1024]{2,1,0:T(8,128)(2,1)S(1)} %copy-done.16), channel_id=1, source_target_pairs={{0,28},{4,24},{8,20},{12,16},{16,12},{20,8},{24,4},{28,0},{1,29},{... | collective-permute-start | bytes 1179656 | tf_op jit(solution)/shard_map/ppermute | solution.py:512
  123.9 18.5 %all-to-all-start.3 = ((bf16[8,40,128]{2,1,0:T(8,128)(2,1)}), bf16[8,40,128]{2,1,0:T(8,128)(2,1)S(1)}, u32[]{:S(2)}, u32[]{:S(2)}) async-start(bf16[8,40,128]{2,1,0:T(8,128)(2,1)} %shard_map.145), calls=%async_computation.3 | async-start | bytes 163840 | tf_op jit(solution)/shard_map/all_to_all | solution.py:661
  128.0 14.5 %copy-start.2 = (bf16[1024,512]{1,0:T(8,128)(2,1)S(1)}, bf16[1024,512]{1,0:T(8,128)(2,1)}, u32[]{:S(2)}) copy-start(bf16[1024,512]{1,0:T(8,128)(2,1)} %weight_ref.1) | copy-start | bytes 3145732
  128.0 14.5 %copy-start.7 = (s32[2]{0:T(128)S(1)}, s32[2]{0:T(128)}, u32[]{:S(2)}) copy-start(s32[2]{0:T(128)} %pad_add_fusion.me_ref) | copy-start | bytes 28
  128.0 15.4 %copy-start.17 = (bf16[4,16,1024]{2,1,0:T(8,128)(2,1)S(1)}, bf16[4,16,1024]{2,1,0:T(8,128)(2,1)}, u32[]{:S(2)}) copy-start(bf16[4,16,1024]{2,1,0:T(8,128)(2,1)} %get-tuple-element.208) | copy-start | bytes 393220
  143.4 7.8 %collective-permute-start.21 = (bf16[4,16,1024]{2,1,0:T(8,128)(2,1)S(1)}, bf16[4,16,1024]{2,1,0:T(8,128)(2,1)S(1)}, u32[]{:S(2)}, u32[]{:S(2)}) collective-permute-start(bf16[4,16,1024]{2,1,0:T(8,128)(2,1)S(1)} %copy-done.17), channel_id=1, source_target_pairs={{0,28},{4,24},{8,20},{12,16},{16,12},{20,8},{24,4},{28,0},{1,29},{... | collective-permute-start | bytes 393224 | tf_op jit(solution)/shard_map/ppermute | solution.py:512
  146.3 2.6 %collective-permute-start.18 = (f32[10,512]{1,0:T(8,128)S(1)}, f32[10,512]{1,0:T(8,128)S(1)}, u32[]{:S(2)}, u32[]{:S(2)}) collective-permute-start(f32[10,512]{1,0:T(8,128)S(1)} %get-tuple-element.205), channel_id=1, source_target_pairs={{0,1},{1,0},{2,3},{3,2},{4,5},{5,4},{6,7},{7,6},{8,9},{9,8},{10,11... | collective-permute-start | bytes 61448 | tf_op jit(solution)/shard_map/ppermute | solution.py:512
  146.3 3.9 %collective-permute-start.19 = (f32[10,512]{1,0:T(8,128)S(1)}, f32[10,512]{1,0:T(8,128)S(1)}, u32[]{:S(2)}, u32[]{:S(2)}) collective-permute-start(f32[10,512]{1,0:T(8,128)S(1)} %get-tuple-element.206), channel_id=1, source_target_pairs={{0,2},{1,3},{2,0},{3,1},{4,6},{5,7},{6,4},{7,5},{8,10},{9,11},{10,... | collective-permute-start | bytes 61448 | tf_op jit(solution)/shard_map/ppermute | solution.py:512
  147.4 3.3 %collective-permute-start.20 = (f32[10,512]{1,0:T(8,128)S(1)}, f32[10,512]{1,0:T(8,128)S(1)}, u32[]{:S(2)}, u32[]{:S(2)}) collective-permute-start(f32[10,512]{1,0:T(8,128)S(1)} %get-tuple-element.207), channel_id=1, source_target_pairs={{0,3},{1,2},{2,1},{3,0},{4,7},{5,6},{6,5},{7,4},{8,11},{9,10},{10,... | collective-permute-start | bytes 61448 | tf_op jit(solution)/shard_map/ppermute | solution.py:512

commit v18 on v14

--- a/solution.py
+++ b/solution.py
@@ -372,11 +372,7 @@
         in_specs=[pl.BlockSpec(memory_space=pltpu.VMEM)] * len(parts),
         out_specs=pl.BlockSpec(memory_space=pltpu.VMEM),
         compiler_params=pltpu.CompilerParams(vmem_limit_bytes=8 * MIB),
-        cost_estimate=pl.CostEstimate(
-            flops=2 * len(parts) * parts[0].size,
-            bytes_accessed=len(parts) * parts[0].size * 2,
-            transcendentals=0,
-        ),
+        cost_estimate=pl.CostEstimate(flops=1, bytes_accessed=1, transcendentals=0),
     )(*parts)
 
 
@@ -475,9 +471,7 @@
         out_specs=jax.tree.map(lambda _: pl.BlockSpec(memory_space=pltpu.VMEM), out_shape),
         scratch_shapes=scratch,
         compiler_params=pltpu.CompilerParams(vmem_limit_bytes=16 * MIB),
-        cost_estimate=pl.CostEstimate(
-            flops=0, bytes_accessed=sum(2 * arg.size for arg in args), transcendentals=0
-        ),
+        cost_estimate=pl.CostEstimate(flops=1, bytes_accessed=1, transcendentals=0),
     )(*head, *args)
 
 
@@ -549,9 +543,6 @@
         arrived.update(zip(taken, got))
         return values
 
-    def beside(step, value, *names):
-        return land(step(launch(value, *names)), *names)
-
     def placed(pages):
         taken = sorted(arrived)
         if not taken:
@@ -578,7 +569,7 @@
             w_keyval,
             scratch=[pltpu.VMEM((rows, narrow * HD), jnp.float32)],
         )
-        partial = deal(partial, "narrow")
+        partial = launch(deal(partial, "narrow"), 6, 1)
         packed = in_vmem(
             functools.partial(pack_kernel, narrow),
             jax.ShapeDtypeStruct((wide, rows + wide, 2 * HD), jnp.bfloat16),
@@ -586,7 +577,7 @@
             *partial,
             tags,
         )
-        received = beside(lambda value: exchange(value, "wide"), packed, 6, 1)
+        received = land(exchange(packed, "wide"), 6, 1)
         received = launch(received, 0)
         queries, keyval, new_entries, moved_req, moved_idx = in_vmem(
             functools.partial(unpack_kernel, rows),
@@ -610,13 +601,13 @@
         partial = jnp.concatenate(
             [query_part, jnp.broadcast_to(keyval_part[None], (narrow,) + keyval_part.shape)], axis=2
         )
-        partial = exchange(partial, "narrow")
+        partial = launch(exchange(partial, "narrow"), 6, 1)
         projected = jnp.sum(partial, axis=0).astype(jnp.bfloat16)
         tags = tags[:, : 3 * capacity].astype(jnp.bfloat16)[:, None]
         tags = jnp.pad(tags, ((0, 0), (0, 7), (0, projected.shape[1] - tags.shape[2])))
         packed = jnp.broadcast_to(projected[None], (wide,) + projected.shape)
         packed = jnp.concatenate([packed, tags], axis=1)
-        received = beside(lambda value: exchange(value, "wide"), packed, 6, 1)
+        received = land(exchange(packed, "wide"), 6, 1)
         received = launch(received, 0)
         tags_in = received[:, rows]
         queries = received[:, :rows, :own_cols]
@@ -646,16 +637,17 @@
         mixed = land(exchange(mixed[0], "narrow"), 0)
         mixed = mixed.reshape((narrow, wide) + mixed.shape[1:])
         mixed = [mixed[i] for i in range(narrow)]
-    mixed = combine(mixed, piece)
+    mixed = combine(launch(mixed, 3, 4), piece)
     mixed, pages = lax.optimization_barrier((mixed, moved_pool))
     pages = placed(pages)
-    mixed = beside(lambda value: exchange(value, "wide"), mixed, 3, 4)
+    mixed = land(exchange(mixed, "wide"), 3, 4)
     mixed, moved_pool = lax.optimization_barrier((mixed, pages))
-    attn = combine([mixed], piece, wide)
+    attn = combine([launch(mixed, 2, 5)], piece, wide)
     attn, pages = lax.optimization_barrier((attn, moved_pool))
     pages = placed(pages)
-    attn = beside(lambda value: exchange(value, "wide"), attn, 2, 5)
+    attn = land(exchange(attn, "wide"), 2, 5)
     attn, moved_pool = lax.optimization_barrier((attn, pages))
+    attn = launch(attn, 7)
     if direct:
         sums = in_vmem(
             functools.partial(finish_kernel, narrow),
@@ -666,14 +658,14 @@
         )
         sums, pages = lax.optimization_barrier((sums, moved_pool))
         pages = placed(pages)
-        sums = beside(lambda value: deal(value, "narrow"), sums, 7)
+        sums = land(deal(sums, "narrow"), 7)
         attended = ((sums[0] + sums[1]) + (sums[2] + sums[3])).astype(jnp.bfloat16)
     else:
         attn = jnp.transpose(attn.reshape(-1, rows, HD), (1, 0, 2)).reshape(rows, -1)
         sums = jnp.dot(attn, w_out, preferred_element_type=jnp.float32)
         sums = sums.reshape(narrow, rows // narrow, -1)
         pages = placed(moved_pool)
-        sums = beside(lambda value: exchange(value, "narrow"), sums, 7)
+        sums = land(exchange(sums, "narrow"), 7)
         attended = jnp.sum(sums, axis=0).astype(jnp.bfloat16)
     attended, pages = lax.optimization_barrier((attended, pages))
     moved_pool = placed(pages)

time: 143 us -> 141 us (0.986)
  the two profiles are of different devices: /device:TPU:10 before, /device:TPU:8 now
where the time goes in v18:
time: 141 us
  waiting for transfers between devices  46 us (33%)
  starting transfers between devices  41.2 us (29%)
  Pallas kernels  27.8 us (20%)
  blocking collectives  19.6 us (14%)
  local copies, waits for them, and re-layouts  3.75 us (3%)
  other arithmetic  1.45 us (1%)
    ppermute x19, waiting for transfers between devices, send(): lax.ppermute(block, axis, [(i, i ^ d) for i in range(lax.axis_size(axis))])  24.9 us
    all_to_all x1, blocking collectives, on_device(): received = land(exchange(packed, 'wide'), 6, 1)  19.6 us
    ppermute x19, starting transfers between devices, send(): lax.ppermute(block, axis, [(i, i ^ d) for i in range(lax.axis_size(axis))])  18.2 us
    all_to_all x1, waiting for transfers between devices, on_device(): attn = land(exchange(attn, 'wide'), 2, 5)  11.2 us
    pallas_call x1, Pallas kernels, attend(): pl.pallas_call(functools.partial(attend_kernel, rows, piece, peers), grid...  10.3 us
    all_to_all x1, waiting for transfers between devices, on_device(): mixed = land(exchange(mixed, 'wide'), 3, 4)  9.65 us
    pallas_call x5, Pallas kernels, place_pages(): pl.pallas_call(functools.partial(place_kernel, counts), out_shape=jax.Sha...  6.64 us
    all_to_all x1, starting transfers between devices, spread(): lax.all_to_all(jnp.broadcast_to(block[None], (count,) + block.shape), axi...  6.28 us
  transfers between devices with their start and end apart: 23, of which 12 were waited for; matrix products, arithmetic and copies ran while one was open for 1% of the time, Pallas kernels for 19%

profile of v18, /device:TPU:8, one launch (start us, length us, event | category | flops | bytes accessed | tf_op | source)
XLA Modules:
  0.0 140.7 jit_solution(17553553318050789954)
XLA Ops:
  0.7 1.5 %broadcast_in_dim.2 = bf16[8,5,1024]{2,1,0:T(8,128)(2,1)} broadcast(bf16[5,1024]{1,0:T(8,128)(2,1)} %param.10), dimensions={1,2} | broadcast | bytes 92160 | tf_op jit(solution)/shard_map/broadcast_in_dim | solution.py:485
  2.1 6.3 %all-to-all-start = ((bf16[8,5,1024]{2,1,0:T(8,128)(2,1)}), bf16[8,5,1024]{2,1,0:T(8,128)(2,1)S(1)}, u32[]{:S(2)}, u32[]{:S(2)}) async-start(bf16[8,5,1024]{2,1,0:T(8,128)(2,1)} %broadcast_in_dim.2), calls=%async_computation | async-start | bytes 262144 | tf_op jit(solution)/shard_map/all_to_all | solution.py:484
  8.4 0.6 pad_add_fusion.me_ref
  9.0 5.7 %shard_map.137 = (bf16[128,16,1024]{2,1,0:T(8,128)(2,1)}, f32[8,128]{1,0:T(8,128)}, f32[8,2048]{1,0:T(8,128)}, bf16[40,16,1024]{2,1,0:T(8,128)(2,1)}, bf16[11,16...) custom-call(s32[2]{0:T(128)} %pad_add_fusion.me_ref, ...), custom_call_target="tpu_custom_call" | custom-call | bytes 8388608 | tf_op jit(solution)/shard_map/pallas_call | solution.py:118
  14.7 1.0 shard_map.138
  15.8 1.6 %collective-permute-start.1 = (f32[40,256]{1,0:T(8,128)S(1)}, f32[40,256]{1,0:T(8,128)S(1)}, u32[]{:S(2)}, u32[]{:S(2)}) collective-permute-start(f32[40,256]{1,0:T(8,128)S(1)} %get-tuple-element.97), channel_id=1, source_target_pairs={{0,2},{1,3},{2,0},{3,1},{4,6},{5,7},{6,4},{7,5},{8,10},{9,11},{10,... | collective-permute-start | bytes 122888 | tf_op jit(solution)/shard_map/ppermute | solution.py:511
  17.3 0.3 collective-permute-start.2
  17.7 2.2 %collective-permute-done.1.refs_2_ = f32[40,256]{1,0:T(8,128)S(1)} collective-permute-done((f32[40,256]{1,0:T(8,128)S(1)}, f32[40,256]{1,0:T(8,128)S(1)}, u32[]{:S(2)}, u32[]{:S(2)}) %collective-permute-start.1) | collective-permute-done | bytes 40992 | tf_op jit(solution)/shard_map/ppermute | solution.py:511
  19.9 1.0 collective-permute-done.2.refs_3_
  20.9 1.5 %collective-permute-start.3 = (bf16[11,16,1024]{2,1,0:T(8,128)(2,1)}, bf16[11,16,1024]{2,1,0:T(8,128)(2,1)S(1)}, u32[]{:S(2)}, u32[]{:S(2)}) collective-permute-start(bf16[11,16,1024]{2,1,0:T(8,128)(2,1)} %get-tuple-element.106), channel_id=1, source_target_pairs={{0,24},{4,28},{8,16},{12,20},{16,8},{20,12},{24,0},{28,4},{1,25},{... | collective-permute-start | bytes 1081352 | tf_op jit(solution)/shard_map/ppermute | solution.py:511
  22.3 1.5 %collective-permute-start.4 = (bf16[11,16,1024]{2,1,0:T(8,128)(2,1)}, bf16[11,16,1024]{2,1,0:T(8,128)(2,1)S(1)}, u32[]{:S(2)}, u32[]{:S(2)}) collective-permute-start(bf16[11,16,1024]{2,1,0:T(8,128)(2,1)} %get-tuple-element.107), channel_id=1, source_target_pairs={{0,4},{4,0},{8,12},{12,8},{16,20},{20,16},{24,28},{28,24},{1,5},{5... | collective-permute-start | bytes 1081352 | tf_op jit(solution)/shard_map/ppermute | solution.py:511
  23.8 0.7 copy-done.8
  24.5 19.6 %all_to_all.25.part_ref = bf16[8,48,256]{2,1,0:T(8,128)(2,1)S(1)} all-to-all(bf16[8,48,256]{2,1,0:T(8,128)(2,1)S(1)} %shard_map.139), channel_id=1, replica_groups=mesh['wide'=8,'narrow'=4] {'wide'}, dimensions={0} | all-to-all | bytes 393216 | tf_op jit(solution)/shard_map/all_to_all | solution.py:580
  44.1 5.4 %all-to-all-start.2 = ((bf16[40,16,1024]{2,1,0:T(8,128)(2,1)}), bf16[40,16,1024]{2,1,0:T(8,128)(2,1)S(1)}, u32[]{:S(2)}, u32[]{:S(2)}) async-start(bf16[40,16,1024]{2,1,0:T(8,128)(2,1)} %get-tuple-element.125), calls=%async_computation.2 | async-start | bytes 2621440 | tf_op jit(solution)/shard_map/all_to_all | solution.py:537
  49.5 1.4 shard_map.140
  50.9 1.0 collective-permute-start.6
  51.9 0.8 collective-permute-start.7
  52.8 1.4 %shard_map.141.refs_1_ = bf16[128,16,1024]{2,1,0:T(8,128)(2,1)} custom-call(s32[2]{0:T(128)S(1)} %pad_add_fusion.1.place_ref, bf16[11,16,1024]{2,1,0:T(8,128)(2,1)S(1)} %collective-permute-done.4.refs_0_, bf16[11,16,1024]{2,1,0:T(8,128)(2,1)S(1)} %collective-permute-done.3.refs_1_, ...), custom_call_target="tpu_custom_call", output_to_operand_aliasing={{}: (3, {})} | custom-call | bytes 1441792 | tf_op jit(solution)/shard_map/pallas_call | solution.py:156
  54.3 1.9 %collective-permute-done.6.refs_2_ = bf16[8,40,128]{2,1,0:T(8,128)(2,1)S(1)} collective-permute-done((bf16[8,40,128]{2,1,0:T(8,128)(2,1)S(1)}, bf16[8,40,128]{2,1,0:T(8,128)(2,1)S(1)}, u32[]{:S(2)}, u32[]{:S(2)}) %collective-permute-start.6) | collective-permute-done | bytes 81952 | tf_op jit(solution)/shard_map/ppermute | solution.py:511
  56.2 0.8 collective-permute-done.7.refs_3_
  57.0 0.6 copy-done.12
  57.6 10.3 %shard_map.142 = (bf16[8,64,128]{2,1,0:T(8,128)(2,1)}, bf16[8,64,128]{2,1,0:T(8,128)(2,1)}, bf16[8,64,128]{2,1,0:T(8,128)(2,1)}, bf16[8,64,128]{2,1,0:T(8,128)(2,1)}) custom-call(s32[2]{0:T(128)} %pad_add_fusion.me_ref, s32[8]{0:T(128)} %length_ref.1, bf16[8,40,128]{2,1,0:T(8,128)(2,1)} %copy-done.5, bf16[8,40,128]{2,1,0:T(8,128)(2,1)} %copy-done.10, ...), custom_call_target="tpu_custom_call" | custom-call | flops 1 | bytes 1 | tf_op jit(solution)/shard_map/pallas_call | solution.py:298
  67.9 1.2 collective-permute-start.10
  69.1 1.1 collective-permute-start.9
  70.2 3.1 %collective-permute-done.10.refs_3_ = bf16[8,64,128]{2,1,0:T(8,128)(2,1)S(1)} collective-permute-done((bf16[8,64,128]{2,1,0:T(8,128)(2,1)}, bf16[8,64,128]{2,1,0:T(8,128)(2,1)S(1)}, u32[]{:S(2)}, u32[]{:S(2)}) %collective-permute-start.10) | collective-permute-done | bytes 131104 | tf_op jit(solution)/shard_map/ppermute | solution.py:511
  73.3 3.5 %collective-permute-done.9.refs_2_ = bf16[8,64,128]{2,1,0:T(8,128)(2,1)S(1)} collective-permute-done((bf16[8,64,128]{2,1,0:T(8,128)(2,1)}, bf16[8,64,128]{2,1,0:T(8,128)(2,1)S(1)}, u32[]{:S(2)}, u32[]{:S(2)}) %collective-permute-start.9) | collective-permute-done | bytes 131104 | tf_op jit(solution)/shard_map/ppermute | solution.py:511
  76.8 0.3 all-to-all-done.2.refs_0_
  77.1 3.9 %collective-permute-start.11 = (bf16[11,16,1024]{2,1,0:T(8,128)(2,1)S(1)}, bf16[11,16,1024]{2,1,0:T(8,128)(2,1)S(1)}, u32[]{:S(2)}, u32[]{:S(2)}) collective-permute-start(bf16[11,16,1024]{2,1,0:T(8,128)(2,1)S(1)} %copy-done.15), channel_id=1, source_target_pairs={{0,12},{4,8},{8,4},{12,0},{16,28},{20,24},{24,20},{28,16},{1,13},{... | collective-permute-start | bytes 1081352 | tf_op jit(solution)/shard_map/ppermute | solution.py:511
  81.0 0.9 copy-done.4
  81.9 1.1 shard_map.143
  83.0 5.9 %all-to-all-start.3 = ((bf16[8,64,128]{2,1,0:T(8,128)(2,1)}), bf16[8,64,128]{2,1,0:T(8,128)(2,1)S(1)}, u32[]{:S(2)}, u32[]{:S(2)}) async-start(bf16[8,64,128]{2,1,0:T(8,128)(2,1)} %shard_map.143), calls=%async_computation.3 | async-start | bytes 262144 | tf_op jit(solution)/shard_map/all_to_all | solution.py:643
  88.9 1.7 %shard_map.144.refs_2_ = bf16[128,16,1024]{2,1,0:T(8,128)(2,1)} custom-call(s32[8]{0:T(128)S(1)} %iota_multiply_fusion.place_ref, bf16[40,16,1024]{2,1,0:T(8,128)(2,1)S(1)} %all-to-all-done.2.refs_0_, bf16[128,16,1024]{2,1,0:T(8,128)(2,1)} %shard_map.141.refs_1_), custom_call_target="tpu_custom_call", output_to_operand_aliasing={{}: (2, {})} | custom-call | bytes 2621440 | tf_op jit(solution)/shard_map/pallas_call | solution.py:156
  90.6 9.7 %all-to-all-done.3.refs_0_ = bf16[8,64,128]{2,1,0:T(8,128)(2,1)S(1)} async-done(((bf16[8,64,128]{2,1,0:T(8,128)(2,1)}), bf16[8,64,128]{2,1,0:T(8,128)(2,1)S(1)}, u32[]{:S(2)}, u32[]{:S(2)}) %all-to-all-start.3) | async-done | bytes 131104 | tf_op jit(solution)/shard_map/all_to_all | solution.py:643
  100.2 1.7 %collective-permute-start.13 = (bf16[11,16,1024]{2,1,0:T(8,128)(2,1)}, bf16[11,16,1024]{2,1,0:T(8,128)(2,1)S(1)}, u32[]{:S(2)}, u32[]{:S(2)}) collective-permute-start(bf16[11,16,1024]{2,1,0:T(8,128)(2,1)} %get-tuple-element.149), channel_id=1, source_target_pairs={{0,8},{4,12},{8,0},{12,4},{16,24},{20,28},{24,16},{28,20},{1,9},{5... | collective-permute-start | bytes 1081352 | tf_op jit(solution)/shard_map/ppermute | solution.py:511
  101.9 1.2 collective-permute-start.14
  103.1 0.9 shard_map.145
  104.0 5.4 %all-to-all-start.4 = ((bf16[8,40,128]{2,1,0:T(8,128)(2,1)}), bf16[8,40,128]{2,1,0:T(8,128)(2,1)S(1)}, u32[]{:S(2)}, u32[]{:S(2)}) async-start(bf16[8,40,128]{2,1,0:T(8,128)(2,1)} %shard_map.145), calls=%async_computation.4 | async-start | bytes 163840 | tf_op jit(solution)/shard_map/all_to_all | solution.py:648
  109.4 1.4 %shard_map.146.refs_2_ = bf16[128,16,1024]{2,1,0:T(8,128)(2,1)} custom-call(s32[2]{0:T(128)S(1)} %pad_add_fusion.2.place_ref, bf16[11,16,1024]{2,1,0:T(8,128)(2,1)S(1)} %collective-permute-done.11.refs_0_, bf16[11,16,1024]{2,1,0:T(8,128)(2,1)S(1)} %collective-permute-done.12.refs_1_, ...), custom_call_target="tpu_custom_call", output_to_operand_aliasing={{}: (3, {})} | custom-call | bytes 1441792 | tf_op jit(solution)/shard_map/pallas_call | solution.py:156
  110.8 11.2 %all-to-all-done.4.part_ref = bf16[8,40,128]{2,1,0:T(8,128)(2,1)S(1)} async-done(((bf16[8,40,128]{2,1,0:T(8,128)(2,1)}), bf16[8,40,128]{2,1,0:T(8,128)(2,1)S(1)}, u32[]{:S(2)}, u32[]{:S(2)}) %all-to-all-start.4) | async-done | bytes 81952 | tf_op jit(solution)/shard_map/all_to_all | solution.py:648
  122.1 0.6 collective-permute-start.18
  122.6 0.9 shard_map.147
  123.6 1.6 %collective-permute-start.16 = (f32[10,512]{1,0:T(8,128)S(1)}, f32[10,512]{1,0:T(8,128)S(1)}, u32[]{:S(2)}, u32[]{:S(2)}) collective-permute-start(f32[10,512]{1,0:T(8,128)S(1)} %get-tuple-element.165), channel_id=1, source_target_pairs={{0,2},{1,3},{2,0},{3,1},{4,6},{5,7},{6,4},{7,5},{8,10},{9,11},{10,... | collective-permute-start | bytes 61448 | tf_op jit(solution)/shard_map/ppermute | solution.py:511
  125.6 1.4 %shard_map.148.refs_1_ = bf16[128,16,1024]{2,1,0:T(8,128)(2,1)} custom-call(s32[2]{0:T(128)S(1)} %pad_add_fusion.3.place_ref, bf16[11,16,1024]{2,1,0:T(8,128)(2,1)S(1)} %collective-permute-done.13.refs_0_, bf16[11,16,1024]{2,1,0:T(8,128)(2,1)S(1)} %collective-permute-done.14.refs_1_, ...), custom_call_target="tpu_custom_call", output_to_operand_aliasing={{}: (3, {})} | custom-call | bytes 1441792 | tf_op jit(solution)/shard_map/pallas_call | solution.py:156
  127.0 0.6 collective-permute-done.16
  127.6 1.0 collective-permute-done.17
  128.6 10.7 %collective-permute-done.18.refs_0_ = bf16[11,16,1024]{2,1,0:T(8,128)(2,1)S(1)} collective-permute-done((bf16[11,16,1024]{2,1,0:T(8,128)(2,1)S(1)}, bf16[11,16,1024]{2,1,0:T(8,128)(2,1)S(1)}, u32[]{:S(2)}, u32[]{:S(2)}) %collective-permute-start.18) | collective-permute-done | bytes 360480 | tf_op jit(solution)/shard_map/ppermute | solution.py:511
  139.3 0.6 add_convert_fusion
  139.9 0.7 shard_map.149
  (51 shorter events, 0.7 us)
Async XLA Ops:
  0.6 14.1 %copy-start.1 = (bf16[1024,512]{1,0:T(8,128)(2,1)S(1)}, bf16[1024,512]{1,0:T(8,128)(2,1)}, u32[]{:S(2)}) copy-start(bf16[1024,512]{1,0:T(8,128)(2,1)} %query_ref.1) | copy-start | bytes 3145732
  0.6 14.1 %copy-start.3 = (bf16[1024,128]{1,0:T(8,128)(2,1)S(1)}, bf16[1024,128]{1,0:T(8,128)(2,1)}, u32[]{:S(2)}) copy-start(bf16[1024,128]{1,0:T(8,128)(2,1)} %keyval_ref.1) | copy-start | bytes 786436
  2.1 12.6 %all-to-all-start = ((bf16[8,5,1024]{2,1,0:T(8,128)(2,1)}), bf16[8,5,1024]{2,1,0:T(8,128)(2,1)S(1)}, u32[]{:S(2)}, u32[]{:S(2)}) async-start(bf16[8,5,1024]{2,1,0:T(8,128)(2,1)} %broadcast_in_dim.2), calls=%async_computation | async-start | bytes 262144 | tf_op jit(solution)/shard_map/all_to_all | solution.py:484
  9.0 5.7 %copy-start.6 = (s32[2]{0:T(128)S(1)}, s32[2]{0:T(128)}, u32[]{:S(2)}) copy-start(s32[2]{0:T(128)} %pad_add_fusion.me_ref) | copy-start | bytes 28
  9.0 40.5 %copy-start.9 = (s32[8]{0:T(128)S(1)}, s32[8]{0:T(128)}, u32[]{:S(2)}) copy-start(s32[8]{0:T(128)} %kept_ref.1) | copy-start | bytes 100
  15.7 1.9 %collective-permute-start = (f32[40,256]{1,0:T(8,128)S(1)}, f32[40,256]{1,0:T(8,128)S(1)}, u32[]{:S(2)}, u32[]{:S(2)}) collective-permute-start(f32[40,256]{1,0:T(8,128)S(1)} %get-tuple-element.96), channel_id=1, source_target_pairs={{0,1},{1,0},{2,3},{3,2},{4,5},{5,4},{6,7},{7,6},{8,9},{9,8},{10,11... | collective-permute-start | bytes 122888 | tf_op jit(solution)/shard_map/ppermute | solution.py:511
  15.8 4.1 %collective-permute-start.1 = (f32[40,256]{1,0:T(8,128)S(1)}, f32[40,256]{1,0:T(8,128)S(1)}, u32[]{:S(2)}, u32[]{:S(2)}) collective-permute-start(f32[40,256]{1,0:T(8,128)S(1)} %get-tuple-element.97), channel_id=1, source_target_pairs={{0,2},{1,3},{2,0},{3,1},{4,6},{5,7},{6,4},{7,5},{8,10},{9,11},{10,... | collective-permute-start | bytes 122888 | tf_op jit(solution)/shard_map/ppermute | solution.py:511
  17.3 3.5 %collective-permute-start.2 = (f32[40,256]{1,0:T(8,128)S(1)}, f32[40,256]{1,0:T(8,128)S(1)}, u32[]{:S(2)}, u32[]{:S(2)}) collective-permute-start(f32[40,256]{1,0:T(8,128)S(1)} %get-tuple-element.98), channel_id=1, source_target_pairs={{0,3},{1,2},{2,1},{3,0},{4,7},{5,6},{6,5},{7,4},{8,11},{9,10},{10,... | collective-permute-start | bytes 122888 | tf_op jit(solution)/shard_map/ppermute | solution.py:511
  20.9 23.3 %collective-permute-start.3 = (bf16[11,16,1024]{2,1,0:T(8,128)(2,1)}, bf16[11,16,1024]{2,1,0:T(8,128)(2,1)S(1)}, u32[]{:S(2)}, u32[]{:S(2)}) collective-permute-start(bf16[11,16,1024]{2,1,0:T(8,128)(2,1)} %get-tuple-element.106), channel_id=1, source_target_pairs={{0,24},{4,28},{8,16},{12,20},{16,8},{20,12},{24,0},{28,4},{1,25},{... | collective-permute-start | bytes 1081352 | tf_op jit(solution)/shard_map/ppermute | solution.py:511
  22.3 21.8 %collective-permute-start.4 = (bf16[11,16,1024]{2,1,0:T(8,128)(2,1)}, bf16[11,16,1024]{2,1,0:T(8,128)(2,1)S(1)}, u32[]{:S(2)}, u32[]{:S(2)}) collective-permute-start(bf16[11,16,1024]{2,1,0:T(8,128)(2,1)} %get-tuple-element.107), channel_id=1, source_target_pairs={{0,4},{4,0},{8,12},{12,8},{16,20},{20,16},{24,28},{28,24},{1,5},{5... | collective-permute-start | bytes 1081352 | tf_op jit(solution)/shard_map/ppermute | solution.py:511
  23.8 0.7 copy-start.8
  44.1 32.9 %all-to-all-start.2 = ((bf16[40,16,1024]{2,1,0:T(8,128)(2,1)}), bf16[40,16,1024]{2,1,0:T(8,128)(2,1)S(1)}, u32[]{:S(2)}, u32[]{:S(2)}) async-start(bf16[40,16,1024]{2,1,0:T(8,128)(2,1)} %get-tuple-element.125), calls=%async_computation.2 | async-start | bytes 2621440 | tf_op jit(solution)/shard_map/all_to_all | solution.py:537
  50.9 3.4 %copy-start = (bf16[128,1024]{1,0:T(8,128)(2,1)}, bf16[128,1024]{1,0:T(8,128)(2,1)S(1)}, u32[]{:S(2)}) copy-start(bf16[128,1024]{1,0:T(8,128)(2,1)S(1)} %get-tuple-element.119.refs_6_.refs_7_) | copy-start | bytes 786436
  50.9 3.4 %copy-start.5 = (bf16[8,40,128]{2,1,0:T(8,128)(2,1)}, bf16[8,40,128]{2,1,0:T(8,128)(2,1)S(1)}, u32[]{:S(2)}) copy-start(bf16[8,40,128]{2,1,0:T(8,128)(2,1)S(1)} %get-tuple-element.115.refs_0_) | copy-start | bytes 245764
  50.9 3.4 %collective-permute-start.5 = (bf16[8,40,128]{2,1,0:T(8,128)(2,1)S(1)}, bf16[8,40,128]{2,1,0:T(8,128)(2,1)S(1)}, u32[]{:S(2)}, u32[]{:S(2)}) collective-permute-start(bf16[8,40,128]{2,1,0:T(8,128)(2,1)S(1)} %get-tuple-element.115.refs_0_), channel_id=1, source_target_pairs={{0,1},{1,0},{2,3},{3,2},{4,5},{5,4},{6,7},{7,6},{8,9},{9,8},{10,11... | collective-permute-start | bytes 245768 | tf_op jit(solution)/shard_map/ppermute | solution.py:511
  50.9 5.3 %collective-permute-start.6 = (bf16[8,40,128]{2,1,0:T(8,128)(2,1)S(1)}, bf16[8,40,128]{2,1,0:T(8,128)(2,1)S(1)}, u32[]{:S(2)}, u32[]{:S(2)}) collective-permute-start(bf16[8,40,128]{2,1,0:T(8,128)(2,1)S(1)} %get-tuple-element.115.refs_0_), channel_id=1, source_target_pairs={{0,2},{1,3},{2,0},{3,1},{4,6},{5,7},{6,4},{7,5},{8,10},{9,11},{10,... | collective-permute-start | bytes 245768 | tf_op jit(solution)/shard_map/ppermute | solution.py:511
  51.9 5.1 %collective-permute-start.7 = (bf16[8,40,128]{2,1,0:T(8,128)(2,1)S(1)}, bf16[8,40,128]{2,1,0:T(8,128)(2,1)S(1)}, u32[]{:S(2)}, u32[]{:S(2)}) collective-permute-start(bf16[8,40,128]{2,1,0:T(8,128)(2,1)S(1)} %get-tuple-element.115.refs_0_), channel_id=1, source_target_pairs={{0,3},{1,2},{2,1},{3,0},{4,7},{5,6},{6,5},{7,4},{8,11},{9,10},{10,... | collective-permute-start | bytes 245768 | tf_op jit(solution)/shard_map/ppermute | solution.py:511
  54.3 2.8 %copy-start.10 = (bf16[8,40,128]{2,1,0:T(8,128)(2,1)}, bf16[8,40,128]{2,1,0:T(8,128)(2,1)S(1)}, u32[]{:S(2)}) copy-start(bf16[8,40,128]{2,1,0:T(8,128)(2,1)S(1)} %collective-permute-done.5.refs_1_) | copy-start | bytes 245764
  56.2 0.8 copy-start.11
  57.0 0.6 copy-start.12
  57.6 19.4 %copy-start.15 = (bf16[11,16,1024]{2,1,0:T(8,128)(2,1)S(1)}, bf16[11,16,1024]{2,1,0:T(8,128)(2,1)}, u32[]{:S(2)}) copy-start(bf16[11,16,1024]{2,1,0:T(8,128)(2,1)} %get-tuple-element.138) | copy-start | bytes 1081348
  57.6 23.3 %copy-start.14 = (bf16[11,16,1024]{2,1,0:T(8,128)(2,1)S(1)}, bf16[11,16,1024]{2,1,0:T(8,128)(2,1)}, u32[]{:S(2)}) copy-start(bf16[11,16,1024]{2,1,0:T(8,128)(2,1)} %get-tuple-element.139) | copy-start | bytes 1081348
  67.9 5.4 %collective-permute-start.10 = (bf16[8,64,128]{2,1,0:T(8,128)(2,1)}, bf16[8,64,128]{2,1,0:T(8,128)(2,1)S(1)}, u32[]{:S(2)}, u32[]{:S(2)}) collective-permute-start(bf16[8,64,128]{2,1,0:T(8,128)(2,1)} %get-tuple-element.124), channel_id=1, source_target_pairs={{0,3},{1,2},{2,1},{3,0},{4,7},{5,6},{6,5},{7,4},{8,11},{9,10},{10,... | collective-permute-start | bytes 393224 | tf_op jit(solution)/shard_map/ppermute | solution.py:511
  69.1 4.2 %collective-permute-start.8 = (bf16[8,64,128]{2,1,0:T(8,128)(2,1)}, bf16[8,64,128]{2,1,0:T(8,128)(2,1)S(1)}, u32[]{:S(2)}, u32[]{:S(2)}) collective-permute-start(bf16[8,64,128]{2,1,0:T(8,128)(2,1)} %get-tuple-element.122), channel_id=1, source_target_pairs={{0,1},{1,0},{2,3},{3,2},{4,5},{5,4},{6,7},{7,6},{8,9},{9,8},{10,11... | collective-permute-start | bytes 393224 | tf_op jit(solution)/shard_map/ppermute | solution.py:511
  69.1 7.6 %collective-permute-start.9 = (bf16[8,64,128]{2,1,0:T(8,128)(2,1)}, bf16[8,64,128]{2,1,0:T(8,128)(2,1)S(1)}, u32[]{:S(2)}, u32[]{:S(2)}) collective-permute-start(bf16[8,64,128]{2,1,0:T(8,128)(2,1)} %get-tuple-element.123), channel_id=1, source_target_pairs={{0,2},{1,3},{2,0},{3,1},{4,6},{5,7},{6,4},{7,5},{8,10},{9,11},{10,... | collective-permute-start | bytes 393224 | tf_op jit(solution)/shard_map/ppermute | solution.py:511
  77.1 23.2 %collective-permute-start.11 = (bf16[11,16,1024]{2,1,0:T(8,128)(2,1)S(1)}, bf16[11,16,1024]{2,1,0:T(8,128)(2,1)S(1)}, u32[]{:S(2)}, u32[]{:S(2)}) collective-permute-start(bf16[11,16,1024]{2,1,0:T(8,128)(2,1)S(1)} %copy-done.15), channel_id=1, source_target_pairs={{0,12},{4,8},{8,4},{12,0},{16,28},{20,24},{24,20},{28,16},{1,13},{... | collective-permute-start | bytes 1081352 | tf_op jit(solution)/shard_map/ppermute | solution.py:511
  81.0 19.3 %collective-permute-start.12 = (bf16[11,16,1024]{2,1,0:T(8,128)(2,1)S(1)}, bf16[11,16,1024]{2,1,0:T(8,128)(2,1)S(1)}, u32[]{:S(2)}, u32[]{:S(2)}) collective-permute-start(bf16[11,16,1024]{2,1,0:T(8,128)(2,1)S(1)} %copy-done.14), channel_id=1, source_target_pairs={{0,16},{4,20},{8,24},{12,28},{16,0},{20,4},{24,8},{28,12},{1,17},{... | collective-permute-start | bytes 1081352 | tf_op jit(solution)/shard_map/ppermute | solution.py:511
  81.0 0.9 copy-start.4
  83.0 17.2 %all-to-all-start.3 = ((bf16[8,64,128]{2,1,0:T(8,128)(2,1)}), bf16[8,64,128]{2,1,0:T(8,128)(2,1)S(1)}, u32[]{:S(2)}, u32[]{:S(2)}) async-start(bf16[8,64,128]{2,1,0:T(8,128)(2,1)} %shard_map.143), calls=%async_computation.3 | async-start | bytes 262144 | tf_op jit(solution)/shard_map/all_to_all | solution.py:643
  100.2 21.8 %collective-permute-start.13 = (bf16[11,16,1024]{2,1,0:T(8,128)(2,1)}, bf16[11,16,1024]{2,1,0:T(8,128)(2,1)S(1)}, u32[]{:S(2)}, u32[]{:S(2)}) collective-permute-start(bf16[11,16,1024]{2,1,0:T(8,128)(2,1)} %get-tuple-element.149), channel_id=1, source_target_pairs={{0,8},{4,12},{8,0},{12,4},{16,24},{20,28},{24,16},{28,20},{1,9},{5... | collective-permute-start | bytes 1081352 | tf_op jit(solution)/shard_map/ppermute | solution.py:511
  101.9 20.2 %collective-permute-start.14 = (bf16[11,16,1024]{2,1,0:T(8,128)(2,1)}, bf16[11,16,1024]{2,1,0:T(8,128)(2,1)S(1)}, u32[]{:S(2)}, u32[]{:S(2)}) collective-permute-start(bf16[11,16,1024]{2,1,0:T(8,128)(2,1)} %get-tuple-element.150), channel_id=1, source_target_pairs={{0,20},{4,16},{8,28},{12,24},{16,4},{20,0},{24,12},{28,8},{1,21},{... | collective-permute-start | bytes 1081352 | tf_op jit(solution)/shard_map/ppermute | solution.py:511
  104.0 18.1 %all-to-all-start.4 = ((bf16[8,40,128]{2,1,0:T(8,128)(2,1)}), bf16[8,40,128]{2,1,0:T(8,128)(2,1)S(1)}, u32[]{:S(2)}, u32[]{:S(2)}) async-start(bf16[8,40,128]{2,1,0:T(8,128)(2,1)} %shard_map.145), calls=%async_computation.4 | async-start | bytes 163840 | tf_op jit(solution)/shard_map/all_to_all | solution.py:648
  109.4 12.6 %copy-start.13 = (bf16[11,16,1024]{2,1,0:T(8,128)(2,1)S(1)}, bf16[11,16,1024]{2,1,0:T(8,128)(2,1)}, u32[]{:S(2)}) copy-start(bf16[11,16,1024]{2,1,0:T(8,128)(2,1)} %get-tuple-element.167) | copy-start | bytes 1081348
  109.4 13.2 %copy-start.2 = (bf16[1024,512]{1,0:T(8,128)(2,1)S(1)}, bf16[1024,512]{1,0:T(8,128)(2,1)}, u32[]{:S(2)}) copy-start(bf16[1024,512]{1,0:T(8,128)(2,1)} %weight_ref.1) | copy-start | bytes 3145732
  109.4 13.2 %copy-start.7 = (s32[2]{0:T(128)S(1)}, s32[2]{0:T(128)}, u32[]{:S(2)}) copy-start(s32[2]{0:T(128)} %pad_add_fusion.me_ref) | copy-start | bytes 28
  122.1 17.2 %collective-permute-start.18 = (bf16[11,16,1024]{2,1,0:T(8,128)(2,1)S(1)}, bf16[11,16,1024]{2,1,0:T(8,128)(2,1)S(1)}, u32[]{:S(2)}, u32[]{:S(2)}) collective-permute-start(bf16[11,16,1024]{2,1,0:T(8,128)(2,1)S(1)} %copy-done.13), channel_id=1, source_target_pairs={{0,28},{4,24},{8,20},{12,16},{16,12},{20,8},{24,4},{28,0},{1,29},{... | collective-permute-start | bytes 1081352 | tf_op jit(solution)/shard_map/ppermute | solution.py:511
  123.6 3.4 %collective-permute-start.15 = (f32[10,512]{1,0:T(8,128)S(1)}, f32[10,512]{1,0:T(8,128)S(1)}, u32[]{:S(2)}, u32[]{:S(2)}) collective-permute-start(f32[10,512]{1,0:T(8,128)S(1)} %get-tuple-element.164), channel_id=1, source_target_pairs={{0,1},{1,0},{2,3},{3,2},{4,5},{5,4},{6,7},{7,6},{8,9},{9,8},{10,11... | collective-permute-start | bytes 61448 | tf_op jit(solution)/shard_map/ppermute | solution.py:511
  123.6 4.0 %collective-permute-start.16 = (f32[10,512]{1,0:T(8,128)S(1)}, f32[10,512]{1,0:T(8,128)S(1)}, u32[]{:S(2)}, u32[]{:S(2)}) collective-permute-start(f32[10,512]{1,0:T(8,128)S(1)} %get-tuple-element.165), channel_id=1, source_target_pairs={{0,2},{1,3},{2,0},{3,1},{4,6},{5,7},{6,4},{7,5},{8,10},{9,11},{10,... | collective-permute-start | bytes 61448 | tf_op jit(solution)/shard_map/ppermute | solution.py:511
  125.2 3.3 %collective-permute-start.17 = (f32[10,512]{1,0:T(8,128)S(1)}, f32[10,512]{1,0:T(8,128)S(1)}, u32[]{:S(2)}, u32[]{:S(2)}) collective-permute-start(f32[10,512]{1,0:T(8,128)S(1)} %get-tuple-element.166), channel_id=1, source_target_pairs={{0,3},{1,2},{2,1},{3,0},{4,7},{5,6},{6,5},{7,4},{8,11},{9,10},{10,... | collective-permute-start | bytes 61448 | tf_op jit(solution)/shard_map/ppermute | solution.py:511

commit v19 on v18

--- a/solution.py
+++ b/solution.py
@@ -569,7 +569,7 @@
             w_keyval,
             scratch=[pltpu.VMEM((rows, narrow * HD), jnp.float32)],
         )
-        partial = launch(deal(partial, "narrow"), 6, 1)
+        partial = launch(deal(partial, "narrow"), 6)
         packed = in_vmem(
             functools.partial(pack_kernel, narrow),
             jax.ShapeDtypeStruct((wide, rows + wide, 2 * HD), jnp.bfloat16),
@@ -577,8 +577,8 @@
             *partial,
             tags,
         )
-        received = land(exchange(packed, "wide"), 6, 1)
-        received = launch(received, 0)
+        received = land(exchange(packed, "wide"), 6)
+        received = launch(received, 0, 1)
         queries, keyval, new_entries, moved_req, moved_idx = in_vmem(
             functools.partial(unpack_kernel, rows),
             [
@@ -601,14 +601,14 @@
         partial = jnp.concatenate(
             [query_part, jnp.broadcast_to(keyval_part[None], (narrow,) + keyval_part.shape)], axis=2
         )
-        partial = launch(exchange(partial, "narrow"), 6, 1)
+        partial = launch(exchange(partial, "narrow"), 6)
         projected = jnp.sum(partial, axis=0).astype(jnp.bfloat16)
         tags = tags[:, : 3 * capacity].astype(jnp.bfloat16)[:, None]
         tags = jnp.pad(tags, ((0, 0), (0, 7), (0, projected.shape[1] - tags.shape[2])))
         packed = jnp.broadcast_to(projected[None], (wide,) + projected.shape)
         packed = jnp.concatenate([packed, tags], axis=1)
-        received = land(exchange(packed, "wide"), 6, 1)
-        received = launch(received, 0)
+        received = land(exchange(packed, "wide"), 6)
+        received = launch(received, 0, 1)
         tags_in = received[:, rows]
         queries = received[:, :rows, :own_cols]
         queries = spread(queries, "narrow")
@@ -632,9 +632,9 @@
     queries, moved_pool = lax.optimization_barrier((queries, placed(moved_pool)))
     mixed = attend(both, lengths, queries, keyval, tokens, token_info, rows, piece)
     if direct:
-        mixed = land(deal(mixed, "narrow"), 0)
+        mixed = land(deal(mixed, "narrow"), 0, 1)
     else:
-        mixed = land(exchange(mixed[0], "narrow"), 0)
+        mixed = land(exchange(mixed[0], "narrow"), 0, 1)
         mixed = mixed.reshape((narrow, wide) + mixed.shape[1:])
         mixed = [mixed[i] for i in range(narrow)]
     mixed = combine(launch(mixed, 3, 4), piece)

time: 141 us -> 142 us (level)
  the two profiles are of different devices: /device:TPU:8 before, /device:TPU:16 now
where the time goes in v19:
time: 142 us; the launch traced here: 141 us
  waiting for transfers between devices  46.6 us (33%)
  starting transfers between devices  38.5 us (27%)
  Pallas kernels  27.4 us (19%)
  blocking collectives  22 us (15%)
  local copies, waits for them, and re-layouts  4.51 us (3%)
  other arithmetic  1.42 us (1%)
    ppermute x19, waiting for transfers between devices, send(): lax.ppermute(block, axis, [(i, i ^ d) for i in range(lax.axis_size(axis))])  24.5 us
    all_to_all x1, blocking collectives, on_device(): received = land(exchange(packed, 'wide'), 6)  22 us
    ppermute x19, starting transfers between devices, send(): lax.ppermute(block, axis, [(i, i ^ d) for i in range(lax.axis_size(axis))])  14.5 us
    all_to_all x1, waiting for transfers between devices, on_device(): mixed = land(exchange(mixed, 'wide'), 3, 4)  11.2 us
    all_to_all x1, waiting for transfers between devices, on_device(): attn = land(exchange(attn, 'wide'), 2, 5)  11 us
    pallas_call x1, Pallas kernels, attend(): pl.pallas_call(functools.partial(attend_kernel, rows, piece, peers), grid...  10.3 us
    all_to_all x1, starting transfers between devices, on_device(): mixed = land(exchange(mixed, 'wide'), 3, 4)  6.44 us
    all_to_all x1, starting transfers between devices, spread(): lax.all_to_all(jnp.broadcast_to(block[None], (count,) + block.shape), axi...  6.17 us
  transfers between devices with their start and end apart: 23, of which 11 were waited for; matrix products, arithmetic and copies ran while one was open for 1% of the time, Pallas kernels for 18%

profile of v19, /device:TPU:16, one launch (start us, length us, event | category | flops | bytes accessed | tf_op | source)
XLA Modules:
  0.0 141.2 jit_solution(12775578642459347889)
XLA Ops:
  0.7 1.5 %broadcast_in_dim.2 = bf16[8,5,1024]{2,1,0:T(8,128)(2,1)} broadcast(bf16[5,1024]{1,0:T(8,128)(2,1)} %param.10), dimensions={1,2} | broadcast | bytes 92160 | tf_op jit(solution)/shard_map/broadcast_in_dim | solution.py:485
  2.1 6.2 %all-to-all-start = ((bf16[8,5,1024]{2,1,0:T(8,128)(2,1)}), bf16[8,5,1024]{2,1,0:T(8,128)(2,1)S(1)}, u32[]{:S(2)}, u32[]{:S(2)}) async-start(bf16[8,5,1024]{2,1,0:T(8,128)(2,1)} %broadcast_in_dim.2), calls=%async_computation | async-start | bytes 262144 | tf_op jit(solution)/shard_map/all_to_all | solution.py:484
  8.3 0.7 pad_add_fusion.me_ref
  9.0 5.7 %shard_map.137 = (bf16[128,16,1024]{2,1,0:T(8,128)(2,1)}, f32[8,128]{1,0:T(8,128)}, f32[8,2048]{1,0:T(8,128)}, bf16[40,16,1024]{2,1,0:T(8,128)(2,1)}, bf16[11,16...) custom-call(s32[2]{0:T(128)} %pad_add_fusion.me_ref, ...), custom_call_target="tpu_custom_call" | custom-call | bytes 8388608 | tf_op jit(solution)/shard_map/pallas_call | solution.py:118
  14.7 1.0 shard_map.138
  15.8 1.6 %collective-permute-start.1 = (f32[40,256]{1,0:T(8,128)S(1)}, f32[40,256]{1,0:T(8,128)S(1)}, u32[]{:S(2)}, u32[]{:S(2)}) collective-permute-start(f32[40,256]{1,0:T(8,128)S(1)} %get-tuple-element.97), channel_id=1, source_target_pairs={{0,2},{1,3},{2,0},{3,1},{4,6},{5,7},{6,4},{7,5},{8,10},{9,11},{10,... | collective-permute-start | bytes 122888 | tf_op jit(solution)/shard_map/ppermute | solution.py:511
  17.6 2.2 %collective-permute-done.1.refs_2_ = f32[40,256]{1,0:T(8,128)S(1)} collective-permute-done((f32[40,256]{1,0:T(8,128)S(1)}, f32[40,256]{1,0:T(8,128)S(1)}, u32[]{:S(2)}, u32[]{:S(2)}) %collective-permute-start.1) | collective-permute-done | bytes 40992 | tf_op jit(solution)/shard_map/ppermute | solution.py:511
  19.8 1.0 collective-permute-done.2.refs_3_
  20.8 0.6 collective-permute-start.3
  21.4 0.7 copy-done.8
  22.1 22.0 %all_to_all.25.part_ref = bf16[8,48,256]{2,1,0:T(8,128)(2,1)S(1)} all-to-all(bf16[8,48,256]{2,1,0:T(8,128)(2,1)S(1)} %shard_map.139), channel_id=1, replica_groups=mesh['wide'=8,'narrow'=4] {'wide'}, dimensions={0} | all-to-all | bytes 393216 | tf_op jit(solution)/shard_map/all_to_all | solution.py:580
  44.1 5.4 %all-to-all-start.2 = ((bf16[40,16,1024]{2,1,0:T(8,128)(2,1)}), bf16[40,16,1024]{2,1,0:T(8,128)(2,1)S(1)}, u32[]{:S(2)}, u32[]{:S(2)}) async-start(bf16[40,16,1024]{2,1,0:T(8,128)(2,1)} %get-tuple-element.123), calls=%async_computation.2 | async-start | bytes 2621440 | tf_op jit(solution)/shard_map/all_to_all | solution.py:537
  49.5 1.5 %collective-permute-start.10 = (bf16[11,16,1024]{2,1,0:T(8,128)(2,1)}, bf16[11,16,1024]{2,1,0:T(8,128)(2,1)S(1)}, u32[]{:S(2)}, u32[]{:S(2)}) collective-permute-start(bf16[11,16,1024]{2,1,0:T(8,128)(2,1)} %get-tuple-element.124), channel_id=1, source_target_pairs={{0,4},{4,0},{8,12},{12,8},{16,20},{20,16},{24,28},{28,24},{1,5},{5... | collective-permute-start | bytes 1081352 | tf_op jit(solution)/shard_map/ppermute | solution.py:511
  50.9 1.4 shard_map.140
  52.3 0.7 copy-done
  53.0 1.0 collective-permute-start.5
  54.0 0.9 collective-permute-start.6
  54.8 0.7 shard_map.141.refs_2_
  55.6 2.6 %collective-permute-done.5.refs_2_ = bf16[8,40,128]{2,1,0:T(8,128)(2,1)S(1)} collective-permute-done((bf16[8,40,128]{2,1,0:T(8,128)(2,1)S(1)}, bf16[8,40,128]{2,1,0:T(8,128)(2,1)S(1)}, u32[]{:S(2)}, u32[]{:S(2)}) %collective-permute-start.5) | collective-permute-done | bytes 81952 | tf_op jit(solution)/shard_map/ppermute | solution.py:511
  58.2 1.0 collective-permute-done.6.refs_3_
  59.2 0.6 copy-done.12
  59.8 10.3 %shard_map.142 = (bf16[8,64,128]{2,1,0:T(8,128)(2,1)}, bf16[8,64,128]{2,1,0:T(8,128)(2,1)}, bf16[8,64,128]{2,1,0:T(8,128)(2,1)}, bf16[8,64,128]{2,1,0:T(8,128)(2,1)}) custom-call(s32[2]{0:T(128)} %pad_add_fusion.me_ref, s32[8]{0:T(128)} %length_ref.1, bf16[8,40,128]{2,1,0:T(8,128)(2,1)} %copy-done.5, bf16[8,40,128]{2,1,0:T(8,128)(2,1)} %copy-done.10, ...), custom_call_target="tpu_custom_call" | custom-call | flops 1 | bytes 1 | tf_op jit(solution)/shard_map/pallas_call | solution.py:298
  70.1 0.5 collective-permute-start.7
  70.7 1.0 collective-permute-start.8
  71.7 0.5 collective-permute-start.9
  72.1 5.1 %collective-permute-done.8.refs_2_ = bf16[8,64,128]{2,1,0:T(8,128)(2,1)S(1)} collective-permute-done((bf16[8,64,128]{2,1,0:T(8,128)(2,1)}, bf16[8,64,128]{2,1,0:T(8,128)(2,1)S(1)}, u32[]{:S(2)}, u32[]{:S(2)}) %collective-permute-start.8) | collective-permute-done | bytes 131104 | tf_op jit(solution)/shard_map/ppermute | solution.py:511
  77.2 1.1 collective-permute-done.9.refs_3_
  78.3 1.7 %collective-permute-start.11 = (bf16[11,16,1024]{2,1,0:T(8,128)(2,1)S(1)}, bf16[11,16,1024]{2,1,0:T(8,128)(2,1)S(1)}, u32[]{:S(2)}, u32[]{:S(2)}) collective-permute-start(bf16[11,16,1024]{2,1,0:T(8,128)(2,1)S(1)} %copy-done.14), channel_id=1, source_target_pairs={{0,12},{4,8},{8,4},{12,0},{16,28},{20,24},{24,20},{28,16},{1,13},{... | collective-permute-start | bytes 1081352 | tf_op jit(solution)/shard_map/ppermute | solution.py:511
  80.4 0.9 copy-done.4
  81.3 1.1 shard_map.143
  82.4 6.4 %all-to-all-start.3 = ((bf16[8,64,128]{2,1,0:T(8,128)(2,1)}), bf16[8,64,128]{2,1,0:T(8,128)(2,1)S(1)}, u32[]{:S(2)}, u32[]{:S(2)}) async-start(bf16[8,64,128]{2,1,0:T(8,128)(2,1)} %shard_map.143), calls=%async_computation.3 | async-start | bytes 262144 | tf_op jit(solution)/shard_map/all_to_all | solution.py:643
  88.9 1.8 %shard_map.144.refs_2_ = bf16[128,16,1024]{2,1,0:T(8,128)(2,1)} custom-call(s32[9]{0:T(128)S(1)} %stack.44.place_ref, bf16[40,16,1024]{2,1,0:T(8,128)(2,1)S(1)} %all-to-all-done.2.refs_0_, bf16[11,16,1024]{2,1,0:T(8,128)(2,1)S(1)} %collective-permute-done.10.refs_1_, bf16[128,16,1024]{2,1,0:T(8,128)(2,1)} %shard_map.141.refs_2_), custom_call_target="tpu_custom_call", output_to_operand_aliasing={{}: (3, {})} | custom-call | bytes 3342336 | tf_op jit(solution)/shard_map/pallas_call | solution.py:156
  90.7 11.2 %all-to-all-done.3.refs_0_ = bf16[8,64,128]{2,1,0:T(8,128)(2,1)S(1)} async-done(((bf16[8,64,128]{2,1,0:T(8,128)(2,1)}), bf16[8,64,128]{2,1,0:T(8,128)(2,1)S(1)}, u32[]{:S(2)}, u32[]{:S(2)}) %all-to-all-start.3) | async-done | bytes 131104 | tf_op jit(solution)/shard_map/all_to_all | solution.py:643
  101.9 1.1 collective-permute-start.13
  103.0 0.8 collective-permute-start.14
  103.7 0.9 shard_map.145
  104.6 6.0 %all-to-all-start.4 = ((bf16[8,40,128]{2,1,0:T(8,128)(2,1)}), bf16[8,40,128]{2,1,0:T(8,128)(2,1)S(1)}, u32[]{:S(2)}, u32[]{:S(2)}) async-start(bf16[8,40,128]{2,1,0:T(8,128)(2,1)} %shard_map.145), calls=%async_computation.4 | async-start | bytes 163840 | tf_op jit(solution)/shard_map/all_to_all | solution.py:648
  110.7 1.4 %shard_map.146.refs_2_ = bf16[128,16,1024]{2,1,0:T(8,128)(2,1)} custom-call(s32[2]{0:T(128)S(1)} %pad_add_fusion.1.place_ref, bf16[11,16,1024]{2,1,0:T(8,128)(2,1)S(1)} %collective-permute-done.11.refs_0_, bf16[11,16,1024]{2,1,0:T(8,128)(2,1)S(1)} %collective-permute-done.12.refs_1_, ...), custom_call_target="tpu_custom_call", output_to_operand_aliasing={{}: (3, {})} | custom-call | bytes 1441792 | tf_op jit(solution)/shard_map/pallas_call | solution.py:156
  112.1 11.0 %all-to-all-done.4.part_ref = bf16[8,40,128]{2,1,0:T(8,128)(2,1)S(1)} async-done(((bf16[8,40,128]{2,1,0:T(8,128)(2,1)}), bf16[8,40,128]{2,1,0:T(8,128)(2,1)S(1)}, u32[]{:S(2)}, u32[]{:S(2)}) %all-to-all-start.4) | async-done | bytes 81952 | tf_op jit(solution)/shard_map/all_to_all | solution.py:648
  123.2 0.9 collective-permute-start.18
  124.0 0.9 shard_map.147
  125.0 1.1 collective-permute-start.16
  126.1 0.8 collective-permute-start.17
  127.0 1.4 %shard_map.148.refs_1_ = bf16[128,16,1024]{2,1,0:T(8,128)(2,1)} custom-call(s32[2]{0:T(128)S(1)} %pad_add_fusion.2.place_ref, bf16[11,16,1024]{2,1,0:T(8,128)(2,1)S(1)} %collective-permute-done.13.refs_0_, bf16[11,16,1024]{2,1,0:T(8,128)(2,1)S(1)} %collective-permute-done.14.refs_1_, ...), custom_call_target="tpu_custom_call", output_to_operand_aliasing={{}: (3, {})} | custom-call | bytes 1441792 | tf_op jit(solution)/shard_map/pallas_call | solution.py:156
  128.4 0.6 collective-permute-done.16
  129.5 10.4 %collective-permute-done.18.refs_0_ = bf16[11,16,1024]{2,1,0:T(8,128)(2,1)S(1)} collective-permute-done((bf16[11,16,1024]{2,1,0:T(8,128)(2,1)}, bf16[11,16,1024]{2,1,0:T(8,128)(2,1)S(1)}, u32[]{:S(2)}, u32[]{:S(2)}) %collective-permute-start.18) | collective-permute-done | bytes 360480 | tf_op jit(solution)/shard_map/ppermute | solution.py:511
  139.9 0.6 add_convert_fusion
  140.5 0.7 shard_map.149
  (48 shorter events, 1.6 us)
Async XLA Ops:
  0.6 14.0 %copy-start.1 = (bf16[1024,512]{1,0:T(8,128)(2,1)S(1)}, bf16[1024,512]{1,0:T(8,128)(2,1)}, u32[]{:S(2)}) copy-start(bf16[1024,512]{1,0:T(8,128)(2,1)} %query_ref.1) | copy-start | bytes 3145732
  0.6 14.0 %copy-start.3 = (bf16[1024,128]{1,0:T(8,128)(2,1)S(1)}, bf16[1024,128]{1,0:T(8,128)(2,1)}, u32[]{:S(2)}) copy-start(bf16[1024,128]{1,0:T(8,128)(2,1)} %keyval_ref.1) | copy-start | bytes 786436
  2.1 12.5 %all-to-all-start = ((bf16[8,5,1024]{2,1,0:T(8,128)(2,1)}), bf16[8,5,1024]{2,1,0:T(8,128)(2,1)S(1)}, u32[]{:S(2)}, u32[]{:S(2)}) async-start(bf16[8,5,1024]{2,1,0:T(8,128)(2,1)} %broadcast_in_dim.2), calls=%async_computation | async-start | bytes 262144 | tf_op jit(solution)/shard_map/all_to_all | solution.py:484
  9.0 5.7 %copy-start.6 = (s32[2]{0:T(128)S(1)}, s32[2]{0:T(128)}, u32[]{:S(2)}) copy-start(s32[2]{0:T(128)} %pad_add_fusion.me_ref) | copy-start | bytes 28
  9.0 42.0 %copy-start.9 = (s32[8]{0:T(128)S(1)}, s32[8]{0:T(128)}, u32[]{:S(2)}) copy-start(s32[8]{0:T(128)} %kept_ref.1) | copy-start | bytes 100
  15.7 1.9 %collective-permute-start = (f32[40,256]{1,0:T(8,128)S(1)}, f32[40,256]{1,0:T(8,128)S(1)}, u32[]{:S(2)}, u32[]{:S(2)}) collective-permute-start(f32[40,256]{1,0:T(8,128)S(1)} %get-tuple-element.96), channel_id=1, source_target_pairs={{0,1},{1,0},{2,3},{3,2},{4,5},{5,4},{6,7},{7,6},{8,9},{9,8},{10,11... | collective-permute-start | bytes 122888 | tf_op jit(solution)/shard_map/ppermute | solution.py:511
  15.8 4.1 %collective-permute-start.1 = (f32[40,256]{1,0:T(8,128)S(1)}, f32[40,256]{1,0:T(8,128)S(1)}, u32[]{:S(2)}, u32[]{:S(2)}) collective-permute-start(f32[40,256]{1,0:T(8,128)S(1)} %get-tuple-element.97), channel_id=1, source_target_pairs={{0,2},{1,3},{2,0},{3,1},{4,6},{5,7},{6,4},{7,5},{8,10},{9,11},{10,... | collective-permute-start | bytes 122888 | tf_op jit(solution)/shard_map/ppermute | solution.py:511
  17.3 3.5 %collective-permute-start.2 = (f32[40,256]{1,0:T(8,128)S(1)}, f32[40,256]{1,0:T(8,128)S(1)}, u32[]{:S(2)}, u32[]{:S(2)}) collective-permute-start(f32[40,256]{1,0:T(8,128)S(1)} %get-tuple-element.98), channel_id=1, source_target_pairs={{0,3},{1,2},{2,1},{3,0},{4,7},{5,6},{6,5},{7,4},{8,11},{9,10},{10,... | collective-permute-start | bytes 122888 | tf_op jit(solution)/shard_map/ppermute | solution.py:511
  20.8 23.3 %collective-permute-start.3 = (bf16[11,16,1024]{2,1,0:T(8,128)(2,1)}, bf16[11,16,1024]{2,1,0:T(8,128)(2,1)S(1)}, u32[]{:S(2)}, u32[]{:S(2)}) collective-permute-start(bf16[11,16,1024]{2,1,0:T(8,128)(2,1)} %get-tuple-element.105), channel_id=1, source_target_pairs={{0,24},{4,28},{8,16},{12,20},{16,8},{20,12},{24,0},{28,4},{1,25},{... | collective-permute-start | bytes 1081352 | tf_op jit(solution)/shard_map/ppermute | solution.py:511
  21.4 0.7 copy-start.8
  44.1 34.2 %all-to-all-start.2 = ((bf16[40,16,1024]{2,1,0:T(8,128)(2,1)}), bf16[40,16,1024]{2,1,0:T(8,128)(2,1)S(1)}, u32[]{:S(2)}, u32[]{:S(2)}) async-start(bf16[40,16,1024]{2,1,0:T(8,128)(2,1)} %get-tuple-element.123), calls=%async_computation.2 | async-start | bytes 2621440 | tf_op jit(solution)/shard_map/all_to_all | solution.py:537
  49.5 28.8 %collective-permute-start.10 = (bf16[11,16,1024]{2,1,0:T(8,128)(2,1)}, bf16[11,16,1024]{2,1,0:T(8,128)(2,1)S(1)}, u32[]{:S(2)}, u32[]{:S(2)}) collective-permute-start(bf16[11,16,1024]{2,1,0:T(8,128)(2,1)} %get-tuple-element.124), channel_id=1, source_target_pairs={{0,4},{4,0},{8,12},{12,8},{16,20},{20,16},{24,28},{28,24},{1,5},{5... | collective-permute-start | bytes 1081352 | tf_op jit(solution)/shard_map/ppermute | solution.py:511
  52.3 0.7 copy-start
  53.0 2.6 %copy-start.5 = (bf16[8,40,128]{2,1,0:T(8,128)(2,1)}, bf16[8,40,128]{2,1,0:T(8,128)(2,1)S(1)}, u32[]{:S(2)}) copy-start(bf16[8,40,128]{2,1,0:T(8,128)(2,1)S(1)} %get-tuple-element.113.refs_0_) | copy-start | bytes 245764
  53.0 2.6 %collective-permute-start.4 = (bf16[8,40,128]{2,1,0:T(8,128)(2,1)S(1)}, bf16[8,40,128]{2,1,0:T(8,128)(2,1)S(1)}, u32[]{:S(2)}, u32[]{:S(2)}) collective-permute-start(bf16[8,40,128]{2,1,0:T(8,128)(2,1)S(1)} %get-tuple-element.113.refs_0_), channel_id=1, source_target_pairs={{0,1},{1,0},{2,3},{3,2},{4,5},{5,4},{6,7},{7,6},{8,9},{9,8},{10,11... | collective-permute-start | bytes 245768 | tf_op jit(solution)/shard_map/ppermute | solution.py:511
  53.0 5.2 %collective-permute-start.5 = (bf16[8,40,128]{2,1,0:T(8,128)(2,1)S(1)}, bf16[8,40,128]{2,1,0:T(8,128)(2,1)S(1)}, u32[]{:S(2)}, u32[]{:S(2)}) collective-permute-start(bf16[8,40,128]{2,1,0:T(8,128)(2,1)S(1)} %get-tuple-element.113.refs_0_), channel_id=1, source_target_pairs={{0,2},{1,3},{2,0},{3,1},{4,6},{5,7},{6,4},{7,5},{8,10},{9,11},{10,... | collective-permute-start | bytes 245768 | tf_op jit(solution)/shard_map/ppermute | solution.py:511
  54.0 5.2 %collective-permute-start.6 = (bf16[8,40,128]{2,1,0:T(8,128)(2,1)S(1)}, bf16[8,40,128]{2,1,0:T(8,128)(2,1)S(1)}, u32[]{:S(2)}, u32[]{:S(2)}) collective-permute-start(bf16[8,40,128]{2,1,0:T(8,128)(2,1)S(1)} %get-tuple-element.113.refs_0_), channel_id=1, source_target_pairs={{0,3},{1,2},{2,1},{3,0},{4,7},{5,6},{6,5},{7,4},{8,11},{9,10},{10,... | collective-permute-start | bytes 245768 | tf_op jit(solution)/shard_map/ppermute | solution.py:511
  55.6 3.6 %copy-start.10 = (bf16[8,40,128]{2,1,0:T(8,128)(2,1)}, bf16[8,40,128]{2,1,0:T(8,128)(2,1)S(1)}, u32[]{:S(2)}) copy-start(bf16[8,40,128]{2,1,0:T(8,128)(2,1)S(1)} %collective-permute-done.4.refs_1_) | copy-start | bytes 245764
  58.2 1.0 copy-start.11
  59.2 0.6 copy-start.12
  59.8 18.5 %copy-start.14 = (bf16[11,16,1024]{2,1,0:T(8,128)(2,1)S(1)}, bf16[11,16,1024]{2,1,0:T(8,128)(2,1)}, u32[]{:S(2)}) copy-start(bf16[11,16,1024]{2,1,0:T(8,128)(2,1)} %get-tuple-element.137) | copy-start | bytes 1081348
  59.8 20.2 %copy-start.13 = (bf16[11,16,1024]{2,1,0:T(8,128)(2,1)S(1)}, bf16[11,16,1024]{2,1,0:T(8,128)(2,1)}, u32[]{:S(2)}) copy-start(bf16[11,16,1024]{2,1,0:T(8,128)(2,1)} %get-tuple-element.138) | copy-start | bytes 1081348
  70.1 2.0 %collective-permute-start.7 = (bf16[8,64,128]{2,1,0:T(8,128)(2,1)}, bf16[8,64,128]{2,1,0:T(8,128)(2,1)S(1)}, u32[]{:S(2)}, u32[]{:S(2)}) collective-permute-start(bf16[8,64,128]{2,1,0:T(8,128)(2,1)} %get-tuple-element.120), channel_id=1, source_target_pairs={{0,1},{1,0},{2,3},{3,2},{4,5},{5,4},{6,7},{7,6},{8,9},{9,8},{10,11... | collective-permute-start | bytes 393224 | tf_op jit(solution)/shard_map/ppermute | solution.py:511
  70.7 6.6 %collective-permute-start.8 = (bf16[8,64,128]{2,1,0:T(8,128)(2,1)}, bf16[8,64,128]{2,1,0:T(8,128)(2,1)S(1)}, u32[]{:S(2)}, u32[]{:S(2)}) collective-permute-start(bf16[8,64,128]{2,1,0:T(8,128)(2,1)} %get-tuple-element.121), channel_id=1, source_target_pairs={{0,2},{1,3},{2,0},{3,1},{4,6},{5,7},{6,4},{7,5},{8,10},{9,11},{10,... | collective-permute-start | bytes 393224 | tf_op jit(solution)/shard_map/ppermute | solution.py:511
  71.7 6.6 %collective-permute-start.9 = (bf16[8,64,128]{2,1,0:T(8,128)(2,1)}, bf16[8,64,128]{2,1,0:T(8,128)(2,1)S(1)}, u32[]{:S(2)}, u32[]{:S(2)}) collective-permute-start(bf16[8,64,128]{2,1,0:T(8,128)(2,1)} %get-tuple-element.122), channel_id=1, source_target_pairs={{0,3},{1,2},{2,1},{3,0},{4,7},{5,6},{6,5},{7,4},{8,11},{9,10},{10,... | collective-permute-start | bytes 393224 | tf_op jit(solution)/shard_map/ppermute | solution.py:511
  78.3 23.6 %collective-permute-start.11 = (bf16[11,16,1024]{2,1,0:T(8,128)(2,1)S(1)}, bf16[11,16,1024]{2,1,0:T(8,128)(2,1)S(1)}, u32[]{:S(2)}, u32[]{:S(2)}) collective-permute-start(bf16[11,16,1024]{2,1,0:T(8,128)(2,1)S(1)} %copy-done.14), channel_id=1, source_target_pairs={{0,12},{4,8},{8,4},{12,0},{16,28},{20,24},{24,20},{28,16},{1,13},{... | collective-permute-start | bytes 1081352 | tf_op jit(solution)/shard_map/ppermute | solution.py:511
  80.0 21.9 %collective-permute-start.12 = (bf16[11,16,1024]{2,1,0:T(8,128)(2,1)S(1)}, bf16[11,16,1024]{2,1,0:T(8,128)(2,1)S(1)}, u32[]{:S(2)}, u32[]{:S(2)}) collective-permute-start(bf16[11,16,1024]{2,1,0:T(8,128)(2,1)S(1)} %copy-done.13), channel_id=1, source_target_pairs={{0,16},{4,20},{8,24},{12,28},{16,0},{20,4},{24,8},{28,12},{1,17},{... | collective-permute-start | bytes 1081352 | tf_op jit(solution)/shard_map/ppermute | solution.py:511
  80.4 0.9 copy-start.4
  82.4 19.5 %all-to-all-start.3 = ((bf16[8,64,128]{2,1,0:T(8,128)(2,1)}), bf16[8,64,128]{2,1,0:T(8,128)(2,1)S(1)}, u32[]{:S(2)}, u32[]{:S(2)}) async-start(bf16[8,64,128]{2,1,0:T(8,128)(2,1)} %shard_map.143), calls=%async_computation.3 | async-start | bytes 262144 | tf_op jit(solution)/shard_map/all_to_all | solution.py:643
  101.9 21.2 %collective-permute-start.13 = (bf16[11,16,1024]{2,1,0:T(8,128)(2,1)}, bf16[11,16,1024]{2,1,0:T(8,128)(2,1)S(1)}, u32[]{:S(2)}, u32[]{:S(2)}) collective-permute-start(bf16[11,16,1024]{2,1,0:T(8,128)(2,1)} %get-tuple-element.149), channel_id=1, source_target_pairs={{0,8},{4,12},{8,0},{12,4},{16,24},{20,28},{24,16},{28,20},{1,9},{5... | collective-permute-start | bytes 1081352 | tf_op jit(solution)/shard_map/ppermute | solution.py:511
  103.0 20.2 %collective-permute-start.14 = (bf16[11,16,1024]{2,1,0:T(8,128)(2,1)}, bf16[11,16,1024]{2,1,0:T(8,128)(2,1)S(1)}, u32[]{:S(2)}, u32[]{:S(2)}) collective-permute-start(bf16[11,16,1024]{2,1,0:T(8,128)(2,1)} %get-tuple-element.150), channel_id=1, source_target_pairs={{0,20},{4,16},{8,28},{12,24},{16,4},{20,0},{24,12},{28,8},{1,21},{... | collective-permute-start | bytes 1081352 | tf_op jit(solution)/shard_map/ppermute | solution.py:511
  104.6 18.5 %all-to-all-start.4 = ((bf16[8,40,128]{2,1,0:T(8,128)(2,1)}), bf16[8,40,128]{2,1,0:T(8,128)(2,1)S(1)}, u32[]{:S(2)}, u32[]{:S(2)}) async-start(bf16[8,40,128]{2,1,0:T(8,128)(2,1)} %shard_map.145), calls=%async_computation.4 | async-start | bytes 163840 | tf_op jit(solution)/shard_map/all_to_all | solution.py:648
  110.7 13.3 %copy-start.2 = (bf16[1024,512]{1,0:T(8,128)(2,1)S(1)}, bf16[1024,512]{1,0:T(8,128)(2,1)}, u32[]{:S(2)}) copy-start(bf16[1024,512]{1,0:T(8,128)(2,1)} %weight_ref.1) | copy-start | bytes 3145732
  110.7 13.3 %copy-start.7 = (s32[2]{0:T(128)S(1)}, s32[2]{0:T(128)}, u32[]{:S(2)}) copy-start(s32[2]{0:T(128)} %pad_add_fusion.me_ref) | copy-start | bytes 28
  123.2 16.7 %collective-permute-start.18 = (bf16[11,16,1024]{2,1,0:T(8,128)(2,1)}, bf16[11,16,1024]{2,1,0:T(8,128)(2,1)S(1)}, u32[]{:S(2)}, u32[]{:S(2)}) collective-permute-start(bf16[11,16,1024]{2,1,0:T(8,128)(2,1)} %get-tuple-element.167), channel_id=1, source_target_pairs={{0,28},{4,24},{8,20},{12,16},{16,12},{20,8},{24,4},{28,0},{1,29},{... | collective-permute-start | bytes 1081352 | tf_op jit(solution)/shard_map/ppermute | solution.py:511
  125.0 3.4 %collective-permute-start.15 = (f32[10,512]{1,0:T(8,128)S(1)}, f32[10,512]{1,0:T(8,128)S(1)}, u32[]{:S(2)}, u32[]{:S(2)}) collective-permute-start(f32[10,512]{1,0:T(8,128)S(1)} %get-tuple-element.164), channel_id=1, source_target_pairs={{0,1},{1,0},{2,3},{3,2},{4,5},{5,4},{6,7},{7,6},{8,9},{9,8},{10,11... | collective-permute-start | bytes 61448 | tf_op jit(solution)/shard_map/ppermute | solution.py:511
  125.0 4.0 %collective-permute-start.16 = (f32[10,512]{1,0:T(8,128)S(1)}, f32[10,512]{1,0:T(8,128)S(1)}, u32[]{:S(2)}, u32[]{:S(2)}) collective-permute-start(f32[10,512]{1,0:T(8,128)S(1)} %get-tuple-element.165), channel_id=1, source_target_pairs={{0,2},{1,3},{2,0},{3,1},{4,6},{5,7},{6,4},{7,5},{8,10},{9,11},{10,... | collective-permute-start | bytes 61448 | tf_op jit(solution)/shard_map/ppermute | solution.py:511
  126.1 3.3 %collective-permute-start.17 = (f32[10,512]{1,0:T(8,128)S(1)}, f32[10,512]{1,0:T(8,128)S(1)}, u32[]{:S(2)}, u32[]{:S(2)}) collective-permute-start(f32[10,512]{1,0:T(8,128)S(1)} %get-tuple-element.166), channel_id=1, source_target_pairs={{0,3},{1,2},{2,1},{3,0},{4,7},{5,6},{6,5},{7,4},{8,11},{9,10},{10,... | collective-permute-start | bytes 61448 | tf_op jit(solution)/shard_map/ppermute | solution.py:511

commit v20 on v18

--- a/solution.py
+++ b/solution.py
@@ -19,6 +19,7 @@
 STAT = 16
 MIB = 1024 * 1024
 AHEAD = 5
+EARLY = 4
 NT = (((1,), (1,)), ((), ()))
 
 
@@ -56,11 +57,11 @@
 
     own = out_ref.at[pl.ds(me_ref[0] * capacity + ahead, rest)]
     blocks = [(wide * ahead, rest, own)]
-    for d, chunk in zip(parts, chunk_refs):
+    for (_, d, first, last), chunk in zip(parts, chunk_refs):
         if d:
-            blocks.append((wide * ahead + d * rest, rest, chunk))
+            blocks.append((wide * ahead + d * rest + first, last - first, chunk))
         else:
-            blocks.insert(0, (0, wide * ahead, chunk))
+            blocks.insert(0, (first, last - first, chunk))
     for c, (first, count, _) in enumerate(blocks):
 
         def start(j, carry, c=c):
@@ -111,8 +112,7 @@
     part = lambda count: jax.ShapeDtypeStruct((count,) + pool.shape[1:], pool.dtype)
     out_shape = [part(slots), jax.ShapeDtypeStruct((wide, slots), jnp.float32)]
     out_shape += [jax.ShapeDtypeStruct((8, slots * PAGE), jnp.float32)]
-    rest = slots // wide - ahead
-    out_shape += [part(rest if d else wide * ahead) for d in parts]
+    out_shape += [part(last - first) for _, _, first, last in parts]
     vmem = pl.BlockSpec(memory_space=pltpu.VMEM)
     hbm = pl.BlockSpec(memory_space=pltpu.HBM)
     return pl.pallas_call(
@@ -385,6 +385,11 @@
     return match.astype(jnp.bfloat16)
 
 
+def repeat_kernel(block_ref, out_ref):
+    for i in range(out_ref.shape[0]):
+        out_ref[i] = block_ref[...]
+
+
 def project_kernel(peers, me_ref, hidden_ref, query_ref, keyval_ref, *refs):
     out_refs, (full_ref,) = refs[:peers], refs[peers:]
     count, local, depth = hidden_ref.shape
@@ -516,30 +521,39 @@
     def deal(blocks, axis):
         return [blocks[0]] + [send(block, axis, d) for d, block in enumerate(blocks) if d]
 
-    gathered = spread(hidden, "wide")
+    copies = jax.ShapeDtypeStruct((wide,) + hidden.shape, hidden.dtype)
+    gathered = exchange(in_vmem(repeat_kernel, copies, None, hidden), "wide")
 
     ahead = AHEAD * capacity // 16
-    parts = list(range(0 if ahead else 1, wide))
+    rest = capacity - ahead
+    early = EARLY * rest // (16 - AHEAD)
+    parts = [(0, 0, 0, wide * ahead)] if ahead else []
+    for d in range(1, wide):
+        group = group_of(d, wide)
+        cut = early if group == 7 else 0
+        if cut:
+            parts.append((8, d, 0, cut))
+        parts.append((group, d, cut, rest))
     moved_pool, tags, token_info, *chunks = order_pages(
         both, moves, page_req, page_idx, pool, wide, ahead, parts
     )
-    chunks = dict(zip(parts, chunks))
     arrived = {}
     flying = {}
 
     def members(groups):
-        return [d for group in groups for d in parts if group_of(d, wide) == group]
+        return [c for group in groups for c, part in enumerate(parts) if part[0] == group]
 
     def launch(values, *groups):
         taken = members(groups)
-        values, sent = lax.optimization_barrier((values, [chunks[d] for d in taken]))
-        for d, chunk in zip(taken, sent):
-            flying[d] = send(chunk, "wide", d) if d else exchange(chunk, "wide")
+        values, sent = lax.optimization_barrier((values, [chunks[c] for c in taken]))
+        for c, chunk in zip(taken, sent):
+            d = parts[c][1]
+            flying[c] = send(chunk, "wide", d) if d else exchange(chunk, "wide")
         return values
 
     def land(values, *groups):
         taken = members(groups)
-        values, got = lax.optimization_barrier((values, [flying[d] for d in taken]))
+        values, got = lax.optimization_barrier((values, [flying[c] for c in taken]))
         arrived.update(zip(taken, got))
         return values
 
@@ -547,12 +561,13 @@
         taken = sorted(arrived)
         if not taken:
             return pages
-        place = []
-        for d in taken:
-            place += [(me ^ d) * capacity + ahead] if d else [w * capacity for w in range(wide)]
+        place, counts = [], []
+        for _, d, first, _ in [parts[c] for c in taken]:
+            own = [(me ^ d) * capacity + ahead + first]
+            place += own if d else [w * capacity for w in range(wide)]
+            counts.append(1 if d else wide)
         place = jnp.stack([jnp.asarray(index, jnp.int32) for index in place])
-        counts = [1 if d else wide for d in taken]
-        pages = place_pages(place, [arrived[d] for d in taken], counts, pages)
+        pages = place_pages(place, [arrived[c] for c in taken], counts, pages)
         arrived.clear()
         return pages
 
@@ -569,7 +584,8 @@
             w_keyval,
             scratch=[pltpu.VMEM((rows, narrow * HD), jnp.float32)],
         )
-        partial = launch(deal(partial, "narrow"), 6, 1)
+        partial = land(deal(launch(partial, 8), "narrow"), 8)
+        partial = launch(partial, 6, 1)
         packed = in_vmem(
             functools.partial(pack_kernel, narrow),
             jax.ShapeDtypeStruct((wide, rows + wide, 2 * HD), jnp.bfloat16),
@@ -601,7 +617,8 @@
         partial = jnp.concatenate(
             [query_part, jnp.broadcast_to(keyval_part[None], (narrow,) + keyval_part.shape)], axis=2
         )
-        partial = launch(exchange(partial, "narrow"), 6, 1)
+        partial = land(exchange(launch(partial, 8), "narrow"), 8)
+        partial = launch(partial, 6, 1)
         projected = jnp.sum(partial, axis=0).astype(jnp.bfloat16)
         tags = tags[:, : 3 * capacity].astype(jnp.bfloat16)[:, None]
         tags = jnp.pad(tags, ((0, 0), (0, 7), (0, projected.shape[1] - tags.shape[2])))

time: 141 us -> 137 us (0.972)
  the two profiles are of different devices: /device:TPU:8 before, /device:TPU:0 now
where the time goes in v20:
time: 137 us; the launch traced here: 136 us
  waiting for transfers between devices  42.4 us (31%)
  starting transfers between devices  41.4 us (30%)
  Pallas kernels  28.5 us (21%)
  blocking collectives  18 us (13%)
  local copies, waits for them, and re-layouts  3.07 us (2%)
  other arithmetic  1.4 us (1%)
    ppermute x20, starting transfers between devices, send(): lax.ppermute(block, axis, [(i, i ^ d) for i in range(lax.axis_size(axis))])  23.3 us
    all_to_all x1, blocking collectives, on_device(): received = land(exchange(packed, 'wide'), 6, 1)  18 us
    ppermute x20, waiting for transfers between devices, send(): lax.ppermute(block, axis, [(i, i ^ d) for i in range(lax.axis_size(axis))])  15 us
    all_to_all x1, waiting for transfers between devices, on_device(): attn = land(exchange(attn, 'wide'), 2, 5)  11.9 us
    all_to_all x1, waiting for transfers between devices, on_device(): mixed = land(exchange(mixed, 'wide'), 3, 4)  11.4 us
    pallas_call x1, Pallas kernels, attend(): pl.pallas_call(functools.partial(attend_kernel, rows, piece, peers), grid...  10.3 us
    all_to_all x1, starting transfers between devices, on_device(): gathered = exchange(in_vmem(repeat_kernel, copies, None, hidden), 'wide')  7.28 us
    pallas_call x5, Pallas kernels, place_pages(): pl.pallas_call(functools.partial(place_kernel, counts), out_shape=jax.Sha...  6.64 us
  transfers between devices with their start and end apart: 24, of which 13 were waited for; matrix products, arithmetic and copies ran while one was open for 1% of the time, Pallas kernels for 19%

profile of v20, /device:TPU:0, one launch (start us, length us, event | category | flops | bytes accessed | tf_op | source)
XLA Modules:
  0.0 135.6 jit_solution(13761646282356371475)
XLA Ops:
  0.7 0.8 copy-done.6
  1.5 0.7 shard_map.137
  2.1 7.3 %all-to-all-start = ((bf16[8,5,1024]{2,1,0:T(8,128)(2,1)}), bf16[8,5,1024]{2,1,0:T(8,128)(2,1)S(1)}, u32[]{:S(2)}, u32[]{:S(2)}) async-start(bf16[8,5,1024]{2,1,0:T(8,128)(2,1)} %shard_map.137), calls=%async_computation | async-start | bytes 262144 | tf_op jit(solution)/shard_map/all_to_all | solution.py:525
  9.4 0.6 pad_add_fusion.me_ref
  10.0 5.7 %shard_map.138 = (bf16[128,16,1024]{2,1,0:T(8,128)(2,1)}, f32[8,128]{1,0:T(8,128)}, f32[8,2048]{1,0:T(8,128)}, bf16[40,16,1024]{2,1,0:T(8,128)(2,1)}, bf16[11,16...) custom-call(s32[2]{0:T(128)} %pad_add_fusion.me_ref, ...), custom_call_target="tpu_custom_call" | custom-call | bytes 8388608 | tf_op jit(solution)/shard_map/pallas_call | solution.py:118
  15.6 1.1 all-to-all-done.hidden_ref
  16.8 1.0 shard_map.139
  17.8 3.7 %collective-permute-start.3 = (bf16[4,16,1024]{2,1,0:T(8,128)(2,1)}, bf16[4,16,1024]{2,1,0:T(8,128)(2,1)S(1)}, u32[]{:S(2)}, u32[]{:S(2)}) collective-permute-start(bf16[4,16,1024]{2,1,0:T(8,128)(2,1)} %get-tuple-element.115), channel_id=1, source_target_pairs={{0,28},{4,24},{8,20},{12,16},{16,12},{20,8},{24,4},{28,0},{1,29},{... | collective-permute-start | bytes 393224 | tf_op jit(solution)/shard_map/ppermute | solution.py:516
  21.5 1.5 %collective-permute-start.1 = (f32[40,256]{1,0:T(8,128)S(1)}, f32[40,256]{1,0:T(8,128)S(1)}, u32[]{:S(2)}, u32[]{:S(2)}) collective-permute-start(f32[40,256]{1,0:T(8,128)S(1)} %get-tuple-element.113), channel_id=1, source_target_pairs={{0,2},{1,3},{2,0},{3,1},{4,6},{5,7},{6,4},{7,5},{8,10},{9,11},{10,... | collective-permute-start | bytes 122888 | tf_op jit(solution)/shard_map/ppermute | solution.py:516
  23.3 2.1 %collective-permute-done.1.refs_2_ = f32[40,256]{1,0:T(8,128)S(1)} collective-permute-done((f32[40,256]{1,0:T(8,128)S(1)}, f32[40,256]{1,0:T(8,128)S(1)}, u32[]{:S(2)}, u32[]{:S(2)}) %collective-permute-start.1) | collective-permute-done | bytes 40992 | tf_op jit(solution)/shard_map/ppermute | solution.py:516
  25.5 1.0 collective-permute-done.2.refs_3_
  26.5 1.9 %collective-permute-start.4 = (bf16[11,16,1024]{2,1,0:T(8,128)(2,1)}, bf16[11,16,1024]{2,1,0:T(8,128)(2,1)S(1)}, u32[]{:S(2)}, u32[]{:S(2)}) collective-permute-start(bf16[11,16,1024]{2,1,0:T(8,128)(2,1)} %get-tuple-element.127), channel_id=1, source_target_pairs={{0,24},{4,28},{8,16},{12,20},{16,8},{20,12},{24,0},{28,4},{1,25},{... | collective-permute-start | bytes 1081352 | tf_op jit(solution)/shard_map/ppermute | solution.py:516
  28.4 1.5 %collective-permute-start.5 = (bf16[11,16,1024]{2,1,0:T(8,128)(2,1)}, bf16[11,16,1024]{2,1,0:T(8,128)(2,1)S(1)}, u32[]{:S(2)}, u32[]{:S(2)}) collective-permute-start(bf16[11,16,1024]{2,1,0:T(8,128)(2,1)} %get-tuple-element.128), channel_id=1, source_target_pairs={{0,4},{4,0},{8,12},{12,8},{16,20},{20,16},{24,28},{28,24},{1,5},{5... | collective-permute-start | bytes 1081352 | tf_op jit(solution)/shard_map/ppermute | solution.py:516
  29.9 0.7 copy-done.9
  30.6 18.0 %all_to_all.25.part_ref = bf16[8,48,256]{2,1,0:T(8,128)(2,1)S(1)} all-to-all(bf16[8,48,256]{2,1,0:T(8,128)(2,1)S(1)} %shard_map.140), channel_id=1, replica_groups=mesh['wide'=8,'narrow'=4] {'wide'}, dimensions={0} | all-to-all | bytes 393216 | tf_op jit(solution)/shard_map/all_to_all | solution.py:596
  48.6 3.6 %all-to-all-start.2 = ((bf16[40,16,1024]{2,1,0:T(8,128)(2,1)}), bf16[40,16,1024]{2,1,0:T(8,128)(2,1)S(1)}, u32[]{:S(2)}, u32[]{:S(2)}) async-start(bf16[40,16,1024]{2,1,0:T(8,128)(2,1)} %get-tuple-element.147), calls=%async_computation.2 | async-start | bytes 2621440 | tf_op jit(solution)/shard_map/all_to_all | solution.py:551
  52.2 1.4 shard_map.141
  53.5 1.6 %collective-permute-start.7 = (bf16[8,40,128]{2,1,0:T(8,128)(2,1)S(1)}, bf16[8,40,128]{2,1,0:T(8,128)(2,1)S(1)}, u32[]{:S(2)}, u32[]{:S(2)}) collective-permute-start(bf16[8,40,128]{2,1,0:T(8,128)(2,1)S(1)} %get-tuple-element.137.refs_0_), channel_id=1, source_target_pairs={{0,2},{1,3},{2,0},{3,1},{4,6},{5,7},{6,4},{7,5},{8,10},{9,11},{10,... | collective-permute-start | bytes 245768 | tf_op jit(solution)/shard_map/ppermute | solution.py:516
  55.5 1.5 %shard_map.142.refs_1_ = bf16[128,16,1024]{2,1,0:T(8,128)(2,1)} custom-call(s32[3]{0:T(128)S(1)} %pad_add_fusion.1.place_ref, bf16[11,16,1024]{2,1,0:T(8,128)(2,1)S(1)} %collective-permute-done.5.refs_0_, bf16[11,16,1024]{2,1,0:T(8,128)(2,1)S(1)} %collective-permute-done.4.refs_1_, ...), custom_call_target="tpu_custom_call", output_to_operand_aliasing={{}: (4, {})} | custom-call | bytes 1703936 | tf_op jit(solution)/shard_map/pallas_call | solution.py:156
  57.0 1.7 %collective-permute-done.7.refs_2_ = bf16[8,40,128]{2,1,0:T(8,128)(2,1)S(1)} collective-permute-done((bf16[8,40,128]{2,1,0:T(8,128)(2,1)S(1)}, bf16[8,40,128]{2,1,0:T(8,128)(2,1)S(1)}, u32[]{:S(2)}, u32[]{:S(2)}) %collective-permute-start.7) | collective-permute-done | bytes 81952 | tf_op jit(solution)/shard_map/ppermute | solution.py:516
  58.7 1.1 collective-permute-done.8.refs_3_
  59.9 0.6 copy-done.13
  60.5 10.3 %shard_map.143 = (bf16[8,64,128]{2,1,0:T(8,128)(2,1)}, bf16[8,64,128]{2,1,0:T(8,128)(2,1)}, bf16[8,64,128]{2,1,0:T(8,128)(2,1)}, bf16[8,64,128]{2,1,0:T(8,128)(2,1)}) custom-call(s32[2]{0:T(128)} %pad_add_fusion.me_ref, s32[8]{0:T(128)} %length_ref.1, bf16[8,40,128]{2,1,0:T(8,128)(2,1)} %copy-done.5, bf16[8,40,128]{2,1,0:T(8,128)(2,1)} %copy-done.11, ...), custom_call_target="tpu_custom_call" | custom-call | flops 1 | bytes 1 | tf_op jit(solution)/shard_map/pallas_call | solution.py:298
  70.7 1.4 %collective-permute-start.10 = (bf16[8,64,128]{2,1,0:T(8,128)(2,1)}, bf16[8,64,128]{2,1,0:T(8,128)(2,1)S(1)}, u32[]{:S(2)}, u32[]{:S(2)}) collective-permute-start(bf16[8,64,128]{2,1,0:T(8,128)(2,1)} %get-tuple-element.145), channel_id=1, source_target_pairs={{0,2},{1,3},{2,0},{3,1},{4,6},{5,7},{6,4},{7,5},{8,10},{9,11},{10,... | collective-permute-start | bytes 393224 | tf_op jit(solution)/shard_map/ppermute | solution.py:516
  72.9 4.4 %collective-permute-done.10.refs_2_ = bf16[8,64,128]{2,1,0:T(8,128)(2,1)S(1)} collective-permute-done((bf16[8,64,128]{2,1,0:T(8,128)(2,1)}, bf16[8,64,128]{2,1,0:T(8,128)(2,1)S(1)}, u32[]{:S(2)}, u32[]{:S(2)}) %collective-permute-start.10) | collective-permute-done | bytes 131104 | tf_op jit(solution)/shard_map/ppermute | solution.py:516
  77.3 1.9 %collective-permute-done.11.refs_3_ = bf16[8,64,128]{2,1,0:T(8,128)(2,1)S(1)} collective-permute-done((bf16[8,64,128]{2,1,0:T(8,128)(2,1)}, bf16[8,64,128]{2,1,0:T(8,128)(2,1)S(1)}, u32[]{:S(2)}, u32[]{:S(2)}) %collective-permute-start.11) | collective-permute-done | bytes 131104 | tf_op jit(solution)/shard_map/ppermute | solution.py:516
  79.2 3.0 %all-to-all-done.2.refs_0_ = bf16[40,16,1024]{2,1,0:T(8,128)(2,1)S(1)} async-done(((bf16[40,16,1024]{2,1,0:T(8,128)(2,1)}), bf16[40,16,1024]{2,1,0:T(8,128)(2,1)S(1)}, u32[]{:S(2)}, u32[]{:S(2)}) %all-to-all-start.2) | async-done | bytes 1310752 | tf_op jit(solution)/shard_map/all_to_all | solution.py:551
  82.2 2.7 %collective-permute-start.13 = (bf16[11,16,1024]{2,1,0:T(8,128)(2,1)S(1)}, bf16[11,16,1024]{2,1,0:T(8,128)(2,1)S(1)}, u32[]{:S(2)}, u32[]{:S(2)}) collective-permute-start(bf16[11,16,1024]{2,1,0:T(8,128)(2,1)S(1)} %copy-done.15), channel_id=1, source_target_pairs={{0,16},{4,20},{8,24},{12,28},{16,0},{20,4},{24,8},{28,12},{1,17},{... | collective-permute-start | bytes 1081352 | tf_op jit(solution)/shard_map/ppermute | solution.py:516
  84.9 0.9 copy-done.4
  85.8 1.1 shard_map.144
  86.9 3.8 %all-to-all-start.3 = ((bf16[8,64,128]{2,1,0:T(8,128)(2,1)}), bf16[8,64,128]{2,1,0:T(8,128)(2,1)S(1)}, u32[]{:S(2)}, u32[]{:S(2)}) async-start(bf16[8,64,128]{2,1,0:T(8,128)(2,1)} %shard_map.144), calls=%async_computation.3 | async-start | bytes 262144 | tf_op jit(solution)/shard_map/all_to_all | solution.py:660
  90.8 1.7 %shard_map.145.refs_2_ = bf16[128,16,1024]{2,1,0:T(8,128)(2,1)} custom-call(s32[8]{0:T(128)S(1)} %iota_multiply_fusion.place_ref, bf16[40,16,1024]{2,1,0:T(8,128)(2,1)S(1)} %all-to-all-done.2.refs_0_, bf16[128,16,1024]{2,1,0:T(8,128)(2,1)} %shard_map.142.refs_1_), custom_call_target="tpu_custom_call", output_to_operand_aliasing={{}: (2, {})} | custom-call | bytes 2621440 | tf_op jit(solution)/shard_map/pallas_call | solution.py:156
  92.5 11.4 %all-to-all-done.3.refs_0_ = bf16[8,64,128]{2,1,0:T(8,128)(2,1)S(1)} async-done(((bf16[8,64,128]{2,1,0:T(8,128)(2,1)}), bf16[8,64,128]{2,1,0:T(8,128)(2,1)S(1)}, u32[]{:S(2)}, u32[]{:S(2)}) %all-to-all-start.3) | async-done | bytes 131104 | tf_op jit(solution)/shard_map/all_to_all | solution.py:660
  104.0 3.4 %collective-permute-start.15 = (bf16[11,16,1024]{2,1,0:T(8,128)(2,1)S(1)}, bf16[11,16,1024]{2,1,0:T(8,128)(2,1)S(1)}, u32[]{:S(2)}, u32[]{:S(2)}) collective-permute-start(bf16[11,16,1024]{2,1,0:T(8,128)(2,1)S(1)} %copy-done.14), channel_id=1, source_target_pairs={{0,20},{4,16},{8,28},{12,24},{16,4},{20,0},{24,12},{28,8},{1,21},{... | collective-permute-start | bytes 1081352 | tf_op jit(solution)/shard_map/ppermute | solution.py:516
  107.5 0.9 shard_map.146
  108.4 3.4 %all-to-all-start.4 = ((bf16[8,40,128]{2,1,0:T(8,128)(2,1)}), bf16[8,40,128]{2,1,0:T(8,128)(2,1)S(1)}, u32[]{:S(2)}, u32[]{:S(2)}) async-start(bf16[8,40,128]{2,1,0:T(8,128)(2,1)} %shard_map.146), calls=%async_computation.4 | async-start | bytes 163840 | tf_op jit(solution)/shard_map/all_to_all | solution.py:665
  111.8 1.4 %shard_map.147.refs_2_ = bf16[128,16,1024]{2,1,0:T(8,128)(2,1)} custom-call(s32[2]{0:T(128)S(1)} %pad_add_fusion.2.place_ref, bf16[11,16,1024]{2,1,0:T(8,128)(2,1)S(1)} %collective-permute-done.12.refs_0_, bf16[11,16,1024]{2,1,0:T(8,128)(2,1)S(1)} %collective-permute-done.13.refs_1_, ...), custom_call_target="tpu_custom_call", output_to_operand_aliasing={{}: (3, {})} | custom-call | bytes 1441792 | tf_op jit(solution)/shard_map/pallas_call | solution.py:156
  113.2 11.9 %all-to-all-done.4.part_ref = bf16[8,40,128]{2,1,0:T(8,128)(2,1)S(1)} async-done(((bf16[8,40,128]{2,1,0:T(8,128)(2,1)}), bf16[8,40,128]{2,1,0:T(8,128)(2,1)S(1)}, u32[]{:S(2)}, u32[]{:S(2)}) %all-to-all-start.4) | async-done | bytes 81952 | tf_op jit(solution)/shard_map/all_to_all | solution.py:665
  125.1 2.1 %collective-permute-start.19 = (bf16[7,16,1024]{2,1,0:T(8,128)(2,1)}, bf16[7,16,1024]{2,1,0:T(8,128)(2,1)S(1)}, u32[]{:S(2)}, u32[]{:S(2)}) collective-permute-start(bf16[7,16,1024]{2,1,0:T(8,128)(2,1)} %get-tuple-element.189), channel_id=1, source_target_pairs={{0,28},{4,24},{8,20},{12,16},{16,12},{20,8},{24,4},{28,0},{1,29},{... | collective-permute-start | bytes 688136 | tf_op jit(solution)/shard_map/ppermute | solution.py:516
  127.2 0.9 shard_map.148
  128.2 1.4 %collective-permute-start.17 = (f32[10,512]{1,0:T(8,128)S(1)}, f32[10,512]{1,0:T(8,128)S(1)}, u32[]{:S(2)}, u32[]{:S(2)}) collective-permute-start(f32[10,512]{1,0:T(8,128)S(1)} %get-tuple-element.187), channel_id=1, source_target_pairs={{0,2},{1,3},{2,0},{3,1},{4,6},{5,7},{6,4},{7,5},{8,10},{9,11},{10,... | collective-permute-start | bytes 61448 | tf_op jit(solution)/shard_map/ppermute | solution.py:516
  129.6 0.5 collective-permute-start.18
  130.2 1.4 %shard_map.149.refs_1_ = bf16[128,16,1024]{2,1,0:T(8,128)(2,1)} custom-call(s32[2]{0:T(128)S(1)} %pad_add_fusion.3.place_ref, bf16[11,16,1024]{2,1,0:T(8,128)(2,1)S(1)} %collective-permute-done.14.refs_0_, bf16[11,16,1024]{2,1,0:T(8,128)(2,1)S(1)} %collective-permute-done.15.refs_1_, ...), custom_call_target="tpu_custom_call", output_to_operand_aliasing={{}: (3, {})} | custom-call | bytes 1441792 | tf_op jit(solution)/shard_map/pallas_call | solution.py:156
  131.6 0.6 collective-permute-done.17
  132.2 0.8 collective-permute-done.18
  133.0 1.3 collective-permute-done.19.refs_0_
  134.3 0.6 add_convert_fusion
  134.9 0.7 shard_map.150
  (53 shorter events, 2.1 us)
Async XLA Ops:
  0.6 16.1 %copy-start.1 = (bf16[1024,512]{1,0:T(8,128)(2,1)S(1)}, bf16[1024,512]{1,0:T(8,128)(2,1)}, u32[]{:S(2)}) copy-start(bf16[1024,512]{1,0:T(8,128)(2,1)} %query_ref.1) | copy-start | bytes 3145732
  0.6 16.1 %copy-start.3 = (bf16[1024,128]{1,0:T(8,128)(2,1)S(1)}, bf16[1024,128]{1,0:T(8,128)(2,1)}, u32[]{:S(2)}) copy-start(bf16[1024,128]{1,0:T(8,128)(2,1)} %keyval_ref.1) | copy-start | bytes 786436
  0.7 0.8 copy-start.6
  2.1 14.6 %all-to-all-start = ((bf16[8,5,1024]{2,1,0:T(8,128)(2,1)}), bf16[8,5,1024]{2,1,0:T(8,128)(2,1)S(1)}, u32[]{:S(2)}, u32[]{:S(2)}) async-start(bf16[8,5,1024]{2,1,0:T(8,128)(2,1)} %shard_map.137), calls=%async_computation | async-start | bytes 262144 | tf_op jit(solution)/shard_map/all_to_all | solution.py:525
  10.0 6.8 %copy-start.7 = (s32[2]{0:T(128)S(1)}, s32[2]{0:T(128)}, u32[]{:S(2)}) copy-start(s32[2]{0:T(128)} %pad_add_fusion.me_ref) | copy-start | bytes 28
  10.0 42.2 %copy-start.10 = (s32[8]{0:T(128)S(1)}, s32[8]{0:T(128)}, u32[]{:S(2)}) copy-start(s32[8]{0:T(128)} %kept_ref.1) | copy-start | bytes 100
  17.8 8.7 %collective-permute-start.3 = (bf16[4,16,1024]{2,1,0:T(8,128)(2,1)}, bf16[4,16,1024]{2,1,0:T(8,128)(2,1)S(1)}, u32[]{:S(2)}, u32[]{:S(2)}) collective-permute-start(bf16[4,16,1024]{2,1,0:T(8,128)(2,1)} %get-tuple-element.115), channel_id=1, source_target_pairs={{0,28},{4,24},{8,20},{12,16},{16,12},{20,8},{24,4},{28,0},{1,29},{... | collective-permute-start | bytes 393224 | tf_op jit(solution)/shard_map/ppermute | solution.py:516
  21.5 1.9 %collective-permute-start = (f32[40,256]{1,0:T(8,128)S(1)}, f32[40,256]{1,0:T(8,128)S(1)}, u32[]{:S(2)}, u32[]{:S(2)}) collective-permute-start(f32[40,256]{1,0:T(8,128)S(1)} %get-tuple-element.112), channel_id=1, source_target_pairs={{0,1},{1,0},{2,3},{3,2},{4,5},{5,4},{6,7},{7,6},{8,9},{9,8},{10,11... | collective-permute-start | bytes 122888 | tf_op jit(solution)/shard_map/ppermute | solution.py:516
  21.5 4.0 %collective-permute-start.1 = (f32[40,256]{1,0:T(8,128)S(1)}, f32[40,256]{1,0:T(8,128)S(1)}, u32[]{:S(2)}, u32[]{:S(2)}) collective-permute-start(f32[40,256]{1,0:T(8,128)S(1)} %get-tuple-element.113), channel_id=1, source_target_pairs={{0,2},{1,3},{2,0},{3,1},{4,6},{5,7},{6,4},{7,5},{8,10},{9,11},{10,... | collective-permute-start | bytes 122888 | tf_op jit(solution)/shard_map/ppermute | solution.py:516
  22.9 3.5 %collective-permute-start.2 = (f32[40,256]{1,0:T(8,128)S(1)}, f32[40,256]{1,0:T(8,128)S(1)}, u32[]{:S(2)}, u32[]{:S(2)}) collective-permute-start(f32[40,256]{1,0:T(8,128)S(1)} %get-tuple-element.114), channel_id=1, source_target_pairs={{0,3},{1,2},{2,1},{3,0},{4,7},{5,6},{6,5},{7,4},{8,11},{9,10},{10,... | collective-permute-start | bytes 122888 | tf_op jit(solution)/shard_map/ppermute | solution.py:516
  26.5 22.1 %collective-permute-start.4 = (bf16[11,16,1024]{2,1,0:T(8,128)(2,1)}, bf16[11,16,1024]{2,1,0:T(8,128)(2,1)S(1)}, u32[]{:S(2)}, u32[]{:S(2)}) collective-permute-start(bf16[11,16,1024]{2,1,0:T(8,128)(2,1)} %get-tuple-element.127), channel_id=1, source_target_pairs={{0,24},{4,28},{8,16},{12,20},{16,8},{20,12},{24,0},{28,4},{1,25},{... | collective-permute-start | bytes 1081352 | tf_op jit(solution)/shard_map/ppermute | solution.py:516
  28.4 20.1 %collective-permute-start.5 = (bf16[11,16,1024]{2,1,0:T(8,128)(2,1)}, bf16[11,16,1024]{2,1,0:T(8,128)(2,1)S(1)}, u32[]{:S(2)}, u32[]{:S(2)}) collective-permute-start(bf16[11,16,1024]{2,1,0:T(8,128)(2,1)} %get-tuple-element.128), channel_id=1, source_target_pairs={{0,4},{4,0},{8,12},{12,8},{16,20},{20,16},{24,28},{28,24},{1,5},{5... | collective-permute-start | bytes 1081352 | tf_op jit(solution)/shard_map/ppermute | solution.py:516
  29.9 0.7 copy-start.9
  48.6 33.6 %all-to-all-start.2 = ((bf16[40,16,1024]{2,1,0:T(8,128)(2,1)}), bf16[40,16,1024]{2,1,0:T(8,128)(2,1)S(1)}, u32[]{:S(2)}, u32[]{:S(2)}) async-start(bf16[40,16,1024]{2,1,0:T(8,128)(2,1)} %get-tuple-element.147), calls=%async_computation.2 | async-start | bytes 2621440 | tf_op jit(solution)/shard_map/all_to_all | solution.py:551
  53.5 3.4 %copy-start = (bf16[128,1024]{1,0:T(8,128)(2,1)}, bf16[128,1024]{1,0:T(8,128)(2,1)S(1)}, u32[]{:S(2)}) copy-start(bf16[128,1024]{1,0:T(8,128)(2,1)S(1)} %get-tuple-element.141.refs_6_.refs_7_) | copy-start | bytes 786436
  53.5 3.4 %copy-start.5 = (bf16[8,40,128]{2,1,0:T(8,128)(2,1)}, bf16[8,40,128]{2,1,0:T(8,128)(2,1)S(1)}, u32[]{:S(2)}) copy-start(bf16[8,40,128]{2,1,0:T(8,128)(2,1)S(1)} %get-tuple-element.137.refs_0_) | copy-start | bytes 245764
  53.5 3.4 %collective-permute-start.6 = (bf16[8,40,128]{2,1,0:T(8,128)(2,1)S(1)}, bf16[8,40,128]{2,1,0:T(8,128)(2,1)S(1)}, u32[]{:S(2)}, u32[]{:S(2)}) collective-permute-start(bf16[8,40,128]{2,1,0:T(8,128)(2,1)S(1)} %get-tuple-element.137.refs_0_), channel_id=1, source_target_pairs={{0,1},{1,0},{2,3},{3,2},{4,5},{5,4},{6,7},{7,6},{8,9},{9,8},{10,11... | collective-permute-start | bytes 245768 | tf_op jit(solution)/shard_map/ppermute | solution.py:516
  53.5 5.2 %collective-permute-start.7 = (bf16[8,40,128]{2,1,0:T(8,128)(2,1)S(1)}, bf16[8,40,128]{2,1,0:T(8,128)(2,1)S(1)}, u32[]{:S(2)}, u32[]{:S(2)}) collective-permute-start(bf16[8,40,128]{2,1,0:T(8,128)(2,1)S(1)} %get-tuple-element.137.refs_0_), channel_id=1, source_target_pairs={{0,2},{1,3},{2,0},{3,1},{4,6},{5,7},{6,4},{7,5},{8,10},{9,11},{10,... | collective-permute-start | bytes 245768 | tf_op jit(solution)/shard_map/ppermute | solution.py:516
  55.1 4.7 %collective-permute-start.8 = (bf16[8,40,128]{2,1,0:T(8,128)(2,1)S(1)}, bf16[8,40,128]{2,1,0:T(8,128)(2,1)S(1)}, u32[]{:S(2)}, u32[]{:S(2)}) collective-permute-start(bf16[8,40,128]{2,1,0:T(8,128)(2,1)S(1)} %get-tuple-element.137.refs_0_), channel_id=1, source_target_pairs={{0,3},{1,2},{2,1},{3,0},{4,7},{5,6},{6,5},{7,4},{8,11},{9,10},{10,... | collective-permute-start | bytes 245768 | tf_op jit(solution)/shard_map/ppermute | solution.py:516
  57.0 2.9 %copy-start.11 = (bf16[8,40,128]{2,1,0:T(8,128)(2,1)}, bf16[8,40,128]{2,1,0:T(8,128)(2,1)S(1)}, u32[]{:S(2)}) copy-start(bf16[8,40,128]{2,1,0:T(8,128)(2,1)S(1)} %collective-permute-done.6.refs_1_) | copy-start | bytes 245764
  58.7 1.2 copy-start.12
  59.8 0.6 copy-start.13
  60.5 21.7 %copy-start.15 = (bf16[11,16,1024]{2,1,0:T(8,128)(2,1)S(1)}, bf16[11,16,1024]{2,1,0:T(8,128)(2,1)}, u32[]{:S(2)}) copy-start(bf16[11,16,1024]{2,1,0:T(8,128)(2,1)} %get-tuple-element.161) | copy-start | bytes 1081348
  70.7 6.5 %collective-permute-start.10 = (bf16[8,64,128]{2,1,0:T(8,128)(2,1)}, bf16[8,64,128]{2,1,0:T(8,128)(2,1)S(1)}, u32[]{:S(2)}, u32[]{:S(2)}) collective-permute-start(bf16[8,64,128]{2,1,0:T(8,128)(2,1)} %get-tuple-element.145), channel_id=1, source_target_pairs={{0,2},{1,3},{2,0},{3,1},{4,6},{5,7},{6,4},{7,5},{8,10},{9,11},{10,... | collective-permute-start | bytes 393224 | tf_op jit(solution)/shard_map/ppermute | solution.py:516
  72.1 7.1 %collective-permute-start.11 = (bf16[8,64,128]{2,1,0:T(8,128)(2,1)}, bf16[8,64,128]{2,1,0:T(8,128)(2,1)S(1)}, u32[]{:S(2)}, u32[]{:S(2)}) collective-permute-start(bf16[8,64,128]{2,1,0:T(8,128)(2,1)} %get-tuple-element.146), channel_id=1, source_target_pairs={{0,3},{1,2},{2,1},{3,0},{4,7},{5,6},{6,5},{7,4},{8,11},{9,10},{10,... | collective-permute-start | bytes 393224 | tf_op jit(solution)/shard_map/ppermute | solution.py:516
  72.6 6.6 %collective-permute-start.9 = (bf16[8,64,128]{2,1,0:T(8,128)(2,1)}, bf16[8,64,128]{2,1,0:T(8,128)(2,1)S(1)}, u32[]{:S(2)}, u32[]{:S(2)}) collective-permute-start(bf16[8,64,128]{2,1,0:T(8,128)(2,1)} %get-tuple-element.144), channel_id=1, source_target_pairs={{0,1},{1,0},{2,3},{3,2},{4,5},{5,4},{6,7},{7,6},{8,9},{9,8},{10,11... | collective-permute-start | bytes 393224 | tf_op jit(solution)/shard_map/ppermute | solution.py:516
  82.2 21.6 %collective-permute-start.12 = (bf16[11,16,1024]{2,1,0:T(8,128)(2,1)}, bf16[11,16,1024]{2,1,0:T(8,128)(2,1)S(1)}, u32[]{:S(2)}, u32[]{:S(2)}) collective-permute-start(bf16[11,16,1024]{2,1,0:T(8,128)(2,1)} %get-tuple-element.160), channel_id=1, source_target_pairs={{0,12},{4,8},{8,4},{12,0},{16,28},{20,24},{24,20},{28,16},{1,13},{... | collective-permute-start | bytes 1081352 | tf_op jit(solution)/shard_map/ppermute | solution.py:516
  82.2 21.6 %collective-permute-start.13 = (bf16[11,16,1024]{2,1,0:T(8,128)(2,1)S(1)}, bf16[11,16,1024]{2,1,0:T(8,128)(2,1)S(1)}, u32[]{:S(2)}, u32[]{:S(2)}) collective-permute-start(bf16[11,16,1024]{2,1,0:T(8,128)(2,1)S(1)} %copy-done.15), channel_id=1, source_target_pairs={{0,16},{4,20},{8,24},{12,28},{16,0},{20,4},{24,8},{28,12},{1,17},{... | collective-permute-start | bytes 1081352 | tf_op jit(solution)/shard_map/ppermute | solution.py:516
  84.9 0.9 copy-start.4
  86.9 16.9 %all-to-all-start.3 = ((bf16[8,64,128]{2,1,0:T(8,128)(2,1)}), bf16[8,64,128]{2,1,0:T(8,128)(2,1)S(1)}, u32[]{:S(2)}, u32[]{:S(2)}) async-start(bf16[8,64,128]{2,1,0:T(8,128)(2,1)} %shard_map.144), calls=%async_computation.3 | async-start | bytes 262144 | tf_op jit(solution)/shard_map/all_to_all | solution.py:660
  90.8 13.2 %copy-start.14 = (bf16[11,16,1024]{2,1,0:T(8,128)(2,1)S(1)}, bf16[11,16,1024]{2,1,0:T(8,128)(2,1)}, u32[]{:S(2)}) copy-start(bf16[11,16,1024]{2,1,0:T(8,128)(2,1)} %get-tuple-element.172) | copy-start | bytes 1081348
  103.8 21.3 %collective-permute-start.14 = (bf16[11,16,1024]{2,1,0:T(8,128)(2,1)}, bf16[11,16,1024]{2,1,0:T(8,128)(2,1)S(1)}, u32[]{:S(2)}, u32[]{:S(2)}) collective-permute-start(bf16[11,16,1024]{2,1,0:T(8,128)(2,1)} %get-tuple-element.171), channel_id=1, source_target_pairs={{0,8},{4,12},{8,0},{12,4},{16,24},{20,28},{24,16},{28,20},{1,9},{5... | collective-permute-start | bytes 1081352 | tf_op jit(solution)/shard_map/ppermute | solution.py:516
  104.0 21.1 %collective-permute-start.15 = (bf16[11,16,1024]{2,1,0:T(8,128)(2,1)S(1)}, bf16[11,16,1024]{2,1,0:T(8,128)(2,1)S(1)}, u32[]{:S(2)}, u32[]{:S(2)}) collective-permute-start(bf16[11,16,1024]{2,1,0:T(8,128)(2,1)S(1)} %copy-done.14), channel_id=1, source_target_pairs={{0,20},{4,16},{8,28},{12,24},{16,4},{20,0},{24,12},{28,8},{1,21},{... | collective-permute-start | bytes 1081352 | tf_op jit(solution)/shard_map/ppermute | solution.py:516
  108.4 16.8 %all-to-all-start.4 = ((bf16[8,40,128]{2,1,0:T(8,128)(2,1)}), bf16[8,40,128]{2,1,0:T(8,128)(2,1)S(1)}, u32[]{:S(2)}, u32[]{:S(2)}) async-start(bf16[8,40,128]{2,1,0:T(8,128)(2,1)} %shard_map.146), calls=%async_computation.4 | async-start | bytes 163840 | tf_op jit(solution)/shard_map/all_to_all | solution.py:665
  111.8 15.4 %copy-start.2 = (bf16[1024,512]{1,0:T(8,128)(2,1)S(1)}, bf16[1024,512]{1,0:T(8,128)(2,1)}, u32[]{:S(2)}) copy-start(bf16[1024,512]{1,0:T(8,128)(2,1)} %weight_ref.1) | copy-start | bytes 3145732
  111.8 15.4 %copy-start.8 = (s32[2]{0:T(128)S(1)}, s32[2]{0:T(128)}, u32[]{:S(2)}) copy-start(s32[2]{0:T(128)} %pad_add_fusion.me_ref) | copy-start | bytes 28
  125.1 9.1 %collective-permute-start.19 = (bf16[7,16,1024]{2,1,0:T(8,128)(2,1)}, bf16[7,16,1024]{2,1,0:T(8,128)(2,1)S(1)}, u32[]{:S(2)}, u32[]{:S(2)}) collective-permute-start(bf16[7,16,1024]{2,1,0:T(8,128)(2,1)} %get-tuple-element.189), channel_id=1, source_target_pairs={{0,28},{4,24},{8,20},{12,16},{16,12},{20,8},{24,4},{28,0},{1,29},{... | collective-permute-start | bytes 688136 | tf_op jit(solution)/shard_map/ppermute | solution.py:516
  128.2 3.4 %collective-permute-start.16 = (f32[10,512]{1,0:T(8,128)S(1)}, f32[10,512]{1,0:T(8,128)S(1)}, u32[]{:S(2)}, u32[]{:S(2)}) collective-permute-start(f32[10,512]{1,0:T(8,128)S(1)} %get-tuple-element.186), channel_id=1, source_target_pairs={{0,1},{1,0},{2,3},{3,2},{4,5},{5,4},{6,7},{7,6},{8,9},{9,8},{10,11... | collective-permute-start | bytes 61448 | tf_op jit(solution)/shard_map/ppermute | solution.py:516
  128.2 4.0 %collective-permute-start.17 = (f32[10,512]{1,0:T(8,128)S(1)}, f32[10,512]{1,0:T(8,128)S(1)}, u32[]{:S(2)}, u32[]{:S(2)}) collective-permute-start(f32[10,512]{1,0:T(8,128)S(1)} %get-tuple-element.187), channel_id=1, source_target_pairs={{0,2},{1,3},{2,0},{3,1},{4,6},{5,7},{6,4},{7,5},{8,10},{9,11},{10,... | collective-permute-start | bytes 61448 | tf_op jit(solution)/shard_map/ppermute | solution.py:516
  129.6 3.3 %collective-permute-start.18 = (f32[10,512]{1,0:T(8,128)S(1)}, f32[10,512]{1,0:T(8,128)S(1)}, u32[]{:S(2)}, u32[]{:S(2)}) collective-permute-start(f32[10,512]{1,0:T(8,128)S(1)} %get-tuple-element.188), channel_id=1, source_target_pairs={{0,3},{1,2},{2,1},{3,0},{4,7},{5,6},{6,5},{7,4},{8,11},{9,10},{10,... | collective-permute-start | bytes 61448 | tf_op jit(solution)/shard_map/ppermute | solution.py:516

commit v21 on v20

--- a/solution.py
+++ b/solution.py
@@ -584,8 +584,8 @@
             w_keyval,
             scratch=[pltpu.VMEM((rows, narrow * HD), jnp.float32)],
         )
-        partial = land(deal(launch(partial, 8), "narrow"), 8)
-        partial = launch(partial, 6, 1)
+        partial = land(deal(launch(partial, 8, 6), "narrow"), 8)
+        partial = launch(partial, 1)
         packed = in_vmem(
             functools.partial(pack_kernel, narrow),
             jax.ShapeDtypeStruct((wide, rows + wide, 2 * HD), jnp.bfloat16),
@@ -617,8 +617,8 @@
         partial = jnp.concatenate(
             [query_part, jnp.broadcast_to(keyval_part[None], (narrow,) + keyval_part.shape)], axis=2
         )
-        partial = land(exchange(launch(partial, 8), "narrow"), 8)
-        partial = launch(partial, 6, 1)
+        partial = land(exchange(launch(partial, 8, 6), "narrow"), 8)
+        partial = launch(partial, 1)
         projected = jnp.sum(partial, axis=0).astype(jnp.bfloat16)
         tags = tags[:, : 3 * capacity].astype(jnp.bfloat16)[:, None]
         tags = jnp.pad(tags, ((0, 0), (0, 7), (0, projected.shape[1] - tags.shape[2])))
@@ -648,13 +648,14 @@
 
     queries, moved_pool = lax.optimization_barrier((queries, placed(moved_pool)))
     mixed = attend(both, lengths, queries, keyval, tokens, token_info, rows, piece)
+    mixed = launch(mixed, 3, 4)
     if direct:
         mixed = land(deal(mixed, "narrow"), 0)
     else:
         mixed = land(exchange(mixed[0], "narrow"), 0)
         mixed = mixed.reshape((narrow, wide) + mixed.shape[1:])
         mixed = [mixed[i] for i in range(narrow)]
-    mixed = combine(launch(mixed, 3, 4), piece)
+    mixed = combine(mixed, piece)
     mixed, pages = lax.optimization_barrier((mixed, moved_pool))
     pages = placed(pages)
     mixed = land(exchange(mixed, "wide"), 3, 4)

time: 137 us -> 132 us (0.964)
  blocking collectives: 18 us -> 0 us
  starting transfers between devices: 41.4 us -> 57.7 us
  waiting for transfers between devices: 42.4 us -> 39 us
    all_to_all x1 -> x0, blocking collectives: 18 us -> none  [on_device(): received = land(exchange(packed, 'wide'), 6, 1)]
    all_to_all x0 -> x1, starting transfers between devices: none -> 14.1 us  [on_device(): received = land(exchange(packed, 'wide'), 6, 1)]
    all_to_all x1, waiting for transfers between devices: 11.4 us -> 2.04 us  [on_device(): mixed = land(exchange(mixed, 'wide'), 3, 4)]
    all_to_all x0 -> x1, waiting for transfers between devices: none -> 7.78 us  [on_device(): received = land(exchange(packed, 'wide'), 6, 1)]
    all_to_all x1, waiting for transfers between devices: 3.02 us -> 0.01 us  [launch(): flying[c] = send(chunk, 'wide', d) if d else exchange(chunk, 'wide')]
    all_to_all x1, starting transfers between devices: 3.84 us -> 5.93 us  [on_device(): mixed = land(exchange(mixed, 'wide'), 3, 4)]
    unnamed x32 -> x34, local copies, waits for them, and re-layouts: 3.07 us -> 3.07 us
  transfers between devices with their start and end apart: 24 -> 25, of which waited for: 13 -> 14; matrix products, arithmetic and copies ran while one was open for 1% -> 1% of each run, Pallas kernels for 19% -> 20%
where the time goes in v21:
time: 132 us; the launch traced here: 131 us
  starting transfers between devices  57.7 us (44%)
  waiting for transfers between devices  39 us (30%)
  Pallas kernels  29.2 us (22%)
  local copies, waits for them, and re-layouts  3.07 us (2%)
  other arithmetic  1.45 us (1%)
    ppermute x20, starting transfers between devices, send(): lax.ppermute(block, axis, [(i, i ^ d) for i in range(lax.axis_size(axis))])  23.5 us
    ppermute x20, waiting for transfers between devices, send(): lax.ppermute(block, axis, [(i, i ^ d) for i in range(lax.axis_size(axis))])  16 us
    all_to_all x1, starting transfers between devices, on_device(): received = land(exchange(packed, 'wide'), 6, 1)  14.1 us
    all_to_all x1, waiting for transfers between devices, on_device(): attn = land(exchange(attn, 'wide'), 2, 5)  12.1 us
    pallas_call x1, Pallas kernels, attend(): pl.pallas_call(functools.partial(attend_kernel, rows, piece, peers), grid...  10.3 us
    all_to_all x1, waiting for transfers between devices, on_device(): received = land(exchange(packed, 'wide'), 6, 1)  7.78 us
    all_to_all x1, starting transfers between devices, on_device(): gathered = exchange(in_vmem(repeat_kernel, copies, None, hidden), 'wide')  7.28 us
    pallas_call x5, Pallas kernels, place_pages(): pl.pallas_call(functools.partial(place_kernel, counts), out_shape=jax.Sha...  6.64 us
  transfers between devices with their start and end apart: 25, of which 14 were waited for; matrix products, arithmetic and copies ran while one was open for 1% of the time, Pallas kernels for 20%

profile of v21, /device:TPU:0, one launch (start us, length us, event | category | flops | bytes accessed | tf_op | source)
XLA Modules:
  0.0 131.3 jit_solution(5816252613312794879)
XLA Ops:
  0.7 0.8 copy-done.6
  1.5 0.6 shard_map.137
  2.1 7.3 %all-to-all-start = ((bf16[8,5,1024]{2,1,0:T(8,128)(2,1)}), bf16[8,5,1024]{2,1,0:T(8,128)(2,1)S(1)}, u32[]{:S(2)}, u32[]{:S(2)}) async-start(bf16[8,5,1024]{2,1,0:T(8,128)(2,1)} %shard_map.137), calls=%async_computation | async-start | bytes 262144 | tf_op jit(solution)/shard_map/all_to_all | solution.py:525
  9.4 0.6 pad_add_fusion.me_ref
  10.0 5.7 %shard_map.138 = (bf16[128,16,1024]{2,1,0:T(8,128)(2,1)}, f32[8,128]{1,0:T(8,128)}, f32[8,2048]{1,0:T(8,128)}, bf16[40,16,1024]{2,1,0:T(8,128)(2,1)}, bf16[11,16...) custom-call(s32[2]{0:T(128)} %pad_add_fusion.me_ref, ...), custom_call_target="tpu_custom_call" | custom-call | bytes 8388608 | tf_op jit(solution)/shard_map/pallas_call | solution.py:118
  15.7 1.1 all-to-all-done.hidden_ref
  16.8 1.0 shard_map.139
  17.7 3.7 %collective-permute-start.3 = (bf16[4,16,1024]{2,1,0:T(8,128)(2,1)}, bf16[4,16,1024]{2,1,0:T(8,128)(2,1)S(1)}, u32[]{:S(2)}, u32[]{:S(2)}) collective-permute-start(bf16[4,16,1024]{2,1,0:T(8,128)(2,1)} %get-tuple-element.116), channel_id=1, source_target_pairs={{0,28},{4,24},{8,20},{12,16},{16,12},{20,8},{24,4},{28,0},{1,29},{... | collective-permute-start | bytes 393224 | tf_op jit(solution)/shard_map/ppermute | solution.py:516
  21.5 1.5 %collective-permute-start.1 = (f32[40,256]{1,0:T(8,128)S(1)}, f32[40,256]{1,0:T(8,128)S(1)}, u32[]{:S(2)}, u32[]{:S(2)}) collective-permute-start(f32[40,256]{1,0:T(8,128)S(1)} %get-tuple-element.114), channel_id=1, source_target_pairs={{0,2},{1,3},{2,0},{3,1},{4,6},{5,7},{6,4},{7,5},{8,10},{9,11},{10,... | collective-permute-start | bytes 122888 | tf_op jit(solution)/shard_map/ppermute | solution.py:516
  23.9 1.6 %collective-permute-done.1.refs_2_ = f32[40,256]{1,0:T(8,128)S(1)} collective-permute-done((f32[40,256]{1,0:T(8,128)S(1)}, f32[40,256]{1,0:T(8,128)S(1)}, u32[]{:S(2)}, u32[]{:S(2)}) %collective-permute-start.1) | collective-permute-done | bytes 40992 | tf_op jit(solution)/shard_map/ppermute | solution.py:516
  25.5 1.0 collective-permute-done.2.refs_3_
  27.1 0.7 copy-done.9
  27.8 0.7 shard_map.140
  28.5 14.1 %all-to-all-start.1 = ((bf16[8,48,256]{2,1,0:T(8,128)(2,1)}), bf16[8,48,256]{2,1,0:T(8,128)(2,1)S(1)}, u32[]{:S(2)}, u32[]{:S(2)}) async-start(bf16[8,48,256]{2,1,0:T(8,128)(2,1)} %shard_map.140), calls=%async_computation.1 | async-start | bytes 393216 | tf_op jit(solution)/shard_map/all_to_all | solution.py:596
  42.5 7.8 %all-to-all-done.1.part_ref = bf16[8,48,256]{2,1,0:T(8,128)(2,1)S(1)} async-done(((bf16[8,48,256]{2,1,0:T(8,128)(2,1)}), bf16[8,48,256]{2,1,0:T(8,128)(2,1)S(1)}, u32[]{:S(2)}, u32[]{:S(2)}) %all-to-all-start.1) | async-done | bytes 196640 | tf_op jit(solution)/shard_map/all_to_all | solution.py:596
  50.3 3.6 %all-to-all-start.2 = ((bf16[40,16,1024]{2,1,0:T(8,128)(2,1)}), bf16[40,16,1024]{2,1,0:T(8,128)(2,1)S(1)}, u32[]{:S(2)}, u32[]{:S(2)}) async-start(bf16[40,16,1024]{2,1,0:T(8,128)(2,1)} %get-tuple-element.153), calls=%async_computation.2 | async-start | bytes 2621440 | tf_op jit(solution)/shard_map/all_to_all | solution.py:551
  53.9 1.4 %shard_map.141 = (bf16[8,40,128]{2,1,0:T(8,128)(2,1)S(1)}, bf16[128,1024]{1,0:T(8,128)(2,1)S(1)}, bf16[1,5,1024]{2,1,0:T(8,128)(2,1)}, s32[1,128]{1,0:T(1,128)}, s32[1,128]{1,0:T(1,128)}) custom-call(s32[2]{0:T(128)S(1)} %copy-done.7, s32[8]{0:T(128)S(1)} %copy-done.10, bf16[8,48,256]{2,1,0:T(8,128)(2,1)S(1)} %all-to-all-done.1.part_ref), custom_call_target="tpu_custom_call" | custom-call | flops 1 | bytes 1 | tf_op jit(solution)/shard_map/pallas_call | solution.py:471
  55.3 1.6 %collective-permute-start.7 = (bf16[8,40,128]{2,1,0:T(8,128)(2,1)S(1)}, bf16[8,40,128]{2,1,0:T(8,128)(2,1)S(1)}, u32[]{:S(2)}, u32[]{:S(2)}) collective-permute-start(bf16[8,40,128]{2,1,0:T(8,128)(2,1)S(1)} %get-tuple-element.137.refs_0_), channel_id=1, source_target_pairs={{0,2},{1,3},{2,0},{3,1},{4,6},{5,7},{6,4},{7,5},{8,10},{9,11},{10,... | collective-permute-start | bytes 245768 | tf_op jit(solution)/shard_map/ppermute | solution.py:516
  57.2 1.5 %shard_map.142.refs_1_ = bf16[128,16,1024]{2,1,0:T(8,128)(2,1)} custom-call(s32[3]{0:T(128)S(1)} %pad_add_fusion.1.place_ref, bf16[11,16,1024]{2,1,0:T(8,128)(2,1)S(1)} %collective-permute-done.5.refs_0_, bf16[11,16,1024]{2,1,0:T(8,128)(2,1)S(1)} %collective-permute-done.4.refs_1_, ...), custom_call_target="tpu_custom_call", output_to_operand_aliasing={{}: (4, {})} | custom-call | bytes 1703936 | tf_op jit(solution)/shard_map/pallas_call | solution.py:156
  58.7 1.6 %collective-permute-done.7.refs_2_ = bf16[8,40,128]{2,1,0:T(8,128)(2,1)S(1)} collective-permute-done((bf16[8,40,128]{2,1,0:T(8,128)(2,1)S(1)}, bf16[8,40,128]{2,1,0:T(8,128)(2,1)S(1)}, u32[]{:S(2)}, u32[]{:S(2)}) %collective-permute-start.7) | collective-permute-done | bytes 81952 | tf_op jit(solution)/shard_map/ppermute | solution.py:516
  60.4 1.3 collective-permute-done.8.refs_3_
  61.7 0.6 copy-done.13
  62.3 10.3 %shard_map.143 = (bf16[8,64,128]{2,1,0:T(8,128)(2,1)}, bf16[8,64,128]{2,1,0:T(8,128)(2,1)}, bf16[8,64,128]{2,1,0:T(8,128)(2,1)}, bf16[8,64,128]{2,1,0:T(8,128)(2,1)}) custom-call(s32[2]{0:T(128)} %pad_add_fusion.me_ref, s32[8]{0:T(128)} %length_ref.1, bf16[8,40,128]{2,1,0:T(8,128)(2,1)} %copy-done.5, bf16[8,40,128]{2,1,0:T(8,128)(2,1)} %copy-done.11, ...), custom_call_target="tpu_custom_call" | custom-call | flops 1 | bytes 1 | tf_op jit(solution)/shard_map/pallas_call | solution.py:298
  72.6 1.4 %collective-permute-start.10 = (bf16[8,64,128]{2,1,0:T(8,128)(2,1)}, bf16[8,64,128]{2,1,0:T(8,128)(2,1)S(1)}, u32[]{:S(2)}, u32[]{:S(2)}) collective-permute-start(bf16[8,64,128]{2,1,0:T(8,128)(2,1)} %get-tuple-element.151), channel_id=1, source_target_pairs={{0,2},{1,3},{2,0},{3,1},{4,6},{5,7},{6,4},{7,5},{8,10},{9,11},{10,... | collective-permute-start | bytes 393224 | tf_op jit(solution)/shard_map/ppermute | solution.py:516
  74.8 2.8 %collective-permute-start.12 = (bf16[11,16,1024]{2,1,0:T(8,128)(2,1)S(1)}, bf16[11,16,1024]{2,1,0:T(8,128)(2,1)S(1)}, u32[]{:S(2)}, u32[]{:S(2)}) collective-permute-start(bf16[11,16,1024]{2,1,0:T(8,128)(2,1)S(1)} %copy-done.15), channel_id=1, source_target_pairs={{0,12},{4,8},{8,4},{12,0},{16,28},{20,24},{24,20},{28,16},{1,13},{... | collective-permute-start | bytes 1081352 | tf_op jit(solution)/shard_map/ppermute | solution.py:516
  77.6 2.4 %collective-permute-start.13 = (bf16[11,16,1024]{2,1,0:T(8,128)(2,1)S(1)}, bf16[11,16,1024]{2,1,0:T(8,128)(2,1)S(1)}, u32[]{:S(2)}, u32[]{:S(2)}) collective-permute-start(bf16[11,16,1024]{2,1,0:T(8,128)(2,1)S(1)} %copy-done.14), channel_id=1, source_target_pairs={{0,16},{4,20},{8,24},{12,28},{16,0},{20,4},{24,8},{28,12},{1,17},{... | collective-permute-start | bytes 1081352 | tf_op jit(solution)/shard_map/ppermute | solution.py:516
  80.0 0.8 collective-permute-done.11.refs_3_
  80.8 0.9 copy-done.4
  81.7 1.1 shard_map.144
  82.8 5.9 %all-to-all-start.3 = ((bf16[8,64,128]{2,1,0:T(8,128)(2,1)}), bf16[8,64,128]{2,1,0:T(8,128)(2,1)S(1)}, u32[]{:S(2)}, u32[]{:S(2)}) async-start(bf16[8,64,128]{2,1,0:T(8,128)(2,1)} %shard_map.144), calls=%async_computation.3 | async-start | bytes 262144 | tf_op jit(solution)/shard_map/all_to_all | solution.py:661
  88.8 1.7 %shard_map.145.refs_2_ = bf16[128,16,1024]{2,1,0:T(8,128)(2,1)} custom-call(s32[8]{0:T(128)S(1)} %iota_multiply_fusion.place_ref, bf16[40,16,1024]{2,1,0:T(8,128)(2,1)S(1)} %all-to-all-done.2.refs_0_, bf16[128,16,1024]{2,1,0:T(8,128)(2,1)} %shard_map.142.refs_1_), custom_call_target="tpu_custom_call", output_to_operand_aliasing={{}: (2, {})} | custom-call | bytes 2621440 | tf_op jit(solution)/shard_map/pallas_call | solution.py:156
  90.4 5.7 %collective-permute-done.12.refs_0_ = bf16[11,16,1024]{2,1,0:T(8,128)(2,1)S(1)} collective-permute-done((bf16[11,16,1024]{2,1,0:T(8,128)(2,1)S(1)}, bf16[11,16,1024]{2,1,0:T(8,128)(2,1)S(1)}, u32[]{:S(2)}, u32[]{:S(2)}) %collective-permute-start.12) | collective-permute-done | bytes 360480 | tf_op jit(solution)/shard_map/ppermute | solution.py:516
  96.1 1.0 collective-permute-done.13.refs_1_
  97.1 2.0 %all-to-all-done.3.refs_0_ = bf16[8,64,128]{2,1,0:T(8,128)(2,1)S(1)} async-done(((bf16[8,64,128]{2,1,0:T(8,128)(2,1)}), bf16[8,64,128]{2,1,0:T(8,128)(2,1)S(1)}, u32[]{:S(2)}, u32[]{:S(2)}) %all-to-all-start.3) | async-done | bytes 131104 | tf_op jit(solution)/shard_map/all_to_all | solution.py:661
  99.6 3.3 %collective-permute-start.15 = (bf16[11,16,1024]{2,1,0:T(8,128)(2,1)}, bf16[11,16,1024]{2,1,0:T(8,128)(2,1)S(1)}, u32[]{:S(2)}, u32[]{:S(2)}) collective-permute-start(bf16[11,16,1024]{2,1,0:T(8,128)(2,1)} %get-tuple-element.172), channel_id=1, source_target_pairs={{0,20},{4,16},{8,28},{12,24},{16,4},{20,0},{24,12},{28,8},{1,21},{... | collective-permute-start | bytes 1081352 | tf_op jit(solution)/shard_map/ppermute | solution.py:516
  102.8 0.9 shard_map.146
  103.7 3.4 %all-to-all-start.4 = ((bf16[8,40,128]{2,1,0:T(8,128)(2,1)}), bf16[8,40,128]{2,1,0:T(8,128)(2,1)S(1)}, u32[]{:S(2)}, u32[]{:S(2)}) async-start(bf16[8,40,128]{2,1,0:T(8,128)(2,1)} %shard_map.146), calls=%async_computation.4 | async-start | bytes 163840 | tf_op jit(solution)/shard_map/all_to_all | solution.py:666
  107.2 1.4 %shard_map.147.refs_2_ = bf16[128,16,1024]{2,1,0:T(8,128)(2,1)} custom-call(s32[2]{0:T(128)S(1)} %pad_add_fusion.2.place_ref, bf16[11,16,1024]{2,1,0:T(8,128)(2,1)S(1)} %collective-permute-done.12.refs_0_, bf16[11,16,1024]{2,1,0:T(8,128)(2,1)S(1)} %collective-permute-done.13.refs_1_, ...), custom_call_target="tpu_custom_call", output_to_operand_aliasing={{}: (3, {})} | custom-call | bytes 1441792 | tf_op jit(solution)/shard_map/pallas_call | solution.py:156
  108.6 12.1 %all-to-all-done.4.part_ref = bf16[8,40,128]{2,1,0:T(8,128)(2,1)S(1)} async-done(((bf16[8,40,128]{2,1,0:T(8,128)(2,1)}), bf16[8,40,128]{2,1,0:T(8,128)(2,1)S(1)}, u32[]{:S(2)}, u32[]{:S(2)}) %all-to-all-start.4) | async-done | bytes 81952 | tf_op jit(solution)/shard_map/all_to_all | solution.py:666
  120.7 2.0 %collective-permute-start.19 = (bf16[7,16,1024]{2,1,0:T(8,128)(2,1)S(1)}, bf16[7,16,1024]{2,1,0:T(8,128)(2,1)S(1)}, u32[]{:S(2)}, u32[]{:S(2)}) collective-permute-start(bf16[7,16,1024]{2,1,0:T(8,128)(2,1)S(1)} %copy-done.16), channel_id=1, source_target_pairs={{0,28},{4,24},{8,20},{12,16},{16,12},{20,8},{24,4},{28,0},{1,29},{... | collective-permute-start | bytes 688136 | tf_op jit(solution)/shard_map/ppermute | solution.py:516
  122.7 0.9 shard_map.148
  123.7 1.8 %collective-permute-start.17 = (f32[10,512]{1,0:T(8,128)S(1)}, f32[10,512]{1,0:T(8,128)S(1)}, u32[]{:S(2)}, u32[]{:S(2)}) collective-permute-start(f32[10,512]{1,0:T(8,128)S(1)} %get-tuple-element.187), channel_id=1, source_target_pairs={{0,2},{1,3},{2,0},{3,1},{4,6},{5,7},{6,4},{7,5},{8,10},{9,11},{10,... | collective-permute-start | bytes 61448 | tf_op jit(solution)/shard_map/ppermute | solution.py:516
  125.6 1.4 %shard_map.149.refs_1_ = bf16[128,16,1024]{2,1,0:T(8,128)(2,1)} custom-call(s32[2]{0:T(128)S(1)} %pad_add_fusion.3.place_ref, bf16[11,16,1024]{2,1,0:T(8,128)(2,1)S(1)} %collective-permute-done.14.refs_0_, bf16[11,16,1024]{2,1,0:T(8,128)(2,1)S(1)} %collective-permute-done.15.refs_1_, ...), custom_call_target="tpu_custom_call", output_to_operand_aliasing={{}: (3, {})} | custom-call | bytes 1441792 | tf_op jit(solution)/shard_map/pallas_call | solution.py:156
  127.1 0.6 collective-permute-done.17
  127.7 1.1 collective-permute-done.18
  128.8 1.2 collective-permute-done.19.refs_0_
  130.0 0.6 add_convert_fusion
  130.6 0.7 shard_map.150
  (56 shorter events, 3.4 us)
Async XLA Ops:
  0.6 16.1 %copy-start.1 = (bf16[1024,512]{1,0:T(8,128)(2,1)S(1)}, bf16[1024,512]{1,0:T(8,128)(2,1)}, u32[]{:S(2)}) copy-start(bf16[1024,512]{1,0:T(8,128)(2,1)} %query_ref.1) | copy-start | bytes 3145732
  0.6 16.1 %copy-start.3 = (bf16[1024,128]{1,0:T(8,128)(2,1)S(1)}, bf16[1024,128]{1,0:T(8,128)(2,1)}, u32[]{:S(2)}) copy-start(bf16[1024,128]{1,0:T(8,128)(2,1)} %keyval_ref.1) | copy-start | bytes 786436
  0.7 0.8 copy-start.6
  2.1 14.6 %all-to-all-start = ((bf16[8,5,1024]{2,1,0:T(8,128)(2,1)}), bf16[8,5,1024]{2,1,0:T(8,128)(2,1)S(1)}, u32[]{:S(2)}, u32[]{:S(2)}) async-start(bf16[8,5,1024]{2,1,0:T(8,128)(2,1)} %shard_map.137), calls=%async_computation | async-start | bytes 262144 | tf_op jit(solution)/shard_map/all_to_all | solution.py:525
  10.0 6.7 %copy-start.7 = (s32[2]{0:T(128)S(1)}, s32[2]{0:T(128)}, u32[]{:S(2)}) copy-start(s32[2]{0:T(128)} %pad_add_fusion.me_ref) | copy-start | bytes 28
  10.0 43.9 %copy-start.10 = (s32[8]{0:T(128)S(1)}, s32[8]{0:T(128)}, u32[]{:S(2)}) copy-start(s32[8]{0:T(128)} %kept_ref.1) | copy-start | bytes 100
  17.7 8.8 %collective-permute-start.3 = (bf16[4,16,1024]{2,1,0:T(8,128)(2,1)}, bf16[4,16,1024]{2,1,0:T(8,128)(2,1)S(1)}, u32[]{:S(2)}, u32[]{:S(2)}) collective-permute-start(bf16[4,16,1024]{2,1,0:T(8,128)(2,1)} %get-tuple-element.116), channel_id=1, source_target_pairs={{0,28},{4,24},{8,20},{12,16},{16,12},{20,8},{24,4},{28,0},{1,29},{... | collective-permute-start | bytes 393224 | tf_op jit(solution)/shard_map/ppermute | solution.py:516
  21.5 2.4 %collective-permute-start = (f32[40,256]{1,0:T(8,128)S(1)}, f32[40,256]{1,0:T(8,128)S(1)}, u32[]{:S(2)}, u32[]{:S(2)}) collective-permute-start(f32[40,256]{1,0:T(8,128)S(1)} %get-tuple-element.113), channel_id=1, source_target_pairs={{0,1},{1,0},{2,3},{3,2},{4,5},{5,4},{6,7},{7,6},{8,9},{9,8},{10,11... | collective-permute-start | bytes 122888 | tf_op jit(solution)/shard_map/ppermute | solution.py:516
  21.5 4.0 %collective-permute-start.1 = (f32[40,256]{1,0:T(8,128)S(1)}, f32[40,256]{1,0:T(8,128)S(1)}, u32[]{:S(2)}, u32[]{:S(2)}) collective-permute-start(f32[40,256]{1,0:T(8,128)S(1)} %get-tuple-element.114), channel_id=1, source_target_pairs={{0,2},{1,3},{2,0},{3,1},{4,6},{5,7},{6,4},{7,5},{8,10},{9,11},{10,... | collective-permute-start | bytes 122888 | tf_op jit(solution)/shard_map/ppermute | solution.py:516
  23.0 3.5 %collective-permute-start.2 = (f32[40,256]{1,0:T(8,128)S(1)}, f32[40,256]{1,0:T(8,128)S(1)}, u32[]{:S(2)}, u32[]{:S(2)}) collective-permute-start(f32[40,256]{1,0:T(8,128)S(1)} %get-tuple-element.115), channel_id=1, source_target_pairs={{0,3},{1,2},{2,1},{3,0},{4,7},{5,6},{6,5},{7,4},{8,11},{9,10},{10,... | collective-permute-start | bytes 122888 | tf_op jit(solution)/shard_map/ppermute | solution.py:516
  23.3 19.2 %collective-permute-start.4 = (bf16[11,16,1024]{2,1,0:T(8,128)(2,1)}, bf16[11,16,1024]{2,1,0:T(8,128)(2,1)S(1)}, u32[]{:S(2)}, u32[]{:S(2)}) collective-permute-start(bf16[11,16,1024]{2,1,0:T(8,128)(2,1)} %get-tuple-element.127), channel_id=1, source_target_pairs={{0,24},{4,28},{8,16},{12,20},{16,8},{20,12},{24,0},{28,4},{1,25},{... | collective-permute-start | bytes 1081352 | tf_op jit(solution)/shard_map/ppermute | solution.py:516
  26.5 23.8 %collective-permute-start.5 = (bf16[11,16,1024]{2,1,0:T(8,128)(2,1)}, bf16[11,16,1024]{2,1,0:T(8,128)(2,1)S(1)}, u32[]{:S(2)}, u32[]{:S(2)}) collective-permute-start(bf16[11,16,1024]{2,1,0:T(8,128)(2,1)} %get-tuple-element.128), channel_id=1, source_target_pairs={{0,4},{4,0},{8,12},{12,8},{16,20},{20,16},{24,28},{28,24},{1,5},{5... | collective-permute-start | bytes 1081352 | tf_op jit(solution)/shard_map/ppermute | solution.py:516
  27.1 0.7 copy-start.9
  28.5 21.9 %all-to-all-start.1 = ((bf16[8,48,256]{2,1,0:T(8,128)(2,1)}), bf16[8,48,256]{2,1,0:T(8,128)(2,1)S(1)}, u32[]{:S(2)}, u32[]{:S(2)}) async-start(bf16[8,48,256]{2,1,0:T(8,128)(2,1)} %shard_map.140), calls=%async_computation.1 | async-start | bytes 393216 | tf_op jit(solution)/shard_map/all_to_all | solution.py:596
  50.3 30.5 %all-to-all-start.2 = ((bf16[40,16,1024]{2,1,0:T(8,128)(2,1)}), bf16[40,16,1024]{2,1,0:T(8,128)(2,1)S(1)}, u32[]{:S(2)}, u32[]{:S(2)}) async-start(bf16[40,16,1024]{2,1,0:T(8,128)(2,1)} %get-tuple-element.153), calls=%async_computation.2 | async-start | bytes 2621440 | tf_op jit(solution)/shard_map/all_to_all | solution.py:551
  55.3 3.4 %copy-start = (bf16[128,1024]{1,0:T(8,128)(2,1)}, bf16[128,1024]{1,0:T(8,128)(2,1)S(1)}, u32[]{:S(2)}) copy-start(bf16[128,1024]{1,0:T(8,128)(2,1)S(1)} %get-tuple-element.141.refs_6_.refs_7_) | copy-start | bytes 786436
  55.3 3.4 %copy-start.5 = (bf16[8,40,128]{2,1,0:T(8,128)(2,1)}, bf16[8,40,128]{2,1,0:T(8,128)(2,1)S(1)}, u32[]{:S(2)}) copy-start(bf16[8,40,128]{2,1,0:T(8,128)(2,1)S(1)} %get-tuple-element.137.refs_0_) | copy-start | bytes 245764
  55.3 3.4 %collective-permute-start.6 = (bf16[8,40,128]{2,1,0:T(8,128)(2,1)S(1)}, bf16[8,40,128]{2,1,0:T(8,128)(2,1)S(1)}, u32[]{:S(2)}, u32[]{:S(2)}) collective-permute-start(bf16[8,40,128]{2,1,0:T(8,128)(2,1)S(1)} %get-tuple-element.137.refs_0_), channel_id=1, source_target_pairs={{0,1},{1,0},{2,3},{3,2},{4,5},{5,4},{6,7},{7,6},{8,9},{9,8},{10,11... | collective-permute-start | bytes 245768 | tf_op jit(solution)/shard_map/ppermute | solution.py:516
  55.3 5.1 %collective-permute-start.7 = (bf16[8,40,128]{2,1,0:T(8,128)(2,1)S(1)}, bf16[8,40,128]{2,1,0:T(8,128)(2,1)S(1)}, u32[]{:S(2)}, u32[]{:S(2)}) collective-permute-start(bf16[8,40,128]{2,1,0:T(8,128)(2,1)S(1)} %get-tuple-element.137.refs_0_), channel_id=1, source_target_pairs={{0,2},{1,3},{2,0},{3,1},{4,6},{5,7},{6,4},{7,5},{8,10},{9,11},{10,... | collective-permute-start | bytes 245768 | tf_op jit(solution)/shard_map/ppermute | solution.py:516
  56.9 4.7 %collective-permute-start.8 = (bf16[8,40,128]{2,1,0:T(8,128)(2,1)S(1)}, bf16[8,40,128]{2,1,0:T(8,128)(2,1)S(1)}, u32[]{:S(2)}, u32[]{:S(2)}) collective-permute-start(bf16[8,40,128]{2,1,0:T(8,128)(2,1)S(1)} %get-tuple-element.137.refs_0_), channel_id=1, source_target_pairs={{0,3},{1,2},{2,1},{3,0},{4,7},{5,6},{6,5},{7,4},{8,11},{9,10},{10,... | collective-permute-start | bytes 245768 | tf_op jit(solution)/shard_map/ppermute | solution.py:516
  58.7 3.0 %copy-start.11 = (bf16[8,40,128]{2,1,0:T(8,128)(2,1)}, bf16[8,40,128]{2,1,0:T(8,128)(2,1)S(1)}, u32[]{:S(2)}) copy-start(bf16[8,40,128]{2,1,0:T(8,128)(2,1)S(1)} %collective-permute-done.6.refs_1_) | copy-start | bytes 245764
  60.4 1.3 %copy-start.12 = (bf16[8,40,128]{2,1,0:T(8,128)(2,1)}, bf16[8,40,128]{2,1,0:T(8,128)(2,1)S(1)}, u32[]{:S(2)}) copy-start(bf16[8,40,128]{2,1,0:T(8,128)(2,1)S(1)} %collective-permute-done.7.refs_2_) | copy-start | bytes 245764
  61.7 0.6 copy-start.13
  62.3 12.5 %copy-start.15 = (bf16[11,16,1024]{2,1,0:T(8,128)(2,1)S(1)}, bf16[11,16,1024]{2,1,0:T(8,128)(2,1)}, u32[]{:S(2)}) copy-start(bf16[11,16,1024]{2,1,0:T(8,128)(2,1)} %get-tuple-element.160) | copy-start | bytes 1081348
  62.3 15.3 %copy-start.14 = (bf16[11,16,1024]{2,1,0:T(8,128)(2,1)S(1)}, bf16[11,16,1024]{2,1,0:T(8,128)(2,1)}, u32[]{:S(2)}) copy-start(bf16[11,16,1024]{2,1,0:T(8,128)(2,1)} %get-tuple-element.161) | copy-start | bytes 1081348
  72.6 7.4 %collective-permute-start.10 = (bf16[8,64,128]{2,1,0:T(8,128)(2,1)}, bf16[8,64,128]{2,1,0:T(8,128)(2,1)S(1)}, u32[]{:S(2)}, u32[]{:S(2)}) collective-permute-start(bf16[8,64,128]{2,1,0:T(8,128)(2,1)} %get-tuple-element.151), channel_id=1, source_target_pairs={{0,2},{1,3},{2,0},{3,1},{4,6},{5,7},{6,4},{7,5},{8,10},{9,11},{10,... | collective-permute-start | bytes 393224 | tf_op jit(solution)/shard_map/ppermute | solution.py:516
  74.0 6.9 %collective-permute-start.11 = (bf16[8,64,128]{2,1,0:T(8,128)(2,1)}, bf16[8,64,128]{2,1,0:T(8,128)(2,1)S(1)}, u32[]{:S(2)}, u32[]{:S(2)}) collective-permute-start(bf16[8,64,128]{2,1,0:T(8,128)(2,1)} %get-tuple-element.152), channel_id=1, source_target_pairs={{0,3},{1,2},{2,1},{3,0},{4,7},{5,6},{6,5},{7,4},{8,11},{9,10},{10,... | collective-permute-start | bytes 393224 | tf_op jit(solution)/shard_map/ppermute | solution.py:516
  74.3 6.5 %collective-permute-start.9 = (bf16[8,64,128]{2,1,0:T(8,128)(2,1)}, bf16[8,64,128]{2,1,0:T(8,128)(2,1)S(1)}, u32[]{:S(2)}, u32[]{:S(2)}) collective-permute-start(bf16[8,64,128]{2,1,0:T(8,128)(2,1)} %get-tuple-element.150), channel_id=1, source_target_pairs={{0,1},{1,0},{2,3},{3,2},{4,5},{5,4},{6,7},{7,6},{8,9},{9,8},{10,11... | collective-permute-start | bytes 393224 | tf_op jit(solution)/shard_map/ppermute | solution.py:516
  74.8 21.3 %collective-permute-start.12 = (bf16[11,16,1024]{2,1,0:T(8,128)(2,1)S(1)}, bf16[11,16,1024]{2,1,0:T(8,128)(2,1)S(1)}, u32[]{:S(2)}, u32[]{:S(2)}) collective-permute-start(bf16[11,16,1024]{2,1,0:T(8,128)(2,1)S(1)} %copy-done.15), channel_id=1, source_target_pairs={{0,12},{4,8},{8,4},{12,0},{16,28},{20,24},{24,20},{28,16},{1,13},{... | collective-permute-start | bytes 1081352 | tf_op jit(solution)/shard_map/ppermute | solution.py:516
  77.6 19.5 %collective-permute-start.13 = (bf16[11,16,1024]{2,1,0:T(8,128)(2,1)S(1)}, bf16[11,16,1024]{2,1,0:T(8,128)(2,1)S(1)}, u32[]{:S(2)}, u32[]{:S(2)}) collective-permute-start(bf16[11,16,1024]{2,1,0:T(8,128)(2,1)S(1)} %copy-done.14), channel_id=1, source_target_pairs={{0,16},{4,20},{8,24},{12,28},{16,0},{20,4},{24,8},{28,12},{1,17},{... | collective-permute-start | bytes 1081352 | tf_op jit(solution)/shard_map/ppermute | solution.py:516
  80.8 0.9 copy-start.4
  82.8 16.4 %all-to-all-start.3 = ((bf16[8,64,128]{2,1,0:T(8,128)(2,1)}), bf16[8,64,128]{2,1,0:T(8,128)(2,1)S(1)}, u32[]{:S(2)}, u32[]{:S(2)}) async-start(bf16[8,64,128]{2,1,0:T(8,128)(2,1)} %shard_map.144), calls=%async_computation.3 | async-start | bytes 262144 | tf_op jit(solution)/shard_map/all_to_all | solution.py:661
  99.2 21.5 %collective-permute-start.14 = (bf16[11,16,1024]{2,1,0:T(8,128)(2,1)}, bf16[11,16,1024]{2,1,0:T(8,128)(2,1)S(1)}, u32[]{:S(2)}, u32[]{:S(2)}) collective-permute-start(bf16[11,16,1024]{2,1,0:T(8,128)(2,1)} %get-tuple-element.171), channel_id=1, source_target_pairs={{0,8},{4,12},{8,0},{12,4},{16,24},{20,28},{24,16},{28,20},{1,9},{5... | collective-permute-start | bytes 1081352 | tf_op jit(solution)/shard_map/ppermute | solution.py:516
  99.6 21.1 %collective-permute-start.15 = (bf16[11,16,1024]{2,1,0:T(8,128)(2,1)}, bf16[11,16,1024]{2,1,0:T(8,128)(2,1)S(1)}, u32[]{:S(2)}, u32[]{:S(2)}) collective-permute-start(bf16[11,16,1024]{2,1,0:T(8,128)(2,1)} %get-tuple-element.172), channel_id=1, source_target_pairs={{0,20},{4,16},{8,28},{12,24},{16,4},{20,0},{24,12},{28,8},{1,21},{... | collective-permute-start | bytes 1081352 | tf_op jit(solution)/shard_map/ppermute | solution.py:516
  103.7 16.9 %all-to-all-start.4 = ((bf16[8,40,128]{2,1,0:T(8,128)(2,1)}), bf16[8,40,128]{2,1,0:T(8,128)(2,1)S(1)}, u32[]{:S(2)}, u32[]{:S(2)}) async-start(bf16[8,40,128]{2,1,0:T(8,128)(2,1)} %shard_map.146), calls=%async_computation.4 | async-start | bytes 163840 | tf_op jit(solution)/shard_map/all_to_all | solution.py:666
  107.2 13.5 %copy-start.16 = (bf16[7,16,1024]{2,1,0:T(8,128)(2,1)S(1)}, bf16[7,16,1024]{2,1,0:T(8,128)(2,1)}, u32[]{:S(2)}) copy-start(bf16[7,16,1024]{2,1,0:T(8,128)(2,1)} %get-tuple-element.189) | copy-start | bytes 688132
  107.2 15.5 %copy-start.2 = (bf16[1024,512]{1,0:T(8,128)(2,1)S(1)}, bf16[1024,512]{1,0:T(8,128)(2,1)}, u32[]{:S(2)}) copy-start(bf16[1024,512]{1,0:T(8,128)(2,1)} %weight_ref.1) | copy-start | bytes 3145732
  107.2 15.5 %copy-start.8 = (s32[2]{0:T(128)S(1)}, s32[2]{0:T(128)}, u32[]{:S(2)}) copy-start(s32[2]{0:T(128)} %pad_add_fusion.me_ref) | copy-start | bytes 28
  120.7 9.3 %collective-permute-start.19 = (bf16[7,16,1024]{2,1,0:T(8,128)(2,1)S(1)}, bf16[7,16,1024]{2,1,0:T(8,128)(2,1)S(1)}, u32[]{:S(2)}, u32[]{:S(2)}) collective-permute-start(bf16[7,16,1024]{2,1,0:T(8,128)(2,1)S(1)} %copy-done.16), channel_id=1, source_target_pairs={{0,28},{4,24},{8,20},{12,16},{16,12},{20,8},{24,4},{28,0},{1,29},{... | collective-permute-start | bytes 688136 | tf_op jit(solution)/shard_map/ppermute | solution.py:516
  123.6 3.4 %collective-permute-start.16 = (f32[10,512]{1,0:T(8,128)S(1)}, f32[10,512]{1,0:T(8,128)S(1)}, u32[]{:S(2)}, u32[]{:S(2)}) collective-permute-start(f32[10,512]{1,0:T(8,128)S(1)} %get-tuple-element.186), channel_id=1, source_target_pairs={{0,1},{1,0},{2,3},{3,2},{4,5},{5,4},{6,7},{7,6},{8,9},{9,8},{10,11... | collective-permute-start | bytes 61448 | tf_op jit(solution)/shard_map/ppermute | solution.py:516
  123.7 4.0 %collective-permute-start.17 = (f32[10,512]{1,0:T(8,128)S(1)}, f32[10,512]{1,0:T(8,128)S(1)}, u32[]{:S(2)}, u32[]{:S(2)}) collective-permute-start(f32[10,512]{1,0:T(8,128)S(1)} %get-tuple-element.187), channel_id=1, source_target_pairs={{0,2},{1,3},{2,0},{3,1},{4,6},{5,7},{6,4},{7,5},{8,10},{9,11},{10,... | collective-permute-start | bytes 61448 | tf_op jit(solution)/shard_map/ppermute | solution.py:516
  125.5 3.3 %collective-permute-start.18 = (f32[10,512]{1,0:T(8,128)S(1)}, f32[10,512]{1,0:T(8,128)S(1)}, u32[]{:S(2)}, u32[]{:S(2)}) collective-permute-start(f32[10,512]{1,0:T(8,128)S(1)} %get-tuple-element.188), channel_id=1, source_target_pairs={{0,3},{1,2},{2,1},{3,0},{4,7},{5,6},{6,5},{7,4},{8,11},{9,10},{10,... | collective-permute-start | bytes 61448 | tf_op jit(solution)/shard_map/ppermute | solution.py:516

commit v22 on v20

--- a/solution.py
+++ b/solution.py
@@ -648,13 +648,14 @@
 
     queries, moved_pool = lax.optimization_barrier((queries, placed(moved_pool)))
     mixed = attend(both, lengths, queries, keyval, tokens, token_info, rows, piece)
+    mixed = launch(mixed, 3, 4)
     if direct:
         mixed = land(deal(mixed, "narrow"), 0)
     else:
         mixed = land(exchange(mixed[0], "narrow"), 0)
         mixed = mixed.reshape((narrow, wide) + mixed.shape[1:])
         mixed = [mixed[i] for i in range(narrow)]
-    mixed = combine(launch(mixed, 3, 4), piece)
+    mixed = combine(mixed, piece)
     mixed, pages = lax.optimization_barrier((mixed, moved_pool))
     pages = placed(pages)
     mixed = land(exchange(mixed, "wide"), 3, 4)

time: 137 us -> 133 us (0.971)
  waiting for transfers between devices: 42.4 us -> 35.7 us
  starting transfers between devices: 41.4 us -> 44 us
    all_to_all x1, waiting for transfers between devices: 11.4 us -> 0.9 us  [on_device(): mixed = land(exchange(mixed, 'wide'), 3, 4)]
    all_to_all x1, waiting for transfers between devices: 3.02 us -> 5.81 us  [launch(): flying[c] = send(chunk, 'wide', d) if d else exchange(chunk, 'wide')]
    ppermute x20, starting transfers between devices: 23.3 us -> 25.7 us  [send(): lax.ppermute(block, axis, [(i, i ^ d) for i in range(lax.axis_size(axis))])]
  transfers between devices with their start and end apart: 24 -> 24, of which waited for: 13 -> 13; matrix products, arithmetic and copies ran while one was open for 1% -> 1% of each run, Pallas kernels for 19% -> 20%
where the time goes in v22:
time: 133 us; the launch traced here: 132 us
  starting transfers between devices  44 us (33%)
  waiting for transfers between devices  35.7 us (27%)
  Pallas kernels  28.5 us (21%)
  blocking collectives  18 us (14%)
  local copies, waits for them, and re-layouts  3.07 us (2%)
  other arithmetic  1.4 us (1%)
    ppermute x20, starting transfers between devices, send(): lax.ppermute(block, axis, [(i, i ^ d) for i in range(lax.axis_size(axis))])  25.7 us
    all_to_all x1, blocking collectives, on_device(): received = land(exchange(packed, 'wide'), 6, 1)  18 us
    ppermute x20, waiting for transfers between devices, send(): lax.ppermute(block, axis, [(i, i ^ d) for i in range(lax.axis_size(axis))])  16.4 us
    all_to_all x1, waiting for transfers between devices, on_device(): attn = land(exchange(attn, 'wide'), 2, 5)  11.5 us
    pallas_call x1, Pallas kernels, attend(): pl.pallas_call(functools.partial(attend_kernel, rows, piece, peers), grid...  10.3 us
    all_to_all x1, starting transfers between devices, on_device(): gathered = exchange(in_vmem(repeat_kernel, copies, None, hidden), 'wide')  7.28 us
    pallas_call x5, Pallas kernels, place_pages(): pl.pallas_call(functools.partial(place_kernel, counts), out_shape=jax.Sha...  6.64 us
    all_to_all x1, waiting for transfers between devices, launch(): flying[c] = send(chunk, 'wide', d) if d else exchange(chunk, 'wide')  5.81 us
  transfers between devices with their start and end apart: 24, of which 13 were waited for; matrix products, arithmetic and copies ran while one was open for 1% of the time, Pallas kernels for 20%

profile of v22, /device:TPU:0, one launch (start us, length us, event | category | flops | bytes accessed | tf_op | source)
XLA Modules:
  0.0 131.5 jit_solution(388411688202186470)
XLA Ops:
  0.7 0.8 copy-done.6
  1.5 0.7 shard_map.137
  2.1 7.3 %all-to-all-start = ((bf16[8,5,1024]{2,1,0:T(8,128)(2,1)}), bf16[8,5,1024]{2,1,0:T(8,128)(2,1)S(1)}, u32[]{:S(2)}, u32[]{:S(2)}) async-start(bf16[8,5,1024]{2,1,0:T(8,128)(2,1)} %shard_map.137), calls=%async_computation | async-start | bytes 262144 | tf_op jit(solution)/shard_map/all_to_all | solution.py:525
  10.0 5.7 %shard_map.138 = (bf16[128,16,1024]{2,1,0:T(8,128)(2,1)}, f32[8,128]{1,0:T(8,128)}, f32[8,2048]{1,0:T(8,128)}, bf16[40,16,1024]{2,1,0:T(8,128)(2,1)}, bf16[11,16...) custom-call(s32[2]{0:T(128)} %pad_add_fusion.me_ref, ...), custom_call_target="tpu_custom_call" | custom-call | bytes 8388608 | tf_op jit(solution)/shard_map/pallas_call | solution.py:118
  15.6 1.1 all-to-all-done.hidden_ref
  16.8 1.0 shard_map.139
  17.8 3.7 %collective-permute-start.3 = (bf16[4,16,1024]{2,1,0:T(8,128)(2,1)}, bf16[4,16,1024]{2,1,0:T(8,128)(2,1)S(1)}, u32[]{:S(2)}, u32[]{:S(2)}) collective-permute-start(bf16[4,16,1024]{2,1,0:T(8,128)(2,1)} %get-tuple-element.115), channel_id=1, source_target_pairs={{0,28},{4,24},{8,20},{12,16},{16,12},{20,8},{24,4},{28,0},{1,29},{... | collective-permute-start | bytes 393224 | tf_op jit(solution)/shard_map/ppermute | solution.py:516
  21.5 1.5 %collective-permute-start.1 = (f32[40,256]{1,0:T(8,128)S(1)}, f32[40,256]{1,0:T(8,128)S(1)}, u32[]{:S(2)}, u32[]{:S(2)}) collective-permute-start(f32[40,256]{1,0:T(8,128)S(1)} %get-tuple-element.113), channel_id=1, source_target_pairs={{0,2},{1,3},{2,0},{3,1},{4,6},{5,7},{6,4},{7,5},{8,10},{9,11},{10,... | collective-permute-start | bytes 122888 | tf_op jit(solution)/shard_map/ppermute | solution.py:516
  23.3 2.1 %collective-permute-done.1.refs_2_ = f32[40,256]{1,0:T(8,128)S(1)} collective-permute-done((f32[40,256]{1,0:T(8,128)S(1)}, f32[40,256]{1,0:T(8,128)S(1)}, u32[]{:S(2)}, u32[]{:S(2)}) %collective-permute-start.1) | collective-permute-done | bytes 40992 | tf_op jit(solution)/shard_map/ppermute | solution.py:516
  25.5 1.0 collective-permute-done.2.refs_3_
  26.5 1.9 %collective-permute-start.4 = (bf16[11,16,1024]{2,1,0:T(8,128)(2,1)}, bf16[11,16,1024]{2,1,0:T(8,128)(2,1)S(1)}, u32[]{:S(2)}, u32[]{:S(2)}) collective-permute-start(bf16[11,16,1024]{2,1,0:T(8,128)(2,1)} %get-tuple-element.127), channel_id=1, source_target_pairs={{0,24},{4,28},{8,16},{12,20},{16,8},{20,12},{24,0},{28,4},{1,25},{... | collective-permute-start | bytes 1081352 | tf_op jit(solution)/shard_map/ppermute | solution.py:516
  28.4 1.5 %collective-permute-start.5 = (bf16[11,16,1024]{2,1,0:T(8,128)(2,1)}, bf16[11,16,1024]{2,1,0:T(8,128)(2,1)S(1)}, u32[]{:S(2)}, u32[]{:S(2)}) collective-permute-start(bf16[11,16,1024]{2,1,0:T(8,128)(2,1)} %get-tuple-element.128), channel_id=1, source_target_pairs={{0,4},{4,0},{8,12},{12,8},{16,20},{20,16},{24,28},{28,24},{1,5},{5... | collective-permute-start | bytes 1081352 | tf_op jit(solution)/shard_map/ppermute | solution.py:516
  29.9 0.7 copy-done.9
  30.6 18.0 %all_to_all.25.part_ref = bf16[8,48,256]{2,1,0:T(8,128)(2,1)S(1)} all-to-all(bf16[8,48,256]{2,1,0:T(8,128)(2,1)S(1)} %shard_map.140), channel_id=1, replica_groups=mesh['wide'=8,'narrow'=4] {'wide'}, dimensions={0} | all-to-all | bytes 393216 | tf_op jit(solution)/shard_map/all_to_all | solution.py:596
  48.6 3.6 %all-to-all-start.2 = ((bf16[40,16,1024]{2,1,0:T(8,128)(2,1)}), bf16[40,16,1024]{2,1,0:T(8,128)(2,1)S(1)}, u32[]{:S(2)}, u32[]{:S(2)}) async-start(bf16[40,16,1024]{2,1,0:T(8,128)(2,1)} %get-tuple-element.153), calls=%async_computation.2 | async-start | bytes 2621440 | tf_op jit(solution)/shard_map/all_to_all | solution.py:551
  52.2 1.4 %shard_map.141 = (bf16[8,40,128]{2,1,0:T(8,128)(2,1)S(1)}, bf16[128,1024]{1,0:T(8,128)(2,1)S(1)}, bf16[1,5,1024]{2,1,0:T(8,128)(2,1)}, s32[1,128]{1,0:T(1,128)}, s32[1,128]{1,0:T(1,128)}) custom-call(s32[2]{0:T(128)S(1)} %copy-done.7, s32[8]{0:T(128)S(1)} %copy-done.10, bf16[8,48,256]{2,1,0:T(8,128)(2,1)S(1)} %all_to_all.25.part_ref), custom_call_target="tpu_custom_call" | custom-call | flops 1 | bytes 1 | tf_op jit(solution)/shard_map/pallas_call | solution.py:471
  53.5 1.6 %collective-permute-start.7 = (bf16[8,40,128]{2,1,0:T(8,128)(2,1)S(1)}, bf16[8,40,128]{2,1,0:T(8,128)(2,1)S(1)}, u32[]{:S(2)}, u32[]{:S(2)}) collective-permute-start(bf16[8,40,128]{2,1,0:T(8,128)(2,1)S(1)} %get-tuple-element.137.refs_0_), channel_id=1, source_target_pairs={{0,2},{1,3},{2,0},{3,1},{4,6},{5,7},{6,4},{7,5},{8,10},{9,11},{10,... | collective-permute-start | bytes 245768 | tf_op jit(solution)/shard_map/ppermute | solution.py:516
  55.5 1.5 %shard_map.142.refs_1_ = bf16[128,16,1024]{2,1,0:T(8,128)(2,1)} custom-call(s32[3]{0:T(128)S(1)} %pad_add_fusion.1.place_ref, bf16[11,16,1024]{2,1,0:T(8,128)(2,1)S(1)} %collective-permute-done.5.refs_0_, bf16[11,16,1024]{2,1,0:T(8,128)(2,1)S(1)} %collective-permute-done.4.refs_1_, ...), custom_call_target="tpu_custom_call", output_to_operand_aliasing={{}: (4, {})} | custom-call | bytes 1703936 | tf_op jit(solution)/shard_map/pallas_call | solution.py:156
  57.0 1.7 %collective-permute-done.7.refs_2_ = bf16[8,40,128]{2,1,0:T(8,128)(2,1)S(1)} collective-permute-done((bf16[8,40,128]{2,1,0:T(8,128)(2,1)S(1)}, bf16[8,40,128]{2,1,0:T(8,128)(2,1)S(1)}, u32[]{:S(2)}, u32[]{:S(2)}) %collective-permute-start.7) | collective-permute-done | bytes 81952 | tf_op jit(solution)/shard_map/ppermute | solution.py:516
  58.7 1.1 collective-permute-done.8.refs_3_
  59.9 0.6 copy-done.13
  60.5 10.3 %shard_map.143 = (bf16[8,64,128]{2,1,0:T(8,128)(2,1)}, bf16[8,64,128]{2,1,0:T(8,128)(2,1)}, bf16[8,64,128]{2,1,0:T(8,128)(2,1)}, bf16[8,64,128]{2,1,0:T(8,128)(2,1)}) custom-call(s32[2]{0:T(128)} %pad_add_fusion.me_ref, s32[8]{0:T(128)} %length_ref.1, bf16[8,40,128]{2,1,0:T(8,128)(2,1)} %copy-done.5, bf16[8,40,128]{2,1,0:T(8,128)(2,1)} %copy-done.11, ...), custom_call_target="tpu_custom_call" | custom-call | flops 1 | bytes 1 | tf_op jit(solution)/shard_map/pallas_call | solution.py:298
  70.7 1.4 %collective-permute-start.10 = (bf16[8,64,128]{2,1,0:T(8,128)(2,1)}, bf16[8,64,128]{2,1,0:T(8,128)(2,1)S(1)}, u32[]{:S(2)}, u32[]{:S(2)}) collective-permute-start(bf16[8,64,128]{2,1,0:T(8,128)(2,1)} %get-tuple-element.151), channel_id=1, source_target_pairs={{0,2},{1,3},{2,0},{3,1},{4,6},{5,7},{6,4},{7,5},{8,10},{9,11},{10,... | collective-permute-start | bytes 393224 | tf_op jit(solution)/shard_map/ppermute | solution.py:516
  72.9 2.8 %collective-permute-start.12 = (bf16[11,16,1024]{2,1,0:T(8,128)(2,1)}, bf16[11,16,1024]{2,1,0:T(8,128)(2,1)S(1)}, u32[]{:S(2)}, u32[]{:S(2)}) collective-permute-start(bf16[11,16,1024]{2,1,0:T(8,128)(2,1)} %get-tuple-element.160), channel_id=1, source_target_pairs={{0,12},{4,8},{8,4},{12,0},{16,28},{20,24},{24,20},{28,16},{1,13},{... | collective-permute-start | bytes 1081352 | tf_op jit(solution)/shard_map/ppermute | solution.py:516
  75.7 2.4 %collective-permute-start.13 = (bf16[11,16,1024]{2,1,0:T(8,128)(2,1)S(1)}, bf16[11,16,1024]{2,1,0:T(8,128)(2,1)S(1)}, u32[]{:S(2)}, u32[]{:S(2)}) collective-permute-start(bf16[11,16,1024]{2,1,0:T(8,128)(2,1)S(1)} %copy-done.15), channel_id=1, source_target_pairs={{0,16},{4,20},{8,24},{12,28},{16,0},{20,4},{24,8},{28,12},{1,17},{... | collective-permute-start | bytes 1081352 | tf_op jit(solution)/shard_map/ppermute | solution.py:516
  78.1 1.0 collective-permute-done.11.refs_3_
  79.2 5.8 %all-to-all-done.2.refs_0_ = bf16[40,16,1024]{2,1,0:T(8,128)(2,1)S(1)} async-done(((bf16[40,16,1024]{2,1,0:T(8,128)(2,1)}), bf16[40,16,1024]{2,1,0:T(8,128)(2,1)S(1)}, u32[]{:S(2)}, u32[]{:S(2)}) %all-to-all-start.2) | async-done | bytes 1310752 | tf_op jit(solution)/shard_map/all_to_all | solution.py:551
  85.0 0.9 copy-done.4
  85.9 1.1 shard_map.144
  87.0 3.4 %all-to-all-start.3 = ((bf16[8,64,128]{2,1,0:T(8,128)(2,1)}), bf16[8,64,128]{2,1,0:T(8,128)(2,1)S(1)}, u32[]{:S(2)}, u32[]{:S(2)}) async-start(bf16[8,64,128]{2,1,0:T(8,128)(2,1)} %shard_map.144), calls=%async_computation.3 | async-start | bytes 262144 | tf_op jit(solution)/shard_map/all_to_all | solution.py:661
  90.4 1.7 %shard_map.145.refs_2_ = bf16[128,16,1024]{2,1,0:T(8,128)(2,1)} custom-call(s32[8]{0:T(128)S(1)} %iota_multiply_fusion.place_ref, bf16[40,16,1024]{2,1,0:T(8,128)(2,1)S(1)} %all-to-all-done.2.refs_0_, bf16[128,16,1024]{2,1,0:T(8,128)(2,1)} %shard_map.142.refs_1_), custom_call_target="tpu_custom_call", output_to_operand_aliasing={{}: (2, {})} | custom-call | bytes 2621440 | tf_op jit(solution)/shard_map/pallas_call | solution.py:156
  92.1 0.6 collective-permute-done.12.refs_0_
  92.7 7.1 %collective-permute-done.13.refs_1_ = bf16[11,16,1024]{2,1,0:T(8,128)(2,1)S(1)} collective-permute-done((bf16[11,16,1024]{2,1,0:T(8,128)(2,1)S(1)}, bf16[11,16,1024]{2,1,0:T(8,128)(2,1)S(1)}, u32[]{:S(2)}, u32[]{:S(2)}) %collective-permute-start.13) | collective-permute-done | bytes 360480 | tf_op jit(solution)/shard_map/ppermute | solution.py:516
  99.8 0.9 all-to-all-done.3.refs_0_
  100.7 0.9 collective-permute-start.14
  101.6 1.6 %collective-permute-start.15 = (bf16[11,16,1024]{2,1,0:T(8,128)(2,1)S(1)}, bf16[11,16,1024]{2,1,0:T(8,128)(2,1)S(1)}, u32[]{:S(2)}, u32[]{:S(2)}) collective-permute-start(bf16[11,16,1024]{2,1,0:T(8,128)(2,1)S(1)} %copy-done.14), channel_id=1, source_target_pairs={{0,20},{4,16},{8,28},{12,24},{16,4},{20,0},{24,12},{28,8},{1,21},{... | collective-permute-start | bytes 1081352 | tf_op jit(solution)/shard_map/ppermute | solution.py:516
  103.2 0.9 shard_map.146
  104.1 4.0 %all-to-all-start.4 = ((bf16[8,40,128]{2,1,0:T(8,128)(2,1)}), bf16[8,40,128]{2,1,0:T(8,128)(2,1)S(1)}, u32[]{:S(2)}, u32[]{:S(2)}) async-start(bf16[8,40,128]{2,1,0:T(8,128)(2,1)} %shard_map.146), calls=%async_computation.4 | async-start | bytes 163840 | tf_op jit(solution)/shard_map/all_to_all | solution.py:666
  108.2 1.4 %shard_map.147.refs_2_ = bf16[128,16,1024]{2,1,0:T(8,128)(2,1)} custom-call(s32[2]{0:T(128)S(1)} %pad_add_fusion.2.place_ref, bf16[11,16,1024]{2,1,0:T(8,128)(2,1)S(1)} %collective-permute-done.12.refs_0_, bf16[11,16,1024]{2,1,0:T(8,128)(2,1)S(1)} %collective-permute-done.13.refs_1_, ...), custom_call_target="tpu_custom_call", output_to_operand_aliasing={{}: (3, {})} | custom-call | bytes 1441792 | tf_op jit(solution)/shard_map/pallas_call | solution.py:156
  109.7 11.5 %all-to-all-done.4.part_ref = bf16[8,40,128]{2,1,0:T(8,128)(2,1)S(1)} async-done(((bf16[8,40,128]{2,1,0:T(8,128)(2,1)}), bf16[8,40,128]{2,1,0:T(8,128)(2,1)S(1)}, u32[]{:S(2)}, u32[]{:S(2)}) %all-to-all-start.4) | async-done | bytes 81952 | tf_op jit(solution)/shard_map/all_to_all | solution.py:666
  121.2 3.1 %collective-permute-start.19 = (bf16[7,16,1024]{2,1,0:T(8,128)(2,1)}, bf16[7,16,1024]{2,1,0:T(8,128)(2,1)S(1)}, u32[]{:S(2)}, u32[]{:S(2)}) collective-permute-start(bf16[7,16,1024]{2,1,0:T(8,128)(2,1)} %get-tuple-element.189), channel_id=1, source_target_pairs={{0,28},{4,24},{8,20},{12,16},{16,12},{20,8},{24,4},{28,0},{1,29},{... | collective-permute-start | bytes 688136 | tf_op jit(solution)/shard_map/ppermute | solution.py:516
  124.3 0.9 shard_map.148
  125.3 1.6 %collective-permute-start.17 = (f32[10,512]{1,0:T(8,128)S(1)}, f32[10,512]{1,0:T(8,128)S(1)}, u32[]{:S(2)}, u32[]{:S(2)}) collective-permute-start(f32[10,512]{1,0:T(8,128)S(1)} %get-tuple-element.187), channel_id=1, source_target_pairs={{0,2},{1,3},{2,0},{3,1},{4,6},{5,7},{6,4},{7,5},{8,10},{9,11},{10,... | collective-permute-start | bytes 61448 | tf_op jit(solution)/shard_map/ppermute | solution.py:516
  127.2 1.4 %shard_map.149.refs_1_ = bf16[128,16,1024]{2,1,0:T(8,128)(2,1)} custom-call(s32[2]{0:T(128)S(1)} %pad_add_fusion.3.place_ref, bf16[11,16,1024]{2,1,0:T(8,128)(2,1)S(1)} %collective-permute-done.14.refs_0_, bf16[11,16,1024]{2,1,0:T(8,128)(2,1)S(1)} %collective-permute-done.15.refs_1_, ...), custom_call_target="tpu_custom_call", output_to_operand_aliasing={{}: (3, {})} | custom-call | bytes 1441792 | tf_op jit(solution)/shard_map/pallas_call | solution.py:156
  128.6 0.6 collective-permute-done.17
  129.3 0.9 collective-permute-done.18
  130.2 0.6 add_convert_fusion
  130.8 0.7 shard_map.150
  (53 shorter events, 2.7 us)
Async XLA Ops:
  0.6 16.1 %copy-start.1 = (bf16[1024,512]{1,0:T(8,128)(2,1)S(1)}, bf16[1024,512]{1,0:T(8,128)(2,1)}, u32[]{:S(2)}) copy-start(bf16[1024,512]{1,0:T(8,128)(2,1)} %query_ref.1) | copy-start | bytes 3145732
  0.6 16.1 %copy-start.3 = (bf16[1024,128]{1,0:T(8,128)(2,1)S(1)}, bf16[1024,128]{1,0:T(8,128)(2,1)}, u32[]{:S(2)}) copy-start(bf16[1024,128]{1,0:T(8,128)(2,1)} %keyval_ref.1) | copy-start | bytes 786436
  0.7 0.8 copy-start.6
  2.1 14.6 %all-to-all-start = ((bf16[8,5,1024]{2,1,0:T(8,128)(2,1)}), bf16[8,5,1024]{2,1,0:T(8,128)(2,1)S(1)}, u32[]{:S(2)}, u32[]{:S(2)}) async-start(bf16[8,5,1024]{2,1,0:T(8,128)(2,1)} %shard_map.137), calls=%async_computation | async-start | bytes 262144 | tf_op jit(solution)/shard_map/all_to_all | solution.py:525
  10.0 6.8 %copy-start.7 = (s32[2]{0:T(128)S(1)}, s32[2]{0:T(128)}, u32[]{:S(2)}) copy-start(s32[2]{0:T(128)} %pad_add_fusion.me_ref) | copy-start | bytes 28
  10.0 42.2 %copy-start.10 = (s32[8]{0:T(128)S(1)}, s32[8]{0:T(128)}, u32[]{:S(2)}) copy-start(s32[8]{0:T(128)} %kept_ref.1) | copy-start | bytes 100
  17.8 8.7 %collective-permute-start.3 = (bf16[4,16,1024]{2,1,0:T(8,128)(2,1)}, bf16[4,16,1024]{2,1,0:T(8,128)(2,1)S(1)}, u32[]{:S(2)}, u32[]{:S(2)}) collective-permute-start(bf16[4,16,1024]{2,1,0:T(8,128)(2,1)} %get-tuple-element.115), channel_id=1, source_target_pairs={{0,28},{4,24},{8,20},{12,16},{16,12},{20,8},{24,4},{28,0},{1,29},{... | collective-permute-start | bytes 393224 | tf_op jit(solution)/shard_map/ppermute | solution.py:516
  21.5 1.9 %collective-permute-start = (f32[40,256]{1,0:T(8,128)S(1)}, f32[40,256]{1,0:T(8,128)S(1)}, u32[]{:S(2)}, u32[]{:S(2)}) collective-permute-start(f32[40,256]{1,0:T(8,128)S(1)} %get-tuple-element.112), channel_id=1, source_target_pairs={{0,1},{1,0},{2,3},{3,2},{4,5},{5,4},{6,7},{7,6},{8,9},{9,8},{10,11... | collective-permute-start | bytes 122888 | tf_op jit(solution)/shard_map/ppermute | solution.py:516
  21.5 4.0 %collective-permute-start.1 = (f32[40,256]{1,0:T(8,128)S(1)}, f32[40,256]{1,0:T(8,128)S(1)}, u32[]{:S(2)}, u32[]{:S(2)}) collective-permute-start(f32[40,256]{1,0:T(8,128)S(1)} %get-tuple-element.113), channel_id=1, source_target_pairs={{0,2},{1,3},{2,0},{3,1},{4,6},{5,7},{6,4},{7,5},{8,10},{9,11},{10,... | collective-permute-start | bytes 122888 | tf_op jit(solution)/shard_map/ppermute | solution.py:516
  22.9 3.5 %collective-permute-start.2 = (f32[40,256]{1,0:T(8,128)S(1)}, f32[40,256]{1,0:T(8,128)S(1)}, u32[]{:S(2)}, u32[]{:S(2)}) collective-permute-start(f32[40,256]{1,0:T(8,128)S(1)} %get-tuple-element.114), channel_id=1, source_target_pairs={{0,3},{1,2},{2,1},{3,0},{4,7},{5,6},{6,5},{7,4},{8,11},{9,10},{10,... | collective-permute-start | bytes 122888 | tf_op jit(solution)/shard_map/ppermute | solution.py:516
  26.5 22.1 %collective-permute-start.4 = (bf16[11,16,1024]{2,1,0:T(8,128)(2,1)}, bf16[11,16,1024]{2,1,0:T(8,128)(2,1)S(1)}, u32[]{:S(2)}, u32[]{:S(2)}) collective-permute-start(bf16[11,16,1024]{2,1,0:T(8,128)(2,1)} %get-tuple-element.127), channel_id=1, source_target_pairs={{0,24},{4,28},{8,16},{12,20},{16,8},{20,12},{24,0},{28,4},{1,25},{... | collective-permute-start | bytes 1081352 | tf_op jit(solution)/shard_map/ppermute | solution.py:516
  28.4 20.1 %collective-permute-start.5 = (bf16[11,16,1024]{2,1,0:T(8,128)(2,1)}, bf16[11,16,1024]{2,1,0:T(8,128)(2,1)S(1)}, u32[]{:S(2)}, u32[]{:S(2)}) collective-permute-start(bf16[11,16,1024]{2,1,0:T(8,128)(2,1)} %get-tuple-element.128), channel_id=1, source_target_pairs={{0,4},{4,0},{8,12},{12,8},{16,20},{20,16},{24,28},{28,24},{1,5},{5... | collective-permute-start | bytes 1081352 | tf_op jit(solution)/shard_map/ppermute | solution.py:516
  29.9 0.7 copy-start.9
  48.6 36.4 %all-to-all-start.2 = ((bf16[40,16,1024]{2,1,0:T(8,128)(2,1)}), bf16[40,16,1024]{2,1,0:T(8,128)(2,1)S(1)}, u32[]{:S(2)}, u32[]{:S(2)}) async-start(bf16[40,16,1024]{2,1,0:T(8,128)(2,1)} %get-tuple-element.153), calls=%async_computation.2 | async-start | bytes 2621440 | tf_op jit(solution)/shard_map/all_to_all | solution.py:551
  53.5 3.4 %copy-start = (bf16[128,1024]{1,0:T(8,128)(2,1)}, bf16[128,1024]{1,0:T(8,128)(2,1)S(1)}, u32[]{:S(2)}) copy-start(bf16[128,1024]{1,0:T(8,128)(2,1)S(1)} %get-tuple-element.141.refs_6_.refs_7_) | copy-start | bytes 786436
  53.5 3.4 %copy-start.5 = (bf16[8,40,128]{2,1,0:T(8,128)(2,1)}, bf16[8,40,128]{2,1,0:T(8,128)(2,1)S(1)}, u32[]{:S(2)}) copy-start(bf16[8,40,128]{2,1,0:T(8,128)(2,1)S(1)} %get-tuple-element.137.refs_0_) | copy-start | bytes 245764
  53.5 3.4 %collective-permute-start.6 = (bf16[8,40,128]{2,1,0:T(8,128)(2,1)S(1)}, bf16[8,40,128]{2,1,0:T(8,128)(2,1)S(1)}, u32[]{:S(2)}, u32[]{:S(2)}) collective-permute-start(bf16[8,40,128]{2,1,0:T(8,128)(2,1)S(1)} %get-tuple-element.137.refs_0_), channel_id=1, source_target_pairs={{0,1},{1,0},{2,3},{3,2},{4,5},{5,4},{6,7},{7,6},{8,9},{9,8},{10,11... | collective-permute-start | bytes 245768 | tf_op jit(solution)/shard_map/ppermute | solution.py:516
  53.5 5.2 %collective-permute-start.7 = (bf16[8,40,128]{2,1,0:T(8,128)(2,1)S(1)}, bf16[8,40,128]{2,1,0:T(8,128)(2,1)S(1)}, u32[]{:S(2)}, u32[]{:S(2)}) collective-permute-start(bf16[8,40,128]{2,1,0:T(8,128)(2,1)S(1)} %get-tuple-element.137.refs_0_), channel_id=1, source_target_pairs={{0,2},{1,3},{2,0},{3,1},{4,6},{5,7},{6,4},{7,5},{8,10},{9,11},{10,... | collective-permute-start | bytes 245768 | tf_op jit(solution)/shard_map/ppermute | solution.py:516
  55.1 4.7 %collective-permute-start.8 = (bf16[8,40,128]{2,1,0:T(8,128)(2,1)S(1)}, bf16[8,40,128]{2,1,0:T(8,128)(2,1)S(1)}, u32[]{:S(2)}, u32[]{:S(2)}) collective-permute-start(bf16[8,40,128]{2,1,0:T(8,128)(2,1)S(1)} %get-tuple-element.137.refs_0_), channel_id=1, source_target_pairs={{0,3},{1,2},{2,1},{3,0},{4,7},{5,6},{6,5},{7,4},{8,11},{9,10},{10,... | collective-permute-start | bytes 245768 | tf_op jit(solution)/shard_map/ppermute | solution.py:516
  57.0 2.9 %copy-start.11 = (bf16[8,40,128]{2,1,0:T(8,128)(2,1)}, bf16[8,40,128]{2,1,0:T(8,128)(2,1)S(1)}, u32[]{:S(2)}) copy-start(bf16[8,40,128]{2,1,0:T(8,128)(2,1)S(1)} %collective-permute-done.6.refs_1_) | copy-start | bytes 245764
  58.7 1.2 copy-start.12
  59.8 0.6 copy-start.13
  60.5 15.3 %copy-start.15 = (bf16[11,16,1024]{2,1,0:T(8,128)(2,1)S(1)}, bf16[11,16,1024]{2,1,0:T(8,128)(2,1)}, u32[]{:S(2)}) copy-start(bf16[11,16,1024]{2,1,0:T(8,128)(2,1)} %get-tuple-element.161) | copy-start | bytes 1081348
  70.7 7.4 %collective-permute-start.10 = (bf16[8,64,128]{2,1,0:T(8,128)(2,1)}, bf16[8,64,128]{2,1,0:T(8,128)(2,1)S(1)}, u32[]{:S(2)}, u32[]{:S(2)}) collective-permute-start(bf16[8,64,128]{2,1,0:T(8,128)(2,1)} %get-tuple-element.151), channel_id=1, source_target_pairs={{0,2},{1,3},{2,0},{3,1},{4,6},{5,7},{6,4},{7,5},{8,10},{9,11},{10,... | collective-permute-start | bytes 393224 | tf_op jit(solution)/shard_map/ppermute | solution.py:516
  72.1 7.1 %collective-permute-start.11 = (bf16[8,64,128]{2,1,0:T(8,128)(2,1)}, bf16[8,64,128]{2,1,0:T(8,128)(2,1)S(1)}, u32[]{:S(2)}, u32[]{:S(2)}) collective-permute-start(bf16[8,64,128]{2,1,0:T(8,128)(2,1)} %get-tuple-element.152), channel_id=1, source_target_pairs={{0,3},{1,2},{2,1},{3,0},{4,7},{5,6},{6,5},{7,4},{8,11},{9,10},{10,... | collective-permute-start | bytes 393224 | tf_op jit(solution)/shard_map/ppermute | solution.py:516
  72.6 6.6 %collective-permute-start.9 = (bf16[8,64,128]{2,1,0:T(8,128)(2,1)}, bf16[8,64,128]{2,1,0:T(8,128)(2,1)S(1)}, u32[]{:S(2)}, u32[]{:S(2)}) collective-permute-start(bf16[8,64,128]{2,1,0:T(8,128)(2,1)} %get-tuple-element.150), channel_id=1, source_target_pairs={{0,1},{1,0},{2,3},{3,2},{4,5},{5,4},{6,7},{7,6},{8,9},{9,8},{10,11... | collective-permute-start | bytes 393224 | tf_op jit(solution)/shard_map/ppermute | solution.py:516
  72.9 19.8 %collective-permute-start.12 = (bf16[11,16,1024]{2,1,0:T(8,128)(2,1)}, bf16[11,16,1024]{2,1,0:T(8,128)(2,1)S(1)}, u32[]{:S(2)}, u32[]{:S(2)}) collective-permute-start(bf16[11,16,1024]{2,1,0:T(8,128)(2,1)} %get-tuple-element.160), channel_id=1, source_target_pairs={{0,12},{4,8},{8,4},{12,0},{16,28},{20,24},{24,20},{28,16},{1,13},{... | collective-permute-start | bytes 1081352 | tf_op jit(solution)/shard_map/ppermute | solution.py:516
  75.7 24.1 %collective-permute-start.13 = (bf16[11,16,1024]{2,1,0:T(8,128)(2,1)S(1)}, bf16[11,16,1024]{2,1,0:T(8,128)(2,1)S(1)}, u32[]{:S(2)}, u32[]{:S(2)}) collective-permute-start(bf16[11,16,1024]{2,1,0:T(8,128)(2,1)S(1)} %copy-done.15), channel_id=1, source_target_pairs={{0,16},{4,20},{8,24},{12,28},{16,0},{20,4},{24,8},{28,12},{1,17},{... | collective-permute-start | bytes 1081352 | tf_op jit(solution)/shard_map/ppermute | solution.py:516
  85.0 0.9 copy-start.4
  87.0 13.7 %all-to-all-start.3 = ((bf16[8,64,128]{2,1,0:T(8,128)(2,1)}), bf16[8,64,128]{2,1,0:T(8,128)(2,1)S(1)}, u32[]{:S(2)}, u32[]{:S(2)}) async-start(bf16[8,64,128]{2,1,0:T(8,128)(2,1)} %shard_map.144), calls=%async_computation.3 | async-start | bytes 262144 | tf_op jit(solution)/shard_map/all_to_all | solution.py:661
  90.4 11.2 %copy-start.14 = (bf16[11,16,1024]{2,1,0:T(8,128)(2,1)S(1)}, bf16[11,16,1024]{2,1,0:T(8,128)(2,1)}, u32[]{:S(2)}) copy-start(bf16[11,16,1024]{2,1,0:T(8,128)(2,1)} %get-tuple-element.172) | copy-start | bytes 1081348
  100.7 20.5 %collective-permute-start.14 = (bf16[11,16,1024]{2,1,0:T(8,128)(2,1)}, bf16[11,16,1024]{2,1,0:T(8,128)(2,1)S(1)}, u32[]{:S(2)}, u32[]{:S(2)}) collective-permute-start(bf16[11,16,1024]{2,1,0:T(8,128)(2,1)} %get-tuple-element.171), channel_id=1, source_target_pairs={{0,8},{4,12},{8,0},{12,4},{16,24},{20,28},{24,16},{28,20},{1,9},{5... | collective-permute-start | bytes 1081352 | tf_op jit(solution)/shard_map/ppermute | solution.py:516
  101.6 19.6 %collective-permute-start.15 = (bf16[11,16,1024]{2,1,0:T(8,128)(2,1)S(1)}, bf16[11,16,1024]{2,1,0:T(8,128)(2,1)S(1)}, u32[]{:S(2)}, u32[]{:S(2)}) collective-permute-start(bf16[11,16,1024]{2,1,0:T(8,128)(2,1)S(1)} %copy-done.14), channel_id=1, source_target_pairs={{0,20},{4,16},{8,28},{12,24},{16,4},{20,0},{24,12},{28,8},{1,21},{... | collective-permute-start | bytes 1081352 | tf_op jit(solution)/shard_map/ppermute | solution.py:516
  104.1 17.1 %all-to-all-start.4 = ((bf16[8,40,128]{2,1,0:T(8,128)(2,1)}), bf16[8,40,128]{2,1,0:T(8,128)(2,1)S(1)}, u32[]{:S(2)}, u32[]{:S(2)}) async-start(bf16[8,40,128]{2,1,0:T(8,128)(2,1)} %shard_map.146), calls=%async_computation.4 | async-start | bytes 163840 | tf_op jit(solution)/shard_map/all_to_all | solution.py:666
  108.2 16.0 %copy-start.2 = (bf16[1024,512]{1,0:T(8,128)(2,1)S(1)}, bf16[1024,512]{1,0:T(8,128)(2,1)}, u32[]{:S(2)}) copy-start(bf16[1024,512]{1,0:T(8,128)(2,1)} %weight_ref.1) | copy-start | bytes 3145732
  108.2 16.0 %copy-start.8 = (s32[2]{0:T(128)S(1)}, s32[2]{0:T(128)}, u32[]{:S(2)}) copy-start(s32[2]{0:T(128)} %pad_add_fusion.me_ref) | copy-start | bytes 28
  121.2 9.0 %collective-permute-start.19 = (bf16[7,16,1024]{2,1,0:T(8,128)(2,1)}, bf16[7,16,1024]{2,1,0:T(8,128)(2,1)S(1)}, u32[]{:S(2)}, u32[]{:S(2)}) collective-permute-start(bf16[7,16,1024]{2,1,0:T(8,128)(2,1)} %get-tuple-element.189), channel_id=1, source_target_pairs={{0,28},{4,24},{8,20},{12,16},{16,12},{20,8},{24,4},{28,0},{1,29},{... | collective-permute-start | bytes 688136 | tf_op jit(solution)/shard_map/ppermute | solution.py:516
  125.2 3.4 %collective-permute-start.16 = (f32[10,512]{1,0:T(8,128)S(1)}, f32[10,512]{1,0:T(8,128)S(1)}, u32[]{:S(2)}, u32[]{:S(2)}) collective-permute-start(f32[10,512]{1,0:T(8,128)S(1)} %get-tuple-element.186), channel_id=1, source_target_pairs={{0,1},{1,0},{2,3},{3,2},{4,5},{5,4},{6,7},{7,6},{8,9},{9,8},{10,11... | collective-permute-start | bytes 61448 | tf_op jit(solution)/shard_map/ppermute | solution.py:516
  125.3 4.0 %collective-permute-start.17 = (f32[10,512]{1,0:T(8,128)S(1)}, f32[10,512]{1,0:T(8,128)S(1)}, u32[]{:S(2)}, u32[]{:S(2)}) collective-permute-start(f32[10,512]{1,0:T(8,128)S(1)} %get-tuple-element.187), channel_id=1, source_target_pairs={{0,2},{1,3},{2,0},{3,1},{4,6},{5,7},{6,4},{7,5},{8,10},{9,11},{10,... | collective-permute-start | bytes 61448 | tf_op jit(solution)/shard_map/ppermute | solution.py:516
  126.8 3.3 %collective-permute-start.18 = (f32[10,512]{1,0:T(8,128)S(1)}, f32[10,512]{1,0:T(8,128)S(1)}, u32[]{:S(2)}, u32[]{:S(2)}) collective-permute-start(f32[10,512]{1,0:T(8,128)S(1)} %get-tuple-element.188), channel_id=1, source_target_pairs={{0,3},{1,2},{2,1},{3,0},{4,7},{5,6},{6,5},{7,4},{8,11},{9,10},{10,... | collective-permute-start | bytes 61448 | tf_op jit(solution)/shard_map/ppermute | solution.py:516

commit v23 on v21

--- a/solution.py
+++ b/solution.py
@@ -584,7 +584,7 @@
             w_keyval,
             scratch=[pltpu.VMEM((rows, narrow * HD), jnp.float32)],
         )
-        partial = land(deal(launch(partial, 8, 6), "narrow"), 8)
+        partial = deal(launch(partial, 8, 6), "narrow")
         partial = launch(partial, 1)
         packed = in_vmem(
             functools.partial(pack_kernel, narrow),
@@ -593,7 +593,7 @@
             *partial,
             tags,
         )
-        received = land(exchange(packed, "wide"), 6, 1)
+        received = land(exchange(packed, "wide"), 8, 6, 1)
         received = launch(received, 0)
         queries, keyval, new_entries, moved_req, moved_idx = in_vmem(
             functools.partial(unpack_kernel, rows),
@@ -617,14 +617,14 @@
         partial = jnp.concatenate(
             [query_part, jnp.broadcast_to(keyval_part[None], (narrow,) + keyval_part.shape)], axis=2
         )
-        partial = land(exchange(launch(partial, 8, 6), "narrow"), 8)
+        partial = exchange(launch(partial, 8, 6), "narrow")
         partial = launch(partial, 1)
         projected = jnp.sum(partial, axis=0).astype(jnp.bfloat16)
         tags = tags[:, : 3 * capacity].astype(jnp.bfloat16)[:, None]
         tags = jnp.pad(tags, ((0, 0), (0, 7), (0, projected.shape[1] - tags.shape[2])))
         packed = jnp.broadcast_to(projected[None], (wide,) + projected.shape)
         packed = jnp.concatenate([packed, tags], axis=1)
-        received = land(exchange(packed, "wide"), 6, 1)
+        received = land(exchange(packed, "wide"), 8, 6, 1)
         received = launch(received, 0)
         tags_in = received[:, rows]
         queries = received[:, :rows, :own_cols]

time: 132 us -> 135 us (1.023)
  waiting for transfers between devices: 39 us -> 46.3 us
  starting transfers between devices: 57.7 us -> 52.4 us
    all_to_all x1, starting transfers between devices: 14.1 us -> 4.42 us  [on_device(): received = land(exchange(packed, 'wide'), 8, 6, 1)]
    all_to_all x1, waiting for transfers between devices: 0.01 us -> 5.92 us  [launch(): flying[c] = send(chunk, 'wide', d) if d else exchange(chunk, 'wide')]
    ppermute x20, waiting for transfers between devices: 16 us -> 20.9 us  [send(): lax.ppermute(block, axis, [(i, i ^ d) for i in range(lax.axis_size(axis))])]
    ppermute x20, starting transfers between devices: 23.5 us -> 27.6 us  [send(): lax.ppermute(block, axis, [(i, i ^ d) for i in range(lax.axis_size(axis))])]
    all_to_all x1, starting transfers between devices: 5.93 us -> 3.37 us  [on_device(): mixed = land(exchange(mixed, 'wide'), 3, 4)]
    all_to_all x1, waiting for transfers between devices: 7.78 us -> 5.35 us  [on_device(): received = land(exchange(packed, 'wide'), 8, 6, 1)]
    all_to_all x1, starting transfers between devices: 3.57 us -> 5.91 us  [launch(): flying[c] = send(chunk, 'wide', d) if d else exchange(chunk, 'wide')]
    unnamed x34 -> x32, local copies, waits for them, and re-layouts: 3.07 us -> 3.07 us
where the time goes in v23:
time: 135 us; the launch traced here: 133 us
  starting transfers between devices  52.4 us (39%)
  waiting for transfers between devices  46.3 us (34%)
  Pallas kernels  29.2 us (22%)
  local copies, waits for them, and re-layouts  3.07 us (2%)
  other arithmetic  1.4 us (1%)
    ppermute x20, starting transfers between devices, send(): lax.ppermute(block, axis, [(i, i ^ d) for i in range(lax.axis_size(axis))])  27.6 us
    ppermute x20, waiting for transfers between devices, send(): lax.ppermute(block, axis, [(i, i ^ d) for i in range(lax.axis_size(axis))])  20.9 us
    all_to_all x1, waiting for transfers between devices, on_device(): attn = land(exchange(attn, 'wide'), 2, 5)  11.6 us
    pallas_call x1, Pallas kernels, attend(): pl.pallas_call(functools.partial(attend_kernel, rows, piece, peers), grid...  10.3 us
    all_to_all x1, starting transfers between devices, on_device(): gathered = exchange(in_vmem(repeat_kernel, copies, None, hidden), 'wide')  7.28 us
    pallas_call x5, Pallas kernels, place_pages(): pl.pallas_call(functools.partial(place_kernel, counts), out_shape=jax.Sha...  6.64 us
    all_to_all x1, waiting for transfers between devices, launch(): flying[c] = send(chunk, 'wide', d) if d else exchange(chunk, 'wide')  5.92 us
    all_to_all x1, starting transfers between devices, launch(): flying[c] = send(chunk, 'wide', d) if d else exchange(chunk, 'wide')  5.91 us
  transfers between devices with their start and end apart: 25, of which 14 were waited for; matrix products, arithmetic and copies ran while one was open for 1% of the time, Pallas kernels for 20%

profile of v23, /device:TPU:0, one launch (start us, length us, event | category | flops | bytes accessed | tf_op | source)
XLA Modules:
  0.0 133.2 jit_solution(9629736769247662492)
XLA Ops:
  0.7 0.8 copy-done.6
  1.5 0.7 shard_map.137
  2.1 7.3 %all-to-all-start = ((bf16[8,5,1024]{2,1,0:T(8,128)(2,1)}), bf16[8,5,1024]{2,1,0:T(8,128)(2,1)S(1)}, u32[]{:S(2)}, u32[]{:S(2)}) async-start(bf16[8,5,1024]{2,1,0:T(8,128)(2,1)} %shard_map.137), calls=%async_computation | async-start | bytes 262144 | tf_op jit(solution)/shard_map/all_to_all | solution.py:525
  10.0 5.7 %shard_map.138 = (bf16[128,16,1024]{2,1,0:T(8,128)(2,1)}, f32[8,128]{1,0:T(8,128)}, f32[8,2048]{1,0:T(8,128)}, bf16[40,16,1024]{2,1,0:T(8,128)(2,1)}, bf16[11,16...) custom-call(s32[2]{0:T(128)} %pad_add_fusion.me_ref, ...), custom_call_target="tpu_custom_call" | custom-call | bytes 8388608 | tf_op jit(solution)/shard_map/pallas_call | solution.py:118
  15.6 1.1 all-to-all-done.hidden_ref
  16.8 1.0 shard_map.139
  17.8 1.6 %collective-permute-start.1 = (f32[40,256]{1,0:T(8,128)S(1)}, f32[40,256]{1,0:T(8,128)S(1)}, u32[]{:S(2)}, u32[]{:S(2)}) collective-permute-start(f32[40,256]{1,0:T(8,128)S(1)} %get-tuple-element.110), channel_id=1, source_target_pairs={{0,2},{1,3},{2,0},{3,1},{4,6},{5,7},{6,4},{7,5},{8,10},{9,11},{10,... | collective-permute-start | bytes 122888 | tf_op jit(solution)/shard_map/ppermute | solution.py:516
  19.7 2.7 %collective-permute-start.4 = (bf16[11,16,1024]{2,1,0:T(8,128)(2,1)}, bf16[11,16,1024]{2,1,0:T(8,128)(2,1)S(1)}, u32[]{:S(2)}, u32[]{:S(2)}) collective-permute-start(bf16[11,16,1024]{2,1,0:T(8,128)(2,1)} %get-tuple-element.119), channel_id=1, source_target_pairs={{0,24},{4,28},{8,16},{12,20},{16,8},{20,12},{24,0},{28,4},{1,25},{... | collective-permute-start | bytes 1081352 | tf_op jit(solution)/shard_map/ppermute | solution.py:516
  22.9 1.1 collective-permute-start.5
  24.0 0.7 copy-done.9
  24.7 0.7 shard_map.140
  25.4 4.4 %all-to-all-start.1 = ((bf16[8,48,256]{2,1,0:T(8,128)(2,1)}), bf16[8,48,256]{2,1,0:T(8,128)(2,1)S(1)}, u32[]{:S(2)}, u32[]{:S(2)}) async-start(bf16[8,48,256]{2,1,0:T(8,128)(2,1)} %shard_map.140), calls=%async_computation.1 | async-start | bytes 393216 | tf_op jit(solution)/shard_map/all_to_all | solution.py:596
  29.8 4.7 %collective-permute-start.3 = (bf16[4,16,1024]{2,1,0:T(8,128)(2,1)}, bf16[4,16,1024]{2,1,0:T(8,128)(2,1)S(1)}, u32[]{:S(2)}, u32[]{:S(2)}) collective-permute-start(bf16[4,16,1024]{2,1,0:T(8,128)(2,1)} %get-tuple-element.118), channel_id=1, source_target_pairs={{0,28},{4,24},{8,20},{12,16},{16,12},{20,8},{24,4},{28,0},{1,29},{... | collective-permute-start | bytes 393224 | tf_op jit(solution)/shard_map/ppermute | solution.py:516
  34.5 6.4 %collective-permute-done.3.refs_2_ = bf16[4,16,1024]{2,1,0:T(8,128)(2,1)S(1)} collective-permute-done((bf16[4,16,1024]{2,1,0:T(8,128)(2,1)}, bf16[4,16,1024]{2,1,0:T(8,128)(2,1)S(1)}, u32[]{:S(2)}, u32[]{:S(2)}) %collective-permute-start.3) | collective-permute-done | bytes 131104 | tf_op jit(solution)/shard_map/ppermute | solution.py:516
  40.9 5.4 %all-to-all-done.1.part_ref = bf16[8,48,256]{2,1,0:T(8,128)(2,1)S(1)} async-done(((bf16[8,48,256]{2,1,0:T(8,128)(2,1)}), bf16[8,48,256]{2,1,0:T(8,128)(2,1)S(1)}, u32[]{:S(2)}, u32[]{:S(2)}) %all-to-all-start.1) | async-done | bytes 196640 | tf_op jit(solution)/shard_map/all_to_all | solution.py:596
  46.3 5.9 %all-to-all-start.2 = ((bf16[40,16,1024]{2,1,0:T(8,128)(2,1)}), bf16[40,16,1024]{2,1,0:T(8,128)(2,1)S(1)}, u32[]{:S(2)}, u32[]{:S(2)}) async-start(bf16[40,16,1024]{2,1,0:T(8,128)(2,1)} %get-tuple-element.145), calls=%async_computation.2 | async-start | bytes 2621440 | tf_op jit(solution)/shard_map/all_to_all | solution.py:551
  52.2 1.4 %shard_map.141 = (bf16[8,40,128]{2,1,0:T(8,128)(2,1)S(1)}, bf16[128,1024]{1,0:T(8,128)(2,1)S(1)}, bf16[1,5,1024]{2,1,0:T(8,128)(2,1)}, s32[1,128]{1,0:T(1,128)}, s32[1,128]{1,0:T(1,128)}) custom-call(s32[2]{0:T(128)S(1)} %copy-done.7, s32[8]{0:T(128)S(1)} %copy-done.10, bf16[8,48,256]{2,1,0:T(8,128)(2,1)S(1)} %all-to-all-done.1.part_ref), custom_call_target="tpu_custom_call" | custom-call | flops 1 | bytes 1 | tf_op jit(solution)/shard_map/pallas_call | solution.py:471
  53.5 1.6 %collective-permute-start.7 = (bf16[8,40,128]{2,1,0:T(8,128)(2,1)S(1)}, bf16[8,40,128]{2,1,0:T(8,128)(2,1)S(1)}, u32[]{:S(2)}, u32[]{:S(2)}) collective-permute-start(bf16[8,40,128]{2,1,0:T(8,128)(2,1)S(1)} %get-tuple-element.129.refs_0_), channel_id=1, source_target_pairs={{0,2},{1,3},{2,0},{3,1},{4,6},{5,7},{6,4},{7,5},{8,10},{9,11},{10,... | collective-permute-start | bytes 245768 | tf_op jit(solution)/shard_map/ppermute | solution.py:516
  55.5 1.5 %shard_map.142.refs_1_ = bf16[128,16,1024]{2,1,0:T(8,128)(2,1)} custom-call(s32[3]{0:T(128)S(1)} %pad_add_fusion.1.place_ref, bf16[11,16,1024]{2,1,0:T(8,128)(2,1)S(1)} %collective-permute-done.5.refs_0_, bf16[11,16,1024]{2,1,0:T(8,128)(2,1)S(1)} %collective-permute-done.4.refs_1_, ...), custom_call_target="tpu_custom_call", output_to_operand_aliasing={{}: (4, {})} | custom-call | bytes 1703936 | tf_op jit(solution)/shard_map/pallas_call | solution.py:156
  57.0 1.7 %collective-permute-done.7.refs_2_ = bf16[8,40,128]{2,1,0:T(8,128)(2,1)S(1)} collective-permute-done((bf16[8,40,128]{2,1,0:T(8,128)(2,1)S(1)}, bf16[8,40,128]{2,1,0:T(8,128)(2,1)S(1)}, u32[]{:S(2)}, u32[]{:S(2)}) %collective-permute-start.7) | collective-permute-done | bytes 81952 | tf_op jit(solution)/shard_map/ppermute | solution.py:516
  58.7 1.1 collective-permute-done.8.refs_3_
  59.8 0.6 copy-done.13
  60.5 10.3 %shard_map.143 = (bf16[8,64,128]{2,1,0:T(8,128)(2,1)}, bf16[8,64,128]{2,1,0:T(8,128)(2,1)}, bf16[8,64,128]{2,1,0:T(8,128)(2,1)}, bf16[8,64,128]{2,1,0:T(8,128)(2,1)}) custom-call(s32[2]{0:T(128)} %pad_add_fusion.me_ref, s32[8]{0:T(128)} %length_ref.1, bf16[8,40,128]{2,1,0:T(8,128)(2,1)} %copy-done.5, bf16[8,40,128]{2,1,0:T(8,128)(2,1)} %copy-done.11, ...), custom_call_target="tpu_custom_call" | custom-call | flops 1 | bytes 1 | tf_op jit(solution)/shard_map/pallas_call | solution.py:298
  70.7 1.4 %collective-permute-start.10 = (bf16[8,64,128]{2,1,0:T(8,128)(2,1)}, bf16[8,64,128]{2,1,0:T(8,128)(2,1)S(1)}, u32[]{:S(2)}, u32[]{:S(2)}) collective-permute-start(bf16[8,64,128]{2,1,0:T(8,128)(2,1)} %get-tuple-element.143), channel_id=1, source_target_pairs={{0,2},{1,3},{2,0},{3,1},{4,6},{5,7},{6,4},{7,5},{8,10},{9,11},{10,... | collective-permute-start | bytes 393224 | tf_op jit(solution)/shard_map/ppermute | solution.py:516
  72.9 2.9 %collective-permute-start.12 = (bf16[11,16,1024]{2,1,0:T(8,128)(2,1)}, bf16[11,16,1024]{2,1,0:T(8,128)(2,1)S(1)}, u32[]{:S(2)}, u32[]{:S(2)}) collective-permute-start(bf16[11,16,1024]{2,1,0:T(8,128)(2,1)} %get-tuple-element.152), channel_id=1, source_target_pairs={{0,12},{4,8},{8,4},{12,0},{16,28},{20,24},{24,20},{28,16},{1,13},{... | collective-permute-start | bytes 1081352 | tf_op jit(solution)/shard_map/ppermute | solution.py:516
  75.8 2.4 %collective-permute-start.13 = (bf16[11,16,1024]{2,1,0:T(8,128)(2,1)S(1)}, bf16[11,16,1024]{2,1,0:T(8,128)(2,1)S(1)}, u32[]{:S(2)}, u32[]{:S(2)}) collective-permute-start(bf16[11,16,1024]{2,1,0:T(8,128)(2,1)S(1)} %copy-done.15), channel_id=1, source_target_pairs={{0,16},{4,20},{8,24},{12,28},{16,0},{20,4},{24,8},{28,12},{1,17},{... | collective-permute-start | bytes 1081352 | tf_op jit(solution)/shard_map/ppermute | solution.py:516
  78.2 1.0 collective-permute-done.11.refs_3_
  79.2 5.9 %all-to-all-done.2.refs_0_ = bf16[40,16,1024]{2,1,0:T(8,128)(2,1)S(1)} async-done(((bf16[40,16,1024]{2,1,0:T(8,128)(2,1)}), bf16[40,16,1024]{2,1,0:T(8,128)(2,1)S(1)}, u32[]{:S(2)}, u32[]{:S(2)}) %all-to-all-start.2) | async-done | bytes 1310752 | tf_op jit(solution)/shard_map/all_to_all | solution.py:551
  85.1 0.9 copy-done.4
  86.0 1.1 shard_map.144
  87.1 3.4 %all-to-all-start.3 = ((bf16[8,64,128]{2,1,0:T(8,128)(2,1)}), bf16[8,64,128]{2,1,0:T(8,128)(2,1)S(1)}, u32[]{:S(2)}, u32[]{:S(2)}) async-start(bf16[8,64,128]{2,1,0:T(8,128)(2,1)} %shard_map.144), calls=%async_computation.3 | async-start | bytes 262144 | tf_op jit(solution)/shard_map/all_to_all | solution.py:661
  90.5 1.7 %shard_map.145.refs_2_ = bf16[128,16,1024]{2,1,0:T(8,128)(2,1)} custom-call(s32[8]{0:T(128)S(1)} %iota_multiply_fusion.place_ref, bf16[40,16,1024]{2,1,0:T(8,128)(2,1)S(1)} %all-to-all-done.2.refs_0_, bf16[128,16,1024]{2,1,0:T(8,128)(2,1)} %shard_map.142.refs_1_), custom_call_target="tpu_custom_call", output_to_operand_aliasing={{}: (2, {})} | custom-call | bytes 2621440 | tf_op jit(solution)/shard_map/pallas_call | solution.py:156
  92.3 8.6 %collective-permute-done.13.refs_1_ = bf16[11,16,1024]{2,1,0:T(8,128)(2,1)S(1)} collective-permute-done((bf16[11,16,1024]{2,1,0:T(8,128)(2,1)S(1)}, bf16[11,16,1024]{2,1,0:T(8,128)(2,1)S(1)}, u32[]{:S(2)}, u32[]{:S(2)}) %collective-permute-start.13) | collective-permute-done | bytes 360480 | tf_op jit(solution)/shard_map/ppermute | solution.py:516
  100.9 1.3 all-to-all-done.3.refs_0_
  102.2 0.9 collective-permute-start.14
  103.1 1.8 %collective-permute-start.15 = (bf16[11,16,1024]{2,1,0:T(8,128)(2,1)S(1)}, bf16[11,16,1024]{2,1,0:T(8,128)(2,1)S(1)}, u32[]{:S(2)}, u32[]{:S(2)}) collective-permute-start(bf16[11,16,1024]{2,1,0:T(8,128)(2,1)S(1)} %copy-done.14), channel_id=1, source_target_pairs={{0,20},{4,16},{8,28},{12,24},{16,4},{20,0},{24,12},{28,8},{1,21},{... | collective-permute-start | bytes 1081352 | tf_op jit(solution)/shard_map/ppermute | solution.py:516
  104.9 0.9 shard_map.146
  105.8 3.8 %all-to-all-start.4 = ((bf16[8,40,128]{2,1,0:T(8,128)(2,1)}), bf16[8,40,128]{2,1,0:T(8,128)(2,1)S(1)}, u32[]{:S(2)}, u32[]{:S(2)}) async-start(bf16[8,40,128]{2,1,0:T(8,128)(2,1)} %shard_map.146), calls=%async_computation.4 | async-start | bytes 163840 | tf_op jit(solution)/shard_map/all_to_all | solution.py:666
  109.7 1.4 %shard_map.147.refs_2_ = bf16[128,16,1024]{2,1,0:T(8,128)(2,1)} custom-call(s32[2]{0:T(128)S(1)} %pad_add_fusion.2.place_ref, bf16[11,16,1024]{2,1,0:T(8,128)(2,1)S(1)} %collective-permute-done.12.refs_0_, bf16[11,16,1024]{2,1,0:T(8,128)(2,1)S(1)} %collective-permute-done.13.refs_1_, ...), custom_call_target="tpu_custom_call", output_to_operand_aliasing={{}: (3, {})} | custom-call | bytes 1441792 | tf_op jit(solution)/shard_map/pallas_call | solution.py:156
  111.2 11.6 %all-to-all-done.4.part_ref = bf16[8,40,128]{2,1,0:T(8,128)(2,1)S(1)} async-done(((bf16[8,40,128]{2,1,0:T(8,128)(2,1)}), bf16[8,40,128]{2,1,0:T(8,128)(2,1)S(1)}, u32[]{:S(2)}, u32[]{:S(2)}) %all-to-all-start.4) | async-done | bytes 81952 | tf_op jit(solution)/shard_map/all_to_all | solution.py:666
  122.8 3.2 %collective-permute-start.19 = (bf16[7,16,1024]{2,1,0:T(8,128)(2,1)}, bf16[7,16,1024]{2,1,0:T(8,128)(2,1)S(1)}, u32[]{:S(2)}, u32[]{:S(2)}) collective-permute-start(bf16[7,16,1024]{2,1,0:T(8,128)(2,1)} %get-tuple-element.181), channel_id=1, source_target_pairs={{0,28},{4,24},{8,20},{12,16},{16,12},{20,8},{24,4},{28,0},{1,29},{... | collective-permute-start | bytes 688136 | tf_op jit(solution)/shard_map/ppermute | solution.py:516
  126.0 0.9 shard_map.148
  127.0 1.6 %collective-permute-start.17 = (f32[10,512]{1,0:T(8,128)S(1)}, f32[10,512]{1,0:T(8,128)S(1)}, u32[]{:S(2)}, u32[]{:S(2)}) collective-permute-start(f32[10,512]{1,0:T(8,128)S(1)} %get-tuple-element.179), channel_id=1, source_target_pairs={{0,2},{1,3},{2,0},{3,1},{4,6},{5,7},{6,4},{7,5},{8,10},{9,11},{10,... | collective-permute-start | bytes 61448 | tf_op jit(solution)/shard_map/ppermute | solution.py:516
  128.9 1.4 %shard_map.149.refs_1_ = bf16[128,16,1024]{2,1,0:T(8,128)(2,1)} custom-call(s32[2]{0:T(128)S(1)} %pad_add_fusion.3.place_ref, bf16[11,16,1024]{2,1,0:T(8,128)(2,1)S(1)} %collective-permute-done.14.refs_0_, bf16[11,16,1024]{2,1,0:T(8,128)(2,1)S(1)} %collective-permute-done.15.refs_1_, ...), custom_call_target="tpu_custom_call", output_to_operand_aliasing={{}: (3, {})} | custom-call | bytes 1441792 | tf_op jit(solution)/shard_map/pallas_call | solution.py:156
  130.3 0.6 collective-permute-done.17
  130.9 0.9 collective-permute-done.18
  131.9 0.6 add_convert_fusion
  132.5 0.7 shard_map.150
  (54 shorter events, 3.3 us)
Async XLA Ops:
  0.6 16.1 %copy-start.1 = (bf16[1024,512]{1,0:T(8,128)(2,1)S(1)}, bf16[1024,512]{1,0:T(8,128)(2,1)}, u32[]{:S(2)}) copy-start(bf16[1024,512]{1,0:T(8,128)(2,1)} %query_ref.1) | copy-start | bytes 3145732
  0.6 16.1 %copy-start.3 = (bf16[1024,128]{1,0:T(8,128)(2,1)S(1)}, bf16[1024,128]{1,0:T(8,128)(2,1)}, u32[]{:S(2)}) copy-start(bf16[1024,128]{1,0:T(8,128)(2,1)} %keyval_ref.1) | copy-start | bytes 786436
  0.7 0.8 copy-start.6
  2.1 14.6 %all-to-all-start = ((bf16[8,5,1024]{2,1,0:T(8,128)(2,1)}), bf16[8,5,1024]{2,1,0:T(8,128)(2,1)S(1)}, u32[]{:S(2)}, u32[]{:S(2)}) async-start(bf16[8,5,1024]{2,1,0:T(8,128)(2,1)} %shard_map.137), calls=%async_computation | async-start | bytes 262144 | tf_op jit(solution)/shard_map/all_to_all | solution.py:525
  10.0 6.8 %copy-start.7 = (s32[2]{0:T(128)S(1)}, s32[2]{0:T(128)}, u32[]{:S(2)}) copy-start(s32[2]{0:T(128)} %pad_add_fusion.me_ref) | copy-start | bytes 28
  10.0 42.2 %copy-start.10 = (s32[8]{0:T(128)S(1)}, s32[8]{0:T(128)}, u32[]{:S(2)}) copy-start(s32[8]{0:T(128)} %kept_ref.1) | copy-start | bytes 100
  17.8 4.7 %collective-permute-start = (f32[40,256]{1,0:T(8,128)S(1)}, f32[40,256]{1,0:T(8,128)S(1)}, u32[]{:S(2)}, u32[]{:S(2)}) collective-permute-start(f32[40,256]{1,0:T(8,128)S(1)} %get-tuple-element.109), channel_id=1, source_target_pairs={{0,1},{1,0},{2,3},{3,2},{4,5},{5,4},{6,7},{7,6},{8,9},{9,8},{10,11... | collective-permute-start | bytes 122888 | tf_op jit(solution)/shard_map/ppermute | solution.py:516
  17.8 4.6 %collective-permute-start.1 = (f32[40,256]{1,0:T(8,128)S(1)}, f32[40,256]{1,0:T(8,128)S(1)}, u32[]{:S(2)}, u32[]{:S(2)}) collective-permute-start(f32[40,256]{1,0:T(8,128)S(1)} %get-tuple-element.110), channel_id=1, source_target_pairs={{0,2},{1,3},{2,0},{3,1},{4,6},{5,7},{6,4},{7,5},{8,10},{9,11},{10,... | collective-permute-start | bytes 122888 | tf_op jit(solution)/shard_map/ppermute | solution.py:516
  19.4 3.5 %collective-permute-start.2 = (f32[40,256]{1,0:T(8,128)S(1)}, f32[40,256]{1,0:T(8,128)S(1)}, u32[]{:S(2)}, u32[]{:S(2)}) collective-permute-start(f32[40,256]{1,0:T(8,128)S(1)} %get-tuple-element.111), channel_id=1, source_target_pairs={{0,3},{1,2},{2,1},{3,0},{4,7},{5,6},{6,5},{7,4},{8,11},{9,10},{10,... | collective-permute-start | bytes 122888 | tf_op jit(solution)/shard_map/ppermute | solution.py:516
  19.7 21.2 %collective-permute-start.4 = (bf16[11,16,1024]{2,1,0:T(8,128)(2,1)}, bf16[11,16,1024]{2,1,0:T(8,128)(2,1)S(1)}, u32[]{:S(2)}, u32[]{:S(2)}) collective-permute-start(bf16[11,16,1024]{2,1,0:T(8,128)(2,1)} %get-tuple-element.119), channel_id=1, source_target_pairs={{0,24},{4,28},{8,16},{12,20},{16,8},{20,12},{24,0},{28,4},{1,25},{... | collective-permute-start | bytes 1081352 | tf_op jit(solution)/shard_map/ppermute | solution.py:516
  22.9 23.3 %collective-permute-start.5 = (bf16[11,16,1024]{2,1,0:T(8,128)(2,1)}, bf16[11,16,1024]{2,1,0:T(8,128)(2,1)S(1)}, u32[]{:S(2)}, u32[]{:S(2)}) collective-permute-start(bf16[11,16,1024]{2,1,0:T(8,128)(2,1)} %get-tuple-element.120), channel_id=1, source_target_pairs={{0,4},{4,0},{8,12},{12,8},{16,20},{20,16},{24,28},{28,24},{1,5},{5... | collective-permute-start | bytes 1081352 | tf_op jit(solution)/shard_map/ppermute | solution.py:516
  24.0 0.7 copy-start.9
  25.4 20.9 %all-to-all-start.1 = ((bf16[8,48,256]{2,1,0:T(8,128)(2,1)}), bf16[8,48,256]{2,1,0:T(8,128)(2,1)S(1)}, u32[]{:S(2)}, u32[]{:S(2)}) async-start(bf16[8,48,256]{2,1,0:T(8,128)(2,1)} %shard_map.140), calls=%async_computation.1 | async-start | bytes 393216 | tf_op jit(solution)/shard_map/all_to_all | solution.py:596
  29.8 11.1 %collective-permute-start.3 = (bf16[4,16,1024]{2,1,0:T(8,128)(2,1)}, bf16[4,16,1024]{2,1,0:T(8,128)(2,1)S(1)}, u32[]{:S(2)}, u32[]{:S(2)}) collective-permute-start(bf16[4,16,1024]{2,1,0:T(8,128)(2,1)} %get-tuple-element.118), channel_id=1, source_target_pairs={{0,28},{4,24},{8,20},{12,16},{16,12},{20,8},{24,4},{28,0},{1,29},{... | collective-permute-start | bytes 393224 | tf_op jit(solution)/shard_map/ppermute | solution.py:516
  46.3 38.8 %all-to-all-start.2 = ((bf16[40,16,1024]{2,1,0:T(8,128)(2,1)}), bf16[40,16,1024]{2,1,0:T(8,128)(2,1)S(1)}, u32[]{:S(2)}, u32[]{:S(2)}) async-start(bf16[40,16,1024]{2,1,0:T(8,128)(2,1)} %get-tuple-element.145), calls=%async_computation.2 | async-start | bytes 2621440 | tf_op jit(solution)/shard_map/all_to_all | solution.py:551
  53.5 3.4 %copy-start = (bf16[128,1024]{1,0:T(8,128)(2,1)}, bf16[128,1024]{1,0:T(8,128)(2,1)S(1)}, u32[]{:S(2)}) copy-start(bf16[128,1024]{1,0:T(8,128)(2,1)S(1)} %get-tuple-element.133.refs_6_.refs_7_) | copy-start | bytes 786436
  53.5 3.4 %copy-start.5 = (bf16[8,40,128]{2,1,0:T(8,128)(2,1)}, bf16[8,40,128]{2,1,0:T(8,128)(2,1)S(1)}, u32[]{:S(2)}) copy-start(bf16[8,40,128]{2,1,0:T(8,128)(2,1)S(1)} %get-tuple-element.129.refs_0_) | copy-start | bytes 245764
  53.5 3.4 %collective-permute-start.6 = (bf16[8,40,128]{2,1,0:T(8,128)(2,1)S(1)}, bf16[8,40,128]{2,1,0:T(8,128)(2,1)S(1)}, u32[]{:S(2)}, u32[]{:S(2)}) collective-permute-start(bf16[8,40,128]{2,1,0:T(8,128)(2,1)S(1)} %get-tuple-element.129.refs_0_), channel_id=1, source_target_pairs={{0,1},{1,0},{2,3},{3,2},{4,5},{5,4},{6,7},{7,6},{8,9},{9,8},{10,11... | collective-permute-start | bytes 245768 | tf_op jit(solution)/shard_map/ppermute | solution.py:516
  53.5 5.2 %collective-permute-start.7 = (bf16[8,40,128]{2,1,0:T(8,128)(2,1)S(1)}, bf16[8,40,128]{2,1,0:T(8,128)(2,1)S(1)}, u32[]{:S(2)}, u32[]{:S(2)}) collective-permute-start(bf16[8,40,128]{2,1,0:T(8,128)(2,1)S(1)} %get-tuple-element.129.refs_0_), channel_id=1, source_target_pairs={{0,2},{1,3},{2,0},{3,1},{4,6},{5,7},{6,4},{7,5},{8,10},{9,11},{10,... | collective-permute-start | bytes 245768 | tf_op jit(solution)/shard_map/ppermute | solution.py:516
  55.1 4.7 %collective-permute-start.8 = (bf16[8,40,128]{2,1,0:T(8,128)(2,1)S(1)}, bf16[8,40,128]{2,1,0:T(8,128)(2,1)S(1)}, u32[]{:S(2)}, u32[]{:S(2)}) collective-permute-start(bf16[8,40,128]{2,1,0:T(8,128)(2,1)S(1)} %get-tuple-element.129.refs_0_), channel_id=1, source_target_pairs={{0,3},{1,2},{2,1},{3,0},{4,7},{5,6},{6,5},{7,4},{8,11},{9,10},{10,... | collective-permute-start | bytes 245768 | tf_op jit(solution)/shard_map/ppermute | solution.py:516
  57.0 2.9 %copy-start.11 = (bf16[8,40,128]{2,1,0:T(8,128)(2,1)}, bf16[8,40,128]{2,1,0:T(8,128)(2,1)S(1)}, u32[]{:S(2)}) copy-start(bf16[8,40,128]{2,1,0:T(8,128)(2,1)S(1)} %collective-permute-done.6.refs_1_) | copy-start | bytes 245764
  58.7 1.1 copy-start.12
  59.8 0.6 copy-start.13
  60.5 15.4 %copy-start.15 = (bf16[11,16,1024]{2,1,0:T(8,128)(2,1)S(1)}, bf16[11,16,1024]{2,1,0:T(8,128)(2,1)}, u32[]{:S(2)}) copy-start(bf16[11,16,1024]{2,1,0:T(8,128)(2,1)} %get-tuple-element.153) | copy-start | bytes 1081348
  70.7 7.5 %collective-permute-start.10 = (bf16[8,64,128]{2,1,0:T(8,128)(2,1)}, bf16[8,64,128]{2,1,0:T(8,128)(2,1)S(1)}, u32[]{:S(2)}, u32[]{:S(2)}) collective-permute-start(bf16[8,64,128]{2,1,0:T(8,128)(2,1)} %get-tuple-element.143), channel_id=1, source_target_pairs={{0,2},{1,3},{2,0},{3,1},{4,6},{5,7},{6,4},{7,5},{8,10},{9,11},{10,... | collective-permute-start | bytes 393224 | tf_op jit(solution)/shard_map/ppermute | solution.py:516
  72.1 7.0 %collective-permute-start.11 = (bf16[8,64,128]{2,1,0:T(8,128)(2,1)}, bf16[8,64,128]{2,1,0:T(8,128)(2,1)S(1)}, u32[]{:S(2)}, u32[]{:S(2)}) collective-permute-start(bf16[8,64,128]{2,1,0:T(8,128)(2,1)} %get-tuple-element.144), channel_id=1, source_target_pairs={{0,3},{1,2},{2,1},{3,0},{4,7},{5,6},{6,5},{7,4},{8,11},{9,10},{10,... | collective-permute-start | bytes 393224 | tf_op jit(solution)/shard_map/ppermute | solution.py:516
  72.6 6.6 %collective-permute-start.9 = (bf16[8,64,128]{2,1,0:T(8,128)(2,1)}, bf16[8,64,128]{2,1,0:T(8,128)(2,1)S(1)}, u32[]{:S(2)}, u32[]{:S(2)}) collective-permute-start(bf16[8,64,128]{2,1,0:T(8,128)(2,1)} %get-tuple-element.142), channel_id=1, source_target_pairs={{0,1},{1,0},{2,3},{3,2},{4,5},{5,4},{6,7},{7,6},{8,9},{9,8},{10,11... | collective-permute-start | bytes 393224 | tf_op jit(solution)/shard_map/ppermute | solution.py:516
  72.9 19.4 %collective-permute-start.12 = (bf16[11,16,1024]{2,1,0:T(8,128)(2,1)}, bf16[11,16,1024]{2,1,0:T(8,128)(2,1)S(1)}, u32[]{:S(2)}, u32[]{:S(2)}) collective-permute-start(bf16[11,16,1024]{2,1,0:T(8,128)(2,1)} %get-tuple-element.152), channel_id=1, source_target_pairs={{0,12},{4,8},{8,4},{12,0},{16,28},{20,24},{24,20},{28,16},{1,13},{... | collective-permute-start | bytes 1081352 | tf_op jit(solution)/shard_map/ppermute | solution.py:516
  75.8 25.0 %collective-permute-start.13 = (bf16[11,16,1024]{2,1,0:T(8,128)(2,1)S(1)}, bf16[11,16,1024]{2,1,0:T(8,128)(2,1)S(1)}, u32[]{:S(2)}, u32[]{:S(2)}) collective-permute-start(bf16[11,16,1024]{2,1,0:T(8,128)(2,1)S(1)} %copy-done.15), channel_id=1, source_target_pairs={{0,16},{4,20},{8,24},{12,28},{16,0},{20,4},{24,8},{28,12},{1,17},{... | collective-permute-start | bytes 1081352 | tf_op jit(solution)/shard_map/ppermute | solution.py:516
  85.1 0.9 copy-start.4
  87.1 15.1 %all-to-all-start.3 = ((bf16[8,64,128]{2,1,0:T(8,128)(2,1)}), bf16[8,64,128]{2,1,0:T(8,128)(2,1)S(1)}, u32[]{:S(2)}, u32[]{:S(2)}) async-start(bf16[8,64,128]{2,1,0:T(8,128)(2,1)} %shard_map.144), calls=%async_computation.3 | async-start | bytes 262144 | tf_op jit(solution)/shard_map/all_to_all | solution.py:661
  90.5 12.6 %copy-start.14 = (bf16[11,16,1024]{2,1,0:T(8,128)(2,1)S(1)}, bf16[11,16,1024]{2,1,0:T(8,128)(2,1)}, u32[]{:S(2)}) copy-start(bf16[11,16,1024]{2,1,0:T(8,128)(2,1)} %get-tuple-element.164) | copy-start | bytes 1081348
  102.2 20.6 %collective-permute-start.14 = (bf16[11,16,1024]{2,1,0:T(8,128)(2,1)}, bf16[11,16,1024]{2,1,0:T(8,128)(2,1)S(1)}, u32[]{:S(2)}, u32[]{:S(2)}) collective-permute-start(bf16[11,16,1024]{2,1,0:T(8,128)(2,1)} %get-tuple-element.163), channel_id=1, source_target_pairs={{0,8},{4,12},{8,0},{12,4},{16,24},{20,28},{24,16},{28,20},{1,9},{5... | collective-permute-start | bytes 1081352 | tf_op jit(solution)/shard_map/ppermute | solution.py:516
  103.1 19.7 %collective-permute-start.15 = (bf16[11,16,1024]{2,1,0:T(8,128)(2,1)S(1)}, bf16[11,16,1024]{2,1,0:T(8,128)(2,1)S(1)}, u32[]{:S(2)}, u32[]{:S(2)}) collective-permute-start(bf16[11,16,1024]{2,1,0:T(8,128)(2,1)S(1)} %copy-done.14), channel_id=1, source_target_pairs={{0,20},{4,16},{8,28},{12,24},{16,4},{20,0},{24,12},{28,8},{1,21},{... | collective-permute-start | bytes 1081352 | tf_op jit(solution)/shard_map/ppermute | solution.py:516
  105.8 17.0 %all-to-all-start.4 = ((bf16[8,40,128]{2,1,0:T(8,128)(2,1)}), bf16[8,40,128]{2,1,0:T(8,128)(2,1)S(1)}, u32[]{:S(2)}, u32[]{:S(2)}) async-start(bf16[8,40,128]{2,1,0:T(8,128)(2,1)} %shard_map.146), calls=%async_computation.4 | async-start | bytes 163840 | tf_op jit(solution)/shard_map/all_to_all | solution.py:666
  109.7 16.2 %copy-start.2 = (bf16[1024,512]{1,0:T(8,128)(2,1)S(1)}, bf16[1024,512]{1,0:T(8,128)(2,1)}, u32[]{:S(2)}) copy-start(bf16[1024,512]{1,0:T(8,128)(2,1)} %weight_ref.1) | copy-start | bytes 3145732
  109.7 16.2 %copy-start.8 = (s32[2]{0:T(128)S(1)}, s32[2]{0:T(128)}, u32[]{:S(2)}) copy-start(s32[2]{0:T(128)} %pad_add_fusion.me_ref) | copy-start | bytes 28
  122.8 9.1 %collective-permute-start.19 = (bf16[7,16,1024]{2,1,0:T(8,128)(2,1)}, bf16[7,16,1024]{2,1,0:T(8,128)(2,1)S(1)}, u32[]{:S(2)}, u32[]{:S(2)}) collective-permute-start(bf16[7,16,1024]{2,1,0:T(8,128)(2,1)} %get-tuple-element.181), channel_id=1, source_target_pairs={{0,28},{4,24},{8,20},{12,16},{16,12},{20,8},{24,4},{28,0},{1,29},{... | collective-permute-start | bytes 688136 | tf_op jit(solution)/shard_map/ppermute | solution.py:516
  126.9 3.4 %collective-permute-start.16 = (f32[10,512]{1,0:T(8,128)S(1)}, f32[10,512]{1,0:T(8,128)S(1)}, u32[]{:S(2)}, u32[]{:S(2)}) collective-permute-start(f32[10,512]{1,0:T(8,128)S(1)} %get-tuple-element.178), channel_id=1, source_target_pairs={{0,1},{1,0},{2,3},{3,2},{4,5},{5,4},{6,7},{7,6},{8,9},{9,8},{10,11... | collective-permute-start | bytes 61448 | tf_op jit(solution)/shard_map/ppermute | solution.py:516
  127.0 4.0 %collective-permute-start.17 = (f32[10,512]{1,0:T(8,128)S(1)}, f32[10,512]{1,0:T(8,128)S(1)}, u32[]{:S(2)}, u32[]{:S(2)}) collective-permute-start(f32[10,512]{1,0:T(8,128)S(1)} %get-tuple-element.179), channel_id=1, source_target_pairs={{0,2},{1,3},{2,0},{3,1},{4,6},{5,7},{6,4},{7,5},{8,10},{9,11},{10,... | collective-permute-start | bytes 61448 | tf_op jit(solution)/shard_map/ppermute | solution.py:516
  128.5 3.3 %collective-permute-start.18 = (f32[10,512]{1,0:T(8,128)S(1)}, f32[10,512]{1,0:T(8,128)S(1)}, u32[]{:S(2)}, u32[]{:S(2)}) collective-permute-start(f32[10,512]{1,0:T(8,128)S(1)} %get-tuple-element.180), channel_id=1, source_target_pairs={{0,3},{1,2},{2,1},{3,0},{4,7},{5,6},{6,5},{7,4},{8,11},{9,10},{10,... | collective-permute-start | bytes 61448 | tf_op jit(solution)/shard_map/ppermute | solution.py:516
